TPU v7x, 32 devices: a whole 2x2x4 slice. The times are simulated.
32 devices in a mesh: group: 2 (over y), obs: 4 (over z), node: 2 (over x), mp: 2 (over core).
Axes of the slice: x: 2, y: 2, z: 4, core: 2. Of those that a mesh axis runs over, the one named last changes fastest.
Arguments:
- obs_feat: bfloat16 [2048, 512], P(('group', 'obs', 'node')), parts along dimension 0, may hold values from -6 to 6
- node_state: bfloat16 [5120, 512], P(('group', 'obs', 'node')), parts along dimension 0, may hold values from -6 to 6
- grad_agg: bfloat16 [5120, 512], P(('group', 'obs', 'node')), parts along dimension 0, may hold values from -6 to 6
- owner: int32 [2048, 2], P(('group', 'obs', 'node')), parts along dimension 0, may hold values from 0 to 7, all different within a row; in each aligned block of 128 rows (0 to 127, 128 to 255, ...) at most 64 rows name the same one
- local_idx: int32 [2048, 2], P(('group', 'obs', 'node')), parts along dimension 0, may hold values from 0 to 319
- slot: int32 [2048], P(('group', 'obs', 'node')), parts along dimension 0, may hold values from 0 to 5
- w_obs: bfloat16 [512, 512], P(None, 'mp'), may hold values from -0.25 to 0.25
- w_node: bfloat16 [512, 512], P(None, 'mp'), may hold values from -0.25 to 0.25
- slot_bias: float32 [6, 512], P(None, 'mp'), may hold values from -4 to 4
- w_out: bfloat16 [512, 512], P('mp'), may hold values from -0.25 to 0.25
Outputs:
- grad_obs: bfloat16 [2048, 512], P(('group', 'obs', 'node'), 'mp'), parts along dimension 0
- grad_node: float32 [5120, 512], P(('group', 'obs', 'node'), 'mp'), parts along dimension 0
- grad_w_obs: float32 [1024, 512], P('group', 'mp'), parts along dimension 0
- grad_w_node: float32 [1024, 512], P('group', 'mp'), parts along dimension 0
- grad_w_out: float32 [1024, 512], P(('group', 'mp')), parts along dimension 0
- grad_slot_bias: float32 [12, 512], P('group', 'mp'), parts along dimension 0
There are 2 independent parts, one for each index of `group`. A program takes and returns all parts, laid end to end along the dimension named above; an argument that names none is the same for every part. Nothing has to cross between parts.
Inputs may be any that keep to these rules, and one draw needn't show every extreme that they name: `owner`: each row names 2 different regions; among the rows of one device no region is named more than 64 times, a bound that some block reaches.
All inputs are finite; a program needn't handle non-finite values.
Results may differ from a plain program's by a relative error of at most 0.011.
Values may be sent and summed in bfloat16 or wider, within the bound.
No kernel may reach another device: no remote copies, remote signals or barrier semaphores. Data moves between devices by JAX's collectives and lax.ppermute only.
A program may use at most 64 MiB of HBM per device.

v0:
```python
import jax
import jax.numpy as jnp
from jax import lax
from jax.sharding import PartitionSpec as P


def contract_rows(left, right):
    return lax.dot_general(
        left, right, (((0,), (0,)), ((), ())), preferred_element_type=jnp.float32
    )


def contract_cols(left, right):
    return lax.dot_general(
        left, right, (((1,), (1,)), ((), ())), preferred_element_type=jnp.float32
    )


def local(obs_feat, node_state, grad_agg, owner, local_idx, slot, w_obs, w_node, slot_bias, w_out):
    owners = lax.axis_size(("obs", "node"))
    obs_dev, fanout = owner.shape
    node_dev, width = node_state.shape
    hidden_width = w_obs.shape[1]
    cap = max(2, 2 * obs_dev * fanout // owners)
    edges = obs_dev * fanout
    dest = owner.reshape(edges)
    wanted = local_idx.reshape(edges)
    hits = (dest[:, None] == jnp.arange(owners, dtype=jnp.int32)[None, :]).astype(jnp.int32)
    before = jnp.cumsum(hits, axis=0) - hits
    rank = jnp.sum(before * hits, axis=1)
    place = dest * cap + rank
    requests = jnp.full((owners * cap,), -1, jnp.int32).at[place].set(wanted)
    asked = lax.all_to_all(requests, ("obs", "node"), split_axis=0, concat_axis=0, tiled=True)
    safe_rows = jnp.where(asked >= 0, asked, 0)
    sent_state = jnp.take(node_state, safe_rows, axis=0)
    sent_grad = jnp.take(grad_agg, safe_rows, axis=0)
    got_state, got_grad = (
        lax.all_to_all(sent_state, ("obs", "node"), split_axis=0, concat_axis=0, tiled=True),
        lax.all_to_all(sent_grad, ("obs", "node"), split_axis=0, concat_axis=0, tiled=True),
    )
    edge_state = jnp.take(got_state, place, axis=0)
    edge_grad = jnp.take(got_grad, place, axis=0)
    slot_hot = (slot[:, None] == jnp.arange(slot_bias.shape[0], dtype=jnp.int32)[None, :]).astype(
        jnp.float32
    )
    bias = jnp.dot(slot_hot, slot_bias, precision=lax.Precision.HIGHEST)
    obs_part = jnp.dot(obs_feat, w_obs, preferred_element_type=jnp.float32) + bias
    node_part = jnp.dot(edge_state, w_node, preferred_element_type=jnp.float32)
    pre = (obs_part[:, None, :] + node_part.reshape(obs_dev, fanout, hidden_width)).reshape(
        edges, hidden_width
    )
    sig = jax.nn.sigmoid(pre)
    zvals = (pre * sig).astype(jnp.bfloat16)
    g_z = contract_cols(edge_grad, w_out)
    g_a = (g_z * sig * (1.0 + pre * (1.0 - sig))).astype(jnp.bfloat16)
    obs_hidden = jnp.sum(
        g_a.astype(jnp.float32).reshape(obs_dev, fanout, hidden_width), axis=1
    ).astype(jnp.bfloat16)
    obs_partial = contract_cols(obs_hidden, w_obs)
    term = contract_cols(g_a, w_node)
    buffer = jnp.zeros((owners * cap, width), jnp.float32).at[place].set(term)
    arrived = lax.all_to_all(
        buffer.astype(jnp.bfloat16), ("obs", "node"), split_axis=0, concat_axis=0, tiled=True
    ).astype(buffer.dtype)
    node_partial = jnp.zeros((node_dev, width), jnp.float32).at[safe_rows].add(arrived)
    grad_obs, grad_node = (
        lax.psum_scatter(
            obs_partial.astype(jnp.bfloat16), "mp", scatter_dimension=1, tiled=True
        ).astype(jnp.float32),
        lax.psum_scatter(
            node_partial.astype(jnp.bfloat16), "mp", scatter_dimension=1, tiled=True
        ).astype(jnp.float32),
    )
    grad_w_obs = contract_rows(obs_feat, obs_hidden)
    grad_w_node = contract_rows(edge_state, g_a)
    grad_w_out = contract_rows(zvals, edge_grad)
    grad_slot = lax.dot_general(
        slot_hot,
        obs_hidden.astype(jnp.float32),
        (((0,), (0,)), ((), ())),
        precision=lax.Precision.HIGHEST,
    )
    sums = lax.psum((grad_w_obs, grad_w_node, grad_w_out, grad_slot), ("obs", "node"))
    return (grad_obs.astype(jnp.bfloat16), grad_node, sums[0], sums[1], sums[2], sums[3])


def solution(mesh):
    return jax.shard_map(
        local,
        mesh=mesh,
        in_specs=(
            P(("group", "obs", "node"), None),
            P(("group", "obs", "node"), None),
            P(("group", "obs", "node"), None),
            P(("group", "obs", "node"), None),
            P(("group", "obs", "node"), None),
            P(("group", "obs", "node")),
            P(None, "mp"),
            P(None, "mp"),
            P(None, "mp"),
            P("mp", None),
        ),
        out_specs=(
            P(("group", "obs", "node"), "mp"),
            P(("group", "obs", "node"), "mp"),
            P("group", "mp"),
            P("group", "mp"),
            P(("group", "mp"), None),
            P("group", "mp"),
        ),
        check_vma=False,
    )
```

profile of v0, /device:TPU:0, one launch (start us, length us, event | category | flops | bytes accessed | tf_op | source)
XLA Modules:
  0.0 186.8 jit_solution(14266729617627377719)
XLA Ops:
  8.0 0.8 copy.22
  8.8 0.1 eq.42
  9.0 0.1 eq.38
  9.1 0.5 copy-done.9
  9.7 0.6 reduce-window.6
  10.3 0.2 slice_reduce_fusion
  10.5 0.6 copy-done.8
  11.2 0.1 mul.37
  11.3 0.5 copy-done.10
  12.1 0.5 slice-done
  12.8 1.4 scatter_custom_fusion
  14.2 13.5 %all_to_all.48 = s32[8,64,1]{1,2,0:T(1,128)S(1)} all-to-all(s32[8,64,1]{1,2,0:T(1,128)S(1)} %bitcast.41), channel_id=1, replica_groups=mesh['group'=2,'obs'=4,'node'=2,'mp'=2] {'obs','node'}, dimensions={0} | all-to-all | bytes 4096 | tf_op jit(solution)/shard_map/all_to_all | solution.py:33
  27.8 0.5 broadcast.127
  28.3 0.7 reduce.8
  29.1 2.0 %gather_fusion = bf16[512,512]{1,0:T(8,128)(2,1)S(1)} fusion(bf16[320,512]{1,0:T(8,128)(2,1)S(1)} %copy-done, s32[1024]{0:T(1024)S(1)} %pad_clamp_fusion.1), kind=kCustom, calls=%fused_computation.clone | custom fusion | bytes 1050624 | tf_op jit(solution)/shard_map/jit(_take)/gather | solution.py:36
  31.1 2.0 %gather_fusion.2 = bf16[512,512]{1,0:T(8,128)(2,1)S(1)} fusion(bf16[320,512]{1,0:T(8,128)(2,1)S(1)} %copy-done.1, s32[1024]{0:T(1024)S(1)} %pad_clamp_fusion.1), kind=kCustom, calls=%fused_computation.2.clone | custom fusion | bytes 1050624 | tf_op jit(solution)/shard_map/jit(_take)/gather | solution.py:35
  33.0 1.0 broadcast_select_fusion.1
  34.0 15.7 %all_to_all.49 = bf16[8,64,512]{2,1,0:T(8,128)(2,1)S(1)} all-to-all(bf16[8,64,512]{2,1,0:T(8,128)(2,1)S(1)} %bitcast.38), channel_id=1, replica_groups=mesh['group'=2,'obs'=4,'node'=2,'mp'=2] {'obs','node'}, dimensions={0} | all-to-all | bytes 1048576 | tf_op jit(solution)/shard_map/all_to_all | solution.py:38
  49.7 3.8 %all-to-all-start.1 = ((bf16[8,64,512]{2,1,0:T(8,128)(2,1)}), bf16[8,64,512]{2,1,0:T(8,128)(2,1)S(1)}, u32[]{:S(2)}, u32[]{:S(2)}) async-start(bf16[8,64,512]{2,1,0:T(8,128)(2,1)} %bitcast.5), calls=%async_computation.1 | async-start | bytes 1048576 | tf_op jit(solution)/shard_map/all_to_all | solution.py:39
  53.6 0.3 fusion.11
  53.8 0.6 copy-done.6
  54.4 0.2 convolution_add_fusion.1
  54.7 0.2 add.87
  54.9 1.2 gather_fusion.3
  56.1 11.5 %all-to-all-done.1 = bf16[8,64,512]{2,1,0:T(8,128)(2,1)S(1)} async-done(((bf16[8,64,512]{2,1,0:T(8,128)(2,1)}), bf16[8,64,512]{2,1,0:T(8,128)(2,1)S(1)}, u32[]{:S(2)}, u32[]{:S(2)}) %all-to-all-start.1) | async-done | bytes 524320 | tf_op jit(solution)/shard_map/all_to_all | solution.py:39
  67.5 1.2 gather_fusion.1
  68.7 0.3 convolution_add_fusion
  69.0 1.1 fusion.7
  70.1 0.3 fusion.1
  70.4 1.1 fusion.9
  71.6 0.3 reduce
  71.9 1.0 convolution_bitcast_fusion
  73.0 0.3 fusion.24
  73.3 1.7 scatter_custom_fusion.1
  75.0 0.9 convert_element_type.44
  75.8 3.7 %all-to-all-start.3 = ((bf16[8,64,512]{2,1,0:T(8,128)(2,1)}), bf16[8,64,512]{2,1,0:T(8,128)(2,1)S(1)}, u32[]{:S(2)}, u32[]{:S(2)}) async-start(bf16[8,64,512]{2,1,0:T(8,128)(2,1)} %bitcast.10), calls=%async_computation.4 | async-start | bytes 1048576 | tf_op jit(solution)/shard_map/all_to_all | solution.py:62
  79.6 28.1 %all-to-all-done.3 = bf16[8,64,512]{2,1,0:T(8,128)(2,1)S(1)} async-done(((bf16[8,64,512]{2,1,0:T(8,128)(2,1)}), bf16[8,64,512]{2,1,0:T(8,128)(2,1)S(1)}, u32[]{:S(2)}, u32[]{:S(2)}) %all-to-all-start.3) | async-done | bytes 524320 | tf_op jit(solution)/shard_map/all_to_all | solution.py:62
  107.7 4.1 %scatter_custom_fusion.2 = f32[320,512]{1,0:T(8,128)S(1)} fusion(s32[512]{0:T(512)S(1)} %bitcast.43, bf16[512,512]{1,0:T(8,128)(2,1)S(1)} %bitcast.39, f32[]{:T(128)} %constant.28.clone.1), kind=kCustom, calls=%fused_computation.14 | custom fusion | flops 524288 | bytes 1179652 | tf_op jit(solution)/shard_map/scatter-add | solution.py:65
  111.8 0.8 convert_element_type.47
  112.7 0.9 convolution_convert_fusion
  113.6 0.2 fusion.10
  113.8 19.1 %psum.31 = f32[6,256]{1,0:T(8,128)} all-reduce(f32[6,256]{1,0:T(8,128)S(1)} %fusion.10), channel_id=1, replica_groups=mesh['group'=2,'obs'=4,'node'=2,'mp'=2] {'obs','node'}, use_global_device_ids=true, to_apply=%region_12.15 | all-reduce | flops 1536 | bytes 12288 | tf_op jit(solution)/shard_map/psum | solution.py:83
  132.9 40.6 %all-reduce.3.cloned.1.call-done = (f32[512,256]{0,1:T(8,128)}, f32[512,256]{1,0:T(8,128)}, f32[256,512]{1,0:T(8,128)}) async-done(((f32[512,256]{0,1:T(8,128)}, f32[512,256]{1,0:T(8,128)}, f32[256,512]{1,0:T(8,128)}), (f32[512,256]{0,1:T(8,128)}, f32[512,256]{1,0:T(8,128)}, f32[256,512]{1,0:T(8,128)})) %all-reduce.3.cloned.1.call-update) | async-done | bytes 1572880 | tf_op jit(solution)/shard_map/psum | solution.py:83
  173.5 2.1 %copy.27 = f32[512,256]{1,0:T(8,128)} copy(f32[512,256]{0,1:T(8,128)} %get-tuple-element.26) | data formatting | bytes 1048576
  175.6 1.7 convert_element_type.48
  177.3 0.8 copy.31
  178.1 0.4 copy-done.4
  178.5 0.8 copy.32
  (49 shorter events, 1.2 us)
Async XLA Ops:
  8.0 21.0 %copy-start = (bf16[320,512]{1,0:T(8,128)(2,1)S(1)}, bf16[320,512]{1,0:T(8,128)(2,1)}, u32[]{:S(2)}) copy-start(bf16[320,512]{1,0:T(8,128)(2,1)} %param.16) | copy-start | bytes 983044
  9.0 0.7 copy-start.9
  10.5 0.6 copy-start.8
  11.2 0.7 copy-start.10
  12.0 0.7 slice-start
  29.1 2.0 %copy-start.1 = (bf16[320,512]{1,0:T(8,128)(2,1)S(1)}, bf16[320,512]{1,0:T(8,128)(2,1)}, u32[]{:S(2)}) copy-start(bf16[320,512]{1,0:T(8,128)(2,1)} %param.15) | copy-start | bytes 983044
  49.7 3.8 %copy-start.7 = (f32[6,256]{1,0:T(8,128)S(1)}, f32[6,256]{1,0:T(8,128)}, u32[]{:S(2)}) copy-start(f32[6,256]{1,0:T(8,128)} %param.22) | copy-start | bytes 18436
  49.7 3.8 %copy-start.11 = (s32[128]{0:T(128)S(1)}, s32[128]{0:T(128)}, u32[]{:S(2)}) copy-start(s32[128]{0:T(128)} %param.19) | copy-start | bytes 1540
  49.7 4.1 %copy-start.2 = (bf16[512,256]{1,0:T(8,128)(2,1)S(1)}, bf16[512,256]{1,0:T(8,128)(2,1)}, u32[]{:S(2)}) copy-start(bf16[512,256]{1,0:T(8,128)(2,1)} %param.20) | copy-start | bytes 786436
  49.7 17.8 %all-to-all-start.1 = ((bf16[8,64,512]{2,1,0:T(8,128)(2,1)}), bf16[8,64,512]{2,1,0:T(8,128)(2,1)S(1)}, u32[]{:S(2)}, u32[]{:S(2)}) async-start(bf16[8,64,512]{2,1,0:T(8,128)(2,1)} %bitcast.5), calls=%async_computation.1 | async-start | bytes 1048576 | tf_op jit(solution)/shard_map/all_to_all | solution.py:39
  53.5 0.9 copy-start.6
  53.5 120.0 %all-reduce.3.cloned.1.call-start = ((), (), s32[]{:S(2)}) async-start(), calls=%async_computation.8 | async-start | bytes 3145728 | tf_op jit(solution)/shard_map/psum | solution.py:83
  67.5 1.2 copy-start.3
  69.0 1.1 copy-start.12
  75.8 31.9 %all-to-all-start.3 = ((bf16[8,64,512]{2,1,0:T(8,128)(2,1)}), bf16[8,64,512]{2,1,0:T(8,128)(2,1)S(1)}, u32[]{:S(2)}, u32[]{:S(2)}) async-start(bf16[8,64,512]{2,1,0:T(8,128)(2,1)} %bitcast.10), calls=%async_computation.4 | async-start | bytes 1048576 | tf_op jit(solution)/shard_map/all_to_all | solution.py:62
  79.5 96.2 %reduce-scatter.5.cloned.1.call-start = ((), (), s32[]{:S(2)}) async-start(), calls=%async_computation.7 | async-start | bytes 491520 | tf_op jit(solution)/shard_map/reduce_scatter | solution.py:70
  112.6 64.7 %reduce-scatter.3.cloned.1.call-start = ((), (), s32[]{:S(2)}) async-start(), calls=%async_computation.6 | async-start | bytes 196608 | tf_op jit(solution)/shard_map/reduce_scatter | solution.py:67
  173.5 3.8 %copy-start.5 = (f32[512,256]{1,0:T(8,128)S(1)}, f32[512,256]{1,0:T(8,128)}, u32[]{:S(2)}) copy-start(f32[512,256]{1,0:T(8,128)} %get-tuple-element.36) | copy-start | bytes 1572868
  177.3 1.2 copy-start.4
Sparse Core Ops, SparseCore 0:
  73.1 100.3 all-reduce.2
Sparse Core Ops, SparseCore 1:
  112.7 5.5 reduce-scatter.4
  121.0 8.6 reduce-scatter.2
where the time goes:
time: 187 us
  waiting for transfers between devices  80.2 us (43%)
  blocking collectives  48.3 us (26%)
  local copies, waits for them, and re-layouts  19.1 us (10%)
  between operations  15.7 us (8%)
  other arithmetic  10.1 us (5%)
  starting transfers between devices  7.54 us (4%)
  matrix products  5.68 us (3%)
    psum x1, waiting for transfers between devices, local(): lax.psum((grad_w_obs, grad_w_node, grad_w_out, grad_slot), ('obs', 'node'))  40.6 us
    all_to_all x1, waiting for transfers between devices, local(): lax.all_to_all(buffer.astype(jnp.bfloat16), ('obs', 'node'), split_axis=0...  28.1 us
    psum x1, blocking collectives, local(): lax.psum((grad_w_obs, grad_w_node, grad_w_out, grad_slot), ('obs', 'node'))  19.1 us
    all_to_all x1, blocking collectives, local(): lax.all_to_all(sent_state, ('obs', 'node'), split_axis=0, concat_axis=0,...  15.7 us
    all_to_all x1, blocking collectives, local(): lax.all_to_all(requests, ('obs', 'node'), split_axis=0, concat_axis=0, ti...  13.5 us
    all_to_all x1, waiting for transfers between devices, local(): lax.all_to_all(sent_grad, ('obs', 'node'), split_axis=0, concat_axis=0, t...  11.5 us
    unnamed x31, local copies, waits for them, and re-layouts  7.32 us
    scatter-add x1, other arithmetic, local(): jnp.zeros((node_dev, width), jnp.float32).at[safe_rows].add(arrived)  4.11 us
  transfers between devices with their start and end apart: 5, of which 3 were waited for; matrix products, arithmetic and copies ran while one was open for 8% of the time, Pallas kernels for 0%

commit v1 on v0

v1 whole, which is shorter than its diff:
```python
import functools

import jax
import jax.numpy as jnp
from jax import lax
from jax.experimental import pallas as pl
from jax.experimental.pallas import tpu as pltpu
from jax.sharding import PartitionSpec as P

OWNER_AXES = ("obs", "node")
SUBLANES = 16
BF16 = jnp.bfloat16
F32 = jnp.float32


def dot(left, right, left_dim=1, right_dim=0):
    return lax.dot_general(
        left, right, (((left_dim,), (right_dim,)), ((), ())), preferred_element_type=F32
    )


def iota(shape, dim):
    return lax.broadcasted_iota(jnp.int32, shape, dim)


def call(kernel, outs, *args):
    vmem = pl.BlockSpec(memory_space=pltpu.VMEM)
    return pl.pallas_call(
        kernel,
        out_shape=[jax.ShapeDtypeStruct(shape, dtype) for shape, dtype in outs],
        in_specs=[vmem] * len(args),
        out_specs=[vmem] * len(outs),
        compiler_params=pltpu.CompilerParams(vmem_limit_bytes=40 << 20),
    )(*args)


def exchange(blocks):
    return lax.all_to_all(blocks, OWNER_AXES, split_axis=0, concat_axis=0, tiled=True)


def swap_cores(value):
    return lax.ppermute(value, "mp", [(0, 1), (1, 0)])


def other_half(ref):
    half = ref.shape[0] // 2
    me = lax.axis_index("mp")
    mine = ref[pl.ds(pl.multiple_of(me * half, half), half), :]
    theirs = ref[pl.ds(pl.multiple_of((1 - me) * half, half), half), :]
    return mine, theirs


def slot_one_hot(slot_ref, slots):
    obs = slot_ref.shape[1]
    return (iota((slots, obs), 0) == slot_ref[...]).astype(F32)


def pack_kernel(obs_ref, owner_ref, index_ref, slot_ref, w_ref, bias_ref, out_ref, place_ref):
    owners, chunk, lanes = out_ref.shape
    fanout, obs = owner_ref.shape
    cap = (chunk - SUBLANES) * lanes // w_ref.shape[1]
    owner, index = owner_ref[...], index_ref[...]
    hits = [iota((owners, obs), 0) == owner[k : k + 1] for k in range(fanout)]
    count = functools.reduce(jnp.add, [h.astype(F32) for h in hits])
    before = dot(count, (iota((obs, obs), 0) < iota((obs, obs), 1)).astype(F32))
    header = jnp.zeros((SUBLANES, obs), F32)
    pick = None
    for k in range(fanout):
        rank = jnp.sum(jnp.where(hits[k], before, 0.0), axis=0, keepdims=True)
        place = owner[k : k + 1] * cap + rank.astype(jnp.int32)
        place_ref[k : k + 1, :] = place
        mine = iota((owners * cap, obs), 0) == place
        pick = mine if pick is None else pick | mine
        plus = index[k : k + 1] + 1
        fields = (owner[k : k + 1].astype(F32), rank, (plus // 16).astype(F32), (plus % 16).astype(F32))
        for j, row in enumerate(fields):
            header = jnp.where(iota(header.shape, 0) == 4 * k + j, row, header)
    bias = lax.dot_general(
        slot_one_hot(slot_ref, bias_ref.shape[0]),
        bias_ref[...],
        (((0,), (0,)), ((), ())),
        precision=lax.Precision.HIGHEST,
        preferred_element_type=F32,
    )
    part = (dot(obs_ref[...], w_ref[...]) + bias).astype(BF16)
    packed = dot(pick.astype(BF16), part).astype(BF16)
    header = header.astype(BF16)
    for d in range(owners):
        for c in range(part.shape[1] // lanes):
            out_ref[d, c * cap : (c + 1) * cap, :] = packed[
                d * cap : (d + 1) * cap, c * lanes : (c + 1) * lanes
            ]
        out_ref[d, chunk - SUBLANES :, :] = header


def table_kernel(state_ref, agg_ref, w_node_ref, w_out_ref, table_ref):
    hidden = w_node_ref.shape[1]
    parts = (dot(state_ref[...], w_node_ref[...]), dot(agg_ref[...], w_out_ref[...], 1, 1))
    for j, part in enumerate(parts):
        high = part.astype(BF16)
        table_ref[:, 2 * j * hidden : (2 * j + 1) * hidden] = high
        table_ref[:, (2 * j + 1) * hidden : (2 * j + 2) * hidden] = (
            part - high.astype(F32)
        ).astype(BF16)


def edge_kernel(recv_ref, table_ref, act_ref, hot_ref):
    owners, chunk, lanes = recv_ref.shape
    hidden = table_ref.shape[1] // 4
    cap = (chunk - SUBLANES) * lanes // hidden
    me = lax.axis_index(OWNER_AXES).astype(F32)
    columns = []
    parts = []
    for s in range(owners):
        header = recv_ref[s, chunk - SUBLANES :, :].astype(F32)
        plus = jnp.zeros((cap, lanes), F32)
        for k in range(2):
            row = header[4 * k : 4 * k + 4]
            rank = jnp.where(row[0:1] == me, row[1:2], -1.0).astype(jnp.int32)
            plus = plus + jnp.where(iota((cap, lanes), 0) == rank, row[2:3] * 16.0 + row[3:4], 0.0)
        columns.append(jnp.sum(plus, axis=1, keepdims=True).astype(jnp.int32) - 1)
        parts.append(
            jnp.concatenate(
                [recv_ref[s, c * cap : (c + 1) * cap, :] for c in range(hidden // lanes)], axis=1
            ).astype(F32)
        )
    column = jnp.concatenate(columns, axis=0)
    hot = (column == iota(hot_ref.shape, 1)).astype(BF16)
    hot_ref[...] = hot
    rows = dot(hot, table_ref[...])
    pre = jnp.concatenate(parts, axis=0) + (rows[:, :hidden] + rows[:, hidden : 2 * hidden])
    g_z = rows[:, 2 * hidden : 3 * hidden] + rows[:, 3 * hidden :]
    sig = jax.nn.sigmoid(pre)
    act_ref[:, :hidden] = (g_z * sig * (1.0 + pre * (1.0 - sig))).astype(BF16)
    act_ref[:, hidden:] = (pre * sig).astype(BF16)


def put_rows(out_ref, start, rows, value):
    value = value.astype(BF16)
    width = out_ref.shape[2]
    for d in range(out_ref.shape[0]):
        for c in range(value.shape[1] // width):
            at = start + c * rows
            if (d + 1) * rows <= value.shape[0]:
                block = value[d * rows : (d + 1) * rows, c * width : (c + 1) * width]
            else:
                block = jnp.zeros((rows, width), BF16)
            out_ref[d, at : at + rows, :] = block


def chunk_rows(total, owners):
    return max(SUBLANES, total // owners)


def node_kernel(hot_ref, act_ref, state_ref, agg_ref, w_node_ref, sums_ref, keep_ref, send_ref):
    owners = sums_ref.shape[0]
    width = state_ref.shape[1]
    hidden = w_node_ref.shape[1]
    by_node = dot(hot_ref[...], act_ref[...], 0, 0).astype(BF16)
    node_hidden, z_sum = by_node[:, :hidden], by_node[:, hidden:]
    mine, theirs = other_half(w_node_ref)
    send_ref[...] = dot(node_hidden, theirs, 1, 1).astype(BF16)
    keep_ref[...] = dot(node_hidden, mine, 1, 1)
    rows = chunk_rows(width, owners)
    put_rows(sums_ref, 0, rows, dot(state_ref[...], node_hidden, 0, 0))
    put_rows(sums_ref, rows, chunk_rows(hidden, owners), dot(z_sum, agg_ref[...], 0, 0))


def obs_kernel(back_ref, place_ref, slot_ref, obs_ref, w_ref, sums_ref, keep_ref, send_ref, *, slots):
    owners = sums_ref.shape[0]
    width, hidden = w_ref.shape
    fanout, obs = place_ref.shape
    pick = None
    for k in range(fanout):
        mine = iota((back_ref.shape[0], obs), 0) == place_ref[k : k + 1, :]
        pick = mine if pick is None else pick | mine
    obs_hidden = dot(pick.astype(BF16), back_ref[...], 0, 0).astype(BF16)
    mine, theirs = other_half(w_ref)
    send_ref[...] = dot(obs_hidden, theirs, 1, 1).astype(BF16)
    keep_ref[...] = dot(obs_hidden, mine, 1, 1)
    rows = chunk_rows(width, owners)
    put_rows(sums_ref, 0, rows, dot(obs_ref[...], obs_hidden, 0, 0))
    slot_sum = dot(slot_one_hot(slot_ref, slots).astype(BF16), obs_hidden).astype(BF16)
    for d in range(owners):
        sums_ref[d, rows:, :] = slot_sum


def sum_kernel(first_ref, second_ref, out_ref, slot_ref):
    owners, rows, _ = first_ref.shape
    more = out_ref.shape[1] - rows
    first = jnp.sum(first_ref[...].astype(F32), axis=0).astype(BF16)
    second = jnp.sum(second_ref[...].astype(F32), axis=0)
    slot_ref[...] = second[more : more + slot_ref.shape[0]]
    second = second[:more].astype(BF16)
    for d in range(owners):
        out_ref[d, :rows, :] = first
        out_ref[d, rows:, :] = second


def finish_kernel(
    all_ref, node_keep_ref, node_got_ref, obs_keep_ref, obs_got_ref,
    grad_obs_ref, grad_node_ref, w_obs_ref, w_node_ref, w_out_ref,
):
    owners, _, hidden = all_ref.shape
    width = w_obs_ref.shape[0]
    rows, out_rows = chunk_rows(width, owners), chunk_rows(w_out_ref.shape[0], owners)
    pieces = w_out_ref.shape[1] // hidden
    for d in range(owners):
        at = d * rows
        if at < width:
            w_node_ref[at : at + rows, :] = all_ref[d, :rows, :].astype(F32)
            w_obs_ref[at : at + rows, :] = all_ref[d, rows + pieces * out_rows :, :].astype(F32)
        at = d * out_rows
        if at < w_out_ref.shape[0]:
            for c in range(pieces):
                begin = rows + c * out_rows
                w_out_ref[at : at + out_rows, c * hidden : (c + 1) * hidden] = all_ref[
                    d, begin : begin + out_rows, :
                ].astype(F32)
    grad_node_ref[...] = node_keep_ref[...] + node_got_ref[...].astype(F32)
    grad_obs_ref[...] = (obs_keep_ref[...] + obs_got_ref[...].astype(F32)).astype(BF16)


def local(obs_feat, node_state, grad_agg, owner, local_idx, slot, w_obs, w_node, slot_bias, w_out):
    owners = lax.axis_size(OWNER_AXES)
    obs, fanout = owner.shape
    nodes, width = node_state.shape
    hidden = w_obs.shape[1]
    slots = slot_bias.shape[0]
    cap = max(2, 2 * obs * fanout // owners)
    cap = -(-cap // SUBLANES) * SUBLANES
    edges = owners * cap
    half = width // 2
    slot_row = slot.reshape(1, obs)

    chunk = cap * hidden // obs + SUBLANES
    packed, place = call(
        pack_kernel,
        [((owners, chunk, obs), BF16), ((fanout, obs), jnp.int32)],
        obs_feat, owner.T, local_idx.T, slot_row, w_obs, slot_bias,
    )
    (table,) = call(
        table_kernel, [((nodes, 4 * hidden), BF16)], node_state, grad_agg, w_node, w_out
    )
    received = exchange(packed)
    act, hot = call(
        edge_kernel, [((edges, 2 * hidden), BF16), ((edges, nodes), BF16)], received, table
    )
    back = exchange(act[:, :hidden].reshape(owners, cap, hidden)).reshape(edges, hidden)

    rows = chunk_rows(width, owners)
    first = rows + width // hidden * chunk_rows(hidden, owners)
    node_sums, node_keep, node_send = call(
        node_kernel,
        [((owners, first, hidden), BF16), ((nodes, half), F32), ((nodes, half), BF16)],
        hot, act, node_state, grad_agg, w_node,
    )
    node_got = swap_cores(node_send)
    node_sums = exchange(node_sums)
    padded = -(-slots // SUBLANES) * SUBLANES
    obs_sums, obs_keep, obs_send = call(
        functools.partial(obs_kernel, slots=padded),
        [((owners, rows + padded, hidden), BF16), ((obs, half), F32), ((obs, half), BF16)],
        back, place, slot_row, obs_feat, w_obs,
    )
    obs_got = swap_cores(obs_send)
    obs_sums = exchange(obs_sums)
    totals, grad_slot = call(
        sum_kernel,
        [((owners, first + rows, hidden), BF16), ((slots, hidden), F32)],
        node_sums, obs_sums,
    )
    totals = exchange(totals)
    grad_obs, grad_node, grad_w_obs, grad_w_node, grad_w_out = call(
        finish_kernel,
        [
            ((obs, half), BF16),
            ((nodes, half), F32),
            ((width, hidden), F32),
            ((width, hidden), F32),
            ((hidden, width), F32),
        ],
        totals, node_keep, node_got, obs_keep, obs_got,
    )
    return grad_obs, grad_node, grad_w_obs, grad_w_node, grad_w_out, grad_slot


def solution(mesh):
    rows = P(("group", "obs", "node"), None)
    return jax.shard_map(
        local,
        mesh=mesh,
        in_specs=(
            rows, rows, rows, rows, rows,
            P(("group", "obs", "node")),
            P(None, "mp"), P(None, "mp"), P(None, "mp"), P("mp", None),
        ),
        out_specs=(
            P(("group", "obs", "node"), "mp"),
            P(("group", "obs", "node"), "mp"),
            P("group", "mp"),
            P("group", "mp"),
            P(("group", "mp"), None),
            P("group", "mp"),
        ),
        check_vma=False,
    )
```

time: 187 us -> 93.8 us (0.50)
  blocking collectives: 48.3 us -> 14.1 us
  waiting for transfers between devices: 80.2 us -> 47.4 us
  between operations: 15.7 us -> 0.75 us
  local copies, waits for them, and re-layouts: 19.1 us -> 4.92 us
  starting transfers between devices: 7.54 us -> 18.8 us
  other arithmetic: 10.1 us -> 0 us
  Pallas kernels: 0 us -> 7.19 us
  matrix products: 5.68 us -> 0 us
    psum x1 -> x0, waiting for transfers between devices: 40.6 us -> none  [local(): lax.psum((grad_w_obs, grad_w_node, grad_w_out, grad_slot), ('obs', 'node'))]
    psum x1 -> x0, blocking collectives: 19.1 us -> none  [local(): lax.psum((grad_w_obs, grad_w_node, grad_w_out, grad_slot), ('obs', 'node'))]
    all_to_all x2 -> x1, blocking collectives: 29.2 us -> 14.1 us  [exchange(): lax.all_to_all(blocks, OWNER_AXES, split_axis=0, concat_axis=0, tiled=True)]
    all_to_all x2 -> x4, starting transfers between devices: 7.42 us -> 18.2 us  [exchange(): lax.all_to_all(blocks, OWNER_AXES, split_axis=0, concat_axis=0, tiled=True)]
    pallas_call x0 -> x7, Pallas kernels: none -> 7.19 us  [call(): pl.pallas_call(kernel, out_shape=[jax.ShapeDtypeStruct(shape, dtype) for...]
    all_to_all x2 -> x4, waiting for transfers between devices: 39.6 us -> 46.4 us  [exchange(): lax.all_to_all(blocks, OWNER_AXES, split_axis=0, concat_axis=0, tiled=True)]
    gather x4 -> x0, local copies, waits for them, and re-layouts: 6.25 us -> none  [the longest x1 1.97 us: local(): sent_grad = jnp.take(grad_agg, safe_rows, axis=0)]
    dot_general x10 -> x0, matrix products: 5.68 us -> none  [the longest x3 3.3 us: contract_rows(): lax.dot_general(left, right, (((0,), (0,)), ((), ())), preferred_element_...]
  transfers between devices with their start and end apart: 5 -> 6, of which waited for: 3 -> 6; matrix products, arithmetic and copies ran while one was open for 8% -> 0% of each run, Pallas kernels for 0% -> 3%
where the time goes in v1:
time: 93.8 us; the launch traced here: 93.2 us
  waiting for transfers between devices  47.4 us (51%)
  starting transfers between devices  18.8 us (20%)
  blocking collectives  14.1 us (15%)
  Pallas kernels  7.19 us (8%)
  local copies, waits for them, and re-layouts  4.92 us (5%)
    all_to_all x4, waiting for transfers between devices, exchange(): lax.all_to_all(blocks, OWNER_AXES, split_axis=0, concat_axis=0, tiled=True)  46.4 us
    all_to_all x4, starting transfers between devices, exchange(): lax.all_to_all(blocks, OWNER_AXES, split_axis=0, concat_axis=0, tiled=True)  18.2 us
    all_to_all x1, blocking collectives, exchange(): lax.all_to_all(blocks, OWNER_AXES, split_axis=0, concat_axis=0, tiled=True)  14.1 us
    pallas_call x7, Pallas kernels, call(): pl.pallas_call(kernel, out_shape=[jax.ShapeDtypeStruct(shape, dtype) for...  7.19 us
    unnamed x24, local copies, waits for them, and re-layouts  4.2 us
  transfers between devices with their start and end apart: 6, of which 6 were waited for; matrix products, arithmetic and copies ran while one was open for 0% of the time, Pallas kernels for 3%

profile of v1, /device:TPU:0, one launch (start us, length us, event | category | flops | bytes accessed | tf_op | source)
XLA Modules:
  0.0 93.2 jit_solution(14764182205219215544)
XLA Ops:
  0.6 0.0 copy-start.11
  0.6 0.0 copy-start.9
  0.7 0.0 copy-start.10
  0.7 0.7 copy-done.11
  1.3 0.0 copy-done.9
  1.3 0.0 copy-done.10
  1.3 0.0 copy-start.3
  1.3 0.9 %copy-done.3 = bf16[512,256]{1,0:T(8,128)(2,1)S(1)} copy-done((bf16[512,256]{1,0:T(8,128)(2,1)S(1)}, bf16[512,256]{1,0:T(8,128)(2,1)}, u32[]{:S(2)}) %copy-start.3) | copy-done | bytes 262168
  2.3 0.0 copy-start.5
  2.3 0.9 copy-done.5
  3.2 0.0 copy-start.8
  3.2 0.7 copy-done.8
  3.9 0.0 copy-start.1
  3.9 1.4 %shard_map.145 = (bf16[8,144,128]{2,1,0:T(8,128)(2,1)}, s32[2,128]{1,0:T(2,128)S(1)}) custom-call(bf16[128,512]{1,0:T(8,128)(2,1)S(1)} %copy-done.5, s32[2,128]{1,0:T(2,128)S(1)} %bitcast.8, s32[2,128]{1,0:T(2,128)S(1)} %bitcast.9, s32[1,128]{1,0:T(1,128)S(1)} %bitcast.6, bf16[512,256]{1,0:T(8,128)(2,1)S(1)} %copy-done.3, f32[6,256]{1,0:T(8,128)S(1)} %copy-done.8), custom_call_target="tpu_custom_call" | custom-call | tf_op jit(solution)/shard_map/pallas_call | solution.py:28
  5.3 0.0 copy-start
  5.3 0.0 copy-start.2
  5.3 7.4 %all-to-all-start = ((bf16[8,144,128]{2,1,0:T(8,128)(2,1)}), bf16[8,144,128]{2,1,0:T(8,128)(2,1)S(1)}, u32[]{:S(2)}, u32[]{:S(2)}) async-start(bf16[8,144,128]{2,1,0:T(8,128)(2,1)} %get-tuple-element.23), calls=%async_computation | async-start | bytes 589824 | tf_op jit(solution)/shard_map/all_to_all | solution.py:38
  12.6 0.0 copy-done.1
  12.6 0.0 copy-done
  12.7 0.0 copy-done.2
  12.7 0.0 copy-start.7
  12.7 0.9 %copy-done.7 = bf16[256,512]{1,0:T(8,128)(2,1)S(1)} copy-done((bf16[256,512]{1,0:T(8,128)(2,1)S(1)}, bf16[256,512]{1,0:T(8,128)(2,1)}, u32[]{:S(2)}) %copy-start.7) | copy-done | bytes 262168
  13.6 0.3 shard_map.146.table_ref
  14.0 8.3 %all-to-all-done.recv_ref = bf16[8,144,128]{2,1,0:T(8,128)(2,1)S(1)} async-done(((bf16[8,144,128]{2,1,0:T(8,128)(2,1)}), bf16[8,144,128]{2,1,0:T(8,128)(2,1)S(1)}, u32[]{:S(2)}, u32[]{:S(2)}) %all-to-all-start) | async-done | bytes 294944 | tf_op jit(solution)/shard_map/all_to_all | solution.py:38
  22.3 1.0 %shard_map.147 = (bf16[512,512]{1,0:T(8,128)(2,1)S(1)}, bf16[512,320]{1,0:T(8,128)(2,1)S(1)}) custom-call(bf16[8,144,128]{2,1,0:T(8,128)(2,1)S(1)} %all-to-all-done.recv_ref, bf16[320,1024]{1,0:T(8,128)(2,1)S(1)} %shard_map.146.table_ref), custom_call_target="tpu_custom_call" | custom-call | tf_op jit(solution)/shard_map/pallas_call | solution.py:28
  23.3 0.7 slice.3
  24.0 3.6 %all-to-all-start.2 = ((bf16[8,64,256]{2,1,0:T(8,128)(2,1)}), bf16[8,64,256]{2,1,0:T(8,128)(2,1)S(1)}, u32[]{:S(2)}, u32[]{:S(2)}) async-start(bf16[8,64,256]{2,1,0:T(8,128)(2,1)} %bitcast.3), calls=%async_computation.2 | async-start | bytes 524288 | tf_op jit(solution)/shard_map/all_to_all | solution.py:38
  27.6 1.6 %shard_map.148 = (bf16[8,128,256]{2,1,0:T(8,128)(2,1)}, f32[320,256]{1,0:T(8,128)S(1)}, bf16[320,256]{1,0:T(8,128)(2,1)S(1)}) custom-call(bf16[512,320]{1,0:T(8,128)(2,1)S(1)} %get-tuple-element.24.hot_ref, bf16[512,512]{1,0:T(8,128)(2,1)S(1)} %get-tuple-element.25.act_ref, bf16[320,512]{1,0:T(8,128)(2,1)S(1)} %copy-done, bf16[320,512]{1,0:T(8,128)(2,1)S(1)} %copy-done.1, ...), custom_call_target="tpu_custom_call" | custom-call | tf_op jit(solution)/shard_map/pallas_call | solution.py:28
  29.2 6.9 %all-to-all-done.2 = bf16[8,64,256]{2,1,0:T(8,128)(2,1)S(1)} async-done(((bf16[8,64,256]{2,1,0:T(8,128)(2,1)}), bf16[8,64,256]{2,1,0:T(8,128)(2,1)S(1)}, u32[]{:S(2)}, u32[]{:S(2)}) %all-to-all-start.2) | async-done | bytes 262176 | tf_op jit(solution)/shard_map/all_to_all | solution.py:38
  36.1 0.0 copy-start.4
  36.1 0.0 copy-start.6
  36.1 3.7 %all-to-all-start.1 = ((bf16[8,128,256]{2,1,0:T(8,128)(2,1)}), bf16[8,128,256]{2,1,0:T(8,128)(2,1)S(1)}, u32[]{:S(2)}, u32[]{:S(2)}) async-start(bf16[8,128,256]{2,1,0:T(8,128)(2,1)} %get-tuple-element.26), calls=%async_computation.1 | async-start | bytes 1048576 | tf_op jit(solution)/shard_map/all_to_all | solution.py:38
  39.9 0.0 copy-done.4
  39.9 0.0 copy-done.6
  39.9 0.5 shard_map.149
  40.4 13.5 %all-to-all-done.1.first_ref = bf16[8,128,256]{2,1,0:T(8,128)(2,1)S(1)} async-done(((bf16[8,128,256]{2,1,0:T(8,128)(2,1)}), bf16[8,128,256]{2,1,0:T(8,128)(2,1)S(1)}, u32[]{:S(2)}, u32[]{:S(2)}) %all-to-all-start.1) | async-done | bytes 524320 | tf_op jit(solution)/shard_map/all_to_all | solution.py:38
  53.9 14.1 %all_to_all.25.second_ref = bf16[8,80,256]{2,1,0:T(8,128)(2,1)S(1)} all-to-all(bf16[8,80,256]{2,1,0:T(8,128)(2,1)S(1)} %get-tuple-element.28), channel_id=1, replica_groups=mesh['group'=2,'obs'=4,'node'=2,'mp'=2] {'obs','node'}, dimensions={0} | all-to-all | bytes 655360 | tf_op jit(solution)/shard_map/all_to_all | solution.py:38
  68.0 1.0 %shard_map.150 = (bf16[8,192,256]{2,1,0:T(8,128)(2,1)}, f32[6,256]{1,0:T(8,128)}) custom-call(bf16[8,128,256]{2,1,0:T(8,128)(2,1)S(1)} %all-to-all-done.1.first_ref, bf16[8,80,256]{2,1,0:T(8,128)(2,1)S(1)} %all_to_all.25.second_ref), custom_call_target="tpu_custom_call" | custom-call | tf_op jit(solution)/shard_map/pallas_call | solution.py:28
  69.0 3.5 %all-to-all-start.4 = ((bf16[8,192,256]{2,1,0:T(8,128)(2,1)}), bf16[8,192,256]{2,1,0:T(8,128)(2,1)S(1)}, u32[]{:S(2)}, u32[]{:S(2)}) async-start(bf16[8,192,256]{2,1,0:T(8,128)(2,1)} %get-tuple-element.29), calls=%async_computation.4 | async-start | bytes 1572864 | tf_op jit(solution)/shard_map/all_to_all | solution.py:38
  72.6 0.1 collective-permute-start
  72.7 0.5 collective-permute-start.1
  73.2 0.9 collective-permute-done.node_got_ref
  74.0 0.1 collective-permute-done.1.obs_got_ref
  74.1 17.7 %all-to-all-done.4.all_ref = bf16[8,192,256]{2,1,0:T(8,128)(2,1)S(1)} async-done(((bf16[8,192,256]{2,1,0:T(8,128)(2,1)}), bf16[8,192,256]{2,1,0:T(8,128)(2,1)S(1)}, u32[]{:S(2)}, u32[]{:S(2)}) %all-to-all-start.4) | async-done | bytes 786464 | tf_op jit(solution)/shard_map/all_to_all | solution.py:38
  91.8 1.3 %shard_map.151 = (bf16[128,256]{1,0:T(8,128)(2,1)}, f32[320,256]{1,0:T(8,128)}, f32[512,256]{1,0:T(8,128)}, f32[512,256]{1,0:T(8,128)}, f32[256,512]{1,0:T(8,128)}) custom-call(bf16[8,192,256]{2,1,0:T(8,128)(2,1)S(1)} %all-to-all-done.4.all_ref, f32[320,256]{1,0:T(8,128)S(1)} %get-tuple-element.30.node_keep_ref, ...), custom_call_target="tpu_custom_call" | custom-call | tf_op jit(solution)/shard_map/pallas_call | solution.py:28
Async XLA Ops:
  0.6 0.7 copy-start.11
  0.6 0.7 copy-start.9
  0.7 0.7 copy-start.10
  1.3 0.9 %copy-start.3 = (bf16[512,256]{1,0:T(8,128)(2,1)S(1)}, bf16[512,256]{1,0:T(8,128)(2,1)}, u32[]{:S(2)}) copy-start(bf16[512,256]{1,0:T(8,128)(2,1)} %w_ref.3) | copy-start | bytes 786436
  2.3 0.9 copy-start.5
  3.2 0.7 copy-start.8
  3.9 8.7 %copy-start.1 = (bf16[320,512]{1,0:T(8,128)(2,1)S(1)}, bf16[320,512]{1,0:T(8,128)(2,1)}, u32[]{:S(2)}) copy-start(bf16[320,512]{1,0:T(8,128)(2,1)} %agg_ref.3) | copy-start | bytes 983044
  5.3 7.4 %copy-start = (bf16[320,512]{1,0:T(8,128)(2,1)S(1)}, bf16[320,512]{1,0:T(8,128)(2,1)}, u32[]{:S(2)}) copy-start(bf16[320,512]{1,0:T(8,128)(2,1)} %state_ref.3) | copy-start | bytes 983044
  5.3 7.4 %copy-start.2 = (bf16[512,256]{1,0:T(8,128)(2,1)S(1)}, bf16[512,256]{1,0:T(8,128)(2,1)}, u32[]{:S(2)}) copy-start(bf16[512,256]{1,0:T(8,128)(2,1)} %w_node_ref.3) | copy-start | bytes 786436
  5.3 17.0 %all-to-all-start = ((bf16[8,144,128]{2,1,0:T(8,128)(2,1)}), bf16[8,144,128]{2,1,0:T(8,128)(2,1)S(1)}, u32[]{:S(2)}, u32[]{:S(2)}) async-start(bf16[8,144,128]{2,1,0:T(8,128)(2,1)} %get-tuple-element.23), calls=%async_computation | async-start | bytes 589824 | tf_op jit(solution)/shard_map/all_to_all | solution.py:38
  12.7 1.0 %copy-start.7 = (bf16[256,512]{1,0:T(8,128)(2,1)S(1)}, bf16[256,512]{1,0:T(8,128)(2,1)}, u32[]{:S(2)}) copy-start(bf16[256,512]{1,0:T(8,128)(2,1)} %w_out_ref.1) | copy-start | bytes 786436
  24.0 12.1 %all-to-all-start.2 = ((bf16[8,64,256]{2,1,0:T(8,128)(2,1)}), bf16[8,64,256]{2,1,0:T(8,128)(2,1)S(1)}, u32[]{:S(2)}, u32[]{:S(2)}) async-start(bf16[8,64,256]{2,1,0:T(8,128)(2,1)} %bitcast.3), calls=%async_computation.2 | async-start | bytes 524288 | tf_op jit(solution)/shard_map/all_to_all | solution.py:38
  36.1 3.7 %copy-start.4 = (bf16[512,256]{1,0:T(8,128)(2,1)S(1)}, bf16[512,256]{1,0:T(8,128)(2,1)}, u32[]{:S(2)}) copy-start(bf16[512,256]{1,0:T(8,128)(2,1)} %w_ref.3) | copy-start | bytes 786436
  36.1 3.7 %copy-start.6 = (bf16[128,512]{1,0:T(8,128)(2,1)S(1)}, bf16[128,512]{1,0:T(8,128)(2,1)}, u32[]{:S(2)}) copy-start(bf16[128,512]{1,0:T(8,128)(2,1)} %obs_ref.3) | copy-start | bytes 393220
  36.1 17.8 %all-to-all-start.1 = ((bf16[8,128,256]{2,1,0:T(8,128)(2,1)}), bf16[8,128,256]{2,1,0:T(8,128)(2,1)S(1)}, u32[]{:S(2)}, u32[]{:S(2)}) async-start(bf16[8,128,256]{2,1,0:T(8,128)(2,1)} %get-tuple-element.26), calls=%async_computation.1 | async-start | bytes 1048576 | tf_op jit(solution)/shard_map/all_to_all | solution.py:38
  69.0 22.8 %all-to-all-start.4 = ((bf16[8,192,256]{2,1,0:T(8,128)(2,1)}), bf16[8,192,256]{2,1,0:T(8,128)(2,1)S(1)}, u32[]{:S(2)}, u32[]{:S(2)}) async-start(bf16[8,192,256]{2,1,0:T(8,128)(2,1)} %get-tuple-element.29), calls=%async_computation.4 | async-start | bytes 1572864 | tf_op jit(solution)/shard_map/all_to_all | solution.py:38
  72.6 1.5 %collective-permute-start = (bf16[320,256]{1,0:T(8,128)(2,1)S(1)}, bf16[320,256]{1,0:T(8,128)(2,1)S(1)}, u32[]{:S(2)}, u32[]{:S(2)}) collective-permute-start(bf16[320,256]{1,0:T(8,128)(2,1)S(1)} %get-tuple-element.31), channel_id=1, source_target_pairs={{0,1},{1,0},{2,3},{3,2},{4,5},{5,4},{6,7},{7,6},{8,9},{9,8},{10,11... | collective-permute-start | bytes 491528 | tf_op jit(solution)/shard_map/ppermute | solution.py:42
  72.7 1.5 %collective-permute-start.1 = (bf16[128,256]{1,0:T(8,128)(2,1)S(1)}, bf16[128,256]{1,0:T(8,128)(2,1)S(1)}, u32[]{:S(2)}, u32[]{:S(2)}) collective-permute-start(bf16[128,256]{1,0:T(8,128)(2,1)S(1)} %get-tuple-element.33), channel_id=1, source_target_pairs={{0,1},{1,0},{2,3},{3,2},{4,5},{5,4},{6,7},{7,6},{8,9},{9,8},{10,11... | collective-permute-start | bytes 196616 | tf_op jit(solution)/shard_map/ppermute | solution.py:42

commit v2 on v1

v2 whole, which is shorter than its diff:
```python
import functools

import jax
import jax.numpy as jnp
from jax import lax
from jax.experimental import pallas as pl
from jax.experimental.pallas import tpu as pltpu
from jax.sharding import PartitionSpec as P

OWNER_AXES = ("obs", "node")
SUBLANES = 16
BF16 = jnp.bfloat16
F32 = jnp.float32


def dot(left, right, left_dim=1, right_dim=0):
    return lax.dot_general(
        left, right, (((left_dim,), (right_dim,)), ((), ())), preferred_element_type=F32
    )


def iota(shape, dim):
    return lax.broadcasted_iota(jnp.int32, shape, dim)


def call(kernel, outs, *args, scratch=(), in_hbm=False):
    vmem = pl.BlockSpec(memory_space=pltpu.VMEM)
    return pl.pallas_call(
        kernel,
        out_shape=[jax.ShapeDtypeStruct(shape, dtype) for shape, dtype in outs],
        in_specs=[pl.BlockSpec(memory_space=pl.ANY) if in_hbm else vmem] * len(args),
        out_specs=[vmem] * len(outs),
        scratch_shapes=list(scratch),
        compiler_params=pltpu.CompilerParams(vmem_limit_bytes=40 << 20),
    )(*args)


def shift(value, axis, step):
    size = lax.axis_size(axis)
    return lax.ppermute(value, axis, [(i, (i + step) % size) for i in range(size)])


def other_half(ref):
    half = ref.shape[0] // 2
    me = lax.axis_index("mp")
    mine = ref[pl.ds(pl.multiple_of(me * half, half), half), :]
    theirs = ref[pl.ds(pl.multiple_of((1 - me) * half, half), half), :]
    return mine, theirs


def slot_one_hot(slot_ref, slots):
    obs = slot_ref.shape[1]
    return (iota((slots, obs), 0) == slot_ref[...]).astype(F32)


def pack_kernel(cap, *refs):
    hbm, outs, local_refs, sems = refs[:6], refs[6:-7], refs[-7:-1], refs[-1]
    place_ref, outs = outs[0], outs[1:]
    copies = [
        pltpu.make_async_copy(src, dst, sems.at[i]) for i, (src, dst) in enumerate(zip(hbm, local_refs))
    ]
    for copy in copies:
        copy.start()
    for copy in copies:
        copy.wait()
    obs_ref, owner_ref, index_ref, slot_ref, w_ref, bias_ref = local_refs
    owners = len(outs)
    chunk, lanes = outs[0].shape
    fanout, obs = owner_ref.shape
    owner, index = owner_ref[...], index_ref[...]
    hits = [iota((owners, obs), 0) == owner[k : k + 1] for k in range(fanout)]
    count = functools.reduce(jnp.add, [h.astype(F32) for h in hits])
    before = dot(count, (iota((obs, obs), 0) < iota((obs, obs), 1)).astype(F32))
    header = jnp.zeros((SUBLANES, obs), F32)
    places = []
    for k in range(fanout):
        rank = jnp.sum(jnp.where(hits[k], before, 0.0), axis=0, keepdims=True)
        places.append(owner[k : k + 1] * cap + rank.astype(jnp.int32))
        place_ref[k : k + 1, :] = places[k]
        plus = index[k : k + 1] + 1
        fields = (owner[k : k + 1].astype(F32), rank, (plus // 16).astype(F32), (plus % 16).astype(F32))
        for j, row in enumerate(fields):
            header = jnp.where(iota(header.shape, 0) == 4 * k + j, row, header)
    bias = lax.dot_general(
        slot_one_hot(slot_ref, bias_ref.shape[0]),
        bias_ref[...],
        (((0,), (0,)), ((), ())),
        precision=lax.Precision.HIGHEST,
        preferred_element_type=F32,
    )
    part = (dot(obs_ref[...], w_ref[...]) + bias).astype(BF16)
    header = header.astype(BF16)
    me = lax.axis_index(OWNER_AXES)
    for j, out_ref in enumerate(outs):
        slots = iota((cap, obs), 0) + lax.rem(me + j, owners) * cap
        pick = functools.reduce(jnp.logical_or, [slots == place for place in places])
        packed = dot(pick.astype(BF16), part).astype(BF16)
        for c in range(part.shape[1] // lanes):
            out_ref[c * cap : (c + 1) * cap, :] = packed[:, c * lanes : (c + 1) * lanes]
        out_ref[chunk - SUBLANES :, :] = header


def table_kernel(state_ref, agg_ref, w_node_ref, w_out_ref, table_ref):
    hidden = w_node_ref.shape[1]
    parts = (dot(state_ref[...], w_node_ref[...]), dot(agg_ref[...], w_out_ref[...], 1, 1))
    for j, part in enumerate(parts):
        high = part.astype(BF16)
        table_ref[:, 2 * j * hidden : (2 * j + 1) * hidden] = high
        table_ref[:, (2 * j + 1) * hidden : (2 * j + 2) * hidden] = (
            part - high.astype(F32)
        ).astype(BF16)


def edge_kernel(owners, fanout, *refs):
    recv_refs, table_ref = refs[:owners], refs[owners]
    back_refs, act_ref, hot_ref = refs[owners + 1 : 2 * owners + 1], refs[-2], refs[-1]
    chunk, lanes = recv_refs[0].shape
    cap, hidden = back_refs[0].shape
    me = lax.axis_index(OWNER_AXES).astype(F32)
    columns = []
    parts = []
    for recv_ref in recv_refs:
        header = recv_ref[chunk - SUBLANES :, :].astype(F32)
        plus = jnp.zeros((cap, lanes), F32)
        for k in range(fanout):
            row = header[4 * k : 4 * k + 4]
            rank = jnp.where(row[0:1] == me, row[1:2], -1.0).astype(jnp.int32)
            plus = plus + jnp.where(iota((cap, lanes), 0) == rank, row[2:3] * 16.0 + row[3:4], 0.0)
        columns.append(jnp.sum(plus, axis=1, keepdims=True).astype(jnp.int32) - 1)
        parts.append(
            jnp.concatenate(
                [recv_ref[c * cap : (c + 1) * cap, :] for c in range(hidden // lanes)], axis=1
            ).astype(F32)
        )
    column = jnp.concatenate(columns, axis=0)
    hot = (column == iota(hot_ref.shape, 1)).astype(BF16)
    hot_ref[...] = hot
    rows = dot(hot, table_ref[...])
    pre = jnp.concatenate(parts, axis=0) + (rows[:, :hidden] + rows[:, hidden : 2 * hidden])
    g_z = rows[:, 2 * hidden : 3 * hidden] + rows[:, 3 * hidden :]
    sig = jax.nn.sigmoid(pre)
    g_a = (g_z * sig * (1.0 + pre * (1.0 - sig))).astype(BF16)
    act_ref[:, :hidden] = g_a
    act_ref[:, hidden:] = (pre * sig).astype(BF16)
    for j, back_ref in enumerate(back_refs):
        back_ref[...] = g_a[j * cap : (j + 1) * cap]


def split_x(total_ref, lines, tail, keep_ref, send_refs):
    shares = len(send_refs) + 1
    me = lax.axis_index("node")
    for j in range(shares):
        to = lax.rem(me + j, shares)
        out_ref = send_refs[j - 1] if j else keep_ref
        at = begin = 0
        for count in lines:
            part = count // shares
            rows = total_ref[pl.ds(pl.multiple_of(begin + to * part, SUBLANES), part), :]
            out_ref[at : at + part, :] = rows.astype(out_ref.dtype)
            at, begin = at + part, begin + count
        if tail:
            out_ref[at : at + tail, :] = total_ref[begin : begin + tail, :].astype(out_ref.dtype)


def node_kernel(
    lines, hot_ref, act_ref, state_ref, agg_ref, w_node_ref, mine_ref, theirs_ref, keep_ref, *refs
):
    send_refs, total_ref = refs[:-1], refs[-1]
    hidden = w_node_ref.shape[1]
    by_node = dot(hot_ref[...], act_ref[...], 0, 0).astype(BF16)
    node_hidden, z_sum = by_node[:, :hidden], by_node[:, hidden:]
    total_ref[: lines[0], :] = dot(state_ref[...], node_hidden, 0, 0)
    begin = lines[0]
    for c, count in enumerate(lines[1:]):
        total_ref[begin : begin + count, :] = dot(
            z_sum, agg_ref[:, c * hidden : (c + 1) * hidden], 0, 0
        )
        begin += count
    split_x(total_ref, lines, 0, keep_ref, send_refs)
    mine, theirs = other_half(w_node_ref)
    theirs_ref[...] = dot(node_hidden, theirs, 1, 1).astype(BF16)
    mine_ref[...] = dot(node_hidden, mine, 1, 1)


def obs_kernel(
    owners, lines, tail, place_ref, slot_ref, obs_ref, w_ref, *refs
):
    back_refs, mine_ref, theirs_ref, keep_ref = refs[:owners], refs[owners], refs[owners + 1], refs[owners + 2]
    send_refs, total_ref = refs[owners + 3 : -1], refs[-1]
    fanout, obs = place_ref.shape
    cap = back_refs[0].shape[0]
    me = lax.axis_index(OWNER_AXES)
    obs_hidden = None
    for j, back_ref in enumerate(back_refs):
        slots = iota((cap, obs), 0) + lax.rem(me + j, owners) * cap
        pick = functools.reduce(
            jnp.logical_or, [slots == place_ref[k : k + 1, :] for k in range(fanout)]
        )
        part = dot(pick.astype(BF16), back_ref[...], 0, 0)
        obs_hidden = part if obs_hidden is None else obs_hidden + part
    obs_hidden = obs_hidden.astype(BF16)
    total_ref[: lines[0], :] = dot(obs_ref[...], obs_hidden, 0, 0)
    total_ref[lines[0] :, :] = dot(slot_one_hot(slot_ref, tail).astype(BF16), obs_hidden)
    split_x(total_ref, lines, tail, keep_ref, send_refs)
    mine, theirs = other_half(w_ref)
    theirs_ref[...] = dot(obs_hidden, theirs, 1, 1).astype(BF16)
    mine_ref[...] = dot(obs_hidden, mine, 1, 1)


def piece_rows(part, shares):
    return max(SUBLANES, part // shares)


def sum_x_kernel(parts, tail, others, *refs):
    keep_ref, recv_refs = refs[0], refs[1 : others + 1]
    out_ref, send_refs, total_ref = refs[others + 1], refs[others + 2 : -1], refs[-1]
    shares = len(send_refs) + 1
    total = keep_ref[...]
    for recv_ref in recv_refs:
        total = total + recv_ref[...].astype(F32)
    total_ref[...] = total
    me = lax.axis_index("obs")
    for j in range(shares):
        to = lax.rem(me + j, shares)
        ref = send_refs[j - 1] if j else out_ref
        at = begin = 0
        for part in parts:
            piece = piece_rows(part, shares)
            begin_at = begin + jnp.minimum(to, part // piece - 1) * piece
            rows = total_ref[pl.ds(pl.multiple_of(begin_at, SUBLANES), piece), :]
            ref[at : at + piece, :] = rows.astype(ref.dtype)
            at, begin = at + piece, begin + part
        if tail:
            ref[at : at + tail, :] = total_ref[begin : begin + tail, :].astype(ref.dtype)


def sum_z_kernel(others, *refs):
    total = refs[0][...]
    for recv_ref in refs[1 : others + 1]:
        total = total + recv_ref[...].astype(F32)
    out_ref = refs[others + 1]
    rows = out_ref.shape[0]
    out_ref[...] = total[:rows].astype(BF16)
    if len(refs) > others + 2:
        slot_ref = refs[others + 2]
        slot_ref[...] = total[rows : rows + slot_ref.shape[0]]


def spread_kernel(x_shares, z_shares, targets, *refs):
    blocks, out_refs = refs[: x_shares * z_shares], refs[x_shares * z_shares :]
    me_x, me_z = lax.axis_index("node"), lax.axis_index("obs")
    for i, block_ref in enumerate(blocks):
        from_x = lax.rem(me_x - i // z_shares + x_shares, x_shares)
        from_z = lax.rem(me_z - i % z_shares + z_shares, z_shares)
        hidden = block_ref.shape[1]
        at = 0
        for out, count, column in targets:
            part = count // x_shares
            piece = piece_rows(part, z_shares)
            out_ref = out_refs[out]

            def write(out_ref=out_ref, part=part, piece=piece, column=column, at=at, block_ref=block_ref):
                begin = pl.multiple_of(from_x * part + from_z * piece, SUBLANES)
                out_ref[pl.ds(begin, piece), column : column + hidden] = block_ref[
                    at : at + piece, :
                ].astype(F32)

            if part // piece == z_shares:
                write()
            else:
                pl.when(from_z < part // piece)(write)
            at += piece


def merge_kernel(node_ref, node_got_ref, obs_ref, obs_got_ref, grad_node_ref, grad_obs_ref):
    grad_node_ref[...] = node_ref[...] + node_got_ref[...].astype(F32)
    grad_obs_ref[...] = (obs_ref[...] + obs_got_ref[...].astype(F32)).astype(BF16)


def reduce_shares(lines, tail, slots, keep, sends):
    x_shares, z_shares = lax.axis_size("node"), lax.axis_size("obs")
    hidden = keep.shape[1]
    parts = [count // x_shares for count in lines]
    rows = sum(piece_rows(part, z_shares) for part in parts)
    got = [shift(send, "node", j + 1) for j, send in enumerate(sends)]
    keep, *sends = call(
        functools.partial(sum_x_kernel, parts, tail, len(got)),
        [((rows + tail, hidden), F32)] + [((rows + tail, hidden), BF16)] * (z_shares - 1),
        keep, *got,
        scratch=[pltpu.VMEM(keep.shape, F32)],
    )
    got = [shift(send, "obs", j + 1) for j, send in enumerate(sends)]
    return call(
        functools.partial(sum_z_kernel, len(got)),
        [((rows, hidden), BF16)] + ([((slots, hidden), F32)] if tail else []),
        keep, *got,
    )


def gather_pieces(piece):
    x_shares, z_shares = lax.axis_size("node"), lax.axis_size("obs")
    along_z = [piece] + [shift(piece, "obs", j) for j in range(1, z_shares)]
    blocks = list(along_z)
    for j in range(1, x_shares):
        blocks += [shift(block, "node", j) for block in along_z]
    return blocks


def local(obs_feat, node_state, grad_agg, owner, local_idx, slot, w_obs, w_node, slot_bias, w_out):
    owners = lax.axis_size(OWNER_AXES)
    x_shares, z_shares = lax.axis_size("node"), lax.axis_size("obs")
    obs, fanout = owner.shape
    nodes, width = node_state.shape
    hidden = w_obs.shape[1]
    slots = slot_bias.shape[0]
    cap = max(2, 2 * obs * fanout // owners)
    cap = -(-cap // SUBLANES) * SUBLANES
    edges = owners * cap
    half = width // 2
    slot_row = slot.reshape(1, obs)

    chunk = cap * hidden // obs + SUBLANES
    inputs = (obs_feat, owner.T, local_idx.T, slot_row, w_obs, slot_bias)
    place, *packed = call(
        functools.partial(pack_kernel, cap),
        [((fanout, obs), jnp.int32)] + [((chunk, obs), BF16)] * owners,
        *inputs,
        scratch=[pltpu.VMEM(a.shape, a.dtype) for a in inputs] + [pltpu.SemaphoreType.DMA((len(inputs),))],
        in_hbm=True,
    )
    received = packed[:1] + [shift(packed[j], OWNER_AXES, j) for j in range(1, owners)]
    (table,) = call(
        table_kernel, [((nodes, 4 * hidden), BF16)], node_state, grad_agg, w_node, w_out
    )
    *back, act, hot = call(
        functools.partial(edge_kernel, owners, fanout),
        [((cap, hidden), BF16)] * owners + [((edges, 2 * hidden), BF16), ((edges, nodes), BF16)],
        *received, table,
    )
    back = back[:1] + [shift(back[j], OWNER_AXES, -j) for j in range(1, owners)]

    node_lines = [width] + [hidden] * (width // hidden)
    share = sum(node_lines) // x_shares
    node_mine, node_theirs, keep, *sends = call(
        functools.partial(node_kernel, node_lines),
        [((nodes, half), F32), ((nodes, half), BF16), ((share, hidden), F32)]
        + [((share, hidden), BF16)] * (x_shares - 1),
        hot, act, node_state, grad_agg, w_node,
        scratch=[pltpu.VMEM((sum(node_lines), hidden), F32)],
    )
    (node_piece,) = reduce_shares(node_lines, 0, 0, keep, sends)
    node_got = shift(node_theirs, "mp", 1)

    tail = -(-slots // SUBLANES) * SUBLANES
    share = width // x_shares + tail
    obs_mine, obs_theirs, keep, *sends = call(
        functools.partial(obs_kernel, owners, [width], tail),
        [((obs, half), F32), ((obs, half), BF16), ((share, hidden), F32)]
        + [((share, hidden), BF16)] * (x_shares - 1),
        place, slot_row, obs_feat, w_obs, *back,
        scratch=[pltpu.VMEM((width + tail, hidden), F32)],
    )
    obs_piece, grad_slot = reduce_shares([width], tail, slots, keep, sends)
    obs_got = shift(obs_theirs, "mp", 1)

    node_blocks = gather_pieces(node_piece)
    obs_blocks = gather_pieces(obs_piece)
    grad_node, grad_obs = call(
        merge_kernel, [((nodes, half), F32), ((obs, half), BF16)],
        node_mine, node_got, obs_mine, obs_got,
    )
    node_targets = [(0, width, 0)] + [(1, hidden, c * hidden) for c in range(width // hidden)]
    grad_w_node, grad_w_out = call(
        functools.partial(spread_kernel, x_shares, z_shares, node_targets),
        [((width, hidden), F32), ((hidden, width), F32)],
        *node_blocks,
    )
    (grad_w_obs,) = call(
        functools.partial(spread_kernel, x_shares, z_shares, [(0, width, 0)]),
        [((width, hidden), F32)],
        *obs_blocks,
    )
    return grad_obs, grad_node, grad_w_obs, grad_w_node, grad_w_out, grad_slot


def solution(mesh):
    rows = P(("group", "obs", "node"), None)
    return jax.shard_map(
        local,
        mesh=mesh,
        in_specs=(
            rows, rows, rows, rows, rows,
            P(("group", "obs", "node")),
            P(None, "mp"), P(None, "mp"), P(None, "mp"), P("mp", None),
        ),
        out_specs=(
            P(("group", "obs", "node"), "mp"),
            P(("group", "obs", "node"), "mp"),
            P("group", "mp"),
            P("group", "mp"),
            P(("group", "mp"), None),
            P("group", "mp"),
        ),
        check_vma=False,
    )
```

time: 93.8 us -> 82.8 us (0.88)
  waiting for transfers between devices: 47.4 us -> 18.3 us
  starting transfers between devices: 18.8 us -> 47.6 us
  blocking collectives: 14.1 us -> 0 us
  local copies, waits for them, and re-layouts: 4.92 us -> 8.15 us
    ppermute x2 -> x38, starting transfers between devices: 0.57 us -> 47.6 us  [shift(): lax.ppermute(value, axis, [(i, (i + step) % size) for i in range(size)])]
    all_to_all x4 -> x0, waiting for transfers between devices: 46.4 us -> none  [exchange(): lax.all_to_all(blocks, OWNER_AXES, split_axis=0, concat_axis=0, tiled=True)]
    all_to_all x4 -> x0, starting transfers between devices: 18.2 us -> none  [exchange(): lax.all_to_all(blocks, OWNER_AXES, split_axis=0, concat_axis=0, tiled=True)]
    ppermute x2 -> x38, waiting for transfers between devices: 0.98 us -> 18.3 us  [shift(): lax.ppermute(value, axis, [(i, (i + step) % size) for i in range(size)])]
    all_to_all x1 -> x0, blocking collectives: 14.1 us -> none  [exchange(): lax.all_to_all(blocks, OWNER_AXES, split_axis=0, concat_axis=0, tiled=True)]
    unnamed x24 -> x30, local copies, waits for them, and re-layouts: 4.2 us -> 8.15 us
    pallas_call x7 -> x12, Pallas kernels: 7.19 us -> 7.5 us  [call(): pl.pallas_call(kernel, out_shape=[jax.ShapeDtypeStruct(shape, dtype) for...]
  transfers between devices with their start and end apart: 6 -> 38, of which waited for: 6 -> 11; matrix products, arithmetic and copies ran while one was open for 0% -> 0% of each run, Pallas kernels for 3% -> 4%
where the time goes in v2:
time: 82.8 us; the launch traced here: 82.5 us
  starting transfers between devices  47.6 us (57%)
  waiting for transfers between devices  18.3 us (22%)
  local copies, waits for them, and re-layouts  8.15 us (10%)
  Pallas kernels  7.5 us (9%)
  between operations  0.88 us (1%)
    ppermute x38, starting transfers between devices, shift(): lax.ppermute(value, axis, [(i, (i + step) % size) for i in range(size)])  47.6 us
    ppermute x38, waiting for transfers between devices, shift(): lax.ppermute(value, axis, [(i, (i + step) % size) for i in range(size)])  18.3 us
    unnamed x30, local copies, waits for them, and re-layouts  8.15 us
    pallas_call x12, Pallas kernels, call(): pl.pallas_call(kernel, out_shape=[jax.ShapeDtypeStruct(shape, dtype) for...  7.5 us
  transfers between devices with their start and end apart: 38, of which 11 were waited for; matrix products, arithmetic and copies ran while one was open for 0% of the time, Pallas kernels for 4%

profile of v2, /device:TPU:0, one launch (start us, length us, event | category | flops | bytes accessed | tf_op | source)
XLA Modules:
  0.0 82.5 jit_solution(7243516739035626836)
XLA Ops:
  0.7 1.0 %copy-done.5 = bf16[512,256]{1,0:T(8,128)(2,1)S(1)} copy-done((bf16[512,256]{1,0:T(8,128)(2,1)S(1)}, bf16[512,256]{1,0:T(8,128)(2,1)}, u32[]{:S(2)}) %copy-start.5) | copy-done | bytes 262168
  1.6 0.9 %copy-done.7 = bf16[128,512]{1,0:T(8,128)(2,1)S(1)} copy-done((bf16[128,512]{1,0:T(8,128)(2,1)S(1)}, bf16[128,512]{1,0:T(8,128)(2,1)}, u32[]{:S(2)}) %copy-start.7) | copy-done | bytes 131096
  2.5 0.7 copy-done.10
  3.2 0.7 copy-done.11
  3.9 0.7 copy-done.13
  4.6 0.7 copy-done.14
  5.3 0.9 %shard_map.145 = (s32[2,128]{1,0:T(2,128)S(1)}, bf16[144,128]{1,0:T(8,128)(2,1)S(1)}, bf16[144,128]{1,0:T(8,128)(2,1)S(1)}, bf16[144,128]{1,0:T(8,128)(2,1)S(1)}...) custom-call(bf16[128,512]{1,0:T(8,128)(2,1)S(1)} %copy-done.7, ...), custom_call_target="tpu_custom_call" | custom-call | tf_op jit(solution)/shard_map/pallas_call | solution.py:28
  6.1 3.0 %collective-permute-start = (bf16[144,128]{1,0:T(8,128)(2,1)S(1)}, bf16[144,128]{1,0:T(8,128)(2,1)S(1)}, u32[]{:S(2)}, u32[]{:S(2)}) collective-permute-start(bf16[144,128]{1,0:T(8,128)(2,1)S(1)} %get-tuple-element.48), channel_id=1, source_target_pairs={{0,2},{2,4},{4,6},{6,8},{8,10},{10,12},{12,14},{14,0},{1,3},{3,5},... | collective-permute-start | bytes 110600 | tf_op jit(solution)/shard_map/ppermute | solution.py:40
  9.1 1.6 %collective-permute-start.1 = (bf16[144,128]{1,0:T(8,128)(2,1)S(1)}, bf16[144,128]{1,0:T(8,128)(2,1)S(1)}, u32[]{:S(2)}, u32[]{:S(2)}) collective-permute-start(bf16[144,128]{1,0:T(8,128)(2,1)S(1)} %get-tuple-element.49), channel_id=1, source_target_pairs={{0,4},{2,6},{4,8},{6,10},{8,12},{10,14},{12,0},{14,2},{1,5},{3,7},... | collective-permute-start | bytes 110600 | tf_op jit(solution)/shard_map/ppermute | solution.py:40
  10.7 2.6 %collective-permute-start.2 = (bf16[144,128]{1,0:T(8,128)(2,1)S(1)}, bf16[144,128]{1,0:T(8,128)(2,1)S(1)}, u32[]{:S(2)}, u32[]{:S(2)}) collective-permute-start(bf16[144,128]{1,0:T(8,128)(2,1)S(1)} %get-tuple-element.50), channel_id=1, source_target_pairs={{0,6},{2,8},{4,10},{6,12},{8,14},{10,0},{12,2},{14,4},{1,7},{3,9},... | collective-permute-start | bytes 110600 | tf_op jit(solution)/shard_map/ppermute | solution.py:40
  13.3 1.2 %collective-permute-start.3 = (bf16[144,128]{1,0:T(8,128)(2,1)S(1)}, bf16[144,128]{1,0:T(8,128)(2,1)S(1)}, u32[]{:S(2)}, u32[]{:S(2)}) collective-permute-start(bf16[144,128]{1,0:T(8,128)(2,1)S(1)} %get-tuple-element.51), channel_id=1, source_target_pairs={{0,8},{2,10},{4,12},{6,14},{8,0},{10,2},{12,4},{14,6},{1,9},{3,11}... | collective-permute-start | bytes 110600 | tf_op jit(solution)/shard_map/ppermute | solution.py:40
  14.5 2.6 %collective-permute-start.4 = (bf16[144,128]{1,0:T(8,128)(2,1)S(1)}, bf16[144,128]{1,0:T(8,128)(2,1)S(1)}, u32[]{:S(2)}, u32[]{:S(2)}) collective-permute-start(bf16[144,128]{1,0:T(8,128)(2,1)S(1)} %get-tuple-element.52), channel_id=1, source_target_pairs={{0,10},{2,12},{4,14},{6,0},{8,2},{10,4},{12,6},{14,8},{1,11},{3,13... | collective-permute-start | bytes 110600 | tf_op jit(solution)/shard_map/ppermute | solution.py:40
  17.1 1.3 %collective-permute-start.5 = (bf16[144,128]{1,0:T(8,128)(2,1)S(1)}, bf16[144,128]{1,0:T(8,128)(2,1)S(1)}, u32[]{:S(2)}, u32[]{:S(2)}) collective-permute-start(bf16[144,128]{1,0:T(8,128)(2,1)S(1)} %get-tuple-element.53), channel_id=1, source_target_pairs={{0,12},{2,14},{4,0},{6,2},{8,4},{10,6},{12,8},{14,10},{1,13},{3,15... | collective-permute-start | bytes 110600 | tf_op jit(solution)/shard_map/ppermute | solution.py:40
  18.5 1.4 %collective-permute-start.6 = (bf16[144,128]{1,0:T(8,128)(2,1)S(1)}, bf16[144,128]{1,0:T(8,128)(2,1)S(1)}, u32[]{:S(2)}, u32[]{:S(2)}) collective-permute-start(bf16[144,128]{1,0:T(8,128)(2,1)S(1)} %get-tuple-element.54), channel_id=1, source_target_pairs={{0,14},{2,0},{4,2},{6,4},{8,6},{10,8},{12,10},{14,12},{1,15},{3,1}... | collective-permute-start | bytes 110600 | tf_op jit(solution)/shard_map/ppermute | solution.py:40
  19.9 1.0 %copy-done.1 = bf16[320,512]{1,0:T(8,128)(2,1)S(1)} copy-done((bf16[320,512]{1,0:T(8,128)(2,1)S(1)}, bf16[320,512]{1,0:T(8,128)(2,1)}, u32[]{:S(2)}) %copy-start.1) | copy-done | bytes 327704
  20.9 0.9 %copy-done.3 = bf16[512,256]{1,0:T(8,128)(2,1)S(1)} copy-done((bf16[512,256]{1,0:T(8,128)(2,1)S(1)}, bf16[512,256]{1,0:T(8,128)(2,1)}, u32[]{:S(2)}) %copy-start.3) | copy-done | bytes 262168
  21.8 0.9 %copy-done.9 = bf16[256,512]{1,0:T(8,128)(2,1)S(1)} copy-done((bf16[256,512]{1,0:T(8,128)(2,1)S(1)}, bf16[256,512]{1,0:T(8,128)(2,1)}, u32[]{:S(2)}) %copy-start.9) | copy-done | bytes 262168
  23.2 1.0 %shard_map.147 = (bf16[64,256]{1,0:T(8,128)(2,1)S(1)}, bf16[64,256]{1,0:T(8,128)(2,1)S(1)}, bf16[64,256]{1,0:T(8,128)(2,1)S(1)}, bf16[64,256]{1,0:T(8,128)(2,1)S...) custom-call(bf16[144,128]{1,0:T(8,128)(2,1)S(1)} %get-tuple-element., ...), custom_call_target="tpu_custom_call" | custom-call | tf_op jit(solution)/shard_map/pallas_call | solution.py:28
  24.3 1.0 %shard_map.148 = (f32[320,256]{1,0:T(8,128)S(1)}, bf16[320,256]{1,0:T(8,128)(2,1)S(1)}, f32[512,256]{1,0:T(8,128)S(1)}, bf16[512,256]{1,0:T(8,128)(2,1)S(1)}) custom-call(bf16[512,320]{1,0:T(8,128)(2,1)S(1)} %get-tuple-element.55.hot_ref, bf16[512,512]{1,0:T(8,128)(2,1)S(1)} %get-tuple-element.56.act_ref, bf16[320,512]{1,0:T(8,128)(2,1)S(1)} %copy-done, ...), custom_call_target="tpu_custom_call" | custom-call | tf_op jit(solution)/shard_map/pallas_call | solution.py:28
  25.3 0.8 %collective-permute-start.27 = (bf16[512,256]{1,0:T(8,128)(2,1)S(1)}, bf16[512,256]{1,0:T(8,128)(2,1)S(1)}, u32[]{:S(2)}, u32[]{:S(2)}) collective-permute-start(bf16[512,256]{1,0:T(8,128)(2,1)S(1)} %get-tuple-element.80), channel_id=1, source_target_pairs={{0,2},{2,0},{1,3},{3,1},{4,6},{6,4},{5,7},{7,5},{8,10},{10,8},{9,1... | collective-permute-start | bytes 786440 | tf_op jit(solution)/shard_map/ppermute | solution.py:40
  26.1 2.6 %collective-permute-start.8 = (bf16[64,256]{1,0:T(8,128)(2,1)S(1)}, bf16[64,256]{1,0:T(8,128)(2,1)S(1)}, u32[]{:S(2)}, u32[]{:S(2)}) collective-permute-start(bf16[64,256]{1,0:T(8,128)(2,1)S(1)} %get-tuple-element.61), channel_id=1, source_target_pairs={{0,14},{2,0},{4,2},{6,4},{8,6},{10,8},{12,10},{14,12},{1,15},{3,1}... | collective-permute-start | bytes 98312 | tf_op jit(solution)/shard_map/ppermute | solution.py:40
  29.6 4.1 %collective-permute-start.11 = (bf16[64,256]{1,0:T(8,128)(2,1)S(1)}, bf16[64,256]{1,0:T(8,128)(2,1)S(1)}, u32[]{:S(2)}, u32[]{:S(2)}) collective-permute-start(bf16[64,256]{1,0:T(8,128)(2,1)S(1)} %get-tuple-element.64), channel_id=1, source_target_pairs={{0,8},{2,10},{4,12},{6,14},{8,0},{10,2},{12,4},{14,6},{1,9},{3,11}... | collective-permute-start | bytes 98312 | tf_op jit(solution)/shard_map/ppermute | solution.py:40
  33.7 1.1 %collective-permute-start.13 = (bf16[64,256]{1,0:T(8,128)(2,1)S(1)}, bf16[64,256]{1,0:T(8,128)(2,1)S(1)}, u32[]{:S(2)}, u32[]{:S(2)}) collective-permute-start(bf16[64,256]{1,0:T(8,128)(2,1)S(1)} %get-tuple-element.66), channel_id=1, source_target_pairs={{0,4},{2,6},{4,8},{6,10},{8,12},{10,14},{12,0},{14,2},{1,5},{3,7},... | collective-permute-start | bytes 98312 | tf_op jit(solution)/shard_map/ppermute | solution.py:40
  34.8 2.5 %collective-permute-start.14 = (bf16[64,256]{1,0:T(8,128)(2,1)S(1)}, bf16[64,256]{1,0:T(8,128)(2,1)S(1)}, u32[]{:S(2)}, u32[]{:S(2)}) collective-permute-start(bf16[64,256]{1,0:T(8,128)(2,1)S(1)} %get-tuple-element.67), channel_id=1, source_target_pairs={{0,2},{2,4},{4,6},{6,8},{8,10},{10,12},{12,14},{14,0},{1,3},{3,5},... | collective-permute-start | bytes 98312 | tf_op jit(solution)/shard_map/ppermute | solution.py:40
  37.4 2.0 %collective-permute-done.12.refs_5_ = bf16[64,256]{1,0:T(8,128)(2,1)S(1)} collective-permute-done((bf16[64,256]{1,0:T(8,128)(2,1)S(1)}, bf16[64,256]{1,0:T(8,128)(2,1)S(1)}, u32[]{:S(2)}, u32[]{:S(2)}) %collective-permute-start.12) | collective-permute-done | bytes 32800 | tf_op jit(solution)/shard_map/ppermute | solution.py:40
  39.4 2.1 %collective-permute-done.14.refs_7_ = bf16[64,256]{1,0:T(8,128)(2,1)S(1)} collective-permute-done((bf16[64,256]{1,0:T(8,128)(2,1)S(1)}, bf16[64,256]{1,0:T(8,128)(2,1)S(1)}, u32[]{:S(2)}, u32[]{:S(2)}) %collective-permute-start.14) | collective-permute-done | bytes 32800 | tf_op jit(solution)/shard_map/ppermute | solution.py:40
  42.2 0.8 shard_map.149
  43.2 5.0 %collective-permute-done.16.refs_1_ = bf16[272,256]{1,0:T(8,128)(2,1)S(1)} collective-permute-done((bf16[272,256]{1,0:T(8,128)(2,1)S(1)}, bf16[272,256]{1,0:T(8,128)(2,1)S(1)}, u32[]{:S(2)}, u32[]{:S(2)}) %collective-permute-start.16) | collective-permute-done | bytes 139296 | tf_op jit(solution)/shard_map/ppermute | solution.py:40
  48.5 1.3 %collective-permute-start.18 = (bf16[80,256]{1,0:T(8,128)(2,1)S(1)}, bf16[80,256]{1,0:T(8,128)(2,1)S(1)}, u32[]{:S(2)}, u32[]{:S(2)}) collective-permute-start(bf16[80,256]{1,0:T(8,128)(2,1)S(1)} %get-tuple-element.76), channel_id=1, source_target_pairs={{0,8},{4,12},{8,0},{12,4},{1,9},{5,13},{9,1},{13,5},{2,10},{6,14},... | collective-permute-start | bytes 122888 | tf_op jit(solution)/shard_map/ppermute | solution.py:40
  49.7 2.4 %collective-permute-start.19 = (bf16[80,256]{1,0:T(8,128)(2,1)S(1)}, bf16[80,256]{1,0:T(8,128)(2,1)S(1)}, u32[]{:S(2)}, u32[]{:S(2)}) collective-permute-start(bf16[80,256]{1,0:T(8,128)(2,1)S(1)} %get-tuple-element.77), channel_id=1, source_target_pairs={{0,12},{4,0},{8,4},{12,8},{1,13},{5,1},{9,5},{13,9},{2,14},{6,2},{... | collective-permute-start | bytes 122888 | tf_op jit(solution)/shard_map/ppermute | solution.py:40
  52.8 1.6 %collective-permute-done.17.refs_1_ = bf16[80,256]{1,0:T(8,128)(2,1)S(1)} collective-permute-done((bf16[80,256]{1,0:T(8,128)(2,1)S(1)}, bf16[80,256]{1,0:T(8,128)(2,1)S(1)}, u32[]{:S(2)}, u32[]{:S(2)}) %collective-permute-start.17) | collective-permute-done | bytes 40992 | tf_op jit(solution)/shard_map/ppermute | solution.py:40
  54.8 2.3 %collective-permute-start.30 = (bf16[128,256]{1,0:T(8,128)(2,1)S(1)}, bf16[128,256]{1,0:T(8,128)(2,1)S(1)}, u32[]{:S(2)}, u32[]{:S(2)}) collective-permute-start(bf16[128,256]{1,0:T(8,128)(2,1)S(1)} %get-tuple-element.84), channel_id=1, source_target_pairs={{0,12},{4,0},{8,4},{12,8},{1,13},{5,1},{9,5},{13,9},{2,14},{6,2},{... | collective-permute-start | bytes 196616 | tf_op jit(solution)/shard_map/ppermute | solution.py:40
  58.3 1.8 %collective-permute-done.29.refs_2_ = bf16[128,256]{1,0:T(8,128)(2,1)S(1)} collective-permute-done((bf16[128,256]{1,0:T(8,128)(2,1)S(1)}, bf16[128,256]{1,0:T(8,128)(2,1)S(1)}, u32[]{:S(2)}, u32[]{:S(2)}) %collective-permute-start.29) | collective-permute-done | bytes 65568 | tf_op jit(solution)/shard_map/ppermute | solution.py:40
  60.1 3.5 %collective-permute-start.22 = (bf16[64,256]{1,0:T(8,128)(2,1)S(1)}, bf16[64,256]{1,0:T(8,128)(2,1)S(1)}, u32[]{:S(2)}, u32[]{:S(2)}) collective-permute-start(bf16[64,256]{1,0:T(8,128)(2,1)S(1)} %get-tuple-element.78.refs_0_), channel_id=1, source_target_pairs={{0,12},{4,0},{8,4},{12,8},{1,13},{5,1},{9,5},{13,9},{2,14},{6,2},{... | collective-permute-start | bytes 98312 | tf_op jit(solution)/shard_map/ppermute | solution.py:40
  63.7 1.5 %collective-permute-start.32 = (bf16[128,256]{1,0:T(8,128)(2,1)S(1)}, bf16[128,256]{1,0:T(8,128)(2,1)S(1)}, u32[]{:S(2)}, u32[]{:S(2)}) collective-permute-start(bf16[128,256]{1,0:T(8,128)(2,1)S(1)} %shard_map.155.refs_0_), channel_id=1, source_target_pairs={{0,8},{4,12},{8,0},{12,4},{1,9},{5,13},{9,1},{13,5},{2,10},{6,14},... | collective-permute-start | bytes 196616 | tf_op jit(solution)/shard_map/ppermute | solution.py:40
  65.2 2.4 %collective-permute-start.33 = (bf16[128,256]{1,0:T(8,128)(2,1)S(1)}, bf16[128,256]{1,0:T(8,128)(2,1)S(1)}, u32[]{:S(2)}, u32[]{:S(2)}) collective-permute-start(bf16[128,256]{1,0:T(8,128)(2,1)S(1)} %shard_map.155.refs_0_), channel_id=1, source_target_pairs={{0,12},{4,0},{8,4},{12,8},{1,13},{5,1},{9,5},{13,9},{2,14},{6,2},{... | collective-permute-start | bytes 196616 | tf_op jit(solution)/shard_map/ppermute | solution.py:40
  67.6 2.0 %collective-permute-start.24 = (bf16[64,256]{1,0:T(8,128)(2,1)S(1)}, bf16[64,256]{1,0:T(8,128)(2,1)S(1)}, u32[]{:S(2)}, u32[]{:S(2)}) collective-permute-start(bf16[64,256]{1,0:T(8,128)(2,1)S(1)} %collective-permute-done.20.refs_1_), channel_id=1, source_target_pairs={{0,2},{2,0},{1,3},{3,1},{4,6},{6,4},{5,7},{7,5},{8,10},{10,8},{9,1... | collective-permute-start | bytes 98312 | tf_op jit(solution)/shard_map/ppermute | solution.py:40
  69.6 2.2 %collective-permute-done.23.refs_4_ = bf16[64,256]{1,0:T(8,128)(2,1)S(1)} collective-permute-done((bf16[64,256]{1,0:T(8,128)(2,1)S(1)}, bf16[64,256]{1,0:T(8,128)(2,1)S(1)}, u32[]{:S(2)}, u32[]{:S(2)}) %collective-permute-start.23) | collective-permute-done | bytes 32800 | tf_op jit(solution)/shard_map/ppermute | solution.py:40
  71.8 0.7 collective-permute-done.24.refs_5_
  72.5 1.4 %collective-permute-start.34 = (bf16[128,256]{1,0:T(8,128)(2,1)S(1)}, bf16[128,256]{1,0:T(8,128)(2,1)S(1)}, u32[]{:S(2)}, u32[]{:S(2)}) collective-permute-start(bf16[128,256]{1,0:T(8,128)(2,1)S(1)} %shard_map.155.refs_0_), channel_id=1, source_target_pairs={{0,2},{2,0},{1,3},{3,1},{4,6},{6,4},{5,7},{7,5},{8,10},{10,8},{9,1... | collective-permute-start | bytes 196616 | tf_op jit(solution)/shard_map/ppermute | solution.py:40
  73.9 0.7 collective-permute-start.35
  74.6 1.4 %collective-permute-start.36 = (bf16[128,256]{1,0:T(8,128)(2,1)S(1)}, bf16[128,256]{1,0:T(8,128)(2,1)S(1)}, u32[]{:S(2)}, u32[]{:S(2)}) collective-permute-start(bf16[128,256]{1,0:T(8,128)(2,1)S(1)} %collective-permute-done.32.refs_2_), channel_id=1, source_target_pairs={{0,2},{2,0},{1,3},{3,1},{4,6},{6,4},{5,7},{7,5},{8,10},{10,8},{9,1... | collective-permute-start | bytes 196616 | tf_op jit(solution)/shard_map/ppermute | solution.py:40
  75.9 0.7 collective-permute-start.37
  76.6 1.4 %collective-permute-start.26 = (bf16[64,256]{1,0:T(8,128)(2,1)S(1)}, bf16[64,256]{1,0:T(8,128)(2,1)S(1)}, u32[]{:S(2)}, u32[]{:S(2)}) collective-permute-start(bf16[64,256]{1,0:T(8,128)(2,1)S(1)} %collective-permute-done.22.refs_3_), channel_id=1, source_target_pairs={{0,2},{2,0},{1,3},{3,1},{4,6},{6,4},{5,7},{7,5},{8,10},{10,8},{9,1... | collective-permute-start | bytes 98312 | tf_op jit(solution)/shard_map/ppermute | solution.py:40
  78.0 0.8 shard_map.150
  78.7 1.8 %collective-permute-done.26.refs_7_ = bf16[64,256]{1,0:T(8,128)(2,1)S(1)} collective-permute-done((bf16[64,256]{1,0:T(8,128)(2,1)S(1)}, bf16[64,256]{1,0:T(8,128)(2,1)S(1)}, u32[]{:S(2)}, u32[]{:S(2)}) %collective-permute-start.26) | collective-permute-done | bytes 32800 | tf_op jit(solution)/shard_map/ppermute | solution.py:40
  80.5 0.8 %shard_map.153 = f32[512,256]{1,0:T(8,128)} custom-call(bf16[64,256]{1,0:T(8,128)(2,1)S(1)} %get-tuple-element.78.refs_0_, bf16[64,256]{1,0:T(8,128)(2,1)S(1)} %collective-permute-done.20.refs_1_, bf16[64,256]{1,0:T(8,128)(2,1)S(1)} %collective-permute-done.21.refs_2_, bf16[64,256]{1,0:T(8,128)(2,1)S(1)} %collective-permute-done.22.refs_3_, ...), custom_call_target="tpu_custom_call" | custom-call | tf_op jit(solution)/shard_map/pallas_call | solution.py:28
  81.4 1.1 %shard_map.156 = (f32[512,256]{1,0:T(8,128)}, f32[256,512]{1,0:T(8,128)}) custom-call(bf16[128,256]{1,0:T(8,128)(2,1)S(1)} %shard_map.155.refs_0_, bf16[128,256]{1,0:T(8,128)(2,1)S(1)} %collective-permute-done.31.refs_1_, bf16[128,256]{1,0:T(8,128)(2,1)S(1)} %collective-permute-done.32.refs_2_, bf16[128,256]{1,0:T(8,128)(2,1)S(1)} %collective-permute-done.33.refs_3_, ...), custom_call_target="tpu_custom_call" | custom-call | tf_op jit(solution)/shard_map/pallas_call | solution.py:28
  (70 shorter events, 4.8 us)
Async XLA Ops:
  0.6 19.3 %copy-start = (bf16[320,512]{1,0:T(8,128)(2,1)S(1)}, bf16[320,512]{1,0:T(8,128)(2,1)}, u32[]{:S(2)}) copy-start(bf16[320,512]{1,0:T(8,128)(2,1)} %state_ref.3) | copy-start | bytes 983044
  0.6 1.0 %copy-start.5 = (bf16[512,256]{1,0:T(8,128)(2,1)S(1)}, bf16[512,256]{1,0:T(8,128)(2,1)}, u32[]{:S(2)}) copy-start(bf16[512,256]{1,0:T(8,128)(2,1)} %w_ref.1) | copy-start | bytes 786436
  1.6 0.9 %copy-start.7 = (bf16[128,512]{1,0:T(8,128)(2,1)S(1)}, bf16[128,512]{1,0:T(8,128)(2,1)}, u32[]{:S(2)}) copy-start(bf16[128,512]{1,0:T(8,128)(2,1)} %obs_ref.1) | copy-start | bytes 393220
  6.1 11.0 %collective-permute-start = (bf16[144,128]{1,0:T(8,128)(2,1)S(1)}, bf16[144,128]{1,0:T(8,128)(2,1)S(1)}, u32[]{:S(2)}, u32[]{:S(2)}) collective-permute-start(bf16[144,128]{1,0:T(8,128)(2,1)S(1)} %get-tuple-element.48), channel_id=1, source_target_pairs={{0,2},{2,4},{4,6},{6,8},{8,10},{10,12},{12,14},{14,0},{1,3},{3,5},... | collective-permute-start | bytes 110600 | tf_op jit(solution)/shard_map/ppermute | solution.py:40
  9.1 9.3 %collective-permute-start.1 = (bf16[144,128]{1,0:T(8,128)(2,1)S(1)}, bf16[144,128]{1,0:T(8,128)(2,1)S(1)}, u32[]{:S(2)}, u32[]{:S(2)}) collective-permute-start(bf16[144,128]{1,0:T(8,128)(2,1)S(1)} %get-tuple-element.49), channel_id=1, source_target_pairs={{0,4},{2,6},{4,8},{6,10},{8,12},{10,14},{12,0},{14,2},{1,5},{3,7},... | collective-permute-start | bytes 110600 | tf_op jit(solution)/shard_map/ppermute | solution.py:40
  10.7 12.4 %collective-permute-start.2 = (bf16[144,128]{1,0:T(8,128)(2,1)S(1)}, bf16[144,128]{1,0:T(8,128)(2,1)S(1)}, u32[]{:S(2)}, u32[]{:S(2)}) collective-permute-start(bf16[144,128]{1,0:T(8,128)(2,1)S(1)} %get-tuple-element.50), channel_id=1, source_target_pairs={{0,6},{2,8},{4,10},{6,12},{8,14},{10,0},{12,2},{14,4},{1,7},{3,9},... | collective-permute-start | bytes 110600 | tf_op jit(solution)/shard_map/ppermute | solution.py:40
  13.3 9.9 %collective-permute-start.3 = (bf16[144,128]{1,0:T(8,128)(2,1)S(1)}, bf16[144,128]{1,0:T(8,128)(2,1)S(1)}, u32[]{:S(2)}, u32[]{:S(2)}) collective-permute-start(bf16[144,128]{1,0:T(8,128)(2,1)S(1)} %get-tuple-element.51), channel_id=1, source_target_pairs={{0,8},{2,10},{4,12},{6,14},{8,0},{10,2},{12,4},{14,6},{1,9},{3,11}... | collective-permute-start | bytes 110600 | tf_op jit(solution)/shard_map/ppermute | solution.py:40
  14.5 8.7 %collective-permute-start.4 = (bf16[144,128]{1,0:T(8,128)(2,1)S(1)}, bf16[144,128]{1,0:T(8,128)(2,1)S(1)}, u32[]{:S(2)}, u32[]{:S(2)}) collective-permute-start(bf16[144,128]{1,0:T(8,128)(2,1)S(1)} %get-tuple-element.52), channel_id=1, source_target_pairs={{0,10},{2,12},{4,14},{6,0},{8,2},{10,4},{12,6},{14,8},{1,11},{3,13... | collective-permute-start | bytes 110600 | tf_op jit(solution)/shard_map/ppermute | solution.py:40
  17.1 6.0 %collective-permute-start.5 = (bf16[144,128]{1,0:T(8,128)(2,1)S(1)}, bf16[144,128]{1,0:T(8,128)(2,1)S(1)}, u32[]{:S(2)}, u32[]{:S(2)}) collective-permute-start(bf16[144,128]{1,0:T(8,128)(2,1)S(1)} %get-tuple-element.53), channel_id=1, source_target_pairs={{0,12},{2,14},{4,0},{6,2},{8,4},{10,6},{12,8},{14,10},{1,13},{3,15... | collective-permute-start | bytes 110600 | tf_op jit(solution)/shard_map/ppermute | solution.py:40
  18.5 4.7 %collective-permute-start.6 = (bf16[144,128]{1,0:T(8,128)(2,1)S(1)}, bf16[144,128]{1,0:T(8,128)(2,1)S(1)}, u32[]{:S(2)}, u32[]{:S(2)}) collective-permute-start(bf16[144,128]{1,0:T(8,128)(2,1)S(1)} %get-tuple-element.54), channel_id=1, source_target_pairs={{0,14},{2,0},{4,2},{6,4},{8,6},{10,8},{12,10},{14,12},{1,15},{3,1}... | collective-permute-start | bytes 110600 | tf_op jit(solution)/shard_map/ppermute | solution.py:40
  19.9 1.0 %copy-start.1 = (bf16[320,512]{1,0:T(8,128)(2,1)S(1)}, bf16[320,512]{1,0:T(8,128)(2,1)}, u32[]{:S(2)}) copy-start(bf16[320,512]{1,0:T(8,128)(2,1)} %agg_ref.3) | copy-start | bytes 983044
  20.9 0.9 %copy-start.3 = (bf16[512,256]{1,0:T(8,128)(2,1)S(1)}, bf16[512,256]{1,0:T(8,128)(2,1)}, u32[]{:S(2)}) copy-start(bf16[512,256]{1,0:T(8,128)(2,1)} %w_node_ref.3) | copy-start | bytes 786436
  21.8 0.9 %copy-start.9 = (bf16[256,512]{1,0:T(8,128)(2,1)S(1)}, bf16[256,512]{1,0:T(8,128)(2,1)}, u32[]{:S(2)}) copy-start(bf16[256,512]{1,0:T(8,128)(2,1)} %w_out_ref.1) | copy-start | bytes 786436
  23.2 1.1 %copy-start.2 = (bf16[320,512]{1,0:T(8,128)(2,1)S(1)}, bf16[320,512]{1,0:T(8,128)(2,1)}, u32[]{:S(2)}) copy-start(bf16[320,512]{1,0:T(8,128)(2,1)} %agg_ref.3) | copy-start | bytes 983044
  23.2 1.1 %copy-start.4 = (bf16[512,256]{1,0:T(8,128)(2,1)S(1)}, bf16[512,256]{1,0:T(8,128)(2,1)}, u32[]{:S(2)}) copy-start(bf16[512,256]{1,0:T(8,128)(2,1)} %w_node_ref.3) | copy-start | bytes 786436
  24.3 17.3 %copy-start.6 = (bf16[512,256]{1,0:T(8,128)(2,1)S(1)}, bf16[512,256]{1,0:T(8,128)(2,1)}, u32[]{:S(2)}) copy-start(bf16[512,256]{1,0:T(8,128)(2,1)} %w_ref.1) | copy-start | bytes 786436
  24.3 17.3 %copy-start.8 = (bf16[128,512]{1,0:T(8,128)(2,1)S(1)}, bf16[128,512]{1,0:T(8,128)(2,1)}, u32[]{:S(2)}) copy-start(bf16[128,512]{1,0:T(8,128)(2,1)} %obs_ref.1) | copy-start | bytes 393220
  25.3 26.8 %collective-permute-start.27 = (bf16[512,256]{1,0:T(8,128)(2,1)S(1)}, bf16[512,256]{1,0:T(8,128)(2,1)S(1)}, u32[]{:S(2)}, u32[]{:S(2)}) collective-permute-start(bf16[512,256]{1,0:T(8,128)(2,1)S(1)} %get-tuple-element.80), channel_id=1, source_target_pairs={{0,2},{2,0},{1,3},{3,1},{4,6},{6,4},{5,7},{7,5},{8,10},{10,8},{9,1... | collective-permute-start | bytes 786440 | tf_op jit(solution)/shard_map/ppermute | solution.py:40
  26.1 7.5 %collective-permute-start.8 = (bf16[64,256]{1,0:T(8,128)(2,1)S(1)}, bf16[64,256]{1,0:T(8,128)(2,1)S(1)}, u32[]{:S(2)}, u32[]{:S(2)}) collective-permute-start(bf16[64,256]{1,0:T(8,128)(2,1)S(1)} %get-tuple-element.61), channel_id=1, source_target_pairs={{0,14},{2,0},{4,2},{6,4},{8,6},{10,8},{12,10},{14,12},{1,15},{3,1}... | collective-permute-start | bytes 98312 | tf_op jit(solution)/shard_map/ppermute | solution.py:40
  28.8 4.9 %collective-permute-start.9 = (bf16[64,256]{1,0:T(8,128)(2,1)S(1)}, bf16[64,256]{1,0:T(8,128)(2,1)S(1)}, u32[]{:S(2)}, u32[]{:S(2)}) collective-permute-start(bf16[64,256]{1,0:T(8,128)(2,1)S(1)} %get-tuple-element.62), channel_id=1, source_target_pairs={{0,12},{2,14},{4,0},{6,2},{8,4},{10,6},{12,8},{14,10},{1,13},{3,15... | collective-permute-start | bytes 98312 | tf_op jit(solution)/shard_map/ppermute | solution.py:40
  29.3 5.5 %collective-permute-start.10 = (bf16[64,256]{1,0:T(8,128)(2,1)S(1)}, bf16[64,256]{1,0:T(8,128)(2,1)S(1)}, u32[]{:S(2)}, u32[]{:S(2)}) collective-permute-start(bf16[64,256]{1,0:T(8,128)(2,1)S(1)} %get-tuple-element.63), channel_id=1, source_target_pairs={{0,10},{2,12},{4,14},{6,0},{8,2},{10,4},{12,6},{14,8},{1,11},{3,13... | collective-permute-start | bytes 98312 | tf_op jit(solution)/shard_map/ppermute | solution.py:40
  29.6 7.8 %collective-permute-start.11 = (bf16[64,256]{1,0:T(8,128)(2,1)S(1)}, bf16[64,256]{1,0:T(8,128)(2,1)S(1)}, u32[]{:S(2)}, u32[]{:S(2)}) collective-permute-start(bf16[64,256]{1,0:T(8,128)(2,1)S(1)} %get-tuple-element.64), channel_id=1, source_target_pairs={{0,8},{2,10},{4,12},{6,14},{8,0},{10,2},{12,4},{14,6},{1,9},{3,11}... | collective-permute-start | bytes 98312 | tf_op jit(solution)/shard_map/ppermute | solution.py:40
  33.7 5.7 %collective-permute-start.12 = (bf16[64,256]{1,0:T(8,128)(2,1)S(1)}, bf16[64,256]{1,0:T(8,128)(2,1)S(1)}, u32[]{:S(2)}, u32[]{:S(2)}) collective-permute-start(bf16[64,256]{1,0:T(8,128)(2,1)S(1)} %get-tuple-element.65), channel_id=1, source_target_pairs={{0,6},{2,8},{4,10},{6,12},{8,14},{10,0},{12,2},{14,4},{1,7},{3,9},... | collective-permute-start | bytes 98312 | tf_op jit(solution)/shard_map/ppermute | solution.py:40
  33.7 5.8 %collective-permute-start.13 = (bf16[64,256]{1,0:T(8,128)(2,1)S(1)}, bf16[64,256]{1,0:T(8,128)(2,1)S(1)}, u32[]{:S(2)}, u32[]{:S(2)}) collective-permute-start(bf16[64,256]{1,0:T(8,128)(2,1)S(1)} %get-tuple-element.66), channel_id=1, source_target_pairs={{0,4},{2,6},{4,8},{6,10},{8,12},{10,14},{12,0},{14,2},{1,5},{3,7},... | collective-permute-start | bytes 98312 | tf_op jit(solution)/shard_map/ppermute | solution.py:40
  34.8 6.7 %collective-permute-start.14 = (bf16[64,256]{1,0:T(8,128)(2,1)S(1)}, bf16[64,256]{1,0:T(8,128)(2,1)S(1)}, u32[]{:S(2)}, u32[]{:S(2)}) collective-permute-start(bf16[64,256]{1,0:T(8,128)(2,1)S(1)} %get-tuple-element.67), channel_id=1, source_target_pairs={{0,2},{2,4},{4,6},{6,8},{8,10},{10,12},{12,14},{14,0},{1,3},{3,5},... | collective-permute-start | bytes 98312 | tf_op jit(solution)/shard_map/ppermute | solution.py:40
  43.0 5.1 %collective-permute-start.16 = (bf16[272,256]{1,0:T(8,128)(2,1)S(1)}, bf16[272,256]{1,0:T(8,128)(2,1)S(1)}, u32[]{:S(2)}, u32[]{:S(2)}) collective-permute-start(bf16[272,256]{1,0:T(8,128)(2,1)S(1)} %get-tuple-element.73), channel_id=1, source_target_pairs={{0,2},{2,0},{1,3},{3,1},{4,6},{6,4},{5,7},{7,5},{8,10},{10,8},{9,1... | collective-permute-start | bytes 417800 | tf_op jit(solution)/shard_map/ppermute | solution.py:40
  43.1 20.6 %collective-permute-start.7 = (bf16[320,256]{1,0:T(8,128)(2,1)S(1)}, bf16[320,256]{1,0:T(8,128)(2,1)S(1)}, u32[]{:S(2)}, u32[]{:S(2)}) collective-permute-start(bf16[320,256]{1,0:T(8,128)(2,1)S(1)} %get-tuple-element.58), channel_id=1, source_target_pairs={{0,1},{1,0},{2,3},{3,2},{4,5},{5,4},{6,7},{7,6},{8,9},{9,8},{10,11... | collective-permute-start | bytes 491528 | tf_op jit(solution)/shard_map/ppermute | solution.py:40
  48.2 6.2 %collective-permute-start.17 = (bf16[80,256]{1,0:T(8,128)(2,1)S(1)}, bf16[80,256]{1,0:T(8,128)(2,1)S(1)}, u32[]{:S(2)}, u32[]{:S(2)}) collective-permute-start(bf16[80,256]{1,0:T(8,128)(2,1)S(1)} %get-tuple-element.75), channel_id=1, source_target_pairs={{0,4},{4,8},{8,12},{12,0},{1,5},{5,9},{9,13},{13,1},{2,6},{6,10},{... | collective-permute-start | bytes 122888 | tf_op jit(solution)/shard_map/ppermute | solution.py:40
  48.5 6.4 %collective-permute-start.18 = (bf16[80,256]{1,0:T(8,128)(2,1)S(1)}, bf16[80,256]{1,0:T(8,128)(2,1)S(1)}, u32[]{:S(2)}, u32[]{:S(2)}) collective-permute-start(bf16[80,256]{1,0:T(8,128)(2,1)S(1)} %get-tuple-element.76), channel_id=1, source_target_pairs={{0,8},{4,12},{8,0},{12,4},{1,9},{5,13},{9,1},{13,5},{2,10},{6,14},... | collective-permute-start | bytes 122888 | tf_op jit(solution)/shard_map/ppermute | solution.py:40
  49.7 7.5 %collective-permute-start.19 = (bf16[80,256]{1,0:T(8,128)(2,1)S(1)}, bf16[80,256]{1,0:T(8,128)(2,1)S(1)}, u32[]{:S(2)}, u32[]{:S(2)}) collective-permute-start(bf16[80,256]{1,0:T(8,128)(2,1)S(1)} %get-tuple-element.77), channel_id=1, source_target_pairs={{0,12},{4,0},{8,4},{12,8},{1,13},{5,1},{9,5},{13,9},{2,14},{6,2},{... | collective-permute-start | bytes 122888 | tf_op jit(solution)/shard_map/ppermute | solution.py:40
  52.2 6.1 %collective-permute-start.28 = (bf16[128,256]{1,0:T(8,128)(2,1)S(1)}, bf16[128,256]{1,0:T(8,128)(2,1)S(1)}, u32[]{:S(2)}, u32[]{:S(2)}) collective-permute-start(bf16[128,256]{1,0:T(8,128)(2,1)S(1)} %get-tuple-element.82), channel_id=1, source_target_pairs={{0,4},{4,8},{8,12},{12,0},{1,5},{5,9},{9,13},{13,1},{2,6},{6,10},{... | collective-permute-start | bytes 196616 | tf_op jit(solution)/shard_map/ppermute | solution.py:40
  54.4 5.7 %collective-permute-start.29 = (bf16[128,256]{1,0:T(8,128)(2,1)S(1)}, bf16[128,256]{1,0:T(8,128)(2,1)S(1)}, u32[]{:S(2)}, u32[]{:S(2)}) collective-permute-start(bf16[128,256]{1,0:T(8,128)(2,1)S(1)} %get-tuple-element.83), channel_id=1, source_target_pairs={{0,8},{4,12},{8,0},{12,4},{1,9},{5,13},{9,1},{13,5},{2,10},{6,14},... | collective-permute-start | bytes 196616 | tf_op jit(solution)/shard_map/ppermute | solution.py:40
  54.8 5.3 %collective-permute-start.30 = (bf16[128,256]{1,0:T(8,128)(2,1)S(1)}, bf16[128,256]{1,0:T(8,128)(2,1)S(1)}, u32[]{:S(2)}, u32[]{:S(2)}) collective-permute-start(bf16[128,256]{1,0:T(8,128)(2,1)S(1)} %get-tuple-element.84), channel_id=1, source_target_pairs={{0,12},{4,0},{8,4},{12,8},{1,13},{5,1},{9,5},{13,9},{2,14},{6,2},{... | collective-permute-start | bytes 196616 | tf_op jit(solution)/shard_map/ppermute | solution.py:40
  57.2 6.4 %collective-permute-start.15 = (bf16[128,256]{1,0:T(8,128)(2,1)S(1)}, bf16[128,256]{1,0:T(8,128)(2,1)S(1)}, u32[]{:S(2)}, u32[]{:S(2)}) collective-permute-start(bf16[128,256]{1,0:T(8,128)(2,1)S(1)} %get-tuple-element.69), channel_id=1, source_target_pairs={{0,1},{1,0},{2,3},{3,2},{4,5},{5,4},{6,7},{7,6},{8,9},{9,8},{10,11... | collective-permute-start | bytes 196616 | tf_op jit(solution)/shard_map/ppermute | solution.py:40
  58.3 6.8 %collective-permute-start.20 = (bf16[64,256]{1,0:T(8,128)(2,1)S(1)}, bf16[64,256]{1,0:T(8,128)(2,1)S(1)}, u32[]{:S(2)}, u32[]{:S(2)}) collective-permute-start(bf16[64,256]{1,0:T(8,128)(2,1)S(1)} %get-tuple-element.78.refs_0_), channel_id=1, source_target_pairs={{0,4},{4,8},{8,12},{12,0},{1,5},{5,9},{9,13},{13,1},{2,6},{6,10},{... | collective-permute-start | bytes 98312 | tf_op jit(solution)/shard_map/ppermute | solution.py:40
  60.1 7.5 %collective-permute-start.21 = (bf16[64,256]{1,0:T(8,128)(2,1)S(1)}, bf16[64,256]{1,0:T(8,128)(2,1)S(1)}, u32[]{:S(2)}, u32[]{:S(2)}) collective-permute-start(bf16[64,256]{1,0:T(8,128)(2,1)S(1)} %get-tuple-element.78.refs_0_), channel_id=1, source_target_pairs={{0,8},{4,12},{8,0},{12,4},{1,9},{5,13},{9,1},{13,5},{2,10},{6,14},... | collective-permute-start | bytes 98312 | tf_op jit(solution)/shard_map/ppermute | solution.py:40
  60.1 7.5 %collective-permute-start.22 = (bf16[64,256]{1,0:T(8,128)(2,1)S(1)}, bf16[64,256]{1,0:T(8,128)(2,1)S(1)}, u32[]{:S(2)}, u32[]{:S(2)}) collective-permute-start(bf16[64,256]{1,0:T(8,128)(2,1)S(1)} %get-tuple-element.78.refs_0_), channel_id=1, source_target_pairs={{0,12},{4,0},{8,4},{12,8},{1,13},{5,1},{9,5},{13,9},{2,14},{6,2},{... | collective-permute-start | bytes 98312 | tf_op jit(solution)/shard_map/ppermute | solution.py:40
  63.6 10.2 %collective-permute-start.31 = (bf16[128,256]{1,0:T(8,128)(2,1)S(1)}, bf16[128,256]{1,0:T(8,128)(2,1)S(1)}, u32[]{:S(2)}, u32[]{:S(2)}) collective-permute-start(bf16[128,256]{1,0:T(8,128)(2,1)S(1)} %shard_map.155.refs_0_), channel_id=1, source_target_pairs={{0,4},{4,8},{8,12},{12,0},{1,5},{5,9},{9,13},{13,1},{2,6},{6,10},{... | collective-permute-start | bytes 196616 | tf_op jit(solution)/shard_map/ppermute | solution.py:40
  63.7 10.8 %collective-permute-start.32 = (bf16[128,256]{1,0:T(8,128)(2,1)S(1)}, bf16[128,256]{1,0:T(8,128)(2,1)S(1)}, u32[]{:S(2)}, u32[]{:S(2)}) collective-permute-start(bf16[128,256]{1,0:T(8,128)(2,1)S(1)} %shard_map.155.refs_0_), channel_id=1, source_target_pairs={{0,8},{4,12},{8,0},{12,4},{1,9},{5,13},{9,1},{13,5},{2,10},{6,14},... | collective-permute-start | bytes 196616 | tf_op jit(solution)/shard_map/ppermute | solution.py:40
  65.2 10.7 %collective-permute-start.33 = (bf16[128,256]{1,0:T(8,128)(2,1)S(1)}, bf16[128,256]{1,0:T(8,128)(2,1)S(1)}, u32[]{:S(2)}, u32[]{:S(2)}) collective-permute-start(bf16[128,256]{1,0:T(8,128)(2,1)S(1)} %shard_map.155.refs_0_), channel_id=1, source_target_pairs={{0,12},{4,0},{8,4},{12,8},{1,13},{5,1},{9,5},{13,9},{2,14},{6,2},{... | collective-permute-start | bytes 196616 | tf_op jit(solution)/shard_map/ppermute | solution.py:40
  67.6 4.2 %collective-permute-start.23 = (bf16[64,256]{1,0:T(8,128)(2,1)S(1)}, bf16[64,256]{1,0:T(8,128)(2,1)S(1)}, u32[]{:S(2)}, u32[]{:S(2)}) collective-permute-start(bf16[64,256]{1,0:T(8,128)(2,1)S(1)} %get-tuple-element.78.refs_0_), channel_id=1, source_target_pairs={{0,2},{2,0},{1,3},{3,1},{4,6},{6,4},{5,7},{7,5},{8,10},{10,8},{9,1... | collective-permute-start | bytes 98312 | tf_op jit(solution)/shard_map/ppermute | solution.py:40
  67.6 4.9 %collective-permute-start.24 = (bf16[64,256]{1,0:T(8,128)(2,1)S(1)}, bf16[64,256]{1,0:T(8,128)(2,1)S(1)}, u32[]{:S(2)}, u32[]{:S(2)}) collective-permute-start(bf16[64,256]{1,0:T(8,128)(2,1)S(1)} %collective-permute-done.20.refs_1_), channel_id=1, source_target_pairs={{0,2},{2,0},{1,3},{3,1},{4,6},{6,4},{5,7},{7,5},{8,10},{10,8},{9,1... | collective-permute-start | bytes 98312 | tf_op jit(solution)/shard_map/ppermute | solution.py:40
  71.8 4.8 %collective-permute-start.25 = (bf16[64,256]{1,0:T(8,128)(2,1)S(1)}, bf16[64,256]{1,0:T(8,128)(2,1)S(1)}, u32[]{:S(2)}, u32[]{:S(2)}) collective-permute-start(bf16[64,256]{1,0:T(8,128)(2,1)S(1)} %collective-permute-done.21.refs_2_), channel_id=1, source_target_pairs={{0,2},{2,0},{1,3},{3,1},{4,6},{6,4},{5,7},{7,5},{8,10},{10,8},{9,1... | collective-permute-start | bytes 98312 | tf_op jit(solution)/shard_map/ppermute | solution.py:40
  72.5 8.8 %collective-permute-start.34 = (bf16[128,256]{1,0:T(8,128)(2,1)S(1)}, bf16[128,256]{1,0:T(8,128)(2,1)S(1)}, u32[]{:S(2)}, u32[]{:S(2)}) collective-permute-start(bf16[128,256]{1,0:T(8,128)(2,1)S(1)} %shard_map.155.refs_0_), channel_id=1, source_target_pairs={{0,2},{2,0},{1,3},{3,1},{4,6},{6,4},{5,7},{7,5},{8,10},{10,8},{9,1... | collective-permute-start | bytes 196616 | tf_op jit(solution)/shard_map/ppermute | solution.py:40
  73.9 7.5 %collective-permute-start.35 = (bf16[128,256]{1,0:T(8,128)(2,1)S(1)}, bf16[128,256]{1,0:T(8,128)(2,1)S(1)}, u32[]{:S(2)}, u32[]{:S(2)}) collective-permute-start(bf16[128,256]{1,0:T(8,128)(2,1)S(1)} %collective-permute-done.31.refs_1_), channel_id=1, source_target_pairs={{0,2},{2,0},{1,3},{3,1},{4,6},{6,4},{5,7},{7,5},{8,10},{10,8},{9,1... | collective-permute-start | bytes 196616 | tf_op jit(solution)/shard_map/ppermute | solution.py:40
  74.6 6.8 %collective-permute-start.36 = (bf16[128,256]{1,0:T(8,128)(2,1)S(1)}, bf16[128,256]{1,0:T(8,128)(2,1)S(1)}, u32[]{:S(2)}, u32[]{:S(2)}) collective-permute-start(bf16[128,256]{1,0:T(8,128)(2,1)S(1)} %collective-permute-done.32.refs_2_), channel_id=1, source_target_pairs={{0,2},{2,0},{1,3},{3,1},{4,6},{6,4},{5,7},{7,5},{8,10},{10,8},{9,1... | collective-permute-start | bytes 196616 | tf_op jit(solution)/shard_map/ppermute | solution.py:40
  75.9 5.5 %collective-permute-start.37 = (bf16[128,256]{1,0:T(8,128)(2,1)S(1)}, bf16[128,256]{1,0:T(8,128)(2,1)S(1)}, u32[]{:S(2)}, u32[]{:S(2)}) collective-permute-start(bf16[128,256]{1,0:T(8,128)(2,1)S(1)} %collective-permute-done.33.refs_3_), channel_id=1, source_target_pairs={{0,2},{2,0},{1,3},{3,1},{4,6},{6,4},{5,7},{7,5},{8,10},{10,8},{9,1... | collective-permute-start | bytes 196616 | tf_op jit(solution)/shard_map/ppermute | solution.py:40
  76.6 3.9 %collective-permute-start.26 = (bf16[64,256]{1,0:T(8,128)(2,1)S(1)}, bf16[64,256]{1,0:T(8,128)(2,1)S(1)}, u32[]{:S(2)}, u32[]{:S(2)}) collective-permute-start(bf16[64,256]{1,0:T(8,128)(2,1)S(1)} %collective-permute-done.22.refs_3_), channel_id=1, source_target_pairs={{0,2},{2,0},{1,3},{3,1},{4,6},{6,4},{5,7},{7,5},{8,10},{10,8},{9,1... | collective-permute-start | bytes 98312 | tf_op jit(solution)/shard_map/ppermute | solution.py:40
  (5 other events, 3.4 us)

commit v3 on v2

--- a/solution.py
+++ b/solution.py
@@ -31,8 +31,12 @@
         in_specs=[pl.BlockSpec(memory_space=pl.ANY) if in_hbm else vmem] * len(args),
         out_specs=[vmem] * len(outs),
         scratch_shapes=list(scratch),
-        compiler_params=pltpu.CompilerParams(vmem_limit_bytes=40 << 20),
+        compiler_params=pltpu.CompilerParams(vmem_limit_bytes=(60 if in_hbm else 40) << 20),
     )(*args)
+
+
+def exchange(blocks, axes):
+    return lax.all_to_all(blocks, axes, split_axis=0, concat_axis=0, tiled=True)
 
 
 def shift(value, axis, step):
@@ -54,8 +58,8 @@
 
 
 def pack_kernel(cap, *refs):
-    hbm, outs, local_refs, sems = refs[:6], refs[6:-7], refs[-7:-1], refs[-1]
-    place_ref, outs = outs[0], outs[1:]
+    hbm, outs, local_refs, sems = refs[:6], refs[6:8], refs[8:14], refs[14]
+    place_ref, out_ref = outs
     copies = [
         pltpu.make_async_copy(src, dst, sems.at[i]) for i, (src, dst) in enumerate(zip(hbm, local_refs))
     ]
@@ -64,8 +68,7 @@
     for copy in copies:
         copy.wait()
     obs_ref, owner_ref, index_ref, slot_ref, w_ref, bias_ref = local_refs
-    owners = len(outs)
-    chunk, lanes = outs[0].shape
+    owners, chunk, lanes = out_ref.shape
     fanout, obs = owner_ref.shape
     owner, index = owner_ref[...], index_ref[...]
     hits = [iota((owners, obs), 0) == owner[k : k + 1] for k in range(fanout)]
@@ -90,14 +93,15 @@
     )
     part = (dot(obs_ref[...], w_ref[...]) + bias).astype(BF16)
     header = header.astype(BF16)
-    me = lax.axis_index(OWNER_AXES)
-    for j, out_ref in enumerate(outs):
-        slots = iota((cap, obs), 0) + lax.rem(me + j, owners) * cap
-        pick = functools.reduce(jnp.logical_or, [slots == place for place in places])
-        packed = dot(pick.astype(BF16), part).astype(BF16)
+    slots = iota((owners * cap, obs), 0)
+    pick = functools.reduce(jnp.logical_or, [slots == place for place in places])
+    packed = dot(pick.astype(BF16), part).astype(BF16)
+    for d in range(owners):
         for c in range(part.shape[1] // lanes):
-            out_ref[c * cap : (c + 1) * cap, :] = packed[:, c * lanes : (c + 1) * lanes]
-        out_ref[chunk - SUBLANES :, :] = header
+            out_ref[d, c * cap : (c + 1) * cap, :] = packed[
+                d * cap : (d + 1) * cap, c * lanes : (c + 1) * lanes
+            ]
+        out_ref[d, chunk - SUBLANES :, :] = header
 
 
 def table_kernel(state_ref, agg_ref, w_node_ref, w_out_ref, table_ref):
@@ -111,16 +115,14 @@
         ).astype(BF16)
 
 
-def edge_kernel(owners, fanout, *refs):
-    recv_refs, table_ref = refs[:owners], refs[owners]
-    back_refs, act_ref, hot_ref = refs[owners + 1 : 2 * owners + 1], refs[-2], refs[-1]
-    chunk, lanes = recv_refs[0].shape
-    cap, hidden = back_refs[0].shape
+def edge_kernel(fanout, recv_ref, table_ref, back_ref, act_ref, hot_ref):
+    owners, chunk, lanes = recv_ref.shape
+    _, cap, hidden = back_ref.shape
     me = lax.axis_index(OWNER_AXES).astype(F32)
     columns = []
     parts = []
-    for recv_ref in recv_refs:
-        header = recv_ref[chunk - SUBLANES :, :].astype(F32)
+    for s in range(owners):
+        header = recv_ref[s, chunk - SUBLANES :, :].astype(F32)
         plus = jnp.zeros((cap, lanes), F32)
         for k in range(fanout):
             row = header[4 * k : 4 * k + 4]
@@ -129,7 +131,7 @@
         columns.append(jnp.sum(plus, axis=1, keepdims=True).astype(jnp.int32) - 1)
         parts.append(
             jnp.concatenate(
-                [recv_ref[c * cap : (c + 1) * cap, :] for c in range(hidden // lanes)], axis=1
+                [recv_ref[s, c * cap : (c + 1) * cap, :] for c in range(hidden // lanes)], axis=1
             ).astype(F32)
         )
     column = jnp.concatenate(columns, axis=0)
@@ -142,8 +144,8 @@
     g_a = (g_z * sig * (1.0 + pre * (1.0 - sig))).astype(BF16)
     act_ref[:, :hidden] = g_a
     act_ref[:, hidden:] = (pre * sig).astype(BF16)
-    for j, back_ref in enumerate(back_refs):
-        back_ref[...] = g_a[j * cap : (j + 1) * cap]
+    for s in range(owners):
+        back_ref[s] = g_a[s * cap : (s + 1) * cap]
 
 
 def split_x(total_ref, lines, tail, keep_ref, send_refs):
@@ -183,21 +185,15 @@
 
 
 def obs_kernel(
-    owners, lines, tail, place_ref, slot_ref, obs_ref, w_ref, *refs
+    lines, tail, back_ref, place_ref, slot_ref, obs_ref, w_ref, mine_ref, theirs_ref, keep_ref, *refs
 ):
-    back_refs, mine_ref, theirs_ref, keep_ref = refs[:owners], refs[owners], refs[owners + 1], refs[owners + 2]
-    send_refs, total_ref = refs[owners + 3 : -1], refs[-1]
+    send_refs, total_ref = refs[:-1], refs[-1]
     fanout, obs = place_ref.shape
-    cap = back_refs[0].shape[0]
-    me = lax.axis_index(OWNER_AXES)
-    obs_hidden = None
-    for j, back_ref in enumerate(back_refs):
-        slots = iota((cap, obs), 0) + lax.rem(me + j, owners) * cap
-        pick = functools.reduce(
-            jnp.logical_or, [slots == place_ref[k : k + 1, :] for k in range(fanout)]
-        )
-        part = dot(pick.astype(BF16), back_ref[...], 0, 0)
-        obs_hidden = part if obs_hidden is None else obs_hidden + part
+    slots = iota((back_ref.shape[0], obs), 0)
+    pick = functools.reduce(
+        jnp.logical_or, [slots == place_ref[k : k + 1, :] for k in range(fanout)]
+    )
+    obs_hidden = dot(pick.astype(BF16), back_ref[...], 0, 0)
     obs_hidden = obs_hidden.astype(BF16)
     total_ref[: lines[0], :] = dot(obs_ref[...], obs_hidden, 0, 0)
     total_ref[lines[0] :, :] = dot(slot_one_hot(slot_ref, tail).astype(BF16), obs_hidden)
@@ -212,63 +208,51 @@
 
 
 def sum_x_kernel(parts, tail, others, *refs):
-    keep_ref, recv_refs = refs[0], refs[1 : others + 1]
-    out_ref, send_refs, total_ref = refs[others + 1], refs[others + 2 : -1], refs[-1]
-    shares = len(send_refs) + 1
+    keep_ref, recv_refs, out_ref = refs[0], refs[1 : others + 1], refs[others + 1]
+    shares = out_ref.shape[0]
     total = keep_ref[...]
     for recv_ref in recv_refs:
         total = total + recv_ref[...].astype(F32)
-    total_ref[...] = total
-    me = lax.axis_index("obs")
-    for j in range(shares):
-        to = lax.rem(me + j, shares)
-        ref = send_refs[j - 1] if j else out_ref
+    total = total.astype(BF16)
+    for to in range(shares):
         at = begin = 0
         for part in parts:
             piece = piece_rows(part, shares)
-            begin_at = begin + jnp.minimum(to, part // piece - 1) * piece
-            rows = total_ref[pl.ds(pl.multiple_of(begin_at, SUBLANES), piece), :]
-            ref[at : at + piece, :] = rows.astype(ref.dtype)
+            if (to + 1) * piece <= part:
+                rows = total[begin + to * piece : begin + (to + 1) * piece]
+            else:
+                rows = jnp.zeros((piece, total.shape[1]), BF16)
+            out_ref[to, at : at + piece, :] = rows
             at, begin = at + piece, begin + part
         if tail:
-            ref[at : at + tail, :] = total_ref[begin : begin + tail, :].astype(ref.dtype)
-
-
-def sum_z_kernel(others, *refs):
-    total = refs[0][...]
-    for recv_ref in refs[1 : others + 1]:
-        total = total + recv_ref[...].astype(F32)
-    out_ref = refs[others + 1]
-    rows = out_ref.shape[0]
-    out_ref[...] = total[:rows].astype(BF16)
-    if len(refs) > others + 2:
-        slot_ref = refs[others + 2]
+            out_ref[to, at : at + tail, :] = total[begin : begin + tail]
+
+
+def sum_z_kernel(got_ref, out_ref, *slot_refs):
+    total = jnp.sum(got_ref[...].astype(F32), axis=0)
+    shares, rows, _ = out_ref.shape
+    piece = total[:rows].astype(BF16)
+    for to in range(shares):
+        out_ref[to] = piece
+    for slot_ref in slot_refs:
         slot_ref[...] = total[rows : rows + slot_ref.shape[0]]
 
 
-def spread_kernel(x_shares, z_shares, targets, *refs):
-    blocks, out_refs = refs[: x_shares * z_shares], refs[x_shares * z_shares :]
-    me_x, me_z = lax.axis_index("node"), lax.axis_index("obs")
-    for i, block_ref in enumerate(blocks):
-        from_x = lax.rem(me_x - i // z_shares + x_shares, x_shares)
-        from_z = lax.rem(me_z - i % z_shares + z_shares, z_shares)
-        hidden = block_ref.shape[1]
+def spread_kernel(targets, blocks, *out_refs):
+    x_shares = len(blocks)
+    z_shares, _, hidden = blocks[0].shape
+    me = lax.axis_index("node")
+    for j, block_ref in enumerate(blocks):
+        share = lax.rem(me - j + x_shares, x_shares)
         at = 0
         for out, count, column in targets:
             part = count // x_shares
             piece = piece_rows(part, z_shares)
-            out_ref = out_refs[out]
-
-            def write(out_ref=out_ref, part=part, piece=piece, column=column, at=at, block_ref=block_ref):
-                begin = pl.multiple_of(from_x * part + from_z * piece, SUBLANES)
-                out_ref[pl.ds(begin, piece), column : column + hidden] = block_ref[
-                    at : at + piece, :
+            for z in range(part // piece):
+                begin = pl.multiple_of(share * part + z * piece, SUBLANES)
+                out_refs[out][pl.ds(begin, piece), column : column + hidden] = block_ref[
+                    z, at : at + piece, :
                 ].astype(F32)
-
-            if part // piece == z_shares:
-                write()
-            else:
-                pl.when(from_z < part // piece)(write)
             at += piece
 
 
@@ -283,32 +267,33 @@
     parts = [count // x_shares for count in lines]
     rows = sum(piece_rows(part, z_shares) for part in parts)
     got = [shift(send, "node", j + 1) for j, send in enumerate(sends)]
-    keep, *sends = call(
+    (sums,) = call(
         functools.partial(sum_x_kernel, parts, tail, len(got)),
-        [((rows + tail, hidden), F32)] + [((rows + tail, hidden), BF16)] * (z_shares - 1),
+        [((z_shares, rows + tail, hidden), BF16)],
         keep, *got,
-        scratch=[pltpu.VMEM(keep.shape, F32)],
-    )
-    got = [shift(send, "obs", j + 1) for j, send in enumerate(sends)]
+    )
     return call(
-        functools.partial(sum_z_kernel, len(got)),
-        [((rows, hidden), BF16)] + ([((slots, hidden), F32)] if tail else []),
-        keep, *got,
-    )
-
-
-def gather_pieces(piece):
-    x_shares, z_shares = lax.axis_size("node"), lax.axis_size("obs")
-    along_z = [piece] + [shift(piece, "obs", j) for j in range(1, z_shares)]
-    blocks = list(along_z)
-    for j in range(1, x_shares):
-        blocks += [shift(block, "node", j) for block in along_z]
-    return blocks
+        sum_z_kernel,
+        [((z_shares, rows, hidden), BF16)] + ([((slots, hidden), F32)] if tail else []),
+        exchange(sums, "obs"),
+    )
+
+
+def gather_pieces(copies):
+    along_z = exchange(copies, "obs")
+    return [along_z] + [shift(along_z, "node", j) for j in range(1, lax.axis_size("node"))]
+
+
+def spread(targets, blocks, outs):
+    def kernel(*refs):
+        spread_kernel(targets, refs[: len(blocks)], *refs[len(blocks) :])
+
+    return call(kernel, outs, *blocks)
 
 
 def local(obs_feat, node_state, grad_agg, owner, local_idx, slot, w_obs, w_node, slot_bias, w_out):
     owners = lax.axis_size(OWNER_AXES)
-    x_shares, z_shares = lax.axis_size("node"), lax.axis_size("obs")
+    x_shares = lax.axis_size("node")
     obs, fanout = owner.shape
     nodes, width = node_state.shape
     hidden = w_obs.shape[1]
@@ -321,23 +306,23 @@
 
     chunk = cap * hidden // obs + SUBLANES
     inputs = (obs_feat, owner.T, local_idx.T, slot_row, w_obs, slot_bias)
-    place, *packed = call(
+    place, packed = call(
         functools.partial(pack_kernel, cap),
-        [((fanout, obs), jnp.int32)] + [((chunk, obs), BF16)] * owners,
+        [((fanout, obs), jnp.int32), ((owners, chunk, obs), BF16)],
         *inputs,
         scratch=[pltpu.VMEM(a.shape, a.dtype) for a in inputs] + [pltpu.SemaphoreType.DMA((len(inputs),))],
         in_hbm=True,
     )
-    received = packed[:1] + [shift(packed[j], OWNER_AXES, j) for j in range(1, owners)]
+    received = exchange(packed, OWNER_AXES)
     (table,) = call(
         table_kernel, [((nodes, 4 * hidden), BF16)], node_state, grad_agg, w_node, w_out
     )
-    *back, act, hot = call(
-        functools.partial(edge_kernel, owners, fanout),
-        [((cap, hidden), BF16)] * owners + [((edges, 2 * hidden), BF16), ((edges, nodes), BF16)],
-        *received, table,
-    )
-    back = back[:1] + [shift(back[j], OWNER_AXES, -j) for j in range(1, owners)]
+    back, act, hot = call(
+        functools.partial(edge_kernel, fanout),
+        [((owners, cap, hidden), BF16), ((edges, 2 * hidden), BF16), ((edges, nodes), BF16)],
+        received, table,
+    )
+    back = exchange(back, OWNER_AXES).reshape(edges, hidden)
 
     node_lines = [width] + [hidden] * (width // hidden)
     share = sum(node_lines) // x_shares
@@ -354,10 +339,10 @@
     tail = -(-slots // SUBLANES) * SUBLANES
     share = width // x_shares + tail
     obs_mine, obs_theirs, keep, *sends = call(
-        functools.partial(obs_kernel, owners, [width], tail),
+        functools.partial(obs_kernel, [width], tail),
         [((obs, half), F32), ((obs, half), BF16), ((share, hidden), F32)]
         + [((share, hidden), BF16)] * (x_shares - 1),
-        place, slot_row, obs_feat, w_obs, *back,
+        back, place, slot_row, obs_feat, w_obs,
         scratch=[pltpu.VMEM((width + tail, hidden), F32)],
     )
     obs_piece, grad_slot = reduce_shares([width], tail, slots, keep, sends)
@@ -370,16 +355,10 @@
         node_mine, node_got, obs_mine, obs_got,
     )
     node_targets = [(0, width, 0)] + [(1, hidden, c * hidden) for c in range(width // hidden)]
-    grad_w_node, grad_w_out = call(
-        functools.partial(spread_kernel, x_shares, z_shares, node_targets),
-        [((width, hidden), F32), ((hidden, width), F32)],
-        *node_blocks,
-    )
-    (grad_w_obs,) = call(
-        functools.partial(spread_kernel, x_shares, z_shares, [(0, width, 0)]),
-        [((width, hidden), F32)],
-        *obs_blocks,
-    )
+    grad_w_node, grad_w_out = spread(
+        node_targets, node_blocks, [((width, hidden), F32), ((hidden, width), F32)]
+    )
+    (grad_w_obs,) = spread([(0, width, 0)], obs_blocks, [((width, hidden), F32)])
     return grad_obs, grad_node, grad_w_obs, grad_w_node, grad_w_out, grad_slot
 
 

time: 82.8 us -> 87 us (1.051)
  waiting for transfers between devices: 18.3 us -> 41.8 us
  starting transfers between devices: 47.6 us -> 30.3 us
  local copies, waits for them, and re-layouts: 8.15 us -> 1.65 us
  Pallas kernels: 7.5 us -> 11.6 us
    ppermute x38 -> x6, starting transfers between devices: 47.6 us -> 4.34 us  [shift(): lax.ppermute(value, axis, [(i, (i + step) % size) for i in range(size)])]
    all_to_all x0 -> x6, waiting for transfers between devices: none -> 26.2 us  [exchange(): return lax.all_to_all(blocks, axes, split_axis=0, concat_axis=0, tiled=True)]
    all_to_all x0 -> x6, starting transfers between devices: none -> 26 us  [exchange(): return lax.all_to_all(blocks, axes, split_axis=0, concat_axis=0, tiled=True)]
    unnamed x30 -> x16, local copies, waits for them, and re-layouts: 8.15 us -> 1.65 us
    pallas_call x12, Pallas kernels: 7.5 us -> 11.6 us  [call(): pl.pallas_call(kernel, out_shape=[jax.ShapeDtypeStruct(shape, dtype) for...]
    ppermute x38 -> x6, waiting for transfers between devices: 18.3 us -> 15.6 us  [shift(): lax.ppermute(value, axis, [(i, (i + step) % size) for i in range(size)])]
  transfers between devices with their start and end apart: 38 -> 12, of which waited for: 11 -> 9; matrix products, arithmetic and copies ran while one was open for 0% -> 0% of each run, Pallas kernels for 4% -> 7%
where the time goes in v3:
time: 87 us; the launch traced here: 86.2 us
  waiting for transfers between devices  41.8 us (48%)
  starting transfers between devices  30.3 us (35%)
  Pallas kernels  11.6 us (13%)
  local copies, waits for them, and re-layouts  1.65 us (2%)
    all_to_all x6, waiting for transfers between devices, exchange(): return lax.all_to_all(blocks, axes, split_axis=0, concat_axis=0, tiled=True)  26.2 us
    all_to_all x6, starting transfers between devices, exchange(): return lax.all_to_all(blocks, axes, split_axis=0, concat_axis=0, tiled=True)  26 us
    ppermute x6, waiting for transfers between devices, shift(): lax.ppermute(value, axis, [(i, (i + step) % size) for i in range(size)])  15.6 us
    pallas_call x12, Pallas kernels, call(): pl.pallas_call(kernel, out_shape=[jax.ShapeDtypeStruct(shape, dtype) for...  11.6 us
    ppermute x6, starting transfers between devices, shift(): lax.ppermute(value, axis, [(i, (i + step) % size) for i in range(size)])  4.34 us
  transfers between devices with their start and end apart: 12, of which 9 were waited for; matrix products, arithmetic and copies ran while one was open for 0% of the time, Pallas kernels for 7%

profile of v3, /device:TPU:0, one launch (start us, length us, event | category | flops | bytes accessed | tf_op | source)
XLA Modules:
  0.0 86.2 jit_solution(5435702640197206981)
XLA Ops:
  0.6 0.0 copy-start.1
  0.6 2.5 %shard_map.145 = (s32[2,128]{1,0:T(2,128)}, bf16[8,144,128]{2,1,0:T(8,128)(2,1)}) custom-call(bf16[128,512]{1,0:T(8,128)(2,1)} %obs_ref.1, s32[2,128]{1,0:T(2,128)} %bitcast.7, s32[2,128]{1,0:T(2,128)} %bitcast.8, s32[1,128]{1,0:T(1,128)} %bitcast.5, bf16[512,256]{1,0:T(8,128)(2,1)} %w_ref.1, f32[6,256]{1,0:T(8,128)} %refs_5_.1), custom_call_target="tpu_custom_call" | custom-call | tf_op jit(solution)/shard_map/pallas_call | solution.py:28
  3.2 0.0 copy-start
  3.2 0.0 copy-start.2
  3.2 7.4 %all-to-all-start = ((bf16[8,144,128]{2,1,0:T(8,128)(2,1)}), bf16[8,144,128]{2,1,0:T(8,128)(2,1)S(1)}, u32[]{:S(2)}, u32[]{:S(2)}) async-start(bf16[8,144,128]{2,1,0:T(8,128)(2,1)} %get-tuple-element.25), calls=%async_computation | async-start | bytes 589824 | tf_op jit(solution)/shard_map/all_to_all | solution.py:39
  10.6 0.0 copy-done.1
  10.6 0.0 copy-done
  10.6 0.0 copy-done.2
  10.6 0.0 copy-start.5
  10.6 0.9 %copy-done.5 = bf16[256,512]{1,0:T(8,128)(2,1)S(1)} copy-done((bf16[256,512]{1,0:T(8,128)(2,1)S(1)}, bf16[256,512]{1,0:T(8,128)(2,1)}, u32[]{:S(2)}) %copy-start.5) | copy-done | bytes 262168
  11.6 0.3 shard_map.146.table_ref
  11.9 8.3 %all-to-all-done.recv_ref = bf16[8,144,128]{2,1,0:T(8,128)(2,1)S(1)} async-done(((bf16[8,144,128]{2,1,0:T(8,128)(2,1)}), bf16[8,144,128]{2,1,0:T(8,128)(2,1)S(1)}, u32[]{:S(2)}, u32[]{:S(2)}) %all-to-all-start) | async-done | bytes 294944 | tf_op jit(solution)/shard_map/all_to_all | solution.py:39
  20.2 1.7 %shard_map.147 = (bf16[8,64,256]{2,1,0:T(8,128)(2,1)}, bf16[512,512]{1,0:T(8,128)(2,1)S(1)}, bf16[512,320]{1,0:T(8,128)(2,1)S(1)}) custom-call(bf16[8,144,128]{2,1,0:T(8,128)(2,1)S(1)} %all-to-all-done.recv_ref, bf16[320,1024]{1,0:T(8,128)(2,1)S(1)} %shard_map.146.table_ref), custom_call_target="tpu_custom_call" | custom-call | tf_op jit(solution)/shard_map/pallas_call | solution.py:28
  21.9 3.6 %all-to-all-start.1 = ((bf16[8,64,256]{2,1,0:T(8,128)(2,1)}), bf16[8,64,256]{2,1,0:T(8,128)(2,1)S(1)}, u32[]{:S(2)}, u32[]{:S(2)}) async-start(bf16[8,64,256]{2,1,0:T(8,128)(2,1)} %get-tuple-element.30), calls=%async_computation.1 | async-start | bytes 524288 | tf_op jit(solution)/shard_map/all_to_all | solution.py:39
  25.5 1.0 %shard_map.148 = (f32[320,256]{1,0:T(8,128)S(1)}, bf16[320,256]{1,0:T(8,128)(2,1)S(1)}, f32[512,256]{1,0:T(8,128)S(1)}, bf16[512,256]{1,0:T(8,128)(2,1)S(1)}) custom-call(bf16[512,320]{1,0:T(8,128)(2,1)S(1)} %get-tuple-element.26.hot_ref, bf16[512,512]{1,0:T(8,128)(2,1)S(1)} %get-tuple-element.27.act_ref, bf16[320,512]{1,0:T(8,128)(2,1)S(1)} %copy-done, ...), custom_call_target="tpu_custom_call" | custom-call | tf_op jit(solution)/shard_map/pallas_call | solution.py:28
  26.5 2.1 %collective-permute-start.4 = (bf16[512,256]{1,0:T(8,128)(2,1)S(1)}, bf16[512,256]{1,0:T(8,128)(2,1)S(1)}, u32[]{:S(2)}, u32[]{:S(2)}) collective-permute-start(bf16[512,256]{1,0:T(8,128)(2,1)S(1)} %get-tuple-element.40), channel_id=1, source_target_pairs={{0,2},{2,0},{1,3},{3,1},{4,6},{6,4},{5,7},{7,5},{8,10},{10,8},{9,1... | collective-permute-start | bytes 786440 | tf_op jit(solution)/shard_map/ppermute | solution.py:44
  28.6 7.8 %collective-permute-done.4.refs_1_ = bf16[512,256]{1,0:T(8,128)(2,1)S(1)} collective-permute-done((bf16[512,256]{1,0:T(8,128)(2,1)S(1)}, bf16[512,256]{1,0:T(8,128)(2,1)S(1)}, u32[]{:S(2)}, u32[]{:S(2)}) %collective-permute-start.4) | collective-permute-done | bytes 262176 | tf_op jit(solution)/shard_map/ppermute | solution.py:44
  36.4 0.7 shard_map.154
  37.2 0.0 all-to-all-done.1
  37.2 4.5 %all-to-all-start.4 = ((bf16[4,128,256]{2,1,0:T(8,128)(2,1)}), bf16[4,128,256]{2,1,0:T(8,128)(2,1)S(1)}, u32[]{:S(2)}, u32[]{:S(2)}) async-start(bf16[4,128,256]{2,1,0:T(8,128)(2,1)} %shard_map.154), calls=%async_computation.4 | async-start | bytes 524288 | tf_op jit(solution)/shard_map/all_to_all | solution.py:39
  41.7 0.0 copy-done.3
  41.7 0.0 copy-done.4
  41.7 0.6 copy-done.6
  42.3 0.0 copy-done.7
  42.4 0.6 shard_map.149
  43.0 0.8 collective-permute-start.2
  43.8 4.3 %collective-permute-done.2.refs_1_ = bf16[272,256]{1,0:T(8,128)(2,1)S(1)} collective-permute-done((bf16[272,256]{1,0:T(8,128)(2,1)S(1)}, bf16[272,256]{1,0:T(8,128)(2,1)S(1)}, u32[]{:S(2)}, u32[]{:S(2)}) %collective-permute-start.2) | collective-permute-done | bytes 139296 | tf_op jit(solution)/shard_map/ppermute | solution.py:44
  48.1 0.7 shard_map.151
  48.8 1.4 %all-to-all-done.4.got_ref = bf16[4,128,256]{2,1,0:T(8,128)(2,1)S(1)} async-done(((bf16[4,128,256]{2,1,0:T(8,128)(2,1)}), bf16[4,128,256]{2,1,0:T(8,128)(2,1)S(1)}, u32[]{:S(2)}, u32[]{:S(2)}) %all-to-all-start.4) | async-done | bytes 262176 | tf_op jit(solution)/shard_map/all_to_all | solution.py:39
  50.2 3.7 %all-to-all-start.2 = ((bf16[4,80,256]{2,1,0:T(8,128)(2,1)}), bf16[4,80,256]{2,1,0:T(8,128)(2,1)S(1)}, u32[]{:S(2)}, u32[]{:S(2)}) async-start(bf16[4,80,256]{2,1,0:T(8,128)(2,1)} %shard_map.151), calls=%async_computation.2 | async-start | bytes 327680 | tf_op jit(solution)/shard_map/all_to_all | solution.py:39
  53.9 0.7 shard_map.155
  54.6 5.3 %all-to-all-done.2.got_ref = bf16[4,80,256]{2,1,0:T(8,128)(2,1)S(1)} async-done(((bf16[4,80,256]{2,1,0:T(8,128)(2,1)}), bf16[4,80,256]{2,1,0:T(8,128)(2,1)S(1)}, u32[]{:S(2)}, u32[]{:S(2)}) %all-to-all-start.2) | async-done | bytes 163872 | tf_op jit(solution)/shard_map/all_to_all | solution.py:39
  59.9 3.4 %all-to-all-start.5 = ((bf16[4,128,256]{2,1,0:T(8,128)(2,1)}), bf16[4,128,256]{2,1,0:T(8,128)(2,1)S(1)}, u32[]{:S(2)}, u32[]{:S(2)}) async-start(bf16[4,128,256]{2,1,0:T(8,128)(2,1)} %shard_map.155), calls=%async_computation.5 | async-start | bytes 524288 | tf_op jit(solution)/shard_map/all_to_all | solution.py:39
  63.3 0.7 shard_map.152
  64.0 6.1 %all-to-all-done.5.refs_0_ = bf16[4,128,256]{2,1,0:T(8,128)(2,1)S(1)} async-done(((bf16[4,128,256]{2,1,0:T(8,128)(2,1)}), bf16[4,128,256]{2,1,0:T(8,128)(2,1)S(1)}, u32[]{:S(2)}, u32[]{:S(2)}) %all-to-all-start.5) | async-done | bytes 262176 | tf_op jit(solution)/shard_map/all_to_all | solution.py:39
  70.0 3.4 %all-to-all-start.3 = ((bf16[4,64,256]{2,1,0:T(8,128)(2,1)}), bf16[4,64,256]{2,1,0:T(8,128)(2,1)S(1)}, u32[]{:S(2)}, u32[]{:S(2)}) async-start(bf16[4,64,256]{2,1,0:T(8,128)(2,1)} %get-tuple-element.38), calls=%async_computation.3 | async-start | bytes 262144 | tf_op jit(solution)/shard_map/all_to_all | solution.py:39
  73.5 0.7 collective-permute-start.5
  74.2 0.0 collective-permute-start
  74.2 5.2 %all-to-all-done.3.refs_0_ = bf16[4,64,256]{2,1,0:T(8,128)(2,1)S(1)} async-done(((bf16[4,64,256]{2,1,0:T(8,128)(2,1)}), bf16[4,64,256]{2,1,0:T(8,128)(2,1)S(1)}, u32[]{:S(2)}, u32[]{:S(2)}) %all-to-all-start.3) | async-done | bytes 131104 | tf_op jit(solution)/shard_map/all_to_all | solution.py:39
  79.4 0.7 collective-permute-start.3
  80.1 0.0 collective-permute-start.1
  80.1 0.0 collective-permute-done.node_got_ref
  80.1 1.2 %collective-permute-done.1.obs_got_ref = bf16[128,256]{1,0:T(8,128)(2,1)S(1)} collective-permute-done((bf16[128,256]{1,0:T(8,128)(2,1)S(1)}, bf16[128,256]{1,0:T(8,128)(2,1)S(1)}, u32[]{:S(2)}, u32[]{:S(2)}) %collective-permute-start.1) | collective-permute-done | bytes 65568 | tf_op jit(solution)/shard_map/ppermute | solution.py:44
  81.4 0.8 shard_map.150
  82.1 2.2 %collective-permute-done.3.refs_1_ = bf16[4,64,256]{2,1,0:T(8,128)(2,1)S(1)} collective-permute-done((bf16[4,64,256]{2,1,0:T(8,128)(2,1)S(1)}, bf16[4,64,256]{2,1,0:T(8,128)(2,1)S(1)}, u32[]{:S(2)}, u32[]{:S(2)}) %collective-permute-start.3) | collective-permute-done | bytes 131104 | tf_op jit(solution)/shard_map/ppermute | solution.py:44
  84.4 0.8 shard_map.153
  85.2 0.0 collective-permute-done.5.refs_1_
  85.2 1.0 %shard_map.156 = (f32[512,256]{1,0:T(8,128)}, f32[256,512]{1,0:T(8,128)}) custom-call(bf16[4,128,256]{2,1,0:T(8,128)(2,1)S(1)} %all-to-all-done.5.refs_0_, bf16[4,128,256]{2,1,0:T(8,128)(2,1)S(1)} %collective-permute-done.5.refs_1_), custom_call_target="tpu_custom_call" | custom-call | tf_op jit(solution)/shard_map/pallas_call | solution.py:28
  (4 shorter events, 0.0 us)
Async XLA Ops:
  0.6 10.0 %copy-start.1 = (bf16[320,512]{1,0:T(8,128)(2,1)S(1)}, bf16[320,512]{1,0:T(8,128)(2,1)}, u32[]{:S(2)}) copy-start(bf16[320,512]{1,0:T(8,128)(2,1)} %agg_ref.3) | copy-start | bytes 983044
  3.2 7.4 %copy-start = (bf16[320,512]{1,0:T(8,128)(2,1)S(1)}, bf16[320,512]{1,0:T(8,128)(2,1)}, u32[]{:S(2)}) copy-start(bf16[320,512]{1,0:T(8,128)(2,1)} %state_ref.3) | copy-start | bytes 983044
  3.2 7.4 %copy-start.2 = (bf16[512,256]{1,0:T(8,128)(2,1)S(1)}, bf16[512,256]{1,0:T(8,128)(2,1)}, u32[]{:S(2)}) copy-start(bf16[512,256]{1,0:T(8,128)(2,1)} %w_node_ref.3) | copy-start | bytes 786436
  3.2 17.0 %all-to-all-start = ((bf16[8,144,128]{2,1,0:T(8,128)(2,1)}), bf16[8,144,128]{2,1,0:T(8,128)(2,1)S(1)}, u32[]{:S(2)}, u32[]{:S(2)}) async-start(bf16[8,144,128]{2,1,0:T(8,128)(2,1)} %get-tuple-element.25), calls=%async_computation | async-start | bytes 589824 | tf_op jit(solution)/shard_map/all_to_all | solution.py:39
  10.6 1.0 %copy-start.5 = (bf16[256,512]{1,0:T(8,128)(2,1)S(1)}, bf16[256,512]{1,0:T(8,128)(2,1)}, u32[]{:S(2)}) copy-start(bf16[256,512]{1,0:T(8,128)(2,1)} %w_out_ref.1) | copy-start | bytes 786436
  21.9 15.2 %all-to-all-start.1 = ((bf16[8,64,256]{2,1,0:T(8,128)(2,1)}), bf16[8,64,256]{2,1,0:T(8,128)(2,1)S(1)}, u32[]{:S(2)}, u32[]{:S(2)}) async-start(bf16[8,64,256]{2,1,0:T(8,128)(2,1)} %get-tuple-element.30), calls=%async_computation.1 | async-start | bytes 524288 | tf_op jit(solution)/shard_map/all_to_all | solution.py:39
  26.5 9.9 %collective-permute-start.4 = (bf16[512,256]{1,0:T(8,128)(2,1)S(1)}, bf16[512,256]{1,0:T(8,128)(2,1)S(1)}, u32[]{:S(2)}, u32[]{:S(2)}) collective-permute-start(bf16[512,256]{1,0:T(8,128)(2,1)S(1)} %get-tuple-element.40), channel_id=1, source_target_pairs={{0,2},{2,0},{1,3},{3,1},{4,6},{6,4},{5,7},{7,5},{8,10},{10,8},{9,1... | collective-permute-start | bytes 786440 | tf_op jit(solution)/shard_map/ppermute | solution.py:44
  37.2 4.5 %copy-start.3 = (bf16[512,256]{1,0:T(8,128)(2,1)S(1)}, bf16[512,256]{1,0:T(8,128)(2,1)}, u32[]{:S(2)}) copy-start(bf16[512,256]{1,0:T(8,128)(2,1)} %w_ref.1) | copy-start | bytes 786436
  37.2 4.5 %copy-start.4 = (bf16[128,512]{1,0:T(8,128)(2,1)S(1)}, bf16[128,512]{1,0:T(8,128)(2,1)}, u32[]{:S(2)}) copy-start(bf16[128,512]{1,0:T(8,128)(2,1)} %obs_ref.1) | copy-start | bytes 393220
  37.2 13.0 %all-to-all-start.4 = ((bf16[4,128,256]{2,1,0:T(8,128)(2,1)}), bf16[4,128,256]{2,1,0:T(8,128)(2,1)S(1)}, u32[]{:S(2)}, u32[]{:S(2)}) async-start(bf16[4,128,256]{2,1,0:T(8,128)(2,1)} %shard_map.154), calls=%async_computation.4 | async-start | bytes 524288 | tf_op jit(solution)/shard_map/all_to_all | solution.py:39
  41.7 0.7 copy-start.6
  41.7 0.7 copy-start.7
  43.0 5.1 %collective-permute-start.2 = (bf16[272,256]{1,0:T(8,128)(2,1)S(1)}, bf16[272,256]{1,0:T(8,128)(2,1)S(1)}, u32[]{:S(2)}, u32[]{:S(2)}) collective-permute-start(bf16[272,256]{1,0:T(8,128)(2,1)S(1)} %get-tuple-element.37), channel_id=1, source_target_pairs={{0,2},{2,0},{1,3},{3,1},{4,6},{6,4},{5,7},{7,5},{8,10},{10,8},{9,1... | collective-permute-start | bytes 417800 | tf_op jit(solution)/shard_map/ppermute | solution.py:44
  50.2 9.7 %all-to-all-start.2 = ((bf16[4,80,256]{2,1,0:T(8,128)(2,1)}), bf16[4,80,256]{2,1,0:T(8,128)(2,1)S(1)}, u32[]{:S(2)}, u32[]{:S(2)}) async-start(bf16[4,80,256]{2,1,0:T(8,128)(2,1)} %shard_map.151), calls=%async_computation.2 | async-start | bytes 327680 | tf_op jit(solution)/shard_map/all_to_all | solution.py:39
  59.9 10.2 %all-to-all-start.5 = ((bf16[4,128,256]{2,1,0:T(8,128)(2,1)}), bf16[4,128,256]{2,1,0:T(8,128)(2,1)S(1)}, u32[]{:S(2)}, u32[]{:S(2)}) async-start(bf16[4,128,256]{2,1,0:T(8,128)(2,1)} %shard_map.155), calls=%async_computation.5 | async-start | bytes 524288 | tf_op jit(solution)/shard_map/all_to_all | solution.py:39
  70.0 9.4 %all-to-all-start.3 = ((bf16[4,64,256]{2,1,0:T(8,128)(2,1)}), bf16[4,64,256]{2,1,0:T(8,128)(2,1)S(1)}, u32[]{:S(2)}, u32[]{:S(2)}) async-start(bf16[4,64,256]{2,1,0:T(8,128)(2,1)} %get-tuple-element.38), calls=%async_computation.3 | async-start | bytes 262144 | tf_op jit(solution)/shard_map/all_to_all | solution.py:39
  73.5 11.7 %collective-permute-start.5 = (bf16[4,128,256]{2,1,0:T(8,128)(2,1)S(1)}, bf16[4,128,256]{2,1,0:T(8,128)(2,1)S(1)}, u32[]{:S(2)}, u32[]{:S(2)}) collective-permute-start(bf16[4,128,256]{2,1,0:T(8,128)(2,1)S(1)} %all-to-all-done.5.refs_0_), channel_id=1, source_target_pairs={{0,2},{2,0},{1,3},{3,1},{4,6},{6,4},{5,7},{7,5},{8,10},{10,8},{9,1... | collective-permute-start | bytes 786440 | tf_op jit(solution)/shard_map/ppermute | solution.py:44
  74.2 5.9 %collective-permute-start = (bf16[320,256]{1,0:T(8,128)(2,1)S(1)}, bf16[320,256]{1,0:T(8,128)(2,1)S(1)}, u32[]{:S(2)}, u32[]{:S(2)}) collective-permute-start(bf16[320,256]{1,0:T(8,128)(2,1)S(1)} %get-tuple-element.29), channel_id=1, source_target_pairs={{0,1},{1,0},{2,3},{3,2},{4,5},{5,4},{6,7},{7,6},{8,9},{9,8},{10,11... | collective-permute-start | bytes 491528 | tf_op jit(solution)/shard_map/ppermute | solution.py:44
  79.4 5.0 %collective-permute-start.3 = (bf16[4,64,256]{2,1,0:T(8,128)(2,1)S(1)}, bf16[4,64,256]{2,1,0:T(8,128)(2,1)S(1)}, u32[]{:S(2)}, u32[]{:S(2)}) collective-permute-start(bf16[4,64,256]{2,1,0:T(8,128)(2,1)S(1)} %all-to-all-done.3.refs_0_), channel_id=1, source_target_pairs={{0,2},{2,0},{1,3},{3,1},{4,6},{6,4},{5,7},{7,5},{8,10},{10,8},{9,1... | collective-permute-start | bytes 393224 | tf_op jit(solution)/shard_map/ppermute | solution.py:44
  80.1 1.3 %collective-permute-start.1 = (bf16[128,256]{1,0:T(8,128)(2,1)S(1)}, bf16[128,256]{1,0:T(8,128)(2,1)S(1)}, u32[]{:S(2)}, u32[]{:S(2)}) collective-permute-start(bf16[128,256]{1,0:T(8,128)(2,1)S(1)} %get-tuple-element.33), channel_id=1, source_target_pairs={{0,1},{1,0},{2,3},{3,2},{4,5},{5,4},{6,7},{7,6},{8,9},{9,8},{10,11... | collective-permute-start | bytes 196616 | tf_op jit(solution)/shard_map/ppermute | solution.py:44

commit v4 on v3

v4 whole, which is shorter than its diff:
```python
import functools

import jax
import jax.numpy as jnp
from jax import lax
from jax.experimental import pallas as pl
from jax.experimental.pallas import tpu as pltpu
from jax.sharding import PartitionSpec as P

OWNER_AXES = ("obs", "node")
SUBLANES = 16
BF16 = jnp.bfloat16
F32 = jnp.float32


def dot(left, right, left_dim=1, right_dim=0):
    return lax.dot_general(
        left, right, (((left_dim,), (right_dim,)), ((), ())), preferred_element_type=F32
    )


def iota(shape, dim):
    return lax.broadcasted_iota(jnp.int32, shape, dim)


def call(kernel, outs, *args, scratch=()):
    vmem = pl.BlockSpec(memory_space=pltpu.VMEM)
    return pl.pallas_call(
        kernel,
        out_shape=[jax.ShapeDtypeStruct(shape, dtype) for shape, dtype in outs],
        in_specs=[vmem] * len(args),
        out_specs=[vmem] * len(outs),
        scratch_shapes=list(scratch),
        compiler_params=pltpu.CompilerParams(vmem_limit_bytes=40 << 20),
    )(*args)


def call_staged(kernel, outs, *args):
    count = len(args)

    def staged(*refs):
        hbm, out_refs, held, sems = refs[:count], refs[count : -count - 1], refs[-count - 1 : -1], refs[-1]
        copies = [pltpu.make_async_copy(hbm[i], held[i], sems.at[i]) for i in range(count)]
        for copy in copies:
            copy.start()
        for copy in copies:
            copy.wait()
        kernel(*held, *out_refs)

    return pl.pallas_call(
        staged,
        out_shape=[jax.ShapeDtypeStruct(shape, dtype) for shape, dtype in outs],
        in_specs=[pl.BlockSpec(memory_space=pl.ANY)] * count,
        out_specs=[pl.BlockSpec(memory_space=pltpu.VMEM)] * len(outs),
        scratch_shapes=[pltpu.VMEM(a.shape, a.dtype) for a in args]
        + [pltpu.SemaphoreType.DMA((count,))],
        compiler_params=pltpu.CompilerParams(vmem_limit_bytes=60 << 20),
    )(*args)


def exchange(blocks, axes):
    return lax.all_to_all(blocks, axes, split_axis=0, concat_axis=0, tiled=True)


def shift(value, axis, step):
    size = lax.axis_size(axis)
    return lax.ppermute(value, axis, [(i, (i + step) % size) for i in range(size)])


def other_half(ref):
    half = ref.shape[0] // 2
    me = lax.axis_index("mp")
    mine = ref[pl.ds(pl.multiple_of(me * half, half), half), :]
    theirs = ref[pl.ds(pl.multiple_of((1 - me) * half, half), half), :]
    return mine, theirs


def slot_one_hot(slot_ref, slots):
    obs = slot_ref.shape[1]
    return (iota((slots, obs), 0) == slot_ref[...]).astype(F32)


def pack_kernel(cap, *refs):
    obs_ref, owner_ref, index_ref, slot_ref, w_ref, bias_ref, place_ref, *outs = refs
    owners = len(outs)
    chunk, lanes = outs[0].shape
    fanout, obs = owner_ref.shape
    owner, index = owner_ref[...], index_ref[...]
    hits = [iota((owners, obs), 0) == owner[k : k + 1] for k in range(fanout)]
    count = functools.reduce(jnp.add, [h.astype(F32) for h in hits])
    before = dot(count, (iota((obs, obs), 0) < iota((obs, obs), 1)).astype(F32))
    header = jnp.zeros((SUBLANES, obs), F32)
    places = []
    for k in range(fanout):
        rank = jnp.sum(jnp.where(hits[k], before, 0.0), axis=0, keepdims=True)
        places.append(owner[k : k + 1] * cap + rank.astype(jnp.int32))
        place_ref[k : k + 1, :] = places[k]
        plus = index[k : k + 1] + 1
        fields = (owner[k : k + 1].astype(F32), rank, (plus // 16).astype(F32), (plus % 16).astype(F32))
        for j, row in enumerate(fields):
            header = jnp.where(iota(header.shape, 0) == 4 * k + j, row, header)
    bias = lax.dot_general(
        slot_one_hot(slot_ref, bias_ref.shape[0]),
        bias_ref[...],
        (((0,), (0,)), ((), ())),
        precision=lax.Precision.HIGHEST,
        preferred_element_type=F32,
    )
    part = (dot(obs_ref[...], w_ref[...]) + bias).astype(BF16)
    header = header.astype(BF16)
    me = lax.axis_index(OWNER_AXES)
    for j, out_ref in enumerate(outs):
        slots = iota((cap, obs), 0) + lax.rem(me + j, owners) * cap
        pick = functools.reduce(jnp.logical_or, [slots == place for place in places])
        packed = dot(pick.astype(BF16), part).astype(BF16)
        for c in range(part.shape[1] // lanes):
            out_ref[c * cap : (c + 1) * cap, :] = packed[:, c * lanes : (c + 1) * lanes]
        out_ref[chunk - SUBLANES :, :] = header


def table_kernel(state_ref, agg_ref, w_node_ref, w_out_ref, table_ref):
    hidden = w_node_ref.shape[1]
    parts = (dot(state_ref[...], w_node_ref[...]), dot(agg_ref[...], w_out_ref[...], 1, 1))
    for j, part in enumerate(parts):
        high = part.astype(BF16)
        table_ref[:, 2 * j * hidden : (2 * j + 1) * hidden] = high
        table_ref[:, (2 * j + 1) * hidden : (2 * j + 2) * hidden] = (
            part - high.astype(F32)
        ).astype(BF16)


def edge_kernel(owners, fanout, *refs):
    recv_refs, (table_ref, back_ref, act_ref, hot_ref) = refs[:owners], refs[owners:]
    chunk, lanes = recv_refs[0].shape
    _, cap, hidden = back_ref.shape
    me = lax.axis_index(OWNER_AXES)
    me_float = me.astype(F32)
    columns = []
    parts = []
    for recv_ref in recv_refs:
        header = recv_ref[chunk - SUBLANES :, :].astype(F32)
        plus = jnp.zeros((cap, lanes), F32)
        for k in range(fanout):
            row = header[4 * k : 4 * k + 4]
            rank = jnp.where(row[0:1] == me_float, row[1:2], -1.0).astype(jnp.int32)
            plus = plus + jnp.where(iota((cap, lanes), 0) == rank, row[2:3] * 16.0 + row[3:4], 0.0)
        columns.append(jnp.sum(plus, axis=1, keepdims=True).astype(jnp.int32) - 1)
        parts.append(
            jnp.concatenate(
                [recv_ref[c * cap : (c + 1) * cap, :] for c in range(hidden // lanes)], axis=1
            ).astype(F32)
        )
    column = jnp.concatenate(columns, axis=0)
    hot = (column == iota(hot_ref.shape, 1)).astype(BF16)
    hot_ref[...] = hot
    rows = dot(hot, table_ref[...])
    pre = jnp.concatenate(parts, axis=0) + (rows[:, :hidden] + rows[:, hidden : 2 * hidden])
    g_z = rows[:, 2 * hidden : 3 * hidden] + rows[:, 3 * hidden :]
    sig = jax.nn.sigmoid(pre)
    g_a = (g_z * sig * (1.0 + pre * (1.0 - sig))).astype(BF16)
    act_ref[:, :hidden] = g_a
    act_ref[:, hidden:] = (pre * sig).astype(BF16)
    for j in range(owners):
        back_ref[lax.rem(me - j + owners, owners)] = g_a[j * cap : (j + 1) * cap]


def halving_steps():
    bits = [
        [(axis, k) for k in range(lax.axis_size(axis).bit_length() - 1)] for axis in ("node", "obs")
    ]
    steps = []
    for k in range(max(map(len, bits))):
        both = [line[k] for line in bits if k < len(line)]
        steps += [(both[0], both[-1])] + ([(both[1], both[0])] if len(both) > 1 else [])
    return steps


def flip(value, step):
    axes = ("obs", "node", "mp")
    sizes = [lax.axis_size(axis) for axis in axes]
    pairs = []
    for index in range(sizes[0] * sizes[1] * sizes[2]):
        place = [index // (sizes[1] * sizes[2]), index // sizes[2] % sizes[1], index % sizes[2]]
        axis, k = step[place[2] % 2]
        place[axes.index(axis)] ^= 1 << k
        pairs.append((index, (place[0] * sizes[1] + place[1]) * sizes[2] + place[2]))
    return lax.ppermute(value, axes, pairs)


def own_bit(step):
    bits = [(lax.axis_index(axis) >> k) & 1 for axis, k in step]
    return jnp.where(lax.axis_index("mp") % 2 == 0, bits[0], bits[1])


def halves(rows):
    return rows % (2 * SUBLANES) == 0


def split_half(total_ref, step, tail, keep_ref, send_ref):
    rows = total_ref.shape[0] - tail
    if halves(rows):
        rows //= 2
        bit = own_bit(step)
        kept, sent = [pl.ds(pl.multiple_of(b * rows, SUBLANES), rows) for b in (bit, 1 - bit)]
    else:
        kept = sent = pl.ds(0, rows)
    keep_ref[:rows, :] = total_ref[kept, :]
    send_ref[:rows, :] = total_ref[sent, :].astype(BF16)
    if tail:
        both = total_ref[total_ref.shape[0] - tail :, :]
        keep_ref[rows:, :] = both
        send_ref[rows:, :] = both.astype(BF16)


def node_kernel(
    step, hot_ref, act_ref, state_ref, agg_ref, w_node_ref, mine_ref, theirs_ref, keep_ref, send_ref, total_ref
):
    width, hidden = w_node_ref.shape
    by_node = dot(hot_ref[...], act_ref[...], 0, 0).astype(BF16)
    node_hidden, z_sum = by_node[:, :hidden], by_node[:, hidden:]
    total_ref[:width, :] = dot(state_ref[...], node_hidden, 0, 0)
    for c in range(width // hidden):
        begin = width + c * hidden
        total_ref[begin : begin + hidden, :] = dot(
            z_sum, agg_ref[:, c * hidden : (c + 1) * hidden], 0, 0
        )
    split_half(total_ref, step, 0, keep_ref, send_ref)
    mine, theirs = other_half(w_node_ref)
    theirs_ref[...] = dot(node_hidden, theirs, 1, 1).astype(BF16)
    mine_ref[...] = dot(node_hidden, mine, 1, 1)


def obs_kernel(
    step, tail, back_ref, place_ref, slot_ref, obs_ref, w_ref, mine_ref, theirs_ref, keep_ref, send_ref, total_ref
):
    width = w_ref.shape[0]
    fanout, obs = place_ref.shape
    slots = iota((back_ref.shape[0], obs), 0)
    pick = functools.reduce(
        jnp.logical_or, [slots == place_ref[k : k + 1, :] for k in range(fanout)]
    )
    obs_hidden = dot(pick.astype(BF16), back_ref[...], 0, 0)
    obs_hidden = obs_hidden.astype(BF16)
    total_ref[:width, :] = dot(obs_ref[...], obs_hidden, 0, 0)
    total_ref[width:, :] = dot(slot_one_hot(slot_ref, tail).astype(BF16), obs_hidden)
    split_half(total_ref, step, tail, keep_ref, send_ref)
    mine, theirs = other_half(w_ref)
    theirs_ref[...] = dot(obs_hidden, theirs, 1, 1).astype(BF16)
    mine_ref[...] = dot(obs_hidden, mine, 1, 1)


def add_kernel(step, tail, keep_ref, got_ref, next_ref, send_ref, total_ref):
    total_ref[...] = keep_ref[...] + got_ref[...].astype(F32)
    split_half(total_ref, step, tail, next_ref, send_ref)


def last_kernel(keep_ref, got_ref, piece_ref, *slot_refs):
    total = keep_ref[...] + got_ref[...].astype(F32)
    rows = piece_ref.shape[0]
    piece_ref[...] = total[:rows].astype(BF16)
    for slot_ref in slot_refs:
        slot_ref[...] = total[rows : rows + slot_ref.shape[0]]


def join_kernel(step, mine_ref, got_ref, out_ref):
    rows = mine_ref.shape[0]
    bit = own_bit(step)
    out_ref[pl.ds(pl.multiple_of(bit * rows, SUBLANES), rows), :] = mine_ref[...]
    out_ref[pl.ds(pl.multiple_of((1 - bit) * rows, SUBLANES), rows), :] = got_ref[...]


def spread_kernel(step, mine_ref, got_ref, *out_refs):
    mine, got = mine_ref[...], got_ref[...]
    low = own_bit(step) == 0
    joined = [jnp.where(low, mine, got), jnp.where(low, got, mine)]
    half, hidden = mine.shape
    at = 0
    for out_ref in out_refs:
        rows = out_ref.shape[0]
        for c in range(out_ref.shape[1] // hidden):
            for begin in range(0, rows, min(rows, half)):
                count = min(rows, half)
                offset = at % half
                out_ref[begin : begin + count, c * hidden : (c + 1) * hidden] = joined[at // half][
                    offset : offset + count
                ].astype(F32)
                at += count


def merge_kernel(node_ref, node_got_ref, obs_ref, obs_got_ref, grad_node_ref, grad_obs_ref):
    grad_node_ref[...] = node_ref[...] + node_got_ref[...].astype(F32)
    grad_obs_ref[...] = (obs_ref[...] + obs_got_ref[...].astype(F32)).astype(BF16)


def reduce_halving(steps, tail, slots, keep, send):
    hidden = keep.shape[1]
    for done, nxt in zip(steps[:-1], steps[1:]):
        rows = keep.shape[0] - tail
        rows = (rows // 2 if halves(rows) else rows) + tail
        keep, send = call(
            functools.partial(add_kernel, nxt, tail),
            [((rows, hidden), F32), ((rows, hidden), BF16)],
            keep, flip(send, done),
            scratch=[pltpu.VMEM(keep.shape, F32)],
        )
    rows = keep.shape[0] - tail
    return call(
        last_kernel,
        [((rows, hidden), BF16)] + ([((slots, hidden), F32)] if tail else []),
        keep, flip(send, steps[-1]),
    )


def gather_doubling(steps, rows, piece, outs):
    used = []
    for step in steps:
        if halves(rows):
            used.append(step)
            rows //= 2
    for step in used[:0:-1]:
        (piece,) = call(
            functools.partial(join_kernel, step),
            [((2 * piece.shape[0], piece.shape[1]), BF16)],
            piece, flip(piece, step),
        )
    return call(functools.partial(spread_kernel, used[0]), outs, piece, flip(piece, used[0]))


def local(obs_feat, node_state, grad_agg, owner, local_idx, slot, w_obs, w_node, slot_bias, w_out):
    owners = lax.axis_size(OWNER_AXES)
    obs, fanout = owner.shape
    nodes, width = node_state.shape
    hidden = w_obs.shape[1]
    slots = slot_bias.shape[0]
    cap = max(2, 2 * obs * fanout // owners)
    cap = -(-cap // SUBLANES) * SUBLANES
    edges = owners * cap
    half = width // 2
    slot_row = slot.reshape(1, obs)

    chunk = cap * hidden // obs + SUBLANES
    place, *packed = call_staged(
        functools.partial(pack_kernel, cap),
        [((fanout, obs), jnp.int32)] + [((chunk, obs), BF16)] * owners,
        obs_feat, owner.T, local_idx.T, slot_row, w_obs, slot_bias,
    )
    received = packed[:1] + [shift(packed[j], OWNER_AXES, j) for j in range(1, owners)]
    (table,) = call_staged(
        table_kernel, [((nodes, 4 * hidden), BF16)], node_state, grad_agg, w_node, w_out
    )
    back, act, hot = call(
        functools.partial(edge_kernel, owners, fanout),
        [((owners, cap, hidden), BF16), ((edges, 2 * hidden), BF16), ((edges, nodes), BF16)],
        *received, table,
    )
    back = exchange(back, OWNER_AXES).reshape(edges, hidden)

    steps = halving_steps()
    stack = width + width // hidden * hidden
    node_mine, node_theirs, keep, send = call(
        functools.partial(node_kernel, steps[0]),
        [((nodes, half), F32), ((nodes, half), BF16), ((stack // 2, hidden), F32), ((stack // 2, hidden), BF16)],
        hot, act, node_state, grad_agg, w_node,
        scratch=[pltpu.VMEM((stack, hidden), F32)],
    )
    (node_piece,) = reduce_halving(steps, 0, 0, keep, send)
    node_got = shift(node_theirs, "mp", 1)

    tail = -(-slots // SUBLANES) * SUBLANES
    share = width // 2 + tail
    obs_mine, obs_theirs, keep, send = call(
        functools.partial(obs_kernel, steps[0], tail),
        [((obs, half), F32), ((obs, half), BF16), ((share, hidden), F32), ((share, hidden), BF16)],
        back, place, slot_row, obs_feat, w_obs,
        scratch=[pltpu.VMEM((width + tail, hidden), F32)],
    )
    obs_piece, grad_slot = reduce_halving(steps, tail, slots, keep, send)
    obs_got = shift(obs_theirs, "mp", 1)

    grad_node, grad_obs = call(
        merge_kernel, [((nodes, half), F32), ((obs, half), BF16)],
        node_mine, node_got, obs_mine, obs_got,
    )
    grad_w_node, grad_w_out = gather_doubling(
        steps, stack, node_piece, [((width, hidden), F32), ((hidden, width), F32)]
    )
    (grad_w_obs,) = gather_doubling(steps, width, obs_piece, [((width, hidden), F32)])
    return grad_obs, grad_node, grad_w_obs, grad_w_node, grad_w_out, grad_slot


def solution(mesh):
    rows = P(("group", "obs", "node"), None)
    return jax.shard_map(
        local,
        mesh=mesh,
        in_specs=(
            rows, rows, rows, rows, rows,
            P(("group", "obs", "node")),
            P(None, "mp"), P(None, "mp"), P(None, "mp"), P("mp", None),
        ),
        out_specs=(
            P(("group", "obs", "node"), "mp"),
            P(("group", "obs", "node"), "mp"),
            P("group", "mp"),
            P("group", "mp"),
            P(("group", "mp"), None),
            P("group", "mp"),
        ),
        check_vma=False,
    )
```

time: 87 us -> 84.4 us (0.970)
  waiting for transfers between devices: 41.8 us -> 27.4 us
  starting transfers between devices: 30.3 us -> 42.4 us
    all_to_all x6 -> x1, waiting for transfers between devices: 26.2 us -> 0.01 us  [exchange(): return lax.all_to_all(blocks, axes, split_axis=0, concat_axis=0, tiled=True)]
    ppermute x0 -> x12, waiting for transfers between devices: none -> 25.9 us  [flip(): return lax.ppermute(value, axes, pairs)]
    ppermute x0 -> x12, starting transfers between devices: none -> 23.1 us  [flip(): return lax.ppermute(value, axes, pairs)]
    all_to_all x6 -> x1, starting transfers between devices: 26 us -> 5.54 us  [exchange(): return lax.all_to_all(blocks, axes, split_axis=0, concat_axis=0, tiled=True)]
    ppermute x6 -> x9, waiting for transfers between devices: 15.6 us -> 1.5 us  [shift(): lax.ppermute(value, axis, [(i, (i + step) % size) for i in range(size)])]
    ppermute x6 -> x9, starting transfers between devices: 4.34 us -> 13.8 us  [shift(): lax.ppermute(value, axis, [(i, (i + step) % size) for i in range(size)])]
    pallas_call x0 -> x2, Pallas kernels: none -> 4.83 us  [call_staged(): pl.pallas_call(staged, out_shape=[jax.ShapeDtypeStruct(shape, dtype) for...]
    pallas_call x12 -> x16, Pallas kernels: 11.6 us -> 6.88 us  [call(): pl.pallas_call(kernel, out_shape=[jax.ShapeDtypeStruct(shape, dtype) for...]
  transfers between devices with their start and end apart: 12 -> 22, of which waited for: 9 -> 10; matrix products, arithmetic and copies ran while one was open for 0% -> 0% of each run, Pallas kernels for 7% -> 8%
where the time goes in v4:
time: 84.4 us; the launch traced here: 84.1 us
  starting transfers between devices  42.4 us (50%)
  waiting for transfers between devices  27.4 us (32%)
  Pallas kernels  11.7 us (14%)
  local copies, waits for them, and re-layouts  1.79 us (2%)
    ppermute x12, waiting for transfers between devices, flip(): return lax.ppermute(value, axes, pairs)  25.9 us
    ppermute x12, starting transfers between devices, flip(): return lax.ppermute(value, axes, pairs)  23.1 us
    ppermute x9, starting transfers between devices, shift(): lax.ppermute(value, axis, [(i, (i + step) % size) for i in range(size)])  13.8 us
    pallas_call x16, Pallas kernels, call(): pl.pallas_call(kernel, out_shape=[jax.ShapeDtypeStruct(shape, dtype) for...  6.88 us
    all_to_all x1, starting transfers between devices, exchange(): return lax.all_to_all(blocks, axes, split_axis=0, concat_axis=0, tiled=True)  5.54 us
    pallas_call x2, Pallas kernels, call_staged(): pl.pallas_call(staged, out_shape=[jax.ShapeDtypeStruct(shape, dtype) for...  4.83 us
    unnamed x18, local copies, waits for them, and re-layouts  1.79 us
  transfers between devices with their start and end apart: 22, of which 10 were waited for; matrix products, arithmetic and copies ran while one was open for 0% of the time, Pallas kernels for 8%

profile of v4, /device:TPU:0, one launch (start us, length us, event | category | flops | bytes accessed | tf_op | source)
XLA Modules:
  0.0 84.1 jit_solution(17635256301970886230)
XLA Ops:
  0.6 2.4 %shard_map.145 = (s32[2,128]{1,0:T(2,128)}, bf16[144,128]{1,0:T(8,128)(2,1)}, bf16[144,128]{1,0:T(8,128)(2,1)}, bf16[144,128]{1,0:T(8,128)(2,1)}, bf16[144,128]{...) custom-call(bf16[128,512]{1,0:T(8,128)(2,1)} %obs_ref.1, ...), custom_call_target="tpu_custom_call" | custom-call | tf_op jit(solution)/shard_map/pallas_call | solution.py:50
  3.0 3.0 %collective-permute-start = (bf16[144,128]{1,0:T(8,128)(2,1)}, bf16[144,128]{1,0:T(8,128)(2,1)S(1)}, u32[]{:S(2)}, u32[]{:S(2)}) collective-permute-start(bf16[144,128]{1,0:T(8,128)(2,1)} %get-tuple-element.41), channel_id=1, source_target_pairs={{0,2},{2,4},{4,6},{6,8},{8,10},{10,12},{12,14},{14,0},{1,3},{3,5},... | collective-permute-start | bytes 110600 | tf_op jit(solution)/shard_map/ppermute | solution.py:67
  6.0 1.6 %collective-permute-start.1 = (bf16[144,128]{1,0:T(8,128)(2,1)}, bf16[144,128]{1,0:T(8,128)(2,1)S(1)}, u32[]{:S(2)}, u32[]{:S(2)}) collective-permute-start(bf16[144,128]{1,0:T(8,128)(2,1)} %get-tuple-element.42), channel_id=1, source_target_pairs={{0,4},{2,6},{4,8},{6,10},{8,12},{10,14},{12,0},{14,2},{1,5},{3,7},... | collective-permute-start | bytes 110600 | tf_op jit(solution)/shard_map/ppermute | solution.py:67
  7.6 2.6 %collective-permute-start.2 = (bf16[144,128]{1,0:T(8,128)(2,1)}, bf16[144,128]{1,0:T(8,128)(2,1)S(1)}, u32[]{:S(2)}, u32[]{:S(2)}) collective-permute-start(bf16[144,128]{1,0:T(8,128)(2,1)} %get-tuple-element.43), channel_id=1, source_target_pairs={{0,6},{2,8},{4,10},{6,12},{8,14},{10,0},{12,2},{14,4},{1,7},{3,9},... | collective-permute-start | bytes 110600 | tf_op jit(solution)/shard_map/ppermute | solution.py:67
  10.1 1.2 %collective-permute-start.3 = (bf16[144,128]{1,0:T(8,128)(2,1)}, bf16[144,128]{1,0:T(8,128)(2,1)S(1)}, u32[]{:S(2)}, u32[]{:S(2)}) collective-permute-start(bf16[144,128]{1,0:T(8,128)(2,1)} %get-tuple-element.44), channel_id=1, source_target_pairs={{0,8},{2,10},{4,12},{6,14},{8,0},{10,2},{12,4},{14,6},{1,9},{3,11}... | collective-permute-start | bytes 110600 | tf_op jit(solution)/shard_map/ppermute | solution.py:67
  11.4 2.6 %collective-permute-start.4 = (bf16[144,128]{1,0:T(8,128)(2,1)}, bf16[144,128]{1,0:T(8,128)(2,1)S(1)}, u32[]{:S(2)}, u32[]{:S(2)}) collective-permute-start(bf16[144,128]{1,0:T(8,128)(2,1)} %get-tuple-element.45), channel_id=1, source_target_pairs={{0,10},{2,12},{4,14},{6,0},{8,2},{10,4},{12,6},{14,8},{1,11},{3,13... | collective-permute-start | bytes 110600 | tf_op jit(solution)/shard_map/ppermute | solution.py:67
  14.0 1.3 %collective-permute-start.5 = (bf16[144,128]{1,0:T(8,128)(2,1)}, bf16[144,128]{1,0:T(8,128)(2,1)S(1)}, u32[]{:S(2)}, u32[]{:S(2)}) collective-permute-start(bf16[144,128]{1,0:T(8,128)(2,1)} %get-tuple-element.46), channel_id=1, source_target_pairs={{0,12},{2,14},{4,0},{6,2},{8,4},{10,6},{12,8},{14,10},{1,13},{3,15... | collective-permute-start | bytes 110600 | tf_op jit(solution)/shard_map/ppermute | solution.py:67
  15.4 0.0 collective-permute-done.1.refs_2_
  15.4 1.4 %collective-permute-start.6 = (bf16[144,128]{1,0:T(8,128)(2,1)}, bf16[144,128]{1,0:T(8,128)(2,1)S(1)}, u32[]{:S(2)}, u32[]{:S(2)}) collective-permute-start(bf16[144,128]{1,0:T(8,128)(2,1)} %get-tuple-element.47), channel_id=1, source_target_pairs={{0,14},{2,0},{4,2},{6,4},{8,6},{10,8},{12,10},{14,12},{1,15},{3,1}... | collective-permute-start | bytes 110600 | tf_op jit(solution)/shard_map/ppermute | solution.py:67
  16.8 2.5 %shard_map.146.refs_8_ = bf16[320,1024]{1,0:T(8,128)(2,1)} custom-call(bf16[320,512]{1,0:T(8,128)(2,1)} %state_ref.1, bf16[320,512]{1,0:T(8,128)(2,1)} %agg_ref.1, bf16[512,256]{1,0:T(8,128)(2,1)} %w_node_ref.1, bf16[256,512]{1,0:T(8,128)(2,1)} %refs_3_.1), custom_call_target="tpu_custom_call" | custom-call | tf_op jit(solution)/shard_map/pallas_call | solution.py:50
  19.3 0.0 collective-permute-done.3.refs_4_
  19.3 0.0 collective-permute-done.4.refs_5_
  19.3 0.2 collective-permute-done.6.refs_7_
  19.5 1.1 %copy-done = bf16[320,1024]{1,0:T(8,128)(2,1)S(1)} copy-done((bf16[320,1024]{1,0:T(8,128)(2,1)S(1)}, bf16[320,1024]{1,0:T(8,128)(2,1)}, u32[]{:S(2)}) %copy-start) | copy-done | bytes 655384
  20.6 1.7 %shard_map.147 = (bf16[8,64,256]{2,1,0:T(8,128)(2,1)}, bf16[512,512]{1,0:T(8,128)(2,1)S(1)}, bf16[512,320]{1,0:T(8,128)(2,1)S(1)}) custom-call(bf16[144,128]{1,0:T(8,128)(2,1)S(1)} %copy-done.6, bf16[144,128]{1,0:T(8,128)(2,1)S(1)} %collective-permute-done.refs_1_, bf16[144,128]{1,0:T(8,128)(2,1)S(1)} %collective-permute-done.1.refs_2_, ...), custom_call_target="tpu_custom_call" | custom-call | tf_op jit(solution)/shard_map/pallas_call | solution.py:28
  22.4 5.5 %all-to-all-start = ((bf16[8,64,256]{2,1,0:T(8,128)(2,1)}), bf16[8,64,256]{2,1,0:T(8,128)(2,1)S(1)}, u32[]{:S(2)}, u32[]{:S(2)}) async-start(bf16[8,64,256]{2,1,0:T(8,128)(2,1)} %get-tuple-element.52), calls=%async_computation | async-start | bytes 524288 | tf_op jit(solution)/shard_map/all_to_all | solution.py:62
  27.9 1.0 %shard_map.148 = (f32[320,256]{1,0:T(8,128)S(1)}, bf16[320,256]{1,0:T(8,128)(2,1)S(1)}, f32[512,256]{1,0:T(8,128)S(1)}, bf16[512,256]{1,0:T(8,128)(2,1)S(1)}) custom-call(bf16[512,320]{1,0:T(8,128)(2,1)S(1)} %get-tuple-element.48.hot_ref, bf16[512,512]{1,0:T(8,128)(2,1)S(1)} %get-tuple-element.49.act_ref, bf16[320,512]{1,0:T(8,128)(2,1)S(1)} %copy-done.1, ...), custom_call_target="tpu_custom_call" | custom-call | tf_op jit(solution)/shard_map/pallas_call | solution.py:28
  28.9 2.1 %collective-permute-start.15 = (bf16[512,256]{1,0:T(8,128)(2,1)S(1)}, bf16[512,256]{1,0:T(8,128)(2,1)S(1)}, u32[]{:S(2)}, u32[]{:S(2)}) collective-permute-start(bf16[512,256]{1,0:T(8,128)(2,1)S(1)} %get-tuple-element.66), channel_id=1, source_target_pairs={{0,2},{1,5},{2,0},{3,7},{4,6},{5,1},{6,4},{7,3},{8,10},{9,13},{10,... | collective-permute-start | bytes 786440 | tf_op jit(solution)/shard_map/ppermute | solution.py:187
  31.0 5.1 %collective-permute-done.15.got_ref = bf16[512,256]{1,0:T(8,128)(2,1)S(1)} collective-permute-done((bf16[512,256]{1,0:T(8,128)(2,1)S(1)}, bf16[512,256]{1,0:T(8,128)(2,1)S(1)}, u32[]{:S(2)}, u32[]{:S(2)}) %collective-permute-start.15) | collective-permute-done | bytes 262176 | tf_op jit(solution)/shard_map/ppermute | solution.py:187
  36.1 0.1 shard_map.157
  36.2 0.0 copy-start.4
  36.2 3.1 %collective-permute-start.16 = (bf16[256,256]{1,0:T(8,128)(2,1)S(1)}, bf16[256,256]{1,0:T(8,128)(2,1)S(1)}, u32[]{:S(2)}, u32[]{:S(2)}) collective-permute-start(bf16[256,256]{1,0:T(8,128)(2,1)S(1)} %get-tuple-element.68), channel_id=1, source_target_pairs={{0,4},{1,3},{2,6},{3,1},{4,0},{5,7},{6,2},{7,5},{8,12},{9,11},{10,... | collective-permute-start | bytes 393224 | tf_op jit(solution)/shard_map/ppermute | solution.py:187
  39.4 3.6 %collective-permute-done.16.got_ref = bf16[256,256]{1,0:T(8,128)(2,1)S(1)} collective-permute-done((bf16[256,256]{1,0:T(8,128)(2,1)S(1)}, bf16[256,256]{1,0:T(8,128)(2,1)S(1)}, u32[]{:S(2)}, u32[]{:S(2)}) %collective-permute-start.16) | collective-permute-done | bytes 131104 | tf_op jit(solution)/shard_map/ppermute | solution.py:187
  43.1 1.9 %collective-permute-start.17 = (bf16[128,256]{1,0:T(8,128)(2,1)S(1)}, bf16[128,256]{1,0:T(8,128)(2,1)S(1)}, u32[]{:S(2)}, u32[]{:S(2)}) collective-permute-start(bf16[128,256]{1,0:T(8,128)(2,1)S(1)} %get-tuple-element.70), channel_id=1, source_target_pairs={{0,8},{1,9},{2,10},{3,11},{4,12},{5,13},{6,14},{7,15},{8,0},{9,1},... | collective-permute-start | bytes 196616 | tf_op jit(solution)/shard_map/ppermute | solution.py:187
  44.9 0.6 copy-done.7
  45.6 0.0 copy-done.8
  45.6 0.6 shard_map.149
  46.2 1.1 %collective-permute-start.9 = (bf16[272,256]{1,0:T(8,128)(2,1)S(1)}, bf16[272,256]{1,0:T(8,128)(2,1)S(1)}, u32[]{:S(2)}, u32[]{:S(2)}) collective-permute-start(bf16[272,256]{1,0:T(8,128)(2,1)S(1)} %get-tuple-element.59), channel_id=1, source_target_pairs={{0,2},{1,5},{2,0},{3,7},{4,6},{5,1},{6,4},{7,3},{8,10},{9,13},{10,... | collective-permute-start | bytes 417800 | tf_op jit(solution)/shard_map/ppermute | solution.py:187
  47.3 1.5 %collective-permute-done.17.got_ref = bf16[128,256]{1,0:T(8,128)(2,1)S(1)} collective-permute-done((bf16[128,256]{1,0:T(8,128)(2,1)S(1)}, bf16[128,256]{1,0:T(8,128)(2,1)S(1)}, u32[]{:S(2)}, u32[]{:S(2)}) %collective-permute-start.17) | collective-permute-done | bytes 65568 | tf_op jit(solution)/shard_map/ppermute | solution.py:187
  48.9 1.3 %collective-permute-start.18 = (bf16[128,256]{1,0:T(8,128)(2,1)S(1)}, bf16[128,256]{1,0:T(8,128)(2,1)S(1)}, u32[]{:S(2)}, u32[]{:S(2)}) collective-permute-start(bf16[128,256]{1,0:T(8,128)(2,1)S(1)} %shard_map.159.mine_ref), channel_id=1, source_target_pairs={{0,8},{1,9},{2,10},{3,11},{4,12},{5,13},{6,14},{7,15},{8,0},{9,1},... | collective-permute-start | bytes 196616 | tf_op jit(solution)/shard_map/ppermute | solution.py:187
  50.2 4.0 %collective-permute-done.18.got_ref = bf16[128,256]{1,0:T(8,128)(2,1)S(1)} collective-permute-done((bf16[128,256]{1,0:T(8,128)(2,1)S(1)}, bf16[128,256]{1,0:T(8,128)(2,1)S(1)}, u32[]{:S(2)}, u32[]{:S(2)}) %collective-permute-start.18) | collective-permute-done | bytes 65568 | tf_op jit(solution)/shard_map/ppermute | solution.py:187
  54.2 1.4 %collective-permute-start.19 = (bf16[256,256]{1,0:T(8,128)(2,1)S(1)}, bf16[256,256]{1,0:T(8,128)(2,1)S(1)}, u32[]{:S(2)}, u32[]{:S(2)}) collective-permute-start(bf16[256,256]{1,0:T(8,128)(2,1)S(1)} %shard_map.160.mine_ref), channel_id=1, source_target_pairs={{0,4},{1,3},{2,6},{3,1},{4,0},{5,7},{6,2},{7,5},{8,12},{9,11},{10,... | collective-permute-start | bytes 393224 | tf_op jit(solution)/shard_map/ppermute | solution.py:187
  55.6 0.1 shard_map.151
  55.7 0.7 collective-permute-start.10
  56.4 5.2 %collective-permute-done.10.got_ref = bf16[144,256]{1,0:T(8,128)(2,1)S(1)} collective-permute-done((bf16[144,256]{1,0:T(8,128)(2,1)S(1)}, bf16[144,256]{1,0:T(8,128)(2,1)S(1)}, u32[]{:S(2)}, u32[]{:S(2)}) %collective-permute-start.10) | collective-permute-done | bytes 73760 | tf_op jit(solution)/shard_map/ppermute | solution.py:187
  61.6 2.5 %collective-permute-start.11 = (bf16[80,256]{1,0:T(8,128)(2,1)S(1)}, bf16[80,256]{1,0:T(8,128)(2,1)S(1)}, u32[]{:S(2)}, u32[]{:S(2)}) collective-permute-start(bf16[80,256]{1,0:T(8,128)(2,1)S(1)} %get-tuple-element.63), channel_id=1, source_target_pairs={{0,8},{1,9},{2,10},{3,11},{4,12},{5,13},{6,14},{7,15},{8,0},{9,1},... | collective-permute-start | bytes 122888 | tf_op jit(solution)/shard_map/ppermute | solution.py:187
  64.2 0.7 collective-permute-start.20
  64.9 1.7 %collective-permute-done.11.got_ref = bf16[80,256]{1,0:T(8,128)(2,1)S(1)} collective-permute-done((bf16[80,256]{1,0:T(8,128)(2,1)S(1)}, bf16[80,256]{1,0:T(8,128)(2,1)S(1)}, u32[]{:S(2)}, u32[]{:S(2)}) %collective-permute-start.11) | collective-permute-done | bytes 40992 | tf_op jit(solution)/shard_map/ppermute | solution.py:187
  66.6 0.6 shard_map.153
  67.2 2.5 %collective-permute-start.12 = (bf16[64,256]{1,0:T(8,128)(2,1)S(1)}, bf16[64,256]{1,0:T(8,128)(2,1)S(1)}, u32[]{:S(2)}, u32[]{:S(2)}) collective-permute-start(bf16[64,256]{1,0:T(8,128)(2,1)S(1)} %get-tuple-element.64.mine_ref), channel_id=1, source_target_pairs={{0,8},{1,9},{2,10},{3,11},{4,12},{5,13},{6,14},{7,15},{8,0},{9,1},... | collective-permute-start | bytes 98312 | tf_op jit(solution)/shard_map/ppermute | solution.py:187
  69.6 2.3 %collective-permute-done.12.got_ref = bf16[64,256]{1,0:T(8,128)(2,1)S(1)} collective-permute-done((bf16[64,256]{1,0:T(8,128)(2,1)S(1)}, bf16[64,256]{1,0:T(8,128)(2,1)S(1)}, u32[]{:S(2)}, u32[]{:S(2)}) %collective-permute-start.12) | collective-permute-done | bytes 32800 | tf_op jit(solution)/shard_map/ppermute | solution.py:187
  72.0 2.1 %collective-permute-start.13 = (bf16[128,256]{1,0:T(8,128)(2,1)S(1)}, bf16[128,256]{1,0:T(8,128)(2,1)S(1)}, u32[]{:S(2)}, u32[]{:S(2)}) collective-permute-start(bf16[128,256]{1,0:T(8,128)(2,1)S(1)} %shard_map.154.mine_ref), channel_id=1, source_target_pairs={{0,4},{1,3},{2,6},{3,1},{4,0},{5,7},{6,2},{7,5},{8,12},{9,11},{10,... | collective-permute-start | bytes 196616 | tf_op jit(solution)/shard_map/ppermute | solution.py:187
  74.1 2.5 %collective-permute-done.13.got_ref = bf16[128,256]{1,0:T(8,128)(2,1)S(1)} collective-permute-done((bf16[128,256]{1,0:T(8,128)(2,1)S(1)}, bf16[128,256]{1,0:T(8,128)(2,1)S(1)}, u32[]{:S(2)}, u32[]{:S(2)}) %collective-permute-start.13) | collective-permute-done | bytes 65568 | tf_op jit(solution)/shard_map/ppermute | solution.py:187
  76.6 3.6 %collective-permute-start.14 = (bf16[256,256]{1,0:T(8,128)(2,1)S(1)}, bf16[256,256]{1,0:T(8,128)(2,1)S(1)}, u32[]{:S(2)}, u32[]{:S(2)}) collective-permute-start(bf16[256,256]{1,0:T(8,128)(2,1)S(1)} %shard_map.155.mine_ref), channel_id=1, source_target_pairs={{0,2},{1,5},{2,0},{3,7},{4,6},{5,1},{6,4},{7,3},{8,10},{9,13},{10,... | collective-permute-start | bytes 393224 | tf_op jit(solution)/shard_map/ppermute | solution.py:187
  80.2 1.2 %collective-permute-done.8.obs_got_ref = bf16[128,256]{1,0:T(8,128)(2,1)S(1)} collective-permute-done((bf16[128,256]{1,0:T(8,128)(2,1)S(1)}, bf16[128,256]{1,0:T(8,128)(2,1)S(1)}, u32[]{:S(2)}, u32[]{:S(2)}) %collective-permute-start.8) | collective-permute-done | bytes 65568 | tf_op jit(solution)/shard_map/ppermute | solution.py:67
  81.5 0.8 shard_map.150
  82.2 1.0 %shard_map.162 = (f32[512,256]{1,0:T(8,128)}, f32[256,512]{1,0:T(8,128)}) custom-call(bf16[512,256]{1,0:T(8,128)(2,1)S(1)} %shard_map.161.mine_ref, bf16[512,256]{1,0:T(8,128)(2,1)S(1)} %collective-permute-done.20.got_ref), custom_call_target="tpu_custom_call" | custom-call | tf_op jit(solution)/shard_map/pallas_call | solution.py:28
  83.3 0.8 shard_map.156
  (32 shorter events, 0.2 us)
Async XLA Ops:
  3.0 11.0 %collective-permute-start = (bf16[144,128]{1,0:T(8,128)(2,1)}, bf16[144,128]{1,0:T(8,128)(2,1)S(1)}, u32[]{:S(2)}, u32[]{:S(2)}) collective-permute-start(bf16[144,128]{1,0:T(8,128)(2,1)} %get-tuple-element.41), channel_id=1, source_target_pairs={{0,2},{2,4},{4,6},{6,8},{8,10},{10,12},{12,14},{14,0},{1,3},{3,5},... | collective-permute-start | bytes 110600 | tf_op jit(solution)/shard_map/ppermute | solution.py:67
  6.0 9.3 %collective-permute-start.1 = (bf16[144,128]{1,0:T(8,128)(2,1)}, bf16[144,128]{1,0:T(8,128)(2,1)S(1)}, u32[]{:S(2)}, u32[]{:S(2)}) collective-permute-start(bf16[144,128]{1,0:T(8,128)(2,1)} %get-tuple-element.42), channel_id=1, source_target_pairs={{0,4},{2,6},{4,8},{6,10},{8,12},{10,14},{12,0},{14,2},{1,5},{3,7},... | collective-permute-start | bytes 110600 | tf_op jit(solution)/shard_map/ppermute | solution.py:67
  7.6 11.7 %collective-permute-start.2 = (bf16[144,128]{1,0:T(8,128)(2,1)}, bf16[144,128]{1,0:T(8,128)(2,1)S(1)}, u32[]{:S(2)}, u32[]{:S(2)}) collective-permute-start(bf16[144,128]{1,0:T(8,128)(2,1)} %get-tuple-element.43), channel_id=1, source_target_pairs={{0,6},{2,8},{4,10},{6,12},{8,14},{10,0},{12,2},{14,4},{1,7},{3,9},... | collective-permute-start | bytes 110600 | tf_op jit(solution)/shard_map/ppermute | solution.py:67
  10.1 9.1 %collective-permute-start.3 = (bf16[144,128]{1,0:T(8,128)(2,1)}, bf16[144,128]{1,0:T(8,128)(2,1)S(1)}, u32[]{:S(2)}, u32[]{:S(2)}) collective-permute-start(bf16[144,128]{1,0:T(8,128)(2,1)} %get-tuple-element.44), channel_id=1, source_target_pairs={{0,8},{2,10},{4,12},{6,14},{8,0},{10,2},{12,4},{14,6},{1,9},{3,11}... | collective-permute-start | bytes 110600 | tf_op jit(solution)/shard_map/ppermute | solution.py:67
  11.4 7.9 %collective-permute-start.4 = (bf16[144,128]{1,0:T(8,128)(2,1)}, bf16[144,128]{1,0:T(8,128)(2,1)S(1)}, u32[]{:S(2)}, u32[]{:S(2)}) collective-permute-start(bf16[144,128]{1,0:T(8,128)(2,1)} %get-tuple-element.45), channel_id=1, source_target_pairs={{0,10},{2,12},{4,14},{6,0},{8,2},{10,4},{12,6},{14,8},{1,11},{3,13... | collective-permute-start | bytes 110600 | tf_op jit(solution)/shard_map/ppermute | solution.py:67
  14.0 5.3 %collective-permute-start.5 = (bf16[144,128]{1,0:T(8,128)(2,1)}, bf16[144,128]{1,0:T(8,128)(2,1)S(1)}, u32[]{:S(2)}, u32[]{:S(2)}) collective-permute-start(bf16[144,128]{1,0:T(8,128)(2,1)} %get-tuple-element.46), channel_id=1, source_target_pairs={{0,12},{2,14},{4,0},{6,2},{8,4},{10,6},{12,8},{14,10},{1,13},{3,15... | collective-permute-start | bytes 110600 | tf_op jit(solution)/shard_map/ppermute | solution.py:67
  15.4 4.2 %copy-start.6 = (bf16[144,128]{1,0:T(8,128)(2,1)S(1)}, bf16[144,128]{1,0:T(8,128)(2,1)}, u32[]{:S(2)}) copy-start(bf16[144,128]{1,0:T(8,128)(2,1)} %get-tuple-element.40.refs_0_) | copy-start | bytes 110596
  15.4 4.2 %collective-permute-start.6 = (bf16[144,128]{1,0:T(8,128)(2,1)}, bf16[144,128]{1,0:T(8,128)(2,1)S(1)}, u32[]{:S(2)}, u32[]{:S(2)}) collective-permute-start(bf16[144,128]{1,0:T(8,128)(2,1)} %get-tuple-element.47), channel_id=1, source_target_pairs={{0,14},{2,0},{4,2},{6,4},{8,6},{10,8},{12,10},{14,12},{1,15},{3,1}... | collective-permute-start | bytes 110600 | tf_op jit(solution)/shard_map/ppermute | solution.py:67
  19.5 1.1 %copy-start = (bf16[320,1024]{1,0:T(8,128)(2,1)S(1)}, bf16[320,1024]{1,0:T(8,128)(2,1)}, u32[]{:S(2)}) copy-start(bf16[320,1024]{1,0:T(8,128)(2,1)} %shard_map.146.refs_8_) | copy-start | bytes 1966084
  20.6 7.3 %copy-start.2 = (bf16[320,512]{1,0:T(8,128)(2,1)S(1)}, bf16[320,512]{1,0:T(8,128)(2,1)}, u32[]{:S(2)}) copy-start(bf16[320,512]{1,0:T(8,128)(2,1)} %agg_ref.1) | copy-start | bytes 983044
  20.6 7.3 %copy-start.3 = (bf16[512,256]{1,0:T(8,128)(2,1)S(1)}, bf16[512,256]{1,0:T(8,128)(2,1)}, u32[]{:S(2)}) copy-start(bf16[512,256]{1,0:T(8,128)(2,1)} %w_node_ref.1) | copy-start | bytes 786436
  22.4 5.6 %copy-start.1 = (bf16[320,512]{1,0:T(8,128)(2,1)S(1)}, bf16[320,512]{1,0:T(8,128)(2,1)}, u32[]{:S(2)}) copy-start(bf16[320,512]{1,0:T(8,128)(2,1)} %state_ref.1) | copy-start | bytes 983044
  22.4 22.5 %all-to-all-start = ((bf16[8,64,256]{2,1,0:T(8,128)(2,1)}), bf16[8,64,256]{2,1,0:T(8,128)(2,1)S(1)}, u32[]{:S(2)}, u32[]{:S(2)}) async-start(bf16[8,64,256]{2,1,0:T(8,128)(2,1)} %get-tuple-element.52), calls=%async_computation | async-start | bytes 524288 | tf_op jit(solution)/shard_map/all_to_all | solution.py:62
  28.9 7.1 %collective-permute-start.15 = (bf16[512,256]{1,0:T(8,128)(2,1)S(1)}, bf16[512,256]{1,0:T(8,128)(2,1)S(1)}, u32[]{:S(2)}, u32[]{:S(2)}) collective-permute-start(bf16[512,256]{1,0:T(8,128)(2,1)S(1)} %get-tuple-element.66), channel_id=1, source_target_pairs={{0,2},{1,5},{2,0},{3,7},{4,6},{5,1},{6,4},{7,3},{8,10},{9,13},{10,... | collective-permute-start | bytes 786440 | tf_op jit(solution)/shard_map/ppermute | solution.py:187
  36.2 8.7 %copy-start.4 = (bf16[512,256]{1,0:T(8,128)(2,1)S(1)}, bf16[512,256]{1,0:T(8,128)(2,1)}, u32[]{:S(2)}) copy-start(bf16[512,256]{1,0:T(8,128)(2,1)} %w_ref.1) | copy-start | bytes 786436
  36.2 6.8 %collective-permute-start.16 = (bf16[256,256]{1,0:T(8,128)(2,1)S(1)}, bf16[256,256]{1,0:T(8,128)(2,1)S(1)}, u32[]{:S(2)}, u32[]{:S(2)}) collective-permute-start(bf16[256,256]{1,0:T(8,128)(2,1)S(1)} %get-tuple-element.68), channel_id=1, source_target_pairs={{0,4},{1,3},{2,6},{3,1},{4,0},{5,7},{6,2},{7,5},{8,12},{9,11},{10,... | collective-permute-start | bytes 393224 | tf_op jit(solution)/shard_map/ppermute | solution.py:187
  43.0 1.9 %copy-start.5 = (bf16[128,512]{1,0:T(8,128)(2,1)S(1)}, bf16[128,512]{1,0:T(8,128)(2,1)}, u32[]{:S(2)}) copy-start(bf16[128,512]{1,0:T(8,128)(2,1)} %obs_ref.1) | copy-start | bytes 393220
  43.1 5.8 %collective-permute-start.17 = (bf16[128,256]{1,0:T(8,128)(2,1)S(1)}, bf16[128,256]{1,0:T(8,128)(2,1)S(1)}, u32[]{:S(2)}, u32[]{:S(2)}) collective-permute-start(bf16[128,256]{1,0:T(8,128)(2,1)S(1)} %get-tuple-element.70), channel_id=1, source_target_pairs={{0,8},{1,9},{2,10},{3,11},{4,12},{5,13},{6,14},{7,15},{8,0},{9,1},... | collective-permute-start | bytes 196616 | tf_op jit(solution)/shard_map/ppermute | solution.py:187
  44.9 0.7 copy-start.7
  44.9 0.7 copy-start.8
  46.2 9.4 %collective-permute-start.9 = (bf16[272,256]{1,0:T(8,128)(2,1)S(1)}, bf16[272,256]{1,0:T(8,128)(2,1)S(1)}, u32[]{:S(2)}, u32[]{:S(2)}) collective-permute-start(bf16[272,256]{1,0:T(8,128)(2,1)S(1)} %get-tuple-element.59), channel_id=1, source_target_pairs={{0,2},{1,5},{2,0},{3,7},{4,6},{5,1},{6,4},{7,3},{8,10},{9,13},{10,... | collective-permute-start | bytes 417800 | tf_op jit(solution)/shard_map/ppermute | solution.py:187
  48.9 5.2 %collective-permute-start.18 = (bf16[128,256]{1,0:T(8,128)(2,1)S(1)}, bf16[128,256]{1,0:T(8,128)(2,1)S(1)}, u32[]{:S(2)}, u32[]{:S(2)}) collective-permute-start(bf16[128,256]{1,0:T(8,128)(2,1)S(1)} %shard_map.159.mine_ref), channel_id=1, source_target_pairs={{0,8},{1,9},{2,10},{3,11},{4,12},{5,13},{6,14},{7,15},{8,0},{9,1},... | collective-permute-start | bytes 196616 | tf_op jit(solution)/shard_map/ppermute | solution.py:187
  54.2 10.0 %collective-permute-start.19 = (bf16[256,256]{1,0:T(8,128)(2,1)S(1)}, bf16[256,256]{1,0:T(8,128)(2,1)S(1)}, u32[]{:S(2)}, u32[]{:S(2)}) collective-permute-start(bf16[256,256]{1,0:T(8,128)(2,1)S(1)} %shard_map.160.mine_ref), channel_id=1, source_target_pairs={{0,4},{1,3},{2,6},{3,1},{4,0},{5,7},{6,2},{7,5},{8,12},{9,11},{10,... | collective-permute-start | bytes 393224 | tf_op jit(solution)/shard_map/ppermute | solution.py:187
  55.7 5.9 %collective-permute-start.10 = (bf16[144,256]{1,0:T(8,128)(2,1)S(1)}, bf16[144,256]{1,0:T(8,128)(2,1)S(1)}, u32[]{:S(2)}, u32[]{:S(2)}) collective-permute-start(bf16[144,256]{1,0:T(8,128)(2,1)S(1)} %get-tuple-element.61), channel_id=1, source_target_pairs={{0,4},{1,3},{2,6},{3,1},{4,0},{5,7},{6,2},{7,5},{8,12},{9,11},{10,... | collective-permute-start | bytes 221192 | tf_op jit(solution)/shard_map/ppermute | solution.py:187
  61.6 5.0 %collective-permute-start.11 = (bf16[80,256]{1,0:T(8,128)(2,1)S(1)}, bf16[80,256]{1,0:T(8,128)(2,1)S(1)}, u32[]{:S(2)}, u32[]{:S(2)}) collective-permute-start(bf16[80,256]{1,0:T(8,128)(2,1)S(1)} %get-tuple-element.63), channel_id=1, source_target_pairs={{0,8},{1,9},{2,10},{3,11},{4,12},{5,13},{6,14},{7,15},{8,0},{9,1},... | collective-permute-start | bytes 122888 | tf_op jit(solution)/shard_map/ppermute | solution.py:187
  64.2 18.1 %collective-permute-start.20 = (bf16[512,256]{1,0:T(8,128)(2,1)S(1)}, bf16[512,256]{1,0:T(8,128)(2,1)S(1)}, u32[]{:S(2)}, u32[]{:S(2)}) collective-permute-start(bf16[512,256]{1,0:T(8,128)(2,1)S(1)} %shard_map.161.mine_ref), channel_id=1, source_target_pairs={{0,2},{1,5},{2,0},{3,7},{4,6},{5,1},{6,4},{7,3},{8,10},{9,13},{10,... | collective-permute-start | bytes 786440 | tf_op jit(solution)/shard_map/ppermute | solution.py:187
  67.2 4.8 %collective-permute-start.12 = (bf16[64,256]{1,0:T(8,128)(2,1)S(1)}, bf16[64,256]{1,0:T(8,128)(2,1)S(1)}, u32[]{:S(2)}, u32[]{:S(2)}) collective-permute-start(bf16[64,256]{1,0:T(8,128)(2,1)S(1)} %get-tuple-element.64.mine_ref), channel_id=1, source_target_pairs={{0,8},{1,9},{2,10},{3,11},{4,12},{5,13},{6,14},{7,15},{8,0},{9,1},... | collective-permute-start | bytes 98312 | tf_op jit(solution)/shard_map/ppermute | solution.py:187
  72.0 4.6 %collective-permute-start.13 = (bf16[128,256]{1,0:T(8,128)(2,1)S(1)}, bf16[128,256]{1,0:T(8,128)(2,1)S(1)}, u32[]{:S(2)}, u32[]{:S(2)}) collective-permute-start(bf16[128,256]{1,0:T(8,128)(2,1)S(1)} %shard_map.154.mine_ref), channel_id=1, source_target_pairs={{0,4},{1,3},{2,6},{3,1},{4,0},{5,7},{6,2},{7,5},{8,12},{9,11},{10,... | collective-permute-start | bytes 196616 | tf_op jit(solution)/shard_map/ppermute | solution.py:187
  74.1 6.1 %collective-permute-start.7 = (bf16[320,256]{1,0:T(8,128)(2,1)S(1)}, bf16[320,256]{1,0:T(8,128)(2,1)S(1)}, u32[]{:S(2)}, u32[]{:S(2)}) collective-permute-start(bf16[320,256]{1,0:T(8,128)(2,1)S(1)} %get-tuple-element.51), channel_id=1, source_target_pairs={{0,1},{1,0},{2,3},{3,2},{4,5},{5,4},{6,7},{7,6},{8,9},{9,8},{10,11... | collective-permute-start | bytes 491528 | tf_op jit(solution)/shard_map/ppermute | solution.py:67
  76.6 6.7 %collective-permute-start.14 = (bf16[256,256]{1,0:T(8,128)(2,1)S(1)}, bf16[256,256]{1,0:T(8,128)(2,1)S(1)}, u32[]{:S(2)}, u32[]{:S(2)}) collective-permute-start(bf16[256,256]{1,0:T(8,128)(2,1)S(1)} %shard_map.155.mine_ref), channel_id=1, source_target_pairs={{0,2},{1,5},{2,0},{3,7},{4,6},{5,1},{6,4},{7,3},{8,10},{9,13},{10,... | collective-permute-start | bytes 393224 | tf_op jit(solution)/shard_map/ppermute | solution.py:187
  80.2 1.3 %collective-permute-start.8 = (bf16[128,256]{1,0:T(8,128)(2,1)S(1)}, bf16[128,256]{1,0:T(8,128)(2,1)S(1)}, u32[]{:S(2)}, u32[]{:S(2)}) collective-permute-start(bf16[128,256]{1,0:T(8,128)(2,1)S(1)} %get-tuple-element.55), channel_id=1, source_target_pairs={{0,1},{1,0},{2,3},{3,2},{4,5},{5,4},{6,7},{7,6},{8,9},{9,8},{10,11... | collective-permute-start | bytes 196616 | tf_op jit(solution)/shard_map/ppermute | solution.py:67

commit v5 on v4

v5 whole, which is shorter than its diff:
```python
import functools

import jax
import jax.numpy as jnp
from jax import lax
from jax.experimental import pallas as pl
from jax.experimental.pallas import tpu as pltpu
from jax.sharding import PartitionSpec as P

OWNER_AXES = ("obs", "node")
SUBLANES = 16
BUNDLES = 1
BF16 = jnp.bfloat16
F32 = jnp.float32


def dot(left, right, left_dim=1, right_dim=0):
    return lax.dot_general(
        left, right, (((left_dim,), (right_dim,)), ((), ())), preferred_element_type=F32
    )


def iota(shape, dim):
    return lax.broadcasted_iota(jnp.int32, shape, dim)


def call(kernel, outs, *args, scratch=(), after=()):
    vmem = pl.BlockSpec(memory_space=pltpu.VMEM)
    count = len(args)
    specs = [vmem] * count + [pl.BlockSpec(memory_space=pl.ANY)] * len(after)
    args += tuple(after)
    return pl.pallas_call(
        lambda *refs: kernel(*refs[:count], *refs[len(args) :]),
        out_shape=[jax.ShapeDtypeStruct(shape, dtype) for shape, dtype in outs],
        in_specs=specs,
        out_specs=[vmem] * len(outs),
        scratch_shapes=list(scratch),
        compiler_params=pltpu.CompilerParams(vmem_limit_bytes=40 << 20),
    )(*args)


def call_staged(kernel, outs, *args, held=()):
    count = len(args)
    sources = list(args) + [a for a in held if not any(a is b for b in args)]
    kept = [next(i for i, b in enumerate(sources) if a is b) for a in held]
    rest = [i for i in range(len(sources)) if i not in kept]

    def staged(*refs):
        hbm, refs = refs[: len(sources)], refs[len(sources) :]
        out_refs, refs = refs[: len(outs)], refs[len(outs) :]
        buffers = dict(zip(kept, refs[: len(kept)])) | dict(zip(rest, refs[len(kept) : -1]))
        copies = [
            pltpu.make_async_copy(hbm[i], buffers[i], refs[-1].at[i]) for i in range(len(sources))
        ]
        for copy in copies:
            copy.start()
        for copy in copies:
            copy.wait()
        kernel(*[buffers[i] for i in range(count)], *out_refs)

    return pl.pallas_call(
        staged,
        out_shape=[jax.ShapeDtypeStruct(shape, dtype) for shape, dtype in outs]
        + [jax.ShapeDtypeStruct(a.shape, a.dtype) for a in held],
        in_specs=[pl.BlockSpec(memory_space=pltpu.HBM)] * len(sources),
        out_specs=[pl.BlockSpec(memory_space=pltpu.VMEM)] * (len(outs) + len(held)),
        scratch_shapes=[pltpu.VMEM(sources[i].shape, sources[i].dtype) for i in rest]
        + [pltpu.SemaphoreType.DMA((len(sources),))],
        compiler_params=pltpu.CompilerParams(vmem_limit_bytes=40 << 20),
    )(*[pltpu.with_memory_space_constraint(a, pltpu.HBM) for a in sources])


def exchange(blocks, axes):
    return lax.all_to_all(blocks, axes, split_axis=0, concat_axis=0, tiled=True)


def shift(value, axis, step):
    size = lax.axis_size(axis)
    return lax.ppermute(value, axis, [(i, (i + step) % size) for i in range(size)])


def other_half(ref):
    half = ref.shape[0] // 2
    me = lax.axis_index("mp")
    mine = ref[pl.ds(pl.multiple_of(me * half, half), half), :]
    theirs = ref[pl.ds(pl.multiple_of((1 - me) * half, half), half), :]
    return mine, theirs


def column_half(ref, which):
    half = ref.shape[1] // 2
    return ref[:, pl.ds(pl.multiple_of(which * half, 128), half)]


def pack_kernel(cap, obs_ref, owner_ref, index_ref, slot_ref, place_ref, other_ref, *outs):
    owners = len(outs)
    chunk, lanes = outs[0].shape
    fanout, obs = owner_ref.shape
    owner, index = owner_ref[...], index_ref[...]
    hits = [iota((owners, obs), 0) == owner[k : k + 1] for k in range(fanout)]
    count = functools.reduce(jnp.add, [h.astype(F32) for h in hits])
    before = dot(count, (iota((obs, obs), 0) < iota((obs, obs), 1)).astype(F32))
    header = jnp.where(iota((SUBLANES, obs), 0) == 4 * fanout, slot_ref[...].astype(F32), 0.0)
    places = []
    for k in range(fanout):
        rank = jnp.sum(jnp.where(hits[k], before, 0.0), axis=0, keepdims=True)
        places.append(owner[k : k + 1] * cap + rank.astype(jnp.int32))
        place_ref[k : k + 1, :] = places[k]
        plus = index[k : k + 1] + 1
        fields = (owner[k : k + 1].astype(F32), rank, (plus // 16).astype(F32), (plus % 16).astype(F32))
        for j, row in enumerate(fields):
            header = jnp.where(iota(header.shape, 0) == 4 * k + j, row, header)
    header = header.astype(BF16)
    me, core = lax.axis_index(OWNER_AXES), lax.axis_index("mp")
    mine, other = column_half(obs_ref, core), column_half(obs_ref, 1 - core)

    def write(ref, pick, rows):
        packed = dot(pick, rows).astype(BF16)
        for c in range(rows.shape[1] // lanes):
            ref[c * cap : (c + 1) * cap, :] = packed[:, c * lanes : (c + 1) * lanes]
        ref[chunk - SUBLANES :, :] = header

    for j, out_ref in enumerate(outs):
        slots = iota((cap, obs), 0) + lax.rem(me + j, owners) * cap
        pick = functools.reduce(jnp.logical_or, [slots == place for place in places]).astype(BF16)
        write(out_ref, pick, mine)
        if j == 0:
            write(other_ref, pick, other)


def table_kernel(state_ref, agg_ref, w_node_ref, w_out_ref, bias_ref, table_ref):
    hidden = w_node_ref.shape[1]
    nodes, slots = state_ref.shape[0], bias_ref.shape[0]
    table_ref[nodes:, :] = jnp.zeros((table_ref.shape[0] - nodes, table_ref.shape[1]), BF16)

    def put(begin, column, part):
        high = part.astype(BF16)
        table_ref[begin : begin + part.shape[0], column : column + hidden] = high
        table_ref[begin : begin + part.shape[0], column + hidden : column + 2 * hidden] = (
            part - high.astype(F32)
        ).astype(BF16)

    put(0, 0, dot(state_ref[...], w_node_ref[...]))
    put(0, 2 * hidden, dot(agg_ref[...], w_out_ref[...], 1, 1))
    put(nodes, 0, bias_ref[...])


def join_blocks_kernel(*refs):
    out_ref = refs[-1]
    for j, ref in enumerate(refs[:-1]):
        out_ref[j] = ref[...]


def edge_kernel(
    fanout, nodes, own_ref, mine_ref, other_ref, theirs_ref, table_ref, w_obs_ref, act_ref, hot_ref, rows_mine_ref, rows_theirs_ref, *back_refs
):
    owners = len(back_refs)
    chunk, lanes = own_ref.shape
    half = w_obs_ref.shape[0] // 2
    hidden = w_obs_ref.shape[1]
    cap = (chunk - SUBLANES) * lanes // half
    me = lax.axis_index(OWNER_AXES).astype(F32)
    base = 1 << nodes.bit_length()
    columns = []
    for j in range(owners):
        block, other = (mine_ref.at[j - 1], theirs_ref.at[j - 1]) if j else (own_ref, other_ref)
        header = block[chunk - SUBLANES :, :].astype(F32)
        slot = header[4 * fanout : 4 * fanout + 1] * base
        code = jnp.zeros((cap, lanes), F32)
        for k in range(fanout):
            row = header[4 * k : 4 * k + 4]
            rank = jnp.where(row[0:1] == me, row[1:2], -1.0).astype(jnp.int32)
            code = code + jnp.where(
                iota((cap, lanes), 0) == rank, row[2:3] * 16.0 + row[3:4] + slot, 0.0
            )
        columns.append(jnp.sum(code, axis=1, keepdims=True).astype(jnp.int32))
        for c in range(half // lanes):
            rows = slice(j * cap, (j + 1) * cap)
            place = slice(c * lanes, (c + 1) * lanes)
            rows_mine_ref[rows, place] = block[c * cap : (c + 1) * cap, :]
            rows_theirs_ref[rows, place] = other[c * cap : (c + 1) * cap, :]
    code = jnp.concatenate(columns, axis=0)
    index, slot = (code & (base - 1)) - 1, (code >> (base.bit_length() - 1)) + nodes
    column = iota(hot_ref.shape, 1)
    hot = ((column == index) | ((column == slot) & (index >= 0))).astype(BF16)
    hot_ref[...] = hot
    rows = dot(hot, table_ref[...])
    w_mine, w_theirs = other_half(w_obs_ref)
    pre = dot(rows_mine_ref[...], w_mine) + dot(rows_theirs_ref[...], w_theirs)
    pre = pre + (rows[:, :hidden] + rows[:, hidden : 2 * hidden])
    g_z = rows[:, 2 * hidden : 3 * hidden] + rows[:, 3 * hidden :]
    sig = jax.nn.sigmoid(pre)
    g_a = (g_z * sig * (1.0 + pre * (1.0 - sig))).astype(BF16)
    act_ref[:, :hidden] = g_a
    act_ref[:, hidden:] = (pre * sig).astype(BF16)
    for j, back_ref in enumerate(back_refs):
        back_ref[...] = g_a[j * cap : (j + 1) * cap]


def halving_steps():
    bits = [
        [(axis, k) for k in range(lax.axis_size(axis).bit_length() - 1)] for axis in ("node", "obs")
    ]
    steps = []
    for k in range(max(map(len, bits))):
        both = [line[k] for line in bits if k < len(line)]
        steps += [(both[0], both[-1])] + ([(both[1], both[0])] if len(both) > 1 else [])
    return steps


def flip(value, step):
    axes = ("obs", "node", "mp")
    sizes = [lax.axis_size(axis) for axis in axes]
    pairs = []
    for index in range(sizes[0] * sizes[1] * sizes[2]):
        place = [index // (sizes[1] * sizes[2]), index // sizes[2] % sizes[1], index % sizes[2]]
        axis, k = step[place[2] % 2]
        place[axes.index(axis)] ^= 1 << k
        pairs.append((index, (place[0] * sizes[1] + place[1]) * sizes[2] + place[2]))
    return lax.ppermute(value, axes, pairs)


def own_bit(step):
    bits = [(lax.axis_index(axis) >> k) & 1 for axis, k in step]
    return jnp.where(lax.axis_index("mp") % 2 == 0, bits[0], bits[1])


def halves(rows):
    return rows % (2 * SUBLANES) == 0


def split_half(total_ref, start, rows, step, tail, keep_ref, send_ref):
    end = start + rows
    if halves(rows):
        rows //= 2
        bit = own_bit(step)
        kept, sent = [pl.ds(pl.multiple_of(start + b * rows, SUBLANES), rows) for b in (bit, 1 - bit)]
    else:
        kept = sent = pl.ds(start, rows)
    keep_ref[:rows, :] = total_ref[kept, :]
    send_ref[:rows, :] = total_ref[sent, :].astype(BF16)
    if tail:
        both = total_ref[end : end + tail, :]
        keep_ref[rows:, :] = both
        send_ref[rows:, :] = both.astype(BF16)


def weight_kernel(
    step, bundles, tail, hot_ref, act_ref, rows_mine_ref, rows_theirs_ref, state_ref, agg_ref, w_node_ref,
    mine_ref, theirs_ref, *refs
):
    halves_refs, total_ref = refs[:-1], refs[-1]
    width, hidden = w_node_ref.shape
    nodes = state_ref.shape[0]
    sums = dot(hot_ref[...], act_ref[...], 0, 0)
    by_node = sums[:nodes].astype(BF16)
    node_hidden, z_sum = by_node[:, :hidden], by_node[:, hidden:]
    total_ref[:width, :] = dot(state_ref[...], node_hidden, 0, 0)
    begin = width
    for c in range(width // hidden):
        total_ref[begin : begin + hidden, :] = dot(
            z_sum, agg_ref[:, c * hidden : (c + 1) * hidden], 0, 0
        )
        begin += hidden
    g_a = act_ref[:, :hidden]
    core, half = lax.axis_index("mp"), width // 2
    for which, ref in ((core, rows_mine_ref), (1 - core, rows_theirs_ref)):
        total_ref[pl.ds(pl.multiple_of(begin + which * half, SUBLANES), half), :] = dot(ref[...], g_a, 0, 0)
    begin += width
    total_ref[begin:, :] = sums[nodes:, :hidden]
    rows = begin // bundles
    for i in range(bundles):
        split_half(
            total_ref, i * rows, rows, step, tail if i == bundles - 1 else 0,
            halves_refs[2 * i], halves_refs[2 * i + 1],
        )
    mine, theirs = other_half(w_node_ref)
    theirs_ref[...] = dot(node_hidden, theirs, 1, 1).astype(BF16)
    mine_ref[...] = dot(node_hidden, mine, 1, 1)


def obs_kernel(owners, *refs):
    back_refs, (place_ref, w_ref, mine_ref, theirs_ref) = refs[:owners], refs[owners:]
    fanout, obs = place_ref.shape
    cap = back_refs[0].shape[0]
    me = lax.axis_index(OWNER_AXES)
    obs_hidden = None
    for j, back_ref in enumerate(back_refs):
        slots = iota((cap, obs), 0) + lax.rem(me + j, owners) * cap
        pick = functools.reduce(
            jnp.logical_or, [slots == place_ref[k : k + 1, :] for k in range(fanout)]
        )
        part = dot(pick.astype(BF16), back_ref[...], 0, 0)
        obs_hidden = part if obs_hidden is None else obs_hidden + part
    obs_hidden = obs_hidden.astype(BF16)
    mine, theirs = other_half(w_ref)
    theirs_ref[...] = dot(obs_hidden, theirs, 1, 1).astype(BF16)
    mine_ref[...] = dot(obs_hidden, mine, 1, 1)


def add_kernel(step, tail, keep_ref, got_ref, next_ref, send_ref, total_ref):
    total_ref[...] = keep_ref[...] + got_ref[...].astype(F32)
    split_half(total_ref, 0, total_ref.shape[0] - tail, step, tail, next_ref, send_ref)


def last_kernel(keep_ref, got_ref, piece_ref, *slot_refs):
    total = keep_ref[...] + got_ref[...].astype(F32)
    rows = piece_ref.shape[0]
    piece_ref[...] = total[:rows].astype(BF16)
    for slot_ref in slot_refs:
        slot_ref[...] = total[rows : rows + slot_ref.shape[0]]


def join_kernel(step, mine_ref, got_ref, out_ref):
    rows = mine_ref.shape[0]
    bit = own_bit(step)
    out_ref[pl.ds(pl.multiple_of(bit * rows, SUBLANES), rows), :] = mine_ref[...]
    out_ref[pl.ds(pl.multiple_of((1 - bit) * rows, SUBLANES), rows), :] = got_ref[...]


def spread_kernel(step, bundles, *refs):
    low = own_bit(step) == 0
    joined = []
    for i in range(bundles):
        mine, got = refs[2 * i][...], refs[2 * i + 1][...]
        joined += [jnp.where(low, mine, got), jnp.where(low, got, mine)]
    half, hidden = joined[0].shape
    at = 0
    for out_ref in refs[2 * bundles :]:
        for c in range(out_ref.shape[1] // hidden):
            begin = 0
            while begin < out_ref.shape[0]:
                offset = at % half
                count = min(out_ref.shape[0] - begin, half - offset)
                out_ref[begin : begin + count, c * hidden : (c + 1) * hidden] = joined[at // half][
                    offset : offset + count
                ].astype(F32)
                at, begin = at + count, begin + count


def merge_kernel(node_ref, node_got_ref, obs_ref, obs_got_ref, grad_node_ref, grad_obs_ref):
    grad_node_ref[...] = node_ref[...] + node_got_ref[...].astype(F32)
    grad_obs_ref[...] = (obs_ref[...] + obs_got_ref[...].astype(F32)).astype(BF16)


def reduce_halving(steps, tail, slots, keep, send, after):
    hidden = keep.shape[1]
    for done, nxt, wait in zip(steps[:-1], steps[1:], after):
        rows = keep.shape[0] - tail
        rows = (rows // 2 if halves(rows) else rows) + tail
        keep, send = call(
            functools.partial(add_kernel, nxt, tail),
            [((rows, hidden), F32), ((rows, hidden), BF16)],
            keep, flip(send, done),
            scratch=[pltpu.VMEM(keep.shape, F32)],
            after=wait,
        )
    rows = keep.shape[0] - tail
    return call(
        last_kernel,
        [((rows, hidden), BF16)] + ([((slots, hidden), F32)] if tail else []),
        keep, flip(send, steps[-1]),
        after=after[len(steps) - 1],
    )


def gather_doubling(steps, rows, piece, after):
    used = []
    for step in steps:
        if halves(rows):
            used.append(step)
            rows //= 2
    for step in used[:0:-1]:
        (piece,) = call(
            functools.partial(join_kernel, step),
            [((2 * piece.shape[0], piece.shape[1]), BF16)],
            piece, flip(piece, step),
            after=after if step == used[1] else (),
        )
    return piece, flip(piece, used[0])


def local(obs_feat, node_state, grad_agg, owner, local_idx, slot, w_obs, w_node, slot_bias, w_out):
    owners = lax.axis_size(OWNER_AXES)
    obs, fanout = owner.shape
    nodes, width = node_state.shape
    hidden = w_obs.shape[1]
    slots = slot_bias.shape[0]
    cap = max(2, 2 * obs * fanout // owners)
    cap = -(-cap // SUBLANES) * SUBLANES
    edges = owners * cap
    half = width // 2
    slot_row = slot.reshape(1, obs)

    chunk = cap * half // obs + SUBLANES
    place, other, *packed = call_staged(
        functools.partial(pack_kernel, cap),
        [((fanout, obs), jnp.int32)] + [((chunk, obs), BF16)] * (owners + 1),
        obs_feat, owner.T, local_idx.T, slot_row,
    )
    received = [shift(packed[j], OWNER_AXES, j) for j in range(1, owners)]
    tail = -(-slots // SUBLANES) * SUBLANES
    table, state_held, agg_held, w_node_held, w_obs_held = call_staged(
        table_kernel,
        [((nodes + tail, 4 * hidden), BF16)],
        node_state, grad_agg, w_node, w_out, slot_bias,
        held=(node_state, grad_agg, w_node, w_obs),
    )
    (mine,) = call(
        join_blocks_kernel, [((owners - 1, chunk, obs), BF16)], *received,
        after=(w_obs_held,),
    )
    theirs = shift(mine, "mp", 1)
    act, hot, rows_mine, rows_theirs, *back = call(
        functools.partial(edge_kernel, fanout, nodes),
        [((edges, 2 * hidden), BF16), ((edges, nodes + tail), BF16)]
        + [((edges, half), BF16)] * 2
        + [((cap, hidden), BF16)] * owners,
        packed[0], mine, other, theirs, table, w_obs_held,
    )

    steps = halving_steps()
    stack = 2 * width + width // hidden * hidden
    bundles = BUNDLES
    rows = stack // bundles
    shapes = []
    for i in range(bundles):
        share = rows // 2 + (tail if i == bundles - 1 else 0)
        shapes += [((share, hidden), F32), ((share, hidden), BF16)]
    node_mine, node_theirs, *shares = call(
        functools.partial(weight_kernel, steps[0], bundles, tail),
        [((nodes, half), F32), ((nodes, half), BF16)] + shapes,
        hot, act, rows_mine, rows_theirs, state_held, agg_held, w_node_held,
        scratch=[pltpu.VMEM((stack + tail, hidden), F32)],
    )
    node_got = shift(node_theirs, "mp", 1)

    back = back[:1] + [shift(back[j], OWNER_AXES, -j) for j in range(1, owners)]
    obs_mine, obs_theirs = call(
        functools.partial(obs_kernel, owners),
        [((obs, half), F32), ((obs, half), BF16)],
        *back, place, w_obs_held,
    )
    obs_got = shift(obs_theirs, "mp", 1)
    grad_node, grad_obs = call(
        merge_kernel, [((nodes, half), F32), ((obs, half), BF16)],
        node_mine, node_got, obs_mine, obs_got,
    )

    waits = [back[1 + i * (owners - 1) // len(steps) : 1 + (i + 1) * (owners - 1) // len(steps)] for i in range(len(steps))]
    held_back = [pltpu.with_memory_space_constraint(grad_obs, pltpu.HBM)]
    ends = []
    for i in range(bundles):
        last = i == bundles - 1
        piece, *grad_slot = reduce_halving(
            steps, tail if last else 0, slots, shares[2 * i], shares[2 * i + 1], waits
        )
        ends += gather_doubling(steps, rows, piece, held_back)
    grad_w_node, grad_w_out, grad_w_obs = call(
        functools.partial(spread_kernel, steps[0], bundles),
        [((width, hidden), F32), ((hidden, width), F32), ((width, hidden), F32)],
        *ends,
    )
    (grad_slot,) = grad_slot
    return grad_obs, grad_node, grad_w_obs, grad_w_node, grad_w_out, grad_slot


def solution(mesh):
    rows = P(("group", "obs", "node"), None)
    return jax.shard_map(
        local,
        mesh=mesh,
        in_specs=(
            rows, rows, rows, rows, rows,
            P(("group", "obs", "node")),
            P(None, "mp"), P(None, "mp"), P(None, "mp"), P("mp", None),
        ),
        out_specs=(
            P(("group", "obs", "node"), "mp"),
            P(("group", "obs", "node"), "mp"),
            P("group", "mp"),
            P("group", "mp"),
            P(("group", "mp"), None),
            P("group", "mp"),
        ),
        check_vma=False,
    )
```

time: 84.4 us -> 72.9 us (0.86)
  starting transfers between devices: 42.4 us -> 28.7 us
  waiting for transfers between devices: 27.4 us -> 34.3 us
  Pallas kernels: 11.7 us -> 8.91 us
  local copies, waits for them, and re-layouts: 1.79 us -> 0 us
    ppermute x12 -> x6, starting transfers between devices: 23.1 us -> 2.8 us  [flip(): return lax.ppermute(value, axes, pairs)]
    ppermute x9 -> x17, waiting for transfers between devices: 1.5 us -> 18.3 us  [shift(): lax.ppermute(value, axis, [(i, (i + step) % size) for i in range(size)])]
    ppermute x9 -> x17, starting transfers between devices: 13.8 us -> 25.9 us  [shift(): lax.ppermute(value, axis, [(i, (i + step) % size) for i in range(size)])]
    ppermute x12 -> x6, waiting for transfers between devices: 25.9 us -> 16 us  [flip(): return lax.ppermute(value, axes, pairs)]
    all_to_all x1 -> x0, starting transfers between devices: 5.54 us -> none  [exchange(): return lax.all_to_all(blocks, axes, split_axis=0, concat_axis=0, tiled=True)]
    pallas_call x2, Pallas kernels: 4.83 us -> 3.03 us  [call_staged(): pl.pallas_call(staged, out_shape=[jax.ShapeDtypeStruct(shape, dtype) for...]
    unnamed x18 -> x0, local copies, waits for them, and re-layouts: 1.79 us -> none
    pallas_call x16 -> x11, Pallas kernels: 6.88 us -> 5.88 us  [call(): pl.pallas_call(lambda *refs: kernel(*refs[:count], *refs[len(args):]), ou...]
  transfers between devices with their start and end apart: 22 -> 23, of which waited for: 10 -> 13; matrix products, arithmetic and copies ran while one was open for 0% -> 0% of each run, Pallas kernels for 8% -> 4%
where the time goes in v5:
time: 72.9 us; the launch traced here: 72.7 us
  waiting for transfers between devices  34.3 us (47%)
  starting transfers between devices  28.7 us (39%)
  Pallas kernels  8.91 us (12%)
  between operations  0.78 us (1%)
    ppermute x17, starting transfers between devices, shift(): lax.ppermute(value, axis, [(i, (i + step) % size) for i in range(size)])  25.9 us
    ppermute x17, waiting for transfers between devices, shift(): lax.ppermute(value, axis, [(i, (i + step) % size) for i in range(size)])  18.3 us
    ppermute x6, waiting for transfers between devices, flip(): return lax.ppermute(value, axes, pairs)  16 us
    pallas_call x11, Pallas kernels, call(): pl.pallas_call(lambda *refs: kernel(*refs[:count], *refs[len(args):]), ou...  5.88 us
    pallas_call x2, Pallas kernels, call_staged(): pl.pallas_call(staged, out_shape=[jax.ShapeDtypeStruct(shape, dtype) for...  3.03 us
    ppermute x6, starting transfers between devices, flip(): return lax.ppermute(value, axes, pairs)  2.8 us
  transfers between devices with their start and end apart: 23, of which 13 were waited for; matrix products, arithmetic and copies ran while one was open for 0% of the time, Pallas kernels for 4%

profile of v5, /device:TPU:0, one launch (start us, length us, event | category | flops | bytes accessed | tf_op | source)
XLA Modules:
  0.0 72.7 jit_solution(49903638529067623)
XLA Ops:
  0.6 1.3 %shard_map.145 = (s32[2,128]{1,0:T(2,128)S(1)}, bf16[144,128]{1,0:T(8,128)(2,1)S(1)}, bf16[144,128]{1,0:T(8,128)(2,1)S(1)}, bf16[144,128]{1,0:T(8,128)(2,1)S(1)}...) custom-call(bf16[128,512]{1,0:T(8,128)(2,1)} %refs_0_.2, ...), custom_call_target="tpu_custom_call" | custom-call | tf_op jit(solution)/shard_map/pallas_call | solution.py:61
  1.9 3.0 %collective-permute-start = (bf16[144,128]{1,0:T(8,128)(2,1)S(1)}, bf16[144,128]{1,0:T(8,128)(2,1)S(1)}, u32[]{:S(2)}, u32[]{:S(2)}) collective-permute-start(bf16[144,128]{1,0:T(8,128)(2,1)S(1)} %get-tuple-element.51), channel_id=1, source_target_pairs={{0,2},{2,4},{4,6},{6,8},{8,10},{10,12},{12,14},{14,0},{1,3},{3,5},... | collective-permute-start | bytes 110600 | tf_op jit(solution)/shard_map/ppermute | solution.py:79
  4.9 1.6 %collective-permute-start.1 = (bf16[144,128]{1,0:T(8,128)(2,1)S(1)}, bf16[144,128]{1,0:T(8,128)(2,1)S(1)}, u32[]{:S(2)}, u32[]{:S(2)}) collective-permute-start(bf16[144,128]{1,0:T(8,128)(2,1)S(1)} %get-tuple-element.52), channel_id=1, source_target_pairs={{0,4},{2,6},{4,8},{6,10},{8,12},{10,14},{12,0},{14,2},{1,5},{3,7},... | collective-permute-start | bytes 110600 | tf_op jit(solution)/shard_map/ppermute | solution.py:79
  6.5 2.6 %collective-permute-start.2 = (bf16[144,128]{1,0:T(8,128)(2,1)S(1)}, bf16[144,128]{1,0:T(8,128)(2,1)S(1)}, u32[]{:S(2)}, u32[]{:S(2)}) collective-permute-start(bf16[144,128]{1,0:T(8,128)(2,1)S(1)} %get-tuple-element.53), channel_id=1, source_target_pairs={{0,6},{2,8},{4,10},{6,12},{8,14},{10,0},{12,2},{14,4},{1,7},{3,9},... | collective-permute-start | bytes 110600 | tf_op jit(solution)/shard_map/ppermute | solution.py:79
  9.1 1.2 %collective-permute-start.3 = (bf16[144,128]{1,0:T(8,128)(2,1)S(1)}, bf16[144,128]{1,0:T(8,128)(2,1)S(1)}, u32[]{:S(2)}, u32[]{:S(2)}) collective-permute-start(bf16[144,128]{1,0:T(8,128)(2,1)S(1)} %get-tuple-element.54), channel_id=1, source_target_pairs={{0,8},{2,10},{4,12},{6,14},{8,0},{10,2},{12,4},{14,6},{1,9},{3,11}... | collective-permute-start | bytes 110600 | tf_op jit(solution)/shard_map/ppermute | solution.py:79
  10.3 2.6 %collective-permute-start.4 = (bf16[144,128]{1,0:T(8,128)(2,1)S(1)}, bf16[144,128]{1,0:T(8,128)(2,1)S(1)}, u32[]{:S(2)}, u32[]{:S(2)}) collective-permute-start(bf16[144,128]{1,0:T(8,128)(2,1)S(1)} %get-tuple-element.55), channel_id=1, source_target_pairs={{0,10},{2,12},{4,14},{6,0},{8,2},{10,4},{12,6},{14,8},{1,11},{3,13... | collective-permute-start | bytes 110600 | tf_op jit(solution)/shard_map/ppermute | solution.py:79
  12.9 0.0 collective-permute-done.refs_0_
  12.9 1.4 %collective-permute-start.5 = (bf16[144,128]{1,0:T(8,128)(2,1)S(1)}, bf16[144,128]{1,0:T(8,128)(2,1)S(1)}, u32[]{:S(2)}, u32[]{:S(2)}) collective-permute-start(bf16[144,128]{1,0:T(8,128)(2,1)S(1)} %get-tuple-element.56), channel_id=1, source_target_pairs={{0,12},{2,14},{4,0},{6,2},{8,4},{10,6},{12,8},{14,10},{1,13},{3,15... | collective-permute-start | bytes 110600 | tf_op jit(solution)/shard_map/ppermute | solution.py:79
  14.3 1.4 %collective-permute-start.6 = (bf16[144,128]{1,0:T(8,128)(2,1)S(1)}, bf16[144,128]{1,0:T(8,128)(2,1)S(1)}, u32[]{:S(2)}, u32[]{:S(2)}) collective-permute-start(bf16[144,128]{1,0:T(8,128)(2,1)S(1)} %get-tuple-element.57), channel_id=1, source_target_pairs={{0,14},{2,0},{4,2},{6,4},{8,6},{10,8},{12,10},{14,12},{1,15},{3,1}... | collective-permute-start | bytes 110600 | tf_op jit(solution)/shard_map/ppermute | solution.py:79
  15.7 1.7 %shard_map.146 = (bf16[336,1024]{1,0:T(8,128)(2,1)S(1)}, bf16[320,512]{1,0:T(8,128)(2,1)S(1)}, bf16[320,512]{1,0:T(8,128)(2,1)S(1)}, bf16[512,256]{1,0:T(8,128)(2,1)S(1)}, bf16[512,256]{1,0:T(8,128)(2,1)S(1)}) custom-call(bf16[320,512]{1,0:T(8,128)(2,1)} %refs_0_.3, bf16[320,512]{1,0:T(8,128)(2,1)} %refs_1_.1, bf16[512,256]{1,0:T(8,128)(2,1)} %refs_2_.1, ...), custom_call_target="tpu_custom_call" | custom-call | tf_op jit(solution)/shard_map/pallas_call | solution.py:61
  17.4 0.0 collective-permute-done.2.refs_2_
  17.5 0.0 collective-permute-done.5.refs_5_
  17.5 0.8 %collective-permute-done.6.refs_6_ = bf16[144,128]{1,0:T(8,128)(2,1)S(1)} collective-permute-done((bf16[144,128]{1,0:T(8,128)(2,1)S(1)}, bf16[144,128]{1,0:T(8,128)(2,1)S(1)}, u32[]{:S(2)}, u32[]{:S(2)}) %collective-permute-start.6) | collective-permute-done | bytes 36896 | tf_op jit(solution)/shard_map/ppermute | solution.py:79
  18.3 0.1 collective-permute-start.7
  18.3 1.5 %collective-permute-done.7.refs_3_ = bf16[7,144,128]{2,1,0:T(8,128)(2,1)S(1)} collective-permute-done((bf16[7,144,128]{2,1,0:T(8,128)(2,1)S(1)}, bf16[7,144,128]{2,1,0:T(8,128)(2,1)S(1)}, u32[]{:S(2)}, u32[]{:S(2)}) %collective-permute-start.7) | collective-permute-done | bytes 258080 | tf_op jit(solution)/shard_map/ppermute | solution.py:79
  19.9 1.2 %shard_map.148 = (bf16[512,512]{1,0:T(8,128)(2,1)S(1)}, bf16[512,336]{1,0:T(8,128)(2,1)S(1)}, bf16[512,256]{1,0:T(8,128)(2,1)S(1)}, bf16[512,256]{1,0:T(8,128)(2...) custom-call(bf16[144,128]{1,0:T(8,128)(2,1)S(1)} %get-tuple-element., ...), custom_call_target="tpu_custom_call" | custom-call | tf_op jit(solution)/shard_map/pallas_call | solution.py:32
  21.1 1.2 %shard_map.149 = (f32[320,256]{1,0:T(8,128)S(1)}, bf16[320,256]{1,0:T(8,128)(2,1)S(1)}, f32[784,256]{1,0:T(8,128)S(1)}, bf16[784,256]{1,0:T(8,128)(2,1)S(1)}) custom-call(bf16[512,336]{1,0:T(8,128)(2,1)S(1)} %get-tuple-element.61.refs_0_, bf16[512,512]{1,0:T(8,128)(2,1)S(1)} %get-tuple-element.62.refs_1_, bf16[512,256]{1,0:T(8,128)(2,1)S(1)} %get-tuple-element.63.refs_2_, ...), custom_call_target="tpu_custom_call" | custom-call | tf_op jit(solution)/shard_map/pallas_call | solution.py:32
  22.3 1.6 %collective-permute-start.17 = (bf16[784,256]{1,0:T(8,128)(2,1)S(1)}, bf16[784,256]{1,0:T(8,128)(2,1)S(1)}, u32[]{:S(2)}, u32[]{:S(2)}) collective-permute-start(bf16[784,256]{1,0:T(8,128)(2,1)S(1)} %get-tuple-element.84), channel_id=1, source_target_pairs={{0,2},{1,5},{2,0},{3,7},{4,6},{5,1},{6,4},{7,3},{8,10},{9,13},{10,... | collective-permute-start | bytes 1204232 | tf_op jit(solution)/shard_map/ppermute | solution.py:220
  23.9 2.6 %collective-permute-start.9 = (bf16[64,256]{1,0:T(8,128)(2,1)S(1)}, bf16[64,256]{1,0:T(8,128)(2,1)S(1)}, u32[]{:S(2)}, u32[]{:S(2)}) collective-permute-start(bf16[64,256]{1,0:T(8,128)(2,1)S(1)} %get-tuple-element.71), channel_id=1, source_target_pairs={{0,14},{2,0},{4,2},{6,4},{8,6},{10,8},{12,10},{14,12},{1,15},{3,1}... | collective-permute-start | bytes 98312 | tf_op jit(solution)/shard_map/ppermute | solution.py:79
  26.5 0.5 collective-permute-start.10
  27.0 3.5 %collective-permute-done.9.refs_1_.refs_2_ = bf16[64,256]{1,0:T(8,128)(2,1)S(1)} collective-permute-done((bf16[64,256]{1,0:T(8,128)(2,1)S(1)}, bf16[64,256]{1,0:T(8,128)(2,1)S(1)}, u32[]{:S(2)}, u32[]{:S(2)}) %collective-permute-start.9) | collective-permute-done | bytes 32800 | tf_op jit(solution)/shard_map/ppermute | solution.py:79
  30.5 0.2 collective-permute-done.10.refs_2_.refs_3_
  30.8 0.0 collective-permute-done.17.refs_1_
  30.8 0.2 shard_map.152
  30.9 0.9 %collective-permute-start.18 = (bf16[400,256]{1,0:T(8,128)(2,1)S(1)}, bf16[400,256]{1,0:T(8,128)(2,1)S(1)}, u32[]{:S(2)}, u32[]{:S(2)}) collective-permute-start(bf16[400,256]{1,0:T(8,128)(2,1)S(1)} %get-tuple-element.86), channel_id=1, source_target_pairs={{0,4},{1,3},{2,6},{3,1},{4,0},{5,7},{6,2},{7,5},{8,12},{9,11},{10,... | collective-permute-start | bytes 614408 | tf_op jit(solution)/shard_map/ppermute | solution.py:220
  31.8 4.0 %collective-permute-start.11 = (bf16[64,256]{1,0:T(8,128)(2,1)S(1)}, bf16[64,256]{1,0:T(8,128)(2,1)S(1)}, u32[]{:S(2)}, u32[]{:S(2)}) collective-permute-start(bf16[64,256]{1,0:T(8,128)(2,1)S(1)} %get-tuple-element.73), channel_id=1, source_target_pairs={{0,10},{2,12},{4,14},{6,0},{8,2},{10,4},{12,6},{14,8},{1,11},{3,13... | collective-permute-start | bytes 98312 | tf_op jit(solution)/shard_map/ppermute | solution.py:79
  35.8 2.4 %collective-permute-done.11.refs_3_.refs_2_ = bf16[64,256]{1,0:T(8,128)(2,1)S(1)} collective-permute-done((bf16[64,256]{1,0:T(8,128)(2,1)S(1)}, bf16[64,256]{1,0:T(8,128)(2,1)S(1)}, u32[]{:S(2)}, u32[]{:S(2)}) %collective-permute-start.11) | collective-permute-done | bytes 32800 | tf_op jit(solution)/shard_map/ppermute | solution.py:79
  38.2 2.8 %collective-permute-done.12.refs_4_.refs_3_ = bf16[64,256]{1,0:T(8,128)(2,1)S(1)} collective-permute-done((bf16[64,256]{1,0:T(8,128)(2,1)S(1)}, bf16[64,256]{1,0:T(8,128)(2,1)S(1)}, u32[]{:S(2)}, u32[]{:S(2)}) %collective-permute-start.12) | collective-permute-done | bytes 32800 | tf_op jit(solution)/shard_map/ppermute | solution.py:79
  41.0 0.0 collective-permute-done.18.refs_1_
  41.0 0.1 shard_map.153
  41.1 0.2 collective-permute-start.19
  41.2 1.9 %collective-permute-start.13 = (bf16[64,256]{1,0:T(8,128)(2,1)S(1)}, bf16[64,256]{1,0:T(8,128)(2,1)S(1)}, u32[]{:S(2)}, u32[]{:S(2)}) collective-permute-start(bf16[64,256]{1,0:T(8,128)(2,1)S(1)} %get-tuple-element.75), channel_id=1, source_target_pairs={{0,6},{2,8},{4,10},{6,12},{8,14},{10,0},{12,2},{14,4},{1,7},{3,9},... | collective-permute-start | bytes 98312 | tf_op jit(solution)/shard_map/ppermute | solution.py:79
  43.1 2.4 %collective-permute-start.15 = (bf16[64,256]{1,0:T(8,128)(2,1)S(1)}, bf16[64,256]{1,0:T(8,128)(2,1)S(1)}, u32[]{:S(2)}, u32[]{:S(2)}) collective-permute-start(bf16[64,256]{1,0:T(8,128)(2,1)S(1)} %get-tuple-element.77), channel_id=1, source_target_pairs={{0,2},{2,4},{4,6},{6,8},{8,10},{10,12},{12,14},{14,0},{1,3},{3,5},... | collective-permute-start | bytes 98312 | tf_op jit(solution)/shard_map/ppermute | solution.py:79
  45.5 2.7 %collective-permute-done.13.refs_5_.refs_2_ = bf16[64,256]{1,0:T(8,128)(2,1)S(1)} collective-permute-done((bf16[64,256]{1,0:T(8,128)(2,1)S(1)}, bf16[64,256]{1,0:T(8,128)(2,1)S(1)}, u32[]{:S(2)}, u32[]{:S(2)}) %collective-permute-start.13) | collective-permute-done | bytes 32800 | tf_op jit(solution)/shard_map/ppermute | solution.py:79
  48.3 0.6 collective-permute-done.14.refs_6_.refs_3_
  48.8 2.9 %collective-permute-done.15.refs_7_.refs_4_ = bf16[64,256]{1,0:T(8,128)(2,1)S(1)} collective-permute-done((bf16[64,256]{1,0:T(8,128)(2,1)S(1)}, bf16[64,256]{1,0:T(8,128)(2,1)S(1)}, u32[]{:S(2)}, u32[]{:S(2)}) %collective-permute-start.15) | collective-permute-done | bytes 32800 | tf_op jit(solution)/shard_map/ppermute | solution.py:79
  51.7 0.6 shard_map.154
  52.4 5.5 %collective-permute-done.20.refs_1_ = bf16[192,256]{1,0:T(8,128)(2,1)S(1)} collective-permute-done((bf16[192,256]{1,0:T(8,128)(2,1)S(1)}, bf16[192,256]{1,0:T(8,128)(2,1)S(1)}, u32[]{:S(2)}, u32[]{:S(2)}) %collective-permute-start.20) | collective-permute-done | bytes 98336 | tf_op jit(solution)/shard_map/ppermute | solution.py:220
  57.9 0.1 collective-permute-start.21
  58.0 0.1 collective-permute-start.8
  58.1 0.6 shard_map.150
  58.7 0.5 collective-permute-start.16
  59.2 0.9 %collective-permute-done.16.refs_3_ = bf16[128,256]{1,0:T(8,128)(2,1)S(1)} collective-permute-done((bf16[128,256]{1,0:T(8,128)(2,1)S(1)}, bf16[128,256]{1,0:T(8,128)(2,1)S(1)}, u32[]{:S(2)}, u32[]{:S(2)}) %collective-permute-start.16) | collective-permute-done | bytes 65568 | tf_op jit(solution)/shard_map/ppermute | solution.py:79
  60.1 0.8 %shard_map.151 = (f32[320,256]{1,0:T(8,128)}, bf16[128,256]{1,0:T(8,128)(2,1)}) custom-call(f32[320,256]{1,0:T(8,128)S(1)} %get-tuple-element.68.refs_0_, bf16[320,256]{1,0:T(8,128)(2,1)S(1)} %collective-permute-done.8.refs_1_, f32[128,256]{1,0:T(8,128)S(1)} %get-tuple-element.79.refs_2_, bf16[128,256]{1,0:T(8,128)(2,1)S(1)} %collective-permute-done.16.refs_3_), custom_call_target="tpu_custom_call" | custom-call | tf_op jit(solution)/shard_map/pallas_call | solution.py:32
  60.9 2.8 %collective-permute-done.21.refs_1_ = bf16[384,256]{1,0:T(8,128)(2,1)S(1)} collective-permute-done((bf16[384,256]{1,0:T(8,128)(2,1)S(1)}, bf16[384,256]{1,0:T(8,128)(2,1)S(1)}, u32[]{:S(2)}, u32[]{:S(2)}) %collective-permute-start.21) | collective-permute-done | bytes 196640 | tf_op jit(solution)/shard_map/ppermute | solution.py:220
  63.7 0.1 collective-permute-start.22
  63.8 7.8 %collective-permute-done.22.refs_1_ = bf16[768,256]{1,0:T(8,128)(2,1)S(1)} collective-permute-done((bf16[768,256]{1,0:T(8,128)(2,1)S(1)}, bf16[768,256]{1,0:T(8,128)(2,1)S(1)}, u32[]{:S(2)}, u32[]{:S(2)}) %collective-permute-start.22) | collective-permute-done | bytes 393248 | tf_op jit(solution)/shard_map/ppermute | solution.py:220
  71.5 1.2 %shard_map.157 = (f32[512,256]{1,0:T(8,128)}, f32[256,512]{1,0:T(8,128)}, f32[512,256]{1,0:T(8,128)}) custom-call(bf16[768,256]{1,0:T(8,128)(2,1)S(1)} %shard_map.156.refs_0_, bf16[768,256]{1,0:T(8,128)(2,1)S(1)} %collective-permute-done.22.refs_1_), custom_call_target="tpu_custom_call" | custom-call | tf_op jit(solution)/shard_map/pallas_call | solution.py:32
  (11 shorter events, 0.1 us)
Async XLA Ops:
  1.9 11.0 %collective-permute-start = (bf16[144,128]{1,0:T(8,128)(2,1)S(1)}, bf16[144,128]{1,0:T(8,128)(2,1)S(1)}, u32[]{:S(2)}, u32[]{:S(2)}) collective-permute-start(bf16[144,128]{1,0:T(8,128)(2,1)S(1)} %get-tuple-element.51), channel_id=1, source_target_pairs={{0,2},{2,4},{4,6},{6,8},{8,10},{10,12},{12,14},{14,0},{1,3},{3,5},... | collective-permute-start | bytes 110600 | tf_op jit(solution)/shard_map/ppermute | solution.py:79
  4.9 9.3 %collective-permute-start.1 = (bf16[144,128]{1,0:T(8,128)(2,1)S(1)}, bf16[144,128]{1,0:T(8,128)(2,1)S(1)}, u32[]{:S(2)}, u32[]{:S(2)}) collective-permute-start(bf16[144,128]{1,0:T(8,128)(2,1)S(1)} %get-tuple-element.52), channel_id=1, source_target_pairs={{0,4},{2,6},{4,8},{6,10},{8,12},{10,14},{12,0},{14,2},{1,5},{3,7},... | collective-permute-start | bytes 110600 | tf_op jit(solution)/shard_map/ppermute | solution.py:79
  6.5 10.9 %collective-permute-start.2 = (bf16[144,128]{1,0:T(8,128)(2,1)S(1)}, bf16[144,128]{1,0:T(8,128)(2,1)S(1)}, u32[]{:S(2)}, u32[]{:S(2)}) collective-permute-start(bf16[144,128]{1,0:T(8,128)(2,1)S(1)} %get-tuple-element.53), channel_id=1, source_target_pairs={{0,6},{2,8},{4,10},{6,12},{8,14},{10,0},{12,2},{14,4},{1,7},{3,9},... | collective-permute-start | bytes 110600 | tf_op jit(solution)/shard_map/ppermute | solution.py:79
  9.1 8.4 %collective-permute-start.3 = (bf16[144,128]{1,0:T(8,128)(2,1)S(1)}, bf16[144,128]{1,0:T(8,128)(2,1)S(1)}, u32[]{:S(2)}, u32[]{:S(2)}) collective-permute-start(bf16[144,128]{1,0:T(8,128)(2,1)S(1)} %get-tuple-element.54), channel_id=1, source_target_pairs={{0,8},{2,10},{4,12},{6,14},{8,0},{10,2},{12,4},{14,6},{1,9},{3,11}... | collective-permute-start | bytes 110600 | tf_op jit(solution)/shard_map/ppermute | solution.py:79
  10.3 7.2 %collective-permute-start.4 = (bf16[144,128]{1,0:T(8,128)(2,1)S(1)}, bf16[144,128]{1,0:T(8,128)(2,1)S(1)}, u32[]{:S(2)}, u32[]{:S(2)}) collective-permute-start(bf16[144,128]{1,0:T(8,128)(2,1)S(1)} %get-tuple-element.55), channel_id=1, source_target_pairs={{0,10},{2,12},{4,14},{6,0},{8,2},{10,4},{12,6},{14,8},{1,11},{3,13... | collective-permute-start | bytes 110600 | tf_op jit(solution)/shard_map/ppermute | solution.py:79
  12.9 4.5 %collective-permute-start.5 = (bf16[144,128]{1,0:T(8,128)(2,1)S(1)}, bf16[144,128]{1,0:T(8,128)(2,1)S(1)}, u32[]{:S(2)}, u32[]{:S(2)}) collective-permute-start(bf16[144,128]{1,0:T(8,128)(2,1)S(1)} %get-tuple-element.56), channel_id=1, source_target_pairs={{0,12},{2,14},{4,0},{6,2},{8,4},{10,6},{12,8},{14,10},{1,13},{3,15... | collective-permute-start | bytes 110600 | tf_op jit(solution)/shard_map/ppermute | solution.py:79
  14.3 4.0 %collective-permute-start.6 = (bf16[144,128]{1,0:T(8,128)(2,1)S(1)}, bf16[144,128]{1,0:T(8,128)(2,1)S(1)}, u32[]{:S(2)}, u32[]{:S(2)}) collective-permute-start(bf16[144,128]{1,0:T(8,128)(2,1)S(1)} %get-tuple-element.57), channel_id=1, source_target_pairs={{0,14},{2,0},{4,2},{6,4},{8,6},{10,8},{12,10},{14,12},{1,15},{3,1}... | collective-permute-start | bytes 110600 | tf_op jit(solution)/shard_map/ppermute | solution.py:79
  18.3 1.6 %collective-permute-start.7 = (bf16[7,144,128]{2,1,0:T(8,128)(2,1)S(1)}, bf16[7,144,128]{2,1,0:T(8,128)(2,1)S(1)}, u32[]{:S(2)}, u32[]{:S(2)}) collective-permute-start(bf16[7,144,128]{2,1,0:T(8,128)(2,1)S(1)} %shard_map.147.refs_1_), channel_id=1, source_target_pairs={{0,1},{1,0},{2,3},{3,2},{4,5},{5,4},{6,7},{7,6},{8,9},{9,8},{10,11... | collective-permute-start | bytes 774152 | tf_op jit(solution)/shard_map/ppermute | solution.py:79
  22.3 8.5 %collective-permute-start.17 = (bf16[784,256]{1,0:T(8,128)(2,1)S(1)}, bf16[784,256]{1,0:T(8,128)(2,1)S(1)}, u32[]{:S(2)}, u32[]{:S(2)}) collective-permute-start(bf16[784,256]{1,0:T(8,128)(2,1)S(1)} %get-tuple-element.84), channel_id=1, source_target_pairs={{0,2},{1,5},{2,0},{3,7},{4,6},{5,1},{6,4},{7,3},{8,10},{9,13},{10,... | collective-permute-start | bytes 1204232 | tf_op jit(solution)/shard_map/ppermute | solution.py:220
  23.9 6.7 %collective-permute-start.9 = (bf16[64,256]{1,0:T(8,128)(2,1)S(1)}, bf16[64,256]{1,0:T(8,128)(2,1)S(1)}, u32[]{:S(2)}, u32[]{:S(2)}) collective-permute-start(bf16[64,256]{1,0:T(8,128)(2,1)S(1)} %get-tuple-element.71), channel_id=1, source_target_pairs={{0,14},{2,0},{4,2},{6,4},{8,6},{10,8},{12,10},{14,12},{1,15},{3,1}... | collective-permute-start | bytes 98312 | tf_op jit(solution)/shard_map/ppermute | solution.py:79
  26.5 4.2 %collective-permute-start.10 = (bf16[64,256]{1,0:T(8,128)(2,1)S(1)}, bf16[64,256]{1,0:T(8,128)(2,1)S(1)}, u32[]{:S(2)}, u32[]{:S(2)}) collective-permute-start(bf16[64,256]{1,0:T(8,128)(2,1)S(1)} %get-tuple-element.72), channel_id=1, source_target_pairs={{0,12},{2,14},{4,0},{6,2},{8,4},{10,6},{12,8},{14,10},{1,13},{3,15... | collective-permute-start | bytes 98312 | tf_op jit(solution)/shard_map/ppermute | solution.py:79
  30.9 10.0 %collective-permute-start.18 = (bf16[400,256]{1,0:T(8,128)(2,1)S(1)}, bf16[400,256]{1,0:T(8,128)(2,1)S(1)}, u32[]{:S(2)}, u32[]{:S(2)}) collective-permute-start(bf16[400,256]{1,0:T(8,128)(2,1)S(1)} %get-tuple-element.86), channel_id=1, source_target_pairs={{0,4},{1,3},{2,6},{3,1},{4,0},{5,7},{6,2},{7,5},{8,12},{9,11},{10,... | collective-permute-start | bytes 614408 | tf_op jit(solution)/shard_map/ppermute | solution.py:220
  31.8 6.4 %collective-permute-start.11 = (bf16[64,256]{1,0:T(8,128)(2,1)S(1)}, bf16[64,256]{1,0:T(8,128)(2,1)S(1)}, u32[]{:S(2)}, u32[]{:S(2)}) collective-permute-start(bf16[64,256]{1,0:T(8,128)(2,1)S(1)} %get-tuple-element.73), channel_id=1, source_target_pairs={{0,10},{2,12},{4,14},{6,0},{8,2},{10,4},{12,6},{14,8},{1,11},{3,13... | collective-permute-start | bytes 98312 | tf_op jit(solution)/shard_map/ppermute | solution.py:79
  35.8 5.2 %collective-permute-start.12 = (bf16[64,256]{1,0:T(8,128)(2,1)S(1)}, bf16[64,256]{1,0:T(8,128)(2,1)S(1)}, u32[]{:S(2)}, u32[]{:S(2)}) collective-permute-start(bf16[64,256]{1,0:T(8,128)(2,1)S(1)} %get-tuple-element.74), channel_id=1, source_target_pairs={{0,8},{2,10},{4,12},{6,14},{8,0},{10,2},{12,4},{14,6},{1,9},{3,11}... | collective-permute-start | bytes 98312 | tf_op jit(solution)/shard_map/ppermute | solution.py:79
  41.1 10.7 %collective-permute-start.19 = (bf16[208,256]{1,0:T(8,128)(2,1)S(1)}, bf16[208,256]{1,0:T(8,128)(2,1)S(1)}, u32[]{:S(2)}, u32[]{:S(2)}) collective-permute-start(bf16[208,256]{1,0:T(8,128)(2,1)S(1)} %get-tuple-element.88), channel_id=1, source_target_pairs={{0,8},{1,9},{2,10},{3,11},{4,12},{5,13},{6,14},{7,15},{8,0},{9,1},... | collective-permute-start | bytes 319496 | tf_op jit(solution)/shard_map/ppermute | solution.py:220
  41.2 7.0 %collective-permute-start.13 = (bf16[64,256]{1,0:T(8,128)(2,1)S(1)}, bf16[64,256]{1,0:T(8,128)(2,1)S(1)}, u32[]{:S(2)}, u32[]{:S(2)}) collective-permute-start(bf16[64,256]{1,0:T(8,128)(2,1)S(1)} %get-tuple-element.75), channel_id=1, source_target_pairs={{0,6},{2,8},{4,10},{6,12},{8,14},{10,0},{12,2},{14,4},{1,7},{3,9},... | collective-permute-start | bytes 98312 | tf_op jit(solution)/shard_map/ppermute | solution.py:79
  43.1 5.7 %collective-permute-start.14 = (bf16[64,256]{1,0:T(8,128)(2,1)S(1)}, bf16[64,256]{1,0:T(8,128)(2,1)S(1)}, u32[]{:S(2)}, u32[]{:S(2)}) collective-permute-start(bf16[64,256]{1,0:T(8,128)(2,1)S(1)} %get-tuple-element.76), channel_id=1, source_target_pairs={{0,4},{2,6},{4,8},{6,10},{8,12},{10,14},{12,0},{14,2},{1,5},{3,7},... | collective-permute-start | bytes 98312 | tf_op jit(solution)/shard_map/ppermute | solution.py:79
  43.1 8.6 %collective-permute-start.15 = (bf16[64,256]{1,0:T(8,128)(2,1)S(1)}, bf16[64,256]{1,0:T(8,128)(2,1)S(1)}, u32[]{:S(2)}, u32[]{:S(2)}) collective-permute-start(bf16[64,256]{1,0:T(8,128)(2,1)S(1)} %get-tuple-element.77), channel_id=1, source_target_pairs={{0,2},{2,4},{4,6},{6,8},{8,10},{10,12},{12,14},{14,0},{1,3},{3,5},... | collective-permute-start | bytes 98312 | tf_op jit(solution)/shard_map/ppermute | solution.py:79
  52.4 5.5 %collective-permute-start.20 = (bf16[192,256]{1,0:T(8,128)(2,1)S(1)}, bf16[192,256]{1,0:T(8,128)(2,1)S(1)}, u32[]{:S(2)}, u32[]{:S(2)}) collective-permute-start(bf16[192,256]{1,0:T(8,128)(2,1)S(1)} %get-tuple-element.89.refs_0_), channel_id=1, source_target_pairs={{0,8},{1,9},{2,10},{3,11},{4,12},{5,13},{6,14},{7,15},{8,0},{9,1},... | collective-permute-start | bytes 294920 | tf_op jit(solution)/shard_map/ppermute | solution.py:220
  57.9 5.7 %collective-permute-start.21 = (bf16[384,256]{1,0:T(8,128)(2,1)S(1)}, bf16[384,256]{1,0:T(8,128)(2,1)S(1)}, u32[]{:S(2)}, u32[]{:S(2)}) collective-permute-start(bf16[384,256]{1,0:T(8,128)(2,1)S(1)} %shard_map.155.refs_0_), channel_id=1, source_target_pairs={{0,4},{1,3},{2,6},{3,1},{4,0},{5,7},{6,2},{7,5},{8,12},{9,11},{10,... | collective-permute-start | bytes 589832 | tf_op jit(solution)/shard_map/ppermute | solution.py:220
  58.0 2.1 %collective-permute-start.8 = (bf16[320,256]{1,0:T(8,128)(2,1)S(1)}, bf16[320,256]{1,0:T(8,128)(2,1)S(1)}, u32[]{:S(2)}, u32[]{:S(2)}) collective-permute-start(bf16[320,256]{1,0:T(8,128)(2,1)S(1)} %get-tuple-element.69), channel_id=1, source_target_pairs={{0,1},{1,0},{2,3},{3,2},{4,5},{5,4},{6,7},{7,6},{8,9},{9,8},{10,11... | collective-permute-start | bytes 491528 | tf_op jit(solution)/shard_map/ppermute | solution.py:79
  58.7 1.4 %collective-permute-start.16 = (bf16[128,256]{1,0:T(8,128)(2,1)S(1)}, bf16[128,256]{1,0:T(8,128)(2,1)S(1)}, u32[]{:S(2)}, u32[]{:S(2)}) collective-permute-start(bf16[128,256]{1,0:T(8,128)(2,1)S(1)} %get-tuple-element.80), channel_id=1, source_target_pairs={{0,1},{1,0},{2,3},{3,2},{4,5},{5,4},{6,7},{7,6},{8,9},{9,8},{10,11... | collective-permute-start | bytes 196616 | tf_op jit(solution)/shard_map/ppermute | solution.py:79
  63.7 7.8 %collective-permute-start.22 = (bf16[768,256]{1,0:T(8,128)(2,1)S(1)}, bf16[768,256]{1,0:T(8,128)(2,1)S(1)}, u32[]{:S(2)}, u32[]{:S(2)}) collective-permute-start(bf16[768,256]{1,0:T(8,128)(2,1)S(1)} %shard_map.156.refs_0_), channel_id=1, source_target_pairs={{0,2},{1,5},{2,0},{3,7},{4,6},{5,1},{6,4},{7,3},{8,10},{9,13},{10,... | collective-permute-start | bytes 1179656 | tf_op jit(solution)/shard_map/ppermute | solution.py:220

commit v6 on v5

--- a/solution.py
+++ b/solution.py
@@ -92,7 +92,7 @@
     return ref[:, pl.ds(pl.multiple_of(which * half, 128), half)]
 
 
-def pack_kernel(cap, obs_ref, owner_ref, index_ref, slot_ref, place_ref, other_ref, *outs):
+def pack_kernel(cap, obs_ref, owner_ref, index_ref, slot_ref, other_ref, *outs):
     owners = len(outs)
     chunk, lanes = outs[0].shape
     fanout, obs = owner_ref.shape
@@ -105,7 +105,6 @@
     for k in range(fanout):
         rank = jnp.sum(jnp.where(hits[k], before, 0.0), axis=0, keepdims=True)
         places.append(owner[k : k + 1] * cap + rank.astype(jnp.int32))
-        place_ref[k : k + 1, :] = places[k]
         plus = index[k : k + 1] + 1
         fields = (owner[k : k + 1].astype(F32), rank, (plus // 16).astype(F32), (plus % 16).astype(F32))
         for j, row in enumerate(fields):
@@ -152,27 +151,31 @@
 
 
 def edge_kernel(
-    fanout, nodes, own_ref, mine_ref, other_ref, theirs_ref, table_ref, w_obs_ref, act_ref, hot_ref, rows_mine_ref, rows_theirs_ref, *back_refs
+    fanout, nodes, steps, own_ref, mine_ref, other_ref, theirs_ref, table_ref, w_obs_ref,
+    act_ref, hot_ref, rows_mine_ref, rows_theirs_ref, keep_ref, send_ref, total_ref,
 ):
-    owners = len(back_refs)
+    owners = mine_ref.shape[0] + 1
     chunk, lanes = own_ref.shape
     half = w_obs_ref.shape[0] // 2
     hidden = w_obs_ref.shape[1]
     cap = (chunk - SUBLANES) * lanes // half
-    me = lax.axis_index(OWNER_AXES).astype(F32)
+    me = lax.axis_index(OWNER_AXES)
     base = 1 << nodes.bit_length()
     columns = []
+    picks = []
     for j in range(owners):
         block, other = (mine_ref.at[j - 1], theirs_ref.at[j - 1]) if j else (own_ref, other_ref)
         header = block[chunk - SUBLANES :, :].astype(F32)
         slot = header[4 * fanout : 4 * fanout + 1] * base
         code = jnp.zeros((cap, lanes), F32)
+        pick = jnp.zeros((cap, lanes), jnp.bool_)
         for k in range(fanout):
             row = header[4 * k : 4 * k + 4]
-            rank = jnp.where(row[0:1] == me, row[1:2], -1.0).astype(jnp.int32)
-            code = code + jnp.where(
-                iota((cap, lanes), 0) == rank, row[2:3] * 16.0 + row[3:4] + slot, 0.0
-            )
+            rank = jnp.where(row[0:1] == me.astype(F32), row[1:2], -1.0).astype(jnp.int32)
+            hit = iota((cap, lanes), 0) == rank
+            pick = pick | hit
+            code = code + jnp.where(hit, row[2:3] * 16.0 + row[3:4] + slot, 0.0)
+        picks.append(pick.astype(BF16))
         columns.append(jnp.sum(code, axis=1, keepdims=True).astype(jnp.int32))
         for c in range(half // lanes):
             rows = slice(j * cap, (j + 1) * cap)
@@ -193,8 +196,11 @@
     g_a = (g_z * sig * (1.0 + pre * (1.0 - sig))).astype(BF16)
     act_ref[:, :hidden] = g_a
     act_ref[:, hidden:] = (pre * sig).astype(BF16)
-    for j, back_ref in enumerate(back_refs):
-        back_ref[...] = g_a[j * cap : (j + 1) * cap]
+    for j, pick in enumerate(picks):
+        source = lax.rem(me - j + owners, owners)
+        begin = pl.multiple_of(place_of(source, steps) * lanes, SUBLANES)
+        total_ref[pl.ds(begin, lanes), :] = dot(pick, g_a[j * cap : (j + 1) * cap], 0, 0).astype(BF16)
+    split_half(total_ref, 0, owners * lanes, steps[0], 0, keep_ref, send_ref)
 
 
 def halving_steps():
@@ -220,9 +226,21 @@
     return lax.ppermute(value, axes, pairs)
 
 
+def bit_of(step, node, obs):
+    bits = [({"node": node, "obs": obs}[axis] >> k) & 1 for axis, k in step]
+    return jnp.where(lax.axis_index("mp") % 2 == 0, bits[0], bits[1])
+
+
 def own_bit(step):
-    bits = [(lax.axis_index(axis) >> k) & 1 for axis, k in step]
-    return jnp.where(lax.axis_index("mp") % 2 == 0, bits[0], bits[1])
+    return bit_of(step, lax.axis_index("node"), lax.axis_index("obs"))
+
+
+def place_of(owner, steps):
+    shares = lax.axis_size("node")
+    place = 0
+    for step in steps:
+        place = 2 * place + bit_of(step, lax.rem(owner, shares), lax.div(owner, shares))
+    return place
 
 
 def halves(rows):
@@ -279,27 +297,16 @@
     mine_ref[...] = dot(node_hidden, mine, 1, 1)
 
 
-def obs_kernel(owners, *refs):
-    back_refs, (place_ref, w_ref, mine_ref, theirs_ref) = refs[:owners], refs[owners:]
-    fanout, obs = place_ref.shape
-    cap = back_refs[0].shape[0]
-    me = lax.axis_index(OWNER_AXES)
-    obs_hidden = None
-    for j, back_ref in enumerate(back_refs):
-        slots = iota((cap, obs), 0) + lax.rem(me + j, owners) * cap
-        pick = functools.reduce(
-            jnp.logical_or, [slots == place_ref[k : k + 1, :] for k in range(fanout)]
-        )
-        part = dot(pick.astype(BF16), back_ref[...], 0, 0)
-        obs_hidden = part if obs_hidden is None else obs_hidden + part
-    obs_hidden = obs_hidden.astype(BF16)
+def obs_kernel(keep_ref, got_ref, w_ref, mine_ref, theirs_ref):
+    obs_hidden = (keep_ref[...].astype(F32) + got_ref[...].astype(F32)).astype(BF16)
     mine, theirs = other_half(w_ref)
     theirs_ref[...] = dot(obs_hidden, theirs, 1, 1).astype(BF16)
     mine_ref[...] = dot(obs_hidden, mine, 1, 1)
 
 
 def add_kernel(step, tail, keep_ref, got_ref, next_ref, send_ref, total_ref):
-    total_ref[...] = keep_ref[...] + got_ref[...].astype(F32)
+    total = keep_ref[...].astype(F32) + got_ref[...].astype(F32)
+    total_ref[...] = total.astype(total_ref.dtype)
     split_half(total_ref, 0, total_ref.shape[0] - tail, step, tail, next_ref, send_ref)
 
 
@@ -343,41 +350,83 @@
     grad_obs_ref[...] = (obs_ref[...] + obs_got_ref[...].astype(F32)).astype(BF16)
 
 
-def reduce_halving(steps, tail, slots, keep, send, after):
+def half_rows(rows):
+    return rows // 2 if halves(rows) else rows
+
+
+def summing(steps, tail, keep, send, after):
     hidden = keep.shape[1]
-    for done, nxt, wait in zip(steps[:-1], steps[1:], after):
-        rows = keep.shape[0] - tail
-        rows = (rows // 2 if halves(rows) else rows) + tail
+    for done, nxt in zip(steps[:-1], steps[1:]):
+        rows = half_rows(keep.shape[0] - tail) + tail
         keep, send = call(
             functools.partial(add_kernel, nxt, tail),
-            [((rows, hidden), F32), ((rows, hidden), BF16)],
+            [((rows, hidden), keep.dtype), ((rows, hidden), BF16)],
             keep, flip(send, done),
-            scratch=[pltpu.VMEM(keep.shape, F32)],
-            after=wait,
+            scratch=[pltpu.VMEM(keep.shape, keep.dtype)],
+            after=after,
         )
-    rows = keep.shape[0] - tail
-    return call(
-        last_kernel,
-        [((rows, hidden), BF16)] + ([((slots, hidden), F32)] if tail else []),
-        keep, flip(send, steps[-1]),
-        after=after[len(steps) - 1],
-    )
-
-
-def gather_doubling(steps, rows, piece, after):
+        after[:] = [send]
+        yield
+    return keep, flip(send, steps[-1])
+
+
+def weight_chain(steps, rows, tail, slots, keep, send, after):
     used = []
     for step in steps:
         if halves(rows):
             used.append(step)
             rows //= 2
+    keep, got = yield from summing(steps, tail, keep, send, after)
+    piece, *sums = call(
+        last_kernel,
+        [((rows, keep.shape[1]), BF16)] + ([((slots, keep.shape[1]), F32)] if tail else []),
+        keep, got,
+        after=after,
+    )
+    after[:] = [piece]
+    yield
     for step in used[:0:-1]:
         (piece,) = call(
             functools.partial(join_kernel, step),
             [((2 * piece.shape[0], piece.shape[1]), BF16)],
             piece, flip(piece, step),
-            after=after if step == used[1] else (),
+            after=after,
         )
-    return piece, flip(piece, used[0])
+        after[:] = [piece]
+        yield
+    return [piece, flip(piece, used[0])], sums
+
+
+def obs_chain(steps, w_obs, node_mine, node_theirs, keep, send, after):
+    keep, got = yield from summing(steps, 0, keep, send, after)
+    half = w_obs.shape[0] // 2
+    obs_mine, obs_theirs = call(
+        obs_kernel, [((keep.shape[0], half), F32), ((keep.shape[0], half), BF16)], keep, got, w_obs,
+        after=after,
+    )
+    after[:] = [obs_theirs]
+    yield
+    grad_node, grad_obs = call(
+        merge_kernel, [(node_mine.shape, F32), (obs_mine.shape, BF16)],
+        node_mine, shift(node_theirs, "mp", 1), obs_mine, shift(obs_theirs, "mp", 1),
+        after=after,
+    )
+    after[:] = [pltpu.with_memory_space_constraint(grad_obs, pltpu.HBM)]
+    yield
+    return grad_node, grad_obs
+
+
+def in_turns(chains):
+    results = [None] * len(chains)
+    running = list(enumerate(chains))
+    while running:
+        for item in list(running):
+            try:
+                next(item[1])
+            except StopIteration as stop:
+                results[item[0]] = stop.value
+                running.remove(item)
+    return results
 
 
 def local(obs_feat, node_state, grad_agg, owner, local_idx, slot, w_obs, w_node, slot_bias, w_out):
@@ -392,10 +441,11 @@
     half = width // 2
     slot_row = slot.reshape(1, obs)
 
+    steps = halving_steps()
     chunk = cap * half // obs + SUBLANES
-    place, other, *packed = call_staged(
+    other, *packed = call_staged(
         functools.partial(pack_kernel, cap),
-        [((fanout, obs), jnp.int32)] + [((chunk, obs), BF16)] * (owners + 1),
+        [((chunk, obs), BF16)] * (owners + 1),
         obs_feat, owner.T, local_idx.T, slot_row,
     )
     received = [shift(packed[j], OWNER_AXES, j) for j in range(1, owners)]
@@ -411,15 +461,15 @@
         after=(w_obs_held,),
     )
     theirs = shift(mine, "mp", 1)
-    act, hot, rows_mine, rows_theirs, *back = call(
-        functools.partial(edge_kernel, fanout, nodes),
+    act, hot, rows_mine, rows_theirs, obs_keep, obs_send = call(
+        functools.partial(edge_kernel, fanout, nodes, steps),
         [((edges, 2 * hidden), BF16), ((edges, nodes + tail), BF16)]
         + [((edges, half), BF16)] * 2
-        + [((cap, hidden), BF16)] * owners,
+        + [((owners * obs // 2, hidden), BF16)] * 2,
         packed[0], mine, other, theirs, table, w_obs_held,
-    )
-
-    steps = halving_steps()
+        scratch=[pltpu.VMEM((owners * obs, hidden), BF16)],
+    )
+
     stack = 2 * width + width // hidden * hidden
     bundles = BUNDLES
     rows = stack // bundles
@@ -433,35 +483,22 @@
         hot, act, rows_mine, rows_theirs, state_held, agg_held, w_node_held,
         scratch=[pltpu.VMEM((stack + tail, hidden), F32)],
     )
-    node_got = shift(node_theirs, "mp", 1)
-
-    back = back[:1] + [shift(back[j], OWNER_AXES, -j) for j in range(1, owners)]
-    obs_mine, obs_theirs = call(
-        functools.partial(obs_kernel, owners),
-        [((obs, half), F32), ((obs, half), BF16)],
-        *back, place, w_obs_held,
-    )
-    obs_got = shift(obs_theirs, "mp", 1)
-    grad_node, grad_obs = call(
-        merge_kernel, [((nodes, half), F32), ((obs, half), BF16)],
-        node_mine, node_got, obs_mine, obs_got,
-    )
-
-    waits = [back[1 + i * (owners - 1) // len(steps) : 1 + (i + 1) * (owners - 1) // len(steps)] for i in range(len(steps))]
-    held_back = [pltpu.with_memory_space_constraint(grad_obs, pltpu.HBM)]
-    ends = []
-    for i in range(bundles):
-        last = i == bundles - 1
-        piece, *grad_slot = reduce_halving(
-            steps, tail if last else 0, slots, shares[2 * i], shares[2 * i + 1], waits
+    after = []
+    chains = [
+        weight_chain(
+            steps, rows, tail if i == bundles - 1 else 0, slots, shares[2 * i], shares[2 * i + 1], after
         )
-        ends += gather_doubling(steps, rows, piece, held_back)
+        for i in range(bundles)
+    ]
+    chains.append(obs_chain(steps, w_obs_held, node_mine, node_theirs, obs_keep, obs_send, after))
+    *weights, (grad_node, grad_obs) = in_turns(chains)
+    ends = [end for pair, _ in weights for end in pair]
+    (grad_slot,) = weights[-1][1]
     grad_w_node, grad_w_out, grad_w_obs = call(
         functools.partial(spread_kernel, steps[0], bundles),
         [((width, hidden), F32), ((hidden, width), F32), ((width, hidden), F32)],
         *ends,
     )
-    (grad_slot,) = grad_slot
     return grad_obs, grad_node, grad_w_obs, grad_w_node, grad_w_out, grad_slot
 
 

time: 72.9 us -> 69.5 us (0.953)
  starting transfers between devices: 28.7 us -> 22.7 us
  waiting for transfers between devices: 34.3 us -> 36.8 us
    ppermute x6 -> x9, waiting for transfers between devices: 16 us -> 33.5 us  [flip(): return lax.ppermute(value, axes, pairs)]
    ppermute x17 -> x10, waiting for transfers between devices: 18.3 us -> 3.27 us  [shift(): lax.ppermute(value, axis, [(i, (i + step) % size) for i in range(size)])]
    ppermute x17 -> x10, starting transfers between devices: 25.9 us -> 14.4 us  [shift(): lax.ppermute(value, axis, [(i, (i + step) % size) for i in range(size)])]
    ppermute x6 -> x9, starting transfers between devices: 2.8 us -> 8.28 us  [flip(): return lax.ppermute(value, axes, pairs)]
    pallas_call x11 -> x13, Pallas kernels: 5.88 us -> 6.09 us  [call(): pl.pallas_call(lambda *refs: kernel(*refs[:count], *refs[len(args):]), ou...]
  transfers between devices with their start and end apart: 23 -> 19, of which waited for: 13 -> 12; matrix products, arithmetic and copies ran while one was open for 0% -> 0% of each run, Pallas kernels for 4% -> 5%
where the time goes in v6:
time: 69.5 us; the launch traced here: 69.3 us
  waiting for transfers between devices  36.8 us (53%)
  starting transfers between devices  22.7 us (33%)
  Pallas kernels  9.12 us (13%)
  between operations  0.78 us (1%)
    ppermute x9, waiting for transfers between devices, flip(): return lax.ppermute(value, axes, pairs)  33.5 us
    ppermute x10, starting transfers between devices, shift(): lax.ppermute(value, axis, [(i, (i + step) % size) for i in range(size)])  14.4 us
    ppermute x9, starting transfers between devices, flip(): return lax.ppermute(value, axes, pairs)  8.28 us
    pallas_call x13, Pallas kernels, call(): pl.pallas_call(lambda *refs: kernel(*refs[:count], *refs[len(args):]), ou...  6.09 us
    ppermute x10, waiting for transfers between devices, shift(): lax.ppermute(value, axis, [(i, (i + step) % size) for i in range(size)])  3.27 us
    pallas_call x2, Pallas kernels, call_staged(): pl.pallas_call(staged, out_shape=[jax.ShapeDtypeStruct(shape, dtype) for...  3.03 us
  transfers between devices with their start and end apart: 19, of which 12 were waited for; matrix products, arithmetic and copies ran while one was open for 0% of the time, Pallas kernels for 5%

profile of v6, /device:TPU:0, one launch (start us, length us, event | category | flops | bytes accessed | tf_op | source)
XLA Modules:
  0.0 69.3 jit_solution(16670921223540703512)
XLA Ops:
  0.6 1.3 %shard_map.145 = (bf16[144,128]{1,0:T(8,128)(2,1)S(1)}, bf16[144,128]{1,0:T(8,128)(2,1)S(1)}, bf16[144,128]{1,0:T(8,128)(2,1)S(1)}, bf16[144,128]{1,0:T(8,128)(2...) custom-call(bf16[128,512]{1,0:T(8,128)(2,1)} %refs_0_.2, ...), custom_call_target="tpu_custom_call" | custom-call | tf_op jit(solution)/shard_map/pallas_call | solution.py:61
  1.9 3.0 %collective-permute-start = (bf16[144,128]{1,0:T(8,128)(2,1)S(1)}, bf16[144,128]{1,0:T(8,128)(2,1)S(1)}, u32[]{:S(2)}, u32[]{:S(2)}) collective-permute-start(bf16[144,128]{1,0:T(8,128)(2,1)S(1)} %get-tuple-element.48), channel_id=1, source_target_pairs={{0,2},{2,4},{4,6},{6,8},{8,10},{10,12},{12,14},{14,0},{1,3},{3,5},... | collective-permute-start | bytes 110600 | tf_op jit(solution)/shard_map/ppermute | solution.py:79
  4.9 1.6 %collective-permute-start.1 = (bf16[144,128]{1,0:T(8,128)(2,1)S(1)}, bf16[144,128]{1,0:T(8,128)(2,1)S(1)}, u32[]{:S(2)}, u32[]{:S(2)}) collective-permute-start(bf16[144,128]{1,0:T(8,128)(2,1)S(1)} %get-tuple-element.49), channel_id=1, source_target_pairs={{0,4},{2,6},{4,8},{6,10},{8,12},{10,14},{12,0},{14,2},{1,5},{3,7},... | collective-permute-start | bytes 110600 | tf_op jit(solution)/shard_map/ppermute | solution.py:79
  6.5 2.6 %collective-permute-start.2 = (bf16[144,128]{1,0:T(8,128)(2,1)S(1)}, bf16[144,128]{1,0:T(8,128)(2,1)S(1)}, u32[]{:S(2)}, u32[]{:S(2)}) collective-permute-start(bf16[144,128]{1,0:T(8,128)(2,1)S(1)} %get-tuple-element.50), channel_id=1, source_target_pairs={{0,6},{2,8},{4,10},{6,12},{8,14},{10,0},{12,2},{14,4},{1,7},{3,9},... | collective-permute-start | bytes 110600 | tf_op jit(solution)/shard_map/ppermute | solution.py:79
  9.1 1.2 %collective-permute-start.3 = (bf16[144,128]{1,0:T(8,128)(2,1)S(1)}, bf16[144,128]{1,0:T(8,128)(2,1)S(1)}, u32[]{:S(2)}, u32[]{:S(2)}) collective-permute-start(bf16[144,128]{1,0:T(8,128)(2,1)S(1)} %get-tuple-element.51), channel_id=1, source_target_pairs={{0,8},{2,10},{4,12},{6,14},{8,0},{10,2},{12,4},{14,6},{1,9},{3,11}... | collective-permute-start | bytes 110600 | tf_op jit(solution)/shard_map/ppermute | solution.py:79
  10.3 2.6 %collective-permute-start.4 = (bf16[144,128]{1,0:T(8,128)(2,1)S(1)}, bf16[144,128]{1,0:T(8,128)(2,1)S(1)}, u32[]{:S(2)}, u32[]{:S(2)}) collective-permute-start(bf16[144,128]{1,0:T(8,128)(2,1)S(1)} %get-tuple-element.52), channel_id=1, source_target_pairs={{0,10},{2,12},{4,14},{6,0},{8,2},{10,4},{12,6},{14,8},{1,11},{3,13... | collective-permute-start | bytes 110600 | tf_op jit(solution)/shard_map/ppermute | solution.py:79
  12.9 0.0 collective-permute-done.refs_0_
  12.9 1.4 %collective-permute-start.5 = (bf16[144,128]{1,0:T(8,128)(2,1)S(1)}, bf16[144,128]{1,0:T(8,128)(2,1)S(1)}, u32[]{:S(2)}, u32[]{:S(2)}) collective-permute-start(bf16[144,128]{1,0:T(8,128)(2,1)S(1)} %get-tuple-element.53), channel_id=1, source_target_pairs={{0,12},{2,14},{4,0},{6,2},{8,4},{10,6},{12,8},{14,10},{1,13},{3,15... | collective-permute-start | bytes 110600 | tf_op jit(solution)/shard_map/ppermute | solution.py:79
  14.3 0.0 collective-permute-done.1.refs_1_
  14.3 1.4 %collective-permute-start.6 = (bf16[144,128]{1,0:T(8,128)(2,1)S(1)}, bf16[144,128]{1,0:T(8,128)(2,1)S(1)}, u32[]{:S(2)}, u32[]{:S(2)}) collective-permute-start(bf16[144,128]{1,0:T(8,128)(2,1)S(1)} %get-tuple-element.54), channel_id=1, source_target_pairs={{0,14},{2,0},{4,2},{6,4},{8,6},{10,8},{12,10},{14,12},{1,15},{3,1}... | collective-permute-start | bytes 110600 | tf_op jit(solution)/shard_map/ppermute | solution.py:79
  15.7 1.7 %shard_map.146 = (bf16[336,1024]{1,0:T(8,128)(2,1)S(1)}, bf16[320,512]{1,0:T(8,128)(2,1)S(1)}, bf16[320,512]{1,0:T(8,128)(2,1)S(1)}, bf16[512,256]{1,0:T(8,128)(2,1)S(1)}, bf16[512,256]{1,0:T(8,128)(2,1)S(1)}) custom-call(bf16[320,512]{1,0:T(8,128)(2,1)} %refs_0_.3, bf16[320,512]{1,0:T(8,128)(2,1)} %refs_1_.1, bf16[512,256]{1,0:T(8,128)(2,1)} %refs_2_.1, ...), custom_call_target="tpu_custom_call" | custom-call | tf_op jit(solution)/shard_map/pallas_call | solution.py:61
  17.4 0.0 collective-permute-done.2.refs_2_
  17.5 0.0 collective-permute-done.3.refs_3_
  17.5 0.0 collective-permute-done.5.refs_5_
  17.5 0.8 %collective-permute-done.6.refs_6_ = bf16[144,128]{1,0:T(8,128)(2,1)S(1)} collective-permute-done((bf16[144,128]{1,0:T(8,128)(2,1)S(1)}, bf16[144,128]{1,0:T(8,128)(2,1)S(1)}, u32[]{:S(2)}, u32[]{:S(2)}) %collective-permute-start.6) | collective-permute-done | bytes 36896 | tf_op jit(solution)/shard_map/ppermute | solution.py:79
  18.3 0.1 collective-permute-start.7
  18.3 1.5 %collective-permute-done.7.refs_3_ = bf16[7,144,128]{2,1,0:T(8,128)(2,1)S(1)} collective-permute-done((bf16[7,144,128]{2,1,0:T(8,128)(2,1)S(1)}, bf16[7,144,128]{2,1,0:T(8,128)(2,1)S(1)}, u32[]{:S(2)}, u32[]{:S(2)}) %collective-permute-start.7) | collective-permute-done | bytes 258080 | tf_op jit(solution)/shard_map/ppermute | solution.py:79
  19.9 1.6 %shard_map.148 = (bf16[512,512]{1,0:T(8,128)(2,1)S(1)}, bf16[512,336]{1,0:T(8,128)(2,1)S(1)}, bf16[512,256]{1,0:T(8,128)(2,1)S(1)}, bf16[512,256]{1,0:T(8,128)(2...) custom-call(bf16[144,128]{1,0:T(8,128)(2,1)S(1)} %get-tuple-element.47.refs_0_, ...), custom_call_target="tpu_custom_call" | custom-call | tf_op jit(solution)/shard_map/pallas_call | solution.py:32
  21.5 1.2 %shard_map.149 = (f32[320,256]{1,0:T(8,128)S(1)}, bf16[320,256]{1,0:T(8,128)(2,1)S(1)}, f32[784,256]{1,0:T(8,128)S(1)}, bf16[784,256]{1,0:T(8,128)(2,1)S(1)}) custom-call(bf16[512,336]{1,0:T(8,128)(2,1)S(1)} %get-tuple-element.58.refs_0_, bf16[512,512]{1,0:T(8,128)(2,1)S(1)} %get-tuple-element.59.refs_1_, bf16[512,256]{1,0:T(8,128)(2,1)S(1)} %get-tuple-element.60.refs_2_, ...), custom_call_target="tpu_custom_call" | custom-call | tf_op jit(solution)/shard_map/pallas_call | solution.py:32
  22.7 1.6 %collective-permute-start.10 = (bf16[784,256]{1,0:T(8,128)(2,1)S(1)}, bf16[784,256]{1,0:T(8,128)(2,1)S(1)}, u32[]{:S(2)}, u32[]{:S(2)}) collective-permute-start(bf16[784,256]{1,0:T(8,128)(2,1)S(1)} %get-tuple-element.70), channel_id=1, source_target_pairs={{0,2},{1,5},{2,0},{3,7},{4,6},{5,1},{6,4},{7,3},{8,10},{9,13},{10,... | collective-permute-start | bytes 1204232 | tf_op jit(solution)/shard_map/ppermute | solution.py:226
  24.3 0.5 collective-permute-start.9
  24.8 5.8 %collective-permute-done.10.refs_1_ = bf16[784,256]{1,0:T(8,128)(2,1)S(1)} collective-permute-done((bf16[784,256]{1,0:T(8,128)(2,1)S(1)}, bf16[784,256]{1,0:T(8,128)(2,1)S(1)}, u32[]{:S(2)}, u32[]{:S(2)}) %collective-permute-start.10) | collective-permute-done | bytes 401440 | tf_op jit(solution)/shard_map/ppermute | solution.py:226
  30.6 0.2 shard_map.150
  30.8 0.7 %collective-permute-start.12 = (bf16[400,256]{1,0:T(8,128)(2,1)S(1)}, bf16[400,256]{1,0:T(8,128)(2,1)S(1)}, u32[]{:S(2)}, u32[]{:S(2)}) collective-permute-start(bf16[400,256]{1,0:T(8,128)(2,1)S(1)} %get-tuple-element.71.refs_2_), channel_id=1, source_target_pairs={{0,4},{1,3},{2,6},{3,1},{4,0},{5,7},{6,2},{7,5},{8,12},{9,11},{10,... | collective-permute-start | bytes 614408 | tf_op jit(solution)/shard_map/ppermute | solution.py:226
  31.5 2.5 %collective-permute-done.9.refs_1_ = bf16[512,256]{1,0:T(8,128)(2,1)S(1)} collective-permute-done((bf16[512,256]{1,0:T(8,128)(2,1)S(1)}, bf16[512,256]{1,0:T(8,128)(2,1)S(1)}, u32[]{:S(2)}, u32[]{:S(2)}) %collective-permute-start.9) | collective-permute-done | bytes 262176 | tf_op jit(solution)/shard_map/ppermute | solution.py:226
  34.0 0.1 shard_map.151
  34.2 0.7 %collective-permute-start.11 = (bf16[256,256]{1,0:T(8,128)(2,1)S(1)}, bf16[256,256]{1,0:T(8,128)(2,1)S(1)}, u32[]{:S(2)}, u32[]{:S(2)}) collective-permute-start(bf16[256,256]{1,0:T(8,128)(2,1)S(1)} %get-tuple-element.73.refs_2_), channel_id=1, source_target_pairs={{0,4},{1,3},{2,6},{3,1},{4,0},{5,7},{6,2},{7,5},{8,12},{9,11},{10,... | collective-permute-start | bytes 393224 | tf_op jit(solution)/shard_map/ppermute | solution.py:226
  34.9 1.7 %collective-permute-done.12.refs_1_ = bf16[400,256]{1,0:T(8,128)(2,1)S(1)} collective-permute-done((bf16[400,256]{1,0:T(8,128)(2,1)S(1)}, bf16[400,256]{1,0:T(8,128)(2,1)S(1)}, u32[]{:S(2)}, u32[]{:S(2)}) %collective-permute-start.12) | collective-permute-done | bytes 204832 | tf_op jit(solution)/shard_map/ppermute | solution.py:226
  36.6 0.1 shard_map.152
  36.7 1.3 %collective-permute-start.14 = (bf16[208,256]{1,0:T(8,128)(2,1)S(1)}, bf16[208,256]{1,0:T(8,128)(2,1)S(1)}, u32[]{:S(2)}, u32[]{:S(2)}) collective-permute-start(bf16[208,256]{1,0:T(8,128)(2,1)S(1)} %get-tuple-element.75.refs_2_), channel_id=1, source_target_pairs={{0,8},{1,9},{2,10},{3,11},{4,12},{5,13},{6,14},{7,15},{8,0},{9,1},... | collective-permute-start | bytes 319496 | tf_op jit(solution)/shard_map/ppermute | solution.py:226
  37.9 1.2 %collective-permute-done.11.refs_1_ = bf16[256,256]{1,0:T(8,128)(2,1)S(1)} collective-permute-done((bf16[256,256]{1,0:T(8,128)(2,1)S(1)}, bf16[256,256]{1,0:T(8,128)(2,1)S(1)}, u32[]{:S(2)}, u32[]{:S(2)}) %collective-permute-start.11) | collective-permute-done | bytes 131104 | tf_op jit(solution)/shard_map/ppermute | solution.py:226
  39.2 0.1 shard_map.153
  39.3 4.7 %collective-permute-done.14.refs_1_ = bf16[208,256]{1,0:T(8,128)(2,1)S(1)} collective-permute-done((bf16[208,256]{1,0:T(8,128)(2,1)S(1)}, bf16[208,256]{1,0:T(8,128)(2,1)S(1)}, u32[]{:S(2)}, u32[]{:S(2)}) %collective-permute-start.14) | collective-permute-done | bytes 106528 | tf_op jit(solution)/shard_map/ppermute | solution.py:226
  43.9 0.6 shard_map.154
  44.5 0.0 collective-permute-start.16
  44.5 2.9 %collective-permute-start.13 = (bf16[128,256]{1,0:T(8,128)(2,1)S(1)}, bf16[128,256]{1,0:T(8,128)(2,1)S(1)}, u32[]{:S(2)}, u32[]{:S(2)}) collective-permute-start(bf16[128,256]{1,0:T(8,128)(2,1)S(1)} %get-tuple-element.77.refs_2_), channel_id=1, source_target_pairs={{0,8},{1,9},{2,10},{3,11},{4,12},{5,13},{6,14},{7,15},{8,0},{9,1},... | collective-permute-start | bytes 196616 | tf_op jit(solution)/shard_map/ppermute | solution.py:226
  47.5 6.8 %collective-permute-done.13.refs_1_ = bf16[128,256]{1,0:T(8,128)(2,1)S(1)} collective-permute-done((bf16[128,256]{1,0:T(8,128)(2,1)S(1)}, bf16[128,256]{1,0:T(8,128)(2,1)S(1)}, u32[]{:S(2)}, u32[]{:S(2)}) %collective-permute-start.13) | collective-permute-done | bytes 65568 | tf_op jit(solution)/shard_map/ppermute | solution.py:226
  54.2 0.2 shard_map.155
  54.5 0.1 collective-permute-start.17
  54.6 0.1 collective-permute-start.8
  54.7 0.5 collective-permute-start.15
  55.2 0.9 %collective-permute-done.8.refs_1_ = bf16[320,256]{1,0:T(8,128)(2,1)S(1)} collective-permute-done((bf16[320,256]{1,0:T(8,128)(2,1)S(1)}, bf16[320,256]{1,0:T(8,128)(2,1)S(1)}, u32[]{:S(2)}, u32[]{:S(2)}) %collective-permute-start.8) | collective-permute-done | bytes 163872 | tf_op jit(solution)/shard_map/ppermute | solution.py:79
  56.1 0.1 collective-permute-done.15.refs_3_
  56.2 0.8 %shard_map.157 = (f32[320,256]{1,0:T(8,128)}, bf16[128,256]{1,0:T(8,128)(2,1)}) custom-call(f32[320,256]{1,0:T(8,128)S(1)} %get-tuple-element.65.refs_0_, bf16[320,256]{1,0:T(8,128)(2,1)S(1)} %collective-permute-done.8.refs_1_, f32[128,256]{1,0:T(8,128)S(1)} %get-tuple-element.80.refs_2_, bf16[128,256]{1,0:T(8,128)(2,1)S(1)} %collective-permute-done.15.refs_3_, ...), custom_call_target="tpu_custom_call" | custom-call | tf_op jit(solution)/shard_map/pallas_call | solution.py:32
  56.9 3.3 %collective-permute-done.17.refs_1_ = bf16[384,256]{1,0:T(8,128)(2,1)S(1)} collective-permute-done((bf16[384,256]{1,0:T(8,128)(2,1)S(1)}, bf16[384,256]{1,0:T(8,128)(2,1)S(1)}, u32[]{:S(2)}, u32[]{:S(2)}) %collective-permute-start.17) | collective-permute-done | bytes 196640 | tf_op jit(solution)/shard_map/ppermute | solution.py:226
  60.3 0.4 collective-permute-start.18
  60.7 7.4 %collective-permute-done.18.refs_1_ = bf16[768,256]{1,0:T(8,128)(2,1)S(1)} collective-permute-done((bf16[768,256]{1,0:T(8,128)(2,1)S(1)}, bf16[768,256]{1,0:T(8,128)(2,1)S(1)}, u32[]{:S(2)}, u32[]{:S(2)}) %collective-permute-start.18) | collective-permute-done | bytes 393248 | tf_op jit(solution)/shard_map/ppermute | solution.py:226
  68.1 1.2 %shard_map.159 = (f32[512,256]{1,0:T(8,128)}, f32[256,512]{1,0:T(8,128)}, f32[512,256]{1,0:T(8,128)}) custom-call(bf16[768,256]{1,0:T(8,128)(2,1)S(1)} %shard_map.158.refs_0_, bf16[768,256]{1,0:T(8,128)(2,1)S(1)} %collective-permute-done.18.refs_1_), custom_call_target="tpu_custom_call" | custom-call | tf_op jit(solution)/shard_map/pallas_call | solution.py:32
  (5 shorter events, 0.1 us)
Async XLA Ops:
  1.9 11.0 %collective-permute-start = (bf16[144,128]{1,0:T(8,128)(2,1)S(1)}, bf16[144,128]{1,0:T(8,128)(2,1)S(1)}, u32[]{:S(2)}, u32[]{:S(2)}) collective-permute-start(bf16[144,128]{1,0:T(8,128)(2,1)S(1)} %get-tuple-element.48), channel_id=1, source_target_pairs={{0,2},{2,4},{4,6},{6,8},{8,10},{10,12},{12,14},{14,0},{1,3},{3,5},... | collective-permute-start | bytes 110600 | tf_op jit(solution)/shard_map/ppermute | solution.py:79
  4.9 9.3 %collective-permute-start.1 = (bf16[144,128]{1,0:T(8,128)(2,1)S(1)}, bf16[144,128]{1,0:T(8,128)(2,1)S(1)}, u32[]{:S(2)}, u32[]{:S(2)}) collective-permute-start(bf16[144,128]{1,0:T(8,128)(2,1)S(1)} %get-tuple-element.49), channel_id=1, source_target_pairs={{0,4},{2,6},{4,8},{6,10},{8,12},{10,14},{12,0},{14,2},{1,5},{3,7},... | collective-permute-start | bytes 110600 | tf_op jit(solution)/shard_map/ppermute | solution.py:79
  6.5 10.9 %collective-permute-start.2 = (bf16[144,128]{1,0:T(8,128)(2,1)S(1)}, bf16[144,128]{1,0:T(8,128)(2,1)S(1)}, u32[]{:S(2)}, u32[]{:S(2)}) collective-permute-start(bf16[144,128]{1,0:T(8,128)(2,1)S(1)} %get-tuple-element.50), channel_id=1, source_target_pairs={{0,6},{2,8},{4,10},{6,12},{8,14},{10,0},{12,2},{14,4},{1,7},{3,9},... | collective-permute-start | bytes 110600 | tf_op jit(solution)/shard_map/ppermute | solution.py:79
  9.1 8.4 %collective-permute-start.3 = (bf16[144,128]{1,0:T(8,128)(2,1)S(1)}, bf16[144,128]{1,0:T(8,128)(2,1)S(1)}, u32[]{:S(2)}, u32[]{:S(2)}) collective-permute-start(bf16[144,128]{1,0:T(8,128)(2,1)S(1)} %get-tuple-element.51), channel_id=1, source_target_pairs={{0,8},{2,10},{4,12},{6,14},{8,0},{10,2},{12,4},{14,6},{1,9},{3,11}... | collective-permute-start | bytes 110600 | tf_op jit(solution)/shard_map/ppermute | solution.py:79
  10.3 7.2 %collective-permute-start.4 = (bf16[144,128]{1,0:T(8,128)(2,1)S(1)}, bf16[144,128]{1,0:T(8,128)(2,1)S(1)}, u32[]{:S(2)}, u32[]{:S(2)}) collective-permute-start(bf16[144,128]{1,0:T(8,128)(2,1)S(1)} %get-tuple-element.52), channel_id=1, source_target_pairs={{0,10},{2,12},{4,14},{6,0},{8,2},{10,4},{12,6},{14,8},{1,11},{3,13... | collective-permute-start | bytes 110600 | tf_op jit(solution)/shard_map/ppermute | solution.py:79
  12.9 4.5 %collective-permute-start.5 = (bf16[144,128]{1,0:T(8,128)(2,1)S(1)}, bf16[144,128]{1,0:T(8,128)(2,1)S(1)}, u32[]{:S(2)}, u32[]{:S(2)}) collective-permute-start(bf16[144,128]{1,0:T(8,128)(2,1)S(1)} %get-tuple-element.53), channel_id=1, source_target_pairs={{0,12},{2,14},{4,0},{6,2},{8,4},{10,6},{12,8},{14,10},{1,13},{3,15... | collective-permute-start | bytes 110600 | tf_op jit(solution)/shard_map/ppermute | solution.py:79
  14.3 4.0 %collective-permute-start.6 = (bf16[144,128]{1,0:T(8,128)(2,1)S(1)}, bf16[144,128]{1,0:T(8,128)(2,1)S(1)}, u32[]{:S(2)}, u32[]{:S(2)}) collective-permute-start(bf16[144,128]{1,0:T(8,128)(2,1)S(1)} %get-tuple-element.54), channel_id=1, source_target_pairs={{0,14},{2,0},{4,2},{6,4},{8,6},{10,8},{12,10},{14,12},{1,15},{3,1}... | collective-permute-start | bytes 110600 | tf_op jit(solution)/shard_map/ppermute | solution.py:79
  18.3 1.6 %collective-permute-start.7 = (bf16[7,144,128]{2,1,0:T(8,128)(2,1)S(1)}, bf16[7,144,128]{2,1,0:T(8,128)(2,1)S(1)}, u32[]{:S(2)}, u32[]{:S(2)}) collective-permute-start(bf16[7,144,128]{2,1,0:T(8,128)(2,1)S(1)} %shard_map.147.refs_1_), channel_id=1, source_target_pairs={{0,1},{1,0},{2,3},{3,2},{4,5},{5,4},{6,7},{7,6},{8,9},{9,8},{10,11... | collective-permute-start | bytes 774152 | tf_op jit(solution)/shard_map/ppermute | solution.py:79
  22.7 7.9 %collective-permute-start.10 = (bf16[784,256]{1,0:T(8,128)(2,1)S(1)}, bf16[784,256]{1,0:T(8,128)(2,1)S(1)}, u32[]{:S(2)}, u32[]{:S(2)}) collective-permute-start(bf16[784,256]{1,0:T(8,128)(2,1)S(1)} %get-tuple-element.70), channel_id=1, source_target_pairs={{0,2},{1,5},{2,0},{3,7},{4,6},{5,1},{6,4},{7,3},{8,10},{9,13},{10,... | collective-permute-start | bytes 1204232 | tf_op jit(solution)/shard_map/ppermute | solution.py:226
  24.3 9.8 %collective-permute-start.9 = (bf16[512,256]{1,0:T(8,128)(2,1)S(1)}, bf16[512,256]{1,0:T(8,128)(2,1)S(1)}, u32[]{:S(2)}, u32[]{:S(2)}) collective-permute-start(bf16[512,256]{1,0:T(8,128)(2,1)S(1)} %get-tuple-element.68), channel_id=1, source_target_pairs={{0,2},{1,5},{2,0},{3,7},{4,6},{5,1},{6,4},{7,3},{8,10},{9,13},{10,... | collective-permute-start | bytes 786440 | tf_op jit(solution)/shard_map/ppermute | solution.py:226
  30.8 5.8 %collective-permute-start.12 = (bf16[400,256]{1,0:T(8,128)(2,1)S(1)}, bf16[400,256]{1,0:T(8,128)(2,1)S(1)}, u32[]{:S(2)}, u32[]{:S(2)}) collective-permute-start(bf16[400,256]{1,0:T(8,128)(2,1)S(1)} %get-tuple-element.71.refs_2_), channel_id=1, source_target_pairs={{0,4},{1,3},{2,6},{3,1},{4,0},{5,7},{6,2},{7,5},{8,12},{9,11},{10,... | collective-permute-start | bytes 614408 | tf_op jit(solution)/shard_map/ppermute | solution.py:226
  34.2 5.0 %collective-permute-start.11 = (bf16[256,256]{1,0:T(8,128)(2,1)S(1)}, bf16[256,256]{1,0:T(8,128)(2,1)S(1)}, u32[]{:S(2)}, u32[]{:S(2)}) collective-permute-start(bf16[256,256]{1,0:T(8,128)(2,1)S(1)} %get-tuple-element.73.refs_2_), channel_id=1, source_target_pairs={{0,4},{1,3},{2,6},{3,1},{4,0},{5,7},{6,2},{7,5},{8,12},{9,11},{10,... | collective-permute-start | bytes 393224 | tf_op jit(solution)/shard_map/ppermute | solution.py:226
  36.7 7.2 %collective-permute-start.14 = (bf16[208,256]{1,0:T(8,128)(2,1)S(1)}, bf16[208,256]{1,0:T(8,128)(2,1)S(1)}, u32[]{:S(2)}, u32[]{:S(2)}) collective-permute-start(bf16[208,256]{1,0:T(8,128)(2,1)S(1)} %get-tuple-element.75.refs_2_), channel_id=1, source_target_pairs={{0,8},{1,9},{2,10},{3,11},{4,12},{5,13},{6,14},{7,15},{8,0},{9,1},... | collective-permute-start | bytes 319496 | tf_op jit(solution)/shard_map/ppermute | solution.py:226
  44.5 10.0 %collective-permute-start.16 = (bf16[192,256]{1,0:T(8,128)(2,1)S(1)}, bf16[192,256]{1,0:T(8,128)(2,1)S(1)}, u32[]{:S(2)}, u32[]{:S(2)}) collective-permute-start(bf16[192,256]{1,0:T(8,128)(2,1)S(1)} %get-tuple-element.79.refs_3_.refs_0_), channel_id=1, source_target_pairs={{0,8},{1,9},{2,10},{3,11},{4,12},{5,13},{6,14},{7,15},{8,0},{9,1},... | collective-permute-start | bytes 294920 | tf_op jit(solution)/shard_map/ppermute | solution.py:226
  44.5 9.7 %collective-permute-start.13 = (bf16[128,256]{1,0:T(8,128)(2,1)S(1)}, bf16[128,256]{1,0:T(8,128)(2,1)S(1)}, u32[]{:S(2)}, u32[]{:S(2)}) collective-permute-start(bf16[128,256]{1,0:T(8,128)(2,1)S(1)} %get-tuple-element.77.refs_2_), channel_id=1, source_target_pairs={{0,8},{1,9},{2,10},{3,11},{4,12},{5,13},{6,14},{7,15},{8,0},{9,1},... | collective-permute-start | bytes 196616 | tf_op jit(solution)/shard_map/ppermute | solution.py:226
  54.5 5.7 %collective-permute-start.17 = (bf16[384,256]{1,0:T(8,128)(2,1)S(1)}, bf16[384,256]{1,0:T(8,128)(2,1)S(1)}, u32[]{:S(2)}, u32[]{:S(2)}) collective-permute-start(bf16[384,256]{1,0:T(8,128)(2,1)S(1)} %shard_map.156.refs_4_.refs_0_), channel_id=1, source_target_pairs={{0,4},{1,3},{2,6},{3,1},{4,0},{5,7},{6,2},{7,5},{8,12},{9,11},{10,... | collective-permute-start | bytes 589832 | tf_op jit(solution)/shard_map/ppermute | solution.py:226
  54.6 1.5 %collective-permute-start.8 = (bf16[320,256]{1,0:T(8,128)(2,1)S(1)}, bf16[320,256]{1,0:T(8,128)(2,1)S(1)}, u32[]{:S(2)}, u32[]{:S(2)}) collective-permute-start(bf16[320,256]{1,0:T(8,128)(2,1)S(1)} %get-tuple-element.66), channel_id=1, source_target_pairs={{0,1},{1,0},{2,3},{3,2},{4,5},{5,4},{6,7},{7,6},{8,9},{9,8},{10,11... | collective-permute-start | bytes 491528 | tf_op jit(solution)/shard_map/ppermute | solution.py:79
  54.7 1.5 %collective-permute-start.15 = (bf16[128,256]{1,0:T(8,128)(2,1)S(1)}, bf16[128,256]{1,0:T(8,128)(2,1)S(1)}, u32[]{:S(2)}, u32[]{:S(2)}) collective-permute-start(bf16[128,256]{1,0:T(8,128)(2,1)S(1)} %get-tuple-element.81.refs_2_), channel_id=1, source_target_pairs={{0,1},{1,0},{2,3},{3,2},{4,5},{5,4},{6,7},{7,6},{8,9},{9,8},{10,11... | collective-permute-start | bytes 196616 | tf_op jit(solution)/shard_map/ppermute | solution.py:79
  60.3 7.8 %collective-permute-start.18 = (bf16[768,256]{1,0:T(8,128)(2,1)S(1)}, bf16[768,256]{1,0:T(8,128)(2,1)S(1)}, u32[]{:S(2)}, u32[]{:S(2)}) collective-permute-start(bf16[768,256]{1,0:T(8,128)(2,1)S(1)} %shard_map.158.refs_0_), channel_id=1, source_target_pairs={{0,2},{1,5},{2,0},{3,7},{4,6},{5,1},{6,4},{7,3},{8,10},{9,13},{10,... | collective-permute-start | bytes 1179656 | tf_op jit(solution)/shard_map/ppermute | solution.py:226

commit v7 on v6

--- a/solution.py
+++ b/solution.py
@@ -9,7 +9,7 @@
 
 OWNER_AXES = ("obs", "node")
 SUBLANES = 16
-BUNDLES = 1
+BUNDLES = 2
 BF16 = jnp.bfloat16
 F32 = jnp.float32
 

time: 69.5 us -> 67.9 us (0.977)
  waiting for transfers between devices: 36.8 us -> 24.6 us
  starting transfers between devices: 22.7 us -> 33.1 us
    ppermute x9 -> x15, waiting for transfers between devices: 33.5 us -> 21 us  [flip(): return lax.ppermute(value, axes, pairs)]
    ppermute x9 -> x15, starting transfers between devices: 8.28 us -> 19.3 us  [flip(): return lax.ppermute(value, axes, pairs)]
    pallas_call x13 -> x18, Pallas kernels: 6.09 us -> 6.19 us  [call(): pl.pallas_call(lambda *refs: kernel(*refs[:count], *refs[len(args):]), ou...]
  transfers between devices with their start and end apart: 19 -> 25, of which waited for: 12 -> 11; matrix products, arithmetic and copies ran while one was open for 0% -> 0% of each run, Pallas kernels for 5% -> 7%
where the time goes in v7:
time: 67.9 us; the launch traced here: 67.7 us
  starting transfers between devices  33.1 us (49%)
  waiting for transfers between devices  24.6 us (36%)
  Pallas kernels  9.21 us (14%)
  between operations  0.83 us (1%)
    ppermute x15, waiting for transfers between devices, flip(): return lax.ppermute(value, axes, pairs)  21 us
    ppermute x15, starting transfers between devices, flip(): return lax.ppermute(value, axes, pairs)  19.3 us
    ppermute x10, starting transfers between devices, shift(): lax.ppermute(value, axis, [(i, (i + step) % size) for i in range(size)])  13.8 us
    pallas_call x18, Pallas kernels, call(): pl.pallas_call(lambda *refs: kernel(*refs[:count], *refs[len(args):]), ou...  6.19 us
    ppermute x10, waiting for transfers between devices, shift(): lax.ppermute(value, axis, [(i, (i + step) % size) for i in range(size)])  3.54 us
    pallas_call x2, Pallas kernels, call_staged(): pl.pallas_call(staged, out_shape=[jax.ShapeDtypeStruct(shape, dtype) for...  3.03 us
  transfers between devices with their start and end apart: 25, of which 11 were waited for; matrix products, arithmetic and copies ran while one was open for 0% of the time, Pallas kernels for 7%

profile of v7, /device:TPU:0, one launch (start us, length us, event | category | flops | bytes accessed | tf_op | source)
XLA Modules:
  0.0 67.7 jit_solution(13019821085524576318)
XLA Ops:
  0.6 1.3 %shard_map.145 = (bf16[144,128]{1,0:T(8,128)(2,1)S(1)}, bf16[144,128]{1,0:T(8,128)(2,1)S(1)}, bf16[144,128]{1,0:T(8,128)(2,1)S(1)}, bf16[144,128]{1,0:T(8,128)(2...) custom-call(bf16[128,512]{1,0:T(8,128)(2,1)} %refs_0_.2, ...), custom_call_target="tpu_custom_call" | custom-call | tf_op jit(solution)/shard_map/pallas_call | solution.py:61
  1.9 3.0 %collective-permute-start = (bf16[144,128]{1,0:T(8,128)(2,1)S(1)}, bf16[144,128]{1,0:T(8,128)(2,1)S(1)}, u32[]{:S(2)}, u32[]{:S(2)}) collective-permute-start(bf16[144,128]{1,0:T(8,128)(2,1)S(1)} %get-tuple-element.54), channel_id=1, source_target_pairs={{0,2},{2,4},{4,6},{6,8},{8,10},{10,12},{12,14},{14,0},{1,3},{3,5},... | collective-permute-start | bytes 110600 | tf_op jit(solution)/shard_map/ppermute | solution.py:79
  4.9 1.6 %collective-permute-start.1 = (bf16[144,128]{1,0:T(8,128)(2,1)S(1)}, bf16[144,128]{1,0:T(8,128)(2,1)S(1)}, u32[]{:S(2)}, u32[]{:S(2)}) collective-permute-start(bf16[144,128]{1,0:T(8,128)(2,1)S(1)} %get-tuple-element.55), channel_id=1, source_target_pairs={{0,4},{2,6},{4,8},{6,10},{8,12},{10,14},{12,0},{14,2},{1,5},{3,7},... | collective-permute-start | bytes 110600 | tf_op jit(solution)/shard_map/ppermute | solution.py:79
  6.5 2.6 %collective-permute-start.2 = (bf16[144,128]{1,0:T(8,128)(2,1)S(1)}, bf16[144,128]{1,0:T(8,128)(2,1)S(1)}, u32[]{:S(2)}, u32[]{:S(2)}) collective-permute-start(bf16[144,128]{1,0:T(8,128)(2,1)S(1)} %get-tuple-element.56), channel_id=1, source_target_pairs={{0,6},{2,8},{4,10},{6,12},{8,14},{10,0},{12,2},{14,4},{1,7},{3,9},... | collective-permute-start | bytes 110600 | tf_op jit(solution)/shard_map/ppermute | solution.py:79
  9.1 1.2 %collective-permute-start.3 = (bf16[144,128]{1,0:T(8,128)(2,1)S(1)}, bf16[144,128]{1,0:T(8,128)(2,1)S(1)}, u32[]{:S(2)}, u32[]{:S(2)}) collective-permute-start(bf16[144,128]{1,0:T(8,128)(2,1)S(1)} %get-tuple-element.57), channel_id=1, source_target_pairs={{0,8},{2,10},{4,12},{6,14},{8,0},{10,2},{12,4},{14,6},{1,9},{3,11}... | collective-permute-start | bytes 110600 | tf_op jit(solution)/shard_map/ppermute | solution.py:79
  10.3 2.6 %collective-permute-start.4 = (bf16[144,128]{1,0:T(8,128)(2,1)S(1)}, bf16[144,128]{1,0:T(8,128)(2,1)S(1)}, u32[]{:S(2)}, u32[]{:S(2)}) collective-permute-start(bf16[144,128]{1,0:T(8,128)(2,1)S(1)} %get-tuple-element.58), channel_id=1, source_target_pairs={{0,10},{2,12},{4,14},{6,0},{8,2},{10,4},{12,6},{14,8},{1,11},{3,13... | collective-permute-start | bytes 110600 | tf_op jit(solution)/shard_map/ppermute | solution.py:79
  12.9 1.4 %collective-permute-start.5 = (bf16[144,128]{1,0:T(8,128)(2,1)S(1)}, bf16[144,128]{1,0:T(8,128)(2,1)S(1)}, u32[]{:S(2)}, u32[]{:S(2)}) collective-permute-start(bf16[144,128]{1,0:T(8,128)(2,1)S(1)} %get-tuple-element.59), channel_id=1, source_target_pairs={{0,12},{2,14},{4,0},{6,2},{8,4},{10,6},{12,8},{14,10},{1,13},{3,15... | collective-permute-start | bytes 110600 | tf_op jit(solution)/shard_map/ppermute | solution.py:79
  14.3 1.4 %collective-permute-start.6 = (bf16[144,128]{1,0:T(8,128)(2,1)S(1)}, bf16[144,128]{1,0:T(8,128)(2,1)S(1)}, u32[]{:S(2)}, u32[]{:S(2)}) collective-permute-start(bf16[144,128]{1,0:T(8,128)(2,1)S(1)} %get-tuple-element.60), channel_id=1, source_target_pairs={{0,14},{2,0},{4,2},{6,4},{8,6},{10,8},{12,10},{14,12},{1,15},{3,1}... | collective-permute-start | bytes 110600 | tf_op jit(solution)/shard_map/ppermute | solution.py:79
  15.7 1.7 %shard_map.146 = (bf16[336,1024]{1,0:T(8,128)(2,1)S(1)}, bf16[320,512]{1,0:T(8,128)(2,1)S(1)}, bf16[320,512]{1,0:T(8,128)(2,1)S(1)}, bf16[512,256]{1,0:T(8,128)(2,1)S(1)}, bf16[512,256]{1,0:T(8,128)(2,1)S(1)}) custom-call(bf16[320,512]{1,0:T(8,128)(2,1)} %refs_0_.3, bf16[320,512]{1,0:T(8,128)(2,1)} %refs_1_.1, bf16[512,256]{1,0:T(8,128)(2,1)} %refs_2_.1, ...), custom_call_target="tpu_custom_call" | custom-call | tf_op jit(solution)/shard_map/pallas_call | solution.py:61
  17.4 0.0 collective-permute-done.2.refs_2_
  17.5 0.0 collective-permute-done.4.refs_4_
  17.5 0.8 %collective-permute-done.6.refs_6_ = bf16[144,128]{1,0:T(8,128)(2,1)S(1)} collective-permute-done((bf16[144,128]{1,0:T(8,128)(2,1)S(1)}, bf16[144,128]{1,0:T(8,128)(2,1)S(1)}, u32[]{:S(2)}, u32[]{:S(2)}) %collective-permute-start.6) | collective-permute-done | bytes 36896 | tf_op jit(solution)/shard_map/ppermute | solution.py:79
  18.3 0.1 collective-permute-start.7
  18.3 1.5 %collective-permute-done.7.refs_3_ = bf16[7,144,128]{2,1,0:T(8,128)(2,1)S(1)} collective-permute-done((bf16[7,144,128]{2,1,0:T(8,128)(2,1)S(1)}, bf16[7,144,128]{2,1,0:T(8,128)(2,1)S(1)}, u32[]{:S(2)}, u32[]{:S(2)}) %collective-permute-start.7) | collective-permute-done | bytes 258080 | tf_op jit(solution)/shard_map/ppermute | solution.py:79
  19.9 1.6 %shard_map.148 = (bf16[512,512]{1,0:T(8,128)(2,1)S(1)}, bf16[512,336]{1,0:T(8,128)(2,1)S(1)}, bf16[512,256]{1,0:T(8,128)(2,1)S(1)}, bf16[512,256]{1,0:T(8,128)(2...) custom-call(bf16[144,128]{1,0:T(8,128)(2,1)S(1)} %get-tuple-element.53.refs_0_, ...), custom_call_target="tpu_custom_call" | custom-call | tf_op jit(solution)/shard_map/pallas_call | solution.py:32
  21.5 1.6 %collective-permute-start.9 = (bf16[512,256]{1,0:T(8,128)(2,1)S(1)}, bf16[512,256]{1,0:T(8,128)(2,1)S(1)}, u32[]{:S(2)}, u32[]{:S(2)}) collective-permute-start(bf16[512,256]{1,0:T(8,128)(2,1)S(1)} %get-tuple-element.74), channel_id=1, source_target_pairs={{0,2},{1,5},{2,0},{3,7},{4,6},{5,1},{6,4},{7,3},{8,10},{9,13},{10,... | collective-permute-start | bytes 786440 | tf_op jit(solution)/shard_map/ppermute | solution.py:226
  23.1 1.3 %shard_map.149 = (f32[320,256]{1,0:T(8,128)S(1)}, bf16[320,256]{1,0:T(8,128)(2,1)S(1)}, f32[384,256]{1,0:T(8,128)S(1)}, bf16[384,256]{1,0:T(8,128)(2,1)S(1)}, f3...) custom-call(bf16[512,336]{1,0:T(8,128)(2,1)S(1)} %get-tuple-element.64.refs_0_, ...), custom_call_target="tpu_custom_call" | custom-call | tf_op jit(solution)/shard_map/pallas_call | solution.py:32
  24.4 0.5 collective-permute-start.10
  24.9 1.6 %collective-permute-start.11 = (bf16[384,256]{1,0:T(8,128)(2,1)S(1)}, bf16[384,256]{1,0:T(8,128)(2,1)S(1)}, u32[]{:S(2)}, u32[]{:S(2)}) collective-permute-start(bf16[384,256]{1,0:T(8,128)(2,1)S(1)} %get-tuple-element.78), channel_id=1, source_target_pairs={{0,2},{1,5},{2,0},{3,7},{4,6},{5,1},{6,4},{7,3},{8,10},{9,13},{10,... | collective-permute-start | bytes 589832 | tf_op jit(solution)/shard_map/ppermute | solution.py:226
  26.5 5.8 %collective-permute-done.11.refs_1_ = bf16[384,256]{1,0:T(8,128)(2,1)S(1)} collective-permute-done((bf16[384,256]{1,0:T(8,128)(2,1)S(1)}, bf16[384,256]{1,0:T(8,128)(2,1)S(1)}, u32[]{:S(2)}, u32[]{:S(2)}) %collective-permute-start.11) | collective-permute-done | bytes 196640 | tf_op jit(solution)/shard_map/ppermute | solution.py:226
  32.3 0.1 shard_map.150
  32.4 0.1 shard_map.151
  32.5 0.7 collective-permute-start.13
  33.1 1.4 %collective-permute-start.14 = (bf16[192,256]{1,0:T(8,128)(2,1)S(1)}, bf16[192,256]{1,0:T(8,128)(2,1)S(1)}, u32[]{:S(2)}, u32[]{:S(2)}) collective-permute-start(bf16[192,256]{1,0:T(8,128)(2,1)S(1)} %get-tuple-element.79.refs_2_), channel_id=1, source_target_pairs={{0,4},{1,3},{2,6},{3,1},{4,0},{5,7},{6,2},{7,5},{8,12},{9,11},{10,... | collective-permute-start | bytes 294920 | tf_op jit(solution)/shard_map/ppermute | solution.py:226
  34.6 0.1 shard_map.152
  34.7 0.7 collective-permute-start.12
  35.4 2.9 %collective-permute-done.14.refs_1_ = bf16[192,256]{1,0:T(8,128)(2,1)S(1)} collective-permute-done((bf16[192,256]{1,0:T(8,128)(2,1)S(1)}, bf16[192,256]{1,0:T(8,128)(2,1)S(1)}, u32[]{:S(2)}, u32[]{:S(2)}) %collective-permute-start.14) | collective-permute-done | bytes 98336 | tf_op jit(solution)/shard_map/ppermute | solution.py:226
  38.4 2.6 %collective-permute-start.16 = (bf16[112,256]{1,0:T(8,128)(2,1)S(1)}, bf16[112,256]{1,0:T(8,128)(2,1)S(1)}, u32[]{:S(2)}, u32[]{:S(2)}) collective-permute-start(bf16[112,256]{1,0:T(8,128)(2,1)S(1)} %get-tuple-element.86.refs_2_), channel_id=1, source_target_pairs={{0,8},{1,9},{2,10},{3,11},{4,12},{5,13},{6,14},{7,15},{8,0},{9,1},... | collective-permute-start | bytes 172040 | tf_op jit(solution)/shard_map/ppermute | solution.py:226
  41.0 0.4 collective-permute-start.17
  41.4 0.1 shard_map.155
  41.5 2.6 %collective-permute-start.15 = (bf16[128,256]{1,0:T(8,128)(2,1)S(1)}, bf16[128,256]{1,0:T(8,128)(2,1)S(1)}, u32[]{:S(2)}, u32[]{:S(2)}) collective-permute-start(bf16[128,256]{1,0:T(8,128)(2,1)S(1)} %get-tuple-element.88.refs_2_), channel_id=1, source_target_pairs={{0,8},{1,9},{2,10},{3,11},{4,12},{5,13},{6,14},{7,15},{8,0},{9,1},... | collective-permute-start | bytes 196616 | tf_op jit(solution)/shard_map/ppermute | solution.py:226
  44.1 3.7 %collective-permute-done.17.refs_1_ = bf16[96,256]{1,0:T(8,128)(2,1)S(1)} collective-permute-done((bf16[96,256]{1,0:T(8,128)(2,1)S(1)}, bf16[96,256]{1,0:T(8,128)(2,1)S(1)}, u32[]{:S(2)}, u32[]{:S(2)}) %collective-permute-start.17) | collective-permute-done | bytes 49184 | tf_op jit(solution)/shard_map/ppermute | solution.py:226
  47.9 0.1 collective-permute-start.20
  47.9 0.6 shard_map.157
  48.6 2.9 %collective-permute-start.19 = (bf16[96,256]{1,0:T(8,128)(2,1)S(1)}, bf16[96,256]{1,0:T(8,128)(2,1)S(1)}, u32[]{:S(2)}, u32[]{:S(2)}) collective-permute-start(bf16[96,256]{1,0:T(8,128)(2,1)S(1)} %get-tuple-element.91.refs_3_.refs_0_), channel_id=1, source_target_pairs={{0,8},{1,9},{2,10},{3,11},{4,12},{5,13},{6,14},{7,15},{8,0},{9,1},... | collective-permute-start | bytes 147464 | tf_op jit(solution)/shard_map/ppermute | solution.py:226
  51.5 0.2 shard_map.158
  51.7 1.2 %collective-permute-done.20.refs_1_ = bf16[96,256]{1,0:T(8,128)(2,1)S(1)} collective-permute-done((bf16[96,256]{1,0:T(8,128)(2,1)S(1)}, bf16[96,256]{1,0:T(8,128)(2,1)S(1)}, u32[]{:S(2)}, u32[]{:S(2)}) %collective-permute-start.20) | collective-permute-done | bytes 49184 | tf_op jit(solution)/shard_map/ppermute | solution.py:226
  52.9 0.1 collective-permute-start.21
  53.0 0.5 collective-permute-done.19.refs_1_
  53.6 2.1 %collective-permute-start.23 = (bf16[192,256]{1,0:T(8,128)(2,1)S(1)}, bf16[192,256]{1,0:T(8,128)(2,1)S(1)}, u32[]{:S(2)}, u32[]{:S(2)}) collective-permute-start(bf16[192,256]{1,0:T(8,128)(2,1)S(1)} %shard_map.160.refs_4_.refs_0_), channel_id=1, source_target_pairs={{0,4},{1,3},{2,6},{3,1},{4,0},{5,7},{6,2},{7,5},{8,12},{9,11},{10,... | collective-permute-start | bytes 294920 | tf_op jit(solution)/shard_map/ppermute | solution.py:226
  55.6 1.2 %collective-permute-done.18.refs_3_ = bf16[128,256]{1,0:T(8,128)(2,1)S(1)} collective-permute-done((bf16[128,256]{1,0:T(8,128)(2,1)S(1)}, bf16[128,256]{1,0:T(8,128)(2,1)S(1)}, u32[]{:S(2)}, u32[]{:S(2)}) %collective-permute-start.18) | collective-permute-done | bytes 65568 | tf_op jit(solution)/shard_map/ppermute | solution.py:79
  56.9 0.8 %shard_map.161 = (f32[320,256]{1,0:T(8,128)}, bf16[128,256]{1,0:T(8,128)(2,1)}) custom-call(f32[320,256]{1,0:T(8,128)S(1)} %get-tuple-element.71.refs_0_, bf16[320,256]{1,0:T(8,128)(2,1)S(1)} %collective-permute-done.8.refs_1_, f32[128,256]{1,0:T(8,128)S(1)} %get-tuple-element.92.refs_2_, bf16[128,256]{1,0:T(8,128)(2,1)S(1)} %collective-permute-done.18.refs_3_, ...), custom_call_target="tpu_custom_call" | custom-call | tf_op jit(solution)/shard_map/pallas_call | solution.py:32
  57.7 1.0 %collective-permute-done.23.refs_1_ = bf16[192,256]{1,0:T(8,128)(2,1)S(1)} collective-permute-done((bf16[192,256]{1,0:T(8,128)(2,1)S(1)}, bf16[192,256]{1,0:T(8,128)(2,1)S(1)}, u32[]{:S(2)}, u32[]{:S(2)}) %collective-permute-start.23) | collective-permute-done | bytes 98336 | tf_op jit(solution)/shard_map/ppermute | solution.py:226
  58.7 1.5 %collective-permute-start.24 = (bf16[384,256]{1,0:T(8,128)(2,1)S(1)}, bf16[384,256]{1,0:T(8,128)(2,1)S(1)}, u32[]{:S(2)}, u32[]{:S(2)}) collective-permute-start(bf16[384,256]{1,0:T(8,128)(2,1)S(1)} %shard_map.163.refs_2_), channel_id=1, source_target_pairs={{0,2},{1,5},{2,0},{3,7},{4,6},{5,1},{6,4},{7,3},{8,10},{9,13},{10,... | collective-permute-start | bytes 589832 | tf_op jit(solution)/shard_map/ppermute | solution.py:226
  60.2 0.6 collective-permute-start.22
  60.8 3.6 %collective-permute-done.24.refs_3_ = bf16[384,256]{1,0:T(8,128)(2,1)S(1)} collective-permute-done((bf16[384,256]{1,0:T(8,128)(2,1)S(1)}, bf16[384,256]{1,0:T(8,128)(2,1)S(1)}, u32[]{:S(2)}, u32[]{:S(2)}) %collective-permute-start.24) | collective-permute-done | bytes 196640 | tf_op jit(solution)/shard_map/ppermute | solution.py:226
  64.4 2.1 %collective-permute-done.22.refs_1_ = bf16[384,256]{1,0:T(8,128)(2,1)S(1)} collective-permute-done((bf16[384,256]{1,0:T(8,128)(2,1)S(1)}, bf16[384,256]{1,0:T(8,128)(2,1)S(1)}, u32[]{:S(2)}, u32[]{:S(2)}) %collective-permute-start.22) | collective-permute-done | bytes 196640 | tf_op jit(solution)/shard_map/ppermute | solution.py:226
  66.5 1.2 %shard_map.164 = (f32[512,256]{1,0:T(8,128)}, f32[256,512]{1,0:T(8,128)}, f32[512,256]{1,0:T(8,128)}) custom-call(bf16[384,256]{1,0:T(8,128)(2,1)S(1)} %shard_map.162.refs_2_.refs_0_, bf16[384,256]{1,0:T(8,128)(2,1)S(1)} %collective-permute-done.22.refs_1_, bf16[384,256]{1,0:T(8,128)(2,1)S(1)} %shard_map.163.refs_2_, ...), custom_call_target="tpu_custom_call" | custom-call | tf_op jit(solution)/shard_map/pallas_call | solution.py:32
  (22 shorter events, 0.2 us)
Async XLA Ops:
  1.9 11.0 %collective-permute-start = (bf16[144,128]{1,0:T(8,128)(2,1)S(1)}, bf16[144,128]{1,0:T(8,128)(2,1)S(1)}, u32[]{:S(2)}, u32[]{:S(2)}) collective-permute-start(bf16[144,128]{1,0:T(8,128)(2,1)S(1)} %get-tuple-element.54), channel_id=1, source_target_pairs={{0,2},{2,4},{4,6},{6,8},{8,10},{10,12},{12,14},{14,0},{1,3},{3,5},... | collective-permute-start | bytes 110600 | tf_op jit(solution)/shard_map/ppermute | solution.py:79
  4.9 9.3 %collective-permute-start.1 = (bf16[144,128]{1,0:T(8,128)(2,1)S(1)}, bf16[144,128]{1,0:T(8,128)(2,1)S(1)}, u32[]{:S(2)}, u32[]{:S(2)}) collective-permute-start(bf16[144,128]{1,0:T(8,128)(2,1)S(1)} %get-tuple-element.55), channel_id=1, source_target_pairs={{0,4},{2,6},{4,8},{6,10},{8,12},{10,14},{12,0},{14,2},{1,5},{3,7},... | collective-permute-start | bytes 110600 | tf_op jit(solution)/shard_map/ppermute | solution.py:79
  6.5 10.9 %collective-permute-start.2 = (bf16[144,128]{1,0:T(8,128)(2,1)S(1)}, bf16[144,128]{1,0:T(8,128)(2,1)S(1)}, u32[]{:S(2)}, u32[]{:S(2)}) collective-permute-start(bf16[144,128]{1,0:T(8,128)(2,1)S(1)} %get-tuple-element.56), channel_id=1, source_target_pairs={{0,6},{2,8},{4,10},{6,12},{8,14},{10,0},{12,2},{14,4},{1,7},{3,9},... | collective-permute-start | bytes 110600 | tf_op jit(solution)/shard_map/ppermute | solution.py:79
  9.1 8.4 %collective-permute-start.3 = (bf16[144,128]{1,0:T(8,128)(2,1)S(1)}, bf16[144,128]{1,0:T(8,128)(2,1)S(1)}, u32[]{:S(2)}, u32[]{:S(2)}) collective-permute-start(bf16[144,128]{1,0:T(8,128)(2,1)S(1)} %get-tuple-element.57), channel_id=1, source_target_pairs={{0,8},{2,10},{4,12},{6,14},{8,0},{10,2},{12,4},{14,6},{1,9},{3,11}... | collective-permute-start | bytes 110600 | tf_op jit(solution)/shard_map/ppermute | solution.py:79
  10.3 7.2 %collective-permute-start.4 = (bf16[144,128]{1,0:T(8,128)(2,1)S(1)}, bf16[144,128]{1,0:T(8,128)(2,1)S(1)}, u32[]{:S(2)}, u32[]{:S(2)}) collective-permute-start(bf16[144,128]{1,0:T(8,128)(2,1)S(1)} %get-tuple-element.58), channel_id=1, source_target_pairs={{0,10},{2,12},{4,14},{6,0},{8,2},{10,4},{12,6},{14,8},{1,11},{3,13... | collective-permute-start | bytes 110600 | tf_op jit(solution)/shard_map/ppermute | solution.py:79
  12.9 4.5 %collective-permute-start.5 = (bf16[144,128]{1,0:T(8,128)(2,1)S(1)}, bf16[144,128]{1,0:T(8,128)(2,1)S(1)}, u32[]{:S(2)}, u32[]{:S(2)}) collective-permute-start(bf16[144,128]{1,0:T(8,128)(2,1)S(1)} %get-tuple-element.59), channel_id=1, source_target_pairs={{0,12},{2,14},{4,0},{6,2},{8,4},{10,6},{12,8},{14,10},{1,13},{3,15... | collective-permute-start | bytes 110600 | tf_op jit(solution)/shard_map/ppermute | solution.py:79
  14.3 4.0 %collective-permute-start.6 = (bf16[144,128]{1,0:T(8,128)(2,1)S(1)}, bf16[144,128]{1,0:T(8,128)(2,1)S(1)}, u32[]{:S(2)}, u32[]{:S(2)}) collective-permute-start(bf16[144,128]{1,0:T(8,128)(2,1)S(1)} %get-tuple-element.60), channel_id=1, source_target_pairs={{0,14},{2,0},{4,2},{6,4},{8,6},{10,8},{12,10},{14,12},{1,15},{3,1}... | collective-permute-start | bytes 110600 | tf_op jit(solution)/shard_map/ppermute | solution.py:79
  18.3 1.6 %collective-permute-start.7 = (bf16[7,144,128]{2,1,0:T(8,128)(2,1)S(1)}, bf16[7,144,128]{2,1,0:T(8,128)(2,1)S(1)}, u32[]{:S(2)}, u32[]{:S(2)}) collective-permute-start(bf16[7,144,128]{2,1,0:T(8,128)(2,1)S(1)} %shard_map.147.refs_1_), channel_id=1, source_target_pairs={{0,1},{1,0},{2,3},{3,2},{4,5},{5,4},{6,7},{7,6},{8,9},{9,8},{10,11... | collective-permute-start | bytes 774152 | tf_op jit(solution)/shard_map/ppermute | solution.py:79
  21.5 13.1 %collective-permute-start.9 = (bf16[512,256]{1,0:T(8,128)(2,1)S(1)}, bf16[512,256]{1,0:T(8,128)(2,1)S(1)}, u32[]{:S(2)}, u32[]{:S(2)}) collective-permute-start(bf16[512,256]{1,0:T(8,128)(2,1)S(1)} %get-tuple-element.74), channel_id=1, source_target_pairs={{0,2},{1,5},{2,0},{3,7},{4,6},{5,1},{6,4},{7,3},{8,10},{9,13},{10,... | collective-permute-start | bytes 786440 | tf_op jit(solution)/shard_map/ppermute | solution.py:226
  24.4 8.0 %collective-permute-start.10 = (bf16[400,256]{1,0:T(8,128)(2,1)S(1)}, bf16[400,256]{1,0:T(8,128)(2,1)S(1)}, u32[]{:S(2)}, u32[]{:S(2)}) collective-permute-start(bf16[400,256]{1,0:T(8,128)(2,1)S(1)} %get-tuple-element.76), channel_id=1, source_target_pairs={{0,2},{1,5},{2,0},{3,7},{4,6},{5,1},{6,4},{7,3},{8,10},{9,13},{10,... | collective-permute-start | bytes 614408 | tf_op jit(solution)/shard_map/ppermute | solution.py:226
  24.9 7.4 %collective-permute-start.11 = (bf16[384,256]{1,0:T(8,128)(2,1)S(1)}, bf16[384,256]{1,0:T(8,128)(2,1)S(1)}, u32[]{:S(2)}, u32[]{:S(2)}) collective-permute-start(bf16[384,256]{1,0:T(8,128)(2,1)S(1)} %get-tuple-element.78), channel_id=1, source_target_pairs={{0,2},{1,5},{2,0},{3,7},{4,6},{5,1},{6,4},{7,3},{8,10},{9,13},{10,... | collective-permute-start | bytes 589832 | tf_op jit(solution)/shard_map/ppermute | solution.py:226
  32.5 5.9 %collective-permute-start.13 = (bf16[208,256]{1,0:T(8,128)(2,1)S(1)}, bf16[208,256]{1,0:T(8,128)(2,1)S(1)}, u32[]{:S(2)}, u32[]{:S(2)}) collective-permute-start(bf16[208,256]{1,0:T(8,128)(2,1)S(1)} %get-tuple-element.80.refs_2_), channel_id=1, source_target_pairs={{0,4},{1,3},{2,6},{3,1},{4,0},{5,7},{6,2},{7,5},{8,12},{9,11},{10,... | collective-permute-start | bytes 319496 | tf_op jit(solution)/shard_map/ppermute | solution.py:226
  33.1 5.2 %collective-permute-start.14 = (bf16[192,256]{1,0:T(8,128)(2,1)S(1)}, bf16[192,256]{1,0:T(8,128)(2,1)S(1)}, u32[]{:S(2)}, u32[]{:S(2)}) collective-permute-start(bf16[192,256]{1,0:T(8,128)(2,1)S(1)} %get-tuple-element.79.refs_2_), channel_id=1, source_target_pairs={{0,4},{1,3},{2,6},{3,1},{4,0},{5,7},{6,2},{7,5},{8,12},{9,11},{10,... | collective-permute-start | bytes 294920 | tf_op jit(solution)/shard_map/ppermute | solution.py:226
  34.7 6.7 %collective-permute-start.12 = (bf16[256,256]{1,0:T(8,128)(2,1)S(1)}, bf16[256,256]{1,0:T(8,128)(2,1)S(1)}, u32[]{:S(2)}, u32[]{:S(2)}) collective-permute-start(bf16[256,256]{1,0:T(8,128)(2,1)S(1)} %get-tuple-element.82.refs_2_), channel_id=1, source_target_pairs={{0,4},{1,3},{2,6},{3,1},{4,0},{5,7},{6,2},{7,5},{8,12},{9,11},{10,... | collective-permute-start | bytes 393224 | tf_op jit(solution)/shard_map/ppermute | solution.py:226
  38.4 9.5 %collective-permute-start.16 = (bf16[112,256]{1,0:T(8,128)(2,1)S(1)}, bf16[112,256]{1,0:T(8,128)(2,1)S(1)}, u32[]{:S(2)}, u32[]{:S(2)}) collective-permute-start(bf16[112,256]{1,0:T(8,128)(2,1)S(1)} %get-tuple-element.86.refs_2_), channel_id=1, source_target_pairs={{0,8},{1,9},{2,10},{3,11},{4,12},{5,13},{6,14},{7,15},{8,0},{9,1},... | collective-permute-start | bytes 172040 | tf_op jit(solution)/shard_map/ppermute | solution.py:226
  41.0 6.8 %collective-permute-start.17 = (bf16[96,256]{1,0:T(8,128)(2,1)S(1)}, bf16[96,256]{1,0:T(8,128)(2,1)S(1)}, u32[]{:S(2)}, u32[]{:S(2)}) collective-permute-start(bf16[96,256]{1,0:T(8,128)(2,1)S(1)} %get-tuple-element.85.refs_2_), channel_id=1, source_target_pairs={{0,8},{1,9},{2,10},{3,11},{4,12},{5,13},{6,14},{7,15},{8,0},{9,1},... | collective-permute-start | bytes 147464 | tf_op jit(solution)/shard_map/ppermute | solution.py:226
  41.5 10.0 %collective-permute-start.15 = (bf16[128,256]{1,0:T(8,128)(2,1)S(1)}, bf16[128,256]{1,0:T(8,128)(2,1)S(1)}, u32[]{:S(2)}, u32[]{:S(2)}) collective-permute-start(bf16[128,256]{1,0:T(8,128)(2,1)S(1)} %get-tuple-element.88.refs_2_), channel_id=1, source_target_pairs={{0,8},{1,9},{2,10},{3,11},{4,12},{5,13},{6,14},{7,15},{8,0},{9,1},... | collective-permute-start | bytes 196616 | tf_op jit(solution)/shard_map/ppermute | solution.py:226
  44.1 11.5 %collective-permute-start.8 = (bf16[320,256]{1,0:T(8,128)(2,1)S(1)}, bf16[320,256]{1,0:T(8,128)(2,1)S(1)}, u32[]{:S(2)}, u32[]{:S(2)}) collective-permute-start(bf16[320,256]{1,0:T(8,128)(2,1)S(1)} %get-tuple-element.72), channel_id=1, source_target_pairs={{0,1},{1,0},{2,3},{3,2},{4,5},{5,4},{6,7},{7,6},{8,9},{9,8},{10,11... | collective-permute-start | bytes 491528 | tf_op jit(solution)/shard_map/ppermute | solution.py:79
  47.9 5.1 %collective-permute-start.20 = (bf16[96,256]{1,0:T(8,128)(2,1)S(1)}, bf16[96,256]{1,0:T(8,128)(2,1)S(1)}, u32[]{:S(2)}, u32[]{:S(2)}) collective-permute-start(bf16[96,256]{1,0:T(8,128)(2,1)S(1)} %shard_map.156.refs_2_.refs_0_), channel_id=1, source_target_pairs={{0,8},{1,9},{2,10},{3,11},{4,12},{5,13},{6,14},{7,15},{8,0},{9,1},... | collective-permute-start | bytes 147464 | tf_op jit(solution)/shard_map/ppermute | solution.py:226
  48.6 5.0 %collective-permute-start.19 = (bf16[96,256]{1,0:T(8,128)(2,1)S(1)}, bf16[96,256]{1,0:T(8,128)(2,1)S(1)}, u32[]{:S(2)}, u32[]{:S(2)}) collective-permute-start(bf16[96,256]{1,0:T(8,128)(2,1)S(1)} %get-tuple-element.91.refs_3_.refs_0_), channel_id=1, source_target_pairs={{0,8},{1,9},{2,10},{3,11},{4,12},{5,13},{6,14},{7,15},{8,0},{9,1},... | collective-permute-start | bytes 147464 | tf_op jit(solution)/shard_map/ppermute | solution.py:226
  52.9 4.7 %collective-permute-start.21 = (bf16[192,256]{1,0:T(8,128)(2,1)S(1)}, bf16[192,256]{1,0:T(8,128)(2,1)S(1)}, u32[]{:S(2)}, u32[]{:S(2)}) collective-permute-start(bf16[192,256]{1,0:T(8,128)(2,1)S(1)} %shard_map.159.refs_2_.refs_0_), channel_id=1, source_target_pairs={{0,4},{1,3},{2,6},{3,1},{4,0},{5,7},{6,2},{7,5},{8,12},{9,11},{10,... | collective-permute-start | bytes 294920 | tf_op jit(solution)/shard_map/ppermute | solution.py:226
  53.6 5.1 %collective-permute-start.23 = (bf16[192,256]{1,0:T(8,128)(2,1)S(1)}, bf16[192,256]{1,0:T(8,128)(2,1)S(1)}, u32[]{:S(2)}, u32[]{:S(2)}) collective-permute-start(bf16[192,256]{1,0:T(8,128)(2,1)S(1)} %shard_map.160.refs_4_.refs_0_), channel_id=1, source_target_pairs={{0,4},{1,3},{2,6},{3,1},{4,0},{5,7},{6,2},{7,5},{8,12},{9,11},{10,... | collective-permute-start | bytes 294920 | tf_op jit(solution)/shard_map/ppermute | solution.py:226
  55.6 1.3 %collective-permute-start.18 = (bf16[128,256]{1,0:T(8,128)(2,1)S(1)}, bf16[128,256]{1,0:T(8,128)(2,1)S(1)}, u32[]{:S(2)}, u32[]{:S(2)}) collective-permute-start(bf16[128,256]{1,0:T(8,128)(2,1)S(1)} %get-tuple-element.93.refs_2_), channel_id=1, source_target_pairs={{0,1},{1,0},{2,3},{3,2},{4,5},{5,4},{6,7},{7,6},{8,9},{9,8},{10,11... | collective-permute-start | bytes 196616 | tf_op jit(solution)/shard_map/ppermute | solution.py:79
  58.7 5.7 %collective-permute-start.24 = (bf16[384,256]{1,0:T(8,128)(2,1)S(1)}, bf16[384,256]{1,0:T(8,128)(2,1)S(1)}, u32[]{:S(2)}, u32[]{:S(2)}) collective-permute-start(bf16[384,256]{1,0:T(8,128)(2,1)S(1)} %shard_map.163.refs_2_), channel_id=1, source_target_pairs={{0,2},{1,5},{2,0},{3,7},{4,6},{5,1},{6,4},{7,3},{8,10},{9,13},{10,... | collective-permute-start | bytes 589832 | tf_op jit(solution)/shard_map/ppermute | solution.py:226
  60.2 6.3 %collective-permute-start.22 = (bf16[384,256]{1,0:T(8,128)(2,1)S(1)}, bf16[384,256]{1,0:T(8,128)(2,1)S(1)}, u32[]{:S(2)}, u32[]{:S(2)}) collective-permute-start(bf16[384,256]{1,0:T(8,128)(2,1)S(1)} %shard_map.162.refs_2_.refs_0_), channel_id=1, source_target_pairs={{0,2},{1,5},{2,0},{3,7},{4,6},{5,1},{6,4},{7,3},{8,10},{9,13},{10,... | collective-permute-start | bytes 589832 | tf_op jit(solution)/shard_map/ppermute | solution.py:226

commit v8 on v7

--- a/solution.py
+++ b/solution.py
@@ -9,7 +9,6 @@
 
 OWNER_AXES = ("obs", "node")
 SUBLANES = 16
-BUNDLES = 2
 BF16 = jnp.bfloat16
 F32 = jnp.float32
 
@@ -151,8 +150,8 @@
 
 
 def edge_kernel(
-    fanout, nodes, steps, own_ref, mine_ref, other_ref, theirs_ref, table_ref, w_obs_ref,
-    act_ref, hot_ref, rows_mine_ref, rows_theirs_ref, keep_ref, send_ref, total_ref,
+    fanout, nodes, own_ref, mine_ref, other_ref, theirs_ref, table_ref, w_obs_ref,
+    act_ref, hot_ref, rows_mine_ref, rows_theirs_ref, pick_ref,
 ):
     owners = mine_ref.shape[0] + 1
     chunk, lanes = own_ref.shape
@@ -162,7 +161,6 @@
     me = lax.axis_index(OWNER_AXES)
     base = 1 << nodes.bit_length()
     columns = []
-    picks = []
     for j in range(owners):
         block, other = (mine_ref.at[j - 1], theirs_ref.at[j - 1]) if j else (own_ref, other_ref)
         header = block[chunk - SUBLANES :, :].astype(F32)
@@ -175,7 +173,7 @@
             hit = iota((cap, lanes), 0) == rank
             pick = pick | hit
             code = code + jnp.where(hit, row[2:3] * 16.0 + row[3:4] + slot, 0.0)
-        picks.append(pick.astype(BF16))
+        pick_ref[j * cap : (j + 1) * cap, :] = pick.astype(BF16)
         columns.append(jnp.sum(code, axis=1, keepdims=True).astype(jnp.int32))
         for c in range(half // lanes):
             rows = slice(j * cap, (j + 1) * cap)
@@ -193,14 +191,8 @@
     pre = pre + (rows[:, :hidden] + rows[:, hidden : 2 * hidden])
     g_z = rows[:, 2 * hidden : 3 * hidden] + rows[:, 3 * hidden :]
     sig = jax.nn.sigmoid(pre)
-    g_a = (g_z * sig * (1.0 + pre * (1.0 - sig))).astype(BF16)
-    act_ref[:, :hidden] = g_a
+    act_ref[:, :hidden] = (g_z * sig * (1.0 + pre * (1.0 - sig))).astype(BF16)
     act_ref[:, hidden:] = (pre * sig).astype(BF16)
-    for j, pick in enumerate(picks):
-        source = lax.rem(me - j + owners, owners)
-        begin = pl.multiple_of(place_of(source, steps) * lanes, SUBLANES)
-        total_ref[pl.ds(begin, lanes), :] = dot(pick, g_a[j * cap : (j + 1) * cap], 0, 0).astype(BF16)
-    split_half(total_ref, 0, owners * lanes, steps[0], 0, keep_ref, send_ref)
 
 
 def halving_steps():
@@ -247,75 +239,90 @@
     return rows % (2 * SUBLANES) == 0
 
 
-def split_half(total_ref, start, rows, step, tail, keep_ref, send_ref):
-    end = start + rows
-    if halves(rows):
-        rows //= 2
-        bit = own_bit(step)
-        kept, sent = [pl.ds(pl.multiple_of(start + b * rows, SUBLANES), rows) for b in (bit, 1 - bit)]
-    else:
-        kept = sent = pl.ds(start, rows)
-    keep_ref[:rows, :] = total_ref[kept, :]
-    send_ref[:rows, :] = total_ref[sent, :].astype(BF16)
+def half_rows(rows):
+    return rows // 2 if halves(rows) else rows
+
+
+def split_half(total_ref, parts, tail, step, keep_ref, send_ref):
+    begin = at = 0
+    for rows in parts:
+        half = half_rows(rows)
+        kept = sent = pl.ds(begin, rows)
+        if half < rows:
+            bit = own_bit(step)
+            kept, sent = [
+                pl.ds(pl.multiple_of(begin + b * half, SUBLANES), half) for b in (bit, 1 - bit)
+            ]
+        keep_ref[at : at + half, :] = total_ref[kept, :]
+        send_ref[at : at + half, :] = total_ref[sent, :].astype(BF16)
+        begin, at = begin + rows, at + half
     if tail:
-        both = total_ref[end : end + tail, :]
-        keep_ref[rows:, :] = both
-        send_ref[rows:, :] = both.astype(BF16)
-
-
-def weight_kernel(
-    step, bundles, tail, hot_ref, act_ref, rows_mine_ref, rows_theirs_ref, state_ref, agg_ref, w_node_ref,
-    mine_ref, theirs_ref, *refs
-):
-    halves_refs, total_ref = refs[:-1], refs[-1]
-    width, hidden = w_node_ref.shape
-    nodes = state_ref.shape[0]
+        both = total_ref[begin:, :]
+        keep_ref[at:, :] = both
+        send_ref[at:, :] = both.astype(BF16)
+
+
+def node_kernel(step, hot_ref, act_ref, state_ref, agg_ref, hidden_ref, slot_ref, keep_ref, send_ref, total_ref):
+    nodes, width = state_ref.shape
+    hidden = total_ref.shape[1]
     sums = dot(hot_ref[...], act_ref[...], 0, 0)
     by_node = sums[:nodes].astype(BF16)
     node_hidden, z_sum = by_node[:, :hidden], by_node[:, hidden:]
+    hidden_ref[...] = node_hidden
+    slot_ref[...] = sums[nodes:, :hidden]
     total_ref[:width, :] = dot(state_ref[...], node_hidden, 0, 0)
-    begin = width
-    for c in range(width // hidden):
-        total_ref[begin : begin + hidden, :] = dot(
-            z_sum, agg_ref[:, c * hidden : (c + 1) * hidden], 0, 0
+    for begin in range(0, width, hidden):
+        total_ref[width + begin : width + begin + hidden, :] = dot(
+            z_sum, agg_ref[:, begin : begin + hidden], 0, 0
         )
-        begin += hidden
+    split_half(total_ref, [total_ref.shape[0]], 0, step, keep_ref, send_ref)
+
+
+def rows_kernel(
+    steps, owners, act_ref, rows_mine_ref, rows_theirs_ref, pick_ref, slot_ref, keep_ref, send_ref, total_ref
+):
+    edges, obs = pick_ref.shape
+    half, hidden = rows_mine_ref.shape[1], total_ref.shape[1]
     g_a = act_ref[:, :hidden]
-    core, half = lax.axis_index("mp"), width // 2
+    core = lax.axis_index("mp")
     for which, ref in ((core, rows_mine_ref), (1 - core, rows_theirs_ref)):
-        total_ref[pl.ds(pl.multiple_of(begin + which * half, SUBLANES), half), :] = dot(ref[...], g_a, 0, 0)
-    begin += width
-    total_ref[begin:, :] = sums[nodes:, :hidden]
-    rows = begin // bundles
-    for i in range(bundles):
-        split_half(
-            total_ref, i * rows, rows, step, tail if i == bundles - 1 else 0,
-            halves_refs[2 * i], halves_refs[2 * i + 1],
-        )
+        total_ref[pl.ds(pl.multiple_of(which * half, SUBLANES), half), :] = dot(ref[...], g_a, 0, 0)
+    me, cap, begin = lax.axis_index(OWNER_AXES), edges // owners, 2 * half
+    for j in range(owners):
+        source = lax.rem(me - j + owners, owners)
+        place = pl.multiple_of(begin + place_of(source, steps) * obs, SUBLANES)
+        edges_of = slice(j * cap, (j + 1) * cap)
+        total_ref[pl.ds(place, obs), :] = dot(pick_ref[edges_of, :], g_a[edges_of], 0, 0)
+    total_ref[begin + owners * obs :, :] = slot_ref[...]
+    split_half(
+        total_ref, [begin, owners * obs], slot_ref.shape[0], steps[0], keep_ref, send_ref
+    )
+
+
+def grad_node_kernel(hidden_ref, w_node_ref, mine_ref, theirs_ref):
     mine, theirs = other_half(w_node_ref)
-    theirs_ref[...] = dot(node_hidden, theirs, 1, 1).astype(BF16)
-    mine_ref[...] = dot(node_hidden, mine, 1, 1)
-
-
-def obs_kernel(keep_ref, got_ref, w_ref, mine_ref, theirs_ref):
-    obs_hidden = (keep_ref[...].astype(F32) + got_ref[...].astype(F32)).astype(BF16)
+    theirs_ref[...] = dot(hidden_ref[...], theirs, 1, 1).astype(BF16)
+    mine_ref[...] = dot(hidden_ref[...], mine, 1, 1)
+
+
+def add_kernel(parts, tail, step, keep_ref, got_ref, next_ref, send_ref, total_ref):
+    total_ref[...] = keep_ref[...] + got_ref[...].astype(F32)
+    split_half(total_ref, parts, tail, step, next_ref, send_ref)
+
+
+def piece_kernel(keep_ref, got_ref, piece_ref):
+    piece_ref[...] = (keep_ref[...] + got_ref[...].astype(F32)).astype(BF16)
+
+
+def obs_kernel(keep_ref, got_ref, w_ref, piece_ref, slot_ref, mine_ref, theirs_ref):
+    total = keep_ref[...] + got_ref[...].astype(F32)
+    rows, obs = piece_ref.shape[0], mine_ref.shape[0]
+    piece_ref[...] = total[:rows].astype(BF16)
+    slot_ref[...] = total[rows + obs : rows + obs + slot_ref.shape[0]]
+    obs_hidden = total[rows : rows + obs].astype(BF16)
     mine, theirs = other_half(w_ref)
     theirs_ref[...] = dot(obs_hidden, theirs, 1, 1).astype(BF16)
     mine_ref[...] = dot(obs_hidden, mine, 1, 1)
-
-
-def add_kernel(step, tail, keep_ref, got_ref, next_ref, send_ref, total_ref):
-    total = keep_ref[...].astype(F32) + got_ref[...].astype(F32)
-    total_ref[...] = total.astype(total_ref.dtype)
-    split_half(total_ref, 0, total_ref.shape[0] - tail, step, tail, next_ref, send_ref)
-
-
-def last_kernel(keep_ref, got_ref, piece_ref, *slot_refs):
-    total = keep_ref[...] + got_ref[...].astype(F32)
-    rows = piece_ref.shape[0]
-    piece_ref[...] = total[:rows].astype(BF16)
-    for slot_ref in slot_refs:
-        slot_ref[...] = total[rows : rows + slot_ref.shape[0]]
 
 
 def join_kernel(step, mine_ref, got_ref, out_ref):
@@ -325,15 +332,13 @@
     out_ref[pl.ds(pl.multiple_of((1 - bit) * rows, SUBLANES), rows), :] = got_ref[...]
 
 
-def spread_kernel(step, bundles, *refs):
+def spread(step, mine_ref, got_ref, out_refs):
     low = own_bit(step) == 0
-    joined = []
-    for i in range(bundles):
-        mine, got = refs[2 * i][...], refs[2 * i + 1][...]
-        joined += [jnp.where(low, mine, got), jnp.where(low, got, mine)]
-    half, hidden = joined[0].shape
+    mine, got = mine_ref[...], got_ref[...]
+    joined = [jnp.where(low, mine, got), jnp.where(low, got, mine)]
+    half, hidden = mine.shape
     at = 0
-    for out_ref in refs[2 * bundles :]:
+    for out_ref in out_refs:
         for c in range(out_ref.shape[1] // hidden):
             begin = 0
             while begin < out_ref.shape[0]:
@@ -345,24 +350,28 @@
                 at, begin = at + count, begin + count
 
 
-def merge_kernel(node_ref, node_got_ref, obs_ref, obs_got_ref, grad_node_ref, grad_obs_ref):
+def node_out_kernel(
+    step, mine_ref, got_ref, node_ref, node_got_ref, obs_ref, obs_got_ref, w_node_ref, w_out_ref, grad_node_ref, grad_obs_ref
+):
+    spread(step, mine_ref, got_ref, (w_node_ref, w_out_ref))
     grad_node_ref[...] = node_ref[...] + node_got_ref[...].astype(F32)
     grad_obs_ref[...] = (obs_ref[...] + obs_got_ref[...].astype(F32)).astype(BF16)
 
 
-def half_rows(rows):
-    return rows // 2 if halves(rows) else rows
-
-
-def summing(steps, tail, keep, send, after):
+def obs_out_kernel(step, mine_ref, got_ref, w_obs_ref):
+    spread(step, mine_ref, got_ref, (w_obs_ref,))
+
+
+def summing(steps, parts, tail, keep, send, after):
     hidden = keep.shape[1]
     for done, nxt in zip(steps[:-1], steps[1:]):
-        rows = half_rows(keep.shape[0] - tail) + tail
+        parts = [half_rows(rows) for rows in parts]
+        share = sum(map(half_rows, parts)) + tail
         keep, send = call(
-            functools.partial(add_kernel, nxt, tail),
-            [((rows, hidden), keep.dtype), ((rows, hidden), BF16)],
+            functools.partial(add_kernel, parts, tail, nxt),
+            [((share, hidden), F32), ((share, hidden), BF16)],
             keep, flip(send, done),
-            scratch=[pltpu.VMEM(keep.shape, keep.dtype)],
+            scratch=[pltpu.VMEM(keep.shape, F32)],
             after=after,
         )
         after[:] = [send]
@@ -370,21 +379,12 @@
     return keep, flip(send, steps[-1])
 
 
-def weight_chain(steps, rows, tail, slots, keep, send, after):
+def gathering(steps, rows, piece, after):
     used = []
     for step in steps:
         if halves(rows):
             used.append(step)
             rows //= 2
-    keep, got = yield from summing(steps, tail, keep, send, after)
-    piece, *sums = call(
-        last_kernel,
-        [((rows, keep.shape[1]), BF16)] + ([((slots, keep.shape[1]), F32)] if tail else []),
-        keep, got,
-        after=after,
-    )
-    after[:] = [piece]
-    yield
     for step in used[:0:-1]:
         (piece,) = call(
             functools.partial(join_kernel, step),
@@ -394,26 +394,37 @@
         )
         after[:] = [piece]
         yield
-    return [piece, flip(piece, used[0])], sums
-
-
-def obs_chain(steps, w_obs, node_mine, node_theirs, keep, send, after):
-    keep, got = yield from summing(steps, 0, keep, send, after)
-    half = w_obs.shape[0] // 2
-    obs_mine, obs_theirs = call(
-        obs_kernel, [((keep.shape[0], half), F32), ((keep.shape[0], half), BF16)], keep, got, w_obs,
+    return piece, flip(piece, used[0])
+
+
+def final_rows(steps, rows):
+    for _ in steps:
+        rows = half_rows(rows)
+    return rows
+
+
+def node_chain(steps, rows, keep, send, after):
+    keep, got = yield from summing(steps, [rows], 0, keep, send, after)
+    (piece,) = call(piece_kernel, [(keep.shape, BF16)], keep, got, after=after)
+    after[:] = [piece]
+    yield
+    return (yield from gathering(steps, rows, piece, after))
+
+
+def obs_chain(steps, w_obs, parts, tail, slots, keep, send, after):
+    keep, got = yield from summing(steps, parts, tail, keep, send, after)
+    half, hidden = w_obs.shape[0] // 2, w_obs.shape[1]
+    rows, obs = [final_rows(steps, count) for count in parts]
+    piece, grad_slot, obs_mine, obs_theirs = call(
+        obs_kernel,
+        [((rows, hidden), BF16), ((slots, hidden), F32), ((obs, half), F32), ((obs, half), BF16)],
+        keep, got, w_obs,
         after=after,
     )
-    after[:] = [obs_theirs]
+    after[:] = [piece]
     yield
-    grad_node, grad_obs = call(
-        merge_kernel, [(node_mine.shape, F32), (obs_mine.shape, BF16)],
-        node_mine, shift(node_theirs, "mp", 1), obs_mine, shift(obs_theirs, "mp", 1),
-        after=after,
-    )
-    after[:] = [pltpu.with_memory_space_constraint(grad_obs, pltpu.HBM)]
-    yield
-    return grad_node, grad_obs
+    ends = yield from gathering(steps, parts[0], piece, after)
+    return ends, grad_slot, obs_mine, obs_theirs
 
 
 def in_turns(chains):
@@ -461,43 +472,52 @@
         after=(w_obs_held,),
     )
     theirs = shift(mine, "mp", 1)
-    act, hot, rows_mine, rows_theirs, obs_keep, obs_send = call(
-        functools.partial(edge_kernel, fanout, nodes, steps),
+    act, hot, rows_mine, rows_theirs, pick = call(
+        functools.partial(edge_kernel, fanout, nodes),
         [((edges, 2 * hidden), BF16), ((edges, nodes + tail), BF16)]
         + [((edges, half), BF16)] * 2
-        + [((owners * obs // 2, hidden), BF16)] * 2,
+        + [((edges, obs), BF16)],
         packed[0], mine, other, theirs, table, w_obs_held,
-        scratch=[pltpu.VMEM((owners * obs, hidden), BF16)],
-    )
-
-    stack = 2 * width + width // hidden * hidden
-    bundles = BUNDLES
-    rows = stack // bundles
-    shapes = []
-    for i in range(bundles):
-        share = rows // 2 + (tail if i == bundles - 1 else 0)
-        shapes += [((share, hidden), F32), ((share, hidden), BF16)]
-    node_mine, node_theirs, *shares = call(
-        functools.partial(weight_kernel, steps[0], bundles, tail),
-        [((nodes, half), F32), ((nodes, half), BF16)] + shapes,
-        hot, act, rows_mine, rows_theirs, state_held, agg_held, w_node_held,
-        scratch=[pltpu.VMEM((stack + tail, hidden), F32)],
-    )
+    )
+
     after = []
-    chains = [
-        weight_chain(
-            steps, rows, tail if i == bundles - 1 else 0, slots, shares[2 * i], shares[2 * i + 1], after
-        )
-        for i in range(bundles)
-    ]
-    chains.append(obs_chain(steps, w_obs_held, node_mine, node_theirs, obs_keep, obs_send, after))
-    *weights, (grad_node, grad_obs) = in_turns(chains)
-    ends = [end for pair, _ in weights for end in pair]
-    (grad_slot,) = weights[-1][1]
-    grad_w_node, grad_w_out, grad_w_obs = call(
-        functools.partial(spread_kernel, steps[0], bundles),
-        [((width, hidden), F32), ((hidden, width), F32), ((width, hidden), F32)],
-        *ends,
+    stack = width + width // hidden * hidden
+    share = half_rows(stack)
+    node_hidden, slot_sums, keep, send = call(
+        functools.partial(node_kernel, steps[0]),
+        [((nodes, hidden), BF16), ((tail, hidden), F32), ((share, hidden), F32), ((share, hidden), BF16)],
+        hot, act, state_held, agg_held,
+        scratch=[pltpu.VMEM((stack, hidden), F32)],
+    )
+    first = node_chain(steps, stack, keep, send, after)
+    parts = [width, owners * obs]
+    share = sum(map(half_rows, parts)) + tail
+    keep, send = call(
+        functools.partial(rows_kernel, steps, owners),
+        [((share, hidden), F32), ((share, hidden), BF16)],
+        act, rows_mine, rows_theirs, pick, slot_sums,
+        scratch=[pltpu.VMEM((sum(parts) + tail, hidden), F32)],
+    )
+    second = obs_chain(steps, w_obs_held, parts, tail, slots, keep, send, after)
+    node_mine, node_theirs = call(
+        grad_node_kernel, [((nodes, half), F32), ((nodes, half), BF16)], node_hidden, w_node_held
+    )
+    after[:] = [node_theirs]
+    node_ends, (obs_ends, grad_slot, obs_mine, obs_theirs) = in_turns([first, second])
+    grad_w_node, grad_w_out, grad_node, grad_obs = call(
+        functools.partial(node_out_kernel, steps[0]),
+        [
+            ((width, hidden), F32),
+            ((hidden, width), F32),
+            ((nodes, half), F32),
+            ((obs, half), BF16),
+        ],
+        *node_ends, node_mine, shift(node_theirs, "mp", 1), obs_mine, shift(obs_theirs, "mp", 1),
+        after=after,
+    )
+    (grad_w_obs,) = call(
+        functools.partial(obs_out_kernel, steps[0]), [((width, hidden), F32)], *obs_ends,
+        after=[pltpu.with_memory_space_constraint(grad_obs, pltpu.HBM)],
     )
     return grad_obs, grad_node, grad_w_obs, grad_w_node, grad_w_out, grad_slot
 

time: 67.9 us -> 73.8 us (1.087)
  waiting for transfers between devices: 24.6 us -> 36.4 us
  starting transfers between devices: 33.1 us -> 27 us
    ppermute x15 -> x12, waiting for transfers between devices: 21 us -> 32.9 us  [flip(): return lax.ppermute(value, axes, pairs)]
    ppermute x15 -> x12, starting transfers between devices: 19.3 us -> 13.1 us  [flip(): return lax.ppermute(value, axes, pairs)]
    pallas_call x18 -> x17, Pallas kernels: 6.19 us -> 6.34 us  [call(): pl.pallas_call(lambda *refs: kernel(*refs[:count], *refs[len(args):]), ou...]
  transfers between devices with their start and end apart: 25 -> 22, of which waited for: 11 -> 12; matrix products, arithmetic and copies ran while one was open for 0% -> 0% of each run, Pallas kernels for 7% -> 6%
where the time goes in v8:
time: 73.8 us; the launch traced here: 73.6 us
  waiting for transfers between devices  36.4 us (49%)
  starting transfers between devices  27 us (37%)
  Pallas kernels  9.36 us (13%)
  between operations  0.8 us (1%)
    ppermute x12, waiting for transfers between devices, flip(): return lax.ppermute(value, axes, pairs)  32.9 us
    ppermute x10, starting transfers between devices, shift(): lax.ppermute(value, axis, [(i, (i + step) % size) for i in range(size)])  13.8 us
    ppermute x12, starting transfers between devices, flip(): return lax.ppermute(value, axes, pairs)  13.1 us
    pallas_call x17, Pallas kernels, call(): pl.pallas_call(lambda *refs: kernel(*refs[:count], *refs[len(args):]), ou...  6.34 us
    ppermute x10, waiting for transfers between devices, shift(): lax.ppermute(value, axis, [(i, (i + step) % size) for i in range(size)])  3.54 us
    pallas_call x2, Pallas kernels, call_staged(): pl.pallas_call(staged, out_shape=[jax.ShapeDtypeStruct(shape, dtype) for...  3.03 us
  transfers between devices with their start and end apart: 22, of which 12 were waited for; matrix products, arithmetic and copies ran while one was open for 0% of the time, Pallas kernels for 6%

profile of v8, /device:TPU:0, one launch (start us, length us, event | category | flops | bytes accessed | tf_op | source)
XLA Modules:
  0.0 73.6 jit_solution(3641943289809411203)
XLA Ops:
  0.6 1.3 %shard_map.145 = (bf16[144,128]{1,0:T(8,128)(2,1)S(1)}, bf16[144,128]{1,0:T(8,128)(2,1)S(1)}, bf16[144,128]{1,0:T(8,128)(2,1)S(1)}, bf16[144,128]{1,0:T(8,128)(2...) custom-call(bf16[128,512]{1,0:T(8,128)(2,1)} %refs_0_.2, ...), custom_call_target="tpu_custom_call" | custom-call | tf_op jit(solution)/shard_map/pallas_call | solution.py:60
  1.9 3.0 %collective-permute-start = (bf16[144,128]{1,0:T(8,128)(2,1)S(1)}, bf16[144,128]{1,0:T(8,128)(2,1)S(1)}, u32[]{:S(2)}, u32[]{:S(2)}) collective-permute-start(bf16[144,128]{1,0:T(8,128)(2,1)S(1)} %get-tuple-element.50), channel_id=1, source_target_pairs={{0,2},{2,4},{4,6},{6,8},{8,10},{10,12},{12,14},{14,0},{1,3},{3,5},... | collective-permute-start | bytes 110600 | tf_op jit(solution)/shard_map/ppermute | solution.py:78
  4.9 1.6 %collective-permute-start.1 = (bf16[144,128]{1,0:T(8,128)(2,1)S(1)}, bf16[144,128]{1,0:T(8,128)(2,1)S(1)}, u32[]{:S(2)}, u32[]{:S(2)}) collective-permute-start(bf16[144,128]{1,0:T(8,128)(2,1)S(1)} %get-tuple-element.51), channel_id=1, source_target_pairs={{0,4},{2,6},{4,8},{6,10},{8,12},{10,14},{12,0},{14,2},{1,5},{3,7},... | collective-permute-start | bytes 110600 | tf_op jit(solution)/shard_map/ppermute | solution.py:78
  6.5 2.6 %collective-permute-start.2 = (bf16[144,128]{1,0:T(8,128)(2,1)S(1)}, bf16[144,128]{1,0:T(8,128)(2,1)S(1)}, u32[]{:S(2)}, u32[]{:S(2)}) collective-permute-start(bf16[144,128]{1,0:T(8,128)(2,1)S(1)} %get-tuple-element.52), channel_id=1, source_target_pairs={{0,6},{2,8},{4,10},{6,12},{8,14},{10,0},{12,2},{14,4},{1,7},{3,9},... | collective-permute-start | bytes 110600 | tf_op jit(solution)/shard_map/ppermute | solution.py:78
  9.1 1.2 %collective-permute-start.3 = (bf16[144,128]{1,0:T(8,128)(2,1)S(1)}, bf16[144,128]{1,0:T(8,128)(2,1)S(1)}, u32[]{:S(2)}, u32[]{:S(2)}) collective-permute-start(bf16[144,128]{1,0:T(8,128)(2,1)S(1)} %get-tuple-element.53), channel_id=1, source_target_pairs={{0,8},{2,10},{4,12},{6,14},{8,0},{10,2},{12,4},{14,6},{1,9},{3,11}... | collective-permute-start | bytes 110600 | tf_op jit(solution)/shard_map/ppermute | solution.py:78
  10.3 2.6 %collective-permute-start.4 = (bf16[144,128]{1,0:T(8,128)(2,1)S(1)}, bf16[144,128]{1,0:T(8,128)(2,1)S(1)}, u32[]{:S(2)}, u32[]{:S(2)}) collective-permute-start(bf16[144,128]{1,0:T(8,128)(2,1)S(1)} %get-tuple-element.54), channel_id=1, source_target_pairs={{0,10},{2,12},{4,14},{6,0},{8,2},{10,4},{12,6},{14,8},{1,11},{3,13... | collective-permute-start | bytes 110600 | tf_op jit(solution)/shard_map/ppermute | solution.py:78
  12.9 1.4 %collective-permute-start.5 = (bf16[144,128]{1,0:T(8,128)(2,1)S(1)}, bf16[144,128]{1,0:T(8,128)(2,1)S(1)}, u32[]{:S(2)}, u32[]{:S(2)}) collective-permute-start(bf16[144,128]{1,0:T(8,128)(2,1)S(1)} %get-tuple-element.55), channel_id=1, source_target_pairs={{0,12},{2,14},{4,0},{6,2},{8,4},{10,6},{12,8},{14,10},{1,13},{3,15... | collective-permute-start | bytes 110600 | tf_op jit(solution)/shard_map/ppermute | solution.py:78
  14.3 1.4 %collective-permute-start.6 = (bf16[144,128]{1,0:T(8,128)(2,1)S(1)}, bf16[144,128]{1,0:T(8,128)(2,1)S(1)}, u32[]{:S(2)}, u32[]{:S(2)}) collective-permute-start(bf16[144,128]{1,0:T(8,128)(2,1)S(1)} %get-tuple-element.56), channel_id=1, source_target_pairs={{0,14},{2,0},{4,2},{6,4},{8,6},{10,8},{12,10},{14,12},{1,15},{3,1}... | collective-permute-start | bytes 110600 | tf_op jit(solution)/shard_map/ppermute | solution.py:78
  15.7 1.7 %shard_map.146 = (bf16[336,1024]{1,0:T(8,128)(2,1)S(1)}, bf16[320,512]{1,0:T(8,128)(2,1)S(1)}, bf16[320,512]{1,0:T(8,128)(2,1)S(1)}, bf16[512,256]{1,0:T(8,128)(2,1)S(1)}, bf16[512,256]{1,0:T(8,128)(2,1)S(1)}) custom-call(bf16[320,512]{1,0:T(8,128)(2,1)} %refs_0_.3, bf16[320,512]{1,0:T(8,128)(2,1)} %refs_1_.1, bf16[512,256]{1,0:T(8,128)(2,1)} %refs_2_.1, ...), custom_call_target="tpu_custom_call" | custom-call | tf_op jit(solution)/shard_map/pallas_call | solution.py:60
  17.4 0.0 collective-permute-done.2.refs_2_
  17.5 0.0 collective-permute-done.4.refs_4_
  17.5 0.0 collective-permute-done.5.refs_5_
  17.5 0.8 %collective-permute-done.6.refs_6_ = bf16[144,128]{1,0:T(8,128)(2,1)S(1)} collective-permute-done((bf16[144,128]{1,0:T(8,128)(2,1)S(1)}, bf16[144,128]{1,0:T(8,128)(2,1)S(1)}, u32[]{:S(2)}, u32[]{:S(2)}) %collective-permute-start.6) | collective-permute-done | bytes 36896 | tf_op jit(solution)/shard_map/ppermute | solution.py:78
  18.3 0.1 collective-permute-start.7
  18.3 1.5 %collective-permute-done.7.refs_3_ = bf16[7,144,128]{2,1,0:T(8,128)(2,1)S(1)} collective-permute-done((bf16[7,144,128]{2,1,0:T(8,128)(2,1)S(1)}, bf16[7,144,128]{2,1,0:T(8,128)(2,1)S(1)}, u32[]{:S(2)}, u32[]{:S(2)}) %collective-permute-start.7) | collective-permute-done | bytes 258080 | tf_op jit(solution)/shard_map/ppermute | solution.py:78
  19.9 1.2 %shard_map.148 = (bf16[512,512]{1,0:T(8,128)(2,1)S(1)}, bf16[512,336]{1,0:T(8,128)(2,1)S(1)}, bf16[512,256]{1,0:T(8,128)(2,1)S(1)}, bf16[512,256]{1,0:T(8,128)(2,1)S(1)}, bf16[512,128]{1,0:T(8,128)(2,1)S(1)}) custom-call(bf16[144,128]{1,0:T(8,128)(2,1)S(1)} %get-tuple-element.49.refs_0_, bf16[7,144,128]{2,1,0:T(8,128)(2,1)S(1)} %shard_map.147.refs_1_, ...), custom_call_target="tpu_custom_call" | custom-call | tf_op jit(solution)/shard_map/pallas_call | solution.py:31
  21.1 1.0 %shard_map.149 = (bf16[320,256]{1,0:T(8,128)(2,1)S(1)}, f32[16,256]{1,0:T(8,128)S(1)}, f32[512,256]{1,0:T(8,128)S(1)}, bf16[512,256]{1,0:T(8,128)(2,1)S(1)}) custom-call(bf16[512,336]{1,0:T(8,128)(2,1)S(1)} %get-tuple-element.60.refs_0_, bf16[512,512]{1,0:T(8,128)(2,1)S(1)} %get-tuple-element.61.refs_1_.refs_0_, ...), custom_call_target="tpu_custom_call" | custom-call | tf_op jit(solution)/shard_map/pallas_call | solution.py:31
  22.1 0.7 shard_map.152
  22.8 1.6 %collective-permute-start.10 = (bf16[784,256]{1,0:T(8,128)(2,1)S(1)}, bf16[784,256]{1,0:T(8,128)(2,1)S(1)}, u32[]{:S(2)}, u32[]{:S(2)}) collective-permute-start(bf16[784,256]{1,0:T(8,128)(2,1)S(1)} %get-tuple-element.76), channel_id=1, source_target_pairs={{0,2},{1,5},{2,0},{3,7},{4,6},{5,1},{6,4},{7,3},{8,10},{9,13},{10,... | collective-permute-start | bytes 1204232 | tf_op jit(solution)/shard_map/ppermute | solution.py:218
  24.4 0.5 collective-permute-start.8
  24.9 0.3 shard_map.150
  25.1 8.4 %collective-permute-done.8.refs_1_ = bf16[512,256]{1,0:T(8,128)(2,1)S(1)} collective-permute-done((bf16[512,256]{1,0:T(8,128)(2,1)S(1)}, bf16[512,256]{1,0:T(8,128)(2,1)S(1)}, u32[]{:S(2)}, u32[]{:S(2)}) %collective-permute-start.8) | collective-permute-done | bytes 262176 | tf_op jit(solution)/shard_map/ppermute | solution.py:218
  33.5 0.1 shard_map.151
  33.6 0.2 shard_map.153
  33.8 0.7 %collective-permute-start.12 = (bf16[400,256]{1,0:T(8,128)(2,1)S(1)}, bf16[400,256]{1,0:T(8,128)(2,1)S(1)}, u32[]{:S(2)}, u32[]{:S(2)}) collective-permute-start(bf16[400,256]{1,0:T(8,128)(2,1)S(1)} %get-tuple-element.77.refs_2_), channel_id=1, source_target_pairs={{0,4},{1,3},{2,6},{3,1},{4,0},{5,7},{6,2},{7,5},{8,12},{9,11},{10,... | collective-permute-start | bytes 614408 | tf_op jit(solution)/shard_map/ppermute | solution.py:218
  34.5 1.3 %collective-permute-start.9 = (bf16[256,256]{1,0:T(8,128)(2,1)S(1)}, bf16[256,256]{1,0:T(8,128)(2,1)S(1)}, u32[]{:S(2)}, u32[]{:S(2)}) collective-permute-start(bf16[256,256]{1,0:T(8,128)(2,1)S(1)} %get-tuple-element.70.refs_2_), channel_id=1, source_target_pairs={{0,4},{1,3},{2,6},{3,1},{4,0},{5,7},{6,2},{7,5},{8,12},{9,11},{10,... | collective-permute-start | bytes 393224 | tf_op jit(solution)/shard_map/ppermute | solution.py:218
  35.9 5.1 %collective-permute-done.9.refs_1_ = bf16[256,256]{1,0:T(8,128)(2,1)S(1)} collective-permute-done((bf16[256,256]{1,0:T(8,128)(2,1)S(1)}, bf16[256,256]{1,0:T(8,128)(2,1)S(1)}, u32[]{:S(2)}, u32[]{:S(2)}) %collective-permute-start.9) | collective-permute-done | bytes 131104 | tf_op jit(solution)/shard_map/ppermute | solution.py:218
  41.1 1.3 %collective-permute-start.11 = (bf16[128,256]{1,0:T(8,128)(2,1)S(1)}, bf16[128,256]{1,0:T(8,128)(2,1)S(1)}, u32[]{:S(2)}, u32[]{:S(2)}) collective-permute-start(bf16[128,256]{1,0:T(8,128)(2,1)S(1)} %get-tuple-element.79.refs_2_), channel_id=1, source_target_pairs={{0,8},{1,9},{2,10},{3,11},{4,12},{5,13},{6,14},{7,15},{8,0},{9,1},... | collective-permute-start | bytes 196616 | tf_op jit(solution)/shard_map/ppermute | solution.py:218
  42.4 0.0 collective-permute-done.12.refs_1_
  42.4 0.1 shard_map.155
  42.5 1.8 %collective-permute-start.14 = (bf16[208,256]{1,0:T(8,128)(2,1)S(1)}, bf16[208,256]{1,0:T(8,128)(2,1)S(1)}, u32[]{:S(2)}, u32[]{:S(2)}) collective-permute-start(bf16[208,256]{1,0:T(8,128)(2,1)S(1)} %get-tuple-element.81.refs_2_), channel_id=1, source_target_pairs={{0,8},{1,9},{2,10},{3,11},{4,12},{5,13},{6,14},{7,15},{8,0},{9,1},... | collective-permute-start | bytes 319496 | tf_op jit(solution)/shard_map/ppermute | solution.py:218
  44.2 6.3 %collective-permute-done.11.refs_1_ = bf16[128,256]{1,0:T(8,128)(2,1)S(1)} collective-permute-done((bf16[128,256]{1,0:T(8,128)(2,1)S(1)}, bf16[128,256]{1,0:T(8,128)(2,1)S(1)}, u32[]{:S(2)}, u32[]{:S(2)}) %collective-permute-start.11) | collective-permute-done | bytes 65568 | tf_op jit(solution)/shard_map/ppermute | solution.py:218
  50.5 0.1 collective-permute-start.13
  50.6 1.3 %collective-permute-done.14.refs_1_ = bf16[208,256]{1,0:T(8,128)(2,1)S(1)} collective-permute-done((bf16[208,256]{1,0:T(8,128)(2,1)S(1)}, bf16[208,256]{1,0:T(8,128)(2,1)S(1)}, u32[]{:S(2)}, u32[]{:S(2)}) %collective-permute-start.14) | collective-permute-done | bytes 106528 | tf_op jit(solution)/shard_map/ppermute | solution.py:218
  51.8 0.7 shard_map.157
  52.5 3.2 %collective-permute-done.13.refs_1_ = bf16[128,256]{1,0:T(8,128)(2,1)S(1)} collective-permute-done((bf16[128,256]{1,0:T(8,128)(2,1)S(1)}, bf16[128,256]{1,0:T(8,128)(2,1)S(1)}, u32[]{:S(2)}, u32[]{:S(2)}) %collective-permute-start.13) | collective-permute-done | bytes 65568 | tf_op jit(solution)/shard_map/ppermute | solution.py:218
  55.8 0.1 collective-permute-start.15
  55.8 2.5 %collective-permute-start.16 = (bf16[64,256]{1,0:T(8,128)(2,1)S(1)}, bf16[64,256]{1,0:T(8,128)(2,1)S(1)}, u32[]{:S(2)}, u32[]{:S(2)}) collective-permute-start(bf16[64,256]{1,0:T(8,128)(2,1)S(1)} %get-tuple-element.83.refs_2_.refs_0_), channel_id=1, source_target_pairs={{0,8},{1,9},{2,10},{3,11},{4,12},{5,13},{6,14},{7,15},{8,0},{9,1},... | collective-permute-start | bytes 98312 | tf_op jit(solution)/shard_map/ppermute | solution.py:218
  58.3 2.5 %collective-permute-done.16.refs_1_ = bf16[64,256]{1,0:T(8,128)(2,1)S(1)} collective-permute-done((bf16[64,256]{1,0:T(8,128)(2,1)S(1)}, bf16[64,256]{1,0:T(8,128)(2,1)S(1)}, u32[]{:S(2)}, u32[]{:S(2)}) %collective-permute-start.16) | collective-permute-done | bytes 32800 | tf_op jit(solution)/shard_map/ppermute | solution.py:218
  60.8 1.7 %collective-permute-done.15.refs_1_ = bf16[256,256]{1,0:T(8,128)(2,1)S(1)} collective-permute-done((bf16[256,256]{1,0:T(8,128)(2,1)S(1)}, bf16[256,256]{1,0:T(8,128)(2,1)S(1)}, u32[]{:S(2)}, u32[]{:S(2)}) %collective-permute-start.15) | collective-permute-done | bytes 131104 | tf_op jit(solution)/shard_map/ppermute | solution.py:218
  62.6 0.5 collective-permute-start.17
  63.1 0.8 %collective-permute-start.20 = (bf16[128,256]{1,0:T(8,128)(2,1)S(1)}, bf16[128,256]{1,0:T(8,128)(2,1)S(1)}, u32[]{:S(2)}, u32[]{:S(2)}) collective-permute-start(bf16[128,256]{1,0:T(8,128)(2,1)S(1)} %shard_map.159.refs_2_.refs_0_), channel_id=1, source_target_pairs={{0,4},{1,3},{2,6},{3,1},{4,0},{5,7},{6,2},{7,5},{8,12},{9,11},{10,... | collective-permute-start | bytes 196616 | tf_op jit(solution)/shard_map/ppermute | solution.py:218
  63.9 3.8 %collective-permute-done.20.refs_1_ = bf16[128,256]{1,0:T(8,128)(2,1)S(1)} collective-permute-done((bf16[128,256]{1,0:T(8,128)(2,1)S(1)}, bf16[128,256]{1,0:T(8,128)(2,1)S(1)}, u32[]{:S(2)}, u32[]{:S(2)}) %collective-permute-start.20) | collective-permute-done | bytes 65568 | tf_op jit(solution)/shard_map/ppermute | solution.py:218
  67.7 1.9 %collective-permute-start.21 = (bf16[256,256]{1,0:T(8,128)(2,1)S(1)}, bf16[256,256]{1,0:T(8,128)(2,1)S(1)}, u32[]{:S(2)}, u32[]{:S(2)}) collective-permute-start(bf16[256,256]{1,0:T(8,128)(2,1)S(1)} %shard_map.161.refs_6_.refs_0_), channel_id=1, source_target_pairs={{0,2},{1,5},{2,0},{3,7},{4,6},{5,1},{6,4},{7,3},{8,10},{9,13},{10,... | collective-permute-start | bytes 393224 | tf_op jit(solution)/shard_map/ppermute | solution.py:218
  69.7 1.2 %collective-permute-done.19.refs_5_ = bf16[128,256]{1,0:T(8,128)(2,1)S(1)} collective-permute-done((bf16[128,256]{1,0:T(8,128)(2,1)S(1)}, bf16[128,256]{1,0:T(8,128)(2,1)S(1)}, u32[]{:S(2)}, u32[]{:S(2)}) %collective-permute-start.19) | collective-permute-done | bytes 65568 | tf_op jit(solution)/shard_map/ppermute | solution.py:78
  70.9 1.2 %shard_map.162 = (f32[512,256]{1,0:T(8,128)}, f32[256,512]{1,0:T(8,128)}, f32[320,256]{1,0:T(8,128)}, bf16[128,256]{1,0:T(8,128)(2,1)}) custom-call(bf16[512,256]{1,0:T(8,128)(2,1)S(1)} %shard_map.160.refs_2_.refs_0_, bf16[512,256]{1,0:T(8,128)(2,1)S(1)} %collective-permute-done.17.refs_1_, f32[320,256]{1,0:T(8,128)S(1)} %get-tuple-element.84.refs_2_, ...), custom_call_target="tpu_custom_call" | custom-call | tf_op jit(solution)/shard_map/pallas_call | solution.py:31
  72.1 0.7 collective-permute-done.21.refs_1_
  72.8 0.8 %shard_map.163 = f32[512,256]{1,0:T(8,128)} custom-call(bf16[256,256]{1,0:T(8,128)(2,1)S(1)} %shard_map.161.refs_6_.refs_0_, bf16[256,256]{1,0:T(8,128)(2,1)S(1)} %collective-permute-done.21.refs_1_, bf16[128,256]{1,0:T(8,128)(2,1)} %get-tuple-element.43.refs_2_), custom_call_target="tpu_custom_call" | custom-call | tf_op jit(solution)/shard_map/pallas_call | solution.py:31
  (15 shorter events, 0.2 us)
Async XLA Ops:
  1.9 11.0 %collective-permute-start = (bf16[144,128]{1,0:T(8,128)(2,1)S(1)}, bf16[144,128]{1,0:T(8,128)(2,1)S(1)}, u32[]{:S(2)}, u32[]{:S(2)}) collective-permute-start(bf16[144,128]{1,0:T(8,128)(2,1)S(1)} %get-tuple-element.50), channel_id=1, source_target_pairs={{0,2},{2,4},{4,6},{6,8},{8,10},{10,12},{12,14},{14,0},{1,3},{3,5},... | collective-permute-start | bytes 110600 | tf_op jit(solution)/shard_map/ppermute | solution.py:78
  4.9 9.3 %collective-permute-start.1 = (bf16[144,128]{1,0:T(8,128)(2,1)S(1)}, bf16[144,128]{1,0:T(8,128)(2,1)S(1)}, u32[]{:S(2)}, u32[]{:S(2)}) collective-permute-start(bf16[144,128]{1,0:T(8,128)(2,1)S(1)} %get-tuple-element.51), channel_id=1, source_target_pairs={{0,4},{2,6},{4,8},{6,10},{8,12},{10,14},{12,0},{14,2},{1,5},{3,7},... | collective-permute-start | bytes 110600 | tf_op jit(solution)/shard_map/ppermute | solution.py:78
  6.5 10.9 %collective-permute-start.2 = (bf16[144,128]{1,0:T(8,128)(2,1)S(1)}, bf16[144,128]{1,0:T(8,128)(2,1)S(1)}, u32[]{:S(2)}, u32[]{:S(2)}) collective-permute-start(bf16[144,128]{1,0:T(8,128)(2,1)S(1)} %get-tuple-element.52), channel_id=1, source_target_pairs={{0,6},{2,8},{4,10},{6,12},{8,14},{10,0},{12,2},{14,4},{1,7},{3,9},... | collective-permute-start | bytes 110600 | tf_op jit(solution)/shard_map/ppermute | solution.py:78
  9.1 8.4 %collective-permute-start.3 = (bf16[144,128]{1,0:T(8,128)(2,1)S(1)}, bf16[144,128]{1,0:T(8,128)(2,1)S(1)}, u32[]{:S(2)}, u32[]{:S(2)}) collective-permute-start(bf16[144,128]{1,0:T(8,128)(2,1)S(1)} %get-tuple-element.53), channel_id=1, source_target_pairs={{0,8},{2,10},{4,12},{6,14},{8,0},{10,2},{12,4},{14,6},{1,9},{3,11}... | collective-permute-start | bytes 110600 | tf_op jit(solution)/shard_map/ppermute | solution.py:78
  10.3 7.2 %collective-permute-start.4 = (bf16[144,128]{1,0:T(8,128)(2,1)S(1)}, bf16[144,128]{1,0:T(8,128)(2,1)S(1)}, u32[]{:S(2)}, u32[]{:S(2)}) collective-permute-start(bf16[144,128]{1,0:T(8,128)(2,1)S(1)} %get-tuple-element.54), channel_id=1, source_target_pairs={{0,10},{2,12},{4,14},{6,0},{8,2},{10,4},{12,6},{14,8},{1,11},{3,13... | collective-permute-start | bytes 110600 | tf_op jit(solution)/shard_map/ppermute | solution.py:78
  12.9 4.5 %collective-permute-start.5 = (bf16[144,128]{1,0:T(8,128)(2,1)S(1)}, bf16[144,128]{1,0:T(8,128)(2,1)S(1)}, u32[]{:S(2)}, u32[]{:S(2)}) collective-permute-start(bf16[144,128]{1,0:T(8,128)(2,1)S(1)} %get-tuple-element.55), channel_id=1, source_target_pairs={{0,12},{2,14},{4,0},{6,2},{8,4},{10,6},{12,8},{14,10},{1,13},{3,15... | collective-permute-start | bytes 110600 | tf_op jit(solution)/shard_map/ppermute | solution.py:78
  14.3 4.0 %collective-permute-start.6 = (bf16[144,128]{1,0:T(8,128)(2,1)S(1)}, bf16[144,128]{1,0:T(8,128)(2,1)S(1)}, u32[]{:S(2)}, u32[]{:S(2)}) collective-permute-start(bf16[144,128]{1,0:T(8,128)(2,1)S(1)} %get-tuple-element.56), channel_id=1, source_target_pairs={{0,14},{2,0},{4,2},{6,4},{8,6},{10,8},{12,10},{14,12},{1,15},{3,1}... | collective-permute-start | bytes 110600 | tf_op jit(solution)/shard_map/ppermute | solution.py:78
  18.3 1.6 %collective-permute-start.7 = (bf16[7,144,128]{2,1,0:T(8,128)(2,1)S(1)}, bf16[7,144,128]{2,1,0:T(8,128)(2,1)S(1)}, u32[]{:S(2)}, u32[]{:S(2)}) collective-permute-start(bf16[7,144,128]{2,1,0:T(8,128)(2,1)S(1)} %shard_map.147.refs_1_), channel_id=1, source_target_pairs={{0,1},{1,0},{2,3},{3,2},{4,5},{5,4},{6,7},{7,6},{8,9},{9,8},{10,11... | collective-permute-start | bytes 774152 | tf_op jit(solution)/shard_map/ppermute | solution.py:78
  22.8 10.8 %collective-permute-start.10 = (bf16[784,256]{1,0:T(8,128)(2,1)S(1)}, bf16[784,256]{1,0:T(8,128)(2,1)S(1)}, u32[]{:S(2)}, u32[]{:S(2)}) collective-permute-start(bf16[784,256]{1,0:T(8,128)(2,1)S(1)} %get-tuple-element.76), channel_id=1, source_target_pairs={{0,2},{1,5},{2,0},{3,7},{4,6},{5,1},{6,4},{7,3},{8,10},{9,13},{10,... | collective-permute-start | bytes 1204232 | tf_op jit(solution)/shard_map/ppermute | solution.py:218
  24.4 9.1 %collective-permute-start.8 = (bf16[512,256]{1,0:T(8,128)(2,1)S(1)}, bf16[512,256]{1,0:T(8,128)(2,1)S(1)}, u32[]{:S(2)}, u32[]{:S(2)}) collective-permute-start(bf16[512,256]{1,0:T(8,128)(2,1)S(1)} %get-tuple-element.65), channel_id=1, source_target_pairs={{0,2},{1,5},{2,0},{3,7},{4,6},{5,1},{6,4},{7,3},{8,10},{9,13},{10,... | collective-permute-start | bytes 786440 | tf_op jit(solution)/shard_map/ppermute | solution.py:218
  33.8 8.6 %collective-permute-start.12 = (bf16[400,256]{1,0:T(8,128)(2,1)S(1)}, bf16[400,256]{1,0:T(8,128)(2,1)S(1)}, u32[]{:S(2)}, u32[]{:S(2)}) collective-permute-start(bf16[400,256]{1,0:T(8,128)(2,1)S(1)} %get-tuple-element.77.refs_2_), channel_id=1, source_target_pairs={{0,4},{1,3},{2,6},{3,1},{4,0},{5,7},{6,2},{7,5},{8,12},{9,11},{10,... | collective-permute-start | bytes 614408 | tf_op jit(solution)/shard_map/ppermute | solution.py:218
  34.5 6.5 %collective-permute-start.9 = (bf16[256,256]{1,0:T(8,128)(2,1)S(1)}, bf16[256,256]{1,0:T(8,128)(2,1)S(1)}, u32[]{:S(2)}, u32[]{:S(2)}) collective-permute-start(bf16[256,256]{1,0:T(8,128)(2,1)S(1)} %get-tuple-element.70.refs_2_), channel_id=1, source_target_pairs={{0,4},{1,3},{2,6},{3,1},{4,0},{5,7},{6,2},{7,5},{8,12},{9,11},{10,... | collective-permute-start | bytes 393224 | tf_op jit(solution)/shard_map/ppermute | solution.py:218
  41.1 9.4 %collective-permute-start.11 = (bf16[128,256]{1,0:T(8,128)(2,1)S(1)}, bf16[128,256]{1,0:T(8,128)(2,1)S(1)}, u32[]{:S(2)}, u32[]{:S(2)}) collective-permute-start(bf16[128,256]{1,0:T(8,128)(2,1)S(1)} %get-tuple-element.79.refs_2_), channel_id=1, source_target_pairs={{0,8},{1,9},{2,10},{3,11},{4,12},{5,13},{6,14},{7,15},{8,0},{9,1},... | collective-permute-start | bytes 196616 | tf_op jit(solution)/shard_map/ppermute | solution.py:218
  42.5 9.4 %collective-permute-start.14 = (bf16[208,256]{1,0:T(8,128)(2,1)S(1)}, bf16[208,256]{1,0:T(8,128)(2,1)S(1)}, u32[]{:S(2)}, u32[]{:S(2)}) collective-permute-start(bf16[208,256]{1,0:T(8,128)(2,1)S(1)} %get-tuple-element.81.refs_2_), channel_id=1, source_target_pairs={{0,8},{1,9},{2,10},{3,11},{4,12},{5,13},{6,14},{7,15},{8,0},{9,1},... | collective-permute-start | bytes 319496 | tf_op jit(solution)/shard_map/ppermute | solution.py:218
  50.5 5.2 %collective-permute-start.13 = (bf16[128,256]{1,0:T(8,128)(2,1)S(1)}, bf16[128,256]{1,0:T(8,128)(2,1)S(1)}, u32[]{:S(2)}, u32[]{:S(2)}) collective-permute-start(bf16[128,256]{1,0:T(8,128)(2,1)S(1)} %shard_map.156.refs_3_.refs_0_), channel_id=1, source_target_pairs={{0,8},{1,9},{2,10},{3,11},{4,12},{5,13},{6,14},{7,15},{8,0},{9,1},... | collective-permute-start | bytes 196616 | tf_op jit(solution)/shard_map/ppermute | solution.py:218
  55.8 6.8 %collective-permute-start.15 = (bf16[256,256]{1,0:T(8,128)(2,1)S(1)}, bf16[256,256]{1,0:T(8,128)(2,1)S(1)}, u32[]{:S(2)}, u32[]{:S(2)}) collective-permute-start(bf16[256,256]{1,0:T(8,128)(2,1)S(1)} %shard_map.158.refs_2_.refs_0_), channel_id=1, source_target_pairs={{0,4},{1,3},{2,6},{3,1},{4,0},{5,7},{6,2},{7,5},{8,12},{9,11},{10,... | collective-permute-start | bytes 393224 | tf_op jit(solution)/shard_map/ppermute | solution.py:218
  55.8 5.0 %collective-permute-start.16 = (bf16[64,256]{1,0:T(8,128)(2,1)S(1)}, bf16[64,256]{1,0:T(8,128)(2,1)S(1)}, u32[]{:S(2)}, u32[]{:S(2)}) collective-permute-start(bf16[64,256]{1,0:T(8,128)(2,1)S(1)} %get-tuple-element.83.refs_2_.refs_0_), channel_id=1, source_target_pairs={{0,8},{1,9},{2,10},{3,11},{4,12},{5,13},{6,14},{7,15},{8,0},{9,1},... | collective-permute-start | bytes 98312 | tf_op jit(solution)/shard_map/ppermute | solution.py:218
  62.6 8.3 %collective-permute-start.17 = (bf16[512,256]{1,0:T(8,128)(2,1)S(1)}, bf16[512,256]{1,0:T(8,128)(2,1)S(1)}, u32[]{:S(2)}, u32[]{:S(2)}) collective-permute-start(bf16[512,256]{1,0:T(8,128)(2,1)S(1)} %shard_map.160.refs_2_.refs_0_), channel_id=1, source_target_pairs={{0,2},{1,5},{2,0},{3,7},{4,6},{5,1},{6,4},{7,3},{8,10},{9,13},{10,... | collective-permute-start | bytes 786440 | tf_op jit(solution)/shard_map/ppermute | solution.py:218
  63.1 4.6 %collective-permute-start.20 = (bf16[128,256]{1,0:T(8,128)(2,1)S(1)}, bf16[128,256]{1,0:T(8,128)(2,1)S(1)}, u32[]{:S(2)}, u32[]{:S(2)}) collective-permute-start(bf16[128,256]{1,0:T(8,128)(2,1)S(1)} %shard_map.159.refs_2_.refs_0_), channel_id=1, source_target_pairs={{0,4},{1,3},{2,6},{3,1},{4,0},{5,7},{6,2},{7,5},{8,12},{9,11},{10,... | collective-permute-start | bytes 196616 | tf_op jit(solution)/shard_map/ppermute | solution.py:218
  63.9 5.7 %collective-permute-start.18 = (bf16[320,256]{1,0:T(8,128)(2,1)S(1)}, bf16[320,256]{1,0:T(8,128)(2,1)S(1)}, u32[]{:S(2)}, u32[]{:S(2)}) collective-permute-start(bf16[320,256]{1,0:T(8,128)(2,1)S(1)} %get-tuple-element.68.refs_2_), channel_id=1, source_target_pairs={{0,1},{1,0},{2,3},{3,2},{4,5},{5,4},{6,7},{7,6},{8,9},{9,8},{10,11... | collective-permute-start | bytes 491528 | tf_op jit(solution)/shard_map/ppermute | solution.py:78
  67.7 5.0 %collective-permute-start.21 = (bf16[256,256]{1,0:T(8,128)(2,1)S(1)}, bf16[256,256]{1,0:T(8,128)(2,1)S(1)}, u32[]{:S(2)}, u32[]{:S(2)}) collective-permute-start(bf16[256,256]{1,0:T(8,128)(2,1)S(1)} %shard_map.161.refs_6_.refs_0_), channel_id=1, source_target_pairs={{0,2},{1,5},{2,0},{3,7},{4,6},{5,1},{6,4},{7,3},{8,10},{9,13},{10,... | collective-permute-start | bytes 393224 | tf_op jit(solution)/shard_map/ppermute | solution.py:218
  69.7 1.3 %collective-permute-start.19 = (bf16[128,256]{1,0:T(8,128)(2,1)S(1)}, bf16[128,256]{1,0:T(8,128)(2,1)S(1)}, u32[]{:S(2)}, u32[]{:S(2)}) collective-permute-start(bf16[128,256]{1,0:T(8,128)(2,1)S(1)} %get-tuple-element.86), channel_id=1, source_target_pairs={{0,1},{1,0},{2,3},{3,2},{4,5},{5,4},{6,7},{7,6},{8,9},{9,8},{10,11... | collective-permute-start | bytes 196616 | tf_op jit(solution)/shard_map/ppermute | solution.py:78

commit v9 on v7

--- a/solution.py
+++ b/solution.py
@@ -370,6 +370,14 @@
     return keep, flip(send, steps[-1])
 
 
+def final_halvings(steps, rows):
+    count = 0
+    for _ in steps:
+        count += halves(rows)
+        rows = half_rows(rows)
+    return count
+
+
 def weight_chain(steps, rows, tail, slots, keep, send, after):
     used = []
     for step in steps:
@@ -397,7 +405,7 @@
     return [piece, flip(piece, used[0])], sums
 
 
-def obs_chain(steps, w_obs, node_mine, node_theirs, keep, send, after):
+def obs_chain(steps, w_obs, keep, send, after):
     keep, got = yield from summing(steps, 0, keep, send, after)
     half = w_obs.shape[0] // 2
     obs_mine, obs_theirs = call(
@@ -406,27 +414,24 @@
     )
     after[:] = [obs_theirs]
     yield
-    grad_node, grad_obs = call(
-        merge_kernel, [(node_mine.shape, F32), (obs_mine.shape, BF16)],
-        node_mine, shift(node_theirs, "mp", 1), obs_mine, shift(obs_theirs, "mp", 1),
-        after=after,
-    )
-    after[:] = [pltpu.with_memory_space_constraint(grad_obs, pltpu.HBM)]
-    yield
-    return grad_node, grad_obs
-
-
-def in_turns(chains):
-    results = [None] * len(chains)
-    running = list(enumerate(chains))
-    while running:
-        for item in list(running):
-            try:
-                next(item[1])
-            except StopIteration as stop:
-                results[item[0]] = stop.value
-                running.remove(item)
-    return results
+    return obs_mine, obs_theirs
+
+
+def in_turns(chains, other, rounds, turns):
+    def finish(chain):
+        try:
+            next(chain)
+        except StopIteration as stop:
+            return stop.value
+
+    taken = 0
+    for done in range(1, rounds + 1):
+        for chain in chains:
+            next(chain)
+        while taken < turns and -(-(taken + 1) * rounds // turns) <= done:
+            next(other)
+            taken += 1
+    return [finish(chain) for chain in chains], finish(other)
 
 
 def local(obs_feat, node_state, grad_agg, owner, local_idx, slot, w_obs, w_node, slot_bias, w_out):
@@ -490,14 +495,21 @@
         )
         for i in range(bundles)
     ]
-    chains.append(obs_chain(steps, w_obs_held, node_mine, node_theirs, obs_keep, obs_send, after))
-    *weights, (grad_node, grad_obs) = in_turns(chains)
+    rounds = len(steps) + final_halvings(steps, rows) - 1
+    weights, (obs_mine, obs_theirs) = in_turns(
+        chains, obs_chain(steps, w_obs_held, obs_keep, obs_send, after), rounds, len(steps)
+    )
+    grad_node, grad_obs = call(
+        merge_kernel, [((nodes, half), F32), ((obs, half), BF16)],
+        node_mine, shift(node_theirs, "mp", 1), obs_mine, shift(obs_theirs, "mp", 1),
+    )
     ends = [end for pair, _ in weights for end in pair]
     (grad_slot,) = weights[-1][1]
     grad_w_node, grad_w_out, grad_w_obs = call(
         functools.partial(spread_kernel, steps[0], bundles),
         [((width, hidden), F32), ((hidden, width), F32), ((width, hidden), F32)],
         *ends,
+        after=[pltpu.with_memory_space_constraint(grad_obs, pltpu.HBM)],
     )
     return grad_obs, grad_node, grad_w_obs, grad_w_node, grad_w_out, grad_slot
 

time: 67.9 us -> 70.3 us (1.035)
  starting transfers between devices: 33.1 us -> 36.2 us
    ppermute x15, starting transfers between devices: 19.3 us -> 22.3 us  [flip(): return lax.ppermute(value, axes, pairs)]
  transfers between devices with their start and end apart: 25 -> 25, of which waited for: 11 -> 11; matrix products, arithmetic and copies ran while one was open for 0% -> 0% of each run, Pallas kernels for 7% -> 5%
where the time goes in v9:
time: 70.3 us; the launch traced here: 70.1 us
  starting transfers between devices  36.2 us (51%)
  waiting for transfers between devices  23.9 us (34%)
  Pallas kernels  9.22 us (13%)
  between operations  0.83 us (1%)
    ppermute x15, starting transfers between devices, flip(): return lax.ppermute(value, axes, pairs)  22.3 us
    ppermute x15, waiting for transfers between devices, flip(): return lax.ppermute(value, axes, pairs)  20.3 us
    ppermute x10, starting transfers between devices, shift(): lax.ppermute(value, axis, [(i, (i + step) % size) for i in range(size)])  13.9 us
    pallas_call x18, Pallas kernels, call(): pl.pallas_call(lambda *refs: kernel(*refs[:count], *refs[len(args):]), ou...  6.2 us
    ppermute x10, waiting for transfers between devices, shift(): lax.ppermute(value, axis, [(i, (i + step) % size) for i in range(size)])  3.52 us
    pallas_call x2, Pallas kernels, call_staged(): pl.pallas_call(staged, out_shape=[jax.ShapeDtypeStruct(shape, dtype) for...  3.03 us
  transfers between devices with their start and end apart: 25, of which 11 were waited for; matrix products, arithmetic and copies ran while one was open for 0% of the time, Pallas kernels for 5%

profile of v9, /device:TPU:0, one launch (start us, length us, event | category | flops | bytes accessed | tf_op | source)
XLA Modules:
  0.0 70.1 jit_solution(1766595276482637073)
XLA Ops:
  0.6 1.3 %shard_map.145 = (bf16[144,128]{1,0:T(8,128)(2,1)S(1)}, bf16[144,128]{1,0:T(8,128)(2,1)S(1)}, bf16[144,128]{1,0:T(8,128)(2,1)S(1)}, bf16[144,128]{1,0:T(8,128)(2...) custom-call(bf16[128,512]{1,0:T(8,128)(2,1)} %refs_0_.2, ...), custom_call_target="tpu_custom_call" | custom-call | tf_op jit(solution)/shard_map/pallas_call | solution.py:61
  1.9 3.0 %collective-permute-start = (bf16[144,128]{1,0:T(8,128)(2,1)S(1)}, bf16[144,128]{1,0:T(8,128)(2,1)S(1)}, u32[]{:S(2)}, u32[]{:S(2)}) collective-permute-start(bf16[144,128]{1,0:T(8,128)(2,1)S(1)} %get-tuple-element.54), channel_id=1, source_target_pairs={{0,2},{2,4},{4,6},{6,8},{8,10},{10,12},{12,14},{14,0},{1,3},{3,5},... | collective-permute-start | bytes 110600 | tf_op jit(solution)/shard_map/ppermute | solution.py:79
  4.9 1.6 %collective-permute-start.1 = (bf16[144,128]{1,0:T(8,128)(2,1)S(1)}, bf16[144,128]{1,0:T(8,128)(2,1)S(1)}, u32[]{:S(2)}, u32[]{:S(2)}) collective-permute-start(bf16[144,128]{1,0:T(8,128)(2,1)S(1)} %get-tuple-element.55), channel_id=1, source_target_pairs={{0,4},{2,6},{4,8},{6,10},{8,12},{10,14},{12,0},{14,2},{1,5},{3,7},... | collective-permute-start | bytes 110600 | tf_op jit(solution)/shard_map/ppermute | solution.py:79
  6.5 2.6 %collective-permute-start.2 = (bf16[144,128]{1,0:T(8,128)(2,1)S(1)}, bf16[144,128]{1,0:T(8,128)(2,1)S(1)}, u32[]{:S(2)}, u32[]{:S(2)}) collective-permute-start(bf16[144,128]{1,0:T(8,128)(2,1)S(1)} %get-tuple-element.56), channel_id=1, source_target_pairs={{0,6},{2,8},{4,10},{6,12},{8,14},{10,0},{12,2},{14,4},{1,7},{3,9},... | collective-permute-start | bytes 110600 | tf_op jit(solution)/shard_map/ppermute | solution.py:79
  9.1 1.2 %collective-permute-start.3 = (bf16[144,128]{1,0:T(8,128)(2,1)S(1)}, bf16[144,128]{1,0:T(8,128)(2,1)S(1)}, u32[]{:S(2)}, u32[]{:S(2)}) collective-permute-start(bf16[144,128]{1,0:T(8,128)(2,1)S(1)} %get-tuple-element.57), channel_id=1, source_target_pairs={{0,8},{2,10},{4,12},{6,14},{8,0},{10,2},{12,4},{14,6},{1,9},{3,11}... | collective-permute-start | bytes 110600 | tf_op jit(solution)/shard_map/ppermute | solution.py:79
  10.3 2.6 %collective-permute-start.4 = (bf16[144,128]{1,0:T(8,128)(2,1)S(1)}, bf16[144,128]{1,0:T(8,128)(2,1)S(1)}, u32[]{:S(2)}, u32[]{:S(2)}) collective-permute-start(bf16[144,128]{1,0:T(8,128)(2,1)S(1)} %get-tuple-element.58), channel_id=1, source_target_pairs={{0,10},{2,12},{4,14},{6,0},{8,2},{10,4},{12,6},{14,8},{1,11},{3,13... | collective-permute-start | bytes 110600 | tf_op jit(solution)/shard_map/ppermute | solution.py:79
  12.9 0.0 collective-permute-done.refs_0_
  12.9 1.4 %collective-permute-start.5 = (bf16[144,128]{1,0:T(8,128)(2,1)S(1)}, bf16[144,128]{1,0:T(8,128)(2,1)S(1)}, u32[]{:S(2)}, u32[]{:S(2)}) collective-permute-start(bf16[144,128]{1,0:T(8,128)(2,1)S(1)} %get-tuple-element.59), channel_id=1, source_target_pairs={{0,12},{2,14},{4,0},{6,2},{8,4},{10,6},{12,8},{14,10},{1,13},{3,15... | collective-permute-start | bytes 110600 | tf_op jit(solution)/shard_map/ppermute | solution.py:79
  14.3 1.4 %collective-permute-start.6 = (bf16[144,128]{1,0:T(8,128)(2,1)S(1)}, bf16[144,128]{1,0:T(8,128)(2,1)S(1)}, u32[]{:S(2)}, u32[]{:S(2)}) collective-permute-start(bf16[144,128]{1,0:T(8,128)(2,1)S(1)} %get-tuple-element.60), channel_id=1, source_target_pairs={{0,14},{2,0},{4,2},{6,4},{8,6},{10,8},{12,10},{14,12},{1,15},{3,1}... | collective-permute-start | bytes 110600 | tf_op jit(solution)/shard_map/ppermute | solution.py:79
  15.7 1.7 %shard_map.146 = (bf16[336,1024]{1,0:T(8,128)(2,1)S(1)}, bf16[320,512]{1,0:T(8,128)(2,1)S(1)}, bf16[320,512]{1,0:T(8,128)(2,1)S(1)}, bf16[512,256]{1,0:T(8,128)(2,1)S(1)}, bf16[512,256]{1,0:T(8,128)(2,1)S(1)}) custom-call(bf16[320,512]{1,0:T(8,128)(2,1)} %refs_0_.3, bf16[320,512]{1,0:T(8,128)(2,1)} %refs_1_.1, bf16[512,256]{1,0:T(8,128)(2,1)} %refs_2_.1, ...), custom_call_target="tpu_custom_call" | custom-call | tf_op jit(solution)/shard_map/pallas_call | solution.py:61
  17.5 0.8 %collective-permute-done.6.refs_6_ = bf16[144,128]{1,0:T(8,128)(2,1)S(1)} collective-permute-done((bf16[144,128]{1,0:T(8,128)(2,1)S(1)}, bf16[144,128]{1,0:T(8,128)(2,1)S(1)}, u32[]{:S(2)}, u32[]{:S(2)}) %collective-permute-start.6) | collective-permute-done | bytes 36896 | tf_op jit(solution)/shard_map/ppermute | solution.py:79
  18.3 0.1 collective-permute-start.7
  18.3 1.5 %collective-permute-done.7.refs_3_ = bf16[7,144,128]{2,1,0:T(8,128)(2,1)S(1)} collective-permute-done((bf16[7,144,128]{2,1,0:T(8,128)(2,1)S(1)}, bf16[7,144,128]{2,1,0:T(8,128)(2,1)S(1)}, u32[]{:S(2)}, u32[]{:S(2)}) %collective-permute-start.7) | collective-permute-done | bytes 258080 | tf_op jit(solution)/shard_map/ppermute | solution.py:79
  19.9 1.6 %shard_map.148 = (bf16[512,512]{1,0:T(8,128)(2,1)S(1)}, bf16[512,336]{1,0:T(8,128)(2,1)S(1)}, bf16[512,256]{1,0:T(8,128)(2,1)S(1)}, bf16[512,256]{1,0:T(8,128)(2...) custom-call(bf16[144,128]{1,0:T(8,128)(2,1)S(1)} %get-tuple-element.53.refs_0_, ...), custom_call_target="tpu_custom_call" | custom-call | tf_op jit(solution)/shard_map/pallas_call | solution.py:32
  21.5 1.3 %shard_map.149 = (f32[320,256]{1,0:T(8,128)S(1)}, bf16[320,256]{1,0:T(8,128)(2,1)S(1)}, f32[384,256]{1,0:T(8,128)S(1)}, bf16[384,256]{1,0:T(8,128)(2,1)S(1)}, f3...) custom-call(bf16[512,336]{1,0:T(8,128)(2,1)S(1)} %get-tuple-element.64.refs_0_, ...), custom_call_target="tpu_custom_call" | custom-call | tf_op jit(solution)/shard_map/pallas_call | solution.py:32
  22.8 1.6 %collective-permute-start.10 = (bf16[400,256]{1,0:T(8,128)(2,1)S(1)}, bf16[400,256]{1,0:T(8,128)(2,1)S(1)}, u32[]{:S(2)}, u32[]{:S(2)}) collective-permute-start(bf16[400,256]{1,0:T(8,128)(2,1)S(1)} %get-tuple-element.76), channel_id=1, source_target_pairs={{0,2},{1,5},{2,0},{3,7},{4,6},{5,1},{6,4},{7,3},{8,10},{9,13},{10,... | collective-permute-start | bytes 614408 | tf_op jit(solution)/shard_map/ppermute | solution.py:226
  24.4 0.5 collective-permute-start.11
  24.9 1.5 %collective-permute-start.9 = (bf16[512,256]{1,0:T(8,128)(2,1)S(1)}, bf16[512,256]{1,0:T(8,128)(2,1)S(1)}, u32[]{:S(2)}, u32[]{:S(2)}) collective-permute-start(bf16[512,256]{1,0:T(8,128)(2,1)S(1)} %get-tuple-element.74), channel_id=1, source_target_pairs={{0,2},{1,5},{2,0},{3,7},{4,6},{5,1},{6,4},{7,3},{8,10},{9,13},{10,... | collective-permute-start | bytes 786440 | tf_op jit(solution)/shard_map/ppermute | solution.py:226
  26.4 4.3 %collective-permute-done.11.refs_1_ = bf16[384,256]{1,0:T(8,128)(2,1)S(1)} collective-permute-done((bf16[384,256]{1,0:T(8,128)(2,1)S(1)}, bf16[384,256]{1,0:T(8,128)(2,1)S(1)}, u32[]{:S(2)}, u32[]{:S(2)}) %collective-permute-start.11) | collective-permute-done | bytes 196640 | tf_op jit(solution)/shard_map/ppermute | solution.py:226
  30.7 0.1 shard_map.150
  30.8 0.1 shard_map.151
  30.9 0.7 %collective-permute-start.12 = (bf16[208,256]{1,0:T(8,128)(2,1)S(1)}, bf16[208,256]{1,0:T(8,128)(2,1)S(1)}, u32[]{:S(2)}, u32[]{:S(2)}) collective-permute-start(bf16[208,256]{1,0:T(8,128)(2,1)S(1)} %get-tuple-element.81.refs_2_), channel_id=1, source_target_pairs={{0,4},{1,3},{2,6},{3,1},{4,0},{5,7},{6,2},{7,5},{8,12},{9,11},{10,... | collective-permute-start | bytes 319496 | tf_op jit(solution)/shard_map/ppermute | solution.py:226
  31.6 1.4 %collective-permute-start.13 = (bf16[192,256]{1,0:T(8,128)(2,1)S(1)}, bf16[192,256]{1,0:T(8,128)(2,1)S(1)}, u32[]{:S(2)}, u32[]{:S(2)}) collective-permute-start(bf16[192,256]{1,0:T(8,128)(2,1)S(1)} %get-tuple-element.79.refs_2_), channel_id=1, source_target_pairs={{0,4},{1,3},{2,6},{3,1},{4,0},{5,7},{6,2},{7,5},{8,12},{9,11},{10,... | collective-permute-start | bytes 294920 | tf_op jit(solution)/shard_map/ppermute | solution.py:226
  33.0 3.7 %collective-permute-done.13.refs_1_ = bf16[192,256]{1,0:T(8,128)(2,1)S(1)} collective-permute-done((bf16[192,256]{1,0:T(8,128)(2,1)S(1)}, bf16[192,256]{1,0:T(8,128)(2,1)S(1)}, u32[]{:S(2)}, u32[]{:S(2)}) %collective-permute-start.13) | collective-permute-done | bytes 98336 | tf_op jit(solution)/shard_map/ppermute | solution.py:226
  36.8 2.2 %collective-permute-start.15 = (bf16[112,256]{1,0:T(8,128)(2,1)S(1)}, bf16[112,256]{1,0:T(8,128)(2,1)S(1)}, u32[]{:S(2)}, u32[]{:S(2)}) collective-permute-start(bf16[112,256]{1,0:T(8,128)(2,1)S(1)} %get-tuple-element.84.refs_2_), channel_id=1, source_target_pairs={{0,8},{1,9},{2,10},{3,11},{4,12},{5,13},{6,14},{7,15},{8,0},{9,1},... | collective-permute-start | bytes 172040 | tf_op jit(solution)/shard_map/ppermute | solution.py:226
  38.9 0.8 %collective-permute-start.16 = (bf16[96,256]{1,0:T(8,128)(2,1)S(1)}, bf16[96,256]{1,0:T(8,128)(2,1)S(1)}, u32[]{:S(2)}, u32[]{:S(2)}) collective-permute-start(bf16[96,256]{1,0:T(8,128)(2,1)S(1)} %get-tuple-element.83.refs_2_), channel_id=1, source_target_pairs={{0,8},{1,9},{2,10},{3,11},{4,12},{5,13},{6,14},{7,15},{8,0},{9,1},... | collective-permute-start | bytes 147464 | tf_op jit(solution)/shard_map/ppermute | solution.py:226
  39.8 0.1 shard_map.154
  39.9 4.0 %collective-permute-done.16.refs_1_ = bf16[96,256]{1,0:T(8,128)(2,1)S(1)} collective-permute-done((bf16[96,256]{1,0:T(8,128)(2,1)S(1)}, bf16[96,256]{1,0:T(8,128)(2,1)S(1)}, u32[]{:S(2)}, u32[]{:S(2)}) %collective-permute-start.16) | collective-permute-done | bytes 49184 | tf_op jit(solution)/shard_map/ppermute | solution.py:226
  44.0 0.9 %collective-permute-start.18 = (bf16[96,256]{1,0:T(8,128)(2,1)S(1)}, bf16[96,256]{1,0:T(8,128)(2,1)S(1)}, u32[]{:S(2)}, u32[]{:S(2)}) collective-permute-start(bf16[96,256]{1,0:T(8,128)(2,1)S(1)} %shard_map.155.refs_2_.refs_0_), channel_id=1, source_target_pairs={{0,8},{1,9},{2,10},{3,11},{4,12},{5,13},{6,14},{7,15},{8,0},{9,1},... | collective-permute-start | bytes 147464 | tf_op jit(solution)/shard_map/ppermute | solution.py:226
  44.9 0.6 shard_map.156
  45.5 2.1 %collective-permute-start.17 = (bf16[96,256]{1,0:T(8,128)(2,1)S(1)}, bf16[96,256]{1,0:T(8,128)(2,1)S(1)}, u32[]{:S(2)}, u32[]{:S(2)}) collective-permute-start(bf16[96,256]{1,0:T(8,128)(2,1)S(1)} %get-tuple-element.89.refs_2_.refs_0_), channel_id=1, source_target_pairs={{0,8},{1,9},{2,10},{3,11},{4,12},{5,13},{6,14},{7,15},{8,0},{9,1},... | collective-permute-start | bytes 147464 | tf_op jit(solution)/shard_map/ppermute | solution.py:226
  47.6 1.1 %collective-permute-start.14 = (bf16[256,256]{1,0:T(8,128)(2,1)S(1)}, bf16[256,256]{1,0:T(8,128)(2,1)S(1)}, u32[]{:S(2)}, u32[]{:S(2)}) collective-permute-start(bf16[256,256]{1,0:T(8,128)(2,1)S(1)} %get-tuple-element.86.refs_2_), channel_id=1, source_target_pairs={{0,4},{1,3},{2,6},{3,1},{4,0},{5,7},{6,2},{7,5},{8,12},{9,11},{10,... | collective-permute-start | bytes 393224 | tf_op jit(solution)/shard_map/ppermute | solution.py:226
  48.7 0.3 collective-permute-done.18.refs_1_
  49.0 1.2 %collective-permute-start.21 = (bf16[192,256]{1,0:T(8,128)(2,1)S(1)}, bf16[192,256]{1,0:T(8,128)(2,1)S(1)}, u32[]{:S(2)}, u32[]{:S(2)}) collective-permute-start(bf16[192,256]{1,0:T(8,128)(2,1)S(1)} %shard_map.157.refs_2_.refs_0_), channel_id=1, source_target_pairs={{0,4},{1,3},{2,6},{3,1},{4,0},{5,7},{6,2},{7,5},{8,12},{9,11},{10,... | collective-permute-start | bytes 294920 | tf_op jit(solution)/shard_map/ppermute | solution.py:226
  50.2 0.2 collective-permute-done.17.refs_1_
  50.5 2.1 %collective-permute-start.20 = (bf16[192,256]{1,0:T(8,128)(2,1)S(1)}, bf16[192,256]{1,0:T(8,128)(2,1)S(1)}, u32[]{:S(2)}, u32[]{:S(2)}) collective-permute-start(bf16[192,256]{1,0:T(8,128)(2,1)S(1)} %shard_map.158.refs_2_.refs_0_), channel_id=1, source_target_pairs={{0,4},{1,3},{2,6},{3,1},{4,0},{5,7},{6,2},{7,5},{8,12},{9,11},{10,... | collective-permute-start | bytes 294920 | tf_op jit(solution)/shard_map/ppermute | solution.py:226
  52.6 0.2 collective-permute-done.14.refs_1_
  52.8 0.1 shard_map.159
  52.8 2.0 %collective-permute-done.21.refs_1_ = bf16[192,256]{1,0:T(8,128)(2,1)S(1)} collective-permute-done((bf16[192,256]{1,0:T(8,128)(2,1)S(1)}, bf16[192,256]{1,0:T(8,128)(2,1)S(1)}, u32[]{:S(2)}, u32[]{:S(2)}) %collective-permute-start.21) | collective-permute-done | bytes 98336 | tf_op jit(solution)/shard_map/ppermute | solution.py:226
  54.9 2.8 %collective-permute-start.23 = (bf16[384,256]{1,0:T(8,128)(2,1)S(1)}, bf16[384,256]{1,0:T(8,128)(2,1)S(1)}, u32[]{:S(2)}, u32[]{:S(2)}) collective-permute-start(bf16[384,256]{1,0:T(8,128)(2,1)S(1)} %shard_map.160.refs_2_.refs_0_), channel_id=1, source_target_pairs={{0,2},{1,5},{2,0},{3,7},{4,6},{5,1},{6,4},{7,3},{8,10},{9,13},{10,... | collective-permute-start | bytes 589832 | tf_op jit(solution)/shard_map/ppermute | solution.py:226
  57.7 2.1 %collective-permute-start.24 = (bf16[384,256]{1,0:T(8,128)(2,1)S(1)}, bf16[384,256]{1,0:T(8,128)(2,1)S(1)}, u32[]{:S(2)}, u32[]{:S(2)}) collective-permute-start(bf16[384,256]{1,0:T(8,128)(2,1)S(1)} %shard_map.161.refs_3_.refs_2_), channel_id=1, source_target_pairs={{0,2},{1,5},{2,0},{3,7},{4,6},{5,1},{6,4},{7,3},{8,10},{9,13},{10,... | collective-permute-start | bytes 589832 | tf_op jit(solution)/shard_map/ppermute | solution.py:226
  59.8 1.3 %collective-permute-start.19 = (bf16[128,256]{1,0:T(8,128)(2,1)S(1)}, bf16[128,256]{1,0:T(8,128)(2,1)S(1)}, u32[]{:S(2)}, u32[]{:S(2)}) collective-permute-start(bf16[128,256]{1,0:T(8,128)(2,1)S(1)} %get-tuple-element.91.refs_2_), channel_id=1, source_target_pairs={{0,8},{1,9},{2,10},{3,11},{4,12},{5,13},{6,14},{7,15},{8,0},{9,1},... | collective-permute-start | bytes 196616 | tf_op jit(solution)/shard_map/ppermute | solution.py:226
  61.1 5.5 %collective-permute-done.19.refs_1_ = bf16[128,256]{1,0:T(8,128)(2,1)S(1)} collective-permute-done((bf16[128,256]{1,0:T(8,128)(2,1)S(1)}, bf16[128,256]{1,0:T(8,128)(2,1)S(1)}, u32[]{:S(2)}, u32[]{:S(2)}) %collective-permute-start.19) | collective-permute-done | bytes 65568 | tf_op jit(solution)/shard_map/ppermute | solution.py:226
  66.6 0.2 shard_map.162
  66.8 0.1 collective-permute-start.22
  66.9 1.2 %collective-permute-done.22.refs_3_ = bf16[128,256]{1,0:T(8,128)(2,1)S(1)} collective-permute-done((bf16[128,256]{1,0:T(8,128)(2,1)S(1)}, bf16[128,256]{1,0:T(8,128)(2,1)S(1)}, u32[]{:S(2)}, u32[]{:S(2)}) %collective-permute-start.22) | collective-permute-done | bytes 65568 | tf_op jit(solution)/shard_map/ppermute | solution.py:79
  68.1 0.8 %shard_map.163 = (f32[320,256]{1,0:T(8,128)}, bf16[128,256]{1,0:T(8,128)(2,1)}) custom-call(f32[320,256]{1,0:T(8,128)S(1)} %get-tuple-element.71.refs_0_, bf16[320,256]{1,0:T(8,128)(2,1)S(1)} %collective-permute-done.8.refs_1_, f32[128,256]{1,0:T(8,128)S(1)} %get-tuple-element.92.refs_2_, bf16[128,256]{1,0:T(8,128)(2,1)S(1)} %collective-permute-done.22.refs_3_), custom_call_target="tpu_custom_call" | custom-call | tf_op jit(solution)/shard_map/pallas_call | solution.py:32
  68.9 1.2 %shard_map.164 = (f32[512,256]{1,0:T(8,128)}, f32[256,512]{1,0:T(8,128)}, f32[512,256]{1,0:T(8,128)}) custom-call(bf16[384,256]{1,0:T(8,128)(2,1)S(1)} %shard_map.160.refs_2_.refs_0_, bf16[384,256]{1,0:T(8,128)(2,1)S(1)} %collective-permute-done.23.refs_1_, bf16[384,256]{1,0:T(8,128)(2,1)S(1)} %shard_map.161.refs_3_.refs_2_, ...), custom_call_target="tpu_custom_call" | custom-call | tf_op jit(solution)/shard_map/pallas_call | solution.py:32
  (22 shorter events, 0.2 us)
Async XLA Ops:
  1.9 11.0 %collective-permute-start = (bf16[144,128]{1,0:T(8,128)(2,1)S(1)}, bf16[144,128]{1,0:T(8,128)(2,1)S(1)}, u32[]{:S(2)}, u32[]{:S(2)}) collective-permute-start(bf16[144,128]{1,0:T(8,128)(2,1)S(1)} %get-tuple-element.54), channel_id=1, source_target_pairs={{0,2},{2,4},{4,6},{6,8},{8,10},{10,12},{12,14},{14,0},{1,3},{3,5},... | collective-permute-start | bytes 110600 | tf_op jit(solution)/shard_map/ppermute | solution.py:79
  4.9 9.3 %collective-permute-start.1 = (bf16[144,128]{1,0:T(8,128)(2,1)S(1)}, bf16[144,128]{1,0:T(8,128)(2,1)S(1)}, u32[]{:S(2)}, u32[]{:S(2)}) collective-permute-start(bf16[144,128]{1,0:T(8,128)(2,1)S(1)} %get-tuple-element.55), channel_id=1, source_target_pairs={{0,4},{2,6},{4,8},{6,10},{8,12},{10,14},{12,0},{14,2},{1,5},{3,7},... | collective-permute-start | bytes 110600 | tf_op jit(solution)/shard_map/ppermute | solution.py:79
  6.5 10.9 %collective-permute-start.2 = (bf16[144,128]{1,0:T(8,128)(2,1)S(1)}, bf16[144,128]{1,0:T(8,128)(2,1)S(1)}, u32[]{:S(2)}, u32[]{:S(2)}) collective-permute-start(bf16[144,128]{1,0:T(8,128)(2,1)S(1)} %get-tuple-element.56), channel_id=1, source_target_pairs={{0,6},{2,8},{4,10},{6,12},{8,14},{10,0},{12,2},{14,4},{1,7},{3,9},... | collective-permute-start | bytes 110600 | tf_op jit(solution)/shard_map/ppermute | solution.py:79
  9.1 8.4 %collective-permute-start.3 = (bf16[144,128]{1,0:T(8,128)(2,1)S(1)}, bf16[144,128]{1,0:T(8,128)(2,1)S(1)}, u32[]{:S(2)}, u32[]{:S(2)}) collective-permute-start(bf16[144,128]{1,0:T(8,128)(2,1)S(1)} %get-tuple-element.57), channel_id=1, source_target_pairs={{0,8},{2,10},{4,12},{6,14},{8,0},{10,2},{12,4},{14,6},{1,9},{3,11}... | collective-permute-start | bytes 110600 | tf_op jit(solution)/shard_map/ppermute | solution.py:79
  10.3 7.2 %collective-permute-start.4 = (bf16[144,128]{1,0:T(8,128)(2,1)S(1)}, bf16[144,128]{1,0:T(8,128)(2,1)S(1)}, u32[]{:S(2)}, u32[]{:S(2)}) collective-permute-start(bf16[144,128]{1,0:T(8,128)(2,1)S(1)} %get-tuple-element.58), channel_id=1, source_target_pairs={{0,10},{2,12},{4,14},{6,0},{8,2},{10,4},{12,6},{14,8},{1,11},{3,13... | collective-permute-start | bytes 110600 | tf_op jit(solution)/shard_map/ppermute | solution.py:79
  12.9 4.5 %collective-permute-start.5 = (bf16[144,128]{1,0:T(8,128)(2,1)S(1)}, bf16[144,128]{1,0:T(8,128)(2,1)S(1)}, u32[]{:S(2)}, u32[]{:S(2)}) collective-permute-start(bf16[144,128]{1,0:T(8,128)(2,1)S(1)} %get-tuple-element.59), channel_id=1, source_target_pairs={{0,12},{2,14},{4,0},{6,2},{8,4},{10,6},{12,8},{14,10},{1,13},{3,15... | collective-permute-start | bytes 110600 | tf_op jit(solution)/shard_map/ppermute | solution.py:79
  14.3 4.0 %collective-permute-start.6 = (bf16[144,128]{1,0:T(8,128)(2,1)S(1)}, bf16[144,128]{1,0:T(8,128)(2,1)S(1)}, u32[]{:S(2)}, u32[]{:S(2)}) collective-permute-start(bf16[144,128]{1,0:T(8,128)(2,1)S(1)} %get-tuple-element.60), channel_id=1, source_target_pairs={{0,14},{2,0},{4,2},{6,4},{8,6},{10,8},{12,10},{14,12},{1,15},{3,1}... | collective-permute-start | bytes 110600 | tf_op jit(solution)/shard_map/ppermute | solution.py:79
  18.3 1.6 %collective-permute-start.7 = (bf16[7,144,128]{2,1,0:T(8,128)(2,1)S(1)}, bf16[7,144,128]{2,1,0:T(8,128)(2,1)S(1)}, u32[]{:S(2)}, u32[]{:S(2)}) collective-permute-start(bf16[7,144,128]{2,1,0:T(8,128)(2,1)S(1)} %shard_map.147.refs_1_), channel_id=1, source_target_pairs={{0,1},{1,0},{2,3},{3,2},{4,5},{5,4},{6,7},{7,6},{8,9},{9,8},{10,11... | collective-permute-start | bytes 774152 | tf_op jit(solution)/shard_map/ppermute | solution.py:79
  22.8 8.0 %collective-permute-start.10 = (bf16[400,256]{1,0:T(8,128)(2,1)S(1)}, bf16[400,256]{1,0:T(8,128)(2,1)S(1)}, u32[]{:S(2)}, u32[]{:S(2)}) collective-permute-start(bf16[400,256]{1,0:T(8,128)(2,1)S(1)} %get-tuple-element.76), channel_id=1, source_target_pairs={{0,2},{1,5},{2,0},{3,7},{4,6},{5,1},{6,4},{7,3},{8,10},{9,13},{10,... | collective-permute-start | bytes 614408 | tf_op jit(solution)/shard_map/ppermute | solution.py:226
  24.4 6.3 %collective-permute-start.11 = (bf16[384,256]{1,0:T(8,128)(2,1)S(1)}, bf16[384,256]{1,0:T(8,128)(2,1)S(1)}, u32[]{:S(2)}, u32[]{:S(2)}) collective-permute-start(bf16[384,256]{1,0:T(8,128)(2,1)S(1)} %get-tuple-element.78), channel_id=1, source_target_pairs={{0,2},{1,5},{2,0},{3,7},{4,6},{5,1},{6,4},{7,3},{8,10},{9,13},{10,... | collective-permute-start | bytes 589832 | tf_op jit(solution)/shard_map/ppermute | solution.py:226
  24.9 14.9 %collective-permute-start.9 = (bf16[512,256]{1,0:T(8,128)(2,1)S(1)}, bf16[512,256]{1,0:T(8,128)(2,1)S(1)}, u32[]{:S(2)}, u32[]{:S(2)}) collective-permute-start(bf16[512,256]{1,0:T(8,128)(2,1)S(1)} %get-tuple-element.74), channel_id=1, source_target_pairs={{0,2},{1,5},{2,0},{3,7},{4,6},{5,1},{6,4},{7,3},{8,10},{9,13},{10,... | collective-permute-start | bytes 786440 | tf_op jit(solution)/shard_map/ppermute | solution.py:226
  30.9 5.9 %collective-permute-start.12 = (bf16[208,256]{1,0:T(8,128)(2,1)S(1)}, bf16[208,256]{1,0:T(8,128)(2,1)S(1)}, u32[]{:S(2)}, u32[]{:S(2)}) collective-permute-start(bf16[208,256]{1,0:T(8,128)(2,1)S(1)} %get-tuple-element.81.refs_2_), channel_id=1, source_target_pairs={{0,4},{1,3},{2,6},{3,1},{4,0},{5,7},{6,2},{7,5},{8,12},{9,11},{10,... | collective-permute-start | bytes 319496 | tf_op jit(solution)/shard_map/ppermute | solution.py:226
  31.6 5.1 %collective-permute-start.13 = (bf16[192,256]{1,0:T(8,128)(2,1)S(1)}, bf16[192,256]{1,0:T(8,128)(2,1)S(1)}, u32[]{:S(2)}, u32[]{:S(2)}) collective-permute-start(bf16[192,256]{1,0:T(8,128)(2,1)S(1)} %get-tuple-element.79.refs_2_), channel_id=1, source_target_pairs={{0,4},{1,3},{2,6},{3,1},{4,0},{5,7},{6,2},{7,5},{8,12},{9,11},{10,... | collective-permute-start | bytes 294920 | tf_op jit(solution)/shard_map/ppermute | solution.py:226
  36.8 8.1 %collective-permute-start.15 = (bf16[112,256]{1,0:T(8,128)(2,1)S(1)}, bf16[112,256]{1,0:T(8,128)(2,1)S(1)}, u32[]{:S(2)}, u32[]{:S(2)}) collective-permute-start(bf16[112,256]{1,0:T(8,128)(2,1)S(1)} %get-tuple-element.84.refs_2_), channel_id=1, source_target_pairs={{0,8},{1,9},{2,10},{3,11},{4,12},{5,13},{6,14},{7,15},{8,0},{9,1},... | collective-permute-start | bytes 172040 | tf_op jit(solution)/shard_map/ppermute | solution.py:226
  38.9 5.0 %collective-permute-start.16 = (bf16[96,256]{1,0:T(8,128)(2,1)S(1)}, bf16[96,256]{1,0:T(8,128)(2,1)S(1)}, u32[]{:S(2)}, u32[]{:S(2)}) collective-permute-start(bf16[96,256]{1,0:T(8,128)(2,1)S(1)} %get-tuple-element.83.refs_2_), channel_id=1, source_target_pairs={{0,8},{1,9},{2,10},{3,11},{4,12},{5,13},{6,14},{7,15},{8,0},{9,1},... | collective-permute-start | bytes 147464 | tf_op jit(solution)/shard_map/ppermute | solution.py:226
  44.0 5.1 %collective-permute-start.18 = (bf16[96,256]{1,0:T(8,128)(2,1)S(1)}, bf16[96,256]{1,0:T(8,128)(2,1)S(1)}, u32[]{:S(2)}, u32[]{:S(2)}) collective-permute-start(bf16[96,256]{1,0:T(8,128)(2,1)S(1)} %shard_map.155.refs_2_.refs_0_), channel_id=1, source_target_pairs={{0,8},{1,9},{2,10},{3,11},{4,12},{5,13},{6,14},{7,15},{8,0},{9,1},... | collective-permute-start | bytes 147464 | tf_op jit(solution)/shard_map/ppermute | solution.py:226
  45.5 5.0 %collective-permute-start.17 = (bf16[96,256]{1,0:T(8,128)(2,1)S(1)}, bf16[96,256]{1,0:T(8,128)(2,1)S(1)}, u32[]{:S(2)}, u32[]{:S(2)}) collective-permute-start(bf16[96,256]{1,0:T(8,128)(2,1)S(1)} %get-tuple-element.89.refs_2_.refs_0_), channel_id=1, source_target_pairs={{0,8},{1,9},{2,10},{3,11},{4,12},{5,13},{6,14},{7,15},{8,0},{9,1},... | collective-permute-start | bytes 147464 | tf_op jit(solution)/shard_map/ppermute | solution.py:226
  47.6 5.2 %collective-permute-start.14 = (bf16[256,256]{1,0:T(8,128)(2,1)S(1)}, bf16[256,256]{1,0:T(8,128)(2,1)S(1)}, u32[]{:S(2)}, u32[]{:S(2)}) collective-permute-start(bf16[256,256]{1,0:T(8,128)(2,1)S(1)} %get-tuple-element.86.refs_2_), channel_id=1, source_target_pairs={{0,4},{1,3},{2,6},{3,1},{4,0},{5,7},{6,2},{7,5},{8,12},{9,11},{10,... | collective-permute-start | bytes 393224 | tf_op jit(solution)/shard_map/ppermute | solution.py:226
  49.0 5.8 %collective-permute-start.21 = (bf16[192,256]{1,0:T(8,128)(2,1)S(1)}, bf16[192,256]{1,0:T(8,128)(2,1)S(1)}, u32[]{:S(2)}, u32[]{:S(2)}) collective-permute-start(bf16[192,256]{1,0:T(8,128)(2,1)S(1)} %shard_map.157.refs_2_.refs_0_), channel_id=1, source_target_pairs={{0,4},{1,3},{2,6},{3,1},{4,0},{5,7},{6,2},{7,5},{8,12},{9,11},{10,... | collective-permute-start | bytes 294920 | tf_op jit(solution)/shard_map/ppermute | solution.py:226
  50.5 7.2 %collective-permute-start.20 = (bf16[192,256]{1,0:T(8,128)(2,1)S(1)}, bf16[192,256]{1,0:T(8,128)(2,1)S(1)}, u32[]{:S(2)}, u32[]{:S(2)}) collective-permute-start(bf16[192,256]{1,0:T(8,128)(2,1)S(1)} %shard_map.158.refs_2_.refs_0_), channel_id=1, source_target_pairs={{0,4},{1,3},{2,6},{3,1},{4,0},{5,7},{6,2},{7,5},{8,12},{9,11},{10,... | collective-permute-start | bytes 294920 | tf_op jit(solution)/shard_map/ppermute | solution.py:226
  54.9 14.0 %collective-permute-start.23 = (bf16[384,256]{1,0:T(8,128)(2,1)S(1)}, bf16[384,256]{1,0:T(8,128)(2,1)S(1)}, u32[]{:S(2)}, u32[]{:S(2)}) collective-permute-start(bf16[384,256]{1,0:T(8,128)(2,1)S(1)} %shard_map.160.refs_2_.refs_0_), channel_id=1, source_target_pairs={{0,2},{1,5},{2,0},{3,7},{4,6},{5,1},{6,4},{7,3},{8,10},{9,13},{10,... | collective-permute-start | bytes 589832 | tf_op jit(solution)/shard_map/ppermute | solution.py:226
  57.7 11.2 %collective-permute-start.24 = (bf16[384,256]{1,0:T(8,128)(2,1)S(1)}, bf16[384,256]{1,0:T(8,128)(2,1)S(1)}, u32[]{:S(2)}, u32[]{:S(2)}) collective-permute-start(bf16[384,256]{1,0:T(8,128)(2,1)S(1)} %shard_map.161.refs_3_.refs_2_), channel_id=1, source_target_pairs={{0,2},{1,5},{2,0},{3,7},{4,6},{5,1},{6,4},{7,3},{8,10},{9,13},{10,... | collective-permute-start | bytes 589832 | tf_op jit(solution)/shard_map/ppermute | solution.py:226
  59.8 7.1 %collective-permute-start.8 = (bf16[320,256]{1,0:T(8,128)(2,1)S(1)}, bf16[320,256]{1,0:T(8,128)(2,1)S(1)}, u32[]{:S(2)}, u32[]{:S(2)}) collective-permute-start(bf16[320,256]{1,0:T(8,128)(2,1)S(1)} %get-tuple-element.72), channel_id=1, source_target_pairs={{0,1},{1,0},{2,3},{3,2},{4,5},{5,4},{6,7},{7,6},{8,9},{9,8},{10,11... | collective-permute-start | bytes 491528 | tf_op jit(solution)/shard_map/ppermute | solution.py:79
  59.8 6.8 %collective-permute-start.19 = (bf16[128,256]{1,0:T(8,128)(2,1)S(1)}, bf16[128,256]{1,0:T(8,128)(2,1)S(1)}, u32[]{:S(2)}, u32[]{:S(2)}) collective-permute-start(bf16[128,256]{1,0:T(8,128)(2,1)S(1)} %get-tuple-element.91.refs_2_), channel_id=1, source_target_pairs={{0,8},{1,9},{2,10},{3,11},{4,12},{5,13},{6,14},{7,15},{8,0},{9,1},... | collective-permute-start | bytes 196616 | tf_op jit(solution)/shard_map/ppermute | solution.py:226
  66.8 1.3 %collective-permute-start.22 = (bf16[128,256]{1,0:T(8,128)(2,1)S(1)}, bf16[128,256]{1,0:T(8,128)(2,1)S(1)}, u32[]{:S(2)}, u32[]{:S(2)}) collective-permute-start(bf16[128,256]{1,0:T(8,128)(2,1)S(1)} %get-tuple-element.93), channel_id=1, source_target_pairs={{0,1},{1,0},{2,3},{3,2},{4,5},{5,4},{6,7},{7,6},{8,9},{9,8},{10,11... | collective-permute-start | bytes 196616 | tf_op jit(solution)/shard_map/ppermute | solution.py:79

commit v10 on v9

--- a/solution.py
+++ b/solution.py
@@ -247,20 +247,26 @@
     return rows % (2 * SUBLANES) == 0
 
 
+def half_rows(rows):
+    return rows // 2 if halves(rows) else rows
+
+
 def split_half(total_ref, start, rows, step, tail, keep_ref, send_ref):
     end = start + rows
-    if halves(rows):
-        rows //= 2
+    half = half_rows(rows) if step else rows
+    if half < rows:
         bit = own_bit(step)
-        kept, sent = [pl.ds(pl.multiple_of(start + b * rows, SUBLANES), rows) for b in (bit, 1 - bit)]
+        kept, sent = [pl.ds(pl.multiple_of(start + b * half, SUBLANES), half) for b in (bit, 1 - bit)]
+        keep_ref[:half, :] = total_ref[kept, :]
+        send_ref[:half, :] = total_ref[sent, :].astype(BF16)
     else:
-        kept = sent = pl.ds(start, rows)
-    keep_ref[:rows, :] = total_ref[kept, :]
-    send_ref[:rows, :] = total_ref[sent, :].astype(BF16)
+        both = total_ref[start:end, :].astype(BF16)
+        keep_ref[:half, :] = both.astype(keep_ref.dtype)
+        send_ref[:half, :] = both
     if tail:
-        both = total_ref[end : end + tail, :]
-        keep_ref[rows:, :] = both
-        send_ref[rows:, :] = both.astype(BF16)
+        both = total_ref[end : end + tail, :].astype(BF16)
+        keep_ref[half:, :] = both.astype(keep_ref.dtype)
+        send_ref[half:, :] = both
 
 
 def weight_kernel(
@@ -350,88 +356,81 @@
     grad_obs_ref[...] = (obs_ref[...] + obs_got_ref[...].astype(F32)).astype(BF16)
 
 
-def half_rows(rows):
-    return rows // 2 if halves(rows) else rows
-
-
-def summing(steps, tail, keep, send, after):
+def summing(steps, halved, tail, keep, got, after):
     hidden = keep.shape[1]
-    for done, nxt in zip(steps[:-1], steps[1:]):
-        rows = half_rows(keep.shape[0] - tail) + tail
+    for at, following in enumerate(steps[1:], 1):
+        step = following if at < halved else None
+        rows = keep.shape[0] - tail
+        rows = (half_rows(rows) if step else rows) + tail
         keep, send = call(
-            functools.partial(add_kernel, nxt, tail),
+            functools.partial(add_kernel, step, tail),
             [((rows, hidden), keep.dtype), ((rows, hidden), BF16)],
-            keep, flip(send, done),
+            keep, got,
             scratch=[pltpu.VMEM(keep.shape, keep.dtype)],
             after=after,
         )
         after[:] = [send]
+        got = flip(send, following)
         yield
-    return keep, flip(send, steps[-1])
-
-
-def final_halvings(steps, rows):
-    count = 0
-    for _ in steps:
-        count += halves(rows)
-        rows = half_rows(rows)
-    return count
-
-
-def weight_chain(steps, rows, tail, slots, keep, send, after):
+    return keep, got
+
+
+def halving_used(steps, rows):
     used = []
-    for step in steps:
+    for step in steps[:-1]:
         if halves(rows):
             used.append(step)
             rows //= 2
-    keep, got = yield from summing(steps, tail, keep, send, after)
+    return used
+
+
+def weight_chain(steps, rows, tail, slots, keep, got, after):
+    used = halving_used(steps, rows)
+    keep, got = yield from summing(steps, len(steps) - 1, tail, keep, got, after)
     piece, *sums = call(
         last_kernel,
-        [((rows, keep.shape[1]), BF16)] + ([((slots, keep.shape[1]), F32)] if tail else []),
+        [((keep.shape[0] - tail, keep.shape[1]), BF16)]
+        + ([((slots, keep.shape[1]), F32)] if tail else []),
         keep, got,
         after=after,
     )
     after[:] = [piece]
+    got = flip(piece, used[-1])
     yield
-    for step in used[:0:-1]:
+    for step, following in zip(used[:0:-1], used[-2::-1]):
         (piece,) = call(
             functools.partial(join_kernel, step),
             [((2 * piece.shape[0], piece.shape[1]), BF16)],
-            piece, flip(piece, step),
+            piece, got,
             after=after,
         )
         after[:] = [piece]
+        got = flip(piece, following)
         yield
-    return [piece, flip(piece, used[0])], sums
-
-
-def obs_chain(steps, w_obs, keep, send, after):
-    keep, got = yield from summing(steps, 0, keep, send, after)
+    return [piece, got], sums
+
+
+def obs_chain(steps, w_obs, keep, got, after):
+    keep, got = yield from summing(steps, len(steps), 0, keep, got, after)
     half = w_obs.shape[0] // 2
     obs_mine, obs_theirs = call(
         obs_kernel, [((keep.shape[0], half), F32), ((keep.shape[0], half), BF16)], keep, got, w_obs,
         after=after,
     )
     after[:] = [obs_theirs]
+    obs_got = shift(obs_theirs, "mp", 1)
     yield
-    return obs_mine, obs_theirs
-
-
-def in_turns(chains, other, rounds, turns):
-    def finish(chain):
+    return obs_mine, obs_got
+
+
+def in_turns(chains, turns):
+    results = {}
+    for key in turns + [key for key in range(len(chains))]:
         try:
-            next(chain)
+            next(chains[key])
         except StopIteration as stop:
-            return stop.value
-
-    taken = 0
-    for done in range(1, rounds + 1):
-        for chain in chains:
-            next(chain)
-        while taken < turns and -(-(taken + 1) * rounds // turns) <= done:
-            next(other)
-            taken += 1
-    return [finish(chain) for chain in chains], finish(other)
+            results[key] = stop.value
+    return [results[key] for key in range(len(chains))]
 
 
 def local(obs_feat, node_state, grad_agg, owner, local_idx, slot, w_obs, w_node, slot_bias, w_out):
@@ -478,6 +477,7 @@
     stack = 2 * width + width // hidden * hidden
     bundles = BUNDLES
     rows = stack // bundles
+    obs_got = flip(obs_send, steps[0])
     shapes = []
     for i in range(bundles):
         share = rows // 2 + (tail if i == bundles - 1 else 0)
@@ -489,19 +489,22 @@
         scratch=[pltpu.VMEM((stack + tail, hidden), F32)],
     )
     after = []
+    got = [flip(send, steps[0]) for send in shares[1::2]]
     chains = [
         weight_chain(
-            steps, rows, tail if i == bundles - 1 else 0, slots, shares[2 * i], shares[2 * i + 1], after
+            steps, rows, tail if i == bundles - 1 else 0, slots, shares[2 * i], got[i], after
         )
         for i in range(bundles)
     ]
-    rounds = len(steps) + final_halvings(steps, rows) - 1
-    weights, (obs_mine, obs_theirs) = in_turns(
-        chains, obs_chain(steps, w_obs_held, obs_keep, obs_send, after), rounds, len(steps)
+    node_got = shift(node_theirs, "mp", 1)
+    everyone = list(range(1, bundles + 1))
+    turns = ([0] + everyone) * (len(steps) - 1) + everyone + [0] + everyone * (len(halving_used(steps, rows)) - 1)
+    (obs_mine, obs_got), *weights = in_turns(
+        [obs_chain(steps, w_obs_held, obs_keep, obs_got, after)] + chains, turns
     )
     grad_node, grad_obs = call(
         merge_kernel, [((nodes, half), F32), ((obs, half), BF16)],
-        node_mine, shift(node_theirs, "mp", 1), obs_mine, shift(obs_theirs, "mp", 1),
+        node_mine, node_got, obs_mine, obs_got,
     )
     ends = [end for pair, _ in weights for end in pair]
     (grad_slot,) = weights[-1][1]

time: 70.3 us -> 67.4 us (0.959)
  starting transfers between devices: 36.2 us -> 30.4 us
  waiting for transfers between devices: 23.9 us -> 26.5 us
    ppermute x15 -> x13, starting transfers between devices: 22.3 us -> 16.1 us  [flip(): return lax.ppermute(value, axes, pairs)]
    ppermute x15 -> x13, waiting for transfers between devices: 20.3 us -> 23.2 us  [flip(): return lax.ppermute(value, axes, pairs)]
    pallas_call x18 -> x16, Pallas kernels: 6.2 us -> 6.19 us  [call(): pl.pallas_call(lambda *refs: kernel(*refs[:count], *refs[len(args):]), ou...]
  transfers between devices with their start and end apart: 25 -> 23, of which waited for: 11 -> 11; matrix products, arithmetic and copies ran while one was open for 0% -> 0% of each run, Pallas kernels for 5% -> 8%
where the time goes in v10:
time: 67.4 us; the launch traced here: 66.9 us
  starting transfers between devices  30.4 us (45%)
  waiting for transfers between devices  26.5 us (39%)
  Pallas kernels  9.21 us (14%)
  between operations  0.81 us (1%)
    ppermute x13, waiting for transfers between devices, flip(): return lax.ppermute(value, axes, pairs)  23.2 us
    ppermute x13, starting transfers between devices, flip(): return lax.ppermute(value, axes, pairs)  16.1 us
    ppermute x10, starting transfers between devices, shift(): lax.ppermute(value, axis, [(i, (i + step) % size) for i in range(size)])  14.3 us
    pallas_call x16, Pallas kernels, call(): pl.pallas_call(lambda *refs: kernel(*refs[:count], *refs[len(args):]), ou...  6.19 us
    ppermute x10, waiting for transfers between devices, shift(): lax.ppermute(value, axis, [(i, (i + step) % size) for i in range(size)])  3.27 us
    pallas_call x2, Pallas kernels, call_staged(): pl.pallas_call(staged, out_shape=[jax.ShapeDtypeStruct(shape, dtype) for...  3.03 us
  transfers between devices with their start and end apart: 23, of which 11 were waited for; matrix products, arithmetic and copies ran while one was open for 0% of the time, Pallas kernels for 8%

profile of v10, /device:TPU:0, one launch (start us, length us, event | category | flops | bytes accessed | tf_op | source)
XLA Modules:
  0.0 66.9 jit_solution(15916860514036230777)
XLA Ops:
  0.6 1.3 %shard_map.145 = (bf16[144,128]{1,0:T(8,128)(2,1)S(1)}, bf16[144,128]{1,0:T(8,128)(2,1)S(1)}, bf16[144,128]{1,0:T(8,128)(2,1)S(1)}, bf16[144,128]{1,0:T(8,128)(2...) custom-call(bf16[128,512]{1,0:T(8,128)(2,1)} %refs_0_.2, ...), custom_call_target="tpu_custom_call" | custom-call | tf_op jit(solution)/shard_map/pallas_call | solution.py:61
  1.9 3.0 %collective-permute-start = (bf16[144,128]{1,0:T(8,128)(2,1)S(1)}, bf16[144,128]{1,0:T(8,128)(2,1)S(1)}, u32[]{:S(2)}, u32[]{:S(2)}) collective-permute-start(bf16[144,128]{1,0:T(8,128)(2,1)S(1)} %get-tuple-element.54), channel_id=1, source_target_pairs={{0,2},{2,4},{4,6},{6,8},{8,10},{10,12},{12,14},{14,0},{1,3},{3,5},... | collective-permute-start | bytes 110600 | tf_op jit(solution)/shard_map/ppermute | solution.py:79
  4.9 1.6 %collective-permute-start.1 = (bf16[144,128]{1,0:T(8,128)(2,1)S(1)}, bf16[144,128]{1,0:T(8,128)(2,1)S(1)}, u32[]{:S(2)}, u32[]{:S(2)}) collective-permute-start(bf16[144,128]{1,0:T(8,128)(2,1)S(1)} %get-tuple-element.55), channel_id=1, source_target_pairs={{0,4},{2,6},{4,8},{6,10},{8,12},{10,14},{12,0},{14,2},{1,5},{3,7},... | collective-permute-start | bytes 110600 | tf_op jit(solution)/shard_map/ppermute | solution.py:79
  6.5 2.6 %collective-permute-start.2 = (bf16[144,128]{1,0:T(8,128)(2,1)S(1)}, bf16[144,128]{1,0:T(8,128)(2,1)S(1)}, u32[]{:S(2)}, u32[]{:S(2)}) collective-permute-start(bf16[144,128]{1,0:T(8,128)(2,1)S(1)} %get-tuple-element.56), channel_id=1, source_target_pairs={{0,6},{2,8},{4,10},{6,12},{8,14},{10,0},{12,2},{14,4},{1,7},{3,9},... | collective-permute-start | bytes 110600 | tf_op jit(solution)/shard_map/ppermute | solution.py:79
  9.1 1.2 %collective-permute-start.3 = (bf16[144,128]{1,0:T(8,128)(2,1)S(1)}, bf16[144,128]{1,0:T(8,128)(2,1)S(1)}, u32[]{:S(2)}, u32[]{:S(2)}) collective-permute-start(bf16[144,128]{1,0:T(8,128)(2,1)S(1)} %get-tuple-element.57), channel_id=1, source_target_pairs={{0,8},{2,10},{4,12},{6,14},{8,0},{10,2},{12,4},{14,6},{1,9},{3,11}... | collective-permute-start | bytes 110600 | tf_op jit(solution)/shard_map/ppermute | solution.py:79
  10.3 2.6 %collective-permute-start.4 = (bf16[144,128]{1,0:T(8,128)(2,1)S(1)}, bf16[144,128]{1,0:T(8,128)(2,1)S(1)}, u32[]{:S(2)}, u32[]{:S(2)}) collective-permute-start(bf16[144,128]{1,0:T(8,128)(2,1)S(1)} %get-tuple-element.58), channel_id=1, source_target_pairs={{0,10},{2,12},{4,14},{6,0},{8,2},{10,4},{12,6},{14,8},{1,11},{3,13... | collective-permute-start | bytes 110600 | tf_op jit(solution)/shard_map/ppermute | solution.py:79
  12.9 0.0 collective-permute-done.refs_0_
  12.9 1.4 %collective-permute-start.5 = (bf16[144,128]{1,0:T(8,128)(2,1)S(1)}, bf16[144,128]{1,0:T(8,128)(2,1)S(1)}, u32[]{:S(2)}, u32[]{:S(2)}) collective-permute-start(bf16[144,128]{1,0:T(8,128)(2,1)S(1)} %get-tuple-element.59), channel_id=1, source_target_pairs={{0,12},{2,14},{4,0},{6,2},{8,4},{10,6},{12,8},{14,10},{1,13},{3,15... | collective-permute-start | bytes 110600 | tf_op jit(solution)/shard_map/ppermute | solution.py:79
  14.3 0.0 collective-permute-done.1.refs_1_
  14.3 1.4 %collective-permute-start.6 = (bf16[144,128]{1,0:T(8,128)(2,1)S(1)}, bf16[144,128]{1,0:T(8,128)(2,1)S(1)}, u32[]{:S(2)}, u32[]{:S(2)}) collective-permute-start(bf16[144,128]{1,0:T(8,128)(2,1)S(1)} %get-tuple-element.60), channel_id=1, source_target_pairs={{0,14},{2,0},{4,2},{6,4},{8,6},{10,8},{12,10},{14,12},{1,15},{3,1}... | collective-permute-start | bytes 110600 | tf_op jit(solution)/shard_map/ppermute | solution.py:79
  15.7 1.7 %shard_map.146 = (bf16[336,1024]{1,0:T(8,128)(2,1)S(1)}, bf16[320,512]{1,0:T(8,128)(2,1)S(1)}, bf16[320,512]{1,0:T(8,128)(2,1)S(1)}, bf16[512,256]{1,0:T(8,128)(2,1)S(1)}, bf16[512,256]{1,0:T(8,128)(2,1)S(1)}) custom-call(bf16[320,512]{1,0:T(8,128)(2,1)} %refs_0_.3, bf16[320,512]{1,0:T(8,128)(2,1)} %refs_1_.1, bf16[512,256]{1,0:T(8,128)(2,1)} %refs_2_.1, ...), custom_call_target="tpu_custom_call" | custom-call | tf_op jit(solution)/shard_map/pallas_call | solution.py:61
  17.4 0.0 collective-permute-done.2.refs_2_
  17.5 0.8 %collective-permute-done.6.refs_6_ = bf16[144,128]{1,0:T(8,128)(2,1)S(1)} collective-permute-done((bf16[144,128]{1,0:T(8,128)(2,1)S(1)}, bf16[144,128]{1,0:T(8,128)(2,1)S(1)}, u32[]{:S(2)}, u32[]{:S(2)}) %collective-permute-start.6) | collective-permute-done | bytes 36896 | tf_op jit(solution)/shard_map/ppermute | solution.py:79
  18.3 0.1 collective-permute-start.7
  18.3 1.5 %collective-permute-done.7.refs_3_ = bf16[7,144,128]{2,1,0:T(8,128)(2,1)S(1)} collective-permute-done((bf16[7,144,128]{2,1,0:T(8,128)(2,1)S(1)}, bf16[7,144,128]{2,1,0:T(8,128)(2,1)S(1)}, u32[]{:S(2)}, u32[]{:S(2)}) %collective-permute-start.7) | collective-permute-done | bytes 258080 | tf_op jit(solution)/shard_map/ppermute | solution.py:79
  19.9 1.6 %shard_map.148 = (bf16[512,512]{1,0:T(8,128)(2,1)S(1)}, bf16[512,336]{1,0:T(8,128)(2,1)S(1)}, bf16[512,256]{1,0:T(8,128)(2,1)S(1)}, bf16[512,256]{1,0:T(8,128)(2...) custom-call(bf16[144,128]{1,0:T(8,128)(2,1)S(1)} %get-tuple-element.53.refs_0_, ...), custom_call_target="tpu_custom_call" | custom-call | tf_op jit(solution)/shard_map/pallas_call | solution.py:32
  21.5 1.6 %collective-permute-start.9 = (bf16[512,256]{1,0:T(8,128)(2,1)S(1)}, bf16[512,256]{1,0:T(8,128)(2,1)S(1)}, u32[]{:S(2)}, u32[]{:S(2)}) collective-permute-start(bf16[512,256]{1,0:T(8,128)(2,1)S(1)} %get-tuple-element.74), channel_id=1, source_target_pairs={{0,2},{1,5},{2,0},{3,7},{4,6},{5,1},{6,4},{7,3},{8,10},{9,13},{10,... | collective-permute-start | bytes 786440 | tf_op jit(solution)/shard_map/ppermute | solution.py:226
  23.1 1.3 %shard_map.149 = (f32[320,256]{1,0:T(8,128)S(1)}, bf16[320,256]{1,0:T(8,128)(2,1)S(1)}, f32[384,256]{1,0:T(8,128)S(1)}, bf16[384,256]{1,0:T(8,128)(2,1)S(1)}, f3...) custom-call(bf16[512,336]{1,0:T(8,128)(2,1)S(1)} %get-tuple-element.64.refs_0_, ...), custom_call_target="tpu_custom_call" | custom-call | tf_op jit(solution)/shard_map/pallas_call | solution.py:32
  24.4 0.5 collective-permute-start.11
  24.9 1.6 %collective-permute-start.12 = (bf16[384,256]{1,0:T(8,128)(2,1)S(1)}, bf16[384,256]{1,0:T(8,128)(2,1)S(1)}, u32[]{:S(2)}, u32[]{:S(2)}) collective-permute-start(bf16[384,256]{1,0:T(8,128)(2,1)S(1)} %get-tuple-element.80), channel_id=1, source_target_pairs={{0,2},{1,5},{2,0},{3,7},{4,6},{5,1},{6,4},{7,3},{8,10},{9,13},{10,... | collective-permute-start | bytes 589832 | tf_op jit(solution)/shard_map/ppermute | solution.py:226
  26.5 1.5 %collective-permute-done.9.refs_1_ = bf16[512,256]{1,0:T(8,128)(2,1)S(1)} collective-permute-done((bf16[512,256]{1,0:T(8,128)(2,1)S(1)}, bf16[512,256]{1,0:T(8,128)(2,1)S(1)}, u32[]{:S(2)}, u32[]{:S(2)}) %collective-permute-start.9) | collective-permute-done | bytes 262176 | tf_op jit(solution)/shard_map/ppermute | solution.py:226
  27.9 0.1 shard_map.150
  28.1 0.7 %collective-permute-start.10 = (bf16[256,256]{1,0:T(8,128)(2,1)S(1)}, bf16[256,256]{1,0:T(8,128)(2,1)S(1)}, u32[]{:S(2)}, u32[]{:S(2)}) collective-permute-start(bf16[256,256]{1,0:T(8,128)(2,1)S(1)} %get-tuple-element.76.refs_2_), channel_id=1, source_target_pairs={{0,4},{1,3},{2,6},{3,1},{4,0},{5,7},{6,2},{7,5},{8,12},{9,11},{10,... | collective-permute-start | bytes 393224 | tf_op jit(solution)/shard_map/ppermute | solution.py:226
  28.8 4.9 %collective-permute-done.12.refs_1_ = bf16[384,256]{1,0:T(8,128)(2,1)S(1)} collective-permute-done((bf16[384,256]{1,0:T(8,128)(2,1)S(1)}, bf16[384,256]{1,0:T(8,128)(2,1)S(1)}, u32[]{:S(2)}, u32[]{:S(2)}) %collective-permute-start.12) | collective-permute-done | bytes 196640 | tf_op jit(solution)/shard_map/ppermute | solution.py:226
  33.7 0.1 shard_map.151
  33.8 0.1 shard_map.152
  33.9 0.7 %collective-permute-start.14 = (bf16[208,256]{1,0:T(8,128)(2,1)S(1)}, bf16[208,256]{1,0:T(8,128)(2,1)S(1)}, u32[]{:S(2)}, u32[]{:S(2)}) collective-permute-start(bf16[208,256]{1,0:T(8,128)(2,1)S(1)} %get-tuple-element.82.refs_2_), channel_id=1, source_target_pairs={{0,4},{1,3},{2,6},{3,1},{4,0},{5,7},{6,2},{7,5},{8,12},{9,11},{10,... | collective-permute-start | bytes 319496 | tf_op jit(solution)/shard_map/ppermute | solution.py:226
  34.6 1.4 %collective-permute-start.15 = (bf16[192,256]{1,0:T(8,128)(2,1)S(1)}, bf16[192,256]{1,0:T(8,128)(2,1)S(1)}, u32[]{:S(2)}, u32[]{:S(2)}) collective-permute-start(bf16[192,256]{1,0:T(8,128)(2,1)S(1)} %get-tuple-element.81.refs_2_), channel_id=1, source_target_pairs={{0,4},{1,3},{2,6},{3,1},{4,0},{5,7},{6,2},{7,5},{8,12},{9,11},{10,... | collective-permute-start | bytes 294920 | tf_op jit(solution)/shard_map/ppermute | solution.py:226
  36.0 0.1 shard_map.153
  36.0 3.7 %collective-permute-done.15.refs_1_ = bf16[192,256]{1,0:T(8,128)(2,1)S(1)} collective-permute-done((bf16[192,256]{1,0:T(8,128)(2,1)S(1)}, bf16[192,256]{1,0:T(8,128)(2,1)S(1)}, u32[]{:S(2)}, u32[]{:S(2)}) %collective-permute-start.15) | collective-permute-done | bytes 98336 | tf_op jit(solution)/shard_map/ppermute | solution.py:226
  39.8 3.7 %collective-permute-start.16 = (bf16[208,256]{1,0:T(8,128)(2,1)S(1)}, bf16[208,256]{1,0:T(8,128)(2,1)S(1)}, u32[]{:S(2)}, u32[]{:S(2)}) collective-permute-start(bf16[208,256]{1,0:T(8,128)(2,1)S(1)} %get-tuple-element.89.refs_2_), channel_id=1, source_target_pairs={{0,8},{1,9},{2,10},{3,11},{4,12},{5,13},{6,14},{7,15},{8,0},{9,1},... | collective-permute-start | bytes 319496 | tf_op jit(solution)/shard_map/ppermute | solution.py:226
  43.5 0.1 collective-permute-start.17
  43.6 6.0 %collective-permute-done.17.refs_1_ = bf16[192,256]{1,0:T(8,128)(2,1)S(1)} collective-permute-done((bf16[192,256]{1,0:T(8,128)(2,1)S(1)}, bf16[192,256]{1,0:T(8,128)(2,1)S(1)}, u32[]{:S(2)}, u32[]{:S(2)}) %collective-permute-start.17) | collective-permute-done | bytes 98336 | tf_op jit(solution)/shard_map/ppermute | solution.py:226
  49.6 0.2 collective-permute-start.19
  49.8 0.6 shard_map.157
  50.5 1.9 %collective-permute-start.21 = (bf16[192,256]{1,0:T(8,128)(2,1)S(1)}, bf16[192,256]{1,0:T(8,128)(2,1)S(1)}, u32[]{:S(2)}, u32[]{:S(2)}) collective-permute-start(bf16[192,256]{1,0:T(8,128)(2,1)S(1)} %get-tuple-element.91.refs_3_.refs_0_), channel_id=1, source_target_pairs={{0,4},{1,3},{2,6},{3,1},{4,0},{5,7},{6,2},{7,5},{8,12},{9,11},{10,... | collective-permute-start | bytes 294920 | tf_op jit(solution)/shard_map/ppermute | solution.py:226
  52.3 1.5 %collective-permute-start.13 = (bf16[128,256]{1,0:T(8,128)(2,1)S(1)}, bf16[128,256]{1,0:T(8,128)(2,1)S(1)}, u32[]{:S(2)}, u32[]{:S(2)}) collective-permute-start(bf16[128,256]{1,0:T(8,128)(2,1)S(1)} %get-tuple-element.84.refs_2_), channel_id=1, source_target_pairs={{0,8},{1,9},{2,10},{3,11},{4,12},{5,13},{6,14},{7,15},{8,0},{9,1},... | collective-permute-start | bytes 196616 | tf_op jit(solution)/shard_map/ppermute | solution.py:226
  53.9 3.7 %collective-permute-done.13.refs_1_ = bf16[128,256]{1,0:T(8,128)(2,1)S(1)} collective-permute-done((bf16[128,256]{1,0:T(8,128)(2,1)S(1)}, bf16[128,256]{1,0:T(8,128)(2,1)S(1)}, u32[]{:S(2)}, u32[]{:S(2)}) %collective-permute-start.13) | collective-permute-done | bytes 65568 | tf_op jit(solution)/shard_map/ppermute | solution.py:226
  57.6 0.2 shard_map.158
  57.9 1.5 %collective-permute-start.20 = (bf16[384,256]{1,0:T(8,128)(2,1)S(1)}, bf16[384,256]{1,0:T(8,128)(2,1)S(1)}, u32[]{:S(2)}, u32[]{:S(2)}) collective-permute-start(bf16[384,256]{1,0:T(8,128)(2,1)S(1)} %shard_map.160.refs_2_.refs_0_), channel_id=1, source_target_pairs={{0,2},{1,5},{2,0},{3,7},{4,6},{5,1},{6,4},{7,3},{8,10},{9,13},{10,... | collective-permute-start | bytes 589832 | tf_op jit(solution)/shard_map/ppermute | solution.py:226
  59.5 0.6 collective-permute-start.22
  60.1 0.5 collective-permute-start.18
  60.6 0.9 %collective-permute-done.8.refs_1_ = bf16[320,256]{1,0:T(8,128)(2,1)S(1)} collective-permute-done((bf16[320,256]{1,0:T(8,128)(2,1)S(1)}, bf16[320,256]{1,0:T(8,128)(2,1)S(1)}, u32[]{:S(2)}, u32[]{:S(2)}) %collective-permute-start.8) | collective-permute-done | bytes 163872 | tf_op jit(solution)/shard_map/ppermute | solution.py:79
  61.5 0.1 collective-permute-done.18.refs_3_
  61.6 0.8 %shard_map.159 = (f32[320,256]{1,0:T(8,128)}, bf16[128,256]{1,0:T(8,128)(2,1)}) custom-call(f32[320,256]{1,0:T(8,128)S(1)} %get-tuple-element.71.refs_0_, bf16[320,256]{1,0:T(8,128)(2,1)S(1)} %collective-permute-done.8.refs_1_, f32[128,256]{1,0:T(8,128)S(1)} %get-tuple-element.92.refs_2_, bf16[128,256]{1,0:T(8,128)(2,1)S(1)} %collective-permute-done.18.refs_3_), custom_call_target="tpu_custom_call" | custom-call | tf_op jit(solution)/shard_map/pallas_call | solution.py:32
  62.3 1.3 %collective-permute-done.20.refs_1_ = bf16[384,256]{1,0:T(8,128)(2,1)S(1)} collective-permute-done((bf16[384,256]{1,0:T(8,128)(2,1)S(1)}, bf16[384,256]{1,0:T(8,128)(2,1)S(1)}, u32[]{:S(2)}, u32[]{:S(2)}) %collective-permute-start.20) | collective-permute-done | bytes 196640 | tf_op jit(solution)/shard_map/ppermute | solution.py:226
  63.6 2.1 %collective-permute-done.22.refs_3_ = bf16[384,256]{1,0:T(8,128)(2,1)S(1)} collective-permute-done((bf16[384,256]{1,0:T(8,128)(2,1)S(1)}, bf16[384,256]{1,0:T(8,128)(2,1)S(1)}, u32[]{:S(2)}, u32[]{:S(2)}) %collective-permute-start.22) | collective-permute-done | bytes 196640 | tf_op jit(solution)/shard_map/ppermute | solution.py:226
  65.7 1.2 %shard_map.162 = (f32[512,256]{1,0:T(8,128)}, f32[256,512]{1,0:T(8,128)}, f32[512,256]{1,0:T(8,128)}) custom-call(bf16[384,256]{1,0:T(8,128)(2,1)S(1)} %shard_map.160.refs_2_.refs_0_, bf16[384,256]{1,0:T(8,128)(2,1)S(1)} %collective-permute-done.20.refs_1_, bf16[384,256]{1,0:T(8,128)(2,1)S(1)} %shard_map.161.refs_2_, ...), custom_call_target="tpu_custom_call" | custom-call | tf_op jit(solution)/shard_map/pallas_call | solution.py:32
  (16 shorter events, 0.2 us)
Async XLA Ops:
  1.9 11.0 %collective-permute-start = (bf16[144,128]{1,0:T(8,128)(2,1)S(1)}, bf16[144,128]{1,0:T(8,128)(2,1)S(1)}, u32[]{:S(2)}, u32[]{:S(2)}) collective-permute-start(bf16[144,128]{1,0:T(8,128)(2,1)S(1)} %get-tuple-element.54), channel_id=1, source_target_pairs={{0,2},{2,4},{4,6},{6,8},{8,10},{10,12},{12,14},{14,0},{1,3},{3,5},... | collective-permute-start | bytes 110600 | tf_op jit(solution)/shard_map/ppermute | solution.py:79
  4.9 9.3 %collective-permute-start.1 = (bf16[144,128]{1,0:T(8,128)(2,1)S(1)}, bf16[144,128]{1,0:T(8,128)(2,1)S(1)}, u32[]{:S(2)}, u32[]{:S(2)}) collective-permute-start(bf16[144,128]{1,0:T(8,128)(2,1)S(1)} %get-tuple-element.55), channel_id=1, source_target_pairs={{0,4},{2,6},{4,8},{6,10},{8,12},{10,14},{12,0},{14,2},{1,5},{3,7},... | collective-permute-start | bytes 110600 | tf_op jit(solution)/shard_map/ppermute | solution.py:79
  6.5 10.9 %collective-permute-start.2 = (bf16[144,128]{1,0:T(8,128)(2,1)S(1)}, bf16[144,128]{1,0:T(8,128)(2,1)S(1)}, u32[]{:S(2)}, u32[]{:S(2)}) collective-permute-start(bf16[144,128]{1,0:T(8,128)(2,1)S(1)} %get-tuple-element.56), channel_id=1, source_target_pairs={{0,6},{2,8},{4,10},{6,12},{8,14},{10,0},{12,2},{14,4},{1,7},{3,9},... | collective-permute-start | bytes 110600 | tf_op jit(solution)/shard_map/ppermute | solution.py:79
  9.1 8.4 %collective-permute-start.3 = (bf16[144,128]{1,0:T(8,128)(2,1)S(1)}, bf16[144,128]{1,0:T(8,128)(2,1)S(1)}, u32[]{:S(2)}, u32[]{:S(2)}) collective-permute-start(bf16[144,128]{1,0:T(8,128)(2,1)S(1)} %get-tuple-element.57), channel_id=1, source_target_pairs={{0,8},{2,10},{4,12},{6,14},{8,0},{10,2},{12,4},{14,6},{1,9},{3,11}... | collective-permute-start | bytes 110600 | tf_op jit(solution)/shard_map/ppermute | solution.py:79
  10.3 7.2 %collective-permute-start.4 = (bf16[144,128]{1,0:T(8,128)(2,1)S(1)}, bf16[144,128]{1,0:T(8,128)(2,1)S(1)}, u32[]{:S(2)}, u32[]{:S(2)}) collective-permute-start(bf16[144,128]{1,0:T(8,128)(2,1)S(1)} %get-tuple-element.58), channel_id=1, source_target_pairs={{0,10},{2,12},{4,14},{6,0},{8,2},{10,4},{12,6},{14,8},{1,11},{3,13... | collective-permute-start | bytes 110600 | tf_op jit(solution)/shard_map/ppermute | solution.py:79
  12.9 4.5 %collective-permute-start.5 = (bf16[144,128]{1,0:T(8,128)(2,1)S(1)}, bf16[144,128]{1,0:T(8,128)(2,1)S(1)}, u32[]{:S(2)}, u32[]{:S(2)}) collective-permute-start(bf16[144,128]{1,0:T(8,128)(2,1)S(1)} %get-tuple-element.59), channel_id=1, source_target_pairs={{0,12},{2,14},{4,0},{6,2},{8,4},{10,6},{12,8},{14,10},{1,13},{3,15... | collective-permute-start | bytes 110600 | tf_op jit(solution)/shard_map/ppermute | solution.py:79
  14.3 4.0 %collective-permute-start.6 = (bf16[144,128]{1,0:T(8,128)(2,1)S(1)}, bf16[144,128]{1,0:T(8,128)(2,1)S(1)}, u32[]{:S(2)}, u32[]{:S(2)}) collective-permute-start(bf16[144,128]{1,0:T(8,128)(2,1)S(1)} %get-tuple-element.60), channel_id=1, source_target_pairs={{0,14},{2,0},{4,2},{6,4},{8,6},{10,8},{12,10},{14,12},{1,15},{3,1}... | collective-permute-start | bytes 110600 | tf_op jit(solution)/shard_map/ppermute | solution.py:79
  18.3 1.6 %collective-permute-start.7 = (bf16[7,144,128]{2,1,0:T(8,128)(2,1)S(1)}, bf16[7,144,128]{2,1,0:T(8,128)(2,1)S(1)}, u32[]{:S(2)}, u32[]{:S(2)}) collective-permute-start(bf16[7,144,128]{2,1,0:T(8,128)(2,1)S(1)} %shard_map.147.refs_1_), channel_id=1, source_target_pairs={{0,1},{1,0},{2,3},{3,2},{4,5},{5,4},{6,7},{7,6},{8,9},{9,8},{10,11... | collective-permute-start | bytes 774152 | tf_op jit(solution)/shard_map/ppermute | solution.py:79
  21.5 6.4 %collective-permute-start.9 = (bf16[512,256]{1,0:T(8,128)(2,1)S(1)}, bf16[512,256]{1,0:T(8,128)(2,1)S(1)}, u32[]{:S(2)}, u32[]{:S(2)}) collective-permute-start(bf16[512,256]{1,0:T(8,128)(2,1)S(1)} %get-tuple-element.74), channel_id=1, source_target_pairs={{0,2},{1,5},{2,0},{3,7},{4,6},{5,1},{6,4},{7,3},{8,10},{9,13},{10,... | collective-permute-start | bytes 786440 | tf_op jit(solution)/shard_map/ppermute | solution.py:226
  24.4 9.4 %collective-permute-start.11 = (bf16[400,256]{1,0:T(8,128)(2,1)S(1)}, bf16[400,256]{1,0:T(8,128)(2,1)S(1)}, u32[]{:S(2)}, u32[]{:S(2)}) collective-permute-start(bf16[400,256]{1,0:T(8,128)(2,1)S(1)} %get-tuple-element.78), channel_id=1, source_target_pairs={{0,2},{1,5},{2,0},{3,7},{4,6},{5,1},{6,4},{7,3},{8,10},{9,13},{10,... | collective-permute-start | bytes 614408 | tf_op jit(solution)/shard_map/ppermute | solution.py:226
  24.9 8.8 %collective-permute-start.12 = (bf16[384,256]{1,0:T(8,128)(2,1)S(1)}, bf16[384,256]{1,0:T(8,128)(2,1)S(1)}, u32[]{:S(2)}, u32[]{:S(2)}) collective-permute-start(bf16[384,256]{1,0:T(8,128)(2,1)S(1)} %get-tuple-element.80), channel_id=1, source_target_pairs={{0,2},{1,5},{2,0},{3,7},{4,6},{5,1},{6,4},{7,3},{8,10},{9,13},{10,... | collective-permute-start | bytes 589832 | tf_op jit(solution)/shard_map/ppermute | solution.py:226
  28.1 7.9 %collective-permute-start.10 = (bf16[256,256]{1,0:T(8,128)(2,1)S(1)}, bf16[256,256]{1,0:T(8,128)(2,1)S(1)}, u32[]{:S(2)}, u32[]{:S(2)}) collective-permute-start(bf16[256,256]{1,0:T(8,128)(2,1)S(1)} %get-tuple-element.76.refs_2_), channel_id=1, source_target_pairs={{0,4},{1,3},{2,6},{3,1},{4,0},{5,7},{6,2},{7,5},{8,12},{9,11},{10,... | collective-permute-start | bytes 393224 | tf_op jit(solution)/shard_map/ppermute | solution.py:226
  33.9 5.9 %collective-permute-start.14 = (bf16[208,256]{1,0:T(8,128)(2,1)S(1)}, bf16[208,256]{1,0:T(8,128)(2,1)S(1)}, u32[]{:S(2)}, u32[]{:S(2)}) collective-permute-start(bf16[208,256]{1,0:T(8,128)(2,1)S(1)} %get-tuple-element.82.refs_2_), channel_id=1, source_target_pairs={{0,4},{1,3},{2,6},{3,1},{4,0},{5,7},{6,2},{7,5},{8,12},{9,11},{10,... | collective-permute-start | bytes 319496 | tf_op jit(solution)/shard_map/ppermute | solution.py:226
  34.6 5.2 %collective-permute-start.15 = (bf16[192,256]{1,0:T(8,128)(2,1)S(1)}, bf16[192,256]{1,0:T(8,128)(2,1)S(1)}, u32[]{:S(2)}, u32[]{:S(2)}) collective-permute-start(bf16[192,256]{1,0:T(8,128)(2,1)S(1)} %get-tuple-element.81.refs_2_), channel_id=1, source_target_pairs={{0,4},{1,3},{2,6},{3,1},{4,0},{5,7},{6,2},{7,5},{8,12},{9,11},{10,... | collective-permute-start | bytes 294920 | tf_op jit(solution)/shard_map/ppermute | solution.py:226
  39.8 10.0 %collective-permute-start.16 = (bf16[208,256]{1,0:T(8,128)(2,1)S(1)}, bf16[208,256]{1,0:T(8,128)(2,1)S(1)}, u32[]{:S(2)}, u32[]{:S(2)}) collective-permute-start(bf16[208,256]{1,0:T(8,128)(2,1)S(1)} %get-tuple-element.89.refs_2_), channel_id=1, source_target_pairs={{0,8},{1,9},{2,10},{3,11},{4,12},{5,13},{6,14},{7,15},{8,0},{9,1},... | collective-permute-start | bytes 319496 | tf_op jit(solution)/shard_map/ppermute | solution.py:226
  43.5 6.1 %collective-permute-start.17 = (bf16[192,256]{1,0:T(8,128)(2,1)S(1)}, bf16[192,256]{1,0:T(8,128)(2,1)S(1)}, u32[]{:S(2)}, u32[]{:S(2)}) collective-permute-start(bf16[192,256]{1,0:T(8,128)(2,1)S(1)} %get-tuple-element.87.refs_2_), channel_id=1, source_target_pairs={{0,8},{1,9},{2,10},{3,11},{4,12},{5,13},{6,14},{7,15},{8,0},{9,1},... | collective-permute-start | bytes 294920 | tf_op jit(solution)/shard_map/ppermute | solution.py:226
  49.6 8.2 %collective-permute-start.19 = (bf16[192,256]{1,0:T(8,128)(2,1)S(1)}, bf16[192,256]{1,0:T(8,128)(2,1)S(1)}, u32[]{:S(2)}, u32[]{:S(2)}) collective-permute-start(bf16[192,256]{1,0:T(8,128)(2,1)S(1)} %shard_map.156.refs_2_.refs_0_), channel_id=1, source_target_pairs={{0,4},{1,3},{2,6},{3,1},{4,0},{5,7},{6,2},{7,5},{8,12},{9,11},{10,... | collective-permute-start | bytes 294920 | tf_op jit(solution)/shard_map/ppermute | solution.py:226
  50.5 9.0 %collective-permute-start.21 = (bf16[192,256]{1,0:T(8,128)(2,1)S(1)}, bf16[192,256]{1,0:T(8,128)(2,1)S(1)}, u32[]{:S(2)}, u32[]{:S(2)}) collective-permute-start(bf16[192,256]{1,0:T(8,128)(2,1)S(1)} %get-tuple-element.91.refs_3_.refs_0_), channel_id=1, source_target_pairs={{0,4},{1,3},{2,6},{3,1},{4,0},{5,7},{6,2},{7,5},{8,12},{9,11},{10,... | collective-permute-start | bytes 294920 | tf_op jit(solution)/shard_map/ppermute | solution.py:226
  52.3 5.3 %collective-permute-start.13 = (bf16[128,256]{1,0:T(8,128)(2,1)S(1)}, bf16[128,256]{1,0:T(8,128)(2,1)S(1)}, u32[]{:S(2)}, u32[]{:S(2)}) collective-permute-start(bf16[128,256]{1,0:T(8,128)(2,1)S(1)} %get-tuple-element.84.refs_2_), channel_id=1, source_target_pairs={{0,8},{1,9},{2,10},{3,11},{4,12},{5,13},{6,14},{7,15},{8,0},{9,1},... | collective-permute-start | bytes 196616 | tf_op jit(solution)/shard_map/ppermute | solution.py:226
  57.9 5.7 %collective-permute-start.20 = (bf16[384,256]{1,0:T(8,128)(2,1)S(1)}, bf16[384,256]{1,0:T(8,128)(2,1)S(1)}, u32[]{:S(2)}, u32[]{:S(2)}) collective-permute-start(bf16[384,256]{1,0:T(8,128)(2,1)S(1)} %shard_map.160.refs_2_.refs_0_), channel_id=1, source_target_pairs={{0,2},{1,5},{2,0},{3,7},{4,6},{5,1},{6,4},{7,3},{8,10},{9,13},{10,... | collective-permute-start | bytes 589832 | tf_op jit(solution)/shard_map/ppermute | solution.py:226
  59.5 6.3 %collective-permute-start.22 = (bf16[384,256]{1,0:T(8,128)(2,1)S(1)}, bf16[384,256]{1,0:T(8,128)(2,1)S(1)}, u32[]{:S(2)}, u32[]{:S(2)}) collective-permute-start(bf16[384,256]{1,0:T(8,128)(2,1)S(1)} %shard_map.161.refs_2_), channel_id=1, source_target_pairs={{0,2},{1,5},{2,0},{3,7},{4,6},{5,1},{6,4},{7,3},{8,10},{9,13},{10,... | collective-permute-start | bytes 589832 | tf_op jit(solution)/shard_map/ppermute | solution.py:226
  60.1 1.4 %collective-permute-start.8 = (bf16[320,256]{1,0:T(8,128)(2,1)S(1)}, bf16[320,256]{1,0:T(8,128)(2,1)S(1)}, u32[]{:S(2)}, u32[]{:S(2)}) collective-permute-start(bf16[320,256]{1,0:T(8,128)(2,1)S(1)} %get-tuple-element.72), channel_id=1, source_target_pairs={{0,1},{1,0},{2,3},{3,2},{4,5},{5,4},{6,7},{7,6},{8,9},{9,8},{10,11... | collective-permute-start | bytes 491528 | tf_op jit(solution)/shard_map/ppermute | solution.py:79
  60.1 1.5 %collective-permute-start.18 = (bf16[128,256]{1,0:T(8,128)(2,1)S(1)}, bf16[128,256]{1,0:T(8,128)(2,1)S(1)}, u32[]{:S(2)}, u32[]{:S(2)}) collective-permute-start(bf16[128,256]{1,0:T(8,128)(2,1)S(1)} %get-tuple-element.93.refs_2_), channel_id=1, source_target_pairs={{0,1},{1,0},{2,3},{3,2},{4,5},{5,4},{6,7},{7,6},{8,9},{9,8},{10,11... | collective-permute-start | bytes 196616 | tf_op jit(solution)/shard_map/ppermute | solution.py:79

commit v11 on v10

--- a/solution.py
+++ b/solution.py
@@ -221,13 +221,14 @@
     for index in range(sizes[0] * sizes[1] * sizes[2]):
         place = [index // (sizes[1] * sizes[2]), index // sizes[2] % sizes[1], index % sizes[2]]
         axis, k = step[place[2] % 2]
-        place[axes.index(axis)] ^= 1 << k
+        place[axes.index(axis)] ^= (2 << k) - 1
         pairs.append((index, (place[0] * sizes[1] + place[1]) * sizes[2] + place[2]))
     return lax.ppermute(value, axes, pairs)
 
 
 def bit_of(step, node, obs):
-    bits = [({"node": node, "obs": obs}[axis] >> k) & 1 for axis, k in step]
+    codes = {"node": node ^ (node >> 1), "obs": obs ^ (obs >> 1)}
+    bits = [(codes[axis] >> k) & 1 for axis, k in step]
     return jnp.where(lax.axis_index("mp") % 2 == 0, bits[0], bits[1])
 
 

time: 67.4 us -> 69.9 us (1.037)
  waiting for transfers between devices: 26.5 us -> 29 us
    ppermute x13, waiting for transfers between devices: 23.2 us -> 25.7 us  [flip(): return lax.ppermute(value, axes, pairs)]
  transfers between devices with their start and end apart: 23 -> 23, of which waited for: 11 -> 11; matrix products, arithmetic and copies ran while one was open for 0% -> 0% of each run, Pallas kernels for 8% -> 7%
where the time goes in v11:
time: 69.9 us; the launch traced here: 69.8 us
  starting transfers between devices  30.8 us (44%)
  waiting for transfers between devices  29 us (41%)
  Pallas kernels  9.22 us (13%)
  between operations  0.81 us (1%)
    ppermute x13, waiting for transfers between devices, flip(): return lax.ppermute(value, axes, pairs)  25.7 us
    ppermute x13, starting transfers between devices, flip(): return lax.ppermute(value, axes, pairs)  16.4 us
    ppermute x10, starting transfers between devices, shift(): lax.ppermute(value, axis, [(i, (i + step) % size) for i in range(size)])  14.3 us
    pallas_call x16, Pallas kernels, call(): pl.pallas_call(lambda *refs: kernel(*refs[:count], *refs[len(args):]), ou...  6.19 us
    ppermute x10, waiting for transfers between devices, shift(): lax.ppermute(value, axis, [(i, (i + step) % size) for i in range(size)])  3.27 us
    pallas_call x2, Pallas kernels, call_staged(): pl.pallas_call(staged, out_shape=[jax.ShapeDtypeStruct(shape, dtype) for...  3.03 us
  transfers between devices with their start and end apart: 23, of which 11 were waited for; matrix products, arithmetic and copies ran while one was open for 0% of the time, Pallas kernels for 7%

profile of v11, /device:TPU:0, one launch (start us, length us, event | category | flops | bytes accessed | tf_op | source)
XLA Modules:
  0.0 69.8 jit_solution(3370096289027702098)
XLA Ops:
  0.6 1.3 %shard_map.145 = (bf16[144,128]{1,0:T(8,128)(2,1)S(1)}, bf16[144,128]{1,0:T(8,128)(2,1)S(1)}, bf16[144,128]{1,0:T(8,128)(2,1)S(1)}, bf16[144,128]{1,0:T(8,128)(2...) custom-call(bf16[128,512]{1,0:T(8,128)(2,1)} %refs_0_.2, ...), custom_call_target="tpu_custom_call" | custom-call | tf_op jit(solution)/shard_map/pallas_call | solution.py:61
  1.9 3.0 %collective-permute-start = (bf16[144,128]{1,0:T(8,128)(2,1)S(1)}, bf16[144,128]{1,0:T(8,128)(2,1)S(1)}, u32[]{:S(2)}, u32[]{:S(2)}) collective-permute-start(bf16[144,128]{1,0:T(8,128)(2,1)S(1)} %get-tuple-element.54), channel_id=1, source_target_pairs={{0,2},{2,4},{4,6},{6,8},{8,10},{10,12},{12,14},{14,0},{1,3},{3,5},... | collective-permute-start | bytes 110600 | tf_op jit(solution)/shard_map/ppermute | solution.py:79
  4.9 1.6 %collective-permute-start.1 = (bf16[144,128]{1,0:T(8,128)(2,1)S(1)}, bf16[144,128]{1,0:T(8,128)(2,1)S(1)}, u32[]{:S(2)}, u32[]{:S(2)}) collective-permute-start(bf16[144,128]{1,0:T(8,128)(2,1)S(1)} %get-tuple-element.55), channel_id=1, source_target_pairs={{0,4},{2,6},{4,8},{6,10},{8,12},{10,14},{12,0},{14,2},{1,5},{3,7},... | collective-permute-start | bytes 110600 | tf_op jit(solution)/shard_map/ppermute | solution.py:79
  6.5 2.6 %collective-permute-start.2 = (bf16[144,128]{1,0:T(8,128)(2,1)S(1)}, bf16[144,128]{1,0:T(8,128)(2,1)S(1)}, u32[]{:S(2)}, u32[]{:S(2)}) collective-permute-start(bf16[144,128]{1,0:T(8,128)(2,1)S(1)} %get-tuple-element.56), channel_id=1, source_target_pairs={{0,6},{2,8},{4,10},{6,12},{8,14},{10,0},{12,2},{14,4},{1,7},{3,9},... | collective-permute-start | bytes 110600 | tf_op jit(solution)/shard_map/ppermute | solution.py:79
  9.1 1.2 %collective-permute-start.3 = (bf16[144,128]{1,0:T(8,128)(2,1)S(1)}, bf16[144,128]{1,0:T(8,128)(2,1)S(1)}, u32[]{:S(2)}, u32[]{:S(2)}) collective-permute-start(bf16[144,128]{1,0:T(8,128)(2,1)S(1)} %get-tuple-element.57), channel_id=1, source_target_pairs={{0,8},{2,10},{4,12},{6,14},{8,0},{10,2},{12,4},{14,6},{1,9},{3,11}... | collective-permute-start | bytes 110600 | tf_op jit(solution)/shard_map/ppermute | solution.py:79
  10.3 2.6 %collective-permute-start.4 = (bf16[144,128]{1,0:T(8,128)(2,1)S(1)}, bf16[144,128]{1,0:T(8,128)(2,1)S(1)}, u32[]{:S(2)}, u32[]{:S(2)}) collective-permute-start(bf16[144,128]{1,0:T(8,128)(2,1)S(1)} %get-tuple-element.58), channel_id=1, source_target_pairs={{0,10},{2,12},{4,14},{6,0},{8,2},{10,4},{12,6},{14,8},{1,11},{3,13... | collective-permute-start | bytes 110600 | tf_op jit(solution)/shard_map/ppermute | solution.py:79
  12.9 1.4 %collective-permute-start.5 = (bf16[144,128]{1,0:T(8,128)(2,1)S(1)}, bf16[144,128]{1,0:T(8,128)(2,1)S(1)}, u32[]{:S(2)}, u32[]{:S(2)}) collective-permute-start(bf16[144,128]{1,0:T(8,128)(2,1)S(1)} %get-tuple-element.59), channel_id=1, source_target_pairs={{0,12},{2,14},{4,0},{6,2},{8,4},{10,6},{12,8},{14,10},{1,13},{3,15... | collective-permute-start | bytes 110600 | tf_op jit(solution)/shard_map/ppermute | solution.py:79
  14.3 1.4 %collective-permute-start.6 = (bf16[144,128]{1,0:T(8,128)(2,1)S(1)}, bf16[144,128]{1,0:T(8,128)(2,1)S(1)}, u32[]{:S(2)}, u32[]{:S(2)}) collective-permute-start(bf16[144,128]{1,0:T(8,128)(2,1)S(1)} %get-tuple-element.60), channel_id=1, source_target_pairs={{0,14},{2,0},{4,2},{6,4},{8,6},{10,8},{12,10},{14,12},{1,15},{3,1}... | collective-permute-start | bytes 110600 | tf_op jit(solution)/shard_map/ppermute | solution.py:79
  15.7 1.7 %shard_map.146 = (bf16[336,1024]{1,0:T(8,128)(2,1)S(1)}, bf16[320,512]{1,0:T(8,128)(2,1)S(1)}, bf16[320,512]{1,0:T(8,128)(2,1)S(1)}, bf16[512,256]{1,0:T(8,128)(2,1)S(1)}, bf16[512,256]{1,0:T(8,128)(2,1)S(1)}) custom-call(bf16[320,512]{1,0:T(8,128)(2,1)} %refs_0_.3, bf16[320,512]{1,0:T(8,128)(2,1)} %refs_1_.1, bf16[512,256]{1,0:T(8,128)(2,1)} %refs_2_.1, ...), custom_call_target="tpu_custom_call" | custom-call | tf_op jit(solution)/shard_map/pallas_call | solution.py:61
  17.4 0.0 collective-permute-done.2.refs_2_
  17.5 0.0 collective-permute-done.4.refs_4_
  17.5 0.0 collective-permute-done.5.refs_5_
  17.5 0.8 %collective-permute-done.6.refs_6_ = bf16[144,128]{1,0:T(8,128)(2,1)S(1)} collective-permute-done((bf16[144,128]{1,0:T(8,128)(2,1)S(1)}, bf16[144,128]{1,0:T(8,128)(2,1)S(1)}, u32[]{:S(2)}, u32[]{:S(2)}) %collective-permute-start.6) | collective-permute-done | bytes 36896 | tf_op jit(solution)/shard_map/ppermute | solution.py:79
  18.3 0.1 collective-permute-start.7
  18.3 1.5 %collective-permute-done.7.refs_3_ = bf16[7,144,128]{2,1,0:T(8,128)(2,1)S(1)} collective-permute-done((bf16[7,144,128]{2,1,0:T(8,128)(2,1)S(1)}, bf16[7,144,128]{2,1,0:T(8,128)(2,1)S(1)}, u32[]{:S(2)}, u32[]{:S(2)}) %collective-permute-start.7) | collective-permute-done | bytes 258080 | tf_op jit(solution)/shard_map/ppermute | solution.py:79
  19.9 1.6 %shard_map.148 = (bf16[512,512]{1,0:T(8,128)(2,1)S(1)}, bf16[512,336]{1,0:T(8,128)(2,1)S(1)}, bf16[512,256]{1,0:T(8,128)(2,1)S(1)}, bf16[512,256]{1,0:T(8,128)(2...) custom-call(bf16[144,128]{1,0:T(8,128)(2,1)S(1)} %get-tuple-element.53.refs_0_, ...), custom_call_target="tpu_custom_call" | custom-call | tf_op jit(solution)/shard_map/pallas_call | solution.py:32
  21.5 1.6 %collective-permute-start.9 = (bf16[512,256]{1,0:T(8,128)(2,1)S(1)}, bf16[512,256]{1,0:T(8,128)(2,1)S(1)}, u32[]{:S(2)}, u32[]{:S(2)}) collective-permute-start(bf16[512,256]{1,0:T(8,128)(2,1)S(1)} %get-tuple-element.74), channel_id=1, source_target_pairs={{0,2},{1,5},{2,0},{3,7},{4,6},{5,1},{6,4},{7,3},{8,10},{9,13},{10,... | collective-permute-start | bytes 786440 | tf_op jit(solution)/shard_map/ppermute | solution.py:226
  23.1 1.3 %shard_map.149 = (f32[320,256]{1,0:T(8,128)S(1)}, bf16[320,256]{1,0:T(8,128)(2,1)S(1)}, f32[384,256]{1,0:T(8,128)S(1)}, bf16[384,256]{1,0:T(8,128)(2,1)S(1)}, f3...) custom-call(bf16[512,336]{1,0:T(8,128)(2,1)S(1)} %get-tuple-element.64.refs_0_, ...), custom_call_target="tpu_custom_call" | custom-call | tf_op jit(solution)/shard_map/pallas_call | solution.py:32
  24.4 0.5 collective-permute-start.11
  24.9 1.5 %collective-permute-start.12 = (bf16[384,256]{1,0:T(8,128)(2,1)S(1)}, bf16[384,256]{1,0:T(8,128)(2,1)S(1)}, u32[]{:S(2)}, u32[]{:S(2)}) collective-permute-start(bf16[384,256]{1,0:T(8,128)(2,1)S(1)} %get-tuple-element.80), channel_id=1, source_target_pairs={{0,2},{1,5},{2,0},{3,7},{4,6},{5,1},{6,4},{7,3},{8,10},{9,13},{10,... | collective-permute-start | bytes 589832 | tf_op jit(solution)/shard_map/ppermute | solution.py:226
  26.5 1.5 %collective-permute-done.9.refs_1_ = bf16[512,256]{1,0:T(8,128)(2,1)S(1)} collective-permute-done((bf16[512,256]{1,0:T(8,128)(2,1)S(1)}, bf16[512,256]{1,0:T(8,128)(2,1)S(1)}, u32[]{:S(2)}, u32[]{:S(2)}) %collective-permute-start.9) | collective-permute-done | bytes 262176 | tf_op jit(solution)/shard_map/ppermute | solution.py:226
  27.9 0.1 shard_map.150
  28.1 0.7 %collective-permute-start.10 = (bf16[256,256]{1,0:T(8,128)(2,1)S(1)}, bf16[256,256]{1,0:T(8,128)(2,1)S(1)}, u32[]{:S(2)}, u32[]{:S(2)}) collective-permute-start(bf16[256,256]{1,0:T(8,128)(2,1)S(1)} %get-tuple-element.76.refs_2_), channel_id=1, source_target_pairs={{0,4},{1,3},{2,6},{3,1},{4,0},{5,7},{6,2},{7,5},{8,12},{9,11},{10,... | collective-permute-start | bytes 393224 | tf_op jit(solution)/shard_map/ppermute | solution.py:226
  28.8 4.9 %collective-permute-done.12.refs_1_ = bf16[384,256]{1,0:T(8,128)(2,1)S(1)} collective-permute-done((bf16[384,256]{1,0:T(8,128)(2,1)S(1)}, bf16[384,256]{1,0:T(8,128)(2,1)S(1)}, u32[]{:S(2)}, u32[]{:S(2)}) %collective-permute-start.12) | collective-permute-done | bytes 196640 | tf_op jit(solution)/shard_map/ppermute | solution.py:226
  33.7 0.1 shard_map.151
  33.8 0.1 shard_map.152
  33.9 0.7 collective-permute-start.14
  34.6 1.4 %collective-permute-start.15 = (bf16[192,256]{1,0:T(8,128)(2,1)S(1)}, bf16[192,256]{1,0:T(8,128)(2,1)S(1)}, u32[]{:S(2)}, u32[]{:S(2)}) collective-permute-start(bf16[192,256]{1,0:T(8,128)(2,1)S(1)} %get-tuple-element.81.refs_2_), channel_id=1, source_target_pairs={{0,4},{1,3},{2,6},{3,1},{4,0},{5,7},{6,2},{7,5},{8,12},{9,11},{10,... | collective-permute-start | bytes 294920 | tf_op jit(solution)/shard_map/ppermute | solution.py:226
  36.0 0.1 shard_map.153
  36.0 3.7 %collective-permute-done.15.refs_1_ = bf16[192,256]{1,0:T(8,128)(2,1)S(1)} collective-permute-done((bf16[192,256]{1,0:T(8,128)(2,1)S(1)}, bf16[192,256]{1,0:T(8,128)(2,1)S(1)}, u32[]{:S(2)}, u32[]{:S(2)}) %collective-permute-start.15) | collective-permute-done | bytes 98336 | tf_op jit(solution)/shard_map/ppermute | solution.py:226
  39.8 3.2 %collective-permute-start.16 = (bf16[208,256]{1,0:T(8,128)(2,1)S(1)}, bf16[208,256]{1,0:T(8,128)(2,1)S(1)}, u32[]{:S(2)}, u32[]{:S(2)}) collective-permute-start(bf16[208,256]{1,0:T(8,128)(2,1)S(1)} %get-tuple-element.89.refs_2_), channel_id=1, source_target_pairs={{0,12},{1,13},{2,14},{3,15},{4,8},{5,9},{6,10},{7,11},{8,4},{9,5},... | collective-permute-start | bytes 319496 | tf_op jit(solution)/shard_map/ppermute | solution.py:226
  43.0 0.7 collective-permute-start.17
  43.7 5.8 %collective-permute-done.17.refs_1_ = bf16[192,256]{1,0:T(8,128)(2,1)S(1)} collective-permute-done((bf16[192,256]{1,0:T(8,128)(2,1)S(1)}, bf16[192,256]{1,0:T(8,128)(2,1)S(1)}, u32[]{:S(2)}, u32[]{:S(2)}) %collective-permute-start.17) | collective-permute-done | bytes 98336 | tf_op jit(solution)/shard_map/ppermute | solution.py:226
  49.6 1.1 %collective-permute-start.19 = (bf16[192,256]{1,0:T(8,128)(2,1)S(1)}, bf16[192,256]{1,0:T(8,128)(2,1)S(1)}, u32[]{:S(2)}, u32[]{:S(2)}) collective-permute-start(bf16[192,256]{1,0:T(8,128)(2,1)S(1)} %shard_map.156.refs_2_.refs_0_), channel_id=1, source_target_pairs={{0,4},{1,3},{2,6},{3,1},{4,0},{5,7},{6,2},{7,5},{8,12},{9,11},{10,... | collective-permute-start | bytes 294920 | tf_op jit(solution)/shard_map/ppermute | solution.py:226
  50.7 0.6 shard_map.157
  51.3 0.9 %collective-permute-start.21 = (bf16[192,256]{1,0:T(8,128)(2,1)S(1)}, bf16[192,256]{1,0:T(8,128)(2,1)S(1)}, u32[]{:S(2)}, u32[]{:S(2)}) collective-permute-start(bf16[192,256]{1,0:T(8,128)(2,1)S(1)} %get-tuple-element.91.refs_3_.refs_0_), channel_id=1, source_target_pairs={{0,4},{1,3},{2,6},{3,1},{4,0},{5,7},{6,2},{7,5},{8,12},{9,11},{10,... | collective-permute-start | bytes 294920 | tf_op jit(solution)/shard_map/ppermute | solution.py:226
  52.3 1.8 %collective-permute-start.13 = (bf16[128,256]{1,0:T(8,128)(2,1)S(1)}, bf16[128,256]{1,0:T(8,128)(2,1)S(1)}, u32[]{:S(2)}, u32[]{:S(2)}) collective-permute-start(bf16[128,256]{1,0:T(8,128)(2,1)S(1)} %get-tuple-element.84.refs_2_), channel_id=1, source_target_pairs={{0,12},{1,13},{2,14},{3,15},{4,8},{5,9},{6,10},{7,11},{8,4},{9,5},... | collective-permute-start | bytes 196616 | tf_op jit(solution)/shard_map/ppermute | solution.py:226
  54.0 6.4 %collective-permute-done.13.refs_1_ = bf16[128,256]{1,0:T(8,128)(2,1)S(1)} collective-permute-done((bf16[128,256]{1,0:T(8,128)(2,1)S(1)}, bf16[128,256]{1,0:T(8,128)(2,1)S(1)}, u32[]{:S(2)}, u32[]{:S(2)}) %collective-permute-start.13) | collective-permute-done | bytes 65568 | tf_op jit(solution)/shard_map/ppermute | solution.py:226
  60.5 0.2 shard_map.158
  60.8 1.5 %collective-permute-start.20 = (bf16[384,256]{1,0:T(8,128)(2,1)S(1)}, bf16[384,256]{1,0:T(8,128)(2,1)S(1)}, u32[]{:S(2)}, u32[]{:S(2)}) collective-permute-start(bf16[384,256]{1,0:T(8,128)(2,1)S(1)} %shard_map.160.refs_2_.refs_0_), channel_id=1, source_target_pairs={{0,2},{1,5},{2,0},{3,7},{4,6},{5,1},{6,4},{7,3},{8,10},{9,13},{10,... | collective-permute-start | bytes 589832 | tf_op jit(solution)/shard_map/ppermute | solution.py:226
  62.3 0.6 collective-permute-start.22
  63.0 0.5 collective-permute-start.18
  63.5 0.9 %collective-permute-done.8.refs_1_ = bf16[320,256]{1,0:T(8,128)(2,1)S(1)} collective-permute-done((bf16[320,256]{1,0:T(8,128)(2,1)S(1)}, bf16[320,256]{1,0:T(8,128)(2,1)S(1)}, u32[]{:S(2)}, u32[]{:S(2)}) %collective-permute-start.8) | collective-permute-done | bytes 163872 | tf_op jit(solution)/shard_map/ppermute | solution.py:79
  64.4 0.1 collective-permute-done.18.refs_3_
  64.4 0.8 %shard_map.159 = (f32[320,256]{1,0:T(8,128)}, bf16[128,256]{1,0:T(8,128)(2,1)}) custom-call(f32[320,256]{1,0:T(8,128)S(1)} %get-tuple-element.71.refs_0_, bf16[320,256]{1,0:T(8,128)(2,1)S(1)} %collective-permute-done.8.refs_1_, f32[128,256]{1,0:T(8,128)S(1)} %get-tuple-element.92.refs_2_, bf16[128,256]{1,0:T(8,128)(2,1)S(1)} %collective-permute-done.18.refs_3_), custom_call_target="tpu_custom_call" | custom-call | tf_op jit(solution)/shard_map/pallas_call | solution.py:32
  65.2 1.3 %collective-permute-done.20.refs_1_ = bf16[384,256]{1,0:T(8,128)(2,1)S(1)} collective-permute-done((bf16[384,256]{1,0:T(8,128)(2,1)S(1)}, bf16[384,256]{1,0:T(8,128)(2,1)S(1)}, u32[]{:S(2)}, u32[]{:S(2)}) %collective-permute-start.20) | collective-permute-done | bytes 196640 | tf_op jit(solution)/shard_map/ppermute | solution.py:226
  66.5 2.1 %collective-permute-done.22.refs_3_ = bf16[384,256]{1,0:T(8,128)(2,1)S(1)} collective-permute-done((bf16[384,256]{1,0:T(8,128)(2,1)S(1)}, bf16[384,256]{1,0:T(8,128)(2,1)S(1)}, u32[]{:S(2)}, u32[]{:S(2)}) %collective-permute-start.22) | collective-permute-done | bytes 196640 | tf_op jit(solution)/shard_map/ppermute | solution.py:226
  68.6 1.2 %shard_map.162 = (f32[512,256]{1,0:T(8,128)}, f32[256,512]{1,0:T(8,128)}, f32[512,256]{1,0:T(8,128)}) custom-call(bf16[384,256]{1,0:T(8,128)(2,1)S(1)} %shard_map.160.refs_2_.refs_0_, bf16[384,256]{1,0:T(8,128)(2,1)S(1)} %collective-permute-done.20.refs_1_, bf16[384,256]{1,0:T(8,128)(2,1)S(1)} %shard_map.161.refs_2_, ...), custom_call_target="tpu_custom_call" | custom-call | tf_op jit(solution)/shard_map/pallas_call | solution.py:32
  (16 shorter events, 0.2 us)
Async XLA Ops:
  1.9 11.0 %collective-permute-start = (bf16[144,128]{1,0:T(8,128)(2,1)S(1)}, bf16[144,128]{1,0:T(8,128)(2,1)S(1)}, u32[]{:S(2)}, u32[]{:S(2)}) collective-permute-start(bf16[144,128]{1,0:T(8,128)(2,1)S(1)} %get-tuple-element.54), channel_id=1, source_target_pairs={{0,2},{2,4},{4,6},{6,8},{8,10},{10,12},{12,14},{14,0},{1,3},{3,5},... | collective-permute-start | bytes 110600 | tf_op jit(solution)/shard_map/ppermute | solution.py:79
  4.9 9.3 %collective-permute-start.1 = (bf16[144,128]{1,0:T(8,128)(2,1)S(1)}, bf16[144,128]{1,0:T(8,128)(2,1)S(1)}, u32[]{:S(2)}, u32[]{:S(2)}) collective-permute-start(bf16[144,128]{1,0:T(8,128)(2,1)S(1)} %get-tuple-element.55), channel_id=1, source_target_pairs={{0,4},{2,6},{4,8},{6,10},{8,12},{10,14},{12,0},{14,2},{1,5},{3,7},... | collective-permute-start | bytes 110600 | tf_op jit(solution)/shard_map/ppermute | solution.py:79
  6.5 10.9 %collective-permute-start.2 = (bf16[144,128]{1,0:T(8,128)(2,1)S(1)}, bf16[144,128]{1,0:T(8,128)(2,1)S(1)}, u32[]{:S(2)}, u32[]{:S(2)}) collective-permute-start(bf16[144,128]{1,0:T(8,128)(2,1)S(1)} %get-tuple-element.56), channel_id=1, source_target_pairs={{0,6},{2,8},{4,10},{6,12},{8,14},{10,0},{12,2},{14,4},{1,7},{3,9},... | collective-permute-start | bytes 110600 | tf_op jit(solution)/shard_map/ppermute | solution.py:79
  9.1 8.4 %collective-permute-start.3 = (bf16[144,128]{1,0:T(8,128)(2,1)S(1)}, bf16[144,128]{1,0:T(8,128)(2,1)S(1)}, u32[]{:S(2)}, u32[]{:S(2)}) collective-permute-start(bf16[144,128]{1,0:T(8,128)(2,1)S(1)} %get-tuple-element.57), channel_id=1, source_target_pairs={{0,8},{2,10},{4,12},{6,14},{8,0},{10,2},{12,4},{14,6},{1,9},{3,11}... | collective-permute-start | bytes 110600 | tf_op jit(solution)/shard_map/ppermute | solution.py:79
  10.3 7.2 %collective-permute-start.4 = (bf16[144,128]{1,0:T(8,128)(2,1)S(1)}, bf16[144,128]{1,0:T(8,128)(2,1)S(1)}, u32[]{:S(2)}, u32[]{:S(2)}) collective-permute-start(bf16[144,128]{1,0:T(8,128)(2,1)S(1)} %get-tuple-element.58), channel_id=1, source_target_pairs={{0,10},{2,12},{4,14},{6,0},{8,2},{10,4},{12,6},{14,8},{1,11},{3,13... | collective-permute-start | bytes 110600 | tf_op jit(solution)/shard_map/ppermute | solution.py:79
  12.9 4.5 %collective-permute-start.5 = (bf16[144,128]{1,0:T(8,128)(2,1)S(1)}, bf16[144,128]{1,0:T(8,128)(2,1)S(1)}, u32[]{:S(2)}, u32[]{:S(2)}) collective-permute-start(bf16[144,128]{1,0:T(8,128)(2,1)S(1)} %get-tuple-element.59), channel_id=1, source_target_pairs={{0,12},{2,14},{4,0},{6,2},{8,4},{10,6},{12,8},{14,10},{1,13},{3,15... | collective-permute-start | bytes 110600 | tf_op jit(solution)/shard_map/ppermute | solution.py:79
  14.3 4.0 %collective-permute-start.6 = (bf16[144,128]{1,0:T(8,128)(2,1)S(1)}, bf16[144,128]{1,0:T(8,128)(2,1)S(1)}, u32[]{:S(2)}, u32[]{:S(2)}) collective-permute-start(bf16[144,128]{1,0:T(8,128)(2,1)S(1)} %get-tuple-element.60), channel_id=1, source_target_pairs={{0,14},{2,0},{4,2},{6,4},{8,6},{10,8},{12,10},{14,12},{1,15},{3,1}... | collective-permute-start | bytes 110600 | tf_op jit(solution)/shard_map/ppermute | solution.py:79
  18.3 1.6 %collective-permute-start.7 = (bf16[7,144,128]{2,1,0:T(8,128)(2,1)S(1)}, bf16[7,144,128]{2,1,0:T(8,128)(2,1)S(1)}, u32[]{:S(2)}, u32[]{:S(2)}) collective-permute-start(bf16[7,144,128]{2,1,0:T(8,128)(2,1)S(1)} %shard_map.147.refs_1_), channel_id=1, source_target_pairs={{0,1},{1,0},{2,3},{3,2},{4,5},{5,4},{6,7},{7,6},{8,9},{9,8},{10,11... | collective-permute-start | bytes 774152 | tf_op jit(solution)/shard_map/ppermute | solution.py:79
  21.5 6.4 %collective-permute-start.9 = (bf16[512,256]{1,0:T(8,128)(2,1)S(1)}, bf16[512,256]{1,0:T(8,128)(2,1)S(1)}, u32[]{:S(2)}, u32[]{:S(2)}) collective-permute-start(bf16[512,256]{1,0:T(8,128)(2,1)S(1)} %get-tuple-element.74), channel_id=1, source_target_pairs={{0,2},{1,5},{2,0},{3,7},{4,6},{5,1},{6,4},{7,3},{8,10},{9,13},{10,... | collective-permute-start | bytes 786440 | tf_op jit(solution)/shard_map/ppermute | solution.py:226
  24.4 9.4 %collective-permute-start.11 = (bf16[400,256]{1,0:T(8,128)(2,1)S(1)}, bf16[400,256]{1,0:T(8,128)(2,1)S(1)}, u32[]{:S(2)}, u32[]{:S(2)}) collective-permute-start(bf16[400,256]{1,0:T(8,128)(2,1)S(1)} %get-tuple-element.78), channel_id=1, source_target_pairs={{0,2},{1,5},{2,0},{3,7},{4,6},{5,1},{6,4},{7,3},{8,10},{9,13},{10,... | collective-permute-start | bytes 614408 | tf_op jit(solution)/shard_map/ppermute | solution.py:226
  24.9 8.8 %collective-permute-start.12 = (bf16[384,256]{1,0:T(8,128)(2,1)S(1)}, bf16[384,256]{1,0:T(8,128)(2,1)S(1)}, u32[]{:S(2)}, u32[]{:S(2)}) collective-permute-start(bf16[384,256]{1,0:T(8,128)(2,1)S(1)} %get-tuple-element.80), channel_id=1, source_target_pairs={{0,2},{1,5},{2,0},{3,7},{4,6},{5,1},{6,4},{7,3},{8,10},{9,13},{10,... | collective-permute-start | bytes 589832 | tf_op jit(solution)/shard_map/ppermute | solution.py:226
  28.1 7.9 %collective-permute-start.10 = (bf16[256,256]{1,0:T(8,128)(2,1)S(1)}, bf16[256,256]{1,0:T(8,128)(2,1)S(1)}, u32[]{:S(2)}, u32[]{:S(2)}) collective-permute-start(bf16[256,256]{1,0:T(8,128)(2,1)S(1)} %get-tuple-element.76.refs_2_), channel_id=1, source_target_pairs={{0,4},{1,3},{2,6},{3,1},{4,0},{5,7},{6,2},{7,5},{8,12},{9,11},{10,... | collective-permute-start | bytes 393224 | tf_op jit(solution)/shard_map/ppermute | solution.py:226
  33.9 5.9 %collective-permute-start.14 = (bf16[208,256]{1,0:T(8,128)(2,1)S(1)}, bf16[208,256]{1,0:T(8,128)(2,1)S(1)}, u32[]{:S(2)}, u32[]{:S(2)}) collective-permute-start(bf16[208,256]{1,0:T(8,128)(2,1)S(1)} %get-tuple-element.82.refs_2_), channel_id=1, source_target_pairs={{0,4},{1,3},{2,6},{3,1},{4,0},{5,7},{6,2},{7,5},{8,12},{9,11},{10,... | collective-permute-start | bytes 319496 | tf_op jit(solution)/shard_map/ppermute | solution.py:226
  34.6 5.2 %collective-permute-start.15 = (bf16[192,256]{1,0:T(8,128)(2,1)S(1)}, bf16[192,256]{1,0:T(8,128)(2,1)S(1)}, u32[]{:S(2)}, u32[]{:S(2)}) collective-permute-start(bf16[192,256]{1,0:T(8,128)(2,1)S(1)} %get-tuple-element.81.refs_2_), channel_id=1, source_target_pairs={{0,4},{1,3},{2,6},{3,1},{4,0},{5,7},{6,2},{7,5},{8,12},{9,11},{10,... | collective-permute-start | bytes 294920 | tf_op jit(solution)/shard_map/ppermute | solution.py:226
  39.8 10.9 %collective-permute-start.16 = (bf16[208,256]{1,0:T(8,128)(2,1)S(1)}, bf16[208,256]{1,0:T(8,128)(2,1)S(1)}, u32[]{:S(2)}, u32[]{:S(2)}) collective-permute-start(bf16[208,256]{1,0:T(8,128)(2,1)S(1)} %get-tuple-element.89.refs_2_), channel_id=1, source_target_pairs={{0,12},{1,13},{2,14},{3,15},{4,8},{5,9},{6,10},{7,11},{8,4},{9,5},... | collective-permute-start | bytes 319496 | tf_op jit(solution)/shard_map/ppermute | solution.py:226
  43.0 6.5 %collective-permute-start.17 = (bf16[192,256]{1,0:T(8,128)(2,1)S(1)}, bf16[192,256]{1,0:T(8,128)(2,1)S(1)}, u32[]{:S(2)}, u32[]{:S(2)}) collective-permute-start(bf16[192,256]{1,0:T(8,128)(2,1)S(1)} %get-tuple-element.87.refs_2_), channel_id=1, source_target_pairs={{0,12},{1,13},{2,14},{3,15},{4,8},{5,9},{6,10},{7,11},{8,4},{9,5},... | collective-permute-start | bytes 294920 | tf_op jit(solution)/shard_map/ppermute | solution.py:226
  49.6 11.2 %collective-permute-start.19 = (bf16[192,256]{1,0:T(8,128)(2,1)S(1)}, bf16[192,256]{1,0:T(8,128)(2,1)S(1)}, u32[]{:S(2)}, u32[]{:S(2)}) collective-permute-start(bf16[192,256]{1,0:T(8,128)(2,1)S(1)} %shard_map.156.refs_2_.refs_0_), channel_id=1, source_target_pairs={{0,4},{1,3},{2,6},{3,1},{4,0},{5,7},{6,2},{7,5},{8,12},{9,11},{10,... | collective-permute-start | bytes 294920 | tf_op jit(solution)/shard_map/ppermute | solution.py:226
  51.3 10.9 %collective-permute-start.21 = (bf16[192,256]{1,0:T(8,128)(2,1)S(1)}, bf16[192,256]{1,0:T(8,128)(2,1)S(1)}, u32[]{:S(2)}, u32[]{:S(2)}) collective-permute-start(bf16[192,256]{1,0:T(8,128)(2,1)S(1)} %get-tuple-element.91.refs_3_.refs_0_), channel_id=1, source_target_pairs={{0,4},{1,3},{2,6},{3,1},{4,0},{5,7},{6,2},{7,5},{8,12},{9,11},{10,... | collective-permute-start | bytes 294920 | tf_op jit(solution)/shard_map/ppermute | solution.py:226
  52.3 8.2 %collective-permute-start.13 = (bf16[128,256]{1,0:T(8,128)(2,1)S(1)}, bf16[128,256]{1,0:T(8,128)(2,1)S(1)}, u32[]{:S(2)}, u32[]{:S(2)}) collective-permute-start(bf16[128,256]{1,0:T(8,128)(2,1)S(1)} %get-tuple-element.84.refs_2_), channel_id=1, source_target_pairs={{0,12},{1,13},{2,14},{3,15},{4,8},{5,9},{6,10},{7,11},{8,4},{9,5},... | collective-permute-start | bytes 196616 | tf_op jit(solution)/shard_map/ppermute | solution.py:226
  60.8 5.7 %collective-permute-start.20 = (bf16[384,256]{1,0:T(8,128)(2,1)S(1)}, bf16[384,256]{1,0:T(8,128)(2,1)S(1)}, u32[]{:S(2)}, u32[]{:S(2)}) collective-permute-start(bf16[384,256]{1,0:T(8,128)(2,1)S(1)} %shard_map.160.refs_2_.refs_0_), channel_id=1, source_target_pairs={{0,2},{1,5},{2,0},{3,7},{4,6},{5,1},{6,4},{7,3},{8,10},{9,13},{10,... | collective-permute-start | bytes 589832 | tf_op jit(solution)/shard_map/ppermute | solution.py:226
  62.3 6.3 %collective-permute-start.22 = (bf16[384,256]{1,0:T(8,128)(2,1)S(1)}, bf16[384,256]{1,0:T(8,128)(2,1)S(1)}, u32[]{:S(2)}, u32[]{:S(2)}) collective-permute-start(bf16[384,256]{1,0:T(8,128)(2,1)S(1)} %shard_map.161.refs_2_), channel_id=1, source_target_pairs={{0,2},{1,5},{2,0},{3,7},{4,6},{5,1},{6,4},{7,3},{8,10},{9,13},{10,... | collective-permute-start | bytes 589832 | tf_op jit(solution)/shard_map/ppermute | solution.py:226
  63.0 1.4 %collective-permute-start.8 = (bf16[320,256]{1,0:T(8,128)(2,1)S(1)}, bf16[320,256]{1,0:T(8,128)(2,1)S(1)}, u32[]{:S(2)}, u32[]{:S(2)}) collective-permute-start(bf16[320,256]{1,0:T(8,128)(2,1)S(1)} %get-tuple-element.72), channel_id=1, source_target_pairs={{0,1},{1,0},{2,3},{3,2},{4,5},{5,4},{6,7},{7,6},{8,9},{9,8},{10,11... | collective-permute-start | bytes 491528 | tf_op jit(solution)/shard_map/ppermute | solution.py:79
  63.0 1.5 %collective-permute-start.18 = (bf16[128,256]{1,0:T(8,128)(2,1)S(1)}, bf16[128,256]{1,0:T(8,128)(2,1)S(1)}, u32[]{:S(2)}, u32[]{:S(2)}) collective-permute-start(bf16[128,256]{1,0:T(8,128)(2,1)S(1)} %get-tuple-element.93.refs_2_), channel_id=1, source_target_pairs={{0,1},{1,0},{2,3},{3,2},{4,5},{5,4},{6,7},{7,6},{8,9},{9,8},{10,11... | collective-permute-start | bytes 196616 | tf_op jit(solution)/shard_map/ppermute | solution.py:79

commit v12 on v11

--- a/solution.py
+++ b/solution.py
@@ -305,7 +305,8 @@
 
 
 def obs_kernel(keep_ref, got_ref, w_ref, mine_ref, theirs_ref):
-    obs_hidden = (keep_ref[...].astype(F32) + got_ref[...].astype(F32)).astype(BF16)
+    got = got_ref[got_ref.shape[0] - keep_ref.shape[0] :, :]
+    obs_hidden = (keep_ref[...].astype(F32) + got.astype(F32)).astype(BF16)
     mine, theirs = other_half(w_ref)
     theirs_ref[...] = dot(obs_hidden, theirs, 1, 1).astype(BF16)
     mine_ref[...] = dot(obs_hidden, mine, 1, 1)
@@ -317,8 +318,20 @@
     split_half(total_ref, 0, total_ref.shape[0] - tail, step, tail, next_ref, send_ref)
 
 
+def add_with_rows_kernel(
+    step, tail, keep_ref, got_ref, rows_ref, rows_got_ref, next_ref, send_ref, rows_next_ref, total_ref, rows_total_ref
+):
+    share = next_ref.shape[0]
+    total_ref[...] = keep_ref[...] + got_ref[...].astype(F32)
+    split_half(total_ref, 0, share - tail, None, tail, next_ref, send_ref.at[:share])
+    rows_total_ref[...] = (rows_ref[...].astype(F32) + rows_got_ref[...].astype(F32)).astype(BF16)
+    split_half(
+        rows_total_ref, 0, rows_total_ref.shape[0], step, 0, rows_next_ref, send_ref.at[share:]
+    )
+
+
 def last_kernel(keep_ref, got_ref, piece_ref, *slot_refs):
-    total = keep_ref[...] + got_ref[...].astype(F32)
+    total = keep_ref[...] + got_ref[: keep_ref.shape[0], :].astype(F32)
     rows = piece_ref.shape[0]
     piece_ref[...] = total[:rows].astype(BF16)
     for slot_ref in slot_refs:
@@ -385,9 +398,30 @@
     return used
 
 
-def weight_chain(steps, rows, tail, slots, keep, got, after):
+def weight_chain(steps, rows, tail, slots, keep, got, after, returned=None):
     used = halving_used(steps, rows)
-    keep, got = yield from summing(steps, len(steps) - 1, tail, keep, got, after)
+    keep, got = yield from summing(steps[:-1], len(steps) - 1, tail, keep, got, after)
+    if returned:
+        rows_keep, rows_got = returned
+        shape = (half_rows(rows_keep.shape[0]), keep.shape[1])
+        keep, send, rows_keep = call(
+            functools.partial(add_with_rows_kernel, steps[-1], tail),
+            [(keep.shape, F32), ((keep.shape[0] + shape[0], shape[1]), BF16), (shape, BF16)],
+            keep, got, rows_keep, rows_got,
+            scratch=[pltpu.VMEM(keep.shape, F32), pltpu.VMEM(rows_keep.shape, BF16)],
+            after=after,
+        )
+    else:
+        keep, send = call(
+            functools.partial(add_kernel, None, tail),
+            [(keep.shape, F32), (keep.shape, BF16)],
+            keep, got,
+            scratch=[pltpu.VMEM(keep.shape, F32)],
+            after=after,
+        )
+    after[:] = [send]
+    arrived = got = flip(send, steps[-1])
+    yield
     piece, *sums = call(
         last_kernel,
         [((keep.shape[0] - tail, keep.shape[1]), BF16)]
@@ -408,29 +442,20 @@
         after[:] = [piece]
         got = flip(piece, following)
         yield
-    return [piece, got], sums
-
-
-def obs_chain(steps, w_obs, keep, got, after):
-    keep, got = yield from summing(steps, len(steps), 0, keep, got, after)
-    half = w_obs.shape[0] // 2
-    obs_mine, obs_theirs = call(
-        obs_kernel, [((keep.shape[0], half), F32), ((keep.shape[0], half), BF16)], keep, got, w_obs,
-        after=after,
-    )
-    after[:] = [obs_theirs]
-    obs_got = shift(obs_theirs, "mp", 1)
-    yield
-    return obs_mine, obs_got
+    return [piece, got], sums, (rows_keep, arrived) if returned else ()
+
+
+def rows_chain(steps, keep, got, after, out):
+    out += yield from summing(steps[:-1], len(steps), 0, keep, got, after)
 
 
 def in_turns(chains, turns):
     results = {}
-    for key in turns + [key for key in range(len(chains))]:
+    for key in turns + list(range(len(chains))):
         try:
             next(chains[key])
         except StopIteration as stop:
-            results[key] = stop.value
+            results.setdefault(key, stop.value)
     return [results[key] for key in range(len(chains))]
 
 
@@ -490,24 +515,29 @@
         scratch=[pltpu.VMEM((stack + tail, hidden), F32)],
     )
     after = []
+    returned = []
+    chains = [rows_chain(steps, obs_keep, obs_got, after, returned)]
     got = [flip(send, steps[0]) for send in shares[1::2]]
-    chains = [
-        weight_chain(
-            steps, rows, tail if i == bundles - 1 else 0, slots, shares[2 * i], got[i], after
-        )
-        for i in range(bundles)
-    ]
+    for i in range(bundles):
+        last = i == bundles - 1
+        chains.append(
+            weight_chain(
+                steps, rows, tail if last else 0, slots, shares[2 * i], got[i], after, returned if last else None
+            )
+        )
     node_got = shift(node_theirs, "mp", 1)
-    everyone = list(range(1, bundles + 1))
-    turns = ([0] + everyone) * (len(steps) - 1) + everyone + [0] + everyone * (len(halving_used(steps, rows)) - 1)
-    (obs_mine, obs_got), *weights = in_turns(
-        [obs_chain(steps, w_obs_held, obs_keep, obs_got, after)] + chains, turns
+    everyone = list(range(len(chains)))
+    turns = everyone * (len(steps) - 2) + [0] + everyone[1:] * (2 + len(halving_used(steps, rows)) - 1)
+    _, *weights = in_turns(chains, turns)
+    obs_keep, arrived = weights[-1][2]
+    obs_mine, obs_theirs = call(
+        obs_kernel, [((obs, half), F32), ((obs, half), BF16)], obs_keep, arrived, w_obs_held
     )
     grad_node, grad_obs = call(
         merge_kernel, [((nodes, half), F32), ((obs, half), BF16)],
-        node_mine, node_got, obs_mine, obs_got,
-    )
-    ends = [end for pair, _ in weights for end in pair]
+        node_mine, node_got, obs_mine, shift(obs_theirs, "mp", 1),
+    )
+    ends = [end for pair, *_ in weights for end in pair]
     (grad_slot,) = weights[-1][1]
     grad_w_node, grad_w_out, grad_w_obs = call(
         functools.partial(spread_kernel, steps[0], bundles),

time: 69.9 us -> 64.9 us (0.928)
  waiting for transfers between devices: 29 us -> 24.8 us
  starting transfers between devices: 30.8 us -> 29.9 us
    ppermute x13 -> x12, waiting for transfers between devices: 25.7 us -> 21.6 us  [flip(): return lax.ppermute(value, axes, pairs)]
    ppermute x13 -> x12, starting transfers between devices: 16.4 us -> 15.5 us  [flip(): return lax.ppermute(value, axes, pairs)]
    pallas_call x16 -> x15, Pallas kernels: 6.19 us -> 6.2 us  [call(): pl.pallas_call(lambda *refs: kernel(*refs[:count], *refs[len(args):]), ou...]
  transfers between devices with their start and end apart: 23 -> 22, of which waited for: 11 -> 11; matrix products, arithmetic and copies ran while one was open for 0% -> 0% of each run, Pallas kernels for 7% -> 8%
where the time goes in v12:
time: 64.9 us; the launch traced here: 64.7 us
  starting transfers between devices  29.9 us (46%)
  waiting for transfers between devices  24.8 us (38%)
  Pallas kernels  9.22 us (14%)
  between operations  0.8 us (1%)
    ppermute x12, waiting for transfers between devices, flip(): return lax.ppermute(value, axes, pairs)  21.6 us
    ppermute x12, starting transfers between devices, flip(): return lax.ppermute(value, axes, pairs)  15.5 us
    ppermute x10, starting transfers between devices, shift(): lax.ppermute(value, axis, [(i, (i + step) % size) for i in range(size)])  14.4 us
    pallas_call x15, Pallas kernels, call(): pl.pallas_call(lambda *refs: kernel(*refs[:count], *refs[len(args):]), ou...  6.2 us
    ppermute x10, waiting for transfers between devices, shift(): lax.ppermute(value, axis, [(i, (i + step) % size) for i in range(size)])  3.19 us
    pallas_call x2, Pallas kernels, call_staged(): pl.pallas_call(staged, out_shape=[jax.ShapeDtypeStruct(shape, dtype) for...  3.03 us
  transfers between devices with their start and end apart: 22, of which 11 were waited for; matrix products, arithmetic and copies ran while one was open for 0% of the time, Pallas kernels for 8%

profile of v12, /device:TPU:0, one launch (start us, length us, event | category | flops | bytes accessed | tf_op | source)
XLA Modules:
  0.0 64.7 jit_solution(4861229840172680492)
XLA Ops:
  0.6 1.3 %shard_map.145 = (bf16[144,128]{1,0:T(8,128)(2,1)S(1)}, bf16[144,128]{1,0:T(8,128)(2,1)S(1)}, bf16[144,128]{1,0:T(8,128)(2,1)S(1)}, bf16[144,128]{1,0:T(8,128)(2...) custom-call(bf16[128,512]{1,0:T(8,128)(2,1)} %refs_0_.2, ...), custom_call_target="tpu_custom_call" | custom-call | tf_op jit(solution)/shard_map/pallas_call | solution.py:61
  1.9 3.0 %collective-permute-start = (bf16[144,128]{1,0:T(8,128)(2,1)S(1)}, bf16[144,128]{1,0:T(8,128)(2,1)S(1)}, u32[]{:S(2)}, u32[]{:S(2)}) collective-permute-start(bf16[144,128]{1,0:T(8,128)(2,1)S(1)} %get-tuple-element.53), channel_id=1, source_target_pairs={{0,2},{2,4},{4,6},{6,8},{8,10},{10,12},{12,14},{14,0},{1,3},{3,5},... | collective-permute-start | bytes 110600 | tf_op jit(solution)/shard_map/ppermute | solution.py:79
  4.9 1.6 %collective-permute-start.1 = (bf16[144,128]{1,0:T(8,128)(2,1)S(1)}, bf16[144,128]{1,0:T(8,128)(2,1)S(1)}, u32[]{:S(2)}, u32[]{:S(2)}) collective-permute-start(bf16[144,128]{1,0:T(8,128)(2,1)S(1)} %get-tuple-element.54), channel_id=1, source_target_pairs={{0,4},{2,6},{4,8},{6,10},{8,12},{10,14},{12,0},{14,2},{1,5},{3,7},... | collective-permute-start | bytes 110600 | tf_op jit(solution)/shard_map/ppermute | solution.py:79
  6.5 2.6 %collective-permute-start.2 = (bf16[144,128]{1,0:T(8,128)(2,1)S(1)}, bf16[144,128]{1,0:T(8,128)(2,1)S(1)}, u32[]{:S(2)}, u32[]{:S(2)}) collective-permute-start(bf16[144,128]{1,0:T(8,128)(2,1)S(1)} %get-tuple-element.55), channel_id=1, source_target_pairs={{0,6},{2,8},{4,10},{6,12},{8,14},{10,0},{12,2},{14,4},{1,7},{3,9},... | collective-permute-start | bytes 110600 | tf_op jit(solution)/shard_map/ppermute | solution.py:79
  9.1 1.2 %collective-permute-start.3 = (bf16[144,128]{1,0:T(8,128)(2,1)S(1)}, bf16[144,128]{1,0:T(8,128)(2,1)S(1)}, u32[]{:S(2)}, u32[]{:S(2)}) collective-permute-start(bf16[144,128]{1,0:T(8,128)(2,1)S(1)} %get-tuple-element.56), channel_id=1, source_target_pairs={{0,8},{2,10},{4,12},{6,14},{8,0},{10,2},{12,4},{14,6},{1,9},{3,11}... | collective-permute-start | bytes 110600 | tf_op jit(solution)/shard_map/ppermute | solution.py:79
  10.3 2.6 %collective-permute-start.4 = (bf16[144,128]{1,0:T(8,128)(2,1)S(1)}, bf16[144,128]{1,0:T(8,128)(2,1)S(1)}, u32[]{:S(2)}, u32[]{:S(2)}) collective-permute-start(bf16[144,128]{1,0:T(8,128)(2,1)S(1)} %get-tuple-element.57), channel_id=1, source_target_pairs={{0,10},{2,12},{4,14},{6,0},{8,2},{10,4},{12,6},{14,8},{1,11},{3,13... | collective-permute-start | bytes 110600 | tf_op jit(solution)/shard_map/ppermute | solution.py:79
  12.9 1.4 %collective-permute-start.5 = (bf16[144,128]{1,0:T(8,128)(2,1)S(1)}, bf16[144,128]{1,0:T(8,128)(2,1)S(1)}, u32[]{:S(2)}, u32[]{:S(2)}) collective-permute-start(bf16[144,128]{1,0:T(8,128)(2,1)S(1)} %get-tuple-element.58), channel_id=1, source_target_pairs={{0,12},{2,14},{4,0},{6,2},{8,4},{10,6},{12,8},{14,10},{1,13},{3,15... | collective-permute-start | bytes 110600 | tf_op jit(solution)/shard_map/ppermute | solution.py:79
  14.3 1.4 %collective-permute-start.6 = (bf16[144,128]{1,0:T(8,128)(2,1)S(1)}, bf16[144,128]{1,0:T(8,128)(2,1)S(1)}, u32[]{:S(2)}, u32[]{:S(2)}) collective-permute-start(bf16[144,128]{1,0:T(8,128)(2,1)S(1)} %get-tuple-element.59), channel_id=1, source_target_pairs={{0,14},{2,0},{4,2},{6,4},{8,6},{10,8},{12,10},{14,12},{1,15},{3,1}... | collective-permute-start | bytes 110600 | tf_op jit(solution)/shard_map/ppermute | solution.py:79
  15.7 1.7 %shard_map.146 = (bf16[336,1024]{1,0:T(8,128)(2,1)S(1)}, bf16[320,512]{1,0:T(8,128)(2,1)S(1)}, bf16[320,512]{1,0:T(8,128)(2,1)S(1)}, bf16[512,256]{1,0:T(8,128)(2,1)S(1)}, bf16[512,256]{1,0:T(8,128)(2,1)S(1)}) custom-call(bf16[320,512]{1,0:T(8,128)(2,1)} %refs_0_.3, bf16[320,512]{1,0:T(8,128)(2,1)} %refs_1_.1, bf16[512,256]{1,0:T(8,128)(2,1)} %refs_2_.1, ...), custom_call_target="tpu_custom_call" | custom-call | tf_op jit(solution)/shard_map/pallas_call | solution.py:61
  17.4 0.0 collective-permute-done.2.refs_2_
  17.5 0.0 collective-permute-done.4.refs_4_
  17.5 0.0 collective-permute-done.5.refs_5_
  17.5 0.8 %collective-permute-done.6.refs_6_ = bf16[144,128]{1,0:T(8,128)(2,1)S(1)} collective-permute-done((bf16[144,128]{1,0:T(8,128)(2,1)S(1)}, bf16[144,128]{1,0:T(8,128)(2,1)S(1)}, u32[]{:S(2)}, u32[]{:S(2)}) %collective-permute-start.6) | collective-permute-done | bytes 36896 | tf_op jit(solution)/shard_map/ppermute | solution.py:79
  18.3 0.1 collective-permute-start.7
  18.3 1.5 %collective-permute-done.7.refs_3_ = bf16[7,144,128]{2,1,0:T(8,128)(2,1)S(1)} collective-permute-done((bf16[7,144,128]{2,1,0:T(8,128)(2,1)S(1)}, bf16[7,144,128]{2,1,0:T(8,128)(2,1)S(1)}, u32[]{:S(2)}, u32[]{:S(2)}) %collective-permute-start.7) | collective-permute-done | bytes 258080 | tf_op jit(solution)/shard_map/ppermute | solution.py:79
  19.9 1.6 %shard_map.148 = (bf16[512,512]{1,0:T(8,128)(2,1)S(1)}, bf16[512,336]{1,0:T(8,128)(2,1)S(1)}, bf16[512,256]{1,0:T(8,128)(2,1)S(1)}, bf16[512,256]{1,0:T(8,128)(2...) custom-call(bf16[144,128]{1,0:T(8,128)(2,1)S(1)} %get-tuple-element.52.refs_0_, ...), custom_call_target="tpu_custom_call" | custom-call | tf_op jit(solution)/shard_map/pallas_call | solution.py:32
  21.5 1.6 %collective-permute-start.11 = (bf16[512,256]{1,0:T(8,128)(2,1)S(1)}, bf16[512,256]{1,0:T(8,128)(2,1)S(1)}, u32[]{:S(2)}, u32[]{:S(2)}) collective-permute-start(bf16[512,256]{1,0:T(8,128)(2,1)S(1)} %get-tuple-element.77), channel_id=1, source_target_pairs={{0,2},{1,5},{2,0},{3,7},{4,6},{5,1},{6,4},{7,3},{8,10},{9,13},{10,... | collective-permute-start | bytes 786440 | tf_op jit(solution)/shard_map/ppermute | solution.py:226
  23.1 1.3 %shard_map.149 = (f32[320,256]{1,0:T(8,128)S(1)}, bf16[320,256]{1,0:T(8,128)(2,1)S(1)}, f32[384,256]{1,0:T(8,128)S(1)}, bf16[384,256]{1,0:T(8,128)(2,1)S(1)}, f3...) custom-call(bf16[512,336]{1,0:T(8,128)(2,1)S(1)} %get-tuple-element.63.refs_0_, ...), custom_call_target="tpu_custom_call" | custom-call | tf_op jit(solution)/shard_map/pallas_call | solution.py:32
  24.4 0.5 collective-permute-start.9
  24.9 1.5 %collective-permute-start.10 = (bf16[384,256]{1,0:T(8,128)(2,1)S(1)}, bf16[384,256]{1,0:T(8,128)(2,1)S(1)}, u32[]{:S(2)}, u32[]{:S(2)}) collective-permute-start(bf16[384,256]{1,0:T(8,128)(2,1)S(1)} %get-tuple-element.75), channel_id=1, source_target_pairs={{0,2},{1,5},{2,0},{3,7},{4,6},{5,1},{6,4},{7,3},{8,10},{9,13},{10,... | collective-permute-start | bytes 589832 | tf_op jit(solution)/shard_map/ppermute | solution.py:226
  26.5 1.5 %collective-permute-done.11.refs_1_ = bf16[512,256]{1,0:T(8,128)(2,1)S(1)} collective-permute-done((bf16[512,256]{1,0:T(8,128)(2,1)S(1)}, bf16[512,256]{1,0:T(8,128)(2,1)S(1)}, u32[]{:S(2)}, u32[]{:S(2)}) %collective-permute-start.11) | collective-permute-done | bytes 262176 | tf_op jit(solution)/shard_map/ppermute | solution.py:226
  27.9 0.1 shard_map.150
  28.1 0.7 %collective-permute-start.13 = (bf16[256,256]{1,0:T(8,128)(2,1)S(1)}, bf16[256,256]{1,0:T(8,128)(2,1)S(1)}, u32[]{:S(2)}, u32[]{:S(2)}) collective-permute-start(bf16[256,256]{1,0:T(8,128)(2,1)S(1)} %get-tuple-element.78.refs_2_), channel_id=1, source_target_pairs={{0,4},{1,3},{2,6},{3,1},{4,0},{5,7},{6,2},{7,5},{8,12},{9,11},{10,... | collective-permute-start | bytes 393224 | tf_op jit(solution)/shard_map/ppermute | solution.py:226
  28.8 4.9 %collective-permute-done.10.refs_1_ = bf16[384,256]{1,0:T(8,128)(2,1)S(1)} collective-permute-done((bf16[384,256]{1,0:T(8,128)(2,1)S(1)}, bf16[384,256]{1,0:T(8,128)(2,1)S(1)}, u32[]{:S(2)}, u32[]{:S(2)}) %collective-permute-start.10) | collective-permute-done | bytes 196640 | tf_op jit(solution)/shard_map/ppermute | solution.py:226
  33.7 0.1 shard_map.151
  33.8 0.0 collective-permute-done.9.refs_1_
  33.8 0.1 shard_map.152
  33.9 0.7 %collective-permute-start.12 = (bf16[208,256]{1,0:T(8,128)(2,1)S(1)}, bf16[208,256]{1,0:T(8,128)(2,1)S(1)}, u32[]{:S(2)}, u32[]{:S(2)}) collective-permute-start(bf16[208,256]{1,0:T(8,128)(2,1)S(1)} %get-tuple-element.81.refs_2_), channel_id=1, source_target_pairs={{0,4},{1,3},{2,6},{3,1},{4,0},{5,7},{6,2},{7,5},{8,12},{9,11},{10,... | collective-permute-start | bytes 319496 | tf_op jit(solution)/shard_map/ppermute | solution.py:226
  34.6 1.4 %collective-permute-start.14 = (bf16[192,256]{1,0:T(8,128)(2,1)S(1)}, bf16[192,256]{1,0:T(8,128)(2,1)S(1)}, u32[]{:S(2)}, u32[]{:S(2)}) collective-permute-start(bf16[192,256]{1,0:T(8,128)(2,1)S(1)} %get-tuple-element.79.refs_2_), channel_id=1, source_target_pairs={{0,4},{1,3},{2,6},{3,1},{4,0},{5,7},{6,2},{7,5},{8,12},{9,11},{10,... | collective-permute-start | bytes 294920 | tf_op jit(solution)/shard_map/ppermute | solution.py:226
  36.0 3.7 %collective-permute-done.14.refs_1_ = bf16[192,256]{1,0:T(8,128)(2,1)S(1)} collective-permute-done((bf16[192,256]{1,0:T(8,128)(2,1)S(1)}, bf16[192,256]{1,0:T(8,128)(2,1)S(1)}, u32[]{:S(2)}, u32[]{:S(2)}) %collective-permute-start.14) | collective-permute-done | bytes 98336 | tf_op jit(solution)/shard_map/ppermute | solution.py:226
  39.8 0.1 shard_map.154
  39.9 3.2 %collective-permute-start.15 = (bf16[336,256]{1,0:T(8,128)(2,1)S(1)}, bf16[336,256]{1,0:T(8,128)(2,1)S(1)}, u32[]{:S(2)}, u32[]{:S(2)}) collective-permute-start(bf16[336,256]{1,0:T(8,128)(2,1)S(1)} %get-tuple-element.86.refs_2_), channel_id=1, source_target_pairs={{0,12},{1,13},{2,14},{3,15},{4,8},{5,9},{6,10},{7,11},{8,4},{9,5},... | collective-permute-start | bytes 516104 | tf_op jit(solution)/shard_map/ppermute | solution.py:226
  43.1 0.7 %collective-permute-start.17 = (bf16[192,256]{1,0:T(8,128)(2,1)S(1)}, bf16[192,256]{1,0:T(8,128)(2,1)S(1)}, u32[]{:S(2)}, u32[]{:S(2)}) collective-permute-start(bf16[192,256]{1,0:T(8,128)(2,1)S(1)} %get-tuple-element.84.refs_4_), channel_id=1, source_target_pairs={{0,12},{1,13},{2,14},{3,15},{4,8},{5,9},{6,10},{7,11},{8,4},{9,5},... | collective-permute-start | bytes 294920 | tf_op jit(solution)/shard_map/ppermute | solution.py:226
  43.8 5.8 %collective-permute-done.17.refs_1_ = bf16[192,256]{1,0:T(8,128)(2,1)S(1)} collective-permute-done((bf16[192,256]{1,0:T(8,128)(2,1)S(1)}, bf16[192,256]{1,0:T(8,128)(2,1)S(1)}, u32[]{:S(2)}, u32[]{:S(2)}) %collective-permute-start.17) | collective-permute-done | bytes 98336 | tf_op jit(solution)/shard_map/ppermute | solution.py:226
  49.6 1.9 %collective-permute-start.18 = (bf16[192,256]{1,0:T(8,128)(2,1)S(1)}, bf16[192,256]{1,0:T(8,128)(2,1)S(1)}, u32[]{:S(2)}, u32[]{:S(2)}) collective-permute-start(bf16[192,256]{1,0:T(8,128)(2,1)S(1)} %shard_map.157.refs_2_.refs_0_), channel_id=1, source_target_pairs={{0,4},{1,3},{2,6},{3,1},{4,0},{5,7},{6,2},{7,5},{8,12},{9,11},{10,... | collective-permute-start | bytes 294920 | tf_op jit(solution)/shard_map/ppermute | solution.py:226
  51.5 0.6 shard_map.158
  52.2 0.2 collective-permute-start.20
  52.3 3.1 %collective-permute-done.18.refs_1_ = bf16[192,256]{1,0:T(8,128)(2,1)S(1)} collective-permute-done((bf16[192,256]{1,0:T(8,128)(2,1)S(1)}, bf16[192,256]{1,0:T(8,128)(2,1)S(1)}, u32[]{:S(2)}, u32[]{:S(2)}) %collective-permute-start.18) | collective-permute-done | bytes 98336 | tf_op jit(solution)/shard_map/ppermute | solution.py:226
  55.5 1.5 %collective-permute-start.19 = (bf16[384,256]{1,0:T(8,128)(2,1)S(1)}, bf16[384,256]{1,0:T(8,128)(2,1)S(1)}, u32[]{:S(2)}, u32[]{:S(2)}) collective-permute-start(bf16[384,256]{1,0:T(8,128)(2,1)S(1)} %shard_map.159.refs_2_.refs_0_), channel_id=1, source_target_pairs={{0,2},{1,5},{2,0},{3,7},{4,6},{5,1},{6,4},{7,3},{8,10},{9,13},{10,... | collective-permute-start | bytes 589832 | tf_op jit(solution)/shard_map/ppermute | solution.py:226
  57.0 0.8 %collective-permute-done.20.refs_1_ = bf16[192,256]{1,0:T(8,128)(2,1)S(1)} collective-permute-done((bf16[192,256]{1,0:T(8,128)(2,1)S(1)}, bf16[192,256]{1,0:T(8,128)(2,1)S(1)}, u32[]{:S(2)}, u32[]{:S(2)}) %collective-permute-start.20) | collective-permute-done | bytes 98336 | tf_op jit(solution)/shard_map/ppermute | solution.py:226
  57.8 1.5 %collective-permute-start.21 = (bf16[384,256]{1,0:T(8,128)(2,1)S(1)}, bf16[384,256]{1,0:T(8,128)(2,1)S(1)}, u32[]{:S(2)}, u32[]{:S(2)}) collective-permute-start(bf16[384,256]{1,0:T(8,128)(2,1)S(1)} %shard_map.160.refs_2_), channel_id=1, source_target_pairs={{0,2},{1,5},{2,0},{3,7},{4,6},{5,1},{6,4},{7,3},{8,10},{9,13},{10,... | collective-permute-start | bytes 589832 | tf_op jit(solution)/shard_map/ppermute | solution.py:226
  59.3 0.2 shard_map.155
  59.5 0.6 collective-permute-start.16
  60.1 0.6 collective-permute-done.8.refs_1_
  60.7 0.3 collective-permute-done.16.refs_3_
  61.0 0.8 %shard_map.156 = (f32[320,256]{1,0:T(8,128)}, bf16[128,256]{1,0:T(8,128)(2,1)}) custom-call(f32[320,256]{1,0:T(8,128)S(1)} %get-tuple-element.70.refs_0_, bf16[320,256]{1,0:T(8,128)(2,1)S(1)} %collective-permute-done.8.refs_1_, f32[128,256]{1,0:T(8,128)S(1)} %get-tuple-element.87.refs_2_, bf16[128,256]{1,0:T(8,128)(2,1)S(1)} %collective-permute-done.16.refs_3_), custom_call_target="tpu_custom_call" | custom-call | tf_op jit(solution)/shard_map/pallas_call | solution.py:32
  61.8 1.8 %collective-permute-done.21.refs_3_ = bf16[384,256]{1,0:T(8,128)(2,1)S(1)} collective-permute-done((bf16[384,256]{1,0:T(8,128)(2,1)S(1)}, bf16[384,256]{1,0:T(8,128)(2,1)S(1)}, u32[]{:S(2)}, u32[]{:S(2)}) %collective-permute-start.21) | collective-permute-done | bytes 196640 | tf_op jit(solution)/shard_map/ppermute | solution.py:226
  63.6 1.2 %shard_map.161 = (f32[512,256]{1,0:T(8,128)}, f32[256,512]{1,0:T(8,128)}, f32[512,256]{1,0:T(8,128)}) custom-call(bf16[384,256]{1,0:T(8,128)(2,1)S(1)} %shard_map.159.refs_2_.refs_0_, bf16[384,256]{1,0:T(8,128)(2,1)S(1)} %collective-permute-done.19.refs_1_, bf16[384,256]{1,0:T(8,128)(2,1)S(1)} %shard_map.160.refs_2_, ...), custom_call_target="tpu_custom_call" | custom-call | tf_op jit(solution)/shard_map/pallas_call | solution.py:32
  (13 shorter events, 0.1 us)
Async XLA Ops:
  1.9 11.0 %collective-permute-start = (bf16[144,128]{1,0:T(8,128)(2,1)S(1)}, bf16[144,128]{1,0:T(8,128)(2,1)S(1)}, u32[]{:S(2)}, u32[]{:S(2)}) collective-permute-start(bf16[144,128]{1,0:T(8,128)(2,1)S(1)} %get-tuple-element.53), channel_id=1, source_target_pairs={{0,2},{2,4},{4,6},{6,8},{8,10},{10,12},{12,14},{14,0},{1,3},{3,5},... | collective-permute-start | bytes 110600 | tf_op jit(solution)/shard_map/ppermute | solution.py:79
  4.9 9.3 %collective-permute-start.1 = (bf16[144,128]{1,0:T(8,128)(2,1)S(1)}, bf16[144,128]{1,0:T(8,128)(2,1)S(1)}, u32[]{:S(2)}, u32[]{:S(2)}) collective-permute-start(bf16[144,128]{1,0:T(8,128)(2,1)S(1)} %get-tuple-element.54), channel_id=1, source_target_pairs={{0,4},{2,6},{4,8},{6,10},{8,12},{10,14},{12,0},{14,2},{1,5},{3,7},... | collective-permute-start | bytes 110600 | tf_op jit(solution)/shard_map/ppermute | solution.py:79
  6.5 10.9 %collective-permute-start.2 = (bf16[144,128]{1,0:T(8,128)(2,1)S(1)}, bf16[144,128]{1,0:T(8,128)(2,1)S(1)}, u32[]{:S(2)}, u32[]{:S(2)}) collective-permute-start(bf16[144,128]{1,0:T(8,128)(2,1)S(1)} %get-tuple-element.55), channel_id=1, source_target_pairs={{0,6},{2,8},{4,10},{6,12},{8,14},{10,0},{12,2},{14,4},{1,7},{3,9},... | collective-permute-start | bytes 110600 | tf_op jit(solution)/shard_map/ppermute | solution.py:79
  9.1 8.4 %collective-permute-start.3 = (bf16[144,128]{1,0:T(8,128)(2,1)S(1)}, bf16[144,128]{1,0:T(8,128)(2,1)S(1)}, u32[]{:S(2)}, u32[]{:S(2)}) collective-permute-start(bf16[144,128]{1,0:T(8,128)(2,1)S(1)} %get-tuple-element.56), channel_id=1, source_target_pairs={{0,8},{2,10},{4,12},{6,14},{8,0},{10,2},{12,4},{14,6},{1,9},{3,11}... | collective-permute-start | bytes 110600 | tf_op jit(solution)/shard_map/ppermute | solution.py:79
  10.3 7.2 %collective-permute-start.4 = (bf16[144,128]{1,0:T(8,128)(2,1)S(1)}, bf16[144,128]{1,0:T(8,128)(2,1)S(1)}, u32[]{:S(2)}, u32[]{:S(2)}) collective-permute-start(bf16[144,128]{1,0:T(8,128)(2,1)S(1)} %get-tuple-element.57), channel_id=1, source_target_pairs={{0,10},{2,12},{4,14},{6,0},{8,2},{10,4},{12,6},{14,8},{1,11},{3,13... | collective-permute-start | bytes 110600 | tf_op jit(solution)/shard_map/ppermute | solution.py:79
  12.9 4.5 %collective-permute-start.5 = (bf16[144,128]{1,0:T(8,128)(2,1)S(1)}, bf16[144,128]{1,0:T(8,128)(2,1)S(1)}, u32[]{:S(2)}, u32[]{:S(2)}) collective-permute-start(bf16[144,128]{1,0:T(8,128)(2,1)S(1)} %get-tuple-element.58), channel_id=1, source_target_pairs={{0,12},{2,14},{4,0},{6,2},{8,4},{10,6},{12,8},{14,10},{1,13},{3,15... | collective-permute-start | bytes 110600 | tf_op jit(solution)/shard_map/ppermute | solution.py:79
  14.3 4.0 %collective-permute-start.6 = (bf16[144,128]{1,0:T(8,128)(2,1)S(1)}, bf16[144,128]{1,0:T(8,128)(2,1)S(1)}, u32[]{:S(2)}, u32[]{:S(2)}) collective-permute-start(bf16[144,128]{1,0:T(8,128)(2,1)S(1)} %get-tuple-element.59), channel_id=1, source_target_pairs={{0,14},{2,0},{4,2},{6,4},{8,6},{10,8},{12,10},{14,12},{1,15},{3,1}... | collective-permute-start | bytes 110600 | tf_op jit(solution)/shard_map/ppermute | solution.py:79
  18.3 1.6 %collective-permute-start.7 = (bf16[7,144,128]{2,1,0:T(8,128)(2,1)S(1)}, bf16[7,144,128]{2,1,0:T(8,128)(2,1)S(1)}, u32[]{:S(2)}, u32[]{:S(2)}) collective-permute-start(bf16[7,144,128]{2,1,0:T(8,128)(2,1)S(1)} %shard_map.147.refs_1_), channel_id=1, source_target_pairs={{0,1},{1,0},{2,3},{3,2},{4,5},{5,4},{6,7},{7,6},{8,9},{9,8},{10,11... | collective-permute-start | bytes 774152 | tf_op jit(solution)/shard_map/ppermute | solution.py:79
  21.5 6.4 %collective-permute-start.11 = (bf16[512,256]{1,0:T(8,128)(2,1)S(1)}, bf16[512,256]{1,0:T(8,128)(2,1)S(1)}, u32[]{:S(2)}, u32[]{:S(2)}) collective-permute-start(bf16[512,256]{1,0:T(8,128)(2,1)S(1)} %get-tuple-element.77), channel_id=1, source_target_pairs={{0,2},{1,5},{2,0},{3,7},{4,6},{5,1},{6,4},{7,3},{8,10},{9,13},{10,... | collective-permute-start | bytes 786440 | tf_op jit(solution)/shard_map/ppermute | solution.py:226
  24.4 9.4 %collective-permute-start.9 = (bf16[400,256]{1,0:T(8,128)(2,1)S(1)}, bf16[400,256]{1,0:T(8,128)(2,1)S(1)}, u32[]{:S(2)}, u32[]{:S(2)}) collective-permute-start(bf16[400,256]{1,0:T(8,128)(2,1)S(1)} %get-tuple-element.73), channel_id=1, source_target_pairs={{0,2},{1,5},{2,0},{3,7},{4,6},{5,1},{6,4},{7,3},{8,10},{9,13},{10,... | collective-permute-start | bytes 614408 | tf_op jit(solution)/shard_map/ppermute | solution.py:226
  24.9 8.8 %collective-permute-start.10 = (bf16[384,256]{1,0:T(8,128)(2,1)S(1)}, bf16[384,256]{1,0:T(8,128)(2,1)S(1)}, u32[]{:S(2)}, u32[]{:S(2)}) collective-permute-start(bf16[384,256]{1,0:T(8,128)(2,1)S(1)} %get-tuple-element.75), channel_id=1, source_target_pairs={{0,2},{1,5},{2,0},{3,7},{4,6},{5,1},{6,4},{7,3},{8,10},{9,13},{10,... | collective-permute-start | bytes 589832 | tf_op jit(solution)/shard_map/ppermute | solution.py:226
  28.1 11.7 %collective-permute-start.13 = (bf16[256,256]{1,0:T(8,128)(2,1)S(1)}, bf16[256,256]{1,0:T(8,128)(2,1)S(1)}, u32[]{:S(2)}, u32[]{:S(2)}) collective-permute-start(bf16[256,256]{1,0:T(8,128)(2,1)S(1)} %get-tuple-element.78.refs_2_), channel_id=1, source_target_pairs={{0,4},{1,3},{2,6},{3,1},{4,0},{5,7},{6,2},{7,5},{8,12},{9,11},{10,... | collective-permute-start | bytes 393224 | tf_op jit(solution)/shard_map/ppermute | solution.py:226
  33.9 5.9 %collective-permute-start.12 = (bf16[208,256]{1,0:T(8,128)(2,1)S(1)}, bf16[208,256]{1,0:T(8,128)(2,1)S(1)}, u32[]{:S(2)}, u32[]{:S(2)}) collective-permute-start(bf16[208,256]{1,0:T(8,128)(2,1)S(1)} %get-tuple-element.81.refs_2_), channel_id=1, source_target_pairs={{0,4},{1,3},{2,6},{3,1},{4,0},{5,7},{6,2},{7,5},{8,12},{9,11},{10,... | collective-permute-start | bytes 319496 | tf_op jit(solution)/shard_map/ppermute | solution.py:226
  34.6 5.2 %collective-permute-start.14 = (bf16[192,256]{1,0:T(8,128)(2,1)S(1)}, bf16[192,256]{1,0:T(8,128)(2,1)S(1)}, u32[]{:S(2)}, u32[]{:S(2)}) collective-permute-start(bf16[192,256]{1,0:T(8,128)(2,1)S(1)} %get-tuple-element.79.refs_2_), channel_id=1, source_target_pairs={{0,4},{1,3},{2,6},{3,1},{4,0},{5,7},{6,2},{7,5},{8,12},{9,11},{10,... | collective-permute-start | bytes 294920 | tf_op jit(solution)/shard_map/ppermute | solution.py:226
  39.9 11.7 %collective-permute-start.15 = (bf16[336,256]{1,0:T(8,128)(2,1)S(1)}, bf16[336,256]{1,0:T(8,128)(2,1)S(1)}, u32[]{:S(2)}, u32[]{:S(2)}) collective-permute-start(bf16[336,256]{1,0:T(8,128)(2,1)S(1)} %get-tuple-element.86.refs_2_), channel_id=1, source_target_pairs={{0,12},{1,13},{2,14},{3,15},{4,8},{5,9},{6,10},{7,11},{8,4},{9,5},... | collective-permute-start | bytes 516104 | tf_op jit(solution)/shard_map/ppermute | solution.py:226
  43.1 6.5 %collective-permute-start.17 = (bf16[192,256]{1,0:T(8,128)(2,1)S(1)}, bf16[192,256]{1,0:T(8,128)(2,1)S(1)}, u32[]{:S(2)}, u32[]{:S(2)}) collective-permute-start(bf16[192,256]{1,0:T(8,128)(2,1)S(1)} %get-tuple-element.84.refs_4_), channel_id=1, source_target_pairs={{0,12},{1,13},{2,14},{3,15},{4,8},{5,9},{6,10},{7,11},{8,4},{9,5},... | collective-permute-start | bytes 294920 | tf_op jit(solution)/shard_map/ppermute | solution.py:226
  49.6 5.8 %collective-permute-start.18 = (bf16[192,256]{1,0:T(8,128)(2,1)S(1)}, bf16[192,256]{1,0:T(8,128)(2,1)S(1)}, u32[]{:S(2)}, u32[]{:S(2)}) collective-permute-start(bf16[192,256]{1,0:T(8,128)(2,1)S(1)} %shard_map.157.refs_2_.refs_0_), channel_id=1, source_target_pairs={{0,4},{1,3},{2,6},{3,1},{4,0},{5,7},{6,2},{7,5},{8,12},{9,11},{10,... | collective-permute-start | bytes 294920 | tf_op jit(solution)/shard_map/ppermute | solution.py:226
  52.2 5.6 %collective-permute-start.20 = (bf16[192,256]{1,0:T(8,128)(2,1)S(1)}, bf16[192,256]{1,0:T(8,128)(2,1)S(1)}, u32[]{:S(2)}, u32[]{:S(2)}) collective-permute-start(bf16[192,256]{1,0:T(8,128)(2,1)S(1)} %get-tuple-element.93.refs_2_.refs_0_), channel_id=1, source_target_pairs={{0,4},{1,3},{2,6},{3,1},{4,0},{5,7},{6,2},{7,5},{8,12},{9,11},{10,... | collective-permute-start | bytes 294920 | tf_op jit(solution)/shard_map/ppermute | solution.py:226
  55.5 6.3 %collective-permute-start.19 = (bf16[384,256]{1,0:T(8,128)(2,1)S(1)}, bf16[384,256]{1,0:T(8,128)(2,1)S(1)}, u32[]{:S(2)}, u32[]{:S(2)}) collective-permute-start(bf16[384,256]{1,0:T(8,128)(2,1)S(1)} %shard_map.159.refs_2_.refs_0_), channel_id=1, source_target_pairs={{0,2},{1,5},{2,0},{3,7},{4,6},{5,1},{6,4},{7,3},{8,10},{9,13},{10,... | collective-permute-start | bytes 589832 | tf_op jit(solution)/shard_map/ppermute | solution.py:226
  57.8 5.7 %collective-permute-start.21 = (bf16[384,256]{1,0:T(8,128)(2,1)S(1)}, bf16[384,256]{1,0:T(8,128)(2,1)S(1)}, u32[]{:S(2)}, u32[]{:S(2)}) collective-permute-start(bf16[384,256]{1,0:T(8,128)(2,1)S(1)} %shard_map.160.refs_2_), channel_id=1, source_target_pairs={{0,2},{1,5},{2,0},{3,7},{4,6},{5,1},{6,4},{7,3},{8,10},{9,13},{10,... | collective-permute-start | bytes 589832 | tf_op jit(solution)/shard_map/ppermute | solution.py:226
  59.3 1.4 %collective-permute-start.8 = (bf16[320,256]{1,0:T(8,128)(2,1)S(1)}, bf16[320,256]{1,0:T(8,128)(2,1)S(1)}, u32[]{:S(2)}, u32[]{:S(2)}) collective-permute-start(bf16[320,256]{1,0:T(8,128)(2,1)S(1)} %get-tuple-element.71), channel_id=1, source_target_pairs={{0,1},{1,0},{2,3},{3,2},{4,5},{5,4},{6,7},{7,6},{8,9},{9,8},{10,11... | collective-permute-start | bytes 491528 | tf_op jit(solution)/shard_map/ppermute | solution.py:79
  59.5 1.5 %collective-permute-start.16 = (bf16[128,256]{1,0:T(8,128)(2,1)S(1)}, bf16[128,256]{1,0:T(8,128)(2,1)S(1)}, u32[]{:S(2)}, u32[]{:S(2)}) collective-permute-start(bf16[128,256]{1,0:T(8,128)(2,1)S(1)} %get-tuple-element.88), channel_id=1, source_target_pairs={{0,1},{1,0},{2,3},{3,2},{4,5},{5,4},{6,7},{7,6},{8,9},{9,8},{10,11... | collective-permute-start | bytes 196616 | tf_op jit(solution)/shard_map/ppermute | solution.py:79

commit v13 on v12

--- a/solution.py
+++ b/solution.py
@@ -152,7 +152,7 @@
 
 def edge_kernel(
     fanout, nodes, steps, own_ref, mine_ref, other_ref, theirs_ref, table_ref, w_obs_ref,
-    act_ref, hot_ref, rows_mine_ref, rows_theirs_ref, keep_ref, send_ref, total_ref,
+    act_ref, hot_ref, rows_mine_ref, rows_theirs_ref, keep_ref, send_ref, pick_ref, total_ref, packed_ref, picks_ref,
 ):
     owners = mine_ref.shape[0] + 1
     chunk, lanes = own_ref.shape
@@ -161,21 +161,28 @@
     cap = (chunk - SUBLANES) * lanes // half
     me = lax.axis_index(OWNER_AXES)
     base = 1 << nodes.bit_length()
+    partner = partner_of(steps[0]).astype(F32)
     columns = []
     picks = []
+    places = []
     for j in range(owners):
         block, other = (mine_ref.at[j - 1], theirs_ref.at[j - 1]) if j else (own_ref, other_ref)
         header = block[chunk - SUBLANES :, :].astype(F32)
         slot = header[4 * fanout : 4 * fanout + 1] * base
         code = jnp.zeros((cap, lanes), F32)
-        pick = jnp.zeros((cap, lanes), jnp.bool_)
+        pick = partner_pick = jnp.zeros((cap, lanes), jnp.bool_)
         for k in range(fanout):
             row = header[4 * k : 4 * k + 4]
             rank = jnp.where(row[0:1] == me.astype(F32), row[1:2], -1.0).astype(jnp.int32)
             hit = iota((cap, lanes), 0) == rank
             pick = pick | hit
+            rank = jnp.where(row[0:1] == partner, row[1:2], -1.0).astype(jnp.int32)
+            partner_pick = partner_pick | (iota((cap, lanes), 0) == rank)
             code = code + jnp.where(hit, row[2:3] * 16.0 + row[3:4] + slot, 0.0)
         picks.append(pick.astype(BF16))
+        places.append(place_of(lax.rem(me - j + owners, owners), steps))
+        begin = pl.multiple_of(places[j] * cap, SUBLANES)
+        picks_ref[pl.ds(begin, cap), :] = partner_pick.astype(BF16)
         columns.append(jnp.sum(code, axis=1, keepdims=True).astype(jnp.int32))
         for c in range(half // lanes):
             rows = slice(j * cap, (j + 1) * cap)
@@ -197,10 +204,16 @@
     act_ref[:, :hidden] = g_a
     act_ref[:, hidden:] = (pre * sig).astype(BF16)
     for j, pick in enumerate(picks):
-        source = lax.rem(me - j + owners, owners)
-        begin = pl.multiple_of(place_of(source, steps) * lanes, SUBLANES)
-        total_ref[pl.ds(begin, lanes), :] = dot(pick, g_a[j * cap : (j + 1) * cap], 0, 0).astype(BF16)
-    split_half(total_ref, 0, owners * lanes, steps[0], 0, keep_ref, send_ref)
+        rows = g_a[j * cap : (j + 1) * cap]
+        begin = pl.multiple_of(places[j] * lanes, SUBLANES)
+        total_ref[pl.ds(begin, lanes), :] = dot(pick, rows, 0, 0).astype(BF16)
+        packed_ref[pl.ds(pl.multiple_of(places[j] * cap, SUBLANES), cap), :] = rows
+    bit = own_bit(steps[0])
+    for out_ref, ref, which in (
+        (keep_ref, total_ref, bit), (send_ref, packed_ref, 1 - bit), (pick_ref, picks_ref, bit)
+    ):
+        count = out_ref.shape[0]
+        out_ref[...] = ref[pl.ds(pl.multiple_of(which * count, SUBLANES), count), :]
 
 
 def halving_steps():
@@ -234,6 +247,15 @@
 
 def own_bit(step):
     return bit_of(step, lax.axis_index("node"), lax.axis_index("obs"))
+
+
+def partner_of(step):
+    node, obs, shares = lax.axis_index("node"), lax.axis_index("obs"), lax.axis_size("node")
+    owners = []
+    for axis, k in step:
+        mask = (2 << k) - 1
+        owners.append(obs * shares + (node ^ mask) if axis == "node" else (obs ^ mask) * shares + node)
+    return jnp.where(lax.axis_index("mp") % 2 == 0, owners[0], owners[1])
 
 
 def place_of(owner, steps):
@@ -318,6 +340,17 @@
     split_half(total_ref, 0, total_ref.shape[0] - tail, step, tail, next_ref, send_ref)
 
 
+def unpack_kernel(step, keep_ref, got_ref, pick_ref, next_ref, send_ref, total_ref):
+    obs = pick_ref.shape[1]
+    blocks = keep_ref.shape[0] // obs
+    cap = got_ref.shape[0] // blocks
+    for i in range(blocks):
+        edges, rows = slice(i * cap, (i + 1) * cap), slice(i * obs, (i + 1) * obs)
+        total = keep_ref[rows, :].astype(F32) + dot(pick_ref[edges, :], got_ref[edges, :], 0, 0)
+        total_ref[rows, :] = total.astype(BF16)
+    split_half(total_ref, 0, total_ref.shape[0], step, 0, next_ref, send_ref)
+
+
 def add_with_rows_kernel(
     step, tail, keep_ref, got_ref, rows_ref, rows_got_ref, next_ref, send_ref, rows_next_ref, total_ref, rows_total_ref
 ):
@@ -365,7 +398,10 @@
                 at, begin = at + count, begin + count
 
 
-def merge_kernel(node_ref, node_got_ref, obs_ref, obs_got_ref, grad_node_ref, grad_obs_ref):
+def merge_kernel(
+    node_ref, node_got_ref, obs_ref, obs_got_ref, slot_ref, grad_node_ref, grad_obs_ref, grad_slot_ref
+):
+    grad_slot_ref[...] = slot_ref[...]
     grad_node_ref[...] = node_ref[...] + node_got_ref[...].astype(F32)
     grad_obs_ref[...] = (obs_ref[...] + obs_got_ref[...].astype(F32)).astype(BF16)
 
@@ -445,8 +481,19 @@
     return [piece, got], sums, (rows_keep, arrived) if returned else ()
 
 
-def rows_chain(steps, keep, got, after, out):
-    out += yield from summing(steps[:-1], len(steps), 0, keep, got, after)
+def rows_chain(steps, keep, got, pick, after, out):
+    shape = (half_rows(keep.shape[0]), keep.shape[1])
+    keep, send = call(
+        functools.partial(unpack_kernel, steps[1]),
+        [(shape, BF16)] * 2,
+        keep, got, pick,
+        scratch=[pltpu.VMEM(keep.shape, BF16)],
+        after=after,
+    )
+    after[:] = [send]
+    got = flip(send, steps[1])
+    yield
+    out += yield from summing(steps[1:-1], len(steps), 0, keep, got, after)
 
 
 def in_turns(chains, turns):
@@ -491,13 +538,17 @@
         after=(w_obs_held,),
     )
     theirs = shift(mine, "mp", 1)
-    act, hot, rows_mine, rows_theirs, obs_keep, obs_send = call(
+    act, hot, rows_mine, rows_theirs, obs_keep, obs_send, obs_pick = call(
         functools.partial(edge_kernel, fanout, nodes, steps),
         [((edges, 2 * hidden), BF16), ((edges, nodes + tail), BF16)]
         + [((edges, half), BF16)] * 2
-        + [((owners * obs // 2, hidden), BF16)] * 2,
+        + [((owners * obs // 2, hidden), BF16), ((edges // 2, hidden), BF16), ((edges // 2, obs), BF16)],
         packed[0], mine, other, theirs, table, w_obs_held,
-        scratch=[pltpu.VMEM((owners * obs, hidden), BF16)],
+        scratch=[
+            pltpu.VMEM((owners * obs, hidden), BF16),
+            pltpu.VMEM((edges, hidden), BF16),
+            pltpu.VMEM((edges, obs), BF16),
+        ],
     )
 
     stack = 2 * width + width // hidden * hidden
@@ -516,7 +567,7 @@
     )
     after = []
     returned = []
-    chains = [rows_chain(steps, obs_keep, obs_got, after, returned)]
+    chains = [rows_chain(steps, obs_keep, obs_got, obs_pick, after, returned)]
     got = [flip(send, steps[0]) for send in shares[1::2]]
     for i in range(bundles):
         last = i == bundles - 1
@@ -533,12 +584,12 @@
     obs_mine, obs_theirs = call(
         obs_kernel, [((obs, half), F32), ((obs, half), BF16)], obs_keep, arrived, w_obs_held
     )
-    grad_node, grad_obs = call(
-        merge_kernel, [((nodes, half), F32), ((obs, half), BF16)],
-        node_mine, node_got, obs_mine, shift(obs_theirs, "mp", 1),
+    (slot_sums,) = weights[-1][1]
+    grad_node, grad_obs, grad_slot = call(
+        merge_kernel, [((nodes, half), F32), ((obs, half), BF16), ((slots, hidden), F32)],
+        node_mine, node_got, obs_mine, shift(obs_theirs, "mp", 1), slot_sums,
     )
     ends = [end for pair, *_ in weights for end in pair]
-    (grad_slot,) = weights[-1][1]
     grad_w_node, grad_w_out, grad_w_obs = call(
         functools.partial(spread_kernel, steps[0], bundles),
         [((width, hidden), F32), ((hidden, width), F32), ((width, hidden), F32)],

time: 64.9 us -> 66.2 us (1.020)
  starting transfers between devices: 29.9 us -> 31.5 us
    ppermute x12, starting transfers between devices: 15.5 us -> 17.1 us  [flip(): return lax.ppermute(value, axes, pairs)]
  transfers between devices with their start and end apart: 22 -> 22, of which waited for: 11 -> 10; matrix products, arithmetic and copies ran while one was open for 0% -> 0% of each run, Pallas kernels for 8% -> 5%
where the time goes in v13:
time: 66.2 us; the launch traced here: 66 us
  starting transfers between devices  31.5 us (48%)
  waiting for transfers between devices  24.8 us (37%)
  Pallas kernels  8.85 us (13%)
  between operations  0.8 us (1%)
    ppermute x12, waiting for transfers between devices, flip(): return lax.ppermute(value, axes, pairs)  21.6 us
    ppermute x12, starting transfers between devices, flip(): return lax.ppermute(value, axes, pairs)  17.1 us
    ppermute x10, starting transfers between devices, shift(): lax.ppermute(value, axis, [(i, (i + step) % size) for i in range(size)])  14.4 us
    pallas_call x15, Pallas kernels, call(): pl.pallas_call(lambda *refs: kernel(*refs[:count], *refs[len(args):]), ou...  5.83 us
    ppermute x10, waiting for transfers between devices, shift(): lax.ppermute(value, axis, [(i, (i + step) % size) for i in range(size)])  3.19 us
    pallas_call x2, Pallas kernels, call_staged(): pl.pallas_call(staged, out_shape=[jax.ShapeDtypeStruct(shape, dtype) for...  3.03 us
  transfers between devices with their start and end apart: 22, of which 10 were waited for; matrix products, arithmetic and copies ran while one was open for 0% of the time, Pallas kernels for 5%

profile of v13, /device:TPU:0, one launch (start us, length us, event | category | flops | bytes accessed | tf_op | source)
XLA Modules:
  0.0 66.0 jit_solution(15077097233523849755)
XLA Ops:
  0.6 1.3 %shard_map.145 = (bf16[144,128]{1,0:T(8,128)(2,1)S(1)}, bf16[144,128]{1,0:T(8,128)(2,1)S(1)}, bf16[144,128]{1,0:T(8,128)(2,1)S(1)}, bf16[144,128]{1,0:T(8,128)(2...) custom-call(bf16[128,512]{1,0:T(8,128)(2,1)} %refs_0_.2, ...), custom_call_target="tpu_custom_call" | custom-call | tf_op jit(solution)/shard_map/pallas_call | solution.py:61
  1.9 3.0 %collective-permute-start = (bf16[144,128]{1,0:T(8,128)(2,1)S(1)}, bf16[144,128]{1,0:T(8,128)(2,1)S(1)}, u32[]{:S(2)}, u32[]{:S(2)}) collective-permute-start(bf16[144,128]{1,0:T(8,128)(2,1)S(1)} %get-tuple-element.55), channel_id=1, source_target_pairs={{0,2},{2,4},{4,6},{6,8},{8,10},{10,12},{12,14},{14,0},{1,3},{3,5},... | collective-permute-start | bytes 110600 | tf_op jit(solution)/shard_map/ppermute | solution.py:79
  4.9 1.6 %collective-permute-start.1 = (bf16[144,128]{1,0:T(8,128)(2,1)S(1)}, bf16[144,128]{1,0:T(8,128)(2,1)S(1)}, u32[]{:S(2)}, u32[]{:S(2)}) collective-permute-start(bf16[144,128]{1,0:T(8,128)(2,1)S(1)} %get-tuple-element.56), channel_id=1, source_target_pairs={{0,4},{2,6},{4,8},{6,10},{8,12},{10,14},{12,0},{14,2},{1,5},{3,7},... | collective-permute-start | bytes 110600 | tf_op jit(solution)/shard_map/ppermute | solution.py:79
  6.5 2.6 %collective-permute-start.2 = (bf16[144,128]{1,0:T(8,128)(2,1)S(1)}, bf16[144,128]{1,0:T(8,128)(2,1)S(1)}, u32[]{:S(2)}, u32[]{:S(2)}) collective-permute-start(bf16[144,128]{1,0:T(8,128)(2,1)S(1)} %get-tuple-element.57), channel_id=1, source_target_pairs={{0,6},{2,8},{4,10},{6,12},{8,14},{10,0},{12,2},{14,4},{1,7},{3,9},... | collective-permute-start | bytes 110600 | tf_op jit(solution)/shard_map/ppermute | solution.py:79
  9.1 1.2 %collective-permute-start.3 = (bf16[144,128]{1,0:T(8,128)(2,1)S(1)}, bf16[144,128]{1,0:T(8,128)(2,1)S(1)}, u32[]{:S(2)}, u32[]{:S(2)}) collective-permute-start(bf16[144,128]{1,0:T(8,128)(2,1)S(1)} %get-tuple-element.58), channel_id=1, source_target_pairs={{0,8},{2,10},{4,12},{6,14},{8,0},{10,2},{12,4},{14,6},{1,9},{3,11}... | collective-permute-start | bytes 110600 | tf_op jit(solution)/shard_map/ppermute | solution.py:79
  10.3 2.6 %collective-permute-start.4 = (bf16[144,128]{1,0:T(8,128)(2,1)S(1)}, bf16[144,128]{1,0:T(8,128)(2,1)S(1)}, u32[]{:S(2)}, u32[]{:S(2)}) collective-permute-start(bf16[144,128]{1,0:T(8,128)(2,1)S(1)} %get-tuple-element.59), channel_id=1, source_target_pairs={{0,10},{2,12},{4,14},{6,0},{8,2},{10,4},{12,6},{14,8},{1,11},{3,13... | collective-permute-start | bytes 110600 | tf_op jit(solution)/shard_map/ppermute | solution.py:79
  12.9 0.0 collective-permute-done.refs_0_
  12.9 1.4 %collective-permute-start.5 = (bf16[144,128]{1,0:T(8,128)(2,1)S(1)}, bf16[144,128]{1,0:T(8,128)(2,1)S(1)}, u32[]{:S(2)}, u32[]{:S(2)}) collective-permute-start(bf16[144,128]{1,0:T(8,128)(2,1)S(1)} %get-tuple-element.60), channel_id=1, source_target_pairs={{0,12},{2,14},{4,0},{6,2},{8,4},{10,6},{12,8},{14,10},{1,13},{3,15... | collective-permute-start | bytes 110600 | tf_op jit(solution)/shard_map/ppermute | solution.py:79
  14.3 0.0 collective-permute-done.1.refs_1_
  14.3 1.4 %collective-permute-start.6 = (bf16[144,128]{1,0:T(8,128)(2,1)S(1)}, bf16[144,128]{1,0:T(8,128)(2,1)S(1)}, u32[]{:S(2)}, u32[]{:S(2)}) collective-permute-start(bf16[144,128]{1,0:T(8,128)(2,1)S(1)} %get-tuple-element.61), channel_id=1, source_target_pairs={{0,14},{2,0},{4,2},{6,4},{8,6},{10,8},{12,10},{14,12},{1,15},{3,1}... | collective-permute-start | bytes 110600 | tf_op jit(solution)/shard_map/ppermute | solution.py:79
  15.7 1.7 %shard_map.146 = (bf16[336,1024]{1,0:T(8,128)(2,1)S(1)}, bf16[320,512]{1,0:T(8,128)(2,1)S(1)}, bf16[320,512]{1,0:T(8,128)(2,1)S(1)}, bf16[512,256]{1,0:T(8,128)(2,1)S(1)}, bf16[512,256]{1,0:T(8,128)(2,1)S(1)}) custom-call(bf16[320,512]{1,0:T(8,128)(2,1)} %refs_0_.3, bf16[320,512]{1,0:T(8,128)(2,1)} %refs_1_.1, bf16[512,256]{1,0:T(8,128)(2,1)} %refs_2_.1, ...), custom_call_target="tpu_custom_call" | custom-call | tf_op jit(solution)/shard_map/pallas_call | solution.py:61
  17.5 0.0 collective-permute-done.3.refs_3_
  17.5 0.0 collective-permute-done.4.refs_4_
  17.5 0.8 %collective-permute-done.6.refs_6_ = bf16[144,128]{1,0:T(8,128)(2,1)S(1)} collective-permute-done((bf16[144,128]{1,0:T(8,128)(2,1)S(1)}, bf16[144,128]{1,0:T(8,128)(2,1)S(1)}, u32[]{:S(2)}, u32[]{:S(2)}) %collective-permute-start.6) | collective-permute-done | bytes 36896 | tf_op jit(solution)/shard_map/ppermute | solution.py:79
  18.3 0.1 collective-permute-start.7
  18.3 1.5 %collective-permute-done.7.refs_3_ = bf16[7,144,128]{2,1,0:T(8,128)(2,1)S(1)} collective-permute-done((bf16[7,144,128]{2,1,0:T(8,128)(2,1)S(1)}, bf16[7,144,128]{2,1,0:T(8,128)(2,1)S(1)}, u32[]{:S(2)}, u32[]{:S(2)}) %collective-permute-start.7) | collective-permute-done | bytes 258080 | tf_op jit(solution)/shard_map/ppermute | solution.py:79
  19.9 1.6 %shard_map.148 = (bf16[512,512]{1,0:T(8,128)(2,1)S(1)}, bf16[512,336]{1,0:T(8,128)(2,1)S(1)}, bf16[512,256]{1,0:T(8,128)(2,1)S(1)}, bf16[512,256]{1,0:T(8,128)(2...) custom-call(bf16[144,128]{1,0:T(8,128)(2,1)S(1)} %get-tuple-element.54.refs_0_, ...), custom_call_target="tpu_custom_call" | custom-call | tf_op jit(solution)/shard_map/pallas_call | solution.py:32
  21.5 1.3 %shard_map.149 = (f32[320,256]{1,0:T(8,128)S(1)}, bf16[320,256]{1,0:T(8,128)(2,1)S(1)}, f32[384,256]{1,0:T(8,128)S(1)}, bf16[384,256]{1,0:T(8,128)(2,1)S(1)}, f3...) custom-call(bf16[512,336]{1,0:T(8,128)(2,1)S(1)} %get-tuple-element.65.refs_0_, ...), custom_call_target="tpu_custom_call" | custom-call | tf_op jit(solution)/shard_map/pallas_call | solution.py:32
  22.8 1.6 %collective-permute-start.9 = (bf16[400,256]{1,0:T(8,128)(2,1)S(1)}, bf16[400,256]{1,0:T(8,128)(2,1)S(1)}, u32[]{:S(2)}, u32[]{:S(2)}) collective-permute-start(bf16[400,256]{1,0:T(8,128)(2,1)S(1)} %get-tuple-element.75), channel_id=1, source_target_pairs={{0,2},{1,5},{2,0},{3,7},{4,6},{5,1},{6,4},{7,3},{8,10},{9,13},{10,... | collective-permute-start | bytes 614408 | tf_op jit(solution)/shard_map/ppermute | solution.py:239
  24.4 0.5 collective-permute-start.10
  24.9 1.5 %collective-permute-start.11 = (bf16[256,256]{1,0:T(8,128)(2,1)S(1)}, bf16[256,256]{1,0:T(8,128)(2,1)S(1)}, u32[]{:S(2)}, u32[]{:S(2)}) collective-permute-start(bf16[256,256]{1,0:T(8,128)(2,1)S(1)} %get-tuple-element.79), channel_id=1, source_target_pairs={{0,2},{1,5},{2,0},{3,7},{4,6},{5,1},{6,4},{7,3},{8,10},{9,13},{10,... | collective-permute-start | bytes 393224 | tf_op jit(solution)/shard_map/ppermute | solution.py:239
  26.4 5.7 %collective-permute-done.11.refs_1_ = bf16[256,256]{1,0:T(8,128)(2,1)S(1)} collective-permute-done((bf16[256,256]{1,0:T(8,128)(2,1)S(1)}, bf16[256,256]{1,0:T(8,128)(2,1)S(1)}, u32[]{:S(2)}, u32[]{:S(2)}) %collective-permute-start.11) | collective-permute-done | bytes 131104 | tf_op jit(solution)/shard_map/ppermute | solution.py:239
  32.1 0.3 shard_map.150
  32.4 0.7 %collective-permute-start.13 = (bf16[256,256]{1,0:T(8,128)(2,1)S(1)}, bf16[256,256]{1,0:T(8,128)(2,1)S(1)}, u32[]{:S(2)}, u32[]{:S(2)}) collective-permute-start(bf16[256,256]{1,0:T(8,128)(2,1)S(1)} %get-tuple-element.81.refs_2_), channel_id=1, source_target_pairs={{0,4},{1,3},{2,6},{3,1},{4,0},{5,7},{6,2},{7,5},{8,12},{9,11},{10,... | collective-permute-start | bytes 393224 | tf_op jit(solution)/shard_map/ppermute | solution.py:239
  33.2 0.0 collective-permute-done.10.refs_1_
  33.2 0.1 shard_map.151
  33.2 0.0 collective-permute-done.9.refs_1_
  33.3 0.1 shard_map.152
  33.3 1.4 %collective-permute-start.12 = (bf16[208,256]{1,0:T(8,128)(2,1)S(1)}, bf16[208,256]{1,0:T(8,128)(2,1)S(1)}, u32[]{:S(2)}, u32[]{:S(2)}) collective-permute-start(bf16[208,256]{1,0:T(8,128)(2,1)S(1)} %get-tuple-element.84.refs_2_), channel_id=1, source_target_pairs={{0,4},{1,3},{2,6},{3,1},{4,0},{5,7},{6,2},{7,5},{8,12},{9,11},{10,... | collective-permute-start | bytes 319496 | tf_op jit(solution)/shard_map/ppermute | solution.py:239
  34.8 0.7 %collective-permute-start.14 = (bf16[192,256]{1,0:T(8,128)(2,1)S(1)}, bf16[192,256]{1,0:T(8,128)(2,1)S(1)}, u32[]{:S(2)}, u32[]{:S(2)}) collective-permute-start(bf16[192,256]{1,0:T(8,128)(2,1)S(1)} %get-tuple-element.82.refs_2_), channel_id=1, source_target_pairs={{0,4},{1,3},{2,6},{3,1},{4,0},{5,7},{6,2},{7,5},{8,12},{9,11},{10,... | collective-permute-start | bytes 294920 | tf_op jit(solution)/shard_map/ppermute | solution.py:239
  35.4 4.2 %collective-permute-done.14.refs_1_ = bf16[192,256]{1,0:T(8,128)(2,1)S(1)} collective-permute-done((bf16[192,256]{1,0:T(8,128)(2,1)S(1)}, bf16[192,256]{1,0:T(8,128)(2,1)S(1)}, u32[]{:S(2)}, u32[]{:S(2)}) %collective-permute-start.14) | collective-permute-done | bytes 98336 | tf_op jit(solution)/shard_map/ppermute | solution.py:239
  39.7 0.1 shard_map.154
  39.8 2.7 %collective-permute-start.15 = (bf16[336,256]{1,0:T(8,128)(2,1)S(1)}, bf16[336,256]{1,0:T(8,128)(2,1)S(1)}, u32[]{:S(2)}, u32[]{:S(2)}) collective-permute-start(bf16[336,256]{1,0:T(8,128)(2,1)S(1)} %get-tuple-element.89.refs_2_), channel_id=1, source_target_pairs={{0,12},{1,13},{2,14},{3,15},{4,8},{5,9},{6,10},{7,11},{8,4},{9,5},... | collective-permute-start | bytes 516104 | tf_op jit(solution)/shard_map/ppermute | solution.py:239
  42.5 1.2 %collective-permute-start.17 = (bf16[192,256]{1,0:T(8,128)(2,1)S(1)}, bf16[192,256]{1,0:T(8,128)(2,1)S(1)}, u32[]{:S(2)}, u32[]{:S(2)}) collective-permute-start(bf16[192,256]{1,0:T(8,128)(2,1)S(1)} %get-tuple-element.87.refs_4_), channel_id=1, source_target_pairs={{0,12},{1,13},{2,14},{3,15},{4,8},{5,9},{6,10},{7,11},{8,4},{9,5},... | collective-permute-start | bytes 294920 | tf_op jit(solution)/shard_map/ppermute | solution.py:239
  43.7 5.6 %collective-permute-done.17.refs_1_ = bf16[192,256]{1,0:T(8,128)(2,1)S(1)} collective-permute-done((bf16[192,256]{1,0:T(8,128)(2,1)S(1)}, bf16[192,256]{1,0:T(8,128)(2,1)S(1)}, u32[]{:S(2)}, u32[]{:S(2)}) %collective-permute-start.17) | collective-permute-done | bytes 98336 | tf_op jit(solution)/shard_map/ppermute | solution.py:239
  49.3 3.9 %collective-permute-start.18 = (bf16[192,256]{1,0:T(8,128)(2,1)S(1)}, bf16[192,256]{1,0:T(8,128)(2,1)S(1)}, u32[]{:S(2)}, u32[]{:S(2)}) collective-permute-start(bf16[192,256]{1,0:T(8,128)(2,1)S(1)} %shard_map.156.refs_2_.refs_0_), channel_id=1, source_target_pairs={{0,4},{1,3},{2,6},{3,1},{4,0},{5,7},{6,2},{7,5},{8,12},{9,11},{10,... | collective-permute-start | bytes 294920 | tf_op jit(solution)/shard_map/ppermute | solution.py:239
  53.3 0.1 collective-permute-start.20
  53.4 2.5 %collective-permute-done.18.refs_1_ = bf16[192,256]{1,0:T(8,128)(2,1)S(1)} collective-permute-done((bf16[192,256]{1,0:T(8,128)(2,1)S(1)}, bf16[192,256]{1,0:T(8,128)(2,1)S(1)}, u32[]{:S(2)}, u32[]{:S(2)}) %collective-permute-start.18) | collective-permute-done | bytes 98336 | tf_op jit(solution)/shard_map/ppermute | solution.py:239
  55.9 1.6 %collective-permute-start.19 = (bf16[384,256]{1,0:T(8,128)(2,1)S(1)}, bf16[384,256]{1,0:T(8,128)(2,1)S(1)}, u32[]{:S(2)}, u32[]{:S(2)}) collective-permute-start(bf16[384,256]{1,0:T(8,128)(2,1)S(1)} %shard_map.159.refs_2_.refs_0_), channel_id=1, source_target_pairs={{0,2},{1,5},{2,0},{3,7},{4,6},{5,1},{6,4},{7,3},{8,10},{9,13},{10,... | collective-permute-start | bytes 589832 | tf_op jit(solution)/shard_map/ppermute | solution.py:239
  57.5 1.6 %collective-permute-done.20.refs_1_ = bf16[192,256]{1,0:T(8,128)(2,1)S(1)} collective-permute-done((bf16[192,256]{1,0:T(8,128)(2,1)S(1)}, bf16[192,256]{1,0:T(8,128)(2,1)S(1)}, u32[]{:S(2)}, u32[]{:S(2)}) %collective-permute-start.20) | collective-permute-done | bytes 98336 | tf_op jit(solution)/shard_map/ppermute | solution.py:239
  59.1 1.2 %collective-permute-start.21 = (bf16[384,256]{1,0:T(8,128)(2,1)S(1)}, bf16[384,256]{1,0:T(8,128)(2,1)S(1)}, u32[]{:S(2)}, u32[]{:S(2)}) collective-permute-start(bf16[384,256]{1,0:T(8,128)(2,1)S(1)} %shard_map.160.refs_2_), channel_id=1, source_target_pairs={{0,2},{1,5},{2,0},{3,7},{4,6},{5,1},{6,4},{7,3},{8,10},{9,13},{10,... | collective-permute-start | bytes 589832 | tf_op jit(solution)/shard_map/ppermute | solution.py:239
  60.3 0.2 shard_map.155
  60.5 0.6 collective-permute-start.16
  61.1 0.6 collective-permute-done.8.refs_1_
  61.7 0.3 collective-permute-done.16.refs_3_
  62.0 0.8 %shard_map.158 = (f32[320,256]{1,0:T(8,128)}, bf16[128,256]{1,0:T(8,128)(2,1)}, f32[6,256]{1,0:T(8,128)}) custom-call(f32[320,256]{1,0:T(8,128)S(1)} %get-tuple-element.72.refs_0_, bf16[320,256]{1,0:T(8,128)(2,1)S(1)} %collective-permute-done.8.refs_1_, f32[128,256]{1,0:T(8,128)S(1)} %get-tuple-element.90.refs_2_, ...), custom_call_target="tpu_custom_call" | custom-call | tf_op jit(solution)/shard_map/pallas_call | solution.py:32
  62.8 2.0 %collective-permute-done.21.refs_3_ = bf16[384,256]{1,0:T(8,128)(2,1)S(1)} collective-permute-done((bf16[384,256]{1,0:T(8,128)(2,1)S(1)}, bf16[384,256]{1,0:T(8,128)(2,1)S(1)}, u32[]{:S(2)}, u32[]{:S(2)}) %collective-permute-start.21) | collective-permute-done | bytes 196640 | tf_op jit(solution)/shard_map/ppermute | solution.py:239
  64.8 1.2 %shard_map.161 = (f32[512,256]{1,0:T(8,128)}, f32[256,512]{1,0:T(8,128)}, f32[512,256]{1,0:T(8,128)}) custom-call(bf16[384,256]{1,0:T(8,128)(2,1)S(1)} %shard_map.159.refs_2_.refs_0_, bf16[384,256]{1,0:T(8,128)(2,1)S(1)} %collective-permute-done.19.refs_1_, bf16[384,256]{1,0:T(8,128)(2,1)S(1)} %shard_map.160.refs_2_, ...), custom_call_target="tpu_custom_call" | custom-call | tf_op jit(solution)/shard_map/pallas_call | solution.py:32
  (13 shorter events, 0.2 us)
Async XLA Ops:
  1.9 11.0 %collective-permute-start = (bf16[144,128]{1,0:T(8,128)(2,1)S(1)}, bf16[144,128]{1,0:T(8,128)(2,1)S(1)}, u32[]{:S(2)}, u32[]{:S(2)}) collective-permute-start(bf16[144,128]{1,0:T(8,128)(2,1)S(1)} %get-tuple-element.55), channel_id=1, source_target_pairs={{0,2},{2,4},{4,6},{6,8},{8,10},{10,12},{12,14},{14,0},{1,3},{3,5},... | collective-permute-start | bytes 110600 | tf_op jit(solution)/shard_map/ppermute | solution.py:79
  4.9 9.3 %collective-permute-start.1 = (bf16[144,128]{1,0:T(8,128)(2,1)S(1)}, bf16[144,128]{1,0:T(8,128)(2,1)S(1)}, u32[]{:S(2)}, u32[]{:S(2)}) collective-permute-start(bf16[144,128]{1,0:T(8,128)(2,1)S(1)} %get-tuple-element.56), channel_id=1, source_target_pairs={{0,4},{2,6},{4,8},{6,10},{8,12},{10,14},{12,0},{14,2},{1,5},{3,7},... | collective-permute-start | bytes 110600 | tf_op jit(solution)/shard_map/ppermute | solution.py:79
  6.5 10.9 %collective-permute-start.2 = (bf16[144,128]{1,0:T(8,128)(2,1)S(1)}, bf16[144,128]{1,0:T(8,128)(2,1)S(1)}, u32[]{:S(2)}, u32[]{:S(2)}) collective-permute-start(bf16[144,128]{1,0:T(8,128)(2,1)S(1)} %get-tuple-element.57), channel_id=1, source_target_pairs={{0,6},{2,8},{4,10},{6,12},{8,14},{10,0},{12,2},{14,4},{1,7},{3,9},... | collective-permute-start | bytes 110600 | tf_op jit(solution)/shard_map/ppermute | solution.py:79
  9.1 8.4 %collective-permute-start.3 = (bf16[144,128]{1,0:T(8,128)(2,1)S(1)}, bf16[144,128]{1,0:T(8,128)(2,1)S(1)}, u32[]{:S(2)}, u32[]{:S(2)}) collective-permute-start(bf16[144,128]{1,0:T(8,128)(2,1)S(1)} %get-tuple-element.58), channel_id=1, source_target_pairs={{0,8},{2,10},{4,12},{6,14},{8,0},{10,2},{12,4},{14,6},{1,9},{3,11}... | collective-permute-start | bytes 110600 | tf_op jit(solution)/shard_map/ppermute | solution.py:79
  10.3 7.2 %collective-permute-start.4 = (bf16[144,128]{1,0:T(8,128)(2,1)S(1)}, bf16[144,128]{1,0:T(8,128)(2,1)S(1)}, u32[]{:S(2)}, u32[]{:S(2)}) collective-permute-start(bf16[144,128]{1,0:T(8,128)(2,1)S(1)} %get-tuple-element.59), channel_id=1, source_target_pairs={{0,10},{2,12},{4,14},{6,0},{8,2},{10,4},{12,6},{14,8},{1,11},{3,13... | collective-permute-start | bytes 110600 | tf_op jit(solution)/shard_map/ppermute | solution.py:79
  12.9 4.5 %collective-permute-start.5 = (bf16[144,128]{1,0:T(8,128)(2,1)S(1)}, bf16[144,128]{1,0:T(8,128)(2,1)S(1)}, u32[]{:S(2)}, u32[]{:S(2)}) collective-permute-start(bf16[144,128]{1,0:T(8,128)(2,1)S(1)} %get-tuple-element.60), channel_id=1, source_target_pairs={{0,12},{2,14},{4,0},{6,2},{8,4},{10,6},{12,8},{14,10},{1,13},{3,15... | collective-permute-start | bytes 110600 | tf_op jit(solution)/shard_map/ppermute | solution.py:79
  14.3 4.0 %collective-permute-start.6 = (bf16[144,128]{1,0:T(8,128)(2,1)S(1)}, bf16[144,128]{1,0:T(8,128)(2,1)S(1)}, u32[]{:S(2)}, u32[]{:S(2)}) collective-permute-start(bf16[144,128]{1,0:T(8,128)(2,1)S(1)} %get-tuple-element.61), channel_id=1, source_target_pairs={{0,14},{2,0},{4,2},{6,4},{8,6},{10,8},{12,10},{14,12},{1,15},{3,1}... | collective-permute-start | bytes 110600 | tf_op jit(solution)/shard_map/ppermute | solution.py:79
  18.3 1.6 %collective-permute-start.7 = (bf16[7,144,128]{2,1,0:T(8,128)(2,1)S(1)}, bf16[7,144,128]{2,1,0:T(8,128)(2,1)S(1)}, u32[]{:S(2)}, u32[]{:S(2)}) collective-permute-start(bf16[7,144,128]{2,1,0:T(8,128)(2,1)S(1)} %shard_map.147.refs_1_), channel_id=1, source_target_pairs={{0,1},{1,0},{2,3},{3,2},{4,5},{5,4},{6,7},{7,6},{8,9},{9,8},{10,11... | collective-permute-start | bytes 774152 | tf_op jit(solution)/shard_map/ppermute | solution.py:79
  22.8 10.5 %collective-permute-start.9 = (bf16[400,256]{1,0:T(8,128)(2,1)S(1)}, bf16[400,256]{1,0:T(8,128)(2,1)S(1)}, u32[]{:S(2)}, u32[]{:S(2)}) collective-permute-start(bf16[400,256]{1,0:T(8,128)(2,1)S(1)} %get-tuple-element.75), channel_id=1, source_target_pairs={{0,2},{1,5},{2,0},{3,7},{4,6},{5,1},{6,4},{7,3},{8,10},{9,13},{10,... | collective-permute-start | bytes 614408 | tf_op jit(solution)/shard_map/ppermute | solution.py:239
  24.4 8.8 %collective-permute-start.10 = (bf16[384,256]{1,0:T(8,128)(2,1)S(1)}, bf16[384,256]{1,0:T(8,128)(2,1)S(1)}, u32[]{:S(2)}, u32[]{:S(2)}) collective-permute-start(bf16[384,256]{1,0:T(8,128)(2,1)S(1)} %get-tuple-element.77), channel_id=1, source_target_pairs={{0,2},{1,5},{2,0},{3,7},{4,6},{5,1},{6,4},{7,3},{8,10},{9,13},{10,... | collective-permute-start | bytes 589832 | tf_op jit(solution)/shard_map/ppermute | solution.py:239
  24.9 7.2 %collective-permute-start.11 = (bf16[256,256]{1,0:T(8,128)(2,1)S(1)}, bf16[256,256]{1,0:T(8,128)(2,1)S(1)}, u32[]{:S(2)}, u32[]{:S(2)}) collective-permute-start(bf16[256,256]{1,0:T(8,128)(2,1)S(1)} %get-tuple-element.79), channel_id=1, source_target_pairs={{0,2},{1,5},{2,0},{3,7},{4,6},{5,1},{6,4},{7,3},{8,10},{9,13},{10,... | collective-permute-start | bytes 393224 | tf_op jit(solution)/shard_map/ppermute | solution.py:239
  32.4 7.3 %collective-permute-start.13 = (bf16[256,256]{1,0:T(8,128)(2,1)S(1)}, bf16[256,256]{1,0:T(8,128)(2,1)S(1)}, u32[]{:S(2)}, u32[]{:S(2)}) collective-permute-start(bf16[256,256]{1,0:T(8,128)(2,1)S(1)} %get-tuple-element.81.refs_2_), channel_id=1, source_target_pairs={{0,4},{1,3},{2,6},{3,1},{4,0},{5,7},{6,2},{7,5},{8,12},{9,11},{10,... | collective-permute-start | bytes 393224 | tf_op jit(solution)/shard_map/ppermute | solution.py:239
  33.3 6.4 %collective-permute-start.12 = (bf16[208,256]{1,0:T(8,128)(2,1)S(1)}, bf16[208,256]{1,0:T(8,128)(2,1)S(1)}, u32[]{:S(2)}, u32[]{:S(2)}) collective-permute-start(bf16[208,256]{1,0:T(8,128)(2,1)S(1)} %get-tuple-element.84.refs_2_), channel_id=1, source_target_pairs={{0,4},{1,3},{2,6},{3,1},{4,0},{5,7},{6,2},{7,5},{8,12},{9,11},{10,... | collective-permute-start | bytes 319496 | tf_op jit(solution)/shard_map/ppermute | solution.py:239
  34.8 4.9 %collective-permute-start.14 = (bf16[192,256]{1,0:T(8,128)(2,1)S(1)}, bf16[192,256]{1,0:T(8,128)(2,1)S(1)}, u32[]{:S(2)}, u32[]{:S(2)}) collective-permute-start(bf16[192,256]{1,0:T(8,128)(2,1)S(1)} %get-tuple-element.82.refs_2_), channel_id=1, source_target_pairs={{0,4},{1,3},{2,6},{3,1},{4,0},{5,7},{6,2},{7,5},{8,12},{9,11},{10,... | collective-permute-start | bytes 294920 | tf_op jit(solution)/shard_map/ppermute | solution.py:239
  39.8 13.4 %collective-permute-start.15 = (bf16[336,256]{1,0:T(8,128)(2,1)S(1)}, bf16[336,256]{1,0:T(8,128)(2,1)S(1)}, u32[]{:S(2)}, u32[]{:S(2)}) collective-permute-start(bf16[336,256]{1,0:T(8,128)(2,1)S(1)} %get-tuple-element.89.refs_2_), channel_id=1, source_target_pairs={{0,12},{1,13},{2,14},{3,15},{4,8},{5,9},{6,10},{7,11},{8,4},{9,5},... | collective-permute-start | bytes 516104 | tf_op jit(solution)/shard_map/ppermute | solution.py:239
  42.5 6.7 %collective-permute-start.17 = (bf16[192,256]{1,0:T(8,128)(2,1)S(1)}, bf16[192,256]{1,0:T(8,128)(2,1)S(1)}, u32[]{:S(2)}, u32[]{:S(2)}) collective-permute-start(bf16[192,256]{1,0:T(8,128)(2,1)S(1)} %get-tuple-element.87.refs_4_), channel_id=1, source_target_pairs={{0,12},{1,13},{2,14},{3,15},{4,8},{5,9},{6,10},{7,11},{8,4},{9,5},... | collective-permute-start | bytes 294920 | tf_op jit(solution)/shard_map/ppermute | solution.py:239
  49.3 6.5 %collective-permute-start.18 = (bf16[192,256]{1,0:T(8,128)(2,1)S(1)}, bf16[192,256]{1,0:T(8,128)(2,1)S(1)}, u32[]{:S(2)}, u32[]{:S(2)}) collective-permute-start(bf16[192,256]{1,0:T(8,128)(2,1)S(1)} %shard_map.156.refs_2_.refs_0_), channel_id=1, source_target_pairs={{0,4},{1,3},{2,6},{3,1},{4,0},{5,7},{6,2},{7,5},{8,12},{9,11},{10,... | collective-permute-start | bytes 294920 | tf_op jit(solution)/shard_map/ppermute | solution.py:239
  53.3 5.7 %collective-permute-start.20 = (bf16[192,256]{1,0:T(8,128)(2,1)S(1)}, bf16[192,256]{1,0:T(8,128)(2,1)S(1)}, u32[]{:S(2)}, u32[]{:S(2)}) collective-permute-start(bf16[192,256]{1,0:T(8,128)(2,1)S(1)} %get-tuple-element.97.refs_2_.refs_0_), channel_id=1, source_target_pairs={{0,4},{1,3},{2,6},{3,1},{4,0},{5,7},{6,2},{7,5},{8,12},{9,11},{10,... | collective-permute-start | bytes 294920 | tf_op jit(solution)/shard_map/ppermute | solution.py:239
  55.9 6.9 %collective-permute-start.19 = (bf16[384,256]{1,0:T(8,128)(2,1)S(1)}, bf16[384,256]{1,0:T(8,128)(2,1)S(1)}, u32[]{:S(2)}, u32[]{:S(2)}) collective-permute-start(bf16[384,256]{1,0:T(8,128)(2,1)S(1)} %shard_map.159.refs_2_.refs_0_), channel_id=1, source_target_pairs={{0,2},{1,5},{2,0},{3,7},{4,6},{5,1},{6,4},{7,3},{8,10},{9,13},{10,... | collective-permute-start | bytes 589832 | tf_op jit(solution)/shard_map/ppermute | solution.py:239
  59.1 5.7 %collective-permute-start.21 = (bf16[384,256]{1,0:T(8,128)(2,1)S(1)}, bf16[384,256]{1,0:T(8,128)(2,1)S(1)}, u32[]{:S(2)}, u32[]{:S(2)}) collective-permute-start(bf16[384,256]{1,0:T(8,128)(2,1)S(1)} %shard_map.160.refs_2_), channel_id=1, source_target_pairs={{0,2},{1,5},{2,0},{3,7},{4,6},{5,1},{6,4},{7,3},{8,10},{9,13},{10,... | collective-permute-start | bytes 589832 | tf_op jit(solution)/shard_map/ppermute | solution.py:239
  60.3 1.4 %collective-permute-start.8 = (bf16[320,256]{1,0:T(8,128)(2,1)S(1)}, bf16[320,256]{1,0:T(8,128)(2,1)S(1)}, u32[]{:S(2)}, u32[]{:S(2)}) collective-permute-start(bf16[320,256]{1,0:T(8,128)(2,1)S(1)} %get-tuple-element.73), channel_id=1, source_target_pairs={{0,1},{1,0},{2,3},{3,2},{4,5},{5,4},{6,7},{7,6},{8,9},{9,8},{10,11... | collective-permute-start | bytes 491528 | tf_op jit(solution)/shard_map/ppermute | solution.py:79
  60.5 1.5 %collective-permute-start.16 = (bf16[128,256]{1,0:T(8,128)(2,1)S(1)}, bf16[128,256]{1,0:T(8,128)(2,1)S(1)}, u32[]{:S(2)}, u32[]{:S(2)}) collective-permute-start(bf16[128,256]{1,0:T(8,128)(2,1)S(1)} %get-tuple-element.91), channel_id=1, source_target_pairs={{0,1},{1,0},{2,3},{3,2},{4,5},{5,4},{6,7},{7,6},{8,9},{9,8},{10,11... | collective-permute-start | bytes 196616 | tf_op jit(solution)/shard_map/ppermute | solution.py:79

commit v14 on v13

--- a/solution.py
+++ b/solution.py
@@ -9,7 +9,7 @@
 
 OWNER_AXES = ("obs", "node")
 SUBLANES = 16
-BUNDLES = 2
+PARTS = 2
 BF16 = jnp.bfloat16
 F32 = jnp.float32
 
@@ -293,10 +293,9 @@
 
 
 def weight_kernel(
-    step, bundles, tail, hot_ref, act_ref, rows_mine_ref, rows_theirs_ref, state_ref, agg_ref, w_node_ref,
-    mine_ref, theirs_ref, *refs
+    step, tail, hot_ref, act_ref, rows_mine_ref, rows_theirs_ref, state_ref, agg_ref, w_node_ref,
+    mine_ref, theirs_ref, keep_ref, send_ref, total_ref,
 ):
-    halves_refs, total_ref = refs[:-1], refs[-1]
     width, hidden = w_node_ref.shape
     nodes = state_ref.shape[0]
     sums = dot(hot_ref[...], act_ref[...], 0, 0)
@@ -315,12 +314,7 @@
         total_ref[pl.ds(pl.multiple_of(begin + which * half, SUBLANES), half), :] = dot(ref[...], g_a, 0, 0)
     begin += width
     total_ref[begin:, :] = sums[nodes:, :hidden]
-    rows = begin // bundles
-    for i in range(bundles):
-        split_half(
-            total_ref, i * rows, rows, step, tail if i == bundles - 1 else 0,
-            halves_refs[2 * i], halves_refs[2 * i + 1],
-        )
+    split_half(total_ref, 0, begin, step, tail, keep_ref, send_ref)
     mine, theirs = other_half(w_node_ref)
     theirs_ref[...] = dot(node_hidden, theirs, 1, 1).astype(BF16)
     mine_ref[...] = dot(node_hidden, mine, 1, 1)
@@ -351,15 +345,22 @@
     split_half(total_ref, 0, total_ref.shape[0], step, 0, next_ref, send_ref)
 
 
-def add_with_rows_kernel(
-    step, tail, keep_ref, got_ref, rows_ref, rows_got_ref, next_ref, send_ref, rows_next_ref, total_ref, rows_total_ref
-):
-    share = next_ref.shape[0]
+def middle_kernel(step, tail, parts, keep_ref, got_ref, rows_ref, rows_got_ref, rows_next_ref, *refs):
+    part_refs, (total_ref, rows_total_ref) = refs[: 2 * parts], refs[2 * parts :]
     total_ref[...] = keep_ref[...] + got_ref[...].astype(F32)
-    split_half(total_ref, 0, share - tail, None, tail, next_ref, send_ref.at[:share])
+    rows = total_ref.shape[0] - tail
+    part = rows // parts
+    for i in range(parts):
+        keep_ref, send_ref = part_refs[2 * i : 2 * i + 2]
+        both = total_ref[i * part : (i + 1) * part, :].astype(BF16)
+        keep_ref[:part, :] = both.astype(F32)
+        send_ref[:part, :] = both
+    both = total_ref[rows:, :].astype(BF16)
+    part_refs[0][part:, :] = both.astype(F32)
+    part_refs[1][part : part + tail, :] = both
     rows_total_ref[...] = (rows_ref[...].astype(F32) + rows_got_ref[...].astype(F32)).astype(BF16)
     split_half(
-        rows_total_ref, 0, rows_total_ref.shape[0], step, 0, rows_next_ref, send_ref.at[share:]
+        rows_total_ref, 0, rows_total_ref.shape[0], step, 0, rows_next_ref, part_refs[1].at[part + tail :]
     )
 
 
@@ -378,22 +379,25 @@
     out_ref[pl.ds(pl.multiple_of((1 - bit) * rows, SUBLANES), rows), :] = got_ref[...]
 
 
-def spread_kernel(step, bundles, *refs):
+def spread_kernel(step, parts, piece, *refs):
     low = own_bit(step) == 0
     joined = []
-    for i in range(bundles):
+    for i in range(parts):
         mine, got = refs[2 * i][...], refs[2 * i + 1][...]
-        joined += [jnp.where(low, mine, got), jnp.where(low, got, mine)]
-    half, hidden = joined[0].shape
+        joined.append([jnp.where(low, mine, got), jnp.where(low, got, mine)])
+    half, hidden = joined[0][0].shape
+    share = piece // parts
     at = 0
-    for out_ref in refs[2 * bundles :]:
+    for out_ref in refs[2 * parts :]:
         for c in range(out_ref.shape[1] // hidden):
             begin = 0
             while begin < out_ref.shape[0]:
-                offset = at % half
-                count = min(out_ref.shape[0] - begin, half - offset)
-                out_ref[begin : begin + count, c * hidden : (c + 1) * hidden] = joined[at // half][
-                    offset : offset + count
+                number, offset = divmod(at, share)
+                count = min(out_ref.shape[0] - begin, share - offset)
+                place, part = divmod(number, parts)
+                upper, row = divmod(place * share, half)
+                out_ref[begin : begin + count, c * hidden : (c + 1) * hidden] = joined[part][upper][
+                    row + offset : row + offset + count
                 ].astype(F32)
                 at, begin = at + count, begin + count
 
@@ -434,34 +438,15 @@
     return used
 
 
-def weight_chain(steps, rows, tail, slots, keep, got, after, returned=None):
-    used = halving_used(steps, rows)
-    keep, got = yield from summing(steps[:-1], len(steps) - 1, tail, keep, got, after)
-    if returned:
-        rows_keep, rows_got = returned
-        shape = (half_rows(rows_keep.shape[0]), keep.shape[1])
-        keep, send, rows_keep = call(
-            functools.partial(add_with_rows_kernel, steps[-1], tail),
-            [(keep.shape, F32), ((keep.shape[0] + shape[0], shape[1]), BF16), (shape, BF16)],
-            keep, got, rows_keep, rows_got,
-            scratch=[pltpu.VMEM(keep.shape, F32), pltpu.VMEM(rows_keep.shape, BF16)],
-            after=after,
-        )
-    else:
-        keep, send = call(
-            functools.partial(add_kernel, None, tail),
-            [(keep.shape, F32), (keep.shape, BF16)],
-            keep, got,
-            scratch=[pltpu.VMEM(keep.shape, F32)],
-            after=after,
-        )
-    after[:] = [send]
-    arrived = got = flip(send, steps[-1])
-    yield
+def sum_chain(steps, tail, keep, got, after, out):
+    out += yield from summing(steps[:-1], len(steps) - 1, tail, keep, got, after)
+
+
+def gather_chain(used, rows, slots, keep, got, after):
+    hidden = keep.shape[1]
     piece, *sums = call(
         last_kernel,
-        [((keep.shape[0] - tail, keep.shape[1]), BF16)]
-        + ([((slots, keep.shape[1]), F32)] if tail else []),
+        [((rows, hidden), BF16)] + ([((slots, hidden), F32)] if keep.shape[0] > rows else []),
         keep, got,
         after=after,
     )
@@ -471,14 +456,14 @@
     for step, following in zip(used[:0:-1], used[-2::-1]):
         (piece,) = call(
             functools.partial(join_kernel, step),
-            [((2 * piece.shape[0], piece.shape[1]), BF16)],
+            [((2 * piece.shape[0], hidden), BF16)],
             piece, got,
             after=after,
         )
         after[:] = [piece]
         got = flip(piece, following)
         yield
-    return [piece, got], sums, (rows_keep, arrived) if returned else ()
+    return [piece, got], sums
 
 
 def rows_chain(steps, keep, got, pick, after, out):
@@ -552,46 +537,55 @@
     )
 
     stack = 2 * width + width // hidden * hidden
-    bundles = BUNDLES
-    rows = stack // bundles
     obs_got = flip(obs_send, steps[0])
-    shapes = []
-    for i in range(bundles):
-        share = rows // 2 + (tail if i == bundles - 1 else 0)
-        shapes += [((share, hidden), F32), ((share, hidden), BF16)]
-    node_mine, node_theirs, *shares = call(
-        functools.partial(weight_kernel, steps[0], bundles, tail),
-        [((nodes, half), F32), ((nodes, half), BF16)] + shapes,
+    share = half_rows(stack) + tail
+    node_mine, node_theirs, keep, send = call(
+        functools.partial(weight_kernel, steps[0], tail),
+        [((nodes, half), F32), ((nodes, half), BF16), ((share, hidden), F32), ((share, hidden), BF16)],
         hot, act, rows_mine, rows_theirs, state_held, agg_held, w_node_held,
         scratch=[pltpu.VMEM((stack + tail, hidden), F32)],
     )
-    after = []
-    returned = []
-    chains = [rows_chain(steps, obs_keep, obs_got, obs_pick, after, returned)]
-    got = [flip(send, steps[0]) for send in shares[1::2]]
-    for i in range(bundles):
-        last = i == bundles - 1
-        chains.append(
-            weight_chain(
-                steps, rows, tail if last else 0, slots, shares[2 * i], got[i], after, returned if last else None
-            )
-        )
     node_got = shift(node_theirs, "mp", 1)
-    everyone = list(range(len(chains)))
-    turns = everyone * (len(steps) - 2) + [0] + everyone[1:] * (2 + len(halving_used(steps, rows)) - 1)
-    _, *weights = in_turns(chains, turns)
-    obs_keep, arrived = weights[-1][2]
+    after, summed, returned = [], [], []
+    in_turns(
+        [
+            sum_chain(steps, tail, keep, flip(send, steps[0]), after, summed),
+            rows_chain(steps, obs_keep, obs_got, obs_pick, after, returned),
+        ],
+        [0, 1] * (len(steps) - 2),
+    )
+
+    used = halving_used(steps, stack)
+    piece = stack >> len(used)
+    parts = PARTS if piece % (PARTS * SUBLANES) == 0 else 1
+    shares = [piece // parts + (0 if i else tail) for i in range(parts)]
+    shapes = []
+    for i, share in enumerate(shares):
+        shapes += [((share, hidden), F32), ((share + (0 if i else obs), hidden), BF16)]
+    obs_keep, *pieces = call(
+        functools.partial(middle_kernel, steps[-1], tail, parts),
+        [((obs, hidden), BF16)] + shapes,
+        *summed, *returned,
+        scratch=[pltpu.VMEM(summed[0].shape, F32), pltpu.VMEM(returned[0].shape, BF16)],
+        after=after,
+    )
+    after[:] = []
+    arrived = [flip(send, steps[-1]) for send in pieces[1::2]]
+    weights = in_turns(
+        [gather_chain(used, piece // parts, slots, pieces[2 * i], arrived[i], after) for i in range(parts)],
+        list(range(parts)) * len(used),
+    )
     obs_mine, obs_theirs = call(
-        obs_kernel, [((obs, half), F32), ((obs, half), BF16)], obs_keep, arrived, w_obs_held
-    )
-    (slot_sums,) = weights[-1][1]
+        obs_kernel, [((obs, half), F32), ((obs, half), BF16)], obs_keep, arrived[0], w_obs_held
+    )
+    (slot_sums,) = weights[0][1]
     grad_node, grad_obs, grad_slot = call(
         merge_kernel, [((nodes, half), F32), ((obs, half), BF16), ((slots, hidden), F32)],
         node_mine, node_got, obs_mine, shift(obs_theirs, "mp", 1), slot_sums,
     )
-    ends = [end for pair, *_ in weights for end in pair]
+    ends = [end for pair, _ in weights for end in pair]
     grad_w_node, grad_w_out, grad_w_obs = call(
-        functools.partial(spread_kernel, steps[0], bundles),
+        functools.partial(spread_kernel, steps[0], parts, piece),
         [((width, hidden), F32), ((hidden, width), F32), ((width, hidden), F32)],
         *ends,
         after=[pltpu.with_memory_space_constraint(grad_obs, pltpu.HBM)],

time: 66.2 us -> 65.4 us (0.988)
  starting transfers between devices: 31.5 us -> 29.1 us
  waiting for transfers between devices: 24.8 us -> 26.6 us
    ppermute x12 -> x10, starting transfers between devices: 17.1 us -> 14.7 us  [flip(): return lax.ppermute(value, axes, pairs)]
    ppermute x12 -> x10, waiting for transfers between devices: 21.6 us -> 23.4 us  [flip(): return lax.ppermute(value, axes, pairs)]
    pallas_call x15 -> x13, Pallas kernels: 5.83 us -> 5.74 us  [call(): pl.pallas_call(lambda *refs: kernel(*refs[:count], *refs[len(args):]), ou...]
  transfers between devices with their start and end apart: 22 -> 20, of which waited for: 10 -> 12; matrix products, arithmetic and copies ran while one was open for 0% -> 0% of each run, Pallas kernels for 5% -> 5%
where the time goes in v14:
time: 65.4 us; the launch traced here: 65.2 us
  starting transfers between devices  29.1 us (44%)
  waiting for transfers between devices  26.6 us (41%)
  Pallas kernels  8.77 us (13%)
  between operations  0.77 us (1%)
    ppermute x10, waiting for transfers between devices, flip(): return lax.ppermute(value, axes, pairs)  23.4 us
    ppermute x10, starting transfers between devices, flip(): return lax.ppermute(value, axes, pairs)  14.7 us
    ppermute x10, starting transfers between devices, shift(): lax.ppermute(value, axis, [(i, (i + step) % size) for i in range(size)])  14.4 us
    pallas_call x13, Pallas kernels, call(): pl.pallas_call(lambda *refs: kernel(*refs[:count], *refs[len(args):]), ou...  5.74 us
    ppermute x10, waiting for transfers between devices, shift(): lax.ppermute(value, axis, [(i, (i + step) % size) for i in range(size)])  3.19 us
    pallas_call x2, Pallas kernels, call_staged(): pl.pallas_call(staged, out_shape=[jax.ShapeDtypeStruct(shape, dtype) for...  3.03 us
  transfers between devices with their start and end apart: 20, of which 12 were waited for; matrix products, arithmetic and copies ran while one was open for 0% of the time, Pallas kernels for 5%

profile of v14, /device:TPU:0, one launch (start us, length us, event | category | flops | bytes accessed | tf_op | source)
XLA Modules:
  0.0 65.2 jit_solution(2943752591387404943)
XLA Ops:
  0.6 1.3 %shard_map.145 = (bf16[144,128]{1,0:T(8,128)(2,1)S(1)}, bf16[144,128]{1,0:T(8,128)(2,1)S(1)}, bf16[144,128]{1,0:T(8,128)(2,1)S(1)}, bf16[144,128]{1,0:T(8,128)(2...) custom-call(bf16[128,512]{1,0:T(8,128)(2,1)} %refs_0_.2, ...), custom_call_target="tpu_custom_call" | custom-call | tf_op jit(solution)/shard_map/pallas_call | solution.py:61
  1.9 3.0 %collective-permute-start = (bf16[144,128]{1,0:T(8,128)(2,1)S(1)}, bf16[144,128]{1,0:T(8,128)(2,1)S(1)}, u32[]{:S(2)}, u32[]{:S(2)}) collective-permute-start(bf16[144,128]{1,0:T(8,128)(2,1)S(1)} %get-tuple-element.51), channel_id=1, source_target_pairs={{0,2},{2,4},{4,6},{6,8},{8,10},{10,12},{12,14},{14,0},{1,3},{3,5},... | collective-permute-start | bytes 110600 | tf_op jit(solution)/shard_map/ppermute | solution.py:79
  4.9 1.6 %collective-permute-start.1 = (bf16[144,128]{1,0:T(8,128)(2,1)S(1)}, bf16[144,128]{1,0:T(8,128)(2,1)S(1)}, u32[]{:S(2)}, u32[]{:S(2)}) collective-permute-start(bf16[144,128]{1,0:T(8,128)(2,1)S(1)} %get-tuple-element.52), channel_id=1, source_target_pairs={{0,4},{2,6},{4,8},{6,10},{8,12},{10,14},{12,0},{14,2},{1,5},{3,7},... | collective-permute-start | bytes 110600 | tf_op jit(solution)/shard_map/ppermute | solution.py:79
  6.5 2.6 %collective-permute-start.2 = (bf16[144,128]{1,0:T(8,128)(2,1)S(1)}, bf16[144,128]{1,0:T(8,128)(2,1)S(1)}, u32[]{:S(2)}, u32[]{:S(2)}) collective-permute-start(bf16[144,128]{1,0:T(8,128)(2,1)S(1)} %get-tuple-element.53), channel_id=1, source_target_pairs={{0,6},{2,8},{4,10},{6,12},{8,14},{10,0},{12,2},{14,4},{1,7},{3,9},... | collective-permute-start | bytes 110600 | tf_op jit(solution)/shard_map/ppermute | solution.py:79
  9.1 1.2 %collective-permute-start.3 = (bf16[144,128]{1,0:T(8,128)(2,1)S(1)}, bf16[144,128]{1,0:T(8,128)(2,1)S(1)}, u32[]{:S(2)}, u32[]{:S(2)}) collective-permute-start(bf16[144,128]{1,0:T(8,128)(2,1)S(1)} %get-tuple-element.54), channel_id=1, source_target_pairs={{0,8},{2,10},{4,12},{6,14},{8,0},{10,2},{12,4},{14,6},{1,9},{3,11}... | collective-permute-start | bytes 110600 | tf_op jit(solution)/shard_map/ppermute | solution.py:79
  10.3 2.6 %collective-permute-start.4 = (bf16[144,128]{1,0:T(8,128)(2,1)S(1)}, bf16[144,128]{1,0:T(8,128)(2,1)S(1)}, u32[]{:S(2)}, u32[]{:S(2)}) collective-permute-start(bf16[144,128]{1,0:T(8,128)(2,1)S(1)} %get-tuple-element.55), channel_id=1, source_target_pairs={{0,10},{2,12},{4,14},{6,0},{8,2},{10,4},{12,6},{14,8},{1,11},{3,13... | collective-permute-start | bytes 110600 | tf_op jit(solution)/shard_map/ppermute | solution.py:79
  12.9 0.0 collective-permute-done.refs_0_
  12.9 1.4 %collective-permute-start.5 = (bf16[144,128]{1,0:T(8,128)(2,1)S(1)}, bf16[144,128]{1,0:T(8,128)(2,1)S(1)}, u32[]{:S(2)}, u32[]{:S(2)}) collective-permute-start(bf16[144,128]{1,0:T(8,128)(2,1)S(1)} %get-tuple-element.56), channel_id=1, source_target_pairs={{0,12},{2,14},{4,0},{6,2},{8,4},{10,6},{12,8},{14,10},{1,13},{3,15... | collective-permute-start | bytes 110600 | tf_op jit(solution)/shard_map/ppermute | solution.py:79
  14.3 0.0 collective-permute-done.1.refs_1_
  14.3 1.4 %collective-permute-start.6 = (bf16[144,128]{1,0:T(8,128)(2,1)S(1)}, bf16[144,128]{1,0:T(8,128)(2,1)S(1)}, u32[]{:S(2)}, u32[]{:S(2)}) collective-permute-start(bf16[144,128]{1,0:T(8,128)(2,1)S(1)} %get-tuple-element.57), channel_id=1, source_target_pairs={{0,14},{2,0},{4,2},{6,4},{8,6},{10,8},{12,10},{14,12},{1,15},{3,1}... | collective-permute-start | bytes 110600 | tf_op jit(solution)/shard_map/ppermute | solution.py:79
  15.7 1.7 %shard_map.146 = (bf16[336,1024]{1,0:T(8,128)(2,1)S(1)}, bf16[320,512]{1,0:T(8,128)(2,1)S(1)}, bf16[320,512]{1,0:T(8,128)(2,1)S(1)}, bf16[512,256]{1,0:T(8,128)(2,1)S(1)}, bf16[512,256]{1,0:T(8,128)(2,1)S(1)}) custom-call(bf16[320,512]{1,0:T(8,128)(2,1)} %refs_0_.3, bf16[320,512]{1,0:T(8,128)(2,1)} %refs_1_.1, bf16[512,256]{1,0:T(8,128)(2,1)} %refs_2_.1, ...), custom_call_target="tpu_custom_call" | custom-call | tf_op jit(solution)/shard_map/pallas_call | solution.py:61
  17.4 0.0 collective-permute-done.2.refs_2_
  17.5 0.0 collective-permute-done.3.refs_3_
  17.5 0.0 collective-permute-done.5.refs_5_
  17.5 0.8 %collective-permute-done.6.refs_6_ = bf16[144,128]{1,0:T(8,128)(2,1)S(1)} collective-permute-done((bf16[144,128]{1,0:T(8,128)(2,1)S(1)}, bf16[144,128]{1,0:T(8,128)(2,1)S(1)}, u32[]{:S(2)}, u32[]{:S(2)}) %collective-permute-start.6) | collective-permute-done | bytes 36896 | tf_op jit(solution)/shard_map/ppermute | solution.py:79
  18.3 0.1 collective-permute-start.7
  18.3 1.5 %collective-permute-done.7.refs_3_ = bf16[7,144,128]{2,1,0:T(8,128)(2,1)S(1)} collective-permute-done((bf16[7,144,128]{2,1,0:T(8,128)(2,1)S(1)}, bf16[7,144,128]{2,1,0:T(8,128)(2,1)S(1)}, u32[]{:S(2)}, u32[]{:S(2)}) %collective-permute-start.7) | collective-permute-done | bytes 258080 | tf_op jit(solution)/shard_map/ppermute | solution.py:79
  19.9 1.6 %shard_map.148 = (bf16[512,512]{1,0:T(8,128)(2,1)S(1)}, bf16[512,336]{1,0:T(8,128)(2,1)S(1)}, bf16[512,256]{1,0:T(8,128)(2,1)S(1)}, bf16[512,256]{1,0:T(8,128)(2...) custom-call(bf16[144,128]{1,0:T(8,128)(2,1)S(1)} %get-tuple-element.50.refs_0_, ...), custom_call_target="tpu_custom_call" | custom-call | tf_op jit(solution)/shard_map/pallas_call | solution.py:32
  21.5 1.2 %shard_map.149 = (f32[320,256]{1,0:T(8,128)S(1)}, bf16[320,256]{1,0:T(8,128)(2,1)S(1)}, f32[784,256]{1,0:T(8,128)S(1)}, bf16[784,256]{1,0:T(8,128)(2,1)S(1)}) custom-call(bf16[512,336]{1,0:T(8,128)(2,1)S(1)} %get-tuple-element.61.refs_0_, bf16[512,512]{1,0:T(8,128)(2,1)S(1)} %get-tuple-element.62.refs_1_, bf16[512,256]{1,0:T(8,128)(2,1)S(1)} %get-tuple-element.63.refs_2_, ...), custom_call_target="tpu_custom_call" | custom-call | tf_op jit(solution)/shard_map/pallas_call | solution.py:32
  22.7 1.6 %collective-permute-start.9 = (bf16[784,256]{1,0:T(8,128)(2,1)S(1)}, bf16[784,256]{1,0:T(8,128)(2,1)S(1)}, u32[]{:S(2)}, u32[]{:S(2)}) collective-permute-start(bf16[784,256]{1,0:T(8,128)(2,1)S(1)} %get-tuple-element.71), channel_id=1, source_target_pairs={{0,2},{1,5},{2,0},{3,7},{4,6},{5,1},{6,4},{7,3},{8,10},{9,13},{10,... | collective-permute-start | bytes 1204232 | tf_op jit(solution)/shard_map/ppermute | solution.py:239
  24.3 0.5 collective-permute-start.11
  24.8 5.8 %collective-permute-done.9.refs_1_ = bf16[784,256]{1,0:T(8,128)(2,1)S(1)} collective-permute-done((bf16[784,256]{1,0:T(8,128)(2,1)S(1)}, bf16[784,256]{1,0:T(8,128)(2,1)S(1)}, u32[]{:S(2)}, u32[]{:S(2)}) %collective-permute-start.9) | collective-permute-done | bytes 401440 | tf_op jit(solution)/shard_map/ppermute | solution.py:239
  30.6 0.2 shard_map.150
  30.8 0.7 %collective-permute-start.10 = (bf16[400,256]{1,0:T(8,128)(2,1)S(1)}, bf16[400,256]{1,0:T(8,128)(2,1)S(1)}, u32[]{:S(2)}, u32[]{:S(2)}) collective-permute-start(bf16[400,256]{1,0:T(8,128)(2,1)S(1)} %get-tuple-element.73.refs_3_), channel_id=1, source_target_pairs={{0,4},{1,3},{2,6},{3,1},{4,0},{5,7},{6,2},{7,5},{8,12},{9,11},{10,... | collective-permute-start | bytes 614408 | tf_op jit(solution)/shard_map/ppermute | solution.py:239
  31.5 0.5 collective-permute-done.11.refs_1_
  32.0 0.3 shard_map.151
  32.3 0.9 %collective-permute-start.12 = (bf16[256,256]{1,0:T(8,128)(2,1)S(1)}, bf16[256,256]{1,0:T(8,128)(2,1)S(1)}, u32[]{:S(2)}, u32[]{:S(2)}) collective-permute-start(bf16[256,256]{1,0:T(8,128)(2,1)S(1)} %get-tuple-element.78.refs_4_), channel_id=1, source_target_pairs={{0,4},{1,3},{2,6},{3,1},{4,0},{5,7},{6,2},{7,5},{8,12},{9,11},{10,... | collective-permute-start | bytes 393224 | tf_op jit(solution)/shard_map/ppermute | solution.py:239
  33.2 4.8 %collective-permute-done.12.refs_3_ = bf16[256,256]{1,0:T(8,128)(2,1)S(1)} collective-permute-done((bf16[256,256]{1,0:T(8,128)(2,1)S(1)}, bf16[256,256]{1,0:T(8,128)(2,1)S(1)}, u32[]{:S(2)}, u32[]{:S(2)}) %collective-permute-start.12) | collective-permute-done | bytes 131104 | tf_op jit(solution)/shard_map/ppermute | solution.py:239
  38.0 0.1 shard_map.152
  38.2 2.7 %collective-permute-start.13 = (bf16[336,256]{1,0:T(8,128)(2,1)S(1)}, bf16[336,256]{1,0:T(8,128)(2,1)S(1)}, u32[]{:S(2)}, u32[]{:S(2)}) collective-permute-start(bf16[336,256]{1,0:T(8,128)(2,1)S(1)} %get-tuple-element.80), channel_id=1, source_target_pairs={{0,12},{1,13},{2,14},{3,15},{4,8},{5,9},{6,10},{7,11},{8,4},{9,5},... | collective-permute-start | bytes 516104 | tf_op jit(solution)/shard_map/ppermute | solution.py:239
  40.9 1.2 %collective-permute-start.16 = (bf16[192,256]{1,0:T(8,128)(2,1)S(1)}, bf16[192,256]{1,0:T(8,128)(2,1)S(1)}, u32[]{:S(2)}, u32[]{:S(2)}) collective-permute-start(bf16[192,256]{1,0:T(8,128)(2,1)S(1)} %get-tuple-element.89), channel_id=1, source_target_pairs={{0,12},{1,13},{2,14},{3,15},{4,8},{5,9},{6,10},{7,11},{8,4},{9,5},... | collective-permute-start | bytes 294920 | tf_op jit(solution)/shard_map/ppermute | solution.py:239
  42.1 4.5 %collective-permute-done.13.refs_1_ = bf16[336,256]{1,0:T(8,128)(2,1)S(1)} collective-permute-done((bf16[336,256]{1,0:T(8,128)(2,1)S(1)}, bf16[336,256]{1,0:T(8,128)(2,1)S(1)}, u32[]{:S(2)}, u32[]{:S(2)}) %collective-permute-start.13) | collective-permute-done | bytes 172064 | tf_op jit(solution)/shard_map/ppermute | solution.py:239
  46.6 3.9 %collective-permute-start.15 = (bf16[192,256]{1,0:T(8,128)(2,1)S(1)}, bf16[192,256]{1,0:T(8,128)(2,1)S(1)}, u32[]{:S(2)}, u32[]{:S(2)}) collective-permute-start(bf16[192,256]{1,0:T(8,128)(2,1)S(1)} %get-tuple-element.87.refs_2_.refs_0_), channel_id=1, source_target_pairs={{0,4},{1,3},{2,6},{3,1},{4,0},{5,7},{6,2},{7,5},{8,12},{9,11},{10,... | collective-permute-start | bytes 294920 | tf_op jit(solution)/shard_map/ppermute | solution.py:239
  50.5 0.0 collective-permute-done.16.refs_1_
  50.6 1.0 %collective-permute-start.18 = (bf16[192,256]{1,0:T(8,128)(2,1)S(1)}, bf16[192,256]{1,0:T(8,128)(2,1)S(1)}, u32[]{:S(2)}, u32[]{:S(2)}) collective-permute-start(bf16[192,256]{1,0:T(8,128)(2,1)S(1)} %shard_map.156.refs_2_.refs_0_), channel_id=1, source_target_pairs={{0,4},{1,3},{2,6},{3,1},{4,0},{5,7},{6,2},{7,5},{8,12},{9,11},{10,... | collective-permute-start | bytes 294920 | tf_op jit(solution)/shard_map/ppermute | solution.py:239
  51.6 1.5 %collective-permute-done.15.refs_1_ = bf16[192,256]{1,0:T(8,128)(2,1)S(1)} collective-permute-done((bf16[192,256]{1,0:T(8,128)(2,1)S(1)}, bf16[192,256]{1,0:T(8,128)(2,1)S(1)}, u32[]{:S(2)}, u32[]{:S(2)}) %collective-permute-start.15) | collective-permute-done | bytes 98336 | tf_op jit(solution)/shard_map/ppermute | solution.py:239
  53.2 3.0 %collective-permute-done.18.refs_1_ = bf16[192,256]{1,0:T(8,128)(2,1)S(1)} collective-permute-done((bf16[192,256]{1,0:T(8,128)(2,1)S(1)}, bf16[192,256]{1,0:T(8,128)(2,1)S(1)}, u32[]{:S(2)}, u32[]{:S(2)}) %collective-permute-start.18) | collective-permute-done | bytes 98336 | tf_op jit(solution)/shard_map/ppermute | solution.py:239
  56.2 1.7 %collective-permute-start.19 = (bf16[384,256]{1,0:T(8,128)(2,1)S(1)}, bf16[384,256]{1,0:T(8,128)(2,1)S(1)}, u32[]{:S(2)}, u32[]{:S(2)}) collective-permute-start(bf16[384,256]{1,0:T(8,128)(2,1)S(1)} %shard_map.158.refs_2_), channel_id=1, source_target_pairs={{0,2},{1,5},{2,0},{3,7},{4,6},{5,1},{6,4},{7,3},{8,10},{9,13},{10,... | collective-permute-start | bytes 589832 | tf_op jit(solution)/shard_map/ppermute | solution.py:239
  57.9 0.4 collective-permute-start.17
  58.3 0.0 collective-permute-start.8
  58.3 0.2 shard_map.153
  58.5 0.6 collective-permute-start.14
  59.1 0.6 collective-permute-done.8.refs_1_
  59.7 0.3 collective-permute-done.14.refs_3_
  60.0 0.8 %shard_map.155 = (f32[320,256]{1,0:T(8,128)}, bf16[128,256]{1,0:T(8,128)(2,1)}, f32[6,256]{1,0:T(8,128)}) custom-call(f32[320,256]{1,0:T(8,128)S(1)} %get-tuple-element.68.refs_0_, bf16[320,256]{1,0:T(8,128)(2,1)S(1)} %collective-permute-done.8.refs_1_, f32[128,256]{1,0:T(8,128)S(1)} %get-tuple-element.81.refs_2_, ...), custom_call_target="tpu_custom_call" | custom-call | tf_op jit(solution)/shard_map/pallas_call | solution.py:32
  60.8 1.1 %collective-permute-done.19.refs_3_ = bf16[384,256]{1,0:T(8,128)(2,1)S(1)} collective-permute-done((bf16[384,256]{1,0:T(8,128)(2,1)S(1)}, bf16[384,256]{1,0:T(8,128)(2,1)S(1)}, u32[]{:S(2)}, u32[]{:S(2)}) %collective-permute-start.19) | collective-permute-done | bytes 196640 | tf_op jit(solution)/shard_map/ppermute | solution.py:239
  62.0 2.1 %collective-permute-done.17.refs_1_ = bf16[384,256]{1,0:T(8,128)(2,1)S(1)} collective-permute-done((bf16[384,256]{1,0:T(8,128)(2,1)S(1)}, bf16[384,256]{1,0:T(8,128)(2,1)S(1)}, u32[]{:S(2)}, u32[]{:S(2)}) %collective-permute-start.17) | collective-permute-done | bytes 196640 | tf_op jit(solution)/shard_map/ppermute | solution.py:239
  64.1 1.2 %shard_map.159 = (f32[512,256]{1,0:T(8,128)}, f32[256,512]{1,0:T(8,128)}, f32[512,256]{1,0:T(8,128)}) custom-call(bf16[384,256]{1,0:T(8,128)(2,1)S(1)} %shard_map.157.refs_2_.refs_0_, bf16[384,256]{1,0:T(8,128)(2,1)S(1)} %collective-permute-done.17.refs_1_, bf16[384,256]{1,0:T(8,128)(2,1)S(1)} %shard_map.158.refs_2_, ...), custom_call_target="tpu_custom_call" | custom-call | tf_op jit(solution)/shard_map/pallas_call | solution.py:32
  (7 shorter events, 0.1 us)
Async XLA Ops:
  1.9 11.0 %collective-permute-start = (bf16[144,128]{1,0:T(8,128)(2,1)S(1)}, bf16[144,128]{1,0:T(8,128)(2,1)S(1)}, u32[]{:S(2)}, u32[]{:S(2)}) collective-permute-start(bf16[144,128]{1,0:T(8,128)(2,1)S(1)} %get-tuple-element.51), channel_id=1, source_target_pairs={{0,2},{2,4},{4,6},{6,8},{8,10},{10,12},{12,14},{14,0},{1,3},{3,5},... | collective-permute-start | bytes 110600 | tf_op jit(solution)/shard_map/ppermute | solution.py:79
  4.9 9.3 %collective-permute-start.1 = (bf16[144,128]{1,0:T(8,128)(2,1)S(1)}, bf16[144,128]{1,0:T(8,128)(2,1)S(1)}, u32[]{:S(2)}, u32[]{:S(2)}) collective-permute-start(bf16[144,128]{1,0:T(8,128)(2,1)S(1)} %get-tuple-element.52), channel_id=1, source_target_pairs={{0,4},{2,6},{4,8},{6,10},{8,12},{10,14},{12,0},{14,2},{1,5},{3,7},... | collective-permute-start | bytes 110600 | tf_op jit(solution)/shard_map/ppermute | solution.py:79
  6.5 10.9 %collective-permute-start.2 = (bf16[144,128]{1,0:T(8,128)(2,1)S(1)}, bf16[144,128]{1,0:T(8,128)(2,1)S(1)}, u32[]{:S(2)}, u32[]{:S(2)}) collective-permute-start(bf16[144,128]{1,0:T(8,128)(2,1)S(1)} %get-tuple-element.53), channel_id=1, source_target_pairs={{0,6},{2,8},{4,10},{6,12},{8,14},{10,0},{12,2},{14,4},{1,7},{3,9},... | collective-permute-start | bytes 110600 | tf_op jit(solution)/shard_map/ppermute | solution.py:79
  9.1 8.4 %collective-permute-start.3 = (bf16[144,128]{1,0:T(8,128)(2,1)S(1)}, bf16[144,128]{1,0:T(8,128)(2,1)S(1)}, u32[]{:S(2)}, u32[]{:S(2)}) collective-permute-start(bf16[144,128]{1,0:T(8,128)(2,1)S(1)} %get-tuple-element.54), channel_id=1, source_target_pairs={{0,8},{2,10},{4,12},{6,14},{8,0},{10,2},{12,4},{14,6},{1,9},{3,11}... | collective-permute-start | bytes 110600 | tf_op jit(solution)/shard_map/ppermute | solution.py:79
  10.3 7.2 %collective-permute-start.4 = (bf16[144,128]{1,0:T(8,128)(2,1)S(1)}, bf16[144,128]{1,0:T(8,128)(2,1)S(1)}, u32[]{:S(2)}, u32[]{:S(2)}) collective-permute-start(bf16[144,128]{1,0:T(8,128)(2,1)S(1)} %get-tuple-element.55), channel_id=1, source_target_pairs={{0,10},{2,12},{4,14},{6,0},{8,2},{10,4},{12,6},{14,8},{1,11},{3,13... | collective-permute-start | bytes 110600 | tf_op jit(solution)/shard_map/ppermute | solution.py:79
  12.9 4.5 %collective-permute-start.5 = (bf16[144,128]{1,0:T(8,128)(2,1)S(1)}, bf16[144,128]{1,0:T(8,128)(2,1)S(1)}, u32[]{:S(2)}, u32[]{:S(2)}) collective-permute-start(bf16[144,128]{1,0:T(8,128)(2,1)S(1)} %get-tuple-element.56), channel_id=1, source_target_pairs={{0,12},{2,14},{4,0},{6,2},{8,4},{10,6},{12,8},{14,10},{1,13},{3,15... | collective-permute-start | bytes 110600 | tf_op jit(solution)/shard_map/ppermute | solution.py:79
  14.3 4.0 %collective-permute-start.6 = (bf16[144,128]{1,0:T(8,128)(2,1)S(1)}, bf16[144,128]{1,0:T(8,128)(2,1)S(1)}, u32[]{:S(2)}, u32[]{:S(2)}) collective-permute-start(bf16[144,128]{1,0:T(8,128)(2,1)S(1)} %get-tuple-element.57), channel_id=1, source_target_pairs={{0,14},{2,0},{4,2},{6,4},{8,6},{10,8},{12,10},{14,12},{1,15},{3,1}... | collective-permute-start | bytes 110600 | tf_op jit(solution)/shard_map/ppermute | solution.py:79
  18.3 1.6 %collective-permute-start.7 = (bf16[7,144,128]{2,1,0:T(8,128)(2,1)S(1)}, bf16[7,144,128]{2,1,0:T(8,128)(2,1)S(1)}, u32[]{:S(2)}, u32[]{:S(2)}) collective-permute-start(bf16[7,144,128]{2,1,0:T(8,128)(2,1)S(1)} %shard_map.147.refs_1_), channel_id=1, source_target_pairs={{0,1},{1,0},{2,3},{3,2},{4,5},{5,4},{6,7},{7,6},{8,9},{9,8},{10,11... | collective-permute-start | bytes 774152 | tf_op jit(solution)/shard_map/ppermute | solution.py:79
  22.7 7.9 %collective-permute-start.9 = (bf16[784,256]{1,0:T(8,128)(2,1)S(1)}, bf16[784,256]{1,0:T(8,128)(2,1)S(1)}, u32[]{:S(2)}, u32[]{:S(2)}) collective-permute-start(bf16[784,256]{1,0:T(8,128)(2,1)S(1)} %get-tuple-element.71), channel_id=1, source_target_pairs={{0,2},{1,5},{2,0},{3,7},{4,6},{5,1},{6,4},{7,3},{8,10},{9,13},{10,... | collective-permute-start | bytes 1204232 | tf_op jit(solution)/shard_map/ppermute | solution.py:239
  24.3 7.7 %collective-permute-start.11 = (bf16[256,256]{1,0:T(8,128)(2,1)S(1)}, bf16[256,256]{1,0:T(8,128)(2,1)S(1)}, u32[]{:S(2)}, u32[]{:S(2)}) collective-permute-start(bf16[256,256]{1,0:T(8,128)(2,1)S(1)} %get-tuple-element.75), channel_id=1, source_target_pairs={{0,2},{1,5},{2,0},{3,7},{4,6},{5,1},{6,4},{7,3},{8,10},{9,13},{10,... | collective-permute-start | bytes 393224 | tf_op jit(solution)/shard_map/ppermute | solution.py:239
  30.8 7.2 %collective-permute-start.10 = (bf16[400,256]{1,0:T(8,128)(2,1)S(1)}, bf16[400,256]{1,0:T(8,128)(2,1)S(1)}, u32[]{:S(2)}, u32[]{:S(2)}) collective-permute-start(bf16[400,256]{1,0:T(8,128)(2,1)S(1)} %get-tuple-element.73.refs_3_), channel_id=1, source_target_pairs={{0,4},{1,3},{2,6},{3,1},{4,0},{5,7},{6,2},{7,5},{8,12},{9,11},{10,... | collective-permute-start | bytes 614408 | tf_op jit(solution)/shard_map/ppermute | solution.py:239
  32.3 5.7 %collective-permute-start.12 = (bf16[256,256]{1,0:T(8,128)(2,1)S(1)}, bf16[256,256]{1,0:T(8,128)(2,1)S(1)}, u32[]{:S(2)}, u32[]{:S(2)}) collective-permute-start(bf16[256,256]{1,0:T(8,128)(2,1)S(1)} %get-tuple-element.78.refs_4_), channel_id=1, source_target_pairs={{0,4},{1,3},{2,6},{3,1},{4,0},{5,7},{6,2},{7,5},{8,12},{9,11},{10,... | collective-permute-start | bytes 393224 | tf_op jit(solution)/shard_map/ppermute | solution.py:239
  38.2 8.4 %collective-permute-start.13 = (bf16[336,256]{1,0:T(8,128)(2,1)S(1)}, bf16[336,256]{1,0:T(8,128)(2,1)S(1)}, u32[]{:S(2)}, u32[]{:S(2)}) collective-permute-start(bf16[336,256]{1,0:T(8,128)(2,1)S(1)} %get-tuple-element.80), channel_id=1, source_target_pairs={{0,12},{1,13},{2,14},{3,15},{4,8},{5,9},{6,10},{7,11},{8,4},{9,5},... | collective-permute-start | bytes 516104 | tf_op jit(solution)/shard_map/ppermute | solution.py:239
  40.9 9.6 %collective-permute-start.16 = (bf16[192,256]{1,0:T(8,128)(2,1)S(1)}, bf16[192,256]{1,0:T(8,128)(2,1)S(1)}, u32[]{:S(2)}, u32[]{:S(2)}) collective-permute-start(bf16[192,256]{1,0:T(8,128)(2,1)S(1)} %get-tuple-element.89), channel_id=1, source_target_pairs={{0,12},{1,13},{2,14},{3,15},{4,8},{5,9},{6,10},{7,11},{8,4},{9,5},... | collective-permute-start | bytes 294920 | tf_op jit(solution)/shard_map/ppermute | solution.py:239
  46.6 6.5 %collective-permute-start.15 = (bf16[192,256]{1,0:T(8,128)(2,1)S(1)}, bf16[192,256]{1,0:T(8,128)(2,1)S(1)}, u32[]{:S(2)}, u32[]{:S(2)}) collective-permute-start(bf16[192,256]{1,0:T(8,128)(2,1)S(1)} %get-tuple-element.87.refs_2_.refs_0_), channel_id=1, source_target_pairs={{0,4},{1,3},{2,6},{3,1},{4,0},{5,7},{6,2},{7,5},{8,12},{9,11},{10,... | collective-permute-start | bytes 294920 | tf_op jit(solution)/shard_map/ppermute | solution.py:239
  50.6 5.6 %collective-permute-start.18 = (bf16[192,256]{1,0:T(8,128)(2,1)S(1)}, bf16[192,256]{1,0:T(8,128)(2,1)S(1)}, u32[]{:S(2)}, u32[]{:S(2)}) collective-permute-start(bf16[192,256]{1,0:T(8,128)(2,1)S(1)} %shard_map.156.refs_2_.refs_0_), channel_id=1, source_target_pairs={{0,4},{1,3},{2,6},{3,1},{4,0},{5,7},{6,2},{7,5},{8,12},{9,11},{10,... | collective-permute-start | bytes 294920 | tf_op jit(solution)/shard_map/ppermute | solution.py:239
  56.2 5.7 %collective-permute-start.19 = (bf16[384,256]{1,0:T(8,128)(2,1)S(1)}, bf16[384,256]{1,0:T(8,128)(2,1)S(1)}, u32[]{:S(2)}, u32[]{:S(2)}) collective-permute-start(bf16[384,256]{1,0:T(8,128)(2,1)S(1)} %shard_map.158.refs_2_), channel_id=1, source_target_pairs={{0,2},{1,5},{2,0},{3,7},{4,6},{5,1},{6,4},{7,3},{8,10},{9,13},{10,... | collective-permute-start | bytes 589832 | tf_op jit(solution)/shard_map/ppermute | solution.py:239
  57.9 6.2 %collective-permute-start.17 = (bf16[384,256]{1,0:T(8,128)(2,1)S(1)}, bf16[384,256]{1,0:T(8,128)(2,1)S(1)}, u32[]{:S(2)}, u32[]{:S(2)}) collective-permute-start(bf16[384,256]{1,0:T(8,128)(2,1)S(1)} %shard_map.157.refs_2_.refs_0_), channel_id=1, source_target_pairs={{0,2},{1,5},{2,0},{3,7},{4,6},{5,1},{6,4},{7,3},{8,10},{9,13},{10,... | collective-permute-start | bytes 589832 | tf_op jit(solution)/shard_map/ppermute | solution.py:239
  58.3 1.4 %collective-permute-start.8 = (bf16[320,256]{1,0:T(8,128)(2,1)S(1)}, bf16[320,256]{1,0:T(8,128)(2,1)S(1)}, u32[]{:S(2)}, u32[]{:S(2)}) collective-permute-start(bf16[320,256]{1,0:T(8,128)(2,1)S(1)} %get-tuple-element.69), channel_id=1, source_target_pairs={{0,1},{1,0},{2,3},{3,2},{4,5},{5,4},{6,7},{7,6},{8,9},{9,8},{10,11... | collective-permute-start | bytes 491528 | tf_op jit(solution)/shard_map/ppermute | solution.py:79
  58.5 1.5 %collective-permute-start.14 = (bf16[128,256]{1,0:T(8,128)(2,1)S(1)}, bf16[128,256]{1,0:T(8,128)(2,1)S(1)}, u32[]{:S(2)}, u32[]{:S(2)}) collective-permute-start(bf16[128,256]{1,0:T(8,128)(2,1)S(1)} %get-tuple-element.82), channel_id=1, source_target_pairs={{0,1},{1,0},{2,3},{3,2},{4,5},{5,4},{6,7},{7,6},{8,9},{9,8},{10,11... | collective-permute-start | bytes 196616 | tf_op jit(solution)/shard_map/ppermute | solution.py:79

commit v15 on v13

--- a/solution.py
+++ b/solution.py
@@ -577,8 +577,13 @@
             )
         )
     node_got = shift(node_theirs, "mp", 1)
-    everyone = list(range(len(chains)))
-    turns = everyone * (len(steps) - 2) + [0] + everyone[1:] * (2 + len(halving_used(steps, rows)) - 1)
+    middle, last = len(steps) - 1, len(steps) + len(halving_used(steps, rows)) - 1
+    turns = [1]
+    for step in range(1, last):
+        turns += [2, 1] if step == middle else [1, 2]
+        turns += [0] if step < middle else []
+        turns += [0] if step == middle - 1 else []
+    turns += [2]
     _, *weights = in_turns(chains, turns)
     obs_keep, arrived = weights[-1][2]
     obs_mine, obs_theirs = call(

time: 66.2 us -> 62.1 us (0.938)
  waiting for transfers between devices: 24.8 us -> 22 us
  starting transfers between devices: 31.5 us -> 30.3 us
    ppermute x12, waiting for transfers between devices: 21.6 us -> 18.8 us  [flip(): return lax.ppermute(value, axes, pairs)]
    ppermute x12, starting transfers between devices: 17.1 us -> 15.9 us  [flip(): return lax.ppermute(value, axes, pairs)]
where the time goes in v15:
time: 62.1 us; the launch traced here: 62 us
  starting transfers between devices  30.3 us (49%)
  waiting for transfers between devices  22 us (35%)
  Pallas kernels  8.85 us (14%)
  between operations  0.81 us (1%)
    ppermute x12, waiting for transfers between devices, flip(): return lax.ppermute(value, axes, pairs)  18.8 us
    ppermute x12, starting transfers between devices, flip(): return lax.ppermute(value, axes, pairs)  15.9 us
    ppermute x10, starting transfers between devices, shift(): lax.ppermute(value, axis, [(i, (i + step) % size) for i in range(size)])  14.4 us
    pallas_call x15, Pallas kernels, call(): pl.pallas_call(lambda *refs: kernel(*refs[:count], *refs[len(args):]), ou...  5.83 us
    ppermute x10, waiting for transfers between devices, shift(): lax.ppermute(value, axis, [(i, (i + step) % size) for i in range(size)])  3.19 us
    pallas_call x2, Pallas kernels, call_staged(): pl.pallas_call(staged, out_shape=[jax.ShapeDtypeStruct(shape, dtype) for...  3.03 us
  transfers between devices with their start and end apart: 22, of which 10 were waited for; matrix products, arithmetic and copies ran while one was open for 0% of the time, Pallas kernels for 5%

profile of v15, /device:TPU:0, one launch (start us, length us, event | category | flops | bytes accessed | tf_op | source)
XLA Modules:
  0.0 62.0 jit_solution(10702092234805917199)
XLA Ops:
  0.6 1.3 %shard_map.145 = (bf16[144,128]{1,0:T(8,128)(2,1)S(1)}, bf16[144,128]{1,0:T(8,128)(2,1)S(1)}, bf16[144,128]{1,0:T(8,128)(2,1)S(1)}, bf16[144,128]{1,0:T(8,128)(2...) custom-call(bf16[128,512]{1,0:T(8,128)(2,1)} %refs_0_.2, ...), custom_call_target="tpu_custom_call" | custom-call | tf_op jit(solution)/shard_map/pallas_call | solution.py:61
  1.9 3.0 %collective-permute-start = (bf16[144,128]{1,0:T(8,128)(2,1)S(1)}, bf16[144,128]{1,0:T(8,128)(2,1)S(1)}, u32[]{:S(2)}, u32[]{:S(2)}) collective-permute-start(bf16[144,128]{1,0:T(8,128)(2,1)S(1)} %get-tuple-element.55), channel_id=1, source_target_pairs={{0,2},{2,4},{4,6},{6,8},{8,10},{10,12},{12,14},{14,0},{1,3},{3,5},... | collective-permute-start | bytes 110600 | tf_op jit(solution)/shard_map/ppermute | solution.py:79
  4.9 1.6 %collective-permute-start.1 = (bf16[144,128]{1,0:T(8,128)(2,1)S(1)}, bf16[144,128]{1,0:T(8,128)(2,1)S(1)}, u32[]{:S(2)}, u32[]{:S(2)}) collective-permute-start(bf16[144,128]{1,0:T(8,128)(2,1)S(1)} %get-tuple-element.56), channel_id=1, source_target_pairs={{0,4},{2,6},{4,8},{6,10},{8,12},{10,14},{12,0},{14,2},{1,5},{3,7},... | collective-permute-start | bytes 110600 | tf_op jit(solution)/shard_map/ppermute | solution.py:79
  6.5 2.6 %collective-permute-start.2 = (bf16[144,128]{1,0:T(8,128)(2,1)S(1)}, bf16[144,128]{1,0:T(8,128)(2,1)S(1)}, u32[]{:S(2)}, u32[]{:S(2)}) collective-permute-start(bf16[144,128]{1,0:T(8,128)(2,1)S(1)} %get-tuple-element.57), channel_id=1, source_target_pairs={{0,6},{2,8},{4,10},{6,12},{8,14},{10,0},{12,2},{14,4},{1,7},{3,9},... | collective-permute-start | bytes 110600 | tf_op jit(solution)/shard_map/ppermute | solution.py:79
  9.1 1.2 %collective-permute-start.3 = (bf16[144,128]{1,0:T(8,128)(2,1)S(1)}, bf16[144,128]{1,0:T(8,128)(2,1)S(1)}, u32[]{:S(2)}, u32[]{:S(2)}) collective-permute-start(bf16[144,128]{1,0:T(8,128)(2,1)S(1)} %get-tuple-element.58), channel_id=1, source_target_pairs={{0,8},{2,10},{4,12},{6,14},{8,0},{10,2},{12,4},{14,6},{1,9},{3,11}... | collective-permute-start | bytes 110600 | tf_op jit(solution)/shard_map/ppermute | solution.py:79
  10.3 2.6 %collective-permute-start.4 = (bf16[144,128]{1,0:T(8,128)(2,1)S(1)}, bf16[144,128]{1,0:T(8,128)(2,1)S(1)}, u32[]{:S(2)}, u32[]{:S(2)}) collective-permute-start(bf16[144,128]{1,0:T(8,128)(2,1)S(1)} %get-tuple-element.59), channel_id=1, source_target_pairs={{0,10},{2,12},{4,14},{6,0},{8,2},{10,4},{12,6},{14,8},{1,11},{3,13... | collective-permute-start | bytes 110600 | tf_op jit(solution)/shard_map/ppermute | solution.py:79
  12.9 1.4 %collective-permute-start.5 = (bf16[144,128]{1,0:T(8,128)(2,1)S(1)}, bf16[144,128]{1,0:T(8,128)(2,1)S(1)}, u32[]{:S(2)}, u32[]{:S(2)}) collective-permute-start(bf16[144,128]{1,0:T(8,128)(2,1)S(1)} %get-tuple-element.60), channel_id=1, source_target_pairs={{0,12},{2,14},{4,0},{6,2},{8,4},{10,6},{12,8},{14,10},{1,13},{3,15... | collective-permute-start | bytes 110600 | tf_op jit(solution)/shard_map/ppermute | solution.py:79
  14.3 0.0 collective-permute-done.1.refs_1_
  14.3 1.4 %collective-permute-start.6 = (bf16[144,128]{1,0:T(8,128)(2,1)S(1)}, bf16[144,128]{1,0:T(8,128)(2,1)S(1)}, u32[]{:S(2)}, u32[]{:S(2)}) collective-permute-start(bf16[144,128]{1,0:T(8,128)(2,1)S(1)} %get-tuple-element.61), channel_id=1, source_target_pairs={{0,14},{2,0},{4,2},{6,4},{8,6},{10,8},{12,10},{14,12},{1,15},{3,1}... | collective-permute-start | bytes 110600 | tf_op jit(solution)/shard_map/ppermute | solution.py:79
  15.7 1.7 %shard_map.146 = (bf16[336,1024]{1,0:T(8,128)(2,1)S(1)}, bf16[320,512]{1,0:T(8,128)(2,1)S(1)}, bf16[320,512]{1,0:T(8,128)(2,1)S(1)}, bf16[512,256]{1,0:T(8,128)(2,1)S(1)}, bf16[512,256]{1,0:T(8,128)(2,1)S(1)}) custom-call(bf16[320,512]{1,0:T(8,128)(2,1)} %refs_0_.3, bf16[320,512]{1,0:T(8,128)(2,1)} %refs_1_.1, bf16[512,256]{1,0:T(8,128)(2,1)} %refs_2_.1, ...), custom_call_target="tpu_custom_call" | custom-call | tf_op jit(solution)/shard_map/pallas_call | solution.py:61
  17.5 0.0 collective-permute-done.3.refs_3_
  17.5 0.0 collective-permute-done.4.refs_4_
  17.5 0.8 %collective-permute-done.6.refs_6_ = bf16[144,128]{1,0:T(8,128)(2,1)S(1)} collective-permute-done((bf16[144,128]{1,0:T(8,128)(2,1)S(1)}, bf16[144,128]{1,0:T(8,128)(2,1)S(1)}, u32[]{:S(2)}, u32[]{:S(2)}) %collective-permute-start.6) | collective-permute-done | bytes 36896 | tf_op jit(solution)/shard_map/ppermute | solution.py:79
  18.3 0.1 collective-permute-start.7
  18.3 1.5 %collective-permute-done.7.refs_3_ = bf16[7,144,128]{2,1,0:T(8,128)(2,1)S(1)} collective-permute-done((bf16[7,144,128]{2,1,0:T(8,128)(2,1)S(1)}, bf16[7,144,128]{2,1,0:T(8,128)(2,1)S(1)}, u32[]{:S(2)}, u32[]{:S(2)}) %collective-permute-start.7) | collective-permute-done | bytes 258080 | tf_op jit(solution)/shard_map/ppermute | solution.py:79
  19.9 1.6 %shard_map.148 = (bf16[512,512]{1,0:T(8,128)(2,1)S(1)}, bf16[512,336]{1,0:T(8,128)(2,1)S(1)}, bf16[512,256]{1,0:T(8,128)(2,1)S(1)}, bf16[512,256]{1,0:T(8,128)(2...) custom-call(bf16[144,128]{1,0:T(8,128)(2,1)S(1)} %get-tuple-element.54.refs_0_, ...), custom_call_target="tpu_custom_call" | custom-call | tf_op jit(solution)/shard_map/pallas_call | solution.py:32
  21.5 1.3 %shard_map.149 = (f32[320,256]{1,0:T(8,128)S(1)}, bf16[320,256]{1,0:T(8,128)(2,1)S(1)}, f32[384,256]{1,0:T(8,128)S(1)}, bf16[384,256]{1,0:T(8,128)(2,1)S(1)}, f3...) custom-call(bf16[512,336]{1,0:T(8,128)(2,1)S(1)} %get-tuple-element.65.refs_0_, ...), custom_call_target="tpu_custom_call" | custom-call | tf_op jit(solution)/shard_map/pallas_call | solution.py:32
  22.8 1.6 %collective-permute-start.10 = (bf16[384,256]{1,0:T(8,128)(2,1)S(1)}, bf16[384,256]{1,0:T(8,128)(2,1)S(1)}, u32[]{:S(2)}, u32[]{:S(2)}) collective-permute-start(bf16[384,256]{1,0:T(8,128)(2,1)S(1)} %get-tuple-element.77), channel_id=1, source_target_pairs={{0,2},{1,5},{2,0},{3,7},{4,6},{5,1},{6,4},{7,3},{8,10},{9,13},{10,... | collective-permute-start | bytes 589832 | tf_op jit(solution)/shard_map/ppermute | solution.py:239
  24.4 0.5 collective-permute-start.9
  24.9 1.5 %collective-permute-start.13 = (bf16[256,256]{1,0:T(8,128)(2,1)S(1)}, bf16[256,256]{1,0:T(8,128)(2,1)S(1)}, u32[]{:S(2)}, u32[]{:S(2)}) collective-permute-start(bf16[256,256]{1,0:T(8,128)(2,1)S(1)} %get-tuple-element.84), channel_id=1, source_target_pairs={{0,2},{1,5},{2,0},{3,7},{4,6},{5,1},{6,4},{7,3},{8,10},{9,13},{10,... | collective-permute-start | bytes 393224 | tf_op jit(solution)/shard_map/ppermute | solution.py:239
  26.4 2.1 %collective-permute-done.10.refs_1_ = bf16[384,256]{1,0:T(8,128)(2,1)S(1)} collective-permute-done((bf16[384,256]{1,0:T(8,128)(2,1)S(1)}, bf16[384,256]{1,0:T(8,128)(2,1)S(1)}, u32[]{:S(2)}, u32[]{:S(2)}) %collective-permute-start.10) | collective-permute-done | bytes 196640 | tf_op jit(solution)/shard_map/ppermute | solution.py:239
  28.5 0.1 shard_map.150
  28.6 0.7 %collective-permute-start.11 = (bf16[192,256]{1,0:T(8,128)(2,1)S(1)}, bf16[192,256]{1,0:T(8,128)(2,1)S(1)}, u32[]{:S(2)}, u32[]{:S(2)}) collective-permute-start(bf16[192,256]{1,0:T(8,128)(2,1)S(1)} %get-tuple-element.79.refs_2_), channel_id=1, source_target_pairs={{0,4},{1,3},{2,6},{3,1},{4,0},{5,7},{6,2},{7,5},{8,12},{9,11},{10,... | collective-permute-start | bytes 294920 | tf_op jit(solution)/shard_map/ppermute | solution.py:239
  29.3 3.9 %collective-permute-done.11.refs_1_ = bf16[192,256]{1,0:T(8,128)(2,1)S(1)} collective-permute-done((bf16[192,256]{1,0:T(8,128)(2,1)S(1)}, bf16[192,256]{1,0:T(8,128)(2,1)S(1)}, u32[]{:S(2)}, u32[]{:S(2)}) %collective-permute-start.11) | collective-permute-done | bytes 98336 | tf_op jit(solution)/shard_map/ppermute | solution.py:239
  33.3 0.1 shard_map.152
  33.4 0.0 collective-permute-done.13.refs_1_
  33.4 0.3 shard_map.153
  33.7 0.7 %collective-permute-start.14 = (bf16[256,256]{1,0:T(8,128)(2,1)S(1)}, bf16[256,256]{1,0:T(8,128)(2,1)S(1)}, u32[]{:S(2)}, u32[]{:S(2)}) collective-permute-start(bf16[256,256]{1,0:T(8,128)(2,1)S(1)} %get-tuple-element.87.refs_4_), channel_id=1, source_target_pairs={{0,4},{1,3},{2,6},{3,1},{4,0},{5,7},{6,2},{7,5},{8,12},{9,11},{10,... | collective-permute-start | bytes 393224 | tf_op jit(solution)/shard_map/ppermute | solution.py:239
  34.5 1.3 %collective-permute-start.12 = (bf16[208,256]{1,0:T(8,128)(2,1)S(1)}, bf16[208,256]{1,0:T(8,128)(2,1)S(1)}, u32[]{:S(2)}, u32[]{:S(2)}) collective-permute-start(bf16[208,256]{1,0:T(8,128)(2,1)S(1)} %get-tuple-element.82.refs_3_), channel_id=1, source_target_pairs={{0,4},{1,3},{2,6},{3,1},{4,0},{5,7},{6,2},{7,5},{8,12},{9,11},{10,... | collective-permute-start | bytes 319496 | tf_op jit(solution)/shard_map/ppermute | solution.py:239
  35.8 2.7 %collective-permute-start.17 = (bf16[192,256]{1,0:T(8,128)(2,1)S(1)}, bf16[192,256]{1,0:T(8,128)(2,1)S(1)}, u32[]{:S(2)}, u32[]{:S(2)}) collective-permute-start(bf16[192,256]{1,0:T(8,128)(2,1)S(1)} %get-tuple-element.80.refs_2_), channel_id=1, source_target_pairs={{0,12},{1,13},{2,14},{3,15},{4,8},{5,9},{6,10},{7,11},{8,4},{9,5},... | collective-permute-start | bytes 294920 | tf_op jit(solution)/shard_map/ppermute | solution.py:239
  38.5 2.5 %collective-permute-done.12.refs_1_ = bf16[208,256]{1,0:T(8,128)(2,1)S(1)} collective-permute-done((bf16[208,256]{1,0:T(8,128)(2,1)S(1)}, bf16[208,256]{1,0:T(8,128)(2,1)S(1)}, u32[]{:S(2)}, u32[]{:S(2)}) %collective-permute-start.12) | collective-permute-done | bytes 106528 | tf_op jit(solution)/shard_map/ppermute | solution.py:239
  41.0 0.0 collective-permute-done.14.refs_3_
  41.0 0.1 shard_map.154
  41.1 2.7 %collective-permute-start.15 = (bf16[336,256]{1,0:T(8,128)(2,1)S(1)}, bf16[336,256]{1,0:T(8,128)(2,1)S(1)}, u32[]{:S(2)}, u32[]{:S(2)}) collective-permute-start(bf16[336,256]{1,0:T(8,128)(2,1)S(1)} %get-tuple-element.89.refs_2_), channel_id=1, source_target_pairs={{0,12},{1,13},{2,14},{3,15},{4,8},{5,9},{6,10},{7,11},{8,4},{9,5},... | collective-permute-start | bytes 516104 | tf_op jit(solution)/shard_map/ppermute | solution.py:239
  43.8 0.1 collective-permute-start.18
  43.9 5.6 %collective-permute-done.18.refs_1_ = bf16[192,256]{1,0:T(8,128)(2,1)S(1)} collective-permute-done((bf16[192,256]{1,0:T(8,128)(2,1)S(1)}, bf16[192,256]{1,0:T(8,128)(2,1)S(1)}, u32[]{:S(2)}, u32[]{:S(2)}) %collective-permute-start.18) | collective-permute-done | bytes 98336 | tf_op jit(solution)/shard_map/ppermute | solution.py:239
  49.6 1.0 %collective-permute-start.20 = (bf16[192,256]{1,0:T(8,128)(2,1)S(1)}, bf16[192,256]{1,0:T(8,128)(2,1)S(1)}, u32[]{:S(2)}, u32[]{:S(2)}) collective-permute-start(bf16[192,256]{1,0:T(8,128)(2,1)S(1)} %get-tuple-element.97.refs_0_.refs_2_), channel_id=1, source_target_pairs={{0,4},{1,3},{2,6},{3,1},{4,0},{5,7},{6,2},{7,5},{8,12},{9,11},{10,... | collective-permute-start | bytes 294920 | tf_op jit(solution)/shard_map/ppermute | solution.py:239
  50.6 1.9 %collective-permute-start.19 = (bf16[384,256]{1,0:T(8,128)(2,1)S(1)}, bf16[384,256]{1,0:T(8,128)(2,1)S(1)}, u32[]{:S(2)}, u32[]{:S(2)}) collective-permute-start(bf16[384,256]{1,0:T(8,128)(2,1)S(1)} %shard_map.157.refs_2_.refs_0_), channel_id=1, source_target_pairs={{0,2},{1,5},{2,0},{3,7},{4,6},{5,1},{6,4},{7,3},{8,10},{9,13},{10,... | collective-permute-start | bytes 589832 | tf_op jit(solution)/shard_map/ppermute | solution.py:239
  52.5 2.5 %collective-permute-done.20.refs_1_ = bf16[192,256]{1,0:T(8,128)(2,1)S(1)} collective-permute-done((bf16[192,256]{1,0:T(8,128)(2,1)S(1)}, bf16[192,256]{1,0:T(8,128)(2,1)S(1)}, u32[]{:S(2)}, u32[]{:S(2)}) %collective-permute-start.20) | collective-permute-done | bytes 98336 | tf_op jit(solution)/shard_map/ppermute | solution.py:239
  55.0 1.1 %collective-permute-start.21 = (bf16[384,256]{1,0:T(8,128)(2,1)S(1)}, bf16[384,256]{1,0:T(8,128)(2,1)S(1)}, u32[]{:S(2)}, u32[]{:S(2)}) collective-permute-start(bf16[384,256]{1,0:T(8,128)(2,1)S(1)} %shard_map.160.refs_2_), channel_id=1, source_target_pairs={{0,2},{1,5},{2,0},{3,7},{4,6},{5,1},{6,4},{7,3},{8,10},{9,13},{10,... | collective-permute-start | bytes 589832 | tf_op jit(solution)/shard_map/ppermute | solution.py:239
  56.1 0.2 shard_map.155
  56.3 0.6 collective-permute-start.16
  56.9 0.6 collective-permute-done.8.refs_1_
  57.5 0.3 collective-permute-done.16.refs_3_
  57.8 0.8 %shard_map.159 = (f32[320,256]{1,0:T(8,128)}, bf16[128,256]{1,0:T(8,128)(2,1)}, f32[6,256]{1,0:T(8,128)}) custom-call(f32[320,256]{1,0:T(8,128)S(1)} %get-tuple-element.72.refs_0_, bf16[320,256]{1,0:T(8,128)(2,1)S(1)} %collective-permute-done.8.refs_1_, f32[128,256]{1,0:T(8,128)S(1)} %get-tuple-element.90.refs_2_, ...), custom_call_target="tpu_custom_call" | custom-call | tf_op jit(solution)/shard_map/pallas_call | solution.py:32
  58.6 0.0 collective-permute-done.19.refs_1_
  58.6 2.2 %collective-permute-done.21.refs_3_ = bf16[384,256]{1,0:T(8,128)(2,1)S(1)} collective-permute-done((bf16[384,256]{1,0:T(8,128)(2,1)S(1)}, bf16[384,256]{1,0:T(8,128)(2,1)S(1)}, u32[]{:S(2)}, u32[]{:S(2)}) %collective-permute-start.21) | collective-permute-done | bytes 196640 | tf_op jit(solution)/shard_map/ppermute | solution.py:239
  60.8 1.2 %shard_map.161 = (f32[512,256]{1,0:T(8,128)}, f32[256,512]{1,0:T(8,128)}, f32[512,256]{1,0:T(8,128)}) custom-call(bf16[384,256]{1,0:T(8,128)(2,1)S(1)} %shard_map.157.refs_2_.refs_0_, bf16[384,256]{1,0:T(8,128)(2,1)S(1)} %collective-permute-done.19.refs_1_, bf16[384,256]{1,0:T(8,128)(2,1)S(1)} %shard_map.160.refs_2_, ...), custom_call_target="tpu_custom_call" | custom-call | tf_op jit(solution)/shard_map/pallas_call | solution.py:32
  (13 shorter events, 0.2 us)
Async XLA Ops:
  1.9 11.0 %collective-permute-start = (bf16[144,128]{1,0:T(8,128)(2,1)S(1)}, bf16[144,128]{1,0:T(8,128)(2,1)S(1)}, u32[]{:S(2)}, u32[]{:S(2)}) collective-permute-start(bf16[144,128]{1,0:T(8,128)(2,1)S(1)} %get-tuple-element.55), channel_id=1, source_target_pairs={{0,2},{2,4},{4,6},{6,8},{8,10},{10,12},{12,14},{14,0},{1,3},{3,5},... | collective-permute-start | bytes 110600 | tf_op jit(solution)/shard_map/ppermute | solution.py:79
  4.9 9.3 %collective-permute-start.1 = (bf16[144,128]{1,0:T(8,128)(2,1)S(1)}, bf16[144,128]{1,0:T(8,128)(2,1)S(1)}, u32[]{:S(2)}, u32[]{:S(2)}) collective-permute-start(bf16[144,128]{1,0:T(8,128)(2,1)S(1)} %get-tuple-element.56), channel_id=1, source_target_pairs={{0,4},{2,6},{4,8},{6,10},{8,12},{10,14},{12,0},{14,2},{1,5},{3,7},... | collective-permute-start | bytes 110600 | tf_op jit(solution)/shard_map/ppermute | solution.py:79
  6.5 10.9 %collective-permute-start.2 = (bf16[144,128]{1,0:T(8,128)(2,1)S(1)}, bf16[144,128]{1,0:T(8,128)(2,1)S(1)}, u32[]{:S(2)}, u32[]{:S(2)}) collective-permute-start(bf16[144,128]{1,0:T(8,128)(2,1)S(1)} %get-tuple-element.57), channel_id=1, source_target_pairs={{0,6},{2,8},{4,10},{6,12},{8,14},{10,0},{12,2},{14,4},{1,7},{3,9},... | collective-permute-start | bytes 110600 | tf_op jit(solution)/shard_map/ppermute | solution.py:79
  9.1 8.4 %collective-permute-start.3 = (bf16[144,128]{1,0:T(8,128)(2,1)S(1)}, bf16[144,128]{1,0:T(8,128)(2,1)S(1)}, u32[]{:S(2)}, u32[]{:S(2)}) collective-permute-start(bf16[144,128]{1,0:T(8,128)(2,1)S(1)} %get-tuple-element.58), channel_id=1, source_target_pairs={{0,8},{2,10},{4,12},{6,14},{8,0},{10,2},{12,4},{14,6},{1,9},{3,11}... | collective-permute-start | bytes 110600 | tf_op jit(solution)/shard_map/ppermute | solution.py:79
  10.3 7.2 %collective-permute-start.4 = (bf16[144,128]{1,0:T(8,128)(2,1)S(1)}, bf16[144,128]{1,0:T(8,128)(2,1)S(1)}, u32[]{:S(2)}, u32[]{:S(2)}) collective-permute-start(bf16[144,128]{1,0:T(8,128)(2,1)S(1)} %get-tuple-element.59), channel_id=1, source_target_pairs={{0,10},{2,12},{4,14},{6,0},{8,2},{10,4},{12,6},{14,8},{1,11},{3,13... | collective-permute-start | bytes 110600 | tf_op jit(solution)/shard_map/ppermute | solution.py:79
  12.9 4.5 %collective-permute-start.5 = (bf16[144,128]{1,0:T(8,128)(2,1)S(1)}, bf16[144,128]{1,0:T(8,128)(2,1)S(1)}, u32[]{:S(2)}, u32[]{:S(2)}) collective-permute-start(bf16[144,128]{1,0:T(8,128)(2,1)S(1)} %get-tuple-element.60), channel_id=1, source_target_pairs={{0,12},{2,14},{4,0},{6,2},{8,4},{10,6},{12,8},{14,10},{1,13},{3,15... | collective-permute-start | bytes 110600 | tf_op jit(solution)/shard_map/ppermute | solution.py:79
  14.3 4.0 %collective-permute-start.6 = (bf16[144,128]{1,0:T(8,128)(2,1)S(1)}, bf16[144,128]{1,0:T(8,128)(2,1)S(1)}, u32[]{:S(2)}, u32[]{:S(2)}) collective-permute-start(bf16[144,128]{1,0:T(8,128)(2,1)S(1)} %get-tuple-element.61), channel_id=1, source_target_pairs={{0,14},{2,0},{4,2},{6,4},{8,6},{10,8},{12,10},{14,12},{1,15},{3,1}... | collective-permute-start | bytes 110600 | tf_op jit(solution)/shard_map/ppermute | solution.py:79
  18.3 1.6 %collective-permute-start.7 = (bf16[7,144,128]{2,1,0:T(8,128)(2,1)S(1)}, bf16[7,144,128]{2,1,0:T(8,128)(2,1)S(1)}, u32[]{:S(2)}, u32[]{:S(2)}) collective-permute-start(bf16[7,144,128]{2,1,0:T(8,128)(2,1)S(1)} %shard_map.147.refs_1_), channel_id=1, source_target_pairs={{0,1},{1,0},{2,3},{3,2},{4,5},{5,4},{6,7},{7,6},{8,9},{9,8},{10,11... | collective-permute-start | bytes 774152 | tf_op jit(solution)/shard_map/ppermute | solution.py:79
  22.8 5.7 %collective-permute-start.10 = (bf16[384,256]{1,0:T(8,128)(2,1)S(1)}, bf16[384,256]{1,0:T(8,128)(2,1)S(1)}, u32[]{:S(2)}, u32[]{:S(2)}) collective-permute-start(bf16[384,256]{1,0:T(8,128)(2,1)S(1)} %get-tuple-element.77), channel_id=1, source_target_pairs={{0,2},{1,5},{2,0},{3,7},{4,6},{5,1},{6,4},{7,3},{8,10},{9,13},{10,... | collective-permute-start | bytes 589832 | tf_op jit(solution)/shard_map/ppermute | solution.py:239
  24.4 8.9 %collective-permute-start.9 = (bf16[400,256]{1,0:T(8,128)(2,1)S(1)}, bf16[400,256]{1,0:T(8,128)(2,1)S(1)}, u32[]{:S(2)}, u32[]{:S(2)}) collective-permute-start(bf16[400,256]{1,0:T(8,128)(2,1)S(1)} %get-tuple-element.75), channel_id=1, source_target_pairs={{0,2},{1,5},{2,0},{3,7},{4,6},{5,1},{6,4},{7,3},{8,10},{9,13},{10,... | collective-permute-start | bytes 614408 | tf_op jit(solution)/shard_map/ppermute | solution.py:239
  24.9 8.5 %collective-permute-start.13 = (bf16[256,256]{1,0:T(8,128)(2,1)S(1)}, bf16[256,256]{1,0:T(8,128)(2,1)S(1)}, u32[]{:S(2)}, u32[]{:S(2)}) collective-permute-start(bf16[256,256]{1,0:T(8,128)(2,1)S(1)} %get-tuple-element.84), channel_id=1, source_target_pairs={{0,2},{1,5},{2,0},{3,7},{4,6},{5,1},{6,4},{7,3},{8,10},{9,13},{10,... | collective-permute-start | bytes 393224 | tf_op jit(solution)/shard_map/ppermute | solution.py:239
  28.6 4.7 %collective-permute-start.11 = (bf16[192,256]{1,0:T(8,128)(2,1)S(1)}, bf16[192,256]{1,0:T(8,128)(2,1)S(1)}, u32[]{:S(2)}, u32[]{:S(2)}) collective-permute-start(bf16[192,256]{1,0:T(8,128)(2,1)S(1)} %get-tuple-element.79.refs_2_), channel_id=1, source_target_pairs={{0,4},{1,3},{2,6},{3,1},{4,0},{5,7},{6,2},{7,5},{8,12},{9,11},{10,... | collective-permute-start | bytes 294920 | tf_op jit(solution)/shard_map/ppermute | solution.py:239
  33.7 7.2 %collective-permute-start.14 = (bf16[256,256]{1,0:T(8,128)(2,1)S(1)}, bf16[256,256]{1,0:T(8,128)(2,1)S(1)}, u32[]{:S(2)}, u32[]{:S(2)}) collective-permute-start(bf16[256,256]{1,0:T(8,128)(2,1)S(1)} %get-tuple-element.87.refs_4_), channel_id=1, source_target_pairs={{0,4},{1,3},{2,6},{3,1},{4,0},{5,7},{6,2},{7,5},{8,12},{9,11},{10,... | collective-permute-start | bytes 393224 | tf_op jit(solution)/shard_map/ppermute | solution.py:239
  34.5 6.5 %collective-permute-start.12 = (bf16[208,256]{1,0:T(8,128)(2,1)S(1)}, bf16[208,256]{1,0:T(8,128)(2,1)S(1)}, u32[]{:S(2)}, u32[]{:S(2)}) collective-permute-start(bf16[208,256]{1,0:T(8,128)(2,1)S(1)} %get-tuple-element.82.refs_3_), channel_id=1, source_target_pairs={{0,4},{1,3},{2,6},{3,1},{4,0},{5,7},{6,2},{7,5},{8,12},{9,11},{10,... | collective-permute-start | bytes 319496 | tf_op jit(solution)/shard_map/ppermute | solution.py:239
  35.8 8.0 %collective-permute-start.17 = (bf16[192,256]{1,0:T(8,128)(2,1)S(1)}, bf16[192,256]{1,0:T(8,128)(2,1)S(1)}, u32[]{:S(2)}, u32[]{:S(2)}) collective-permute-start(bf16[192,256]{1,0:T(8,128)(2,1)S(1)} %get-tuple-element.80.refs_2_), channel_id=1, source_target_pairs={{0,12},{1,13},{2,14},{3,15},{4,8},{5,9},{6,10},{7,11},{8,4},{9,5},... | collective-permute-start | bytes 294920 | tf_op jit(solution)/shard_map/ppermute | solution.py:239
  41.1 8.5 %collective-permute-start.15 = (bf16[336,256]{1,0:T(8,128)(2,1)S(1)}, bf16[336,256]{1,0:T(8,128)(2,1)S(1)}, u32[]{:S(2)}, u32[]{:S(2)}) collective-permute-start(bf16[336,256]{1,0:T(8,128)(2,1)S(1)} %get-tuple-element.89.refs_2_), channel_id=1, source_target_pairs={{0,12},{1,13},{2,14},{3,15},{4,8},{5,9},{6,10},{7,11},{8,4},{9,5},... | collective-permute-start | bytes 516104 | tf_op jit(solution)/shard_map/ppermute | solution.py:239
  43.8 5.7 %collective-permute-start.18 = (bf16[192,256]{1,0:T(8,128)(2,1)S(1)}, bf16[192,256]{1,0:T(8,128)(2,1)S(1)}, u32[]{:S(2)}, u32[]{:S(2)}) collective-permute-start(bf16[192,256]{1,0:T(8,128)(2,1)S(1)} %shard_map.156.refs_0_.refs_2_), channel_id=1, source_target_pairs={{0,4},{1,3},{2,6},{3,1},{4,0},{5,7},{6,2},{7,5},{8,12},{9,11},{10,... | collective-permute-start | bytes 294920 | tf_op jit(solution)/shard_map/ppermute | solution.py:239
  49.6 5.4 %collective-permute-start.20 = (bf16[192,256]{1,0:T(8,128)(2,1)S(1)}, bf16[192,256]{1,0:T(8,128)(2,1)S(1)}, u32[]{:S(2)}, u32[]{:S(2)}) collective-permute-start(bf16[192,256]{1,0:T(8,128)(2,1)S(1)} %get-tuple-element.97.refs_0_.refs_2_), channel_id=1, source_target_pairs={{0,4},{1,3},{2,6},{3,1},{4,0},{5,7},{6,2},{7,5},{8,12},{9,11},{10,... | collective-permute-start | bytes 294920 | tf_op jit(solution)/shard_map/ppermute | solution.py:239
  50.6 8.0 %collective-permute-start.19 = (bf16[384,256]{1,0:T(8,128)(2,1)S(1)}, bf16[384,256]{1,0:T(8,128)(2,1)S(1)}, u32[]{:S(2)}, u32[]{:S(2)}) collective-permute-start(bf16[384,256]{1,0:T(8,128)(2,1)S(1)} %shard_map.157.refs_2_.refs_0_), channel_id=1, source_target_pairs={{0,2},{1,5},{2,0},{3,7},{4,6},{5,1},{6,4},{7,3},{8,10},{9,13},{10,... | collective-permute-start | bytes 589832 | tf_op jit(solution)/shard_map/ppermute | solution.py:239
  55.0 5.7 %collective-permute-start.21 = (bf16[384,256]{1,0:T(8,128)(2,1)S(1)}, bf16[384,256]{1,0:T(8,128)(2,1)S(1)}, u32[]{:S(2)}, u32[]{:S(2)}) collective-permute-start(bf16[384,256]{1,0:T(8,128)(2,1)S(1)} %shard_map.160.refs_2_), channel_id=1, source_target_pairs={{0,2},{1,5},{2,0},{3,7},{4,6},{5,1},{6,4},{7,3},{8,10},{9,13},{10,... | collective-permute-start | bytes 589832 | tf_op jit(solution)/shard_map/ppermute | solution.py:239
  56.1 1.4 %collective-permute-start.8 = (bf16[320,256]{1,0:T(8,128)(2,1)S(1)}, bf16[320,256]{1,0:T(8,128)(2,1)S(1)}, u32[]{:S(2)}, u32[]{:S(2)}) collective-permute-start(bf16[320,256]{1,0:T(8,128)(2,1)S(1)} %get-tuple-element.73), channel_id=1, source_target_pairs={{0,1},{1,0},{2,3},{3,2},{4,5},{5,4},{6,7},{7,6},{8,9},{9,8},{10,11... | collective-permute-start | bytes 491528 | tf_op jit(solution)/shard_map/ppermute | solution.py:79
  56.3 1.5 %collective-permute-start.16 = (bf16[128,256]{1,0:T(8,128)(2,1)S(1)}, bf16[128,256]{1,0:T(8,128)(2,1)S(1)}, u32[]{:S(2)}, u32[]{:S(2)}) collective-permute-start(bf16[128,256]{1,0:T(8,128)(2,1)S(1)} %get-tuple-element.91), channel_id=1, source_target_pairs={{0,1},{1,0},{2,3},{3,2},{4,5},{5,4},{6,7},{7,6},{8,9},{9,8},{10,11... | collective-permute-start | bytes 196616 | tf_op jit(solution)/shard_map/ppermute | solution.py:79

commit v16 on v15

--- a/solution.py
+++ b/solution.py
@@ -9,7 +9,6 @@
 
 OWNER_AXES = ("obs", "node")
 SUBLANES = 16
-BUNDLES = 2
 BF16 = jnp.bfloat16
 F32 = jnp.float32
 
@@ -315,12 +314,13 @@
         total_ref[pl.ds(pl.multiple_of(begin + which * half, SUBLANES), half), :] = dot(ref[...], g_a, 0, 0)
     begin += width
     total_ref[begin:, :] = sums[nodes:, :hidden]
-    rows = begin // bundles
-    for i in range(bundles):
+    begin = 0
+    for i, rows in enumerate(bundles):
         split_half(
-            total_ref, i * rows, rows, step, tail if i == bundles - 1 else 0,
+            total_ref, begin, rows, step, tail if i == len(bundles) - 1 else 0,
             halves_refs[2 * i], halves_refs[2 * i + 1],
         )
+        begin += rows
     mine, theirs = other_half(w_node_ref)
     theirs_ref[...] = dot(node_hidden, theirs, 1, 1).astype(BF16)
     mine_ref[...] = dot(node_hidden, mine, 1, 1)
@@ -378,15 +378,13 @@
     out_ref[pl.ds(pl.multiple_of((1 - bit) * rows, SUBLANES), rows), :] = got_ref[...]
 
 
-def spread_kernel(step, bundles, *refs):
+def spread_kernel(step, mine_ref, got_ref, *out_refs):
     low = own_bit(step) == 0
-    joined = []
-    for i in range(bundles):
-        mine, got = refs[2 * i][...], refs[2 * i + 1][...]
-        joined += [jnp.where(low, mine, got), jnp.where(low, got, mine)]
+    mine, got = mine_ref[...], got_ref[...]
+    joined = [jnp.where(low, mine, got), jnp.where(low, got, mine)]
     half, hidden = joined[0].shape
     at = 0
-    for out_ref in refs[2 * bundles :]:
+    for out_ref in out_refs:
         for c in range(out_ref.shape[1] // hidden):
             begin = 0
             while begin < out_ref.shape[0]:
@@ -552,12 +550,11 @@
     )
 
     stack = 2 * width + width // hidden * hidden
-    bundles = BUNDLES
-    rows = stack // bundles
+    bundles = [stack - width, width]
     obs_got = flip(obs_send, steps[0])
     shapes = []
-    for i in range(bundles):
-        share = rows // 2 + (tail if i == bundles - 1 else 0)
+    for i, rows in enumerate(bundles):
+        share = half_rows(rows) + (tail if i == len(bundles) - 1 else 0)
         shapes += [((share, hidden), F32), ((share, hidden), BF16)]
     node_mine, node_theirs, *shares = call(
         functools.partial(weight_kernel, steps[0], bundles, tail),
@@ -569,15 +566,15 @@
     returned = []
     chains = [rows_chain(steps, obs_keep, obs_got, obs_pick, after, returned)]
     got = [flip(send, steps[0]) for send in shares[1::2]]
-    for i in range(bundles):
-        last = i == bundles - 1
+    for i, rows in enumerate(bundles):
+        last = i == len(bundles) - 1
         chains.append(
             weight_chain(
                 steps, rows, tail if last else 0, slots, shares[2 * i], got[i], after, returned if last else None
             )
         )
     node_got = shift(node_theirs, "mp", 1)
-    middle, last = len(steps) - 1, len(steps) + len(halving_used(steps, rows)) - 1
+    middle, last = len(steps) - 1, len(steps) + len(halving_used(steps, bundles[0])) - 1
     turns = [1]
     for step in range(1, last):
         turns += [2, 1] if step == middle else [1, 2]
@@ -594,12 +591,17 @@
         merge_kernel, [((nodes, half), F32), ((obs, half), BF16), ((slots, hidden), F32)],
         node_mine, node_got, obs_mine, shift(obs_theirs, "mp", 1), slot_sums,
     )
-    ends = [end for pair, *_ in weights for end in pair]
-    grad_w_node, grad_w_out, grad_w_obs = call(
-        functools.partial(spread_kernel, steps[0], bundles),
-        [((width, hidden), F32), ((hidden, width), F32), ((width, hidden), F32)],
-        *ends,
+    grad_w_node, grad_w_out = call(
+        functools.partial(spread_kernel, steps[0]),
+        [((width, hidden), F32), ((hidden, width), F32)],
+        *weights[0][0],
         after=[pltpu.with_memory_space_constraint(grad_obs, pltpu.HBM)],
+    )
+    (grad_w_obs,) = call(
+        functools.partial(spread_kernel, steps[0]),
+        [((width, hidden), F32)],
+        *weights[1][0],
+        after=[pltpu.with_memory_space_constraint(grad_w_node, pltpu.HBM)],
     )
     return grad_obs, grad_node, grad_w_obs, grad_w_node, grad_w_out, grad_slot
 

time: 62.1 us -> 66.8 us (1.076)
  waiting for transfers between devices: 22 us -> 27.1 us
  starting transfers between devices: 30.3 us -> 29.2 us
  Pallas kernels: 8.85 us -> 9.54 us
    ppermute x12, waiting for transfers between devices: 18.8 us -> 23.6 us  [flip(): return lax.ppermute(value, axes, pairs)]
    pallas_call x15 -> x16, Pallas kernels: 5.83 us -> 6.51 us  [call(): pl.pallas_call(lambda *refs: kernel(*refs[:count], *refs[len(args):]), ou...]
  transfers between devices with their start and end apart: 22 -> 22, of which waited for: 10 -> 10; matrix products, arithmetic and copies ran while one was open for 0% -> 0% of each run, Pallas kernels for 5% -> 6%
where the time goes in v16:
time: 66.8 us; the launch traced here: 66.7 us
  starting transfers between devices  29.2 us (44%)
  waiting for transfers between devices  27.1 us (41%)
  Pallas kernels  9.54 us (14%)
  between operations  0.83 us (1%)
    ppermute x12, waiting for transfers between devices, flip(): return lax.ppermute(value, axes, pairs)  23.6 us
    ppermute x12, starting transfers between devices, flip(): return lax.ppermute(value, axes, pairs)  15.2 us
    ppermute x10, starting transfers between devices, shift(): lax.ppermute(value, axis, [(i, (i + step) % size) for i in range(size)])  14 us
    pallas_call x16, Pallas kernels, call(): pl.pallas_call(lambda *refs: kernel(*refs[:count], *refs[len(args):]), ou...  6.51 us
    ppermute x10, waiting for transfers between devices, shift(): lax.ppermute(value, axis, [(i, (i + step) % size) for i in range(size)])  3.52 us
    pallas_call x2, Pallas kernels, call_staged(): pl.pallas_call(staged, out_shape=[jax.ShapeDtypeStruct(shape, dtype) for...  3.03 us
  transfers between devices with their start and end apart: 22, of which 10 were waited for; matrix products, arithmetic and copies ran while one was open for 0% of the time, Pallas kernels for 6%

profile of v16, /device:TPU:0, one launch (start us, length us, event | category | flops | bytes accessed | tf_op | source)
XLA Modules:
  0.0 66.7 jit_solution(3639197899183175189)
XLA Ops:
  0.6 1.3 %shard_map.145 = (bf16[144,128]{1,0:T(8,128)(2,1)S(1)}, bf16[144,128]{1,0:T(8,128)(2,1)S(1)}, bf16[144,128]{1,0:T(8,128)(2,1)S(1)}, bf16[144,128]{1,0:T(8,128)(2...) custom-call(bf16[128,512]{1,0:T(8,128)(2,1)} %refs_0_.2, ...), custom_call_target="tpu_custom_call" | custom-call | tf_op jit(solution)/shard_map/pallas_call | solution.py:60
  1.9 3.0 %collective-permute-start = (bf16[144,128]{1,0:T(8,128)(2,1)S(1)}, bf16[144,128]{1,0:T(8,128)(2,1)S(1)}, u32[]{:S(2)}, u32[]{:S(2)}) collective-permute-start(bf16[144,128]{1,0:T(8,128)(2,1)S(1)} %get-tuple-element.54), channel_id=1, source_target_pairs={{0,2},{2,4},{4,6},{6,8},{8,10},{10,12},{12,14},{14,0},{1,3},{3,5},... | collective-permute-start | bytes 110600 | tf_op jit(solution)/shard_map/ppermute | solution.py:78
  4.9 1.6 %collective-permute-start.1 = (bf16[144,128]{1,0:T(8,128)(2,1)S(1)}, bf16[144,128]{1,0:T(8,128)(2,1)S(1)}, u32[]{:S(2)}, u32[]{:S(2)}) collective-permute-start(bf16[144,128]{1,0:T(8,128)(2,1)S(1)} %get-tuple-element.55), channel_id=1, source_target_pairs={{0,4},{2,6},{4,8},{6,10},{8,12},{10,14},{12,0},{14,2},{1,5},{3,7},... | collective-permute-start | bytes 110600 | tf_op jit(solution)/shard_map/ppermute | solution.py:78
  6.5 2.6 %collective-permute-start.2 = (bf16[144,128]{1,0:T(8,128)(2,1)S(1)}, bf16[144,128]{1,0:T(8,128)(2,1)S(1)}, u32[]{:S(2)}, u32[]{:S(2)}) collective-permute-start(bf16[144,128]{1,0:T(8,128)(2,1)S(1)} %get-tuple-element.56), channel_id=1, source_target_pairs={{0,6},{2,8},{4,10},{6,12},{8,14},{10,0},{12,2},{14,4},{1,7},{3,9},... | collective-permute-start | bytes 110600 | tf_op jit(solution)/shard_map/ppermute | solution.py:78
  9.1 1.2 %collective-permute-start.3 = (bf16[144,128]{1,0:T(8,128)(2,1)S(1)}, bf16[144,128]{1,0:T(8,128)(2,1)S(1)}, u32[]{:S(2)}, u32[]{:S(2)}) collective-permute-start(bf16[144,128]{1,0:T(8,128)(2,1)S(1)} %get-tuple-element.57), channel_id=1, source_target_pairs={{0,8},{2,10},{4,12},{6,14},{8,0},{10,2},{12,4},{14,6},{1,9},{3,11}... | collective-permute-start | bytes 110600 | tf_op jit(solution)/shard_map/ppermute | solution.py:78
  10.3 2.6 %collective-permute-start.4 = (bf16[144,128]{1,0:T(8,128)(2,1)S(1)}, bf16[144,128]{1,0:T(8,128)(2,1)S(1)}, u32[]{:S(2)}, u32[]{:S(2)}) collective-permute-start(bf16[144,128]{1,0:T(8,128)(2,1)S(1)} %get-tuple-element.58), channel_id=1, source_target_pairs={{0,10},{2,12},{4,14},{6,0},{8,2},{10,4},{12,6},{14,8},{1,11},{3,13... | collective-permute-start | bytes 110600 | tf_op jit(solution)/shard_map/ppermute | solution.py:78
  12.9 0.0 collective-permute-done.refs_0_
  12.9 1.4 %collective-permute-start.5 = (bf16[144,128]{1,0:T(8,128)(2,1)S(1)}, bf16[144,128]{1,0:T(8,128)(2,1)S(1)}, u32[]{:S(2)}, u32[]{:S(2)}) collective-permute-start(bf16[144,128]{1,0:T(8,128)(2,1)S(1)} %get-tuple-element.59), channel_id=1, source_target_pairs={{0,12},{2,14},{4,0},{6,2},{8,4},{10,6},{12,8},{14,10},{1,13},{3,15... | collective-permute-start | bytes 110600 | tf_op jit(solution)/shard_map/ppermute | solution.py:78
  14.3 0.0 collective-permute-done.1.refs_1_
  14.3 1.4 %collective-permute-start.6 = (bf16[144,128]{1,0:T(8,128)(2,1)S(1)}, bf16[144,128]{1,0:T(8,128)(2,1)S(1)}, u32[]{:S(2)}, u32[]{:S(2)}) collective-permute-start(bf16[144,128]{1,0:T(8,128)(2,1)S(1)} %get-tuple-element.60), channel_id=1, source_target_pairs={{0,14},{2,0},{4,2},{6,4},{8,6},{10,8},{12,10},{14,12},{1,15},{3,1}... | collective-permute-start | bytes 110600 | tf_op jit(solution)/shard_map/ppermute | solution.py:78
  15.7 1.7 %shard_map.146 = (bf16[336,1024]{1,0:T(8,128)(2,1)S(1)}, bf16[320,512]{1,0:T(8,128)(2,1)S(1)}, bf16[320,512]{1,0:T(8,128)(2,1)S(1)}, bf16[512,256]{1,0:T(8,128)(2,1)S(1)}, bf16[512,256]{1,0:T(8,128)(2,1)S(1)}) custom-call(bf16[320,512]{1,0:T(8,128)(2,1)} %refs_0_.3, bf16[320,512]{1,0:T(8,128)(2,1)} %refs_1_.1, bf16[512,256]{1,0:T(8,128)(2,1)} %refs_2_.1, ...), custom_call_target="tpu_custom_call" | custom-call | tf_op jit(solution)/shard_map/pallas_call | solution.py:60
  17.4 0.0 collective-permute-done.2.refs_2_
  17.5 0.0 collective-permute-done.3.refs_3_
  17.5 0.8 %collective-permute-done.6.refs_6_ = bf16[144,128]{1,0:T(8,128)(2,1)S(1)} collective-permute-done((bf16[144,128]{1,0:T(8,128)(2,1)S(1)}, bf16[144,128]{1,0:T(8,128)(2,1)S(1)}, u32[]{:S(2)}, u32[]{:S(2)}) %collective-permute-start.6) | collective-permute-done | bytes 36896 | tf_op jit(solution)/shard_map/ppermute | solution.py:78
  18.3 0.1 collective-permute-start.7
  18.3 1.5 %collective-permute-done.7.refs_3_ = bf16[7,144,128]{2,1,0:T(8,128)(2,1)S(1)} collective-permute-done((bf16[7,144,128]{2,1,0:T(8,128)(2,1)S(1)}, bf16[7,144,128]{2,1,0:T(8,128)(2,1)S(1)}, u32[]{:S(2)}, u32[]{:S(2)}) %collective-permute-start.7) | collective-permute-done | bytes 258080 | tf_op jit(solution)/shard_map/ppermute | solution.py:78
  19.9 1.6 %shard_map.148 = (bf16[512,512]{1,0:T(8,128)(2,1)S(1)}, bf16[512,336]{1,0:T(8,128)(2,1)S(1)}, bf16[512,256]{1,0:T(8,128)(2,1)S(1)}, bf16[512,256]{1,0:T(8,128)(2...) custom-call(bf16[144,128]{1,0:T(8,128)(2,1)S(1)} %get-tuple-element.53.refs_0_, ...), custom_call_target="tpu_custom_call" | custom-call | tf_op jit(solution)/shard_map/pallas_call | solution.py:31
  21.5 1.3 %shard_map.149 = (f32[320,256]{1,0:T(8,128)S(1)}, bf16[320,256]{1,0:T(8,128)(2,1)S(1)}, f32[512,256]{1,0:T(8,128)S(1)}, bf16[512,256]{1,0:T(8,128)(2,1)S(1)}, f3...) custom-call(bf16[512,336]{1,0:T(8,128)(2,1)S(1)} %get-tuple-element.64.refs_0_, ...), custom_call_target="tpu_custom_call" | custom-call | tf_op jit(solution)/shard_map/pallas_call | solution.py:31
  22.8 1.6 %collective-permute-start.10 = (bf16[512,256]{1,0:T(8,128)(2,1)S(1)}, bf16[512,256]{1,0:T(8,128)(2,1)S(1)}, u32[]{:S(2)}, u32[]{:S(2)}) collective-permute-start(bf16[512,256]{1,0:T(8,128)(2,1)S(1)} %get-tuple-element.76), channel_id=1, source_target_pairs={{0,2},{1,5},{2,0},{3,7},{4,6},{5,1},{6,4},{7,3},{8,10},{9,13},{10,... | collective-permute-start | bytes 786440 | tf_op jit(solution)/shard_map/ppermute | solution.py:238
  24.4 0.5 collective-permute-start.9
  24.9 4.3 %collective-permute-done.10.refs_1_ = bf16[512,256]{1,0:T(8,128)(2,1)S(1)} collective-permute-done((bf16[512,256]{1,0:T(8,128)(2,1)S(1)}, bf16[512,256]{1,0:T(8,128)(2,1)S(1)}, u32[]{:S(2)}, u32[]{:S(2)}) %collective-permute-start.10) | collective-permute-done | bytes 262176 | tf_op jit(solution)/shard_map/ppermute | solution.py:238
  29.3 0.1 shard_map.150
  29.4 0.7 %collective-permute-start.11 = (bf16[256,256]{1,0:T(8,128)(2,1)S(1)}, bf16[256,256]{1,0:T(8,128)(2,1)S(1)}, u32[]{:S(2)}, u32[]{:S(2)}) collective-permute-start(bf16[256,256]{1,0:T(8,128)(2,1)S(1)} %get-tuple-element.78.refs_2_), channel_id=1, source_target_pairs={{0,4},{1,3},{2,6},{3,1},{4,0},{5,7},{6,2},{7,5},{8,12},{9,11},{10,... | collective-permute-start | bytes 393224 | tf_op jit(solution)/shard_map/ppermute | solution.py:238
  30.1 1.0 %collective-permute-start.13 = (bf16[256,256]{1,0:T(8,128)(2,1)S(1)}, bf16[256,256]{1,0:T(8,128)(2,1)S(1)}, u32[]{:S(2)}, u32[]{:S(2)}) collective-permute-start(bf16[256,256]{1,0:T(8,128)(2,1)S(1)} %get-tuple-element.83), channel_id=1, source_target_pairs={{0,2},{1,5},{2,0},{3,7},{4,6},{5,1},{6,4},{7,3},{8,10},{9,13},{10,... | collective-permute-start | bytes 393224 | tf_op jit(solution)/shard_map/ppermute | solution.py:238
  31.1 4.3 %collective-permute-done.11.refs_1_ = bf16[256,256]{1,0:T(8,128)(2,1)S(1)} collective-permute-done((bf16[256,256]{1,0:T(8,128)(2,1)S(1)}, bf16[256,256]{1,0:T(8,128)(2,1)S(1)}, u32[]{:S(2)}, u32[]{:S(2)}) %collective-permute-start.11) | collective-permute-done | bytes 131104 | tf_op jit(solution)/shard_map/ppermute | solution.py:238
  35.4 0.1 shard_map.152
  35.5 0.3 shard_map.153
  35.8 1.0 %collective-permute-start.14 = (bf16[256,256]{1,0:T(8,128)(2,1)S(1)}, bf16[256,256]{1,0:T(8,128)(2,1)S(1)}, u32[]{:S(2)}, u32[]{:S(2)}) collective-permute-start(bf16[256,256]{1,0:T(8,128)(2,1)S(1)} %get-tuple-element.86.refs_4_), channel_id=1, source_target_pairs={{0,4},{1,3},{2,6},{3,1},{4,0},{5,7},{6,2},{7,5},{8,12},{9,11},{10,... | collective-permute-start | bytes 393224 | tf_op jit(solution)/shard_map/ppermute | solution.py:238
  36.8 2.7 %collective-permute-start.17 = (bf16[256,256]{1,0:T(8,128)(2,1)S(1)}, bf16[256,256]{1,0:T(8,128)(2,1)S(1)}, u32[]{:S(2)}, u32[]{:S(2)}) collective-permute-start(bf16[256,256]{1,0:T(8,128)(2,1)S(1)} %get-tuple-element.79.refs_2_), channel_id=1, source_target_pairs={{0,12},{1,13},{2,14},{3,15},{4,8},{5,9},{6,10},{7,11},{8,4},{9,5},... | collective-permute-start | bytes 393224 | tf_op jit(solution)/shard_map/ppermute | solution.py:238
  39.5 0.6 collective-permute-start.12
  40.0 5.0 %collective-permute-done.12.refs_1_ = bf16[144,256]{1,0:T(8,128)(2,1)S(1)} collective-permute-done((bf16[144,256]{1,0:T(8,128)(2,1)S(1)}, bf16[144,256]{1,0:T(8,128)(2,1)S(1)}, u32[]{:S(2)}, u32[]{:S(2)}) %collective-permute-start.12) | collective-permute-done | bytes 73760 | tf_op jit(solution)/shard_map/ppermute | solution.py:238
  45.0 0.1 shard_map.154
  45.2 1.2 %collective-permute-start.18 = (bf16[256,256]{1,0:T(8,128)(2,1)S(1)}, bf16[256,256]{1,0:T(8,128)(2,1)S(1)}, u32[]{:S(2)}, u32[]{:S(2)}) collective-permute-start(bf16[256,256]{1,0:T(8,128)(2,1)S(1)} %shard_map.156.refs_0_.refs_2_), channel_id=1, source_target_pairs={{0,4},{1,3},{2,6},{3,1},{4,0},{5,7},{6,2},{7,5},{8,12},{9,11},{10,... | collective-permute-start | bytes 393224 | tf_op jit(solution)/shard_map/ppermute | solution.py:238
  46.4 3.4 %collective-permute-start.15 = (bf16[272,256]{1,0:T(8,128)(2,1)S(1)}, bf16[272,256]{1,0:T(8,128)(2,1)S(1)}, u32[]{:S(2)}, u32[]{:S(2)}) collective-permute-start(bf16[272,256]{1,0:T(8,128)(2,1)S(1)} %get-tuple-element.88.refs_2_), channel_id=1, source_target_pairs={{0,12},{1,13},{2,14},{3,15},{4,8},{5,9},{6,10},{7,11},{8,4},{9,5},... | collective-permute-start | bytes 417800 | tf_op jit(solution)/shard_map/ppermute | solution.py:238
  49.7 2.4 %collective-permute-done.18.refs_1_ = bf16[256,256]{1,0:T(8,128)(2,1)S(1)} collective-permute-done((bf16[256,256]{1,0:T(8,128)(2,1)S(1)}, bf16[256,256]{1,0:T(8,128)(2,1)S(1)}, u32[]{:S(2)}, u32[]{:S(2)}) %collective-permute-start.18) | collective-permute-done | bytes 131104 | tf_op jit(solution)/shard_map/ppermute | solution.py:238
  52.2 1.1 %collective-permute-start.21 = (bf16[512,256]{1,0:T(8,128)(2,1)S(1)}, bf16[512,256]{1,0:T(8,128)(2,1)S(1)}, u32[]{:S(2)}, u32[]{:S(2)}) collective-permute-start(bf16[512,256]{1,0:T(8,128)(2,1)S(1)} %shard_map.157.refs_2_.refs_0_), channel_id=1, source_target_pairs={{0,2},{1,5},{2,0},{3,7},{4,6},{5,1},{6,4},{7,3},{8,10},{9,13},{10,... | collective-permute-start | bytes 786440 | tf_op jit(solution)/shard_map/ppermute | solution.py:238
  53.3 2.4 %collective-permute-done.15.refs_1_ = bf16[272,256]{1,0:T(8,128)(2,1)S(1)} collective-permute-done((bf16[272,256]{1,0:T(8,128)(2,1)S(1)}, bf16[272,256]{1,0:T(8,128)(2,1)S(1)}, u32[]{:S(2)}, u32[]{:S(2)}) %collective-permute-start.15) | collective-permute-done | bytes 139296 | tf_op jit(solution)/shard_map/ppermute | solution.py:238
  55.8 0.1 collective-permute-start.19
  55.8 0.1 collective-permute-start.8
  55.9 4.9 %collective-permute-done.19.refs_1_ = bf16[128,256]{1,0:T(8,128)(2,1)S(1)} collective-permute-done((bf16[128,256]{1,0:T(8,128)(2,1)S(1)}, bf16[128,256]{1,0:T(8,128)(2,1)S(1)}, u32[]{:S(2)}, u32[]{:S(2)}) %collective-permute-start.19) | collective-permute-done | bytes 65568 | tf_op jit(solution)/shard_map/ppermute | solution.py:238
  60.8 1.4 %collective-permute-start.20 = (bf16[256,256]{1,0:T(8,128)(2,1)S(1)}, bf16[256,256]{1,0:T(8,128)(2,1)S(1)}, u32[]{:S(2)}, u32[]{:S(2)}) collective-permute-start(bf16[256,256]{1,0:T(8,128)(2,1)S(1)} %shard_map.160.refs_0_), channel_id=1, source_target_pairs={{0,2},{1,5},{2,0},{3,7},{4,6},{5,1},{6,4},{7,3},{8,10},{9,13},{10,... | collective-permute-start | bytes 393224 | tf_op jit(solution)/shard_map/ppermute | solution.py:238
  62.2 0.2 shard_map.155
  62.5 0.1 collective-permute-start.16
  62.6 1.2 %collective-permute-done.16.refs_3_ = bf16[128,256]{1,0:T(8,128)(2,1)S(1)} collective-permute-done((bf16[128,256]{1,0:T(8,128)(2,1)S(1)}, bf16[128,256]{1,0:T(8,128)(2,1)S(1)}, u32[]{:S(2)}, u32[]{:S(2)}) %collective-permute-start.16) | collective-permute-done | bytes 65568 | tf_op jit(solution)/shard_map/ppermute | solution.py:78
  63.8 0.8 %shard_map.159 = (f32[320,256]{1,0:T(8,128)}, bf16[128,256]{1,0:T(8,128)(2,1)}, f32[6,256]{1,0:T(8,128)}) custom-call(f32[320,256]{1,0:T(8,128)S(1)} %get-tuple-element.71.refs_0_, bf16[320,256]{1,0:T(8,128)(2,1)S(1)} %collective-permute-done.8.refs_1_, f32[128,256]{1,0:T(8,128)S(1)} %get-tuple-element.89.refs_2_, ...), custom_call_target="tpu_custom_call" | custom-call | tf_op jit(solution)/shard_map/pallas_call | solution.py:31
  64.6 1.0 %shard_map.161 = (f32[512,256]{1,0:T(8,128)}, f32[256,512]{1,0:T(8,128)}) custom-call(bf16[512,256]{1,0:T(8,128)(2,1)S(1)} %shard_map.157.refs_2_.refs_0_, bf16[512,256]{1,0:T(8,128)(2,1)S(1)} %collective-permute-done.21.refs_1_, bf16[128,256]{1,0:T(8,128)(2,1)} %get-tuple-element.47.refs_2_), custom_call_target="tpu_custom_call" | custom-call | tf_op jit(solution)/shard_map/pallas_call | solution.py:31
  65.6 0.2 collective-permute-done.20.refs_1_
  65.8 0.8 %shard_map.162 = f32[512,256]{1,0:T(8,128)} custom-call(bf16[256,256]{1,0:T(8,128)(2,1)S(1)} %shard_map.160.refs_0_, bf16[256,256]{1,0:T(8,128)(2,1)S(1)} %collective-permute-done.20.refs_1_, f32[512,256]{1,0:T(8,128)} %get-tuple-element.50.refs_2_), custom_call_target="tpu_custom_call" | custom-call | tf_op jit(solution)/shard_map/pallas_call | solution.py:31
  (14 shorter events, 0.2 us)
Async XLA Ops:
  1.9 11.0 %collective-permute-start = (bf16[144,128]{1,0:T(8,128)(2,1)S(1)}, bf16[144,128]{1,0:T(8,128)(2,1)S(1)}, u32[]{:S(2)}, u32[]{:S(2)}) collective-permute-start(bf16[144,128]{1,0:T(8,128)(2,1)S(1)} %get-tuple-element.54), channel_id=1, source_target_pairs={{0,2},{2,4},{4,6},{6,8},{8,10},{10,12},{12,14},{14,0},{1,3},{3,5},... | collective-permute-start | bytes 110600 | tf_op jit(solution)/shard_map/ppermute | solution.py:78
  4.9 9.3 %collective-permute-start.1 = (bf16[144,128]{1,0:T(8,128)(2,1)S(1)}, bf16[144,128]{1,0:T(8,128)(2,1)S(1)}, u32[]{:S(2)}, u32[]{:S(2)}) collective-permute-start(bf16[144,128]{1,0:T(8,128)(2,1)S(1)} %get-tuple-element.55), channel_id=1, source_target_pairs={{0,4},{2,6},{4,8},{6,10},{8,12},{10,14},{12,0},{14,2},{1,5},{3,7},... | collective-permute-start | bytes 110600 | tf_op jit(solution)/shard_map/ppermute | solution.py:78
  6.5 10.9 %collective-permute-start.2 = (bf16[144,128]{1,0:T(8,128)(2,1)S(1)}, bf16[144,128]{1,0:T(8,128)(2,1)S(1)}, u32[]{:S(2)}, u32[]{:S(2)}) collective-permute-start(bf16[144,128]{1,0:T(8,128)(2,1)S(1)} %get-tuple-element.56), channel_id=1, source_target_pairs={{0,6},{2,8},{4,10},{6,12},{8,14},{10,0},{12,2},{14,4},{1,7},{3,9},... | collective-permute-start | bytes 110600 | tf_op jit(solution)/shard_map/ppermute | solution.py:78
  9.1 8.4 %collective-permute-start.3 = (bf16[144,128]{1,0:T(8,128)(2,1)S(1)}, bf16[144,128]{1,0:T(8,128)(2,1)S(1)}, u32[]{:S(2)}, u32[]{:S(2)}) collective-permute-start(bf16[144,128]{1,0:T(8,128)(2,1)S(1)} %get-tuple-element.57), channel_id=1, source_target_pairs={{0,8},{2,10},{4,12},{6,14},{8,0},{10,2},{12,4},{14,6},{1,9},{3,11}... | collective-permute-start | bytes 110600 | tf_op jit(solution)/shard_map/ppermute | solution.py:78
  10.3 7.2 %collective-permute-start.4 = (bf16[144,128]{1,0:T(8,128)(2,1)S(1)}, bf16[144,128]{1,0:T(8,128)(2,1)S(1)}, u32[]{:S(2)}, u32[]{:S(2)}) collective-permute-start(bf16[144,128]{1,0:T(8,128)(2,1)S(1)} %get-tuple-element.58), channel_id=1, source_target_pairs={{0,10},{2,12},{4,14},{6,0},{8,2},{10,4},{12,6},{14,8},{1,11},{3,13... | collective-permute-start | bytes 110600 | tf_op jit(solution)/shard_map/ppermute | solution.py:78
  12.9 4.5 %collective-permute-start.5 = (bf16[144,128]{1,0:T(8,128)(2,1)S(1)}, bf16[144,128]{1,0:T(8,128)(2,1)S(1)}, u32[]{:S(2)}, u32[]{:S(2)}) collective-permute-start(bf16[144,128]{1,0:T(8,128)(2,1)S(1)} %get-tuple-element.59), channel_id=1, source_target_pairs={{0,12},{2,14},{4,0},{6,2},{8,4},{10,6},{12,8},{14,10},{1,13},{3,15... | collective-permute-start | bytes 110600 | tf_op jit(solution)/shard_map/ppermute | solution.py:78
  14.3 4.0 %collective-permute-start.6 = (bf16[144,128]{1,0:T(8,128)(2,1)S(1)}, bf16[144,128]{1,0:T(8,128)(2,1)S(1)}, u32[]{:S(2)}, u32[]{:S(2)}) collective-permute-start(bf16[144,128]{1,0:T(8,128)(2,1)S(1)} %get-tuple-element.60), channel_id=1, source_target_pairs={{0,14},{2,0},{4,2},{6,4},{8,6},{10,8},{12,10},{14,12},{1,15},{3,1}... | collective-permute-start | bytes 110600 | tf_op jit(solution)/shard_map/ppermute | solution.py:78
  18.3 1.6 %collective-permute-start.7 = (bf16[7,144,128]{2,1,0:T(8,128)(2,1)S(1)}, bf16[7,144,128]{2,1,0:T(8,128)(2,1)S(1)}, u32[]{:S(2)}, u32[]{:S(2)}) collective-permute-start(bf16[7,144,128]{2,1,0:T(8,128)(2,1)S(1)} %shard_map.147.refs_1_), channel_id=1, source_target_pairs={{0,1},{1,0},{2,3},{3,2},{4,5},{5,4},{6,7},{7,6},{8,9},{9,8},{10,11... | collective-permute-start | bytes 774152 | tf_op jit(solution)/shard_map/ppermute | solution.py:78
  22.8 6.4 %collective-permute-start.10 = (bf16[512,256]{1,0:T(8,128)(2,1)S(1)}, bf16[512,256]{1,0:T(8,128)(2,1)S(1)}, u32[]{:S(2)}, u32[]{:S(2)}) collective-permute-start(bf16[512,256]{1,0:T(8,128)(2,1)S(1)} %get-tuple-element.76), channel_id=1, source_target_pairs={{0,2},{1,5},{2,0},{3,7},{4,6},{5,1},{6,4},{7,3},{8,10},{9,13},{10,... | collective-permute-start | bytes 786440 | tf_op jit(solution)/shard_map/ppermute | solution.py:238
  24.4 11.0 %collective-permute-start.9 = (bf16[272,256]{1,0:T(8,128)(2,1)S(1)}, bf16[272,256]{1,0:T(8,128)(2,1)S(1)}, u32[]{:S(2)}, u32[]{:S(2)}) collective-permute-start(bf16[272,256]{1,0:T(8,128)(2,1)S(1)} %get-tuple-element.74), channel_id=1, source_target_pairs={{0,2},{1,5},{2,0},{3,7},{4,6},{5,1},{6,4},{7,3},{8,10},{9,13},{10,... | collective-permute-start | bytes 417800 | tf_op jit(solution)/shard_map/ppermute | solution.py:238
  29.4 6.0 %collective-permute-start.11 = (bf16[256,256]{1,0:T(8,128)(2,1)S(1)}, bf16[256,256]{1,0:T(8,128)(2,1)S(1)}, u32[]{:S(2)}, u32[]{:S(2)}) collective-permute-start(bf16[256,256]{1,0:T(8,128)(2,1)S(1)} %get-tuple-element.78.refs_2_), channel_id=1, source_target_pairs={{0,4},{1,3},{2,6},{3,1},{4,0},{5,7},{6,2},{7,5},{8,12},{9,11},{10,... | collective-permute-start | bytes 393224 | tf_op jit(solution)/shard_map/ppermute | solution.py:238
  30.1 5.4 %collective-permute-start.13 = (bf16[256,256]{1,0:T(8,128)(2,1)S(1)}, bf16[256,256]{1,0:T(8,128)(2,1)S(1)}, u32[]{:S(2)}, u32[]{:S(2)}) collective-permute-start(bf16[256,256]{1,0:T(8,128)(2,1)S(1)} %get-tuple-element.83), channel_id=1, source_target_pairs={{0,2},{1,5},{2,0},{3,7},{4,6},{5,1},{6,4},{7,3},{8,10},{9,13},{10,... | collective-permute-start | bytes 393224 | tf_op jit(solution)/shard_map/ppermute | solution.py:238
  35.8 9.2 %collective-permute-start.14 = (bf16[256,256]{1,0:T(8,128)(2,1)S(1)}, bf16[256,256]{1,0:T(8,128)(2,1)S(1)}, u32[]{:S(2)}, u32[]{:S(2)}) collective-permute-start(bf16[256,256]{1,0:T(8,128)(2,1)S(1)} %get-tuple-element.86.refs_4_), channel_id=1, source_target_pairs={{0,4},{1,3},{2,6},{3,1},{4,0},{5,7},{6,2},{7,5},{8,12},{9,11},{10,... | collective-permute-start | bytes 393224 | tf_op jit(solution)/shard_map/ppermute | solution.py:238
  36.8 8.3 %collective-permute-start.17 = (bf16[256,256]{1,0:T(8,128)(2,1)S(1)}, bf16[256,256]{1,0:T(8,128)(2,1)S(1)}, u32[]{:S(2)}, u32[]{:S(2)}) collective-permute-start(bf16[256,256]{1,0:T(8,128)(2,1)S(1)} %get-tuple-element.79.refs_2_), channel_id=1, source_target_pairs={{0,12},{1,13},{2,14},{3,15},{4,8},{5,9},{6,10},{7,11},{8,4},{9,5},... | collective-permute-start | bytes 393224 | tf_op jit(solution)/shard_map/ppermute | solution.py:238
  39.5 5.6 %collective-permute-start.12 = (bf16[144,256]{1,0:T(8,128)(2,1)S(1)}, bf16[144,256]{1,0:T(8,128)(2,1)S(1)}, u32[]{:S(2)}, u32[]{:S(2)}) collective-permute-start(bf16[144,256]{1,0:T(8,128)(2,1)S(1)} %get-tuple-element.81.refs_3_), channel_id=1, source_target_pairs={{0,4},{1,3},{2,6},{3,1},{4,0},{5,7},{6,2},{7,5},{8,12},{9,11},{10,... | collective-permute-start | bytes 221192 | tf_op jit(solution)/shard_map/ppermute | solution.py:238
  45.2 7.0 %collective-permute-start.18 = (bf16[256,256]{1,0:T(8,128)(2,1)S(1)}, bf16[256,256]{1,0:T(8,128)(2,1)S(1)}, u32[]{:S(2)}, u32[]{:S(2)}) collective-permute-start(bf16[256,256]{1,0:T(8,128)(2,1)S(1)} %shard_map.156.refs_0_.refs_2_), channel_id=1, source_target_pairs={{0,4},{1,3},{2,6},{3,1},{4,0},{5,7},{6,2},{7,5},{8,12},{9,11},{10,... | collective-permute-start | bytes 393224 | tf_op jit(solution)/shard_map/ppermute | solution.py:238
  46.4 9.4 %collective-permute-start.15 = (bf16[272,256]{1,0:T(8,128)(2,1)S(1)}, bf16[272,256]{1,0:T(8,128)(2,1)S(1)}, u32[]{:S(2)}, u32[]{:S(2)}) collective-permute-start(bf16[272,256]{1,0:T(8,128)(2,1)S(1)} %get-tuple-element.88.refs_2_), channel_id=1, source_target_pairs={{0,12},{1,13},{2,14},{3,15},{4,8},{5,9},{6,10},{7,11},{8,4},{9,5},... | collective-permute-start | bytes 417800 | tf_op jit(solution)/shard_map/ppermute | solution.py:238
  52.2 12.4 %collective-permute-start.21 = (bf16[512,256]{1,0:T(8,128)(2,1)S(1)}, bf16[512,256]{1,0:T(8,128)(2,1)S(1)}, u32[]{:S(2)}, u32[]{:S(2)}) collective-permute-start(bf16[512,256]{1,0:T(8,128)(2,1)S(1)} %shard_map.157.refs_2_.refs_0_), channel_id=1, source_target_pairs={{0,2},{1,5},{2,0},{3,7},{4,6},{5,1},{6,4},{7,3},{8,10},{9,13},{10,... | collective-permute-start | bytes 786440 | tf_op jit(solution)/shard_map/ppermute | solution.py:238
  55.8 5.0 %collective-permute-start.19 = (bf16[128,256]{1,0:T(8,128)(2,1)S(1)}, bf16[128,256]{1,0:T(8,128)(2,1)S(1)}, u32[]{:S(2)}, u32[]{:S(2)}) collective-permute-start(bf16[128,256]{1,0:T(8,128)(2,1)S(1)} %get-tuple-element.96.refs_0_.refs_2_), channel_id=1, source_target_pairs={{0,4},{1,3},{2,6},{3,1},{4,0},{5,7},{6,2},{7,5},{8,12},{9,11},{10,... | collective-permute-start | bytes 196616 | tf_op jit(solution)/shard_map/ppermute | solution.py:238
  55.8 6.7 %collective-permute-start.8 = (bf16[320,256]{1,0:T(8,128)(2,1)S(1)}, bf16[320,256]{1,0:T(8,128)(2,1)S(1)}, u32[]{:S(2)}, u32[]{:S(2)}) collective-permute-start(bf16[320,256]{1,0:T(8,128)(2,1)S(1)} %get-tuple-element.72), channel_id=1, source_target_pairs={{0,1},{1,0},{2,3},{3,2},{4,5},{5,4},{6,7},{7,6},{8,9},{9,8},{10,11... | collective-permute-start | bytes 491528 | tf_op jit(solution)/shard_map/ppermute | solution.py:78
  60.8 5.0 %collective-permute-start.20 = (bf16[256,256]{1,0:T(8,128)(2,1)S(1)}, bf16[256,256]{1,0:T(8,128)(2,1)S(1)}, u32[]{:S(2)}, u32[]{:S(2)}) collective-permute-start(bf16[256,256]{1,0:T(8,128)(2,1)S(1)} %shard_map.160.refs_0_), channel_id=1, source_target_pairs={{0,2},{1,5},{2,0},{3,7},{4,6},{5,1},{6,4},{7,3},{8,10},{9,13},{10,... | collective-permute-start | bytes 393224 | tf_op jit(solution)/shard_map/ppermute | solution.py:238
  62.5 1.3 %collective-permute-start.16 = (bf16[128,256]{1,0:T(8,128)(2,1)S(1)}, bf16[128,256]{1,0:T(8,128)(2,1)S(1)}, u32[]{:S(2)}, u32[]{:S(2)}) collective-permute-start(bf16[128,256]{1,0:T(8,128)(2,1)S(1)} %get-tuple-element.90), channel_id=1, source_target_pairs={{0,1},{1,0},{2,3},{3,2},{4,5},{5,4},{6,7},{7,6},{8,9},{9,8},{10,11... | collective-permute-start | bytes 196616 | tf_op jit(solution)/shard_map/ppermute | solution.py:78

commit v17 on v15

--- a/solution.py
+++ b/solution.py
@@ -287,7 +287,7 @@
         keep_ref[:half, :] = both.astype(keep_ref.dtype)
         send_ref[:half, :] = both
     if tail:
-        both = total_ref[end : end + tail, :].astype(BF16)
+        both = total_ref[total_ref.shape[0] - tail :, :].astype(BF16)
         keep_ref[half:, :] = both.astype(keep_ref.dtype)
         send_ref[half:, :] = both
 
@@ -318,7 +318,7 @@
     rows = begin // bundles
     for i in range(bundles):
         split_half(
-            total_ref, i * rows, rows, step, tail if i == bundles - 1 else 0,
+            total_ref, i * rows, rows, step, 0 if i else tail,
             halves_refs[2 * i], halves_refs[2 * i + 1],
         )
     mine, theirs = other_half(w_node_ref)
@@ -557,7 +557,7 @@
     obs_got = flip(obs_send, steps[0])
     shapes = []
     for i in range(bundles):
-        share = rows // 2 + (tail if i == bundles - 1 else 0)
+        share = rows // 2 + (0 if i else tail)
         shapes += [((share, hidden), F32), ((share, hidden), BF16)]
     node_mine, node_theirs, *shares = call(
         functools.partial(weight_kernel, steps[0], bundles, tail),
@@ -573,23 +573,23 @@
         last = i == bundles - 1
         chains.append(
             weight_chain(
-                steps, rows, tail if last else 0, slots, shares[2 * i], got[i], after, returned if last else None
+                steps, rows, 0 if i else tail, slots, shares[2 * i], got[i], after, returned if last else None
             )
         )
     node_got = shift(node_theirs, "mp", 1)
     middle, last = len(steps) - 1, len(steps) + len(halving_used(steps, rows)) - 1
     turns = [1]
     for step in range(1, last):
-        turns += [2, 1] if step == middle else [1, 2]
         turns += [0] if step < middle else []
         turns += [0] if step == middle - 1 else []
+        turns += [2, 1] if step == middle else [1, 2]
     turns += [2]
     _, *weights = in_turns(chains, turns)
     obs_keep, arrived = weights[-1][2]
     obs_mine, obs_theirs = call(
         obs_kernel, [((obs, half), F32), ((obs, half), BF16)], obs_keep, arrived, w_obs_held
     )
-    (slot_sums,) = weights[-1][1]
+    (slot_sums,) = weights[0][1]
     grad_node, grad_obs, grad_slot = call(
         merge_kernel, [((nodes, half), F32), ((obs, half), BF16), ((slots, hidden), F32)],
         node_mine, node_got, obs_mine, shift(obs_theirs, "mp", 1), slot_sums,

time: 62.1 us -> 61.6 us (level)
  waiting for transfers between devices: 22 us -> 18 us
  starting transfers between devices: 30.3 us -> 33.8 us
    ppermute x12, waiting for transfers between devices: 18.8 us -> 14.8 us  [flip(): return lax.ppermute(value, axes, pairs)]
    ppermute x12, starting transfers between devices: 15.9 us -> 19.4 us  [flip(): return lax.ppermute(value, axes, pairs)]
  transfers between devices with their start and end apart: 22 -> 22, of which waited for: 10 -> 12; matrix products, arithmetic and copies ran while one was open for 0% -> 0% of each run, Pallas kernels for 5% -> 6%
where the time goes in v17:
time: 61.6 us; the launch traced here: 61.4 us
  starting transfers between devices  33.8 us (55%)
  waiting for transfers between devices  18 us (29%)
  Pallas kernels  8.82 us (14%)
  between operations  0.8 us (1%)
    ppermute x12, starting transfers between devices, flip(): return lax.ppermute(value, axes, pairs)  19.4 us
    ppermute x12, waiting for transfers between devices, flip(): return lax.ppermute(value, axes, pairs)  14.8 us
    ppermute x10, starting transfers between devices, shift(): lax.ppermute(value, axis, [(i, (i + step) % size) for i in range(size)])  14.4 us
    pallas_call x15, Pallas kernels, call(): pl.pallas_call(lambda *refs: kernel(*refs[:count], *refs[len(args):]), ou...  5.8 us
    ppermute x10, waiting for transfers between devices, shift(): lax.ppermute(value, axis, [(i, (i + step) % size) for i in range(size)])  3.19 us
    pallas_call x2, Pallas kernels, call_staged(): pl.pallas_call(staged, out_shape=[jax.ShapeDtypeStruct(shape, dtype) for...  3.03 us
  transfers between devices with their start and end apart: 22, of which 12 were waited for; matrix products, arithmetic and copies ran while one was open for 0% of the time, Pallas kernels for 6%

profile of v17, /device:TPU:0, one launch (start us, length us, event | category | flops | bytes accessed | tf_op | source)
XLA Modules:
  0.0 61.4 jit_solution(2849257494771774326)
XLA Ops:
  0.6 1.3 %shard_map.145 = (bf16[144,128]{1,0:T(8,128)(2,1)S(1)}, bf16[144,128]{1,0:T(8,128)(2,1)S(1)}, bf16[144,128]{1,0:T(8,128)(2,1)S(1)}, bf16[144,128]{1,0:T(8,128)(2...) custom-call(bf16[128,512]{1,0:T(8,128)(2,1)} %refs_0_.2, ...), custom_call_target="tpu_custom_call" | custom-call | tf_op jit(solution)/shard_map/pallas_call | solution.py:61
  1.9 3.0 %collective-permute-start = (bf16[144,128]{1,0:T(8,128)(2,1)S(1)}, bf16[144,128]{1,0:T(8,128)(2,1)S(1)}, u32[]{:S(2)}, u32[]{:S(2)}) collective-permute-start(bf16[144,128]{1,0:T(8,128)(2,1)S(1)} %get-tuple-element.55), channel_id=1, source_target_pairs={{0,2},{2,4},{4,6},{6,8},{8,10},{10,12},{12,14},{14,0},{1,3},{3,5},... | collective-permute-start | bytes 110600 | tf_op jit(solution)/shard_map/ppermute | solution.py:79
  4.9 1.6 %collective-permute-start.1 = (bf16[144,128]{1,0:T(8,128)(2,1)S(1)}, bf16[144,128]{1,0:T(8,128)(2,1)S(1)}, u32[]{:S(2)}, u32[]{:S(2)}) collective-permute-start(bf16[144,128]{1,0:T(8,128)(2,1)S(1)} %get-tuple-element.56), channel_id=1, source_target_pairs={{0,4},{2,6},{4,8},{6,10},{8,12},{10,14},{12,0},{14,2},{1,5},{3,7},... | collective-permute-start | bytes 110600 | tf_op jit(solution)/shard_map/ppermute | solution.py:79
  6.5 2.6 %collective-permute-start.2 = (bf16[144,128]{1,0:T(8,128)(2,1)S(1)}, bf16[144,128]{1,0:T(8,128)(2,1)S(1)}, u32[]{:S(2)}, u32[]{:S(2)}) collective-permute-start(bf16[144,128]{1,0:T(8,128)(2,1)S(1)} %get-tuple-element.57), channel_id=1, source_target_pairs={{0,6},{2,8},{4,10},{6,12},{8,14},{10,0},{12,2},{14,4},{1,7},{3,9},... | collective-permute-start | bytes 110600 | tf_op jit(solution)/shard_map/ppermute | solution.py:79
  9.1 1.2 %collective-permute-start.3 = (bf16[144,128]{1,0:T(8,128)(2,1)S(1)}, bf16[144,128]{1,0:T(8,128)(2,1)S(1)}, u32[]{:S(2)}, u32[]{:S(2)}) collective-permute-start(bf16[144,128]{1,0:T(8,128)(2,1)S(1)} %get-tuple-element.58), channel_id=1, source_target_pairs={{0,8},{2,10},{4,12},{6,14},{8,0},{10,2},{12,4},{14,6},{1,9},{3,11}... | collective-permute-start | bytes 110600 | tf_op jit(solution)/shard_map/ppermute | solution.py:79
  10.3 2.6 %collective-permute-start.4 = (bf16[144,128]{1,0:T(8,128)(2,1)S(1)}, bf16[144,128]{1,0:T(8,128)(2,1)S(1)}, u32[]{:S(2)}, u32[]{:S(2)}) collective-permute-start(bf16[144,128]{1,0:T(8,128)(2,1)S(1)} %get-tuple-element.59), channel_id=1, source_target_pairs={{0,10},{2,12},{4,14},{6,0},{8,2},{10,4},{12,6},{14,8},{1,11},{3,13... | collective-permute-start | bytes 110600 | tf_op jit(solution)/shard_map/ppermute | solution.py:79
  12.9 0.0 collective-permute-done.refs_0_
  12.9 1.4 %collective-permute-start.5 = (bf16[144,128]{1,0:T(8,128)(2,1)S(1)}, bf16[144,128]{1,0:T(8,128)(2,1)S(1)}, u32[]{:S(2)}, u32[]{:S(2)}) collective-permute-start(bf16[144,128]{1,0:T(8,128)(2,1)S(1)} %get-tuple-element.60), channel_id=1, source_target_pairs={{0,12},{2,14},{4,0},{6,2},{8,4},{10,6},{12,8},{14,10},{1,13},{3,15... | collective-permute-start | bytes 110600 | tf_op jit(solution)/shard_map/ppermute | solution.py:79
  14.3 0.0 collective-permute-done.1.refs_1_
  14.3 1.4 %collective-permute-start.6 = (bf16[144,128]{1,0:T(8,128)(2,1)S(1)}, bf16[144,128]{1,0:T(8,128)(2,1)S(1)}, u32[]{:S(2)}, u32[]{:S(2)}) collective-permute-start(bf16[144,128]{1,0:T(8,128)(2,1)S(1)} %get-tuple-element.61), channel_id=1, source_target_pairs={{0,14},{2,0},{4,2},{6,4},{8,6},{10,8},{12,10},{14,12},{1,15},{3,1}... | collective-permute-start | bytes 110600 | tf_op jit(solution)/shard_map/ppermute | solution.py:79
  15.7 1.7 %shard_map.146 = (bf16[336,1024]{1,0:T(8,128)(2,1)S(1)}, bf16[320,512]{1,0:T(8,128)(2,1)S(1)}, bf16[320,512]{1,0:T(8,128)(2,1)S(1)}, bf16[512,256]{1,0:T(8,128)(2,1)S(1)}, bf16[512,256]{1,0:T(8,128)(2,1)S(1)}) custom-call(bf16[320,512]{1,0:T(8,128)(2,1)} %refs_0_.3, bf16[320,512]{1,0:T(8,128)(2,1)} %refs_1_.1, bf16[512,256]{1,0:T(8,128)(2,1)} %refs_2_.1, ...), custom_call_target="tpu_custom_call" | custom-call | tf_op jit(solution)/shard_map/pallas_call | solution.py:61
  17.5 0.0 collective-permute-done.3.refs_3_
  17.5 0.8 %collective-permute-done.6.refs_6_ = bf16[144,128]{1,0:T(8,128)(2,1)S(1)} collective-permute-done((bf16[144,128]{1,0:T(8,128)(2,1)S(1)}, bf16[144,128]{1,0:T(8,128)(2,1)S(1)}, u32[]{:S(2)}, u32[]{:S(2)}) %collective-permute-start.6) | collective-permute-done | bytes 36896 | tf_op jit(solution)/shard_map/ppermute | solution.py:79
  18.3 0.1 collective-permute-start.7
  18.3 1.5 %collective-permute-done.7.refs_3_ = bf16[7,144,128]{2,1,0:T(8,128)(2,1)S(1)} collective-permute-done((bf16[7,144,128]{2,1,0:T(8,128)(2,1)S(1)}, bf16[7,144,128]{2,1,0:T(8,128)(2,1)S(1)}, u32[]{:S(2)}, u32[]{:S(2)}) %collective-permute-start.7) | collective-permute-done | bytes 258080 | tf_op jit(solution)/shard_map/ppermute | solution.py:79
  19.9 1.6 %shard_map.148 = (bf16[512,512]{1,0:T(8,128)(2,1)S(1)}, bf16[512,336]{1,0:T(8,128)(2,1)S(1)}, bf16[512,256]{1,0:T(8,128)(2,1)S(1)}, bf16[512,256]{1,0:T(8,128)(2...) custom-call(bf16[144,128]{1,0:T(8,128)(2,1)S(1)} %get-tuple-element.54.refs_0_, ...), custom_call_target="tpu_custom_call" | custom-call | tf_op jit(solution)/shard_map/pallas_call | solution.py:32
  21.5 1.3 %shard_map.149 = (f32[320,256]{1,0:T(8,128)S(1)}, bf16[320,256]{1,0:T(8,128)(2,1)S(1)}, f32[400,256]{1,0:T(8,128)S(1)}, bf16[400,256]{1,0:T(8,128)(2,1)S(1)}, f3...) custom-call(bf16[512,336]{1,0:T(8,128)(2,1)S(1)} %get-tuple-element.65.refs_0_, ...), custom_call_target="tpu_custom_call" | custom-call | tf_op jit(solution)/shard_map/pallas_call | solution.py:32
  22.8 1.6 %collective-permute-start.10 = (bf16[400,256]{1,0:T(8,128)(2,1)S(1)}, bf16[400,256]{1,0:T(8,128)(2,1)S(1)}, u32[]{:S(2)}, u32[]{:S(2)}) collective-permute-start(bf16[400,256]{1,0:T(8,128)(2,1)S(1)} %get-tuple-element.77), channel_id=1, source_target_pairs={{0,2},{1,5},{2,0},{3,7},{4,6},{5,1},{6,4},{7,3},{8,10},{9,13},{10,... | collective-permute-start | bytes 614408 | tf_op jit(solution)/shard_map/ppermute | solution.py:239
  24.4 0.5 collective-permute-start.9
  24.9 1.5 %collective-permute-start.12 = (bf16[256,256]{1,0:T(8,128)(2,1)S(1)}, bf16[256,256]{1,0:T(8,128)(2,1)S(1)}, u32[]{:S(2)}, u32[]{:S(2)}) collective-permute-start(bf16[256,256]{1,0:T(8,128)(2,1)S(1)} %get-tuple-element.81), channel_id=1, source_target_pairs={{0,2},{1,5},{2,0},{3,7},{4,6},{5,1},{6,4},{7,3},{8,10},{9,13},{10,... | collective-permute-start | bytes 393224 | tf_op jit(solution)/shard_map/ppermute | solution.py:239
  26.4 2.2 %collective-permute-done.10.refs_1_ = bf16[400,256]{1,0:T(8,128)(2,1)S(1)} collective-permute-done((bf16[400,256]{1,0:T(8,128)(2,1)S(1)}, bf16[400,256]{1,0:T(8,128)(2,1)S(1)}, u32[]{:S(2)}, u32[]{:S(2)}) %collective-permute-start.10) | collective-permute-done | bytes 204832 | tf_op jit(solution)/shard_map/ppermute | solution.py:239
  28.6 0.1 shard_map.150
  28.7 0.7 %collective-permute-start.11 = (bf16[208,256]{1,0:T(8,128)(2,1)S(1)}, bf16[208,256]{1,0:T(8,128)(2,1)S(1)}, u32[]{:S(2)}, u32[]{:S(2)}) collective-permute-start(bf16[208,256]{1,0:T(8,128)(2,1)S(1)} %get-tuple-element.79.refs_3_), channel_id=1, source_target_pairs={{0,4},{1,3},{2,6},{3,1},{4,0},{5,7},{6,2},{7,5},{8,12},{9,11},{10,... | collective-permute-start | bytes 319496 | tf_op jit(solution)/shard_map/ppermute | solution.py:239
  29.4 3.8 %collective-permute-done.12.refs_1_ = bf16[256,256]{1,0:T(8,128)(2,1)S(1)} collective-permute-done((bf16[256,256]{1,0:T(8,128)(2,1)S(1)}, bf16[256,256]{1,0:T(8,128)(2,1)S(1)}, u32[]{:S(2)}, u32[]{:S(2)}) %collective-permute-start.12) | collective-permute-done | bytes 131104 | tf_op jit(solution)/shard_map/ppermute | solution.py:239
  33.3 0.3 shard_map.151
  33.6 0.7 %collective-permute-start.14 = (bf16[256,256]{1,0:T(8,128)(2,1)S(1)}, bf16[256,256]{1,0:T(8,128)(2,1)S(1)}, u32[]{:S(2)}, u32[]{:S(2)}) collective-permute-start(bf16[256,256]{1,0:T(8,128)(2,1)S(1)} %get-tuple-element.83.refs_2_), channel_id=1, source_target_pairs={{0,4},{1,3},{2,6},{3,1},{4,0},{5,7},{6,2},{7,5},{8,12},{9,11},{10,... | collective-permute-start | bytes 393224 | tf_op jit(solution)/shard_map/ppermute | solution.py:239
  34.3 0.0 collective-permute-done.11.refs_1_
  34.4 0.1 shard_map.153
  34.4 1.4 %collective-permute-start.13 = (bf16[192,256]{1,0:T(8,128)(2,1)S(1)}, bf16[192,256]{1,0:T(8,128)(2,1)S(1)}, u32[]{:S(2)}, u32[]{:S(2)}) collective-permute-start(bf16[192,256]{1,0:T(8,128)(2,1)S(1)} %get-tuple-element.86.refs_4_), channel_id=1, source_target_pairs={{0,4},{1,3},{2,6},{3,1},{4,0},{5,7},{6,2},{7,5},{8,12},{9,11},{10,... | collective-permute-start | bytes 294920 | tf_op jit(solution)/shard_map/ppermute | solution.py:239
  35.9 2.7 %collective-permute-start.17 = (bf16[208,256]{1,0:T(8,128)(2,1)S(1)}, bf16[208,256]{1,0:T(8,128)(2,1)S(1)}, u32[]{:S(2)}, u32[]{:S(2)}) collective-permute-start(bf16[208,256]{1,0:T(8,128)(2,1)S(1)} %get-tuple-element.84.refs_2_), channel_id=1, source_target_pairs={{0,12},{1,13},{2,14},{3,15},{4,8},{5,9},{6,10},{7,11},{8,4},{9,5},... | collective-permute-start | bytes 319496 | tf_op jit(solution)/shard_map/ppermute | solution.py:239
  38.5 0.1 collective-permute-done.14.refs_3_
  38.6 2.2 %collective-permute-done.13.refs_1_ = bf16[192,256]{1,0:T(8,128)(2,1)S(1)} collective-permute-done((bf16[192,256]{1,0:T(8,128)(2,1)S(1)}, bf16[192,256]{1,0:T(8,128)(2,1)S(1)}, u32[]{:S(2)}, u32[]{:S(2)}) %collective-permute-start.13) | collective-permute-done | bytes 98336 | tf_op jit(solution)/shard_map/ppermute | solution.py:239
  40.8 0.1 shard_map.154
  40.9 2.1 %collective-permute-start.15 = (bf16[320,256]{1,0:T(8,128)(2,1)S(1)}, bf16[320,256]{1,0:T(8,128)(2,1)S(1)}, u32[]{:S(2)}, u32[]{:S(2)}) collective-permute-start(bf16[320,256]{1,0:T(8,128)(2,1)S(1)} %get-tuple-element.89.refs_2_), channel_id=1, source_target_pairs={{0,12},{1,13},{2,14},{3,15},{4,8},{5,9},{6,10},{7,11},{8,4},{9,5},... | collective-permute-start | bytes 491528 | tf_op jit(solution)/shard_map/ppermute | solution.py:239
  43.0 0.2 collective-permute-done.17.refs_1_
  43.2 3.0 %collective-permute-start.18 = (bf16[192,256]{1,0:T(8,128)(2,1)S(1)}, bf16[192,256]{1,0:T(8,128)(2,1)S(1)}, u32[]{:S(2)}, u32[]{:S(2)}) collective-permute-start(bf16[192,256]{1,0:T(8,128)(2,1)S(1)} %get-tuple-element.96.refs_0_.refs_2_), channel_id=1, source_target_pairs={{0,4},{1,3},{2,6},{3,1},{4,0},{5,7},{6,2},{7,5},{8,12},{9,11},{10,... | collective-permute-start | bytes 294920 | tf_op jit(solution)/shard_map/ppermute | solution.py:239
  46.2 3.0 %collective-permute-done.18.refs_1_ = bf16[192,256]{1,0:T(8,128)(2,1)S(1)} collective-permute-done((bf16[192,256]{1,0:T(8,128)(2,1)S(1)}, bf16[192,256]{1,0:T(8,128)(2,1)S(1)}, u32[]{:S(2)}, u32[]{:S(2)}) %collective-permute-start.18) | collective-permute-done | bytes 98336 | tf_op jit(solution)/shard_map/ppermute | solution.py:239
  49.3 1.6 %collective-permute-start.20 = (bf16[192,256]{1,0:T(8,128)(2,1)S(1)}, bf16[192,256]{1,0:T(8,128)(2,1)S(1)}, u32[]{:S(2)}, u32[]{:S(2)}) collective-permute-start(bf16[192,256]{1,0:T(8,128)(2,1)S(1)} %shard_map.159.refs_0_.refs_2_), channel_id=1, source_target_pairs={{0,4},{1,3},{2,6},{3,1},{4,0},{5,7},{6,2},{7,5},{8,12},{9,11},{10,... | collective-permute-start | bytes 294920 | tf_op jit(solution)/shard_map/ppermute | solution.py:239
  51.0 1.2 %collective-permute-start.19 = (bf16[384,256]{1,0:T(8,128)(2,1)S(1)}, bf16[384,256]{1,0:T(8,128)(2,1)S(1)}, u32[]{:S(2)}, u32[]{:S(2)}) collective-permute-start(bf16[384,256]{1,0:T(8,128)(2,1)S(1)} %shard_map.158.refs_2_.refs_0_), channel_id=1, source_target_pairs={{0,2},{1,5},{2,0},{3,7},{4,6},{5,1},{6,4},{7,3},{8,10},{9,13},{10,... | collective-permute-start | bytes 589832 | tf_op jit(solution)/shard_map/ppermute | solution.py:239
  52.2 2.1 %collective-permute-done.20.refs_1_ = bf16[192,256]{1,0:T(8,128)(2,1)S(1)} collective-permute-done((bf16[192,256]{1,0:T(8,128)(2,1)S(1)}, bf16[192,256]{1,0:T(8,128)(2,1)S(1)}, u32[]{:S(2)}, u32[]{:S(2)}) %collective-permute-start.20) | collective-permute-done | bytes 98336 | tf_op jit(solution)/shard_map/ppermute | solution.py:239
  54.3 2.3 %collective-permute-start.21 = (bf16[384,256]{1,0:T(8,128)(2,1)S(1)}, bf16[384,256]{1,0:T(8,128)(2,1)S(1)}, u32[]{:S(2)}, u32[]{:S(2)}) collective-permute-start(bf16[384,256]{1,0:T(8,128)(2,1)S(1)} %shard_map.160.refs_2_), channel_id=1, source_target_pairs={{0,2},{1,5},{2,0},{3,7},{4,6},{5,1},{6,4},{7,3},{8,10},{9,13},{10,... | collective-permute-start | bytes 589832 | tf_op jit(solution)/shard_map/ppermute | solution.py:239
  56.6 0.2 shard_map.155
  56.8 0.6 collective-permute-start.16
  57.4 0.6 collective-permute-done.8.refs_1_
  58.0 0.3 collective-permute-done.16.refs_3_
  58.3 0.8 %shard_map.157 = (f32[320,256]{1,0:T(8,128)}, bf16[128,256]{1,0:T(8,128)(2,1)}, f32[6,256]{1,0:T(8,128)}) custom-call(f32[320,256]{1,0:T(8,128)S(1)} %get-tuple-element.72.refs_0_, bf16[320,256]{1,0:T(8,128)(2,1)S(1)} %collective-permute-done.8.refs_1_, f32[128,256]{1,0:T(8,128)S(1)} %get-tuple-element.90.refs_2_, ...), custom_call_target="tpu_custom_call" | custom-call | tf_op jit(solution)/shard_map/pallas_call | solution.py:32
  59.1 1.1 %collective-permute-done.21.refs_3_ = bf16[384,256]{1,0:T(8,128)(2,1)S(1)} collective-permute-done((bf16[384,256]{1,0:T(8,128)(2,1)S(1)}, bf16[384,256]{1,0:T(8,128)(2,1)S(1)}, u32[]{:S(2)}, u32[]{:S(2)}) %collective-permute-start.21) | collective-permute-done | bytes 196640 | tf_op jit(solution)/shard_map/ppermute | solution.py:239
  60.2 1.2 %shard_map.161 = (f32[512,256]{1,0:T(8,128)}, f32[256,512]{1,0:T(8,128)}, f32[512,256]{1,0:T(8,128)}) custom-call(bf16[384,256]{1,0:T(8,128)(2,1)S(1)} %shard_map.158.refs_2_.refs_0_, bf16[384,256]{1,0:T(8,128)(2,1)S(1)} %collective-permute-done.19.refs_1_, bf16[384,256]{1,0:T(8,128)(2,1)S(1)} %shard_map.160.refs_2_, ...), custom_call_target="tpu_custom_call" | custom-call | tf_op jit(solution)/shard_map/pallas_call | solution.py:32
  (13 shorter events, 0.2 us)
Async XLA Ops:
  1.9 11.0 %collective-permute-start = (bf16[144,128]{1,0:T(8,128)(2,1)S(1)}, bf16[144,128]{1,0:T(8,128)(2,1)S(1)}, u32[]{:S(2)}, u32[]{:S(2)}) collective-permute-start(bf16[144,128]{1,0:T(8,128)(2,1)S(1)} %get-tuple-element.55), channel_id=1, source_target_pairs={{0,2},{2,4},{4,6},{6,8},{8,10},{10,12},{12,14},{14,0},{1,3},{3,5},... | collective-permute-start | bytes 110600 | tf_op jit(solution)/shard_map/ppermute | solution.py:79
  4.9 9.3 %collective-permute-start.1 = (bf16[144,128]{1,0:T(8,128)(2,1)S(1)}, bf16[144,128]{1,0:T(8,128)(2,1)S(1)}, u32[]{:S(2)}, u32[]{:S(2)}) collective-permute-start(bf16[144,128]{1,0:T(8,128)(2,1)S(1)} %get-tuple-element.56), channel_id=1, source_target_pairs={{0,4},{2,6},{4,8},{6,10},{8,12},{10,14},{12,0},{14,2},{1,5},{3,7},... | collective-permute-start | bytes 110600 | tf_op jit(solution)/shard_map/ppermute | solution.py:79
  6.5 10.9 %collective-permute-start.2 = (bf16[144,128]{1,0:T(8,128)(2,1)S(1)}, bf16[144,128]{1,0:T(8,128)(2,1)S(1)}, u32[]{:S(2)}, u32[]{:S(2)}) collective-permute-start(bf16[144,128]{1,0:T(8,128)(2,1)S(1)} %get-tuple-element.57), channel_id=1, source_target_pairs={{0,6},{2,8},{4,10},{6,12},{8,14},{10,0},{12,2},{14,4},{1,7},{3,9},... | collective-permute-start | bytes 110600 | tf_op jit(solution)/shard_map/ppermute | solution.py:79
  9.1 8.4 %collective-permute-start.3 = (bf16[144,128]{1,0:T(8,128)(2,1)S(1)}, bf16[144,128]{1,0:T(8,128)(2,1)S(1)}, u32[]{:S(2)}, u32[]{:S(2)}) collective-permute-start(bf16[144,128]{1,0:T(8,128)(2,1)S(1)} %get-tuple-element.58), channel_id=1, source_target_pairs={{0,8},{2,10},{4,12},{6,14},{8,0},{10,2},{12,4},{14,6},{1,9},{3,11}... | collective-permute-start | bytes 110600 | tf_op jit(solution)/shard_map/ppermute | solution.py:79
  10.3 7.2 %collective-permute-start.4 = (bf16[144,128]{1,0:T(8,128)(2,1)S(1)}, bf16[144,128]{1,0:T(8,128)(2,1)S(1)}, u32[]{:S(2)}, u32[]{:S(2)}) collective-permute-start(bf16[144,128]{1,0:T(8,128)(2,1)S(1)} %get-tuple-element.59), channel_id=1, source_target_pairs={{0,10},{2,12},{4,14},{6,0},{8,2},{10,4},{12,6},{14,8},{1,11},{3,13... | collective-permute-start | bytes 110600 | tf_op jit(solution)/shard_map/ppermute | solution.py:79
  12.9 4.5 %collective-permute-start.5 = (bf16[144,128]{1,0:T(8,128)(2,1)S(1)}, bf16[144,128]{1,0:T(8,128)(2,1)S(1)}, u32[]{:S(2)}, u32[]{:S(2)}) collective-permute-start(bf16[144,128]{1,0:T(8,128)(2,1)S(1)} %get-tuple-element.60), channel_id=1, source_target_pairs={{0,12},{2,14},{4,0},{6,2},{8,4},{10,6},{12,8},{14,10},{1,13},{3,15... | collective-permute-start | bytes 110600 | tf_op jit(solution)/shard_map/ppermute | solution.py:79
  14.3 4.0 %collective-permute-start.6 = (bf16[144,128]{1,0:T(8,128)(2,1)S(1)}, bf16[144,128]{1,0:T(8,128)(2,1)S(1)}, u32[]{:S(2)}, u32[]{:S(2)}) collective-permute-start(bf16[144,128]{1,0:T(8,128)(2,1)S(1)} %get-tuple-element.61), channel_id=1, source_target_pairs={{0,14},{2,0},{4,2},{6,4},{8,6},{10,8},{12,10},{14,12},{1,15},{3,1}... | collective-permute-start | bytes 110600 | tf_op jit(solution)/shard_map/ppermute | solution.py:79
  18.3 1.6 %collective-permute-start.7 = (bf16[7,144,128]{2,1,0:T(8,128)(2,1)S(1)}, bf16[7,144,128]{2,1,0:T(8,128)(2,1)S(1)}, u32[]{:S(2)}, u32[]{:S(2)}) collective-permute-start(bf16[7,144,128]{2,1,0:T(8,128)(2,1)S(1)} %shard_map.147.refs_1_), channel_id=1, source_target_pairs={{0,1},{1,0},{2,3},{3,2},{4,5},{5,4},{6,7},{7,6},{8,9},{9,8},{10,11... | collective-permute-start | bytes 774152 | tf_op jit(solution)/shard_map/ppermute | solution.py:79
  22.8 5.8 %collective-permute-start.10 = (bf16[400,256]{1,0:T(8,128)(2,1)S(1)}, bf16[400,256]{1,0:T(8,128)(2,1)S(1)}, u32[]{:S(2)}, u32[]{:S(2)}) collective-permute-start(bf16[400,256]{1,0:T(8,128)(2,1)S(1)} %get-tuple-element.77), channel_id=1, source_target_pairs={{0,2},{1,5},{2,0},{3,7},{4,6},{5,1},{6,4},{7,3},{8,10},{9,13},{10,... | collective-permute-start | bytes 614408 | tf_op jit(solution)/shard_map/ppermute | solution.py:239
  24.4 10.0 %collective-permute-start.9 = (bf16[384,256]{1,0:T(8,128)(2,1)S(1)}, bf16[384,256]{1,0:T(8,128)(2,1)S(1)}, u32[]{:S(2)}, u32[]{:S(2)}) collective-permute-start(bf16[384,256]{1,0:T(8,128)(2,1)S(1)} %get-tuple-element.75), channel_id=1, source_target_pairs={{0,2},{1,5},{2,0},{3,7},{4,6},{5,1},{6,4},{7,3},{8,10},{9,13},{10,... | collective-permute-start | bytes 589832 | tf_op jit(solution)/shard_map/ppermute | solution.py:239
  24.9 8.4 %collective-permute-start.12 = (bf16[256,256]{1,0:T(8,128)(2,1)S(1)}, bf16[256,256]{1,0:T(8,128)(2,1)S(1)}, u32[]{:S(2)}, u32[]{:S(2)}) collective-permute-start(bf16[256,256]{1,0:T(8,128)(2,1)S(1)} %get-tuple-element.81), channel_id=1, source_target_pairs={{0,2},{1,5},{2,0},{3,7},{4,6},{5,1},{6,4},{7,3},{8,10},{9,13},{10,... | collective-permute-start | bytes 393224 | tf_op jit(solution)/shard_map/ppermute | solution.py:239
  28.7 5.6 %collective-permute-start.11 = (bf16[208,256]{1,0:T(8,128)(2,1)S(1)}, bf16[208,256]{1,0:T(8,128)(2,1)S(1)}, u32[]{:S(2)}, u32[]{:S(2)}) collective-permute-start(bf16[208,256]{1,0:T(8,128)(2,1)S(1)} %get-tuple-element.79.refs_3_), channel_id=1, source_target_pairs={{0,4},{1,3},{2,6},{3,1},{4,0},{5,7},{6,2},{7,5},{8,12},{9,11},{10,... | collective-permute-start | bytes 319496 | tf_op jit(solution)/shard_map/ppermute | solution.py:239
  33.6 5.0 %collective-permute-start.14 = (bf16[256,256]{1,0:T(8,128)(2,1)S(1)}, bf16[256,256]{1,0:T(8,128)(2,1)S(1)}, u32[]{:S(2)}, u32[]{:S(2)}) collective-permute-start(bf16[256,256]{1,0:T(8,128)(2,1)S(1)} %get-tuple-element.83.refs_2_), channel_id=1, source_target_pairs={{0,4},{1,3},{2,6},{3,1},{4,0},{5,7},{6,2},{7,5},{8,12},{9,11},{10,... | collective-permute-start | bytes 393224 | tf_op jit(solution)/shard_map/ppermute | solution.py:239
  34.4 6.4 %collective-permute-start.13 = (bf16[192,256]{1,0:T(8,128)(2,1)S(1)}, bf16[192,256]{1,0:T(8,128)(2,1)S(1)}, u32[]{:S(2)}, u32[]{:S(2)}) collective-permute-start(bf16[192,256]{1,0:T(8,128)(2,1)S(1)} %get-tuple-element.86.refs_4_), channel_id=1, source_target_pairs={{0,4},{1,3},{2,6},{3,1},{4,0},{5,7},{6,2},{7,5},{8,12},{9,11},{10,... | collective-permute-start | bytes 294920 | tf_op jit(solution)/shard_map/ppermute | solution.py:239
  35.9 7.3 %collective-permute-start.17 = (bf16[208,256]{1,0:T(8,128)(2,1)S(1)}, bf16[208,256]{1,0:T(8,128)(2,1)S(1)}, u32[]{:S(2)}, u32[]{:S(2)}) collective-permute-start(bf16[208,256]{1,0:T(8,128)(2,1)S(1)} %get-tuple-element.84.refs_2_), channel_id=1, source_target_pairs={{0,12},{1,13},{2,14},{3,15},{4,8},{5,9},{6,10},{7,11},{8,4},{9,5},... | collective-permute-start | bytes 319496 | tf_op jit(solution)/shard_map/ppermute | solution.py:239
  40.9 8.4 %collective-permute-start.15 = (bf16[320,256]{1,0:T(8,128)(2,1)S(1)}, bf16[320,256]{1,0:T(8,128)(2,1)S(1)}, u32[]{:S(2)}, u32[]{:S(2)}) collective-permute-start(bf16[320,256]{1,0:T(8,128)(2,1)S(1)} %get-tuple-element.89.refs_2_), channel_id=1, source_target_pairs={{0,12},{1,13},{2,14},{3,15},{4,8},{5,9},{6,10},{7,11},{8,4},{9,5},... | collective-permute-start | bytes 491528 | tf_op jit(solution)/shard_map/ppermute | solution.py:239
  43.2 6.0 %collective-permute-start.18 = (bf16[192,256]{1,0:T(8,128)(2,1)S(1)}, bf16[192,256]{1,0:T(8,128)(2,1)S(1)}, u32[]{:S(2)}, u32[]{:S(2)}) collective-permute-start(bf16[192,256]{1,0:T(8,128)(2,1)S(1)} %get-tuple-element.96.refs_0_.refs_2_), channel_id=1, source_target_pairs={{0,4},{1,3},{2,6},{3,1},{4,0},{5,7},{6,2},{7,5},{8,12},{9,11},{10,... | collective-permute-start | bytes 294920 | tf_op jit(solution)/shard_map/ppermute | solution.py:239
  49.3 5.0 %collective-permute-start.20 = (bf16[192,256]{1,0:T(8,128)(2,1)S(1)}, bf16[192,256]{1,0:T(8,128)(2,1)S(1)}, u32[]{:S(2)}, u32[]{:S(2)}) collective-permute-start(bf16[192,256]{1,0:T(8,128)(2,1)S(1)} %shard_map.159.refs_0_.refs_2_), channel_id=1, source_target_pairs={{0,4},{1,3},{2,6},{3,1},{4,0},{5,7},{6,2},{7,5},{8,12},{9,11},{10,... | collective-permute-start | bytes 294920 | tf_op jit(solution)/shard_map/ppermute | solution.py:239
  51.0 8.1 %collective-permute-start.19 = (bf16[384,256]{1,0:T(8,128)(2,1)S(1)}, bf16[384,256]{1,0:T(8,128)(2,1)S(1)}, u32[]{:S(2)}, u32[]{:S(2)}) collective-permute-start(bf16[384,256]{1,0:T(8,128)(2,1)S(1)} %shard_map.158.refs_2_.refs_0_), channel_id=1, source_target_pairs={{0,2},{1,5},{2,0},{3,7},{4,6},{5,1},{6,4},{7,3},{8,10},{9,13},{10,... | collective-permute-start | bytes 589832 | tf_op jit(solution)/shard_map/ppermute | solution.py:239
  54.3 5.9 %collective-permute-start.21 = (bf16[384,256]{1,0:T(8,128)(2,1)S(1)}, bf16[384,256]{1,0:T(8,128)(2,1)S(1)}, u32[]{:S(2)}, u32[]{:S(2)}) collective-permute-start(bf16[384,256]{1,0:T(8,128)(2,1)S(1)} %shard_map.160.refs_2_), channel_id=1, source_target_pairs={{0,2},{1,5},{2,0},{3,7},{4,6},{5,1},{6,4},{7,3},{8,10},{9,13},{10,... | collective-permute-start | bytes 589832 | tf_op jit(solution)/shard_map/ppermute | solution.py:239
  56.6 1.4 %collective-permute-start.8 = (bf16[320,256]{1,0:T(8,128)(2,1)S(1)}, bf16[320,256]{1,0:T(8,128)(2,1)S(1)}, u32[]{:S(2)}, u32[]{:S(2)}) collective-permute-start(bf16[320,256]{1,0:T(8,128)(2,1)S(1)} %get-tuple-element.73), channel_id=1, source_target_pairs={{0,1},{1,0},{2,3},{3,2},{4,5},{5,4},{6,7},{7,6},{8,9},{9,8},{10,11... | collective-permute-start | bytes 491528 | tf_op jit(solution)/shard_map/ppermute | solution.py:79
  56.8 1.5 %collective-permute-start.16 = (bf16[128,256]{1,0:T(8,128)(2,1)S(1)}, bf16[128,256]{1,0:T(8,128)(2,1)S(1)}, u32[]{:S(2)}, u32[]{:S(2)}) collective-permute-start(bf16[128,256]{1,0:T(8,128)(2,1)S(1)} %get-tuple-element.91), channel_id=1, source_target_pairs={{0,1},{1,0},{2,3},{3,2},{4,5},{5,4},{6,7},{7,6},{8,9},{9,8},{10,11... | collective-permute-start | bytes 196616 | tf_op jit(solution)/shard_map/ppermute | solution.py:79

commit v18 on v17

--- a/solution.py
+++ b/solution.py
@@ -378,14 +378,13 @@
     out_ref[pl.ds(pl.multiple_of((1 - bit) * rows, SUBLANES), rows), :] = got_ref[...]
 
 
-def spread_kernel(step, bundles, *refs):
+def spread_kernel(step, bundles, at, *refs):
     low = own_bit(step) == 0
     joined = []
     for i in range(bundles):
         mine, got = refs[2 * i][...], refs[2 * i + 1][...]
         joined += [jnp.where(low, mine, got), jnp.where(low, got, mine)]
     half, hidden = joined[0].shape
-    at = 0
     for out_ref in refs[2 * bundles :]:
         for c in range(out_ref.shape[1] // hidden):
             begin = 0
@@ -595,11 +594,17 @@
         node_mine, node_got, obs_mine, shift(obs_theirs, "mp", 1), slot_sums,
     )
     ends = [end for pair, *_ in weights for end in pair]
-    grad_w_node, grad_w_out, grad_w_obs = call(
-        functools.partial(spread_kernel, steps[0], bundles),
-        [((width, hidden), F32), ((hidden, width), F32), ((width, hidden), F32)],
+    (grad_w_node,) = call(
+        functools.partial(spread_kernel, steps[0], 1, 0),
+        [((width, hidden), F32)],
+        *ends[:2],
+        after=[pltpu.with_memory_space_constraint(grad_obs, pltpu.HBM)],
+    )
+    grad_w_out, grad_w_obs = call(
+        functools.partial(spread_kernel, steps[0], bundles, width),
+        [((hidden, width), F32), ((width, hidden), F32)],
         *ends,
-        after=[pltpu.with_memory_space_constraint(grad_obs, pltpu.HBM)],
+        after=[pltpu.with_memory_space_constraint(grad_w_node, pltpu.HBM)],
     )
     return grad_obs, grad_node, grad_w_obs, grad_w_node, grad_w_out, grad_slot
 

time: 61.6 us -> 61.4 us (level)
  waiting for transfers between devices: 18 us -> 17.2 us
  Pallas kernels: 8.82 us -> 9.49 us
    ppermute x12, waiting for transfers between devices: 14.8 us -> 14 us  [flip(): return lax.ppermute(value, axes, pairs)]
    pallas_call x15 -> x16, Pallas kernels: 5.8 us -> 6.47 us  [call(): pl.pallas_call(lambda *refs: kernel(*refs[:count], *refs[len(args):]), ou...]
  transfers between devices with their start and end apart: 22 -> 22, of which waited for: 12 -> 12; matrix products, arithmetic and copies ran while one was open for 0% -> 0% of each run, Pallas kernels for 6% -> 7%
where the time goes in v18:
time: 61.4 us; the launch traced here: 61.3 us
  starting transfers between devices  33.8 us (55%)
  waiting for transfers between devices  17.2 us (28%)
  Pallas kernels  9.49 us (15%)
  between operations  0.8 us (1%)
    ppermute x12, starting transfers between devices, flip(): return lax.ppermute(value, axes, pairs)  19.4 us
    ppermute x10, starting transfers between devices, shift(): lax.ppermute(value, axis, [(i, (i + step) % size) for i in range(size)])  14.4 us
    ppermute x12, waiting for transfers between devices, flip(): return lax.ppermute(value, axes, pairs)  14 us
    pallas_call x16, Pallas kernels, call(): pl.pallas_call(lambda *refs: kernel(*refs[:count], *refs[len(args):]), ou...  6.47 us
    ppermute x10, waiting for transfers between devices, shift(): lax.ppermute(value, axis, [(i, (i + step) % size) for i in range(size)])  3.19 us
    pallas_call x2, Pallas kernels, call_staged(): pl.pallas_call(staged, out_shape=[jax.ShapeDtypeStruct(shape, dtype) for...  3.03 us
  transfers between devices with their start and end apart: 22, of which 12 were waited for; matrix products, arithmetic and copies ran while one was open for 0% of the time, Pallas kernels for 7%

profile of v18, /device:TPU:0, one launch (start us, length us, event | category | flops | bytes accessed | tf_op | source)
XLA Modules:
  0.0 61.3 jit_solution(12302755528306532572)
XLA Ops:
  0.6 1.3 %shard_map.145 = (bf16[144,128]{1,0:T(8,128)(2,1)S(1)}, bf16[144,128]{1,0:T(8,128)(2,1)S(1)}, bf16[144,128]{1,0:T(8,128)(2,1)S(1)}, bf16[144,128]{1,0:T(8,128)(2...) custom-call(bf16[128,512]{1,0:T(8,128)(2,1)} %refs_0_.2, ...), custom_call_target="tpu_custom_call" | custom-call | tf_op jit(solution)/shard_map/pallas_call | solution.py:61
  1.9 3.0 %collective-permute-start = (bf16[144,128]{1,0:T(8,128)(2,1)S(1)}, bf16[144,128]{1,0:T(8,128)(2,1)S(1)}, u32[]{:S(2)}, u32[]{:S(2)}) collective-permute-start(bf16[144,128]{1,0:T(8,128)(2,1)S(1)} %get-tuple-element.54), channel_id=1, source_target_pairs={{0,2},{2,4},{4,6},{6,8},{8,10},{10,12},{12,14},{14,0},{1,3},{3,5},... | collective-permute-start | bytes 110600 | tf_op jit(solution)/shard_map/ppermute | solution.py:79
  4.9 1.6 %collective-permute-start.1 = (bf16[144,128]{1,0:T(8,128)(2,1)S(1)}, bf16[144,128]{1,0:T(8,128)(2,1)S(1)}, u32[]{:S(2)}, u32[]{:S(2)}) collective-permute-start(bf16[144,128]{1,0:T(8,128)(2,1)S(1)} %get-tuple-element.55), channel_id=1, source_target_pairs={{0,4},{2,6},{4,8},{6,10},{8,12},{10,14},{12,0},{14,2},{1,5},{3,7},... | collective-permute-start | bytes 110600 | tf_op jit(solution)/shard_map/ppermute | solution.py:79
  6.5 2.6 %collective-permute-start.2 = (bf16[144,128]{1,0:T(8,128)(2,1)S(1)}, bf16[144,128]{1,0:T(8,128)(2,1)S(1)}, u32[]{:S(2)}, u32[]{:S(2)}) collective-permute-start(bf16[144,128]{1,0:T(8,128)(2,1)S(1)} %get-tuple-element.56), channel_id=1, source_target_pairs={{0,6},{2,8},{4,10},{6,12},{8,14},{10,0},{12,2},{14,4},{1,7},{3,9},... | collective-permute-start | bytes 110600 | tf_op jit(solution)/shard_map/ppermute | solution.py:79
  9.1 1.2 %collective-permute-start.3 = (bf16[144,128]{1,0:T(8,128)(2,1)S(1)}, bf16[144,128]{1,0:T(8,128)(2,1)S(1)}, u32[]{:S(2)}, u32[]{:S(2)}) collective-permute-start(bf16[144,128]{1,0:T(8,128)(2,1)S(1)} %get-tuple-element.57), channel_id=1, source_target_pairs={{0,8},{2,10},{4,12},{6,14},{8,0},{10,2},{12,4},{14,6},{1,9},{3,11}... | collective-permute-start | bytes 110600 | tf_op jit(solution)/shard_map/ppermute | solution.py:79
  10.3 2.6 %collective-permute-start.4 = (bf16[144,128]{1,0:T(8,128)(2,1)S(1)}, bf16[144,128]{1,0:T(8,128)(2,1)S(1)}, u32[]{:S(2)}, u32[]{:S(2)}) collective-permute-start(bf16[144,128]{1,0:T(8,128)(2,1)S(1)} %get-tuple-element.58), channel_id=1, source_target_pairs={{0,10},{2,12},{4,14},{6,0},{8,2},{10,4},{12,6},{14,8},{1,11},{3,13... | collective-permute-start | bytes 110600 | tf_op jit(solution)/shard_map/ppermute | solution.py:79
  12.9 1.4 %collective-permute-start.5 = (bf16[144,128]{1,0:T(8,128)(2,1)S(1)}, bf16[144,128]{1,0:T(8,128)(2,1)S(1)}, u32[]{:S(2)}, u32[]{:S(2)}) collective-permute-start(bf16[144,128]{1,0:T(8,128)(2,1)S(1)} %get-tuple-element.59), channel_id=1, source_target_pairs={{0,12},{2,14},{4,0},{6,2},{8,4},{10,6},{12,8},{14,10},{1,13},{3,15... | collective-permute-start | bytes 110600 | tf_op jit(solution)/shard_map/ppermute | solution.py:79
  14.3 1.4 %collective-permute-start.6 = (bf16[144,128]{1,0:T(8,128)(2,1)S(1)}, bf16[144,128]{1,0:T(8,128)(2,1)S(1)}, u32[]{:S(2)}, u32[]{:S(2)}) collective-permute-start(bf16[144,128]{1,0:T(8,128)(2,1)S(1)} %get-tuple-element.60), channel_id=1, source_target_pairs={{0,14},{2,0},{4,2},{6,4},{8,6},{10,8},{12,10},{14,12},{1,15},{3,1}... | collective-permute-start | bytes 110600 | tf_op jit(solution)/shard_map/ppermute | solution.py:79
  15.7 1.7 %shard_map.146 = (bf16[336,1024]{1,0:T(8,128)(2,1)S(1)}, bf16[320,512]{1,0:T(8,128)(2,1)S(1)}, bf16[320,512]{1,0:T(8,128)(2,1)S(1)}, bf16[512,256]{1,0:T(8,128)(2,1)S(1)}, bf16[512,256]{1,0:T(8,128)(2,1)S(1)}) custom-call(bf16[320,512]{1,0:T(8,128)(2,1)} %refs_0_.3, bf16[320,512]{1,0:T(8,128)(2,1)} %refs_1_.1, bf16[512,256]{1,0:T(8,128)(2,1)} %refs_2_.1, ...), custom_call_target="tpu_custom_call" | custom-call | tf_op jit(solution)/shard_map/pallas_call | solution.py:61
  17.4 0.0 collective-permute-done.2.refs_2_
  17.5 0.0 collective-permute-done.4.refs_4_
  17.5 0.0 collective-permute-done.5.refs_5_
  17.5 0.8 %collective-permute-done.6.refs_6_ = bf16[144,128]{1,0:T(8,128)(2,1)S(1)} collective-permute-done((bf16[144,128]{1,0:T(8,128)(2,1)S(1)}, bf16[144,128]{1,0:T(8,128)(2,1)S(1)}, u32[]{:S(2)}, u32[]{:S(2)}) %collective-permute-start.6) | collective-permute-done | bytes 36896 | tf_op jit(solution)/shard_map/ppermute | solution.py:79
  18.3 0.1 collective-permute-start.7
  18.3 1.5 %collective-permute-done.7.refs_3_ = bf16[7,144,128]{2,1,0:T(8,128)(2,1)S(1)} collective-permute-done((bf16[7,144,128]{2,1,0:T(8,128)(2,1)S(1)}, bf16[7,144,128]{2,1,0:T(8,128)(2,1)S(1)}, u32[]{:S(2)}, u32[]{:S(2)}) %collective-permute-start.7) | collective-permute-done | bytes 258080 | tf_op jit(solution)/shard_map/ppermute | solution.py:79
  19.9 1.6 %shard_map.148 = (bf16[512,512]{1,0:T(8,128)(2,1)S(1)}, bf16[512,336]{1,0:T(8,128)(2,1)S(1)}, bf16[512,256]{1,0:T(8,128)(2,1)S(1)}, bf16[512,256]{1,0:T(8,128)(2...) custom-call(bf16[144,128]{1,0:T(8,128)(2,1)S(1)} %get-tuple-element.53.refs_0_, ...), custom_call_target="tpu_custom_call" | custom-call | tf_op jit(solution)/shard_map/pallas_call | solution.py:32
  21.5 1.3 %shard_map.149 = (f32[320,256]{1,0:T(8,128)S(1)}, bf16[320,256]{1,0:T(8,128)(2,1)S(1)}, f32[400,256]{1,0:T(8,128)S(1)}, bf16[400,256]{1,0:T(8,128)(2,1)S(1)}, f3...) custom-call(bf16[512,336]{1,0:T(8,128)(2,1)S(1)} %get-tuple-element.64.refs_0_, ...), custom_call_target="tpu_custom_call" | custom-call | tf_op jit(solution)/shard_map/pallas_call | solution.py:32
  22.8 1.6 %collective-permute-start.10 = (bf16[400,256]{1,0:T(8,128)(2,1)S(1)}, bf16[400,256]{1,0:T(8,128)(2,1)S(1)}, u32[]{:S(2)}, u32[]{:S(2)}) collective-permute-start(bf16[400,256]{1,0:T(8,128)(2,1)S(1)} %get-tuple-element.76), channel_id=1, source_target_pairs={{0,2},{1,5},{2,0},{3,7},{4,6},{5,1},{6,4},{7,3},{8,10},{9,13},{10,... | collective-permute-start | bytes 614408 | tf_op jit(solution)/shard_map/ppermute | solution.py:239
  24.4 0.5 collective-permute-start.9
  24.9 1.5 %collective-permute-start.12 = (bf16[256,256]{1,0:T(8,128)(2,1)S(1)}, bf16[256,256]{1,0:T(8,128)(2,1)S(1)}, u32[]{:S(2)}, u32[]{:S(2)}) collective-permute-start(bf16[256,256]{1,0:T(8,128)(2,1)S(1)} %get-tuple-element.80), channel_id=1, source_target_pairs={{0,2},{1,5},{2,0},{3,7},{4,6},{5,1},{6,4},{7,3},{8,10},{9,13},{10,... | collective-permute-start | bytes 393224 | tf_op jit(solution)/shard_map/ppermute | solution.py:239
  26.4 2.2 %collective-permute-done.10.refs_1_ = bf16[400,256]{1,0:T(8,128)(2,1)S(1)} collective-permute-done((bf16[400,256]{1,0:T(8,128)(2,1)S(1)}, bf16[400,256]{1,0:T(8,128)(2,1)S(1)}, u32[]{:S(2)}, u32[]{:S(2)}) %collective-permute-start.10) | collective-permute-done | bytes 204832 | tf_op jit(solution)/shard_map/ppermute | solution.py:239
  28.6 0.1 shard_map.150
  28.7 0.7 %collective-permute-start.11 = (bf16[208,256]{1,0:T(8,128)(2,1)S(1)}, bf16[208,256]{1,0:T(8,128)(2,1)S(1)}, u32[]{:S(2)}, u32[]{:S(2)}) collective-permute-start(bf16[208,256]{1,0:T(8,128)(2,1)S(1)} %get-tuple-element.78.refs_3_), channel_id=1, source_target_pairs={{0,4},{1,3},{2,6},{3,1},{4,0},{5,7},{6,2},{7,5},{8,12},{9,11},{10,... | collective-permute-start | bytes 319496 | tf_op jit(solution)/shard_map/ppermute | solution.py:239
  29.4 3.8 %collective-permute-done.12.refs_1_ = bf16[256,256]{1,0:T(8,128)(2,1)S(1)} collective-permute-done((bf16[256,256]{1,0:T(8,128)(2,1)S(1)}, bf16[256,256]{1,0:T(8,128)(2,1)S(1)}, u32[]{:S(2)}, u32[]{:S(2)}) %collective-permute-start.12) | collective-permute-done | bytes 131104 | tf_op jit(solution)/shard_map/ppermute | solution.py:239
  33.3 0.3 shard_map.151
  33.6 0.7 %collective-permute-start.14 = (bf16[256,256]{1,0:T(8,128)(2,1)S(1)}, bf16[256,256]{1,0:T(8,128)(2,1)S(1)}, u32[]{:S(2)}, u32[]{:S(2)}) collective-permute-start(bf16[256,256]{1,0:T(8,128)(2,1)S(1)} %get-tuple-element.82.refs_2_), channel_id=1, source_target_pairs={{0,4},{1,3},{2,6},{3,1},{4,0},{5,7},{6,2},{7,5},{8,12},{9,11},{10,... | collective-permute-start | bytes 393224 | tf_op jit(solution)/shard_map/ppermute | solution.py:239
  34.4 0.1 shard_map.153
  34.4 1.4 %collective-permute-start.13 = (bf16[192,256]{1,0:T(8,128)(2,1)S(1)}, bf16[192,256]{1,0:T(8,128)(2,1)S(1)}, u32[]{:S(2)}, u32[]{:S(2)}) collective-permute-start(bf16[192,256]{1,0:T(8,128)(2,1)S(1)} %get-tuple-element.85.refs_4_), channel_id=1, source_target_pairs={{0,4},{1,3},{2,6},{3,1},{4,0},{5,7},{6,2},{7,5},{8,12},{9,11},{10,... | collective-permute-start | bytes 294920 | tf_op jit(solution)/shard_map/ppermute | solution.py:239
  35.9 2.7 %collective-permute-start.17 = (bf16[208,256]{1,0:T(8,128)(2,1)S(1)}, bf16[208,256]{1,0:T(8,128)(2,1)S(1)}, u32[]{:S(2)}, u32[]{:S(2)}) collective-permute-start(bf16[208,256]{1,0:T(8,128)(2,1)S(1)} %get-tuple-element.83.refs_2_), channel_id=1, source_target_pairs={{0,12},{1,13},{2,14},{3,15},{4,8},{5,9},{6,10},{7,11},{8,4},{9,5},... | collective-permute-start | bytes 319496 | tf_op jit(solution)/shard_map/ppermute | solution.py:239
  38.5 0.1 collective-permute-done.14.refs_3_
  38.6 2.2 %collective-permute-done.13.refs_1_ = bf16[192,256]{1,0:T(8,128)(2,1)S(1)} collective-permute-done((bf16[192,256]{1,0:T(8,128)(2,1)S(1)}, bf16[192,256]{1,0:T(8,128)(2,1)S(1)}, u32[]{:S(2)}, u32[]{:S(2)}) %collective-permute-start.13) | collective-permute-done | bytes 98336 | tf_op jit(solution)/shard_map/ppermute | solution.py:239
  40.8 0.1 shard_map.154
  40.9 2.0 %collective-permute-start.15 = (bf16[320,256]{1,0:T(8,128)(2,1)S(1)}, bf16[320,256]{1,0:T(8,128)(2,1)S(1)}, u32[]{:S(2)}, u32[]{:S(2)}) collective-permute-start(bf16[320,256]{1,0:T(8,128)(2,1)S(1)} %get-tuple-element.88.refs_2_), channel_id=1, source_target_pairs={{0,12},{1,13},{2,14},{3,15},{4,8},{5,9},{6,10},{7,11},{8,4},{9,5},... | collective-permute-start | bytes 491528 | tf_op jit(solution)/shard_map/ppermute | solution.py:239
  42.9 0.3 collective-permute-done.17.refs_1_
  43.2 3.0 %collective-permute-start.18 = (bf16[192,256]{1,0:T(8,128)(2,1)S(1)}, bf16[192,256]{1,0:T(8,128)(2,1)S(1)}, u32[]{:S(2)}, u32[]{:S(2)}) collective-permute-start(bf16[192,256]{1,0:T(8,128)(2,1)S(1)} %get-tuple-element.95.refs_0_.refs_2_), channel_id=1, source_target_pairs={{0,4},{1,3},{2,6},{3,1},{4,0},{5,7},{6,2},{7,5},{8,12},{9,11},{10,... | collective-permute-start | bytes 294920 | tf_op jit(solution)/shard_map/ppermute | solution.py:239
  46.2 3.0 %collective-permute-done.18.refs_1_ = bf16[192,256]{1,0:T(8,128)(2,1)S(1)} collective-permute-done((bf16[192,256]{1,0:T(8,128)(2,1)S(1)}, bf16[192,256]{1,0:T(8,128)(2,1)S(1)}, u32[]{:S(2)}, u32[]{:S(2)}) %collective-permute-start.18) | collective-permute-done | bytes 98336 | tf_op jit(solution)/shard_map/ppermute | solution.py:239
  49.3 1.7 %collective-permute-start.20 = (bf16[192,256]{1,0:T(8,128)(2,1)S(1)}, bf16[192,256]{1,0:T(8,128)(2,1)S(1)}, u32[]{:S(2)}, u32[]{:S(2)}) collective-permute-start(bf16[192,256]{1,0:T(8,128)(2,1)S(1)} %shard_map.159.refs_0_.refs_2_), channel_id=1, source_target_pairs={{0,4},{1,3},{2,6},{3,1},{4,0},{5,7},{6,2},{7,5},{8,12},{9,11},{10,... | collective-permute-start | bytes 294920 | tf_op jit(solution)/shard_map/ppermute | solution.py:239
  51.0 1.2 %collective-permute-start.19 = (bf16[384,256]{1,0:T(8,128)(2,1)S(1)}, bf16[384,256]{1,0:T(8,128)(2,1)S(1)}, u32[]{:S(2)}, u32[]{:S(2)}) collective-permute-start(bf16[384,256]{1,0:T(8,128)(2,1)S(1)} %shard_map.158.refs_2_.refs_0_), channel_id=1, source_target_pairs={{0,2},{1,5},{2,0},{3,7},{4,6},{5,1},{6,4},{7,3},{8,10},{9,13},{10,... | collective-permute-start | bytes 589832 | tf_op jit(solution)/shard_map/ppermute | solution.py:239
  52.2 2.1 %collective-permute-done.20.refs_1_ = bf16[192,256]{1,0:T(8,128)(2,1)S(1)} collective-permute-done((bf16[192,256]{1,0:T(8,128)(2,1)S(1)}, bf16[192,256]{1,0:T(8,128)(2,1)S(1)}, u32[]{:S(2)}, u32[]{:S(2)}) %collective-permute-start.20) | collective-permute-done | bytes 98336 | tf_op jit(solution)/shard_map/ppermute | solution.py:239
  54.3 2.3 %collective-permute-start.21 = (bf16[384,256]{1,0:T(8,128)(2,1)S(1)}, bf16[384,256]{1,0:T(8,128)(2,1)S(1)}, u32[]{:S(2)}, u32[]{:S(2)}) collective-permute-start(bf16[384,256]{1,0:T(8,128)(2,1)S(1)} %shard_map.160.refs_2_), channel_id=1, source_target_pairs={{0,2},{1,5},{2,0},{3,7},{4,6},{5,1},{6,4},{7,3},{8,10},{9,13},{10,... | collective-permute-start | bytes 589832 | tf_op jit(solution)/shard_map/ppermute | solution.py:239
  56.6 0.2 shard_map.155
  56.8 0.6 collective-permute-start.16
  57.4 0.6 collective-permute-done.8.refs_1_
  58.0 0.3 collective-permute-done.16.refs_3_
  58.3 0.8 %shard_map.157 = (f32[320,256]{1,0:T(8,128)}, bf16[128,256]{1,0:T(8,128)(2,1)}, f32[6,256]{1,0:T(8,128)}) custom-call(f32[320,256]{1,0:T(8,128)S(1)} %get-tuple-element.71.refs_0_, bf16[320,256]{1,0:T(8,128)(2,1)S(1)} %collective-permute-done.8.refs_1_, f32[128,256]{1,0:T(8,128)S(1)} %get-tuple-element.89.refs_2_, ...), custom_call_target="tpu_custom_call" | custom-call | tf_op jit(solution)/shard_map/pallas_call | solution.py:32
  59.1 0.8 %shard_map.161.refs_4_ = f32[512,256]{1,0:T(8,128)} custom-call(bf16[384,256]{1,0:T(8,128)(2,1)S(1)} %shard_map.158.refs_2_.refs_0_, bf16[384,256]{1,0:T(8,128)(2,1)S(1)} %collective-permute-done.19.refs_1_, bf16[128,256]{1,0:T(8,128)(2,1)} %get-tuple-element.47.refs_2_), custom_call_target="tpu_custom_call" | custom-call | tf_op jit(solution)/shard_map/pallas_call | solution.py:32
  59.9 0.3 collective-permute-done.21.refs_3_
  60.2 1.0 %shard_map.162 = (f32[256,512]{1,0:T(8,128)}, f32[512,256]{1,0:T(8,128)}) custom-call(bf16[384,256]{1,0:T(8,128)(2,1)S(1)} %shard_map.158.refs_2_.refs_0_, bf16[384,256]{1,0:T(8,128)(2,1)S(1)} %collective-permute-done.19.refs_1_, bf16[384,256]{1,0:T(8,128)(2,1)S(1)} %shard_map.160.refs_2_, bf16[384,256]{1,0:T(8,128)(2,1)S(1)} %collective-permute-done.21.refs_3_, ...), custom_call_target="tpu_custom_call" | custom-call | tf_op jit(solution)/shard_map/pallas_call | solution.py:32
  (14 shorter events, 0.2 us)
Async XLA Ops:
  1.9 11.0 %collective-permute-start = (bf16[144,128]{1,0:T(8,128)(2,1)S(1)}, bf16[144,128]{1,0:T(8,128)(2,1)S(1)}, u32[]{:S(2)}, u32[]{:S(2)}) collective-permute-start(bf16[144,128]{1,0:T(8,128)(2,1)S(1)} %get-tuple-element.54), channel_id=1, source_target_pairs={{0,2},{2,4},{4,6},{6,8},{8,10},{10,12},{12,14},{14,0},{1,3},{3,5},... | collective-permute-start | bytes 110600 | tf_op jit(solution)/shard_map/ppermute | solution.py:79
  4.9 9.3 %collective-permute-start.1 = (bf16[144,128]{1,0:T(8,128)(2,1)S(1)}, bf16[144,128]{1,0:T(8,128)(2,1)S(1)}, u32[]{:S(2)}, u32[]{:S(2)}) collective-permute-start(bf16[144,128]{1,0:T(8,128)(2,1)S(1)} %get-tuple-element.55), channel_id=1, source_target_pairs={{0,4},{2,6},{4,8},{6,10},{8,12},{10,14},{12,0},{14,2},{1,5},{3,7},... | collective-permute-start | bytes 110600 | tf_op jit(solution)/shard_map/ppermute | solution.py:79
  6.5 10.9 %collective-permute-start.2 = (bf16[144,128]{1,0:T(8,128)(2,1)S(1)}, bf16[144,128]{1,0:T(8,128)(2,1)S(1)}, u32[]{:S(2)}, u32[]{:S(2)}) collective-permute-start(bf16[144,128]{1,0:T(8,128)(2,1)S(1)} %get-tuple-element.56), channel_id=1, source_target_pairs={{0,6},{2,8},{4,10},{6,12},{8,14},{10,0},{12,2},{14,4},{1,7},{3,9},... | collective-permute-start | bytes 110600 | tf_op jit(solution)/shard_map/ppermute | solution.py:79
  9.1 8.4 %collective-permute-start.3 = (bf16[144,128]{1,0:T(8,128)(2,1)S(1)}, bf16[144,128]{1,0:T(8,128)(2,1)S(1)}, u32[]{:S(2)}, u32[]{:S(2)}) collective-permute-start(bf16[144,128]{1,0:T(8,128)(2,1)S(1)} %get-tuple-element.57), channel_id=1, source_target_pairs={{0,8},{2,10},{4,12},{6,14},{8,0},{10,2},{12,4},{14,6},{1,9},{3,11}... | collective-permute-start | bytes 110600 | tf_op jit(solution)/shard_map/ppermute | solution.py:79
  10.3 7.2 %collective-permute-start.4 = (bf16[144,128]{1,0:T(8,128)(2,1)S(1)}, bf16[144,128]{1,0:T(8,128)(2,1)S(1)}, u32[]{:S(2)}, u32[]{:S(2)}) collective-permute-start(bf16[144,128]{1,0:T(8,128)(2,1)S(1)} %get-tuple-element.58), channel_id=1, source_target_pairs={{0,10},{2,12},{4,14},{6,0},{8,2},{10,4},{12,6},{14,8},{1,11},{3,13... | collective-permute-start | bytes 110600 | tf_op jit(solution)/shard_map/ppermute | solution.py:79
  12.9 4.5 %collective-permute-start.5 = (bf16[144,128]{1,0:T(8,128)(2,1)S(1)}, bf16[144,128]{1,0:T(8,128)(2,1)S(1)}, u32[]{:S(2)}, u32[]{:S(2)}) collective-permute-start(bf16[144,128]{1,0:T(8,128)(2,1)S(1)} %get-tuple-element.59), channel_id=1, source_target_pairs={{0,12},{2,14},{4,0},{6,2},{8,4},{10,6},{12,8},{14,10},{1,13},{3,15... | collective-permute-start | bytes 110600 | tf_op jit(solution)/shard_map/ppermute | solution.py:79
  14.3 4.0 %collective-permute-start.6 = (bf16[144,128]{1,0:T(8,128)(2,1)S(1)}, bf16[144,128]{1,0:T(8,128)(2,1)S(1)}, u32[]{:S(2)}, u32[]{:S(2)}) collective-permute-start(bf16[144,128]{1,0:T(8,128)(2,1)S(1)} %get-tuple-element.60), channel_id=1, source_target_pairs={{0,14},{2,0},{4,2},{6,4},{8,6},{10,8},{12,10},{14,12},{1,15},{3,1}... | collective-permute-start | bytes 110600 | tf_op jit(solution)/shard_map/ppermute | solution.py:79
  18.3 1.6 %collective-permute-start.7 = (bf16[7,144,128]{2,1,0:T(8,128)(2,1)S(1)}, bf16[7,144,128]{2,1,0:T(8,128)(2,1)S(1)}, u32[]{:S(2)}, u32[]{:S(2)}) collective-permute-start(bf16[7,144,128]{2,1,0:T(8,128)(2,1)S(1)} %shard_map.147.refs_1_), channel_id=1, source_target_pairs={{0,1},{1,0},{2,3},{3,2},{4,5},{5,4},{6,7},{7,6},{8,9},{9,8},{10,11... | collective-permute-start | bytes 774152 | tf_op jit(solution)/shard_map/ppermute | solution.py:79
  22.8 5.8 %collective-permute-start.10 = (bf16[400,256]{1,0:T(8,128)(2,1)S(1)}, bf16[400,256]{1,0:T(8,128)(2,1)S(1)}, u32[]{:S(2)}, u32[]{:S(2)}) collective-permute-start(bf16[400,256]{1,0:T(8,128)(2,1)S(1)} %get-tuple-element.76), channel_id=1, source_target_pairs={{0,2},{1,5},{2,0},{3,7},{4,6},{5,1},{6,4},{7,3},{8,10},{9,13},{10,... | collective-permute-start | bytes 614408 | tf_op jit(solution)/shard_map/ppermute | solution.py:239
  24.4 10.0 %collective-permute-start.9 = (bf16[384,256]{1,0:T(8,128)(2,1)S(1)}, bf16[384,256]{1,0:T(8,128)(2,1)S(1)}, u32[]{:S(2)}, u32[]{:S(2)}) collective-permute-start(bf16[384,256]{1,0:T(8,128)(2,1)S(1)} %get-tuple-element.74), channel_id=1, source_target_pairs={{0,2},{1,5},{2,0},{3,7},{4,6},{5,1},{6,4},{7,3},{8,10},{9,13},{10,... | collective-permute-start | bytes 589832 | tf_op jit(solution)/shard_map/ppermute | solution.py:239
  24.9 8.4 %collective-permute-start.12 = (bf16[256,256]{1,0:T(8,128)(2,1)S(1)}, bf16[256,256]{1,0:T(8,128)(2,1)S(1)}, u32[]{:S(2)}, u32[]{:S(2)}) collective-permute-start(bf16[256,256]{1,0:T(8,128)(2,1)S(1)} %get-tuple-element.80), channel_id=1, source_target_pairs={{0,2},{1,5},{2,0},{3,7},{4,6},{5,1},{6,4},{7,3},{8,10},{9,13},{10,... | collective-permute-start | bytes 393224 | tf_op jit(solution)/shard_map/ppermute | solution.py:239
  28.7 5.6 %collective-permute-start.11 = (bf16[208,256]{1,0:T(8,128)(2,1)S(1)}, bf16[208,256]{1,0:T(8,128)(2,1)S(1)}, u32[]{:S(2)}, u32[]{:S(2)}) collective-permute-start(bf16[208,256]{1,0:T(8,128)(2,1)S(1)} %get-tuple-element.78.refs_3_), channel_id=1, source_target_pairs={{0,4},{1,3},{2,6},{3,1},{4,0},{5,7},{6,2},{7,5},{8,12},{9,11},{10,... | collective-permute-start | bytes 319496 | tf_op jit(solution)/shard_map/ppermute | solution.py:239
  33.6 5.0 %collective-permute-start.14 = (bf16[256,256]{1,0:T(8,128)(2,1)S(1)}, bf16[256,256]{1,0:T(8,128)(2,1)S(1)}, u32[]{:S(2)}, u32[]{:S(2)}) collective-permute-start(bf16[256,256]{1,0:T(8,128)(2,1)S(1)} %get-tuple-element.82.refs_2_), channel_id=1, source_target_pairs={{0,4},{1,3},{2,6},{3,1},{4,0},{5,7},{6,2},{7,5},{8,12},{9,11},{10,... | collective-permute-start | bytes 393224 | tf_op jit(solution)/shard_map/ppermute | solution.py:239
  34.4 6.4 %collective-permute-start.13 = (bf16[192,256]{1,0:T(8,128)(2,1)S(1)}, bf16[192,256]{1,0:T(8,128)(2,1)S(1)}, u32[]{:S(2)}, u32[]{:S(2)}) collective-permute-start(bf16[192,256]{1,0:T(8,128)(2,1)S(1)} %get-tuple-element.85.refs_4_), channel_id=1, source_target_pairs={{0,4},{1,3},{2,6},{3,1},{4,0},{5,7},{6,2},{7,5},{8,12},{9,11},{10,... | collective-permute-start | bytes 294920 | tf_op jit(solution)/shard_map/ppermute | solution.py:239
  35.9 7.3 %collective-permute-start.17 = (bf16[208,256]{1,0:T(8,128)(2,1)S(1)}, bf16[208,256]{1,0:T(8,128)(2,1)S(1)}, u32[]{:S(2)}, u32[]{:S(2)}) collective-permute-start(bf16[208,256]{1,0:T(8,128)(2,1)S(1)} %get-tuple-element.83.refs_2_), channel_id=1, source_target_pairs={{0,12},{1,13},{2,14},{3,15},{4,8},{5,9},{6,10},{7,11},{8,4},{9,5},... | collective-permute-start | bytes 319496 | tf_op jit(solution)/shard_map/ppermute | solution.py:239
  40.9 8.4 %collective-permute-start.15 = (bf16[320,256]{1,0:T(8,128)(2,1)S(1)}, bf16[320,256]{1,0:T(8,128)(2,1)S(1)}, u32[]{:S(2)}, u32[]{:S(2)}) collective-permute-start(bf16[320,256]{1,0:T(8,128)(2,1)S(1)} %get-tuple-element.88.refs_2_), channel_id=1, source_target_pairs={{0,12},{1,13},{2,14},{3,15},{4,8},{5,9},{6,10},{7,11},{8,4},{9,5},... | collective-permute-start | bytes 491528 | tf_op jit(solution)/shard_map/ppermute | solution.py:239
  43.2 6.0 %collective-permute-start.18 = (bf16[192,256]{1,0:T(8,128)(2,1)S(1)}, bf16[192,256]{1,0:T(8,128)(2,1)S(1)}, u32[]{:S(2)}, u32[]{:S(2)}) collective-permute-start(bf16[192,256]{1,0:T(8,128)(2,1)S(1)} %get-tuple-element.95.refs_0_.refs_2_), channel_id=1, source_target_pairs={{0,4},{1,3},{2,6},{3,1},{4,0},{5,7},{6,2},{7,5},{8,12},{9,11},{10,... | collective-permute-start | bytes 294920 | tf_op jit(solution)/shard_map/ppermute | solution.py:239
  49.3 5.0 %collective-permute-start.20 = (bf16[192,256]{1,0:T(8,128)(2,1)S(1)}, bf16[192,256]{1,0:T(8,128)(2,1)S(1)}, u32[]{:S(2)}, u32[]{:S(2)}) collective-permute-start(bf16[192,256]{1,0:T(8,128)(2,1)S(1)} %shard_map.159.refs_0_.refs_2_), channel_id=1, source_target_pairs={{0,4},{1,3},{2,6},{3,1},{4,0},{5,7},{6,2},{7,5},{8,12},{9,11},{10,... | collective-permute-start | bytes 294920 | tf_op jit(solution)/shard_map/ppermute | solution.py:239
  51.0 8.1 %collective-permute-start.19 = (bf16[384,256]{1,0:T(8,128)(2,1)S(1)}, bf16[384,256]{1,0:T(8,128)(2,1)S(1)}, u32[]{:S(2)}, u32[]{:S(2)}) collective-permute-start(bf16[384,256]{1,0:T(8,128)(2,1)S(1)} %shard_map.158.refs_2_.refs_0_), channel_id=1, source_target_pairs={{0,2},{1,5},{2,0},{3,7},{4,6},{5,1},{6,4},{7,3},{8,10},{9,13},{10,... | collective-permute-start | bytes 589832 | tf_op jit(solution)/shard_map/ppermute | solution.py:239
  54.3 5.9 %collective-permute-start.21 = (bf16[384,256]{1,0:T(8,128)(2,1)S(1)}, bf16[384,256]{1,0:T(8,128)(2,1)S(1)}, u32[]{:S(2)}, u32[]{:S(2)}) collective-permute-start(bf16[384,256]{1,0:T(8,128)(2,1)S(1)} %shard_map.160.refs_2_), channel_id=1, source_target_pairs={{0,2},{1,5},{2,0},{3,7},{4,6},{5,1},{6,4},{7,3},{8,10},{9,13},{10,... | collective-permute-start | bytes 589832 | tf_op jit(solution)/shard_map/ppermute | solution.py:239
  56.6 1.4 %collective-permute-start.8 = (bf16[320,256]{1,0:T(8,128)(2,1)S(1)}, bf16[320,256]{1,0:T(8,128)(2,1)S(1)}, u32[]{:S(2)}, u32[]{:S(2)}) collective-permute-start(bf16[320,256]{1,0:T(8,128)(2,1)S(1)} %get-tuple-element.72), channel_id=1, source_target_pairs={{0,1},{1,0},{2,3},{3,2},{4,5},{5,4},{6,7},{7,6},{8,9},{9,8},{10,11... | collective-permute-start | bytes 491528 | tf_op jit(solution)/shard_map/ppermute | solution.py:79
  56.8 1.5 %collective-permute-start.16 = (bf16[128,256]{1,0:T(8,128)(2,1)S(1)}, bf16[128,256]{1,0:T(8,128)(2,1)S(1)}, u32[]{:S(2)}, u32[]{:S(2)}) collective-permute-start(bf16[128,256]{1,0:T(8,128)(2,1)S(1)} %get-tuple-element.90), channel_id=1, source_target_pairs={{0,1},{1,0},{2,3},{3,2},{4,5},{5,4},{6,7},{7,6},{8,9},{9,8},{10,11... | collective-permute-start | bytes 196616 | tf_op jit(solution)/shard_map/ppermute | solution.py:79
